TPU v7x, 32 devices: a whole 2x2x4 slice. The times are simulated.
32 devices in a mesh: dp: 4 (over y, x), expert: 8 (over z, core).
Axes of the slice: x: 2, y: 2, z: 4, core: 2. Of those that a mesh axis runs over, the one named last changes fastest.
Arguments:
- tokens: bfloat16 [1024, 4096], P(('dp', 'expert')), may hold values from -6 to 6
- expert_ids: int32 [1024, 8], P(('dp', 'expert')), may hold values from 0 to 15, all different within a row; in each aligned block of 32 rows (0 to 31, 32 to 63, ...) at most 32 rows name the same one
- gate_vals: float32 [1024, 8], P(('dp', 'expert')), may hold values from 0.05 to 0.35
- gate_q: bfloat16 [4, 4096, 3072], P('dp', None, 'expert'), may hold values from -0.09375 to 0.09375
- up_q: bfloat16 [4, 4096, 3072], P('dp', None, 'expert'), may hold values from -0.09375 to 0.09375
- down_q: bfloat16 [4, 3072, 4096], P('dp', 'expert'), may hold values from -0.21875 to 0.21875
- gate_scale: float32 [4, 32, 24], P('dp', None, 'expert'), may hold values from 0.25 to 2
- up_scale: float32 [4, 32, 24], P('dp', None, 'expert'), may hold values from 0.25 to 2
- down_scale: float32 [4, 24, 32], P('dp', 'expert'), may hold values from 0.25 to 2
Outputs:
- mixed: bfloat16 [1024, 4096], P(('dp', 'expert'))
Inputs may be any that keep to these rules, and one draw needn't show every extreme that they name: `expert_ids`: each token names 8 different experts; the 32 tokens of one device name any one expert at most 32 times, and some device names some expert exactly 32 times.
All inputs are finite; a program needn't handle non-finite values.
Results may differ from a plain program's by a relative error of at most 0.006.
Values may be sent and summed in bfloat16 or wider, within the bound.
No kernel may reach another device: no remote copies, remote signals or barrier semaphores. Data moves between devices by JAX's collectives and lax.ppermute only.
A program may use at most 128 MiB of HBM per device.

v0:
```python
import jax
import jax.numpy as jnp
from jax import lax
from jax.sharding import PartitionSpec as P

BLOCK = 128


def from_partner(block, axis, bit):
    count = lax.axis_size(axis)
    route = []
    for low in range(count):
        high = low | 1 << bit
        if high != low and high < count:
            route += [(low, high), (high, low)]
    return lax.ppermute(block, axis, route)


def dequantize(quant_vals, block_scale):
    row_count, col_count = quant_vals.shape
    blocked = quant_vals.reshape(row_count // BLOCK, BLOCK, col_count // BLOCK, BLOCK).astype(
        jnp.float32
    )
    scaled = blocked * block_scale[:, None, :, None]
    return scaled.reshape(row_count, col_count).astype(jnp.bfloat16)


def expert_ffn(inputs, w_gate, w_up, w_down):
    gate_part = jnp.dot(inputs, w_gate, preferred_element_type=jnp.float32)
    up_part = jnp.dot(inputs, w_up, preferred_element_type=jnp.float32)
    hidden = (jax.nn.silu(gate_part) * up_part).astype(jnp.bfloat16)
    return jnp.dot(hidden, w_down, preferred_element_type=jnp.float32)


def across_groups(blocks):
    return lax.all_to_all(blocks, "dp", split_axis=1, concat_axis=1, tiled=True)


def across_owners(blocks):
    return lax.all_to_all(blocks, "expert", split_axis=0, concat_axis=0, tiled=True)


def return_owners(blocks):
    return lax.all_to_all(blocks, "expert", split_axis=0, concat_axis=0, tiled=True)


def return_groups(blocks):
    return lax.all_to_all(blocks, "dp", split_axis=1, concat_axis=1, tiled=True)


def shards(tokens, expert_ids, gate_vals, gate_q, up_q, down_q, gate_scale, up_scale, down_scale):
    group_count = lax.axis_size("dp")
    owner_count = lax.axis_size("expert")
    token_count, model_width = tokens.shape
    top_count = expert_ids.shape[1]
    pair_count = owner_count // 2
    expert_count = group_count * pair_count
    capacity = 2 * token_count * top_count // expert_count
    half_cap = capacity // 2
    slot_count = owner_count * group_count * half_cap
    routes = expert_ids.reshape(-1)
    onehot = (routes[:, None] == jnp.arange(expert_count, dtype=jnp.int32)[None, :]).astype(
        jnp.int32
    )
    earlier = jnp.cumsum(onehot, axis=0) - onehot
    route_slot = jnp.sum(earlier * onehot, axis=1)
    route_group = routes // pair_count
    route_pair = routes % pair_count
    route_owner = 2 * route_pair + route_slot // half_cap
    route_place = route_slot % half_cap
    route_index = (route_owner * group_count + route_group) * half_cap + route_place
    chosen = jnp.arange(slot_count, dtype=jnp.int32)[:, None] == route_index[None, :]
    chosen = jnp.any(chosen.reshape(slot_count, token_count, top_count), axis=2).astype(
        jnp.bfloat16
    )
    outgoing = jnp.dot(chosen, tokens, preferred_element_type=jnp.float32).astype(jnp.bfloat16)
    outgoing = outgoing.reshape(owner_count, group_count, half_cap, model_width)
    arrived = across_owners(across_groups(outgoing))
    own_rows = arrived.reshape(-1, model_width)
    row_count = own_rows.shape[0]
    w_gate = dequantize(gate_q[0], gate_scale[0])
    w_up = dequantize(up_q[0], up_scale[0])
    w_down = dequantize(down_q[0], down_scale[0])
    partner_rows = from_partner(own_rows, "expert", 0)
    both_rows = jnp.concatenate([own_rows, partner_rows], axis=0)
    partial_value = expert_ffn(both_rows, w_gate, w_up, w_down)
    returned = from_partner(partial_value[row_count:], "expert", 0)
    expert_out = (partial_value[:row_count] + returned).astype(jnp.bfloat16)
    expert_out = expert_out.reshape(owner_count, group_count, half_cap, model_width)
    returned_rows = return_groups(return_owners(expert_out))
    returned_rows = returned_rows.reshape(slot_count, model_width)
    picked = returned_rows[route_index].reshape(token_count, top_count, model_width)
    weighted = jnp.einsum("tkd,tk->td", picked.astype(jnp.float32), gate_vals)
    mixed = tokens.astype(jnp.float32) + weighted
    return mixed.astype(jnp.bfloat16)


def solution(mesh):
    return jax.shard_map(
        shards,
        mesh=mesh,
        in_specs=(
            P(("dp", "expert"), None),
            P(("dp", "expert"), None),
            P(("dp", "expert"), None),
            P("dp", None, "expert"),
            P("dp", None, "expert"),
            P("dp", "expert", None),
            P("dp", None, "expert"),
            P("dp", None, "expert"),
            P("dp", "expert", None),
        ),
        out_specs=P(("dp", "expert"), None),
        check_vma=False,
    )
```

profile of v0, /device:TPU:0, one launch (start us, length us, event | category | flops | bytes accessed | tf_op | source)
XLA Modules:
  0.0 405.8 jit_solution(13315042833576688270)
XLA Ops:
  0.0 0.8 copy.64
  0.8 0.1 eq.47
  0.9 0.1 eq.43
  1.0 0.6 reduce-window.6
  1.5 0.2 slice_reduce_fusion
  1.8 0.1 fusion.30
  2.0 0.2 fusion.17
  2.2 2.2 convolution_convert_fusion
  4.5 0.5 copy.71
  5.0 52.8 %all_to_all.20 = bf16[8,4,16,4096]{3,2,0,1:T(8,128)(2,1)S(1)} all-to-all(bf16[8,4,16,4096]{3,2,0,1:T(8,128)(2,1)S(1)} %copy.71), channel_id=1, replica_groups=mesh['dp'=4,'expert'=8] {'dp'}, dimensions={1} | all-to-all | bytes 8388608 | tf_op jit(solution)/shard_map/all_to_all | solution.py:36
  57.8 0.5 copy.72
  58.3 99.1 %all_to_all.21 = bf16[8,4,16,4096]{3,2,1,0:T(8,128)(2,1)} all-to-all(bf16[8,4,16,4096]{3,2,1,0:T(8,128)(2,1)S(1)} %copy.72), channel_id=1, replica_groups=mesh['dp'=4,'expert'=8] {'expert'}, dimensions={0} | all-to-all | bytes 8388608 | tf_op jit(solution)/shard_map/all_to_all | solution.py:40
  157.4 2.9 copy.74
  160.3 3.2 copy.73
  163.5 1.3 collective-permute-done
  164.9 0.9 mul.115
  165.8 9.6 %fusion.4 = f32[1024,384]{1,0:T(8,128)} fusion(bf16[512,4096]{1,0:T(8,128)(2,1)} %collective-permute-done, bf16[512,4096]{1,0:T(8,128)(2,1)} %bitcast.2, f32[48,8,32,128]{3,2,1,0:T(8,128)S(1)} %bitcast.101, bf16[1,4096,384]{1,2,0:T(8,128)(2,1)S(1)} %copy-done.1), kind=kOutput, calls=%fused_computation.11 | convolution fusion | flops 3242721280 | bytes 19398656 | tf_op jit(solution)/shard_map/dot_general | solution.py:30
  175.3 3.5 mul.110
  178.9 3.5 mul.120
  182.4 35.0 %fusion.8 = f32[1024,4096]{1,0:T(8,128)} fusion(f32[48,8,32,128]{3,2,1,0:T(8,128)} %bitcast.98, bf16[1,384,4096]{2,1,0:T(8,128)(2,1)} %param.14, f32[1024,384]{1,0:T(8,128)} %fusion.4, bf16[512,4096]{1,0:T(8,128)(2,1)} %collective-permute-done, bf16[512,4096]{1,0:T(8,128)(2,1)} %bitcast.2, f32[48,8,32,128]{3,2,1,0:T(8,128)} %bitcast.96, ...), kind=kOutput, calls=%fused_computation.13 | convolution fusion | flops 6471024640 | bytes 45613056 | tf_op jit(solution)/shard_map/dot_general | solution.py:32
  217.4 3.9 slice.20
  221.3 0.2 collective-permute-start.1
  221.5 13.2 %collective-permute-done.1 = f32[512,4096]{1,0:T(8,128)} collective-permute-done((f32[512,4096]{1,0:T(8,128)S(1)}, f32[512,4096]{1,0:T(8,128)}, u32[]{:S(2)}, u32[]{:S(2)}) %collective-permute-start.1) | collective-permute-done | bytes 8388640 | tf_op jit(solution)/shard_map/ppermute | solution.py:16
  234.7 7.0 %fusion = bf16[512,4096]{1,0:T(8,128)(2,1)S(1)} fusion(f32[512,4096]{1,0:T(8,128)} %collective-permute-done.1, f32[1024,4096]{1,0:T(8,128)} %fusion.8), kind=kLoop, calls=%fused_computation.2 | loop fusion | flops 4194304 | bytes 20971520 | tf_op jit(solution)/shard_map/convert_element_type | solution.py:88
  241.7 96.5 %all_to_all.22 = bf16[8,4,16,4096]{3,2,1,0:T(8,128)(2,1)S(1)} all-to-all(bf16[8,4,16,4096]{3,2,1,0:T(8,128)(2,1)S(1)} %bitcast.99), channel_id=1, replica_groups=mesh['dp'=4,'expert'=8] {'expert'}, dimensions={0} | all-to-all | bytes 8388608 | tf_op jit(solution)/shard_map/all_to_all | solution.py:44
  338.2 2.2 copy.75
  340.4 5.2 %all-to-all-start.3 = ((bf16[8,4,16,4096]{3,2,0,1:T(8,128)(2,1)}), bf16[8,4,16,4096]{3,2,0,1:T(8,128)(2,1)}, u32[]{:S(2)}, u32[]{:S(2)}) async-start(bf16[8,4,16,4096]{3,2,0,1:T(8,128)(2,1)} %copy.75), calls=%async_computation.3 | async-start | bytes 8388608 | tf_op jit(solution)/shard_map/all_to_all | solution.py:48
  345.9 46.9 %all-to-all-done.3 = bf16[8,4,16,4096]{3,2,0,1:T(8,128)(2,1)} async-done(((bf16[8,4,16,4096]{3,2,0,1:T(8,128)(2,1)}), bf16[8,4,16,4096]{3,2,0,1:T(8,128)(2,1)}, u32[]{:S(2)}, u32[]{:S(2)}) %all-to-all-start.3) | async-done | bytes 4194336 | tf_op jit(solution)/shard_map/all_to_all | solution.py:48
  392.7 4.7 %copy.76 = bf16[8,4,16,4096]{3,2,1,0:T(8,128)(2,1)} copy(bf16[8,4,16,4096]{3,2,0,1:T(8,128)(2,1)} %all-to-all-done.3) | data formatting | bytes 8388608 | tf_op jit(solution)/shard_map/all_to_all | solution.py:48
  397.4 6.7 %gather_fusion = bf16[256,4096]{1,0:T(8,128)(2,1)S(1)} fusion(bf16[512,4096]{1,0:T(8,128)(2,1)} %bitcast.97, s32[1024]{0:T(1024)S(1)} %pad_clamp_fusion), kind=kCustom, calls=%fused_computation | custom fusion | bytes 4195328 | tf_op jit(solution)/shard_map/gather | solution.py:92
  404.1 0.7 fusion.13
  404.8 1.0 fusion.16
  (27 shorter events, 0.4 us)
Async XLA Ops:
  58.3 99.1 %copy-start.4 = (f32[1,32,3]{1,0,2:T(1,128)S(1)}, f32[1,32,3]{1,0,2:T(1,128)}, u32[]{:S(2)}) copy-start(f32[1,32,3]{1,0,2:T(1,128)} %param.16) | copy-start | bytes 1156
  58.3 99.1 %copy-start = (bf16[1,4096,384]{2,1,0:T(8,128)(2,1)S(1)}, bf16[1,4096,384]{2,1,0:T(8,128)(2,1)}, u32[]{:S(2)}) copy-start(bf16[1,4096,384]{2,1,0:T(8,128)(2,1)} %param.13) | copy-start | bytes 9437188
  157.4 2.9 copy-start.5
  157.4 3.0 copy-start.6
  157.4 7.5 %collective-permute-start = (bf16[512,4096]{1,0:T(8,128)(2,1)}, bf16[512,4096]{1,0:T(8,128)(2,1)}, u32[]{:S(2)}, u32[]{:S(2)}) collective-permute-start(bf16[512,4096]{1,0:T(8,128)(2,1)} %bitcast.2), channel_id=1, source_target_pairs={{0,1},{1,0},{2,3},{3,2},{4,5},{5,4},{6,7},{7,6},{8,9},{9,8},{10,11... | collective-permute-start | bytes 12582920 | tf_op jit(solution)/shard_map/ppermute | solution.py:16
  163.5 2.2 copy-start.1
  221.3 13.4 %collective-permute-start.1 = (f32[512,4096]{1,0:T(8,128)S(1)}, f32[512,4096]{1,0:T(8,128)}, u32[]{:S(2)}, u32[]{:S(2)}) collective-permute-start(f32[512,4096]{1,0:T(8,128)S(1)} %slice.20), channel_id=1, source_target_pairs={{0,1},{1,0},{2,3},{3,2},{4,5},{5,4},{6,7},{7,6},{8,9},{9,8},{10,11... | collective-permute-start | bytes 25165832 | tf_op jit(solution)/shard_map/ppermute | solution.py:16
  340.4 5.3 %copy-start.3 = (f32[32,8]{0,1:T(8,128)S(1)}, f32[32,8]{0,1:T(8,128)}, u32[]{:S(2)}) copy-start(f32[32,8]{0,1:T(8,128)} %param.11) | copy-start | bytes 3076
  340.4 52.3 %all-to-all-start.3 = ((bf16[8,4,16,4096]{3,2,0,1:T(8,128)(2,1)}), bf16[8,4,16,4096]{3,2,0,1:T(8,128)(2,1)}, u32[]{:S(2)}, u32[]{:S(2)}) async-start(bf16[8,4,16,4096]{3,2,0,1:T(8,128)(2,1)} %copy.75), calls=%async_computation.3 | async-start | bytes 8388608 | tf_op jit(solution)/shard_map/all_to_all | solution.py:48
  397.4 7.4 %copy-start.2 = (bf16[32,4096]{1,0:T(8,128)(2,1)S(1)}, bf16[32,4096]{1,0:T(8,128)(2,1)}, u32[]{:S(2)}) copy-start(bf16[32,4096]{1,0:T(8,128)(2,1)} %param.9) | copy-start | bytes 786436
where the time goes:
time: 406 us
  blocking collectives  248 us (61%)
  waiting for transfers between devices  61.4 us (15%)
  matrix products  47.5 us (12%)
  local copies, waits for them, and re-layouts  33.8 us (8%)
  other arithmetic  9.04 us (2%)
  starting transfers between devices  5.42 us (1%)
    all_to_all x1, blocking collectives, across_owners(): lax.all_to_all(blocks, 'expert', split_axis=0, concat_axis=0, tiled=True)  99.1 us
    all_to_all x1, blocking collectives, return_owners(): lax.all_to_all(blocks, 'expert', split_axis=0, concat_axis=0, tiled=True)  96.5 us
    all_to_all x1, blocking collectives, across_groups(): return lax.all_to_all(blocks, 'dp', split_axis=1, concat_axis=1, tiled=True)  52.8 us
    all_to_all x1, waiting for transfers between devices, return_groups(): return lax.all_to_all(blocks, 'dp', split_axis=1, concat_axis=1, tiled=True)  46.9 us
    dot_general x1, matrix products, expert_ffn(): return jnp.dot(hidden, w_down, preferred_element_type=jnp.float32)  35 us
    ppermute x2, waiting for transfers between devices, from_partner(): return lax.ppermute(block, axis, route)  14.5 us
    dot_general x1, matrix products, expert_ffn(): up_part = jnp.dot(inputs, w_up, preferred_element_type=jnp.float32)  9.57 us
  transfers between devices with their start and end apart: 3, of which 3 were waited for; matrix products, arithmetic and copies ran while one was open for 2% of the time, Pallas kernels for 0%

commit v1 on v0

--- a/solution.py
+++ b/solution.py
@@ -40,15 +40,7 @@
     return lax.all_to_all(blocks, "expert", split_axis=0, concat_axis=0, tiled=True)
 
 
-def return_owners(blocks):
-    return lax.all_to_all(blocks, "expert", split_axis=0, concat_axis=0, tiled=True)
-
-
-def return_groups(blocks):
-    return lax.all_to_all(blocks, "dp", split_axis=1, concat_axis=1, tiled=True)
-
-
-def shards(tokens, expert_ids, gate_vals, gate_q, up_q, down_q, gate_scale, up_scale, down_scale):
+def by_rows(tokens, expert_ids, gate_vals, gate_q, up_q, down_q, gate_scale, up_scale, down_scale):
     group_count = lax.axis_size("dp")
     owner_count = lax.axis_size("expert")
     token_count, model_width = tokens.shape
@@ -87,12 +79,43 @@
     returned = from_partner(partial_value[row_count:], "expert", 0)
     expert_out = (partial_value[:row_count] + returned).astype(jnp.bfloat16)
     expert_out = expert_out.reshape(owner_count, group_count, half_cap, model_width)
-    returned_rows = return_groups(return_owners(expert_out))
+    returned_rows = across_groups(across_owners(expert_out))
     returned_rows = returned_rows.reshape(slot_count, model_width)
     picked = returned_rows[route_index].reshape(token_count, top_count, model_width)
     weighted = jnp.einsum("tkd,tk->td", picked.astype(jnp.float32), gate_vals)
     mixed = tokens.astype(jnp.float32) + weighted
     return mixed.astype(jnp.bfloat16)
+
+
+def by_sums(tokens, expert_ids, gate_vals, gate_q, up_q, down_q, gate_scale, up_scale, down_scale):
+    both = ("dp", "expert")
+    pair_count = lax.axis_size("expert") // 2
+    expert_count = lax.axis_size("dp") * pair_count
+    own_expert = lax.axis_index("dp") * pair_count + lax.axis_index("expert") // 2
+    named = expert_ids[:, :, None] == jnp.arange(expert_count, dtype=jnp.int32)[None, None, :]
+    weight = jnp.sum(jnp.where(named, gate_vals[:, :, None], 0.0), axis=1)
+    all_weights = lax.all_gather(weight, both, axis=0, tiled=True)
+    own_weight = jnp.sum(
+        jnp.where(jnp.arange(expert_count)[None, :] == own_expert, all_weights, 0.0), axis=1
+    )
+    all_tokens = lax.all_gather(tokens, both, axis=0, tiled=True)
+    w_gate = dequantize(gate_q[0], gate_scale[0])
+    w_up = dequantize(up_q[0], up_scale[0])
+    w_down = dequantize(down_q[0], down_scale[0])
+    partial_value = expert_ffn(all_tokens, w_gate, w_up, w_down) * own_weight[:, None]
+    summed = lax.psum_scatter(
+        partial_value.astype(jnp.bfloat16), both, scatter_dimension=0, tiled=True
+    )
+    mixed = tokens.astype(jnp.float32) + summed.astype(jnp.float32)
+    return mixed.astype(jnp.bfloat16)
+
+
+def shards(tokens, expert_ids, *weights):
+    expert_count = lax.axis_size("dp") * lax.axis_size("expert") // 2
+    token_count, top_count = expert_ids.shape
+    capacity = 2 * token_count * top_count // expert_count
+    plan = by_rows if capacity < token_count else by_sums
+    return plan(tokens, expert_ids, *weights)
 
 
 def solution(mesh):

time: 406 us -> 286 us (0.70)
  blocking collectives: 248 us -> 45.1 us
  waiting for transfers between devices: 61.4 us -> 181 us
  local copies, waits for them, and re-layouts: 33.8 us -> 13.4 us
  matrix products: 47.5 us -> 30.8 us
  between operations: 0.19 us -> 13.5 us
  other arithmetic: 9.04 us -> 1.82 us
  starting transfers between devices: 5.42 us -> 0.04 us
    all_to_all x3 -> x0, blocking collectives: 248 us -> none  [the longest x1 99.1 us: across_owners(): lax.all_to_all(blocks, 'expert', split_axis=0, concat_axis=0, tiled=True)]
    reduce_scatter x0 -> x1, waiting for transfers between devices: none -> 151 us  [by_sums(): lax.psum_scatter(partial_value.astype(jnp.bfloat16), both, scatter_dimens...]
    all_to_all x1 -> x0, waiting for transfers between devices: 46.9 us -> none  [return_groups(): return lax.all_to_all(blocks, 'dp', split_axis=1, concat_axis=1, tiled=True)]
    all_gather x0 -> x1, blocking collectives: none -> 45.1 us  [by_sums(): all_weights = lax.all_gather(weight, both, axis=0, tiled=True)]
    all_gather x0 -> x1, waiting for transfers between devices: none -> 29.8 us  [by_sums(): all_tokens = lax.all_gather(tokens, both, axis=0, tiled=True)]
    dot_general x1, matrix products: 35 us -> 11 us  [expert_ffn(): return jnp.dot(hidden, w_down, preferred_element_type=jnp.float32)]
    ppermute x2 -> x0, waiting for transfers between devices: 14.5 us -> none  [from_partner(): return lax.ppermute(block, axis, route)]
    all_to_all x3 -> x0, local copies, waits for them, and re-layouts: 7.38 us -> none  [the longest x1 4.65 us: return_groups(): return lax.all_to_all(blocks, 'dp', split_axis=1, concat_axis=1, tiled=True)]
  transfers between devices with their start and end apart: 3 -> 2, of which waited for: 3 -> 2; matrix products, arithmetic and copies ran while one was open for 2% -> 3% of each run, Pallas kernels for 0% -> 0%
where the time goes in v1:
time: 286 us
  waiting for transfers between devices  181 us (63%)
  blocking collectives  45.1 us (16%)
  matrix products  30.8 us (11%)
  between operations  13.5 us (5%)
  local copies, waits for them, and re-layouts  13.4 us (5%)
    reduce_scatter x1, waiting for transfers between devices, by_sums(): lax.psum_scatter(partial_value.astype(jnp.bfloat16), both, scatter_dimens...  151 us
    all_gather x1, blocking collectives, by_sums(): all_weights = lax.all_gather(weight, both, axis=0, tiled=True)  45.1 us
    all_gather x1, waiting for transfers between devices, by_sums(): all_tokens = lax.all_gather(tokens, both, axis=0, tiled=True)  29.8 us
    dot_general x1, matrix products, expert_ffn(): return jnp.dot(hidden, w_down, preferred_element_type=jnp.float32)  11 us
    unnamed x24, local copies, waits for them, and re-layouts  10.8 us
    dot_general x1, matrix products, expert_ffn(): gate_part = jnp.dot(inputs, w_gate, preferred_element_type=jnp.float32)  10.2 us
    dot_general x1, matrix products, expert_ffn(): up_part = jnp.dot(inputs, w_up, preferred_element_type=jnp.float32)  9.57 us
  transfers between devices with their start and end apart: 2, of which 2 were waited for; matrix products, arithmetic and copies ran while one was open for 3% of the time, Pallas kernels for 0%

profile of v1, /device:TPU:0, one launch (start us, length us, event | category | flops | bytes accessed | tf_op | source)
XLA Modules:
  0.0 286.2 jit_solution(12080579735635903007)
XLA Ops:
  6.5 0.0 copy-start.6
  6.5 0.0 all-gather.3.cloned.1.call-start
  6.5 0.7 all-gather.3.cloned.1.call-update
  7.3 0.0 reduce-scatter.2.cloned.1.call-start
  7.3 0.9 copy.49
  8.2 4.8 %copy.27 = bf16[1,4096,384]{1,2,0:T(8,128)(2,1)} copy(bf16[1,4096,384]{2,1,0:T(8,128)(2,1)} %param.12) | data formatting | bytes 6291456 | tf_op args[3]
  12.9 0.0 copy-done.6
  12.9 0.0 copy-done
  13.0 3.0 %copy.28 = bf16[1,4096,384]{1,2,0:T(8,128)(2,1)} copy(bf16[1,4096,384]{2,1,0:T(8,128)(2,1)S(1)} %copy-done) | data formatting | bytes 6291456 | tf_op args[4]
  15.9 0.0 copy-done.4
  15.9 0.0 copy-done.5
  15.9 45.1 %all-gather = f32[32,32,16]{1,2,0:T(8,128)S(1)} all-gather(f32[1,32,16]{1,2,0:T(8,128)S(1)} %bitcast.82), channel_id=1, replica_groups=mesh['dp'=4,'expert'=8] {'dp','expert'}, dimensions={0}, use_global_device_ids=true | all-gather | bytes 67584 | tf_op jit(solution)/shard_map/all_gather | solution.py:97
  61.1 0.1 copy.29
  61.2 0.1 reshape.30
  61.3 0.0 copy-done.7
  61.4 0.1 select_reduce_fusion
  61.5 29.8 %all-gather.3.cloned.1.call-done = bf16[1024,4096]{1,0:T(8,128)(2,1)} async-done(((bf16[32,4096]{1,0:T(8,128)(2,1)}), bf16[1024,4096]{1,0:T(8,128)(2,1)}) %all-gather.3.cloned.1.call-update) | async-done | bytes 8388624 | tf_op jit(solution)/shard_map/all_gather | solution.py:101
  91.3 0.9 mul.58
  92.1 0.0 copy-done.2
  92.1 10.2 %fusion.3 = f32[384,1024]{1,0:T(8,128)S(1)} fusion(bf16[1024,4096]{1,0:T(8,128)(2,1)} %all-gather.3.cloned.1.call-done, f32[48,8,32,128]{3,2,1,0:T(8,128)S(1)} %bitcast.81, bf16[1,4096,384]{1,2,0:T(8,128)(2,1)S(1)} %copy-done.2), kind=kOutput, calls=%fused_computation.7 | convolution fusion | flops 3225944064 | bytes 19398656 | tf_op jit(solution)/shard_map/dot_general | solution.py:29
  102.4 0.0 copy-start.1
  102.4 0.9 mul.63
  103.2 1.0 copy-done.1
  104.2 9.6 %fusion.11 = bf16[1024,384]{0,1:T(8,128)(2,1)S(1)} fusion(f32[384,1024]{1,0:T(8,128)S(1)} %fusion.3, bf16[1024,4096]{1,0:T(8,128)(2,1)} %all-gather.3.cloned.1.call-done, f32[48,8,32,128]{3,2,1,0:T(8,128)S(1)} %bitcast.79, bf16[1,4096,384]{1,2,0:T(8,128)(2,1)S(1)} %copy-done.1), kind=kOutput, calls=%fused_computation.13 | convolution fusion | flops 3228303360 | bytes 20185088 | tf_op jit(solution)/shard_map/dot_general | solution.py:30
  113.8 0.0 copy-start.8
  113.8 0.9 mul.68
  114.7 1.0 copy-done.8
  115.7 11.0 %multiply_convert_fusion = bf16[1024,4096]{1,0:T(8,128)(2,1)} fusion(bf16[1024,384]{0,1:T(8,128)(2,1)S(1)} %fusion.11, f32[1024]{0:T(1024)S(1)} %select_reduce_fusion, f32[48,8,32,128]{3,2,1,0:T(8,128)S(1)} %bitcast.80, bf16[1,384,4096]{2,1,0:T(8,128)(2,1)S(1)} %copy-done.8), kind=kOutput, calls=%fused_computation | convolution fusion | flops 3234332672 | bytes 18616320 | tf_op jit(solution)/shard_map/dot_general | solution.py:32
  126.7 0.0 reduce-scatter.2.cloned.1.call-update
  126.7 150.9 %reduce-scatter.2.cloned.1.call-done = bf16[32,4096]{1,0:T(8,128)(2,1)} async-done(((bf16[1024,4096]{1,0:T(8,128)(2,1)}), bf16[32,4096]{1,0:T(8,128)(2,1)}) %reduce-scatter.2.cloned.1.call-update) | async-done | bytes 262160 | tf_op jit(solution)/shard_map/reduce_scatter | solution.py:106
  277.6 0.0 copy-done.3
  277.6 1.7 add_convert_fusion
  (10 shorter events, 0.0 us)
Async XLA Ops:
  6.5 6.4 %copy-start.6 = (f32[1,32,3]{1,0,2:T(1,128)S(1)}, f32[1,32,3]{1,0,2:T(1,128)}, u32[]{:S(2)}) copy-start(f32[1,32,3]{1,0,2:T(1,128)} %param.16) | copy-start | bytes 1156
  6.5 6.4 %copy-start = (bf16[1,4096,384]{2,1,0:T(8,128)(2,1)S(1)}, bf16[1,4096,384]{2,1,0:T(8,128)(2,1)}, u32[]{:S(2)}) copy-start(bf16[1,4096,384]{2,1,0:T(8,128)(2,1)} %param.13) | copy-start | bytes 9437188
  6.5 84.7 %all-gather.3.cloned.1.call-start = ((), (), s32[]{:S(2)}) async-start(), calls=%async_computation.1 | async-start | bytes 8650752 | tf_op jit(solution)/shard_map/all_gather | solution.py:101
  7.3 270.3 %reduce-scatter.2.cloned.1.call-start = ((), (), s32[]{:S(2)}) async-start(), calls=%async_computation.2 | async-start | bytes 8650752 | tf_op jit(solution)/shard_map/reduce_scatter | solution.py:106
  8.2 7.7 %copy-start.4 = (f32[32,8]{0,1:T(8,128)S(1)}, f32[32,8]{0,1:T(8,128)}, u32[]{:S(2)}) copy-start(f32[32,8]{0,1:T(8,128)} %param.11) | copy-start | bytes 3076
  8.2 7.7 %copy-start.5 = (s32[32,8]{0,1:T(8,128)S(1)}, s32[32,8]{0,1:T(8,128)}, u32[]{:S(2)}) copy-start(s32[32,8]{0,1:T(8,128)} %param.10) | copy-start | bytes 3076
  8.2 53.1 %copy-start.7 = (f32[1,3,32]{2,0,1:T(1,128)S(1)}, f32[1,3,32]{2,0,1:T(1,128)}, u32[]{:S(2)}) copy-start(f32[1,3,32]{2,0,1:T(1,128)} %param.17) | copy-start | bytes 1156
  15.9 76.2 %copy-start.2 = (bf16[1,4096,384]{1,2,0:T(8,128)(2,1)S(1)}, bf16[1,4096,384]{1,2,0:T(8,128)(2,1)}, u32[]{:S(2)}) copy-start(bf16[1,4096,384]{1,2,0:T(8,128)(2,1)} %copy.27) | copy-start | bytes 9437188
  102.4 1.9 copy-start.1
  113.8 1.9 copy-start.8
  126.7 150.9 %copy-start.3 = (bf16[32,4096]{1,0:T(8,128)(2,1)S(1)}, bf16[32,4096]{1,0:T(8,128)(2,1)}, u32[]{:S(2)}) copy-start(bf16[32,4096]{1,0:T(8,128)(2,1)} %param.9) | copy-start | bytes 786436
Sparse Core Ops, SparseCore 0:
  10.3 80.8 all-gather.2
  126.8 150.7 reduce-scatter.1

commit v2 on v1

--- a/solution.py
+++ b/solution.py
@@ -87,27 +87,90 @@
     return mixed.astype(jnp.bfloat16)
 
 
+def gather_groups(block, order):
+    for bit in order:
+        block = jnp.concatenate([block, from_partner(block, "dp", bit)], axis=0)
+    return block
+
+
+def sum_groups(block, order):
+    for bit in reversed(order):
+        kept, sent = jnp.split(block, 2, axis=0)
+        arrived = from_partner(sent, "dp", bit)
+        block = (kept.astype(jnp.float32) + arrived.astype(jnp.float32)).astype(jnp.bfloat16)
+    return block
+
+
+def across_chips(block, far):
+    count = lax.axis_size("expert")
+    return lax.ppermute(block, "expert", [(low, low ^ 2 * far) for low in range(count)])
+
+
 def by_sums(tokens, expert_ids, gate_vals, gate_q, up_q, down_q, gate_scale, up_scale, down_scale):
-    both = ("dp", "expert")
+    token_count, model_width = tokens.shape
+    group_count = lax.axis_size("dp")
     pair_count = lax.axis_size("expert") // 2
-    expert_count = lax.axis_size("dp") * pair_count
+    expert_count = group_count * pair_count
     own_expert = lax.axis_index("dp") * pair_count + lax.axis_index("expert") // 2
+    half = token_count // 2
+    bits = list(range(group_count.bit_length() - 1))
+    orders = (bits, bits[::-1])
+
     named = expert_ids[:, :, None] == jnp.arange(expert_count, dtype=jnp.int32)[None, None, :]
     weight = jnp.sum(jnp.where(named, gate_vals[:, :, None], 0.0), axis=1)
-    all_weights = lax.all_gather(weight, both, axis=0, tiled=True)
-    own_weight = jnp.sum(
-        jnp.where(jnp.arange(expert_count)[None, :] == own_expert, all_weights, 0.0), axis=1
-    )
-    all_tokens = lax.all_gather(tokens, both, axis=0, tiled=True)
+    high = weight.astype(jnp.bfloat16)
+    low = (weight - high.astype(jnp.float32)).astype(jnp.bfloat16)
+    extra = -(-2 * expert_count // BLOCK) * BLOCK
+    pad = jnp.zeros((token_count, extra - 2 * expert_count), jnp.bfloat16)
+    payload = jnp.concatenate([tokens, high, low, pad], axis=1)
+
     w_gate = dequantize(gate_q[0], gate_scale[0])
     w_up = dequantize(up_q[0], up_scale[0])
     w_down = dequantize(down_q[0], down_scale[0])
-    partial_value = expert_ffn(all_tokens, w_gate, w_up, w_down) * own_weight[:, None]
-    summed = lax.psum_scatter(
-        partial_value.astype(jnp.bfloat16), both, scatter_dimension=0, tiled=True
-    )
-    mixed = tokens.astype(jnp.float32) + summed.astype(jnp.float32)
-    return mixed.astype(jnp.bfloat16)
+    in_own = jnp.concatenate([w_gate, w_up], axis=1)
+    in_other = from_partner(in_own, "expert", 0)
+    down_other = from_partner(w_down, "expert", 0)
+    down_both = jnp.concatenate([w_down, down_other], axis=0)
+    hidden_half = w_gate.shape[1]
+
+    def ffn(rows):
+        inputs = rows[:, :model_width]
+        marks = rows[:, model_width:].astype(jnp.float32)
+        column = jnp.arange(extra, dtype=jnp.int32)[None, :]
+        chosen = (column == own_expert) | (column == own_expert + expert_count)
+        row_weight = jnp.sum(jnp.where(chosen, marks, 0.0), axis=1)
+        hidden = []
+        for w_in in (in_own, in_other):
+            parts = jnp.dot(inputs, w_in, preferred_element_type=jnp.float32)
+            hidden.append(
+                (jax.nn.silu(parts[:, :hidden_half]) * parts[:, hidden_half:]).astype(jnp.bfloat16)
+            )
+        hidden = jnp.concatenate(hidden, axis=1)
+        value = jnp.dot(hidden, down_both, preferred_element_type=jnp.float32)
+        return (value * row_weight[:, None]).astype(jnp.bfloat16)
+
+    from_far = {far: across_chips(payload, far) for far in range(1, pair_count)}
+    from_far[0] = payload
+    total = tokens.astype(jnp.float32)
+    step = 2
+    for first in range(0, pair_count, step):
+        fars = range(first, first + step)
+        gathered = []
+        for place, order in enumerate(orders):
+            rows = slice(place * half, (place + 1) * half)
+            block = jnp.stack([from_far[far][rows] for far in fars])[None]
+            gathered.append(gather_groups(block, order))
+        every = jnp.stack(gathered)
+        out = ffn(every.reshape(-1, every.shape[-1]))
+        out = out.reshape(every.shape[:-1] + (model_width,))
+        sums = [sum_groups(out[place], order)[0] for place, order in enumerate(orders)]
+        sums = jnp.concatenate(sums, axis=1)
+        for place, far in enumerate(fars):
+            block = sums[place]
+            if far > 0:
+                block = across_chips(block, far)
+            total = total + block.astype(jnp.float32)
+    return total.astype(jnp.bfloat16)
 
 
 def shards(tokens, expert_ids, *weights):

time: 286 us -> 158 us (0.55)
  the two profiles are of different devices: /device:TPU:0 before, /device:TPU:18 now
where the time goes in v2:
time: 158 us; the launch traced here: 157 us
  waiting for transfers between devices  65.5 us (41%)
  starting transfers between devices  24.4 us (15%)
  other arithmetic  24.1 us (15%)
  local copies, waits for them, and re-layouts  22.4 us (14%)
  matrix products  20.6 us (13%)
    ppermute x18, waiting for transfers between devices, from_partner(): return lax.ppermute(block, axis, route)  44.8 us
    ppermute x6, waiting for transfers between devices, across_chips(): lax.ppermute(block, 'expert', [(low, low ^ 2 * far) for low in range(coun...  20.7 us
    ppermute x18, starting transfers between devices, from_partner(): return lax.ppermute(block, axis, route)  17 us
    convert_element_type x2, other arithmetic, dequantize(): return scaled.reshape(row_count, col_count).astype(jnp.bfloat16)  15 us
    unnamed x21, local copies, waits for them, and re-layouts  14.5 us
    dot_general x4, matrix products, ffn(): parts = jnp.dot(inputs, w_in, preferred_element_type=jnp.float32)  13.1 us
    dot_general x2, matrix products, ffn(): value = jnp.dot(hidden, down_both, preferred_element_type=jnp.float32)  7.51 us
    ppermute x6, starting transfers between devices, across_chips(): lax.ppermute(block, 'expert', [(low, low ^ 2 * far) for low in range(coun...  7.39 us
  transfers between devices with their start and end apart: 24, of which 14 were waited for; matrix products, arithmetic and copies ran while one was open for 35% of the time, Pallas kernels for 0%

profile of v2, /device:TPU:18, one launch (start us, length us, event | category | flops | bytes accessed | tf_op | source)
XLA Modules:
  0.0 157.5 jit_solution(4034294023594370219)
XLA Ops:
  2.4 2.7 %collective-permute-start.13 = (bf16[32,4224]{1,0:T(8,128)(2,1)S(1)}, bf16[32,4224]{1,0:T(8,128)(2,1)}, u32[]{:S(2)}, u32[]{:S(2)}) collective-permute-start(bf16[32,4224]{1,0:T(8,128)(2,1)S(1)} %concatenate.49), channel_id=1, source_target_pairs={{0,6},{1,7},{2,4},{3,5},{4,2},{5,3},{6,0},{7,1},{8,14},{9,15},{10,... | collective-permute-start | bytes 811016 | tf_op jit(solution)/shard_map/ppermute | solution.py:106
  5.1 1.3 collective-permute-start
  7.8 3.2 %copy.20 = bf16[1,4096,384]{1,2,0:T(8,128)(2,1)S(1)} copy(bf16[1,4096,384]{2,1,0:T(8,128)(2,1)} %param.12) | data formatting | bytes 6291456 | tf_op args[3]
  11.0 4.8 %copy.21 = bf16[1,4096,384]{1,2,0:T(8,128)(2,1)} copy(bf16[1,4096,384]{2,1,0:T(8,128)(2,1)} %param.13) | data formatting | bytes 6291456 | tf_op args[4]
  18.5 8.7 %fusion.1 = (bf16[4096,384]{0,1:T(8,128)(2,1)S(1)}, bf16[4096,384]{0,1:T(8,128)(2,1)S(1)}) fusion(f32[48,8,32,128]{3,2,1,0:T(8,128)S(1)} %bitcast.109, bf16[1,4096,384]{1,2,0:T(8,128)(2,1)S(1)} %copy-done, f32[48,8,32,128]{3,2,1,0:T(8,128)S(1)} %bitcast.108, bf16[1,4096,384]{1,2,0:T(8,128)(2,1)S(1)} %copy.20), kind=kLoop, calls=%fused_computation.3 | loop fusion | flops 9437184 | bytes 25165824 | tf_op jit(solution)/shard_map/convert_element_type | solution.py:25
  27.2 3.8 %pad_maximum_fusion = bf16[4096,768]{0,1:T(8,128)(2,1)} fusion(bf16[4096,384]{0,1:T(8,128)(2,1)S(1)} %get-tuple-element.27, bf16[4096,384]{0,1:T(8,128)(2,1)S(1)} %get-tuple-element.28), kind=kLoop, calls=%fused_computation.6 | loop fusion | flops 12582912 | bytes 12582912 | tf_op jit(solution)/shard_map/concatenate | solution.py:130
  33.8 6.4 %fusion = bf16[384,4096]{1,0:T(8,128)(2,1)S(1)} fusion(f32[48,8,32,128]{3,2,1,0:T(8,128)S(1)} %bitcast.107, bf16[1,384,4096]{2,1,0:T(8,128)(2,1)S(1)} %copy-done.5), kind=kLoop, calls=%fused_computation.1 | loop fusion | flops 4718592 | bytes 12582912 | tf_op jit(solution)/shard_map/convert_element_type | solution.py:25
  44.1 1.6 %collective-permute-start.16 = (bf16[1,2,16,4224]{3,2,1,0:T(8,128)(2,1)S(1)}, bf16[1,2,16,4224]{3,2,1,0:T(8,128)(2,1)S(1)}, u32[]{:S(2)}, u32[]{:S(2)}) collective-permute-start(bf16[1,2,16,4224]{3,2,1,0:T(8,128)(2,1)S(1)} %maximum_bitcast_fusion.7), channel_id=1, source_target_pairs={{0,16},{16,0},{8,24},{24,8},{1,17},{17,1},{9,25},{25,9},{2,18},{18... | collective-permute-start | bytes 811016 | tf_op jit(solution)/shard_map/ppermute | solution.py:16
  47.6 1.6 collective-permute-start.1
  49.2 3.7 %collective-permute-done.14 = bf16[1,2,16,4224]{3,2,1,0:T(8,128)(2,1)S(1)} collective-permute-done((bf16[1,2,16,4224]{3,2,1,0:T(8,128)(2,1)S(1)}, bf16[1,2,16,4224]{3,2,1,0:T(8,128)(2,1)S(1)}, u32[]{:S(2)}, u32[]{:S(2)}) %collective-permute-start.14) | collective-permute-done | bytes 270368 | tf_op jit(solution)/shard_map/ppermute | solution.py:16
  52.8 1.5 collective-permute-start.3
  55.1 2.6 %collective-permute-done.1 = bf16[1,2,16,4224]{3,2,1,0:T(8,128)(2,1)S(1)} collective-permute-done((bf16[1,2,16,4224]{3,2,1,0:T(8,128)(2,1)S(1)}, bf16[1,2,16,4224]{3,2,1,0:T(8,128)(2,1)S(1)}, u32[]{:S(2)}, u32[]{:S(2)}) %collective-permute-start.1) | collective-permute-done | bytes 270368 | tf_op jit(solution)/shard_map/ppermute | solution.py:16
  58.3 4.0 %collective-permute-done.3 = bf16[1,2,16,4224]{3,2,1,0:T(8,128)(2,1)S(1)} collective-permute-done((bf16[1,2,16,4224]{3,2,1,0:T(8,128)(2,1)S(1)}, bf16[1,2,16,4224]{3,2,1,0:T(8,128)(2,1)S(1)}, u32[]{:S(2)}, u32[]{:S(2)}) %collective-permute-start.3) | collective-permute-done | bytes 270368 | tf_op jit(solution)/shard_map/ppermute | solution.py:16
  62.2 1.5 collective-permute-start.2
  63.8 10.0 %collective-permute-done.15 = bf16[2,2,16,4224]{3,2,1,0:T(8,128)(2,1)S(1)} collective-permute-done((bf16[2,2,16,4224]{3,2,1,0:T(8,128)(2,1)S(1)}, bf16[2,2,16,4224]{3,2,1,0:T(8,128)(2,1)S(1)}, u32[]{:S(2)}, u32[]{:S(2)}) %collective-permute-start.15) | collective-permute-done | bytes 540704 | tf_op jit(solution)/shard_map/ppermute | solution.py:16
  74.7 8.0 %collective-permute-done.2 = bf16[2,2,16,4224]{3,2,1,0:T(8,128)(2,1)S(1)} collective-permute-done((bf16[2,2,16,4224]{3,2,1,0:T(8,128)(2,1)S(1)}, bf16[2,2,16,4224]{3,2,1,0:T(8,128)(2,1)S(1)}, u32[]{:S(2)}, u32[]{:S(2)}) %collective-permute-start.2) | collective-permute-done | bytes 540704 | tf_op jit(solution)/shard_map/ppermute | solution.py:16
  83.9 1.3 copy-done.4
  86.2 1.8 %fusion.11 = f32[256,768]{1,0:T(8,128)S(1)} fusion(bf16[256,4224]{1,0:T(8,128)(2,1)S(1)} %bitcast.114, bf16[4096,384]{0,1:T(8,128)(2,1)S(1)} %copy-done.2, bf16[4096,384]{0,1:T(8,128)(2,1)S(1)} %copy-done.4), kind=kOutput, calls=%fused_computation.20 | convolution fusion | flops 1623195648 | bytes 9175040 | tf_op jit(solution)/shard_map/dot_general | solution.py:144
  88.2 2.1 %fusion.7 = f32[256,768]{1,0:T(8,128)S(1)} fusion(bf16[256,4224]{1,0:T(8,128)(2,1)S(1)} %bitcast.111, bf16[4096,384]{0,1:T(8,128)(2,1)S(1)} %copy-done.2, bf16[4096,384]{0,1:T(8,128)(2,1)S(1)} %copy-done.4), kind=kOutput, calls=%fused_computation.16 | convolution fusion | flops 1623195648 | bytes 9175040 | tf_op jit(solution)/shard_map/dot_general | solution.py:144
  90.4 4.6 %fusion.9 = f32[256,768]{1,0:T(8,128)S(1)} fusion(bf16[4096,768]{0,1:T(8,128)(2,1)} %collective-permute-done.5, bf16[256,4224]{1,0:T(8,128)(2,1)S(1)} %bitcast.115), kind=kOutput, calls=%fused_computation.18 | convolution fusion | flops 1610612736 | bytes 9175040 | tf_op jit(solution)/shard_map/dot_general | solution.py:144
  95.1 3.8 %fusion.3 = bf16[256,4096]{1,0:T(8,128)(2,1)S(1)} fusion(bf16[384,4096]{1,0:T(8,128)(2,1)} %collective-permute-done.6, bf16[384,4096]{1,0:T(8,128)(2,1)S(1)} %fusion, f32[256]{0:T(256)S(1)} %get-tuple-element.5, bf16[256,384]{1,0:T(8,128)(2,1)S(1)} %fusion.23, bf16[256,384]{1,0:T(8,128)(2,1)S(1)} %fusion.24), kind=kOutput, calls=%fused_computation.10 | convolution fusion | flops 1626079232 | bytes 8782848 | tf_op jit(solution)/shard_map/dot_general | solution.py:149
  99.1 1.6 %collective-permute-start.7 = (bf16[2,2,16,4096]{3,2,1,0:T(8,128)(2,1)S(1)}, bf16[2,2,16,4096]{3,2,1,0:T(8,128)(2,1)S(1)}, u32[]{:S(2)}, u32[]{:S(2)}) collective-permute-start(bf16[2,2,16,4096]{3,2,1,0:T(8,128)(2,1)S(1)} %bitcast.122), channel_id=1, source_target_pairs={{0,16},{16,0},{8,24},{24,8},{1,17},{17,1},{9,25},{25,9},{2,18},{18... | collective-permute-start | bytes 1572872 | tf_op jit(solution)/shard_map/ppermute | solution.py:16
  101.3 4.6 %fusion.5 = f32[256,768]{1,0:T(8,128)S(1)} fusion(bf16[4096,768]{0,1:T(8,128)(2,1)} %collective-permute-done.5, bf16[256,4224]{1,0:T(8,128)(2,1)S(1)} %bitcast.112), kind=kOutput, calls=%fused_computation.14 | convolution fusion | flops 1610612736 | bytes 9175040 | tf_op jit(solution)/shard_map/dot_general | solution.py:144
  106.0 3.8 %fusion.4 = bf16[256,4096]{1,0:T(8,128)(2,1)S(1)} fusion(bf16[384,4096]{1,0:T(8,128)(2,1)} %collective-permute-done.6, bf16[384,4096]{1,0:T(8,128)(2,1)S(1)} %fusion, f32[256]{0:T(256)S(1)} %get-tuple-element.6, bf16[256,384]{1,0:T(8,128)(2,1)S(1)} %fusion.21, bf16[256,384]{1,0:T(8,128)(2,1)S(1)} %fusion.22), kind=kOutput, calls=%fused_computation.11 | convolution fusion | flops 1626079232 | bytes 8782848 | tf_op jit(solution)/shard_map/dot_general | solution.py:149
  110.0 1.6 collective-permute-start.20
  114.5 10.4 %collective-permute-done.20 = bf16[2,2,16,4096]{3,2,1,0:T(8,128)(2,1)S(1)} collective-permute-done((bf16[2,2,16,4096]{3,2,1,0:T(8,128)(2,1)S(1)}, bf16[2,2,16,4096]{3,2,1,0:T(8,128)(2,1)S(1)}, u32[]{:S(2)}, u32[]{:S(2)}) %collective-permute-start.20) | collective-permute-done | bytes 524320 | tf_op jit(solution)/shard_map/ppermute | solution.py:16
  125.8 1.6 collective-permute-start.19
  127.4 3.1 %collective-permute-done.8 = bf16[1,2,16,4096]{3,2,1,0:T(8,128)(2,1)S(1)} collective-permute-done((bf16[1,2,16,4096]{3,2,1,0:T(8,128)(2,1)S(1)}, bf16[1,2,16,4096]{3,2,1,0:T(8,128)(2,1)S(1)}, u32[]{:S(2)}, u32[]{:S(2)}) %collective-permute-start.8) | collective-permute-done | bytes 262176 | tf_op jit(solution)/shard_map/ppermute | solution.py:16
  133.9 2.0 %collective-permute-start.23 = (bf16[32,4096]{1,0:T(8,128)(2,1)S(1)}, bf16[32,4096]{1,0:T(8,128)(2,1)S(1)}, u32[]{:S(2)}, u32[]{:S(2)}) collective-permute-start(bf16[32,4096]{1,0:T(8,128)(2,1)S(1)} %get-tuple-element.18), channel_id=1, source_target_pairs={{0,6},{1,7},{2,4},{3,5},{4,2},{5,3},{6,0},{7,1},{8,14},{9,15},{10,... | collective-permute-start | bytes 786440 | tf_op jit(solution)/shard_map/ppermute | solution.py:106
  135.9 3.9 %collective-permute-done.11 = bf16[32,4096]{1,0:T(8,128)(2,1)S(1)} collective-permute-done((bf16[32,4096]{1,0:T(8,128)(2,1)S(1)}, bf16[32,4096]{1,0:T(8,128)(2,1)S(1)}, u32[]{:S(2)}, u32[]{:S(2)}) %collective-permute-start.11) | collective-permute-done | bytes 262176 | tf_op jit(solution)/shard_map/ppermute | solution.py:106
  139.8 10.9 %collective-permute-done.22 = bf16[32,4096]{1,0:T(8,128)(2,1)S(1)} collective-permute-done((bf16[32,4096]{1,0:T(8,128)(2,1)S(1)}, bf16[32,4096]{1,0:T(8,128)(2,1)S(1)}, u32[]{:S(2)}, u32[]{:S(2)}) %collective-permute-start.22) | collective-permute-done | bytes 262176 | tf_op jit(solution)/shard_map/ppermute | solution.py:106
  150.7 5.9 %collective-permute-done.23 = bf16[32,4096]{1,0:T(8,128)(2,1)S(1)} collective-permute-done((bf16[32,4096]{1,0:T(8,128)(2,1)S(1)}, bf16[32,4096]{1,0:T(8,128)(2,1)S(1)}, u32[]{:S(2)}, u32[]{:S(2)}) %collective-permute-start.23) | collective-permute-done | bytes 262176 | tf_op jit(solution)/shard_map/ppermute | solution.py:106
  (96 shorter events, 29.0 us)
Async XLA Ops:
  2.0 39.4 %collective-permute-start.12 = (bf16[32,4224]{1,0:T(8,128)(2,1)S(1)}, bf16[32,4224]{1,0:T(8,128)(2,1)}, u32[]{:S(2)}, u32[]{:S(2)}) collective-permute-start(bf16[32,4224]{1,0:T(8,128)(2,1)S(1)} %concatenate.49), channel_id=1, source_target_pairs={{0,4},{1,5},{2,6},{3,7},{4,0},{5,1},{6,2},{7,3},{8,12},{9,13},{10,... | collective-permute-start | bytes 811016 | tf_op jit(solution)/shard_map/ppermute | solution.py:106
  2.4 40.0 %collective-permute-start.13 = (bf16[32,4224]{1,0:T(8,128)(2,1)S(1)}, bf16[32,4224]{1,0:T(8,128)(2,1)}, u32[]{:S(2)}, u32[]{:S(2)}) collective-permute-start(bf16[32,4224]{1,0:T(8,128)(2,1)S(1)} %concatenate.49), channel_id=1, source_target_pairs={{0,6},{1,7},{2,4},{3,5},{4,2},{5,3},{6,0},{7,1},{8,14},{9,15},{10,... | collective-permute-start | bytes 811016 | tf_op jit(solution)/shard_map/ppermute | solution.py:106
  5.1 40.6 %collective-permute-start = (bf16[32,4224]{1,0:T(8,128)(2,1)S(1)}, bf16[32,4224]{1,0:T(8,128)(2,1)}, u32[]{:S(2)}, u32[]{:S(2)}) collective-permute-start(bf16[32,4224]{1,0:T(8,128)(2,1)S(1)} %concatenate.49), channel_id=1, source_target_pairs={{0,2},{1,3},{2,0},{3,1},{4,6},{5,7},{6,4},{7,5},{8,10},{9,11},{10,... | collective-permute-start | bytes 811016 | tf_op jit(solution)/shard_map/ppermute | solution.py:106
  16.6 1.9 %copy-start = (bf16[1,4096,384]{1,2,0:T(8,128)(2,1)S(1)}, bf16[1,4096,384]{1,2,0:T(8,128)(2,1)}, u32[]{:S(2)}) copy-start(bf16[1,4096,384]{1,2,0:T(8,128)(2,1)} %copy.21) | copy-start | bytes 9437188
  27.2 3.9 %copy-start.1 = (bf16[4096,384]{0,1:T(8,128)(2,1)}, bf16[4096,384]{0,1:T(8,128)(2,1)S(1)}, u32[]{:S(2)}) copy-start(bf16[4096,384]{0,1:T(8,128)(2,1)S(1)} %get-tuple-element.27) | copy-start | bytes 9437188
  27.2 4.7 %copy-start.3 = (bf16[4096,384]{0,1:T(8,128)(2,1)}, bf16[4096,384]{0,1:T(8,128)(2,1)S(1)}, u32[]{:S(2)}) copy-start(bf16[4096,384]{0,1:T(8,128)(2,1)S(1)} %get-tuple-element.28) | copy-start | bytes 9437188
  27.2 4.7 %copy-start.7 = (f32[1,3,32]{2,0,1:T(1,128)S(1)}, f32[1,3,32]{2,0,1:T(1,128)}, u32[]{:S(2)}) copy-start(f32[1,3,32]{2,0,1:T(1,128)} %param.17) | copy-start | bytes 1156
  31.9 58.5 %collective-permute-start.5 = (bf16[4096,768]{0,1:T(8,128)(2,1)}, bf16[4096,768]{0,1:T(8,128)(2,1)}, u32[]{:S(2)}, u32[]{:S(2)}) collective-permute-start(bf16[4096,768]{0,1:T(8,128)(2,1)} %pad_maximum_fusion), channel_id=1, source_target_pairs={{0,1},{1,0},{2,3},{3,2},{4,5},{5,4},{6,7},{7,6},{8,9},{9,8},{10,11... | collective-permute-start | bytes 18874376 | tf_op jit(solution)/shard_map/ppermute | solution.py:16
  31.9 1.9 %copy-start.5 = (bf16[1,384,4096]{2,1,0:T(8,128)(2,1)S(1)}, bf16[1,384,4096]{2,1,0:T(8,128)(2,1)}, u32[]{:S(2)}) copy-start(bf16[1,384,4096]{2,1,0:T(8,128)(2,1)} %param.14) | copy-start | bytes 9437188
  40.1 55.0 %collective-permute-start.6 = (bf16[384,4096]{1,0:T(8,128)(2,1)S(1)}, bf16[384,4096]{1,0:T(8,128)(2,1)}, u32[]{:S(2)}, u32[]{:S(2)}) collective-permute-start(bf16[384,4096]{1,0:T(8,128)(2,1)S(1)} %fusion), channel_id=1, source_target_pairs={{0,1},{1,0},{2,3},{3,2},{4,5},{5,4},{6,7},{7,6},{8,9},{9,8},{10,11... | collective-permute-start | bytes 9437192 | tf_op jit(solution)/shard_map/ppermute | solution.py:16
  43.4 9.4 %collective-permute-start.14 = (bf16[1,2,16,4224]{3,2,1,0:T(8,128)(2,1)S(1)}, bf16[1,2,16,4224]{3,2,1,0:T(8,128)(2,1)S(1)}, u32[]{:S(2)}, u32[]{:S(2)}) collective-permute-start(bf16[1,2,16,4224]{3,2,1,0:T(8,128)(2,1)S(1)} %maximum_bitcast_fusion.6), channel_id=1, source_target_pairs={{0,8},{8,0},{16,24},{24,16},{1,9},{9,1},{17,25},{25,17},{2,10},{10... | collective-permute-start | bytes 811016 | tf_op jit(solution)/shard_map/ppermute | solution.py:16
  44.1 10.4 %collective-permute-start.16 = (bf16[1,2,16,4224]{3,2,1,0:T(8,128)(2,1)S(1)}, bf16[1,2,16,4224]{3,2,1,0:T(8,128)(2,1)S(1)}, u32[]{:S(2)}, u32[]{:S(2)}) collective-permute-start(bf16[1,2,16,4224]{3,2,1,0:T(8,128)(2,1)S(1)} %maximum_bitcast_fusion.7), channel_id=1, source_target_pairs={{0,16},{16,0},{8,24},{24,8},{1,17},{17,1},{9,25},{25,9},{2,18},{18... | collective-permute-start | bytes 811016 | tf_op jit(solution)/shard_map/ppermute | solution.py:16
  47.6 10.1 %collective-permute-start.1 = (bf16[1,2,16,4224]{3,2,1,0:T(8,128)(2,1)S(1)}, bf16[1,2,16,4224]{3,2,1,0:T(8,128)(2,1)S(1)}, u32[]{:S(2)}, u32[]{:S(2)}) collective-permute-start(bf16[1,2,16,4224]{3,2,1,0:T(8,128)(2,1)S(1)} %maximum_bitcast_fusion.4), channel_id=1, source_target_pairs={{0,8},{8,0},{16,24},{24,16},{1,9},{9,1},{17,25},{25,17},{2,10},{10... | collective-permute-start | bytes 811016 | tf_op jit(solution)/shard_map/ppermute | solution.py:16
  52.8 9.4 %collective-permute-start.3 = (bf16[1,2,16,4224]{3,2,1,0:T(8,128)(2,1)S(1)}, bf16[1,2,16,4224]{3,2,1,0:T(8,128)(2,1)S(1)}, u32[]{:S(2)}, u32[]{:S(2)}) collective-permute-start(bf16[1,2,16,4224]{3,2,1,0:T(8,128)(2,1)S(1)} %maximum_bitcast_fusion.5), channel_id=1, source_target_pairs={{0,16},{16,0},{8,24},{24,8},{1,17},{17,1},{9,25},{25,9},{2,18},{18... | collective-permute-start | bytes 811016 | tf_op jit(solution)/shard_map/ppermute | solution.py:16
  54.4 19.4 %collective-permute-start.15 = (bf16[2,2,16,4224]{3,2,1,0:T(8,128)(2,1)S(1)}, bf16[2,2,16,4224]{3,2,1,0:T(8,128)(2,1)S(1)}, u32[]{:S(2)}, u32[]{:S(2)}) collective-permute-start(bf16[2,2,16,4224]{3,2,1,0:T(8,128)(2,1)S(1)} %pad_maximum_fusion.8), channel_id=1, source_target_pairs={{0,16},{16,0},{8,24},{24,8},{1,17},{17,1},{9,25},{25,9},{2,18},{18... | collective-permute-start | bytes 1622024 | tf_op jit(solution)/shard_map/ppermute | solution.py:16
  57.7 16.8 %collective-permute-start.17 = (bf16[2,2,16,4224]{3,2,1,0:T(8,128)(2,1)S(1)}, bf16[2,2,16,4224]{3,2,1,0:T(8,128)(2,1)S(1)}, u32[]{:S(2)}, u32[]{:S(2)}) collective-permute-start(bf16[2,2,16,4224]{3,2,1,0:T(8,128)(2,1)S(1)} %pad_maximum_fusion.9), channel_id=1, source_target_pairs={{0,8},{8,0},{16,24},{24,16},{1,9},{9,1},{17,25},{25,17},{2,10},{10... | collective-permute-start | bytes 1622024 | tf_op jit(solution)/shard_map/ppermute | solution.py:16
  62.2 20.4 %collective-permute-start.2 = (bf16[2,2,16,4224]{3,2,1,0:T(8,128)(2,1)S(1)}, bf16[2,2,16,4224]{3,2,1,0:T(8,128)(2,1)S(1)}, u32[]{:S(2)}, u32[]{:S(2)}) collective-permute-start(bf16[2,2,16,4224]{3,2,1,0:T(8,128)(2,1)S(1)} %pad_maximum_fusion.6), channel_id=1, source_target_pairs={{0,16},{16,0},{8,24},{24,8},{1,17},{17,1},{9,25},{25,9},{2,18},{18... | collective-permute-start | bytes 1622024 | tf_op jit(solution)/shard_map/ppermute | solution.py:16
  73.8 9.4 %collective-permute-start.4 = (bf16[2,2,16,4224]{3,2,1,0:T(8,128)(2,1)S(1)}, bf16[2,2,16,4224]{3,2,1,0:T(8,128)(2,1)S(1)}, u32[]{:S(2)}, u32[]{:S(2)}) collective-permute-start(bf16[2,2,16,4224]{3,2,1,0:T(8,128)(2,1)S(1)} %pad_maximum_fusion.7), channel_id=1, source_target_pairs={{0,8},{8,0},{16,24},{24,16},{1,9},{9,1},{17,25},{25,17},{2,10},{10... | collective-permute-start | bytes 1622024 | tf_op jit(solution)/shard_map/ppermute | solution.py:16
  83.3 1.9 %copy-start.4 = (bf16[4096,384]{0,1:T(8,128)(2,1)S(1)}, bf16[4096,384]{0,1:T(8,128)(2,1)}, u32[]{:S(2)}) copy-start(bf16[4096,384]{0,1:T(8,128)(2,1)} %copy-done.3) | copy-start | bytes 9437188
  83.6 2.7 %copy-start.2 = (bf16[4096,384]{0,1:T(8,128)(2,1)S(1)}, bf16[4096,384]{0,1:T(8,128)(2,1)}, u32[]{:S(2)}) copy-start(bf16[4096,384]{0,1:T(8,128)(2,1)} %copy-done.1) | copy-start | bytes 9437188
  99.1 12.9 %collective-permute-start.7 = (bf16[2,2,16,4096]{3,2,1,0:T(8,128)(2,1)S(1)}, bf16[2,2,16,4096]{3,2,1,0:T(8,128)(2,1)S(1)}, u32[]{:S(2)}, u32[]{:S(2)}) collective-permute-start(bf16[2,2,16,4096]{3,2,1,0:T(8,128)(2,1)S(1)} %bitcast.122), channel_id=1, source_target_pairs={{0,16},{16,0},{8,24},{24,8},{1,17},{17,1},{9,25},{25,9},{2,18},{18... | collective-permute-start | bytes 1572872 | tf_op jit(solution)/shard_map/ppermute | solution.py:16
  100.7 12.6 %collective-permute-start.9 = (bf16[2,2,16,4096]{3,2,1,0:T(8,128)(2,1)S(1)}, bf16[2,2,16,4096]{3,2,1,0:T(8,128)(2,1)S(1)}, u32[]{:S(2)}, u32[]{:S(2)}) collective-permute-start(bf16[2,2,16,4096]{3,2,1,0:T(8,128)(2,1)S(1)} %bitcast.120), channel_id=1, source_target_pairs={{0,8},{8,0},{16,24},{24,16},{1,9},{9,1},{17,25},{25,17},{2,10},{10... | collective-permute-start | bytes 1572872 | tf_op jit(solution)/shard_map/ppermute | solution.py:16
  110.0 14.9 %collective-permute-start.20 = (bf16[2,2,16,4096]{3,2,1,0:T(8,128)(2,1)S(1)}, bf16[2,2,16,4096]{3,2,1,0:T(8,128)(2,1)S(1)}, u32[]{:S(2)}, u32[]{:S(2)}) collective-permute-start(bf16[2,2,16,4096]{3,2,1,0:T(8,128)(2,1)S(1)} %bitcast.123), channel_id=1, source_target_pairs={{0,8},{8,0},{16,24},{24,16},{1,9},{9,1},{17,25},{25,17},{2,10},{10... | collective-permute-start | bytes 1572872 | tf_op jit(solution)/shard_map/ppermute | solution.py:16
  111.5 14.1 %collective-permute-start.18 = (bf16[2,2,16,4096]{3,2,1,0:T(8,128)(2,1)S(1)}, bf16[2,2,16,4096]{3,2,1,0:T(8,128)(2,1)S(1)}, u32[]{:S(2)}, u32[]{:S(2)}) collective-permute-start(bf16[2,2,16,4096]{3,2,1,0:T(8,128)(2,1)S(1)} %bitcast.121), channel_id=1, source_target_pairs={{0,16},{16,0},{8,24},{24,8},{1,17},{17,1},{9,25},{25,9},{2,18},{18... | collective-permute-start | bytes 1572872 | tf_op jit(solution)/shard_map/ppermute | solution.py:16
  112.2 18.3 %collective-permute-start.8 = (bf16[1,2,16,4096]{3,2,1,0:T(8,128)(2,1)S(1)}, bf16[1,2,16,4096]{3,2,1,0:T(8,128)(2,1)S(1)}, u32[]{:S(2)}, u32[]{:S(2)}) collective-permute-start(bf16[1,2,16,4096]{3,2,1,0:T(8,128)(2,1)S(1)} %split.79), channel_id=1, source_target_pairs={{0,8},{8,0},{16,24},{24,16},{1,9},{9,1},{17,25},{25,17},{2,10},{10... | collective-permute-start | bytes 786440 | tf_op jit(solution)/shard_map/ppermute | solution.py:16
  113.5 17.1 %collective-permute-start.10 = (bf16[1,2,16,4096]{3,2,1,0:T(8,128)(2,1)S(1)}, bf16[1,2,16,4096]{3,2,1,0:T(8,128)(2,1)S(1)}, u32[]{:S(2)}, u32[]{:S(2)}) collective-permute-start(bf16[1,2,16,4096]{3,2,1,0:T(8,128)(2,1)S(1)} %split.83), channel_id=1, source_target_pairs={{0,16},{16,0},{8,24},{24,8},{1,17},{17,1},{9,25},{25,9},{2,18},{18... | collective-permute-start | bytes 786440 | tf_op jit(solution)/shard_map/ppermute | solution.py:16
  125.0 7.6 %collective-permute-start.21 = (bf16[1,2,16,4096]{3,2,1,0:T(8,128)(2,1)S(1)}, bf16[1,2,16,4096]{3,2,1,0:T(8,128)(2,1)S(1)}, u32[]{:S(2)}, u32[]{:S(2)}) collective-permute-start(bf16[1,2,16,4096]{3,2,1,0:T(8,128)(2,1)S(1)} %split.91), channel_id=1, source_target_pairs={{0,16},{16,0},{8,24},{24,8},{1,17},{17,1},{9,25},{25,9},{2,18},{18... | collective-permute-start | bytes 786440 | tf_op jit(solution)/shard_map/ppermute | solution.py:16
  125.8 30.9 %copy-start.6 = (bf16[32,4096]{1,0:T(8,128)(2,1)S(1)}, bf16[32,4096]{1,0:T(8,128)(2,1)}, u32[]{:S(2)}) copy-start(bf16[32,4096]{1,0:T(8,128)(2,1)} %param.9) | copy-start | bytes 786436
  125.8 7.8 %collective-permute-start.19 = (bf16[1,2,16,4096]{3,2,1,0:T(8,128)(2,1)S(1)}, bf16[1,2,16,4096]{3,2,1,0:T(8,128)(2,1)S(1)}, u32[]{:S(2)}, u32[]{:S(2)}) collective-permute-start(bf16[1,2,16,4096]{3,2,1,0:T(8,128)(2,1)S(1)} %split.87), channel_id=1, source_target_pairs={{0,8},{8,0},{16,24},{24,16},{1,9},{9,1},{17,25},{25,17},{2,10},{10... | collective-permute-start | bytes 786440 | tf_op jit(solution)/shard_map/ppermute | solution.py:16
  130.7 9.2 %collective-permute-start.11 = (bf16[32,4096]{1,0:T(8,128)(2,1)S(1)}, bf16[32,4096]{1,0:T(8,128)(2,1)S(1)}, u32[]{:S(2)}, u32[]{:S(2)}) collective-permute-start(bf16[32,4096]{1,0:T(8,128)(2,1)S(1)} %fusion.40), channel_id=1, source_target_pairs={{0,2},{1,3},{2,0},{3,1},{4,6},{5,7},{6,4},{7,5},{8,10},{9,11},{10,... | collective-permute-start | bytes 786440 | tf_op jit(solution)/shard_map/ppermute | solution.py:106
  133.7 17.0 %collective-permute-start.22 = (bf16[32,4096]{1,0:T(8,128)(2,1)S(1)}, bf16[32,4096]{1,0:T(8,128)(2,1)S(1)}, u32[]{:S(2)}, u32[]{:S(2)}) collective-permute-start(bf16[32,4096]{1,0:T(8,128)(2,1)S(1)} %get-tuple-element.17), channel_id=1, source_target_pairs={{0,4},{1,5},{2,6},{3,7},{4,0},{5,1},{6,2},{7,3},{8,12},{9,13},{10,... | collective-permute-start | bytes 786440 | tf_op jit(solution)/shard_map/ppermute | solution.py:106
  133.9 22.7 %collective-permute-start.23 = (bf16[32,4096]{1,0:T(8,128)(2,1)S(1)}, bf16[32,4096]{1,0:T(8,128)(2,1)S(1)}, u32[]{:S(2)}, u32[]{:S(2)}) collective-permute-start(bf16[32,4096]{1,0:T(8,128)(2,1)S(1)} %get-tuple-element.18), channel_id=1, source_target_pairs={{0,6},{1,7},{2,4},{3,5},{4,2},{5,3},{6,0},{7,1},{8,14},{9,15},{10,... | collective-permute-start | bytes 786440 | tf_op jit(solution)/shard_map/ppermute | solution.py:106

commit v3 on v2

--- a/solution.py
+++ b/solution.py
@@ -1,6 +1,10 @@
+import functools
+
 import jax
 import jax.numpy as jnp
 from jax import lax
+from jax.experimental import pallas as pl
+from jax.experimental.pallas import tpu as pltpu
 from jax.sharding import PartitionSpec as P
 
 BLOCK = 128
@@ -101,6 +105,73 @@
     return block
 
 
+def scaled(block, scale):
+    return (block.astype(jnp.float32) * scale).astype(jnp.bfloat16)
+
+
+def in_kernel(block_cols, scales, gate_ref, up_ref, out_ref):
+    strip = gate_ref.shape[0] // BLOCK
+    first = pl.program_id(0) * strip
+    up_at = pl.num_programs(0) * strip * block_cols
+    for row in range(strip):
+        rows = slice(row * BLOCK, (row + 1) * BLOCK)
+        for col in range(block_cols):
+            cols = slice(col * BLOCK, (col + 1) * BLOCK)
+            place = (first + row) * block_cols + col
+            out_ref[rows, cols] = scaled(gate_ref[rows, cols], scales[place])
+            cols_up = slice((block_cols + col) * BLOCK, (block_cols + col + 1) * BLOCK)
+            out_ref[rows, cols_up] = scaled(up_ref[rows, cols], scales[up_at + place])
+
+
+def dequantize_in(gate, up, scales):
+    rows, cols = gate.shape
+    strip = min(rows, 4 * BLOCK)
+    block = pl.BlockSpec((strip, cols), lambda i: (i, 0))
+    return pl.pallas_call(
+        functools.partial(in_kernel, cols // BLOCK),
+        grid=(rows // strip,),
+        in_specs=[pl.BlockSpec(memory_space=pltpu.SMEM), block, block],
+        out_specs=pl.BlockSpec((strip, 2 * cols), lambda i: (i, 0)),
+        out_shape=jax.ShapeDtypeStruct((rows, 2 * cols), jnp.bfloat16),
+        cost_estimate=pl.CostEstimate(
+            flops=2 * rows * cols, bytes_accessed=8 * rows * cols, transcendentals=0
+        ),
+        name="dequantize_in",
+    )(scales, gate, up)
+
+
+def down_kernel(at, block_cols, scales_own, scales_other, own_ref, other_ref, out_ref):
+    strip = own_ref.shape[1] // BLOCK
+    block_rows = own_ref.shape[0] // BLOCK
+    first = pl.program_id(0) * strip
+    for half, (scales, ref) in enumerate(((scales_own, own_ref), (scales_other, other_ref))):
+        for row in range(block_rows):
+            rows = slice(row * BLOCK, (row + 1) * BLOCK)
+            out_row = (half * block_rows + row) * BLOCK
+            for col in range(strip):
+                cols = slice(col * BLOCK, (col + 1) * BLOCK)
+                scale = scales[at + row * block_cols + first + col]
+                out_ref[out_row : out_row + BLOCK, cols] = scaled(ref[rows, cols], scale)
+
+
+def dequantize_down(own, other, scales_own, scales_other, at):
+    rows, cols = own.shape
+    strip = min(cols, 4 * BLOCK)
+    block = pl.BlockSpec((rows, strip), lambda i: (0, i))
+    smem = pl.BlockSpec(memory_space=pltpu.SMEM)
+    return pl.pallas_call(
+        functools.partial(down_kernel, at, cols // BLOCK),
+        grid=(cols // strip,),
+        in_specs=[smem, smem, block, block],
+        out_specs=pl.BlockSpec((2 * rows, strip), lambda i: (0, i)),
+        out_shape=jax.ShapeDtypeStruct((2 * rows, cols), jnp.bfloat16),
+        cost_estimate=pl.CostEstimate(
+            flops=2 * rows * cols, bytes_accessed=8 * rows * cols, transcendentals=0
+        ),
+        name="dequantize_down",
+    )(scales_own, scales_other, own, other)
+
+
 def across_chips(block, far):
     count = lax.axis_size("expert")
     return lax.ppermute(block, "expert", [(low, low ^ 2 * far) for low in range(count)])
@@ -112,7 +183,6 @@
     pair_count = lax.axis_size("expert") // 2
     expert_count = group_count * pair_count
     own_expert = lax.axis_index("dp") * pair_count + lax.axis_index("expert") // 2
-    half = token_count // 2
     bits = list(range(group_count.bit_length() - 1))
     orders = (bits, bits[::-1])
 
@@ -124,14 +194,15 @@
     pad = jnp.zeros((token_count, extra - 2 * expert_count), jnp.bfloat16)
     payload = jnp.concatenate([tokens, high, low, pad], axis=1)
 
-    w_gate = dequantize(gate_q[0], gate_scale[0])
-    w_up = dequantize(up_q[0], up_scale[0])
-    w_down = dequantize(down_q[0], down_scale[0])
-    in_own = jnp.concatenate([w_gate, w_up], axis=1)
-    in_other = from_partner(in_own, "expert", 0)
-    down_other = from_partner(w_down, "expert", 0)
-    down_both = jnp.concatenate([w_down, down_other], axis=0)
-    hidden_half = w_gate.shape[1]
+    quant = [gate_q[0], up_q[0], down_q[0]]
+    hidden_half = gate_q.shape[2]
+    scales = jnp.concatenate([s.reshape(-1) for s in (gate_scale, up_scale, down_scale)])
+    scales_other = from_partner(scales, "expert", 0)
+    gate_other, up_other, down_other = [from_partner(q, "expert", 0) for q in quant]
+    in_own = dequantize_in(quant[0], quant[1], scales)
+    in_other = dequantize_in(gate_other, up_other, scales_other)
+    down_at = gate_scale.size + up_scale.size
+    down_both = dequantize_down(quant[2], down_other, scales, scales_other, down_at)
 
     def ffn(rows):
         inputs = rows[:, :model_width]
@@ -149,27 +220,18 @@
         value = jnp.dot(hidden, down_both, preferred_element_type=jnp.float32)
         return (value * row_weight[:, None]).astype(jnp.bfloat16)
 
-    from_far = {far: across_chips(payload, far) for far in range(1, pair_count)}
-    from_far[0] = payload
+    outs = {}
+    for far in range(pair_count):
+        block = payload if far == 0 else across_chips(payload, far)
+        every = gather_groups(block[None], orders[far % 2])
+        outs[far] = ffn(every.reshape(-1, every.shape[-1]))
     total = tokens.astype(jnp.float32)
-    step = 2
-    for first in range(0, pair_count, step):
-        fars = range(first, first + step)
-        gathered = []
-        for place, order in enumerate(orders):
-            rows = slice(place * half, (place + 1) * half)
-            block = jnp.stack([from_far[far][rows] for far in fars])[None]
-            gathered.append(gather_groups(block, order))
-        every = jnp.stack(gathered)
-        out = ffn(every.reshape(-1, every.shape[-1]))
-        out = out.reshape(every.shape[:-1] + (model_width,))
-        sums = [sum_groups(out[place], order)[0] for place, order in enumerate(orders)]
-        sums = jnp.concatenate(sums, axis=1)
-        for place, far in enumerate(fars):
-            block = sums[place]
-            if far > 0:
-                block = across_chips(block, far)
-            total = total + block.astype(jnp.float32)
+    for far in [*range(2, pair_count), 1, 0][-pair_count:]:
+        out = outs[far].reshape(group_count, token_count, model_width)
+        block = sum_groups(out, orders[far % 2])[0]
+        if far > 0:
+            block = across_chips(block, far)
+        total = total + block.astype(jnp.float32)
     return total.astype(jnp.bfloat16)
 
 

time: 158 us -> 178 us (1.13)
  the two profiles are of different devices: /device:TPU:18 before, /device:TPU:0 now
where the time goes in v3:
time: 178 us; the launch traced here: 177 us
  waiting for transfers between devices  77.6 us (44%)
  starting transfers between devices  44.5 us (25%)
  Pallas kernels  24.7 us (14%)
  matrix products  18.2 us (10%)
  other arithmetic  6.38 us (4%)
  local copies, waits for them, and re-layouts  5.46 us (3%)
    ppermute x20, waiting for transfers between devices, from_partner(): return lax.ppermute(block, axis, route)  59.5 us
    ppermute x6, starting transfers between devices, across_chips(): lax.ppermute(block, 'expert', [(low, low ^ 2 * far) for low in range(coun...  23.7 us
    ppermute x20, starting transfers between devices, from_partner(): return lax.ppermute(block, axis, route)  20.7 us
    ppermute x6, waiting for transfers between devices, across_chips(): lax.ppermute(block, 'expert', [(low, low ^ 2 * far) for low in range(coun...  18.1 us
    pallas_call x2, Pallas kernels, dequantize_in(): pl.pallas_call(functools.partial(in_kernel, cols // BLOCK), grid=(rows //...  16.4 us
    dot_general x8, matrix products, ffn(): parts = jnp.dot(inputs, w_in, preferred_element_type=jnp.float32)  11.2 us
    pallas_call x1, Pallas kernels, dequantize_down(): pl.pallas_call(functools.partial(down_kernel, at, cols // BLOCK), grid=(c...  8.35 us
    dot_general x4, matrix products, ffn(): value = jnp.dot(hidden, down_both, preferred_element_type=jnp.float32)  7.02 us
  transfers between devices with their start and end apart: 26, of which 13 were waited for; matrix products, arithmetic and copies ran while one was open for 12% of the time, Pallas kernels for 9%

profile of v3, /device:TPU:0, one launch (start us, length us, event | category | flops | bytes accessed | tf_op | source)
XLA Modules:
  0.0 177.4 jit_solution(6650026872857633067)
XLA Ops:
  2.0 3.0 %collective-permute-start.22 = (bf16[1,32,4224]{2,1,0:T(8,128)(2,1)S(1)}, bf16[1,32,4224]{2,1,0:T(8,128)(2,1)S(1)}, u32[]{:S(2)}, u32[]{:S(2)}) collective-permute-start(bf16[1,32,4224]{2,1,0:T(8,128)(2,1)S(1)} %bitcast.58), channel_id=1, source_target_pairs={{0,8},{8,0},{16,24},{24,16},{1,9},{9,1},{17,25},{25,17},{2,10},{10... | collective-permute-start | bytes 811016 | tf_op jit(solution)/shard_map/ppermute | solution.py:20
  5.0 2.6 %collective-permute-start = (bf16[32,4224]{1,0:T(8,128)(2,1)S(1)}, bf16[32,4224]{1,0:T(8,128)(2,1)S(1)}, u32[]{:S(2)}, u32[]{:S(2)}) collective-permute-start(bf16[32,4224]{1,0:T(8,128)(2,1)S(1)} %concatenate.46), channel_id=1, source_target_pairs={{0,4},{1,5},{2,6},{3,7},{4,0},{5,1},{6,2},{7,3},{8,12},{9,13},{10,... | collective-permute-start | bytes 811016 | tf_op jit(solution)/shard_map/ppermute | solution.py:177
  7.6 1.6 collective-permute-start.16
  12.5 8.2 %dequantize_in.2 = bf16[4096,768]{1,0:T(8,128)(2,1)} custom-call(f32[288]{0:T(512)} %copy-done.11, bf16[4096,384]{1,0:T(8,128)(2,1)} %bitcast.2.gate_ref, bf16[4096,384]{1,0:T(8,128)(2,1)} %bitcast.3.up_ref), custom_call_target="tpu_custom_call" | custom-call | flops 3145728 | bytes 12582912 | tf_op jit(solution)/shard_map/dequantize_in/pallas_call | solution.py:130
  20.8 5.8 %collective-permute-done = bf16[32,4224]{1,0:T(8,128)(2,1)S(1)} collective-permute-done((bf16[32,4224]{1,0:T(8,128)(2,1)S(1)}, bf16[32,4224]{1,0:T(8,128)(2,1)S(1)}, u32[]{:S(2)}, u32[]{:S(2)}) %collective-permute-start) | collective-permute-done | bytes 270368 | tf_op jit(solution)/shard_map/ppermute | solution.py:177
  26.8 6.3 %collective-permute-done.1 = bf16[1,32,4224]{2,1,0:T(8,128)(2,1)S(1)} collective-permute-done((bf16[1,32,4224]{2,1,0:T(8,128)(2,1)S(1)}, bf16[1,32,4224]{2,1,0:T(8,128)(2,1)S(1)}, u32[]{:S(2)}, u32[]{:S(2)}) %collective-permute-start.1) | collective-permute-done | bytes 270368 | tf_op jit(solution)/shard_map/ppermute | solution.py:20
  33.1 1.5 collective-permute-start.11
  34.7 6.5 %collective-permute-done.11 = bf16[1,32,4224]{2,1,0:T(8,128)(2,1)S(1)} collective-permute-done((bf16[1,32,4224]{2,1,0:T(8,128)(2,1)S(1)}, bf16[1,32,4224]{2,1,0:T(8,128)(2,1)S(1)}, u32[]{:S(2)}, u32[]{:S(2)}) %collective-permute-start.11) | collective-permute-done | bytes 270368 | tf_op jit(solution)/shard_map/ppermute | solution.py:20
  41.3 2.5 %collective-permute-start.17 = (bf16[1,32,4224]{2,1,0:T(8,128)(2,1)S(1)}, bf16[1,32,4224]{2,1,0:T(8,128)(2,1)S(1)}, u32[]{:S(2)}, u32[]{:S(2)}) collective-permute-start(bf16[1,32,4224]{2,1,0:T(8,128)(2,1)S(1)} %bitcast.65), channel_id=1, source_target_pairs={{0,16},{16,0},{8,24},{24,8},{1,17},{17,1},{9,25},{25,9},{2,18},{18... | collective-permute-start | bytes 811016 | tf_op jit(solution)/shard_map/ppermute | solution.py:20
  43.8 7.2 %collective-permute-done.17 = bf16[1,32,4224]{2,1,0:T(8,128)(2,1)S(1)} collective-permute-done((bf16[1,32,4224]{2,1,0:T(8,128)(2,1)S(1)}, bf16[1,32,4224]{2,1,0:T(8,128)(2,1)S(1)}, u32[]{:S(2)}, u32[]{:S(2)}) %collective-permute-start.17) | collective-permute-done | bytes 270368 | tf_op jit(solution)/shard_map/ppermute | solution.py:20
  51.0 2.1 %collective-permute-start.23 = (bf16[2,32,4224]{2,1,0:T(8,128)(2,1)S(1)}, bf16[2,32,4224]{2,1,0:T(8,128)(2,1)S(1)}, u32[]{:S(2)}, u32[]{:S(2)}) collective-permute-start(bf16[2,32,4224]{2,1,0:T(8,128)(2,1)S(1)} %pad_maximum_fusion.7), channel_id=1, source_target_pairs={{0,16},{16,0},{8,24},{24,8},{1,17},{17,1},{9,25},{25,9},{2,18},{18... | collective-permute-start | bytes 1622024 | tf_op jit(solution)/shard_map/ppermute | solution.py:20
  53.2 7.3 %collective-permute-done.23 = bf16[2,32,4224]{2,1,0:T(8,128)(2,1)S(1)} collective-permute-done((bf16[2,32,4224]{2,1,0:T(8,128)(2,1)S(1)}, bf16[2,32,4224]{2,1,0:T(8,128)(2,1)S(1)}, u32[]{:S(2)}, u32[]{:S(2)}) %collective-permute-start.23) | collective-permute-done | bytes 540704 | tf_op jit(solution)/shard_map/ppermute | solution.py:20
  63.0 6.7 %collective-permute-done.12 = bf16[2,32,4224]{2,1,0:T(8,128)(2,1)S(1)} collective-permute-done((bf16[2,32,4224]{2,1,0:T(8,128)(2,1)S(1)}, bf16[2,32,4224]{2,1,0:T(8,128)(2,1)S(1)}, u32[]{:S(2)}, u32[]{:S(2)}) %collective-permute-start.12) | collective-permute-done | bytes 540704 | tf_op jit(solution)/shard_map/ppermute | solution.py:20
  69.8 2.0 %collective-permute-start.2 = (bf16[2,32,4224]{2,1,0:T(8,128)(2,1)S(1)}, bf16[2,32,4224]{2,1,0:T(8,128)(2,1)S(1)}, u32[]{:S(2)}, u32[]{:S(2)}) collective-permute-start(bf16[2,32,4224]{2,1,0:T(8,128)(2,1)S(1)} %pad_maximum_fusion.4), channel_id=1, source_target_pairs={{0,16},{16,0},{8,24},{24,8},{1,17},{17,1},{9,25},{25,9},{2,18},{18... | collective-permute-start | bytes 1622024 | tf_op jit(solution)/shard_map/ppermute | solution.py:20
  71.9 1.1 fusion.18
  73.0 6.1 %collective-permute-done.2 = bf16[2,32,4224]{2,1,0:T(8,128)(2,1)S(1)} collective-permute-done((bf16[2,32,4224]{2,1,0:T(8,128)(2,1)S(1)}, bf16[2,32,4224]{2,1,0:T(8,128)(2,1)S(1)}, u32[]{:S(2)}, u32[]{:S(2)}) %collective-permute-start.2) | collective-permute-done | bytes 540704 | tf_op jit(solution)/shard_map/ppermute | solution.py:20
  80.0 1.1 fusion.22
  82.4 6.0 %collective-permute-done.18 = bf16[2,32,4224]{2,1,0:T(8,128)(2,1)S(1)} collective-permute-done((bf16[2,32,4224]{2,1,0:T(8,128)(2,1)S(1)}, bf16[2,32,4224]{2,1,0:T(8,128)(2,1)S(1)}, u32[]{:S(2)}, u32[]{:S(2)}) %collective-permute-start.18) | collective-permute-done | bytes 540704 | tf_op jit(solution)/shard_map/ppermute | solution.py:20
  90.4 8.2 %dequantize_in.3 = bf16[4096,768]{1,0:T(8,128)(2,1)} custom-call(f32[288]{0:T(512)} %copy-done.12, bf16[4096,384]{1,0:T(8,128)(2,1)} %collective-permute-done.4.gate_ref, bf16[4096,384]{1,0:T(8,128)(2,1)} %collective-permute-done.5.up_ref), custom_call_target="tpu_custom_call" | custom-call | flops 3145728 | bytes 12582912 | tf_op jit(solution)/shard_map/dequantize_in/pallas_call | solution.py:130
  98.6 3.9 %fusion.8 = f32[128,768]{1,0:T(8,128)S(1)} fusion(bf16[4096,768]{1,0:T(8,128)(2,1)} %dequantize_in.3, bf16[128,4224]{1,0:T(8,128)(2,1)S(1)} %bitcast.48), kind=kOutput, calls=%fused_computation.20 | convolution fusion | flops 805306368 | bytes 7733248 | tf_op jit(solution)/shard_map/dot_general | solution.py:215
  106.8 8.4 %dequantize_down.1 = bf16[768,4096]{1,0:T(8,128)(2,1)} custom-call(f32[288]{0:T(512)} %copy-done.11, f32[288]{0:T(512)} %copy-done.12, bf16[384,4096]{1,0:T(8,128)(2,1)} %bitcast.4.own_ref, bf16[384,4096]{1,0:T(8,128)(2,1)} %collective-permute-done.6.other_ref), custom_call_target="tpu_custom_call" | custom-call | flops 3145728 | bytes 12582912 | tf_op jit(solution)/shard_map/dequantize_down/pallas_call | solution.py:162
  115.2 3.9 %fusion.3 = bf16[128,4096]{1,0:T(8,128)(2,1)S(1)} fusion(bf16[768,4096]{1,0:T(8,128)(2,1)} %dequantize_down.1, f32[128]{0:T(128)S(1)} %get-tuple-element.5, bf16[128,384]{1,0:T(8,128)(2,1)S(1)} %fusion.29, bf16[128,384]{1,0:T(8,128)(2,1)S(1)} %copy-done.9), kind=kOutput, calls=%fused_computation.7 | convolution fusion | flops 806748160 | bytes 7537152 | tf_op jit(solution)/shard_map/dot_general | solution.py:220
  119.2 2.1 %collective-permute-start.24 = (bf16[2,32,4096]{2,1,0:T(8,128)(2,1)S(1)}, bf16[2,32,4096]{2,1,0:T(8,128)(2,1)S(1)}, u32[]{:S(2)}, u32[]{:S(2)}) collective-permute-start(bf16[2,32,4096]{2,1,0:T(8,128)(2,1)S(1)} %bitcast.77), channel_id=1, source_target_pairs={{0,16},{16,0},{8,24},{24,8},{1,17},{17,1},{9,25},{25,9},{2,18},{18... | collective-permute-start | bytes 1572872 | tf_op jit(solution)/shard_map/ppermute | solution.py:20
  124.4 1.4 collective-permute-start.13
  127.4 6.7 %collective-permute-done.24 = bf16[2,32,4096]{2,1,0:T(8,128)(2,1)S(1)} collective-permute-done((bf16[2,32,4096]{2,1,0:T(8,128)(2,1)S(1)}, bf16[2,32,4096]{2,1,0:T(8,128)(2,1)S(1)}, u32[]{:S(2)}, u32[]{:S(2)}) %collective-permute-start.24) | collective-permute-done | bytes 524320 | tf_op jit(solution)/shard_map/ppermute | solution.py:20
  135.1 1.9 %collective-permute-done.19 = bf16[2,32,4096]{2,1,0:T(8,128)(2,1)S(1)} collective-permute-done((bf16[2,32,4096]{2,1,0:T(8,128)(2,1)S(1)}, bf16[2,32,4096]{2,1,0:T(8,128)(2,1)S(1)}, u32[]{:S(2)}, u32[]{:S(2)}) %collective-permute-start.19) | collective-permute-done | bytes 524320 | tf_op jit(solution)/shard_map/ppermute | solution.py:20
  138.0 4.6 %collective-permute-done.13 = bf16[2,32,4096]{2,1,0:T(8,128)(2,1)S(1)} collective-permute-done((bf16[2,32,4096]{2,1,0:T(8,128)(2,1)S(1)}, bf16[2,32,4096]{2,1,0:T(8,128)(2,1)S(1)}, u32[]{:S(2)}, u32[]{:S(2)}) %collective-permute-start.13) | collective-permute-done | bytes 524320 | tf_op jit(solution)/shard_map/ppermute | solution.py:20
  144.6 11.7 %collective-permute-start.21 = (bf16[32,4096]{1,0:T(8,128)(2,1)S(1)}, bf16[32,4096]{1,0:T(8,128)(2,1)S(1)}, u32[]{:S(2)}, u32[]{:S(2)}) collective-permute-start(bf16[32,4096]{1,0:T(8,128)(2,1)S(1)} %fusion.27), channel_id=1, source_target_pairs={{0,2},{1,3},{2,0},{3,1},{4,6},{5,7},{6,4},{7,5},{8,10},{9,11},{10,... | collective-permute-start | bytes 786440 | tf_op jit(solution)/shard_map/ppermute | solution.py:177
  156.4 3.5 %collective-permute-start.15 = (bf16[32,4096]{1,0:T(8,128)(2,1)S(1)}, bf16[32,4096]{1,0:T(8,128)(2,1)S(1)}, u32[]{:S(2)}, u32[]{:S(2)}) collective-permute-start(bf16[32,4096]{1,0:T(8,128)(2,1)S(1)} %fusion.26), channel_id=1, source_target_pairs={{0,6},{1,7},{2,4},{3,5},{4,2},{5,3},{6,0},{7,1},{8,14},{9,15},{10,... | collective-permute-start | bytes 786440 | tf_op jit(solution)/shard_map/ppermute | solution.py:177
  159.9 4.2 %collective-permute-start.9 = (bf16[32,4096]{1,0:T(8,128)(2,1)S(1)}, bf16[32,4096]{1,0:T(8,128)(2,1)S(1)}, u32[]{:S(2)}, u32[]{:S(2)}) collective-permute-start(bf16[32,4096]{1,0:T(8,128)(2,1)S(1)} %fusion.25), channel_id=1, source_target_pairs={{0,4},{1,5},{2,6},{3,7},{4,0},{5,1},{6,2},{7,3},{8,12},{9,13},{10,... | collective-permute-start | bytes 786440 | tf_op jit(solution)/shard_map/ppermute | solution.py:177
  164.1 2.9 %collective-permute-done.15 = bf16[32,4096]{1,0:T(8,128)(2,1)S(1)} collective-permute-done((bf16[32,4096]{1,0:T(8,128)(2,1)S(1)}, bf16[32,4096]{1,0:T(8,128)(2,1)S(1)}, u32[]{:S(2)}, u32[]{:S(2)}) %collective-permute-start.15) | collective-permute-done | bytes 262176 | tf_op jit(solution)/shard_map/ppermute | solution.py:177
  167.0 9.5 %collective-permute-done.9 = bf16[32,4096]{1,0:T(8,128)(2,1)S(1)} collective-permute-done((bf16[32,4096]{1,0:T(8,128)(2,1)S(1)}, bf16[32,4096]{1,0:T(8,128)(2,1)S(1)}, u32[]{:S(2)}, u32[]{:S(2)}) %collective-permute-start.9) | collective-permute-done | bytes 262176 | tf_op jit(solution)/shard_map/ppermute | solution.py:177
  (108 shorter events, 26.5 us)
Async XLA Ops:
  2.0 18.8 %collective-permute-start.22 = (bf16[1,32,4224]{2,1,0:T(8,128)(2,1)S(1)}, bf16[1,32,4224]{2,1,0:T(8,128)(2,1)S(1)}, u32[]{:S(2)}, u32[]{:S(2)}) collective-permute-start(bf16[1,32,4224]{2,1,0:T(8,128)(2,1)S(1)} %bitcast.58), channel_id=1, source_target_pairs={{0,8},{8,0},{16,24},{24,16},{1,9},{9,1},{17,25},{25,17},{2,10},{10... | collective-permute-start | bytes 811016 | tf_op jit(solution)/shard_map/ppermute | solution.py:20
  5.0 21.6 %collective-permute-start = (bf16[32,4224]{1,0:T(8,128)(2,1)S(1)}, bf16[32,4224]{1,0:T(8,128)(2,1)S(1)}, u32[]{:S(2)}, u32[]{:S(2)}) collective-permute-start(bf16[32,4224]{1,0:T(8,128)(2,1)S(1)} %concatenate.46), channel_id=1, source_target_pairs={{0,4},{1,5},{2,6},{3,7},{4,0},{5,1},{6,2},{7,3},{8,12},{9,13},{10,... | collective-permute-start | bytes 811016 | tf_op jit(solution)/shard_map/ppermute | solution.py:177
  7.6 27.1 %collective-permute-start.16 = (bf16[32,4224]{1,0:T(8,128)(2,1)S(1)}, bf16[32,4224]{1,0:T(8,128)(2,1)S(1)}, u32[]{:S(2)}, u32[]{:S(2)}) collective-permute-start(bf16[32,4224]{1,0:T(8,128)(2,1)S(1)} %concatenate.46), channel_id=1, source_target_pairs={{0,2},{1,3},{2,0},{3,1},{4,6},{5,7},{6,4},{7,5},{8,10},{9,11},{10,... | collective-permute-start | bytes 811016 | tf_op jit(solution)/shard_map/ppermute | solution.py:177
  9.1 17.5 %collective-permute-start.10 = (bf16[32,4224]{1,0:T(8,128)(2,1)S(1)}, bf16[32,4224]{1,0:T(8,128)(2,1)S(1)}, u32[]{:S(2)}, u32[]{:S(2)}) collective-permute-start(bf16[32,4224]{1,0:T(8,128)(2,1)S(1)} %concatenate.46), channel_id=1, source_target_pairs={{0,6},{1,7},{2,4},{3,5},{4,2},{5,3},{6,0},{7,1},{8,14},{9,15},{10,... | collective-permute-start | bytes 811016 | tf_op jit(solution)/shard_map/ppermute | solution.py:177
  12.0 77.9 %collective-permute-start.3 = (f32[288]{0:T(512)S(1)}, f32[288]{0:T(512)S(1)}, u32[]{:S(2)}, u32[]{:S(2)}) collective-permute-start(f32[288]{0:T(512)S(1)} %pad_maximum_fusion.8.scales.scales_own), channel_id=1, source_target_pairs={{0,1},{1,0},{2,3},{3,2},{4,5},{5,4},{6,7},{7,6},{8,9},{9,8},{10,11... | collective-permute-start | bytes 3464 | tf_op jit(solution)/shard_map/ppermute | solution.py:20
  20.7 69.1 %collective-permute-start.4 = (bf16[4096,384]{1,0:T(8,128)(2,1)}, bf16[4096,384]{1,0:T(8,128)(2,1)}, u32[]{:S(2)}, u32[]{:S(2)}) collective-permute-start(bf16[4096,384]{1,0:T(8,128)(2,1)} %bitcast.2.gate_ref), channel_id=1, source_target_pairs={{0,1},{1,0},{2,3},{3,2},{4,5},{5,4},{6,7},{7,6},{8,9},{9,8},{10,11... | collective-permute-start | bytes 9437192 | tf_op jit(solution)/shard_map/ppermute | solution.py:20
  26.6 26.5 %copy-start.5 = (bf16[32,4224]{1,0:T(8,128)(2,1)}, bf16[32,4224]{1,0:T(8,128)(2,1)S(1)}, u32[]{:S(2)}) copy-start(bf16[32,4224]{1,0:T(8,128)(2,1)S(1)} %collective-permute-done) | copy-start | bytes 811012
  26.6 6.5 %collective-permute-start.1 = (bf16[1,32,4224]{2,1,0:T(8,128)(2,1)S(1)}, bf16[1,32,4224]{2,1,0:T(8,128)(2,1)S(1)}, u32[]{:S(2)}, u32[]{:S(2)}) collective-permute-start(bf16[1,32,4224]{2,1,0:T(8,128)(2,1)S(1)} %bitcast.68), channel_id=1, source_target_pairs={{0,8},{8,0},{16,24},{24,16},{1,9},{9,1},{17,25},{25,17},{2,10},{10... | collective-permute-start | bytes 811016 | tf_op jit(solution)/shard_map/ppermute | solution.py:20
  26.6 34.6 %copy-start.1 = (bf16[4096,768]{1,0:T(8,128)(2,1)S(1)}, bf16[4096,768]{1,0:T(8,128)(2,1)}, u32[]{:S(2)}) copy-start(bf16[4096,768]{1,0:T(8,128)(2,1)} %dequantize_in.2) | copy-start | bytes 18874372
  26.7 63.2 %collective-permute-start.5 = (bf16[4096,384]{1,0:T(8,128)(2,1)}, bf16[4096,384]{1,0:T(8,128)(2,1)}, u32[]{:S(2)}, u32[]{:S(2)}) collective-permute-start(bf16[4096,384]{1,0:T(8,128)(2,1)} %bitcast.3.up_ref), channel_id=1, source_target_pairs={{0,1},{1,0},{2,3},{3,2},{4,5},{5,4},{6,7},{7,6},{8,9},{9,8},{10,11... | collective-permute-start | bytes 9437192 | tf_op jit(solution)/shard_map/ppermute | solution.py:20
  33.1 8.2 %collective-permute-start.11 = (bf16[1,32,4224]{2,1,0:T(8,128)(2,1)S(1)}, bf16[1,32,4224]{2,1,0:T(8,128)(2,1)S(1)}, u32[]{:S(2)}, u32[]{:S(2)}) collective-permute-start(bf16[1,32,4224]{2,1,0:T(8,128)(2,1)S(1)} %bitcast.71), channel_id=1, source_target_pairs={{0,16},{16,0},{8,24},{24,8},{1,17},{17,1},{9,25},{25,9},{2,18},{18... | collective-permute-start | bytes 811016 | tf_op jit(solution)/shard_map/ppermute | solution.py:20
  34.7 72.2 %collective-permute-start.6 = (bf16[384,4096]{1,0:T(8,128)(2,1)}, bf16[384,4096]{1,0:T(8,128)(2,1)}, u32[]{:S(2)}, u32[]{:S(2)}) collective-permute-start(bf16[384,4096]{1,0:T(8,128)(2,1)} %bitcast.4.own_ref), channel_id=1, source_target_pairs={{0,1},{1,0},{2,3},{3,2},{4,5},{5,4},{6,7},{7,6},{8,9},{9,8},{10,11... | collective-permute-start | bytes 9437192 | tf_op jit(solution)/shard_map/ppermute | solution.py:20
  41.3 9.7 %collective-permute-start.17 = (bf16[1,32,4224]{2,1,0:T(8,128)(2,1)S(1)}, bf16[1,32,4224]{2,1,0:T(8,128)(2,1)S(1)}, u32[]{:S(2)}, u32[]{:S(2)}) collective-permute-start(bf16[1,32,4224]{2,1,0:T(8,128)(2,1)S(1)} %bitcast.65), channel_id=1, source_target_pairs={{0,16},{16,0},{8,24},{24,8},{1,17},{17,1},{9,25},{25,9},{2,18},{18... | collective-permute-start | bytes 811016 | tf_op jit(solution)/shard_map/ppermute | solution.py:20
  51.0 9.4 %collective-permute-start.23 = (bf16[2,32,4224]{2,1,0:T(8,128)(2,1)S(1)}, bf16[2,32,4224]{2,1,0:T(8,128)(2,1)S(1)}, u32[]{:S(2)}, u32[]{:S(2)}) collective-permute-start(bf16[2,32,4224]{2,1,0:T(8,128)(2,1)S(1)} %pad_maximum_fusion.7), channel_id=1, source_target_pairs={{0,16},{16,0},{8,24},{24,8},{1,17},{17,1},{9,25},{25,9},{2,18},{18... | collective-permute-start | bytes 1622024 | tf_op jit(solution)/shard_map/ppermute | solution.py:20
  60.4 9.4 %collective-permute-start.12 = (bf16[2,32,4224]{2,1,0:T(8,128)(2,1)S(1)}, bf16[2,32,4224]{2,1,0:T(8,128)(2,1)S(1)}, u32[]{:S(2)}, u32[]{:S(2)}) collective-permute-start(bf16[2,32,4224]{2,1,0:T(8,128)(2,1)S(1)} %pad_maximum_fusion.5), channel_id=1, source_target_pairs={{0,8},{8,0},{16,24},{24,16},{1,9},{9,1},{17,25},{25,17},{2,10},{10... | collective-permute-start | bytes 1622024 | tf_op jit(solution)/shard_map/ppermute | solution.py:20
  69.8 9.4 %collective-permute-start.2 = (bf16[2,32,4224]{2,1,0:T(8,128)(2,1)S(1)}, bf16[2,32,4224]{2,1,0:T(8,128)(2,1)S(1)}, u32[]{:S(2)}, u32[]{:S(2)}) collective-permute-start(bf16[2,32,4224]{2,1,0:T(8,128)(2,1)S(1)} %pad_maximum_fusion.4), channel_id=1, source_target_pairs={{0,16},{16,0},{8,24},{24,8},{1,17},{17,1},{9,25},{25,9},{2,18},{18... | collective-permute-start | bytes 1622024 | tf_op jit(solution)/shard_map/ppermute | solution.py:20
  71.9 7.9 %copy-start.6 = (bf16[32,4224]{1,0:T(8,128)(2,1)S(1)}, bf16[32,4224]{1,0:T(8,128)(2,1)}, u32[]{:S(2)}) copy-start(bf16[32,4224]{1,0:T(8,128)(2,1)} %copy-done.5) | copy-start | bytes 811012
  79.1 9.4 %collective-permute-start.18 = (bf16[2,32,4224]{2,1,0:T(8,128)(2,1)S(1)}, bf16[2,32,4224]{2,1,0:T(8,128)(2,1)S(1)}, u32[]{:S(2)}, u32[]{:S(2)}) collective-permute-start(bf16[2,32,4224]{2,1,0:T(8,128)(2,1)S(1)} %pad_maximum_fusion.6), channel_id=1, source_target_pairs={{0,8},{8,0},{16,24},{24,16},{1,9},{9,1},{17,25},{25,17},{2,10},{10... | collective-permute-start | bytes 1622024 | tf_op jit(solution)/shard_map/ppermute | solution.py:20
  106.8 8.4 %copy-start.9 = (bf16[128,384]{1,0:T(8,128)(2,1)S(1)}, bf16[128,384]{1,0:T(8,128)(2,1)}, u32[]{:S(2)}) copy-start(bf16[128,384]{1,0:T(8,128)(2,1)} %fusion.30) | copy-start | bytes 294916
  115.2 6.1 %copy-start = (bf16[768,4096]{1,0:T(8,128)(2,1)S(1)}, bf16[768,4096]{1,0:T(8,128)(2,1)}, u32[]{:S(2)}) copy-start(bf16[768,4096]{1,0:T(8,128)(2,1)} %dequantize_down.1) | copy-start | bytes 18874372
  119.2 14.9 %collective-permute-start.24 = (bf16[2,32,4096]{2,1,0:T(8,128)(2,1)S(1)}, bf16[2,32,4096]{2,1,0:T(8,128)(2,1)S(1)}, u32[]{:S(2)}, u32[]{:S(2)}) collective-permute-start(bf16[2,32,4096]{2,1,0:T(8,128)(2,1)S(1)} %bitcast.77), channel_id=1, source_target_pairs={{0,16},{16,0},{8,24},{24,8},{1,17},{17,1},{9,25},{25,9},{2,18},{18... | collective-permute-start | bytes 1572872 | tf_op jit(solution)/shard_map/ppermute | solution.py:20
  122.5 14.5 %collective-permute-start.19 = (bf16[2,32,4096]{2,1,0:T(8,128)(2,1)S(1)}, bf16[2,32,4096]{2,1,0:T(8,128)(2,1)S(1)}, u32[]{:S(2)}, u32[]{:S(2)}) collective-permute-start(bf16[2,32,4096]{2,1,0:T(8,128)(2,1)S(1)} %bitcast.75), channel_id=1, source_target_pairs={{0,8},{8,0},{16,24},{24,16},{1,9},{9,1},{17,25},{25,17},{2,10},{10... | collective-permute-start | bytes 1572872 | tf_op jit(solution)/shard_map/ppermute | solution.py:20
  124.4 18.2 %collective-permute-start.13 = (bf16[2,32,4096]{2,1,0:T(8,128)(2,1)S(1)}, bf16[2,32,4096]{2,1,0:T(8,128)(2,1)S(1)}, u32[]{:S(2)}, u32[]{:S(2)}) collective-permute-start(bf16[2,32,4096]{2,1,0:T(8,128)(2,1)S(1)} %bitcast.74), channel_id=1, source_target_pairs={{0,8},{8,0},{16,24},{24,16},{1,9},{9,1},{17,25},{25,17},{2,10},{10... | collective-permute-start | bytes 1572872 | tf_op jit(solution)/shard_map/ppermute | solution.py:20
  126.9 16.7 %collective-permute-start.7 = (bf16[2,32,4096]{2,1,0:T(8,128)(2,1)S(1)}, bf16[2,32,4096]{2,1,0:T(8,128)(2,1)S(1)}, u32[]{:S(2)}, u32[]{:S(2)}) collective-permute-start(bf16[2,32,4096]{2,1,0:T(8,128)(2,1)S(1)} %bitcast.76), channel_id=1, source_target_pairs={{0,16},{16,0},{8,24},{24,8},{1,17},{17,1},{9,25},{25,9},{2,18},{18... | collective-permute-start | bytes 1572872 | tf_op jit(solution)/shard_map/ppermute | solution.py:20
  134.3 29.8 %collective-permute-start.25 = (bf16[1,32,4096]{2,1,0:T(8,128)(2,1)S(1)}, bf16[1,32,4096]{2,1,0:T(8,128)(2,1)S(1)}, u32[]{:S(2)}, u32[]{:S(2)}) collective-permute-start(bf16[1,32,4096]{2,1,0:T(8,128)(2,1)S(1)} %split.91), channel_id=1, source_target_pairs={{0,8},{8,0},{16,24},{24,16},{1,9},{9,1},{17,25},{25,17},{2,10},{10... | collective-permute-start | bytes 786440 | tf_op jit(solution)/shard_map/ppermute | solution.py:20
  137.2 7.4 %collective-permute-start.20 = (bf16[1,32,4096]{2,1,0:T(8,128)(2,1)S(1)}, bf16[1,32,4096]{2,1,0:T(8,128)(2,1)S(1)}, u32[]{:S(2)}, u32[]{:S(2)}) collective-permute-start(bf16[1,32,4096]{2,1,0:T(8,128)(2,1)S(1)} %split.87), channel_id=1, source_target_pairs={{0,16},{16,0},{8,24},{24,8},{1,17},{17,1},{9,25},{25,9},{2,18},{18... | collective-permute-start | bytes 786440 | tf_op jit(solution)/shard_map/ppermute | solution.py:20
  142.8 13.5 %collective-permute-start.14 = (bf16[1,32,4096]{2,1,0:T(8,128)(2,1)S(1)}, bf16[1,32,4096]{2,1,0:T(8,128)(2,1)S(1)}, u32[]{:S(2)}, u32[]{:S(2)}) collective-permute-start(bf16[1,32,4096]{2,1,0:T(8,128)(2,1)S(1)} %split.83), channel_id=1, source_target_pairs={{0,16},{16,0},{8,24},{24,8},{1,17},{17,1},{9,25},{25,9},{2,18},{18... | collective-permute-start | bytes 786440 | tf_op jit(solution)/shard_map/ppermute | solution.py:20
  143.6 32.9 %copy-start.7 = (bf16[32,4096]{1,0:T(8,128)(2,1)S(1)}, bf16[32,4096]{1,0:T(8,128)(2,1)}, u32[]{:S(2)}) copy-start(bf16[32,4096]{1,0:T(8,128)(2,1)} %param.9) | copy-start | bytes 786436
  143.8 16.1 %collective-permute-start.8 = (bf16[1,32,4096]{2,1,0:T(8,128)(2,1)S(1)}, bf16[1,32,4096]{2,1,0:T(8,128)(2,1)S(1)}, u32[]{:S(2)}, u32[]{:S(2)}) collective-permute-start(bf16[1,32,4096]{2,1,0:T(8,128)(2,1)S(1)} %split.79), channel_id=1, source_target_pairs={{0,8},{8,0},{16,24},{24,16},{1,9},{9,1},{17,25},{25,17},{2,10},{10... | collective-permute-start | bytes 786440 | tf_op jit(solution)/shard_map/ppermute | solution.py:20
  144.6 19.5 %collective-permute-start.21 = (bf16[32,4096]{1,0:T(8,128)(2,1)S(1)}, bf16[32,4096]{1,0:T(8,128)(2,1)S(1)}, u32[]{:S(2)}, u32[]{:S(2)}) collective-permute-start(bf16[32,4096]{1,0:T(8,128)(2,1)S(1)} %fusion.27), channel_id=1, source_target_pairs={{0,2},{1,3},{2,0},{3,1},{4,6},{5,7},{6,4},{7,5},{8,10},{9,11},{10,... | collective-permute-start | bytes 786440 | tf_op jit(solution)/shard_map/ppermute | solution.py:177
  156.4 10.6 %collective-permute-start.15 = (bf16[32,4096]{1,0:T(8,128)(2,1)S(1)}, bf16[32,4096]{1,0:T(8,128)(2,1)S(1)}, u32[]{:S(2)}, u32[]{:S(2)}) collective-permute-start(bf16[32,4096]{1,0:T(8,128)(2,1)S(1)} %fusion.26), channel_id=1, source_target_pairs={{0,6},{1,7},{2,4},{3,5},{4,2},{5,3},{6,0},{7,1},{8,14},{9,15},{10,... | collective-permute-start | bytes 786440 | tf_op jit(solution)/shard_map/ppermute | solution.py:177
  159.9 16.5 %collective-permute-start.9 = (bf16[32,4096]{1,0:T(8,128)(2,1)S(1)}, bf16[32,4096]{1,0:T(8,128)(2,1)S(1)}, u32[]{:S(2)}, u32[]{:S(2)}) collective-permute-start(bf16[32,4096]{1,0:T(8,128)(2,1)S(1)} %fusion.25), channel_id=1, source_target_pairs={{0,4},{1,5},{2,6},{3,7},{4,0},{5,1},{6,2},{7,3},{8,12},{9,13},{10,... | collective-permute-start | bytes 786440 | tf_op jit(solution)/shard_map/ppermute | solution.py:177
  (7 other events, 14.1 us)

commit v4 on v3

--- a/solution.py
+++ b/solution.py
@@ -109,67 +109,63 @@
     return (block.astype(jnp.float32) * scale).astype(jnp.bfloat16)
 
 
-def in_kernel(block_cols, scales, gate_ref, up_ref, out_ref):
+def in_kernel(block_cols, gate_scales, up_scales, gate_ref, up_ref, out_ref):
     strip = gate_ref.shape[0] // BLOCK
     first = pl.program_id(0) * strip
-    up_at = pl.num_programs(0) * strip * block_cols
     for row in range(strip):
         rows = slice(row * BLOCK, (row + 1) * BLOCK)
         for col in range(block_cols):
             cols = slice(col * BLOCK, (col + 1) * BLOCK)
             place = (first + row) * block_cols + col
-            out_ref[rows, cols] = scaled(gate_ref[rows, cols], scales[place])
+            out_ref[rows, cols] = scaled(gate_ref[rows, cols], gate_scales[place])
             cols_up = slice((block_cols + col) * BLOCK, (block_cols + col + 1) * BLOCK)
-            out_ref[rows, cols_up] = scaled(up_ref[rows, cols], scales[up_at + place])
-
-
-def dequantize_in(gate, up, scales):
+            out_ref[rows, cols_up] = scaled(up_ref[rows, cols], up_scales[place])
+
+
+def dequantize_in(gate, up, gate_scales, up_scales):
     rows, cols = gate.shape
-    strip = min(rows, 4 * BLOCK)
+    strip = min(rows, 8 * BLOCK)
     block = pl.BlockSpec((strip, cols), lambda i: (i, 0))
+    smem = pl.BlockSpec(memory_space=pltpu.SMEM)
     return pl.pallas_call(
         functools.partial(in_kernel, cols // BLOCK),
         grid=(rows // strip,),
-        in_specs=[pl.BlockSpec(memory_space=pltpu.SMEM), block, block],
+        in_specs=[smem, smem, block, block],
         out_specs=pl.BlockSpec((strip, 2 * cols), lambda i: (i, 0)),
         out_shape=jax.ShapeDtypeStruct((rows, 2 * cols), jnp.bfloat16),
         cost_estimate=pl.CostEstimate(
             flops=2 * rows * cols, bytes_accessed=8 * rows * cols, transcendentals=0
         ),
         name="dequantize_in",
-    )(scales, gate, up)
-
-
-def down_kernel(at, block_cols, scales_own, scales_other, own_ref, other_ref, out_ref):
-    strip = own_ref.shape[1] // BLOCK
-    block_rows = own_ref.shape[0] // BLOCK
+    )(gate_scales, up_scales, gate, up)
+
+
+def down_kernel(block_cols, scales, down_ref, out_ref):
+    strip = down_ref.shape[1] // BLOCK
     first = pl.program_id(0) * strip
-    for half, (scales, ref) in enumerate(((scales_own, own_ref), (scales_other, other_ref))):
-        for row in range(block_rows):
-            rows = slice(row * BLOCK, (row + 1) * BLOCK)
-            out_row = (half * block_rows + row) * BLOCK
-            for col in range(strip):
-                cols = slice(col * BLOCK, (col + 1) * BLOCK)
-                scale = scales[at + row * block_cols + first + col]
-                out_ref[out_row : out_row + BLOCK, cols] = scaled(ref[rows, cols], scale)
-
-
-def dequantize_down(own, other, scales_own, scales_other, at):
-    rows, cols = own.shape
-    strip = min(cols, 4 * BLOCK)
+    for row in range(down_ref.shape[0] // BLOCK):
+        rows = slice(row * BLOCK, (row + 1) * BLOCK)
+        for col in range(strip):
+            cols = slice(col * BLOCK, (col + 1) * BLOCK)
+            scale = scales[row * block_cols + first + col]
+            out_ref[rows, cols] = scaled(down_ref[rows, cols], scale)
+
+
+def dequantize_down(down, scales):
+    rows, cols = down.shape
+    strip = min(cols, 8 * BLOCK)
     block = pl.BlockSpec((rows, strip), lambda i: (0, i))
-    smem = pl.BlockSpec(memory_space=pltpu.SMEM)
     return pl.pallas_call(
-        functools.partial(down_kernel, at, cols // BLOCK),
+        functools.partial(down_kernel, cols // BLOCK),
         grid=(cols // strip,),
-        in_specs=[smem, smem, block, block],
-        out_specs=pl.BlockSpec((2 * rows, strip), lambda i: (0, i)),
-        out_shape=jax.ShapeDtypeStruct((2 * rows, cols), jnp.bfloat16),
+        in_specs=[pl.BlockSpec(memory_space=pltpu.SMEM), block],
+        out_specs=block,
+        out_shape=jax.ShapeDtypeStruct((rows, cols), jnp.bfloat16),
         cost_estimate=pl.CostEstimate(
-            flops=2 * rows * cols, bytes_accessed=8 * rows * cols, transcendentals=0
+            flops=rows * cols, bytes_accessed=4 * rows * cols, transcendentals=0
         ),
         name="dequantize_down",
-    )(scales_own, scales_other, own, other)
+    )(scales, down)
 
 
 def across_chips(block, far):
@@ -194,15 +190,26 @@
     pad = jnp.zeros((token_count, extra - 2 * expert_count), jnp.bfloat16)
     payload = jnp.concatenate([tokens, high, low, pad], axis=1)
 
-    quant = [gate_q[0], up_q[0], down_q[0]]
+    route = [0, *range(2, pair_count), 1][:pair_count]
+    order_of = {far: orders[place % 2] for place, far in enumerate(route)}
+    step = 2
+    blocks = {0: payload[None]}
+    for far in route[1:step]:
+        blocks[far] = across_chips(payload, far)[None]
+    blocks[0] = gather_groups(blocks[0], order_of[0][:1])
+
+    gate_own, up_own, payload = lax.optimization_barrier((gate_q[0], up_q[0], payload))
     hidden_half = gate_q.shape[2]
-    scales = jnp.concatenate([s.reshape(-1) for s in (gate_scale, up_scale, down_scale)])
-    scales_other = from_partner(scales, "expert", 0)
-    gate_other, up_other, down_other = [from_partner(q, "expert", 0) for q in quant]
-    in_own = dequantize_in(quant[0], quant[1], scales)
-    in_other = dequantize_in(gate_other, up_other, scales_other)
-    down_at = gate_scale.size + up_scale.size
-    down_both = dequantize_down(quant[2], down_other, scales, scales_other, down_at)
+    in_own = dequantize_in(gate_own, up_own, gate_scale.reshape(-1), up_scale.reshape(-1))
+    blocks, payload, in_own, down_half = lax.optimization_barrier(
+        (blocks, payload, in_own, down_q[0])
+    )
+    in_other = from_partner(in_own, "expert", 0)
+    for far in route[step:]:
+        blocks[far] = across_chips(payload, far)[None]
+    down_own = dequantize_down(down_half, down_scale.reshape(-1))
+    down_other = from_partner(down_own, "expert", 0)
+    down_both = jnp.concatenate([down_own, down_other], axis=0)
 
     def ffn(rows):
         inputs = rows[:, :model_width]
@@ -221,14 +228,24 @@
         return (value * row_weight[:, None]).astype(jnp.bfloat16)
 
     outs = {}
-    for far in range(pair_count):
-        block = payload if far == 0 else across_chips(payload, far)
-        every = gather_groups(block[None], orders[far % 2])
-        outs[far] = ffn(every.reshape(-1, every.shape[-1]))
+    for first in range(0, pair_count, step):
+        fars = route[first : first + step]
+        for far in fars:
+            blocks[far] = gather_groups(blocks[far], order_of[far][int(far == 0) : -1])
+        if outs:
+            tied = [blocks[far] for far in fars]
+            outs[0], tied = lax.optimization_barrier((outs[0], tied))
+            for far, block in zip(fars, tied):
+                blocks[far] = block
+        for far in fars:
+            blocks[far] = gather_groups(blocks[far], order_of[far][-1:])
+        for far in fars:
+            outs[far] = ffn(blocks[far].reshape(-1, blocks[far].shape[-1]))
+    outs[0], outs[1] = lax.optimization_barrier((outs[0], outs[1]))
     total = tokens.astype(jnp.float32)
-    for far in [*range(2, pair_count), 1, 0][-pair_count:]:
+    for far in route[1:] + route[:1]:
         out = outs[far].reshape(group_count, token_count, model_width)
-        block = sum_groups(out, orders[far % 2])[0]
+        block = sum_groups(out, order_of[far])[0]
         if far > 0:
             block = across_chips(block, far)
         total = total + block.astype(jnp.float32)

time: 178 us -> 139 us (0.78)
  starting transfers between devices: 44.5 us -> 24 us
  Pallas kernels: 24.7 us -> 10.8 us
  waiting for transfers between devices: 77.6 us -> 66.9 us
  matrix products: 18.2 us -> 27.5 us
  other arithmetic: 6.38 us -> 3.79 us
    ppermute x6, starting transfers between devices: 23.7 us -> 6.87 us  [across_chips(): lax.ppermute(block, 'expert', [(low, low ^ 2 * far) for low in range(coun...]
    dot_general x8, matrix products: 11.2 us -> 22.5 us  [ffn(): parts = jnp.dot(inputs, w_in, preferred_element_type=jnp.float32)]
    pallas_call x2 -> x1, Pallas kernels: 16.4 us -> 6.27 us  [dequantize_in(): pl.pallas_call(functools.partial(in_kernel, cols // BLOCK), grid=(rows //...]
    ppermute x20 -> x18, waiting for transfers between devices: 59.5 us -> 52.9 us  [from_partner(): return lax.ppermute(block, axis, route)]
    ppermute x6, waiting for transfers between devices: 18.1 us -> 14 us  [across_chips(): lax.ppermute(block, 'expert', [(low, low ^ 2 * far) for low in range(coun...]
    pallas_call x1, Pallas kernels: 8.35 us -> 4.57 us  [dequantize_down(): pl.pallas_call(functools.partial(down_kernel, cols // BLOCK), grid=(cols...]
    ppermute x20 -> x18, starting transfers between devices: 20.7 us -> 17.1 us  [from_partner(): return lax.ppermute(block, axis, route)]
    dot_general x4, matrix products: 7.02 us -> 5.03 us  [ffn(): value = jnp.dot(hidden, down_both, preferred_element_type=jnp.float32)]
  transfers between devices with their start and end apart: 26 -> 24, of which waited for: 13 -> 14; matrix products, arithmetic and copies ran while one was open for 12% -> 23% of each run, Pallas kernels for 9% -> 8%
where the time goes in v4:
time: 139 us
  waiting for transfers between devices  66.9 us (48%)
  matrix products  27.5 us (20%)
  starting transfers between devices  24 us (17%)
  Pallas kernels  10.8 us (8%)
  local copies, waits for them, and re-layouts  5.11 us (4%)
  other arithmetic  3.79 us (3%)
    ppermute x18, waiting for transfers between devices, from_partner(): return lax.ppermute(block, axis, route)  52.9 us
    dot_general x8, matrix products, ffn(): parts = jnp.dot(inputs, w_in, preferred_element_type=jnp.float32)  22.5 us
    ppermute x18, starting transfers between devices, from_partner(): return lax.ppermute(block, axis, route)  17.1 us
    ppermute x6, waiting for transfers between devices, across_chips(): lax.ppermute(block, 'expert', [(low, low ^ 2 * far) for low in range(coun...  14 us
    ppermute x6, starting transfers between devices, across_chips(): lax.ppermute(block, 'expert', [(low, low ^ 2 * far) for low in range(coun...  6.87 us
    pallas_call x1, Pallas kernels, dequantize_in(): pl.pallas_call(functools.partial(in_kernel, cols // BLOCK), grid=(rows //...  6.27 us
    dot_general x4, matrix products, ffn(): value = jnp.dot(hidden, down_both, preferred_element_type=jnp.float32)  5.03 us
    pallas_call x1, Pallas kernels, dequantize_down(): pl.pallas_call(functools.partial(down_kernel, cols // BLOCK), grid=(cols...  4.57 us
  transfers between devices with their start and end apart: 24, of which 14 were waited for; matrix products, arithmetic and copies ran while one was open for 23% of the time, Pallas kernels for 8%

profile of v4, /device:TPU:0, one launch (start us, length us, event | category | flops | bytes accessed | tf_op | source)
XLA Modules:
  0.0 138.5 jit_solution(10811459758592787638)
XLA Ops:
  2.0 3.0 %collective-permute-start = (bf16[1,32,4224]{2,1,0:T(8,128)(2,1)S(1)}, bf16[1,32,4224]{2,1,0:T(8,128)(2,1)S(1)}, u32[]{:S(2)}, u32[]{:S(2)}) collective-permute-start(bf16[1,32,4224]{2,1,0:T(8,128)(2,1)S(1)} %bitcast.66), channel_id=1, source_target_pairs={{0,8},{8,0},{16,24},{24,16},{1,9},{9,1},{17,25},{25,17},{2,10},{10... | collective-permute-start | bytes 811016 | tf_op jit(solution)/shard_map/ppermute | solution.py:20
  5.0 2.6 %collective-permute-start.1 = (bf16[32,4224]{1,0:T(8,128)(2,1)S(1)}, bf16[32,4224]{1,0:T(8,128)(2,1)S(1)}, u32[]{:S(2)}, u32[]{:S(2)}) collective-permute-start(bf16[32,4224]{1,0:T(8,128)(2,1)S(1)} %concatenate.43), channel_id=1, source_target_pairs={{0,4},{1,5},{2,6},{3,7},{4,0},{5,1},{6,2},{7,3},{8,12},{9,13},{10,... | collective-permute-start | bytes 811016 | tf_op jit(solution)/shard_map/ppermute | solution.py:173
  10.4 6.3 %dequantize_in.1 = bf16[4096,768]{1,0:T(8,128)(2,1)} custom-call(f32[96]{0:T(128)} %reshape.60.gate_scales, f32[96]{0:T(128)} %reshape.61.up_scales, bf16[4096,384]{1,0:T(8,128)(2,1)} %bitcast.57, bf16[4096,384]{1,0:T(8,128)(2,1)} %bitcast.58), custom_call_target="tpu_custom_call" | custom-call | flops 3145728 | bytes 12582912 | tf_op jit(solution)/shard_map/dequantize_in/pallas_call | solution.py:130
  16.7 2.9 %collective-permute-done.1 = bf16[32,4224]{1,0:T(8,128)(2,1)S(1)} collective-permute-done((bf16[32,4224]{1,0:T(8,128)(2,1)S(1)}, bf16[32,4224]{1,0:T(8,128)(2,1)S(1)}, u32[]{:S(2)}, u32[]{:S(2)}) %collective-permute-start.1) | collective-permute-done | bytes 270368 | tf_op jit(solution)/shard_map/ppermute | solution.py:173
  20.3 2.8 %collective-permute-start.10 = (bf16[32,4224]{1,0:T(8,128)(2,1)S(1)}, bf16[32,4224]{1,0:T(8,128)(2,1)S(1)}, u32[]{:S(2)}, u32[]{:S(2)}) collective-permute-start(bf16[32,4224]{1,0:T(8,128)(2,1)S(1)} %concatenate.43), channel_id=1, source_target_pairs={{0,6},{1,7},{2,4},{3,5},{4,2},{5,3},{6,0},{7,1},{8,14},{9,15},{10,... | collective-permute-start | bytes 811016 | tf_op jit(solution)/shard_map/ppermute | solution.py:173
  23.1 1.5 %collective-permute-start.2 = (bf16[1,32,4224]{2,1,0:T(8,128)(2,1)S(1)}, bf16[1,32,4224]{2,1,0:T(8,128)(2,1)S(1)}, u32[]{:S(2)}, u32[]{:S(2)}) collective-permute-start(bf16[1,32,4224]{2,1,0:T(8,128)(2,1)S(1)} %bitcast.63), channel_id=1, source_target_pairs={{0,16},{16,0},{8,24},{24,8},{1,17},{17,1},{9,25},{25,9},{2,18},{18... | collective-permute-start | bytes 811016 | tf_op jit(solution)/shard_map/ppermute | solution.py:20
  25.8 4.6 %dequantize_down.1 = bf16[384,4096]{1,0:T(8,128)(2,1)} custom-call(f32[96]{0:T(128)} %reshape.63.scales, bf16[384,4096]{1,0:T(8,128)(2,1)} %bitcast.56), custom_call_target="tpu_custom_call" | custom-call | flops 1572864 | bytes 6291456 | tf_op jit(solution)/shard_map/dequantize_down/pallas_call | solution.py:158
  30.3 5.8 %collective-permute-done.10 = bf16[32,4224]{1,0:T(8,128)(2,1)S(1)} collective-permute-done((bf16[32,4224]{1,0:T(8,128)(2,1)S(1)}, bf16[32,4224]{1,0:T(8,128)(2,1)S(1)}, u32[]{:S(2)}, u32[]{:S(2)}) %collective-permute-start.10) | collective-permute-done | bytes 270368 | tf_op jit(solution)/shard_map/ppermute | solution.py:173
  36.1 1.5 %collective-permute-start.13 = (bf16[1,32,4224]{2,1,0:T(8,128)(2,1)S(1)}, bf16[1,32,4224]{2,1,0:T(8,128)(2,1)S(1)}, u32[]{:S(2)}, u32[]{:S(2)}) collective-permute-start(bf16[1,32,4224]{2,1,0:T(8,128)(2,1)S(1)} %bitcast.74), channel_id=1, source_target_pairs={{0,16},{16,0},{8,24},{24,8},{1,17},{17,1},{9,25},{25,9},{2,18},{18... | collective-permute-start | bytes 811016 | tf_op jit(solution)/shard_map/ppermute | solution.py:20
  38.3 10.8 %collective-permute-done.13 = bf16[1,32,4224]{2,1,0:T(8,128)(2,1)S(1)} collective-permute-done((bf16[1,32,4224]{2,1,0:T(8,128)(2,1)S(1)}, bf16[1,32,4224]{2,1,0:T(8,128)(2,1)S(1)}, u32[]{:S(2)}, u32[]{:S(2)}) %collective-permute-start.13) | collective-permute-done | bytes 270368 | tf_op jit(solution)/shard_map/ppermute | solution.py:20
  49.8 4.0 %fusion.18 = f32[128,768]{1,0:T(8,128)S(1)} fusion(bf16[4096,768]{1,0:T(8,128)(2,1)} %dequantize_in.1, bf16[128,4224]{1,0:T(8,128)(2,1)S(1)} %bitcast.44), kind=kOutput, calls=%fused_computation.31 | convolution fusion | flops 805306368 | bytes 7733248 | tf_op jit(solution)/shard_map/dot_general | solution.py:222
  54.0 8.7 %collective-permute-done.3 = bf16[2,32,4224]{2,1,0:T(8,128)(2,1)S(1)} collective-permute-done((bf16[2,32,4224]{2,1,0:T(8,128)(2,1)S(1)}, bf16[2,32,4224]{2,1,0:T(8,128)(2,1)S(1)}, u32[]{:S(2)}, u32[]{:S(2)}) %collective-permute-start.3) | collective-permute-done | bytes 540704 | tf_op jit(solution)/shard_map/ppermute | solution.py:20
  64.1 4.0 %fusion.20 = f32[128,768]{1,0:T(8,128)S(1)} fusion(bf16[4096,768]{1,0:T(8,128)(2,1)} %collective-permute-done.4, bf16[128,4224]{1,0:T(8,128)(2,1)S(1)} %bitcast.55), kind=kOutput, calls=%fused_computation.33 | convolution fusion | flops 805306368 | bytes 7733248 | tf_op jit(solution)/shard_map/dot_general | solution.py:222
  68.2 1.2 fusion
  70.1 3.8 %fusion.16 = f32[128,768]{1,0:T(8,128)S(1)} fusion(bf16[4096,768]{1,0:T(8,128)(2,1)} %collective-permute-done.4, bf16[128,4224]{1,0:T(8,128)(2,1)S(1)} %bitcast.46), kind=kOutput, calls=%fused_computation.29 | convolution fusion | flops 805306368 | bytes 7733248 | tf_op jit(solution)/shard_map/dot_general | solution.py:222
  75.2 1.6 %collective-permute-start.14 = (bf16[2,32,4224]{2,1,0:T(8,128)(2,1)S(1)}, bf16[2,32,4224]{2,1,0:T(8,128)(2,1)S(1)}, u32[]{:S(2)}, u32[]{:S(2)}) collective-permute-start(bf16[2,32,4224]{2,1,0:T(8,128)(2,1)S(1)} %pad_maximum_fusion.7), channel_id=1, source_target_pairs={{0,16},{16,0},{8,24},{24,8},{1,17},{17,1},{9,25},{25,9},{2,18},{18... | collective-permute-start | bytes 1622024 | tf_op jit(solution)/shard_map/ppermute | solution.py:20
  76.8 1.5 %collective-permute-start.18 = (bf16[2,32,4224]{2,1,0:T(8,128)(2,1)S(1)}, bf16[2,32,4224]{2,1,0:T(8,128)(2,1)S(1)}, u32[]{:S(2)}, u32[]{:S(2)}) collective-permute-start(bf16[2,32,4224]{2,1,0:T(8,128)(2,1)S(1)} %pad_maximum_fusion.8), channel_id=1, source_target_pairs={{0,8},{8,0},{16,24},{24,16},{1,9},{9,1},{17,25},{25,17},{2,10},{10... | collective-permute-start | bytes 1622024 | tf_op jit(solution)/shard_map/ppermute | solution.py:20
  78.3 6.1 %collective-permute-done.6 = bf16[2,32,4096]{2,1,0:T(8,128)(2,1)S(1)} collective-permute-done((bf16[2,32,4096]{2,1,0:T(8,128)(2,1)S(1)}, bf16[2,32,4096]{2,1,0:T(8,128)(2,1)S(1)}, u32[]{:S(2)}, u32[]{:S(2)}) %collective-permute-start.6) | collective-permute-done | bytes 524320 | tf_op jit(solution)/shard_map/ppermute | solution.py:20
  84.6 1.6 %collective-permute-start.7 = (bf16[1,32,4096]{2,1,0:T(8,128)(2,1)S(1)}, bf16[1,32,4096]{2,1,0:T(8,128)(2,1)S(1)}, u32[]{:S(2)}, u32[]{:S(2)}) collective-permute-start(bf16[1,32,4096]{2,1,0:T(8,128)(2,1)S(1)} %split.79), channel_id=1, source_target_pairs={{0,16},{16,0},{8,24},{24,8},{1,17},{17,1},{9,25},{25,9},{2,18},{18... | collective-permute-start | bytes 786440 | tf_op jit(solution)/shard_map/ppermute | solution.py:20
  86.1 4.3 %collective-permute-done.14 = bf16[2,32,4224]{2,1,0:T(8,128)(2,1)S(1)} collective-permute-done((bf16[2,32,4224]{2,1,0:T(8,128)(2,1)S(1)}, bf16[2,32,4224]{2,1,0:T(8,128)(2,1)S(1)}, u32[]{:S(2)}, u32[]{:S(2)}) %collective-permute-start.14) | collective-permute-done | bytes 540704 | tf_op jit(solution)/shard_map/ppermute | solution.py:20
  91.6 1.9 %collective-permute-done.18 = bf16[2,32,4224]{2,1,0:T(8,128)(2,1)S(1)} collective-permute-done((bf16[2,32,4224]{2,1,0:T(8,128)(2,1)S(1)}, bf16[2,32,4224]{2,1,0:T(8,128)(2,1)S(1)}, u32[]{:S(2)}, u32[]{:S(2)}) %collective-permute-start.18) | collective-permute-done | bytes 540704 | tf_op jit(solution)/shard_map/ppermute | solution.py:20
  94.7 3.9 %fusion.12 = f32[128,768]{1,0:T(8,128)S(1)} fusion(bf16[4096,768]{1,0:T(8,128)(2,1)} %collective-permute-done.4, bf16[128,4224]{1,0:T(8,128)(2,1)S(1)} %bitcast.52), kind=kOutput, calls=%fused_computation.25 | convolution fusion | flops 805306368 | bytes 7733248 | tf_op jit(solution)/shard_map/dot_general | solution.py:222
  98.7 1.4 %fusion.2 = bf16[128,4096]{1,0:T(8,128)(2,1)S(1)} fusion(f32[128]{0:T(128)S(1)} %get-tuple-element.33, bf16[128,384]{1,0:T(8,128)(2,1)S(1)} %get-tuple-element.47, bf16[128,384]{1,0:T(8,128)(2,1)S(1)} %get-tuple-element.48, bf16[384,4096]{1,0:T(8,128)(2,1)S(1)} %collective-permute-done.5, bf16[384,4096]{1,0:T(8,128)(2,1)S(1)} %copy-done), kind=kOutput, calls=%fused_computation.7 | convolution fusion | flops 819331072 | bytes 7537152 | tf_op jit(solution)/shard_map/dot_general | solution.py:227
  100.2 1.6 %collective-permute-start.15 = (bf16[2,32,4096]{2,1,0:T(8,128)(2,1)S(1)}, bf16[2,32,4096]{2,1,0:T(8,128)(2,1)S(1)}, u32[]{:S(2)}, u32[]{:S(2)}) collective-permute-start(bf16[2,32,4096]{2,1,0:T(8,128)(2,1)S(1)} %bitcast.68), channel_id=1, source_target_pairs={{0,16},{16,0},{8,24},{24,8},{1,17},{17,1},{9,25},{25,9},{2,18},{18... | collective-permute-start | bytes 1572872 | tf_op jit(solution)/shard_map/ppermute | solution.py:20
  101.7 3.8 %fusion.8 = f32[128,768]{1,0:T(8,128)S(1)} fusion(bf16[4096,768]{1,0:T(8,128)(2,1)} %collective-permute-done.4, bf16[128,4224]{1,0:T(8,128)(2,1)S(1)} %bitcast.49), kind=kOutput, calls=%fused_computation.21 | convolution fusion | flops 805306368 | bytes 7733248 | tf_op jit(solution)/shard_map/dot_general | solution.py:222
  109.0 6.1 %collective-permute-done.15 = bf16[2,32,4096]{2,1,0:T(8,128)(2,1)S(1)} collective-permute-done((bf16[2,32,4096]{2,1,0:T(8,128)(2,1)S(1)}, bf16[2,32,4096]{2,1,0:T(8,128)(2,1)S(1)}, u32[]{:S(2)}, u32[]{:S(2)}) %collective-permute-start.15) | collective-permute-done | bytes 524320 | tf_op jit(solution)/shard_map/ppermute | solution.py:20
  115.6 5.4 %collective-permute-done.19 = bf16[2,32,4096]{2,1,0:T(8,128)(2,1)S(1)} collective-permute-done((bf16[2,32,4096]{2,1,0:T(8,128)(2,1)S(1)}, bf16[2,32,4096]{2,1,0:T(8,128)(2,1)S(1)}, u32[]{:S(2)}, u32[]{:S(2)}) %collective-permute-start.19) | collective-permute-done | bytes 524320 | tf_op jit(solution)/shard_map/ppermute | solution.py:20
  121.7 3.9 %collective-permute-done.22 = bf16[2,32,4096]{2,1,0:T(8,128)(2,1)S(1)} collective-permute-done((bf16[2,32,4096]{2,1,0:T(8,128)(2,1)S(1)}, bf16[2,32,4096]{2,1,0:T(8,128)(2,1)S(1)}, u32[]{:S(2)}, u32[]{:S(2)}) %collective-permute-start.22) | collective-permute-done | bytes 524320 | tf_op jit(solution)/shard_map/ppermute | solution.py:20
  126.6 1.9 %collective-permute-done.20 = bf16[1,32,4096]{2,1,0:T(8,128)(2,1)S(1)} collective-permute-done((bf16[1,32,4096]{2,1,0:T(8,128)(2,1)S(1)}, bf16[1,32,4096]{2,1,0:T(8,128)(2,1)S(1)}, u32[]{:S(2)}, u32[]{:S(2)}) %collective-permute-start.20) | collective-permute-done | bytes 262176 | tf_op jit(solution)/shard_map/ppermute | solution.py:20
  128.6 3.6 %collective-permute-done.23 = bf16[1,32,4096]{2,1,0:T(8,128)(2,1)S(1)} collective-permute-done((bf16[1,32,4096]{2,1,0:T(8,128)(2,1)S(1)}, bf16[1,32,4096]{2,1,0:T(8,128)(2,1)S(1)}, u32[]{:S(2)}, u32[]{:S(2)}) %collective-permute-start.23) | collective-permute-done | bytes 262176 | tf_op jit(solution)/shard_map/ppermute | solution.py:20
  132.3 2.7 %collective-permute-done.17 = bf16[32,4096]{1,0:T(8,128)(2,1)S(1)} collective-permute-done((bf16[32,4096]{1,0:T(8,128)(2,1)S(1)}, bf16[32,4096]{1,0:T(8,128)(2,1)S(1)}, u32[]{:S(2)}, u32[]{:S(2)}) %collective-permute-start.17) | collective-permute-done | bytes 262176 | tf_op jit(solution)/shard_map/ppermute | solution.py:173
  134.9 2.7 %collective-permute-done.21 = bf16[32,4096]{1,0:T(8,128)(2,1)S(1)} collective-permute-done((bf16[32,4096]{1,0:T(8,128)(2,1)S(1)}, bf16[32,4096]{1,0:T(8,128)(2,1)S(1)}, u32[]{:S(2)}, u32[]{:S(2)}) %collective-permute-start.21) | collective-permute-done | bytes 262176 | tf_op jit(solution)/shard_map/ppermute | solution.py:173
  (86 shorter events, 20.7 us)
Async XLA Ops:
  2.0 14.7 %collective-permute-start = (bf16[1,32,4224]{2,1,0:T(8,128)(2,1)S(1)}, bf16[1,32,4224]{2,1,0:T(8,128)(2,1)S(1)}, u32[]{:S(2)}, u32[]{:S(2)}) collective-permute-start(bf16[1,32,4224]{2,1,0:T(8,128)(2,1)S(1)} %bitcast.66), channel_id=1, source_target_pairs={{0,8},{8,0},{16,24},{24,16},{1,9},{9,1},{17,25},{25,17},{2,10},{10... | collective-permute-start | bytes 811016 | tf_op jit(solution)/shard_map/ppermute | solution.py:20
  5.0 14.6 %collective-permute-start.1 = (bf16[32,4224]{1,0:T(8,128)(2,1)S(1)}, bf16[32,4224]{1,0:T(8,128)(2,1)S(1)}, u32[]{:S(2)}, u32[]{:S(2)}) collective-permute-start(bf16[32,4224]{1,0:T(8,128)(2,1)S(1)} %concatenate.43), channel_id=1, source_target_pairs={{0,4},{1,5},{2,6},{3,7},{4,0},{5,1},{6,2},{7,3},{8,12},{9,13},{10,... | collective-permute-start | bytes 811016 | tf_op jit(solution)/shard_map/ppermute | solution.py:173
  10.4 14.2 %copy-start.2 = (f32[1,3,32]{2,0,1:T(1,128)S(1)}, f32[1,3,32]{2,0,1:T(1,128)}, u32[]{:S(2)}) copy-start(f32[1,3,32]{2,0,1:T(1,128)} %param.17) | copy-start | bytes 1156
  19.6 44.5 %collective-permute-start.4 = (bf16[4096,768]{1,0:T(8,128)(2,1)}, bf16[4096,768]{1,0:T(8,128)(2,1)}, u32[]{:S(2)}, u32[]{:S(2)}) collective-permute-start(bf16[4096,768]{1,0:T(8,128)(2,1)} %dequantize_in.1), channel_id=1, source_target_pairs={{0,1},{1,0},{2,3},{3,2},{4,5},{5,4},{6,7},{7,6},{8,9},{9,8},{10,11... | collective-permute-start | bytes 18874376 | tf_op jit(solution)/shard_map/ppermute | solution.py:20
  19.6 10.7 %collective-permute-start.12 = (bf16[32,4224]{1,0:T(8,128)(2,1)S(1)}, bf16[32,4224]{1,0:T(8,128)(2,1)S(1)}, u32[]{:S(2)}, u32[]{:S(2)}) collective-permute-start(bf16[32,4224]{1,0:T(8,128)(2,1)S(1)} %concatenate.43), channel_id=1, source_target_pairs={{0,2},{1,3},{2,0},{3,1},{4,6},{5,7},{6,4},{7,5},{8,10},{9,11},{10,... | collective-permute-start | bytes 811016 | tf_op jit(solution)/shard_map/ppermute | solution.py:173
  20.3 15.9 %collective-permute-start.10 = (bf16[32,4224]{1,0:T(8,128)(2,1)S(1)}, bf16[32,4224]{1,0:T(8,128)(2,1)S(1)}, u32[]{:S(2)}, u32[]{:S(2)}) collective-permute-start(bf16[32,4224]{1,0:T(8,128)(2,1)S(1)} %concatenate.43), channel_id=1, source_target_pairs={{0,6},{1,7},{2,4},{3,5},{4,2},{5,3},{6,0},{7,1},{8,14},{9,15},{10,... | collective-permute-start | bytes 811016 | tf_op jit(solution)/shard_map/ppermute | solution.py:173
  23.1 14.6 %collective-permute-start.2 = (bf16[1,32,4224]{2,1,0:T(8,128)(2,1)S(1)}, bf16[1,32,4224]{2,1,0:T(8,128)(2,1)S(1)}, u32[]{:S(2)}, u32[]{:S(2)}) collective-permute-start(bf16[1,32,4224]{2,1,0:T(8,128)(2,1)S(1)} %bitcast.63), channel_id=1, source_target_pairs={{0,16},{16,0},{8,24},{24,8},{1,17},{17,1},{9,25},{25,9},{2,18},{18... | collective-permute-start | bytes 811016 | tf_op jit(solution)/shard_map/ppermute | solution.py:20
  25.3 24.4 %collective-permute-start.9 = (bf16[2,32,4224]{2,1,0:T(8,128)(2,1)S(1)}, bf16[2,32,4224]{2,1,0:T(8,128)(2,1)S(1)}, u32[]{:S(2)}, u32[]{:S(2)}) collective-permute-start(bf16[2,32,4224]{2,1,0:T(8,128)(2,1)S(1)} %pad_maximum_fusion.5), channel_id=1, source_target_pairs={{0,16},{16,0},{8,24},{24,8},{1,17},{17,1},{9,25},{25,9},{2,18},{18... | collective-permute-start | bytes 1622024 | tf_op jit(solution)/shard_map/ppermute | solution.py:20
  30.3 37.8 %collective-permute-start.5 = (bf16[384,4096]{1,0:T(8,128)(2,1)}, bf16[384,4096]{1,0:T(8,128)(2,1)S(1)}, u32[]{:S(2)}, u32[]{:S(2)}) collective-permute-start(bf16[384,4096]{1,0:T(8,128)(2,1)} %dequantize_down.1), channel_id=1, source_target_pairs={{0,1},{1,0},{2,3},{3,2},{4,5},{5,4},{6,7},{7,6},{8,9},{9,8},{10,11... | collective-permute-start | bytes 9437192 | tf_op jit(solution)/shard_map/ppermute | solution.py:20
  36.1 12.9 %collective-permute-start.13 = (bf16[1,32,4224]{2,1,0:T(8,128)(2,1)S(1)}, bf16[1,32,4224]{2,1,0:T(8,128)(2,1)S(1)}, u32[]{:S(2)}, u32[]{:S(2)}) collective-permute-start(bf16[1,32,4224]{2,1,0:T(8,128)(2,1)S(1)} %bitcast.74), channel_id=1, source_target_pairs={{0,16},{16,0},{8,24},{24,8},{1,17},{17,1},{9,25},{25,9},{2,18},{18... | collective-permute-start | bytes 811016 | tf_op jit(solution)/shard_map/ppermute | solution.py:20
  37.7 16.2 %collective-permute-start.11 = (bf16[1,32,4224]{2,1,0:T(8,128)(2,1)S(1)}, bf16[1,32,4224]{2,1,0:T(8,128)(2,1)S(1)}, u32[]{:S(2)}, u32[]{:S(2)}) collective-permute-start(bf16[1,32,4224]{2,1,0:T(8,128)(2,1)S(1)} %bitcast.72), channel_id=1, source_target_pairs={{0,8},{8,0},{16,24},{24,16},{1,9},{9,1},{17,25},{25,17},{2,10},{10... | collective-permute-start | bytes 811016 | tf_op jit(solution)/shard_map/ppermute | solution.py:20
  49.1 13.6 %collective-permute-start.3 = (bf16[2,32,4224]{2,1,0:T(8,128)(2,1)S(1)}, bf16[2,32,4224]{2,1,0:T(8,128)(2,1)S(1)}, u32[]{:S(2)}, u32[]{:S(2)}) collective-permute-start(bf16[2,32,4224]{2,1,0:T(8,128)(2,1)S(1)} %pad_maximum_fusion.6), channel_id=1, source_target_pairs={{0,8},{8,0},{16,24},{24,16},{1,9},{9,1},{17,25},{25,17},{2,10},{10... | collective-permute-start | bytes 1622024 | tf_op jit(solution)/shard_map/ppermute | solution.py:20
  49.8 13.1 %slice-start = ((s8[6291456]{0:T(1024)(128)(4,1)}), s8[4194304]{0:T(1024)(128)(4,1)S(1)}, s32[]{:S(2)}) async-start(s8[6291456]{0:T(1024)(128)(4,1)} %bitcast.42), calls=%async_computation | async-start | bytes 8388608
  49.8 13.1 %slice-start.1 = ((s8[6291456]{0:T(1024)(128)(4,1)}), s8[2097152]{0:T(1024)(128)(4,1)S(1)}, s32[]{:S(2)}) async-start(s8[6291456]{0:T(1024)(128)(4,1)} %bitcast.42), calls=%async_computation.1 | async-start | bytes 4194304
  64.0 4.1 %copy-start = (bf16[384,4096]{1,0:T(8,128)(2,1)S(1)}, bf16[384,4096]{1,0:T(8,128)(2,1)}, u32[]{:S(2)}) copy-start(bf16[384,4096]{1,0:T(8,128)(2,1)} %dequantize_down.1) | copy-start | bytes 9437188
  69.5 14.9 %collective-permute-start.6 = (bf16[2,32,4096]{2,1,0:T(8,128)(2,1)S(1)}, bf16[2,32,4096]{2,1,0:T(8,128)(2,1)S(1)}, u32[]{:S(2)}, u32[]{:S(2)}) collective-permute-start(bf16[2,32,4096]{2,1,0:T(8,128)(2,1)S(1)} %bitcast.71), channel_id=1, source_target_pairs={{0,8},{8,0},{16,24},{24,16},{1,9},{9,1},{17,25},{25,17},{2,10},{10... | collective-permute-start | bytes 1572872 | tf_op jit(solution)/shard_map/ppermute | solution.py:20
  75.2 15.2 %collective-permute-start.14 = (bf16[2,32,4224]{2,1,0:T(8,128)(2,1)S(1)}, bf16[2,32,4224]{2,1,0:T(8,128)(2,1)S(1)}, u32[]{:S(2)}, u32[]{:S(2)}) collective-permute-start(bf16[2,32,4224]{2,1,0:T(8,128)(2,1)S(1)} %pad_maximum_fusion.7), channel_id=1, source_target_pairs={{0,16},{16,0},{8,24},{24,8},{1,17},{17,1},{9,25},{25,9},{2,18},{18... | collective-permute-start | bytes 1622024 | tf_op jit(solution)/shard_map/ppermute | solution.py:20
  76.8 16.7 %collective-permute-start.18 = (bf16[2,32,4224]{2,1,0:T(8,128)(2,1)S(1)}, bf16[2,32,4224]{2,1,0:T(8,128)(2,1)S(1)}, u32[]{:S(2)}, u32[]{:S(2)}) collective-permute-start(bf16[2,32,4224]{2,1,0:T(8,128)(2,1)S(1)} %pad_maximum_fusion.8), channel_id=1, source_target_pairs={{0,8},{8,0},{16,24},{24,16},{1,9},{9,1},{17,25},{25,17},{2,10},{10... | collective-permute-start | bytes 1622024 | tf_op jit(solution)/shard_map/ppermute | solution.py:20
  84.6 23.7 %collective-permute-start.7 = (bf16[1,32,4096]{2,1,0:T(8,128)(2,1)S(1)}, bf16[1,32,4096]{2,1,0:T(8,128)(2,1)S(1)}, u32[]{:S(2)}, u32[]{:S(2)}) collective-permute-start(bf16[1,32,4096]{2,1,0:T(8,128)(2,1)S(1)} %split.79), channel_id=1, source_target_pairs={{0,16},{16,0},{8,24},{24,8},{1,17},{17,1},{9,25},{25,9},{2,18},{18... | collective-permute-start | bytes 786440 | tf_op jit(solution)/shard_map/ppermute | solution.py:20
  100.2 14.9 %collective-permute-start.15 = (bf16[2,32,4096]{2,1,0:T(8,128)(2,1)S(1)}, bf16[2,32,4096]{2,1,0:T(8,128)(2,1)S(1)}, u32[]{:S(2)}, u32[]{:S(2)}) collective-permute-start(bf16[2,32,4096]{2,1,0:T(8,128)(2,1)S(1)} %bitcast.68), channel_id=1, source_target_pairs={{0,16},{16,0},{8,24},{24,8},{1,17},{17,1},{9,25},{25,9},{2,18},{18... | collective-permute-start | bytes 1572872 | tf_op jit(solution)/shard_map/ppermute | solution.py:20
  107.0 14.0 %collective-permute-start.19 = (bf16[2,32,4096]{2,1,0:T(8,128)(2,1)S(1)}, bf16[2,32,4096]{2,1,0:T(8,128)(2,1)S(1)}, u32[]{:S(2)}, u32[]{:S(2)}) collective-permute-start(bf16[2,32,4096]{2,1,0:T(8,128)(2,1)S(1)} %bitcast.70), channel_id=1, source_target_pairs={{0,8},{8,0},{16,24},{24,16},{1,9},{9,1},{17,25},{25,17},{2,10},{10... | collective-permute-start | bytes 1572872 | tf_op jit(solution)/shard_map/ppermute | solution.py:20
  107.7 18.0 %collective-permute-start.22 = (bf16[2,32,4096]{2,1,0:T(8,128)(2,1)S(1)}, bf16[2,32,4096]{2,1,0:T(8,128)(2,1)S(1)}, u32[]{:S(2)}, u32[]{:S(2)}) collective-permute-start(bf16[2,32,4096]{2,1,0:T(8,128)(2,1)S(1)} %bitcast.69), channel_id=1, source_target_pairs={{0,16},{16,0},{8,24},{24,8},{1,17},{17,1},{9,25},{25,9},{2,18},{18... | collective-permute-start | bytes 1572872 | tf_op jit(solution)/shard_map/ppermute | solution.py:20
  108.3 20.3 %collective-permute-start.8 = (bf16[32,4096]{1,0:T(8,128)(2,1)S(1)}, bf16[32,4096]{1,0:T(8,128)(2,1)S(1)}, u32[]{:S(2)}, u32[]{:S(2)}) collective-permute-start(bf16[32,4096]{1,0:T(8,128)(2,1)S(1)} %fusion.25), channel_id=1, source_target_pairs={{0,4},{1,5},{2,6},{3,7},{4,0},{5,1},{6,2},{7,3},{8,12},{9,13},{10,... | collective-permute-start | bytes 786440 | tf_op jit(solution)/shard_map/ppermute | solution.py:173
  115.2 22.4 %copy-start.1 = (bf16[32,4096]{1,0:T(8,128)(2,1)S(1)}, bf16[32,4096]{1,0:T(8,128)(2,1)}, u32[]{:S(2)}) copy-start(bf16[32,4096]{1,0:T(8,128)(2,1)} %param.9) | copy-start | bytes 786436
  115.3 11.2 %collective-permute-start.16 = (bf16[1,32,4096]{2,1,0:T(8,128)(2,1)S(1)}, bf16[1,32,4096]{2,1,0:T(8,128)(2,1)S(1)}, u32[]{:S(2)}, u32[]{:S(2)}) collective-permute-start(bf16[1,32,4096]{2,1,0:T(8,128)(2,1)S(1)} %split.83), channel_id=1, source_target_pairs={{0,8},{8,0},{16,24},{24,16},{1,9},{9,1},{17,25},{25,17},{2,10},{10... | collective-permute-start | bytes 786440 | tf_op jit(solution)/shard_map/ppermute | solution.py:20
  121.1 7.3 %collective-permute-start.20 = (bf16[1,32,4096]{2,1,0:T(8,128)(2,1)S(1)}, bf16[1,32,4096]{2,1,0:T(8,128)(2,1)S(1)}, u32[]{:S(2)}, u32[]{:S(2)}) collective-permute-start(bf16[1,32,4096]{2,1,0:T(8,128)(2,1)S(1)} %split.85), channel_id=1, source_target_pairs={{0,16},{16,0},{8,24},{24,8},{1,17},{17,1},{9,25},{25,9},{2,18},{18... | collective-permute-start | bytes 786440 | tf_op jit(solution)/shard_map/ppermute | solution.py:20
  125.8 6.4 %collective-permute-start.23 = (bf16[1,32,4096]{2,1,0:T(8,128)(2,1)S(1)}, bf16[1,32,4096]{2,1,0:T(8,128)(2,1)S(1)}, u32[]{:S(2)}, u32[]{:S(2)}) collective-permute-start(bf16[1,32,4096]{2,1,0:T(8,128)(2,1)S(1)} %split.87), channel_id=1, source_target_pairs={{0,8},{8,0},{16,24},{24,16},{1,9},{9,1},{17,25},{25,17},{2,10},{10... | collective-permute-start | bytes 786440 | tf_op jit(solution)/shard_map/ppermute | solution.py:20
  126.5 8.4 %collective-permute-start.17 = (bf16[32,4096]{1,0:T(8,128)(2,1)S(1)}, bf16[32,4096]{1,0:T(8,128)(2,1)S(1)}, u32[]{:S(2)}, u32[]{:S(2)}) collective-permute-start(bf16[32,4096]{1,0:T(8,128)(2,1)S(1)} %fusion.26), channel_id=1, source_target_pairs={{0,6},{1,7},{2,4},{3,5},{4,2},{5,3},{6,0},{7,1},{8,14},{9,15},{10,... | collective-permute-start | bytes 786440 | tf_op jit(solution)/shard_map/ppermute | solution.py:173
  128.5 9.1 %collective-permute-start.21 = (bf16[32,4096]{1,0:T(8,128)(2,1)S(1)}, bf16[32,4096]{1,0:T(8,128)(2,1)S(1)}, u32[]{:S(2)}, u32[]{:S(2)}) collective-permute-start(bf16[32,4096]{1,0:T(8,128)(2,1)S(1)} %fusion.27), channel_id=1, source_target_pairs={{0,2},{1,3},{2,0},{3,1},{4,6},{5,7},{6,4},{7,5},{8,10},{9,11},{10,... | collective-permute-start | bytes 786440 | tf_op jit(solution)/shard_map/ppermute | solution.py:173

commit v5 on v4

--- a/solution.py
+++ b/solution.py
@@ -91,18 +91,14 @@
     return mixed.astype(jnp.bfloat16)
 
 
-def gather_groups(block, order):
-    for bit in order:
-        block = jnp.concatenate([block, from_partner(block, "dp", bit)], axis=0)
-    return block
-
-
-def sum_groups(block, order):
-    for bit in reversed(order):
-        kept, sent = jnp.split(block, 2, axis=0)
-        arrived = from_partner(sent, "dp", bit)
-        block = (kept.astype(jnp.float32) + arrived.astype(jnp.float32)).astype(jnp.bfloat16)
-    return block
+def gather_step(block, bit):
+    return jnp.concatenate([block, from_partner(block, "dp", bit)], axis=0)
+
+
+def sum_step(block, bit):
+    kept, sent = jnp.split(block, 2, axis=0)
+    arrived = from_partner(sent, "dp", bit)
+    return (kept.astype(jnp.float32) + arrived.astype(jnp.float32)).astype(jnp.bfloat16)
 
 
 def scaled(block, scale):
@@ -168,6 +164,87 @@
     )(scales, down)
 
 
+def silu(v):
+    return v / (1 + jnp.exp(-v))
+
+
+def ffn_kernel(count, experts, in_steps, *refs):
+    own_expert, refs = refs[0], refs[1:]
+    rows_refs, refs = refs[:count], refs[count:]
+    in_own, in_other, down_own, down_other = refs[:4]
+    out_refs, (parts, hidden, weight) = refs[4 : 4 + count], refs[4 + count :]
+    step = pl.program_id(0)
+    depth, width = in_own.shape
+    half = width // 2
+    model_width = in_steps * depth
+
+    def strip(first, size):
+        cols = pl.ds(first, size)
+        return jnp.concatenate([ref[:, cols] for ref in rows_refs], axis=0)
+
+    @pl.when(step < in_steps)
+    def _():
+        rows = strip(pl.multiple_of(step * depth, depth), depth)
+        for place, w_in in enumerate((in_own, in_other)):
+            part = jnp.dot(rows, w_in[...], preferred_element_type=jnp.float32)
+            before = jnp.where(step == 0, 0.0, parts[place])
+            parts[place] = before + part
+
+    @pl.when(step == in_steps)
+    def _():
+        for place in range(2):
+            gate_part, up_part = parts[place][:, :half], parts[place][:, half:]
+            value = (silu(gate_part) * up_part).astype(jnp.bfloat16)
+            hidden[:, place * half : (place + 1) * half] = value
+        marks = strip(model_width, rows_refs[0].shape[1] - model_width).astype(jnp.float32)
+        column = lax.broadcasted_iota(jnp.int32, marks.shape, 1)
+        chosen = (column == own_expert[0]) | (column == own_expert[0] + experts)
+        weight[...] = jnp.sum(jnp.where(chosen, marks, 0.0), axis=1, keepdims=True)
+
+    @pl.when(step >= in_steps)
+    def _():
+        value = jnp.dot(hidden[:, :half], down_own[...], preferred_element_type=jnp.float32)
+        value += jnp.dot(hidden[:, half:], down_other[...], preferred_element_type=jnp.float32)
+        value = (value * weight[...]).astype(jnp.bfloat16)
+        size = out_refs[0].shape[0]
+        for place, out_ref in enumerate(out_refs):
+            out_ref[...] = value[place * size : (place + 1) * size]
+
+
+def expert_layer(rows, own_expert, experts, in_own, in_other, down_own, down_other):
+    count, (size, payload_width) = len(rows), rows[0].shape
+    model_width, width = in_own.shape
+    half = width // 2
+    depth, strip = min(4 * BLOCK, model_width), min(8 * BLOCK, model_width)
+    in_steps, out_steps = model_width // depth, model_width // strip
+    whole = pl.BlockSpec((size, payload_width), lambda i: (0, 0))
+    w_in = pl.BlockSpec((depth, width), lambda i: (jnp.minimum(i, in_steps - 1), 0))
+    at_strip = lambda i: (0, jnp.maximum(i - in_steps, 0))
+    w_down = pl.BlockSpec((half, strip), at_strip)
+    total = count * size
+    return pl.pallas_call(
+        functools.partial(ffn_kernel, count, experts, in_steps),
+        grid=(in_steps + out_steps,),
+        in_specs=[pl.BlockSpec(memory_space=pltpu.SMEM)]
+        + [whole] * count
+        + [w_in, w_in, w_down, w_down],
+        out_specs=[pl.BlockSpec((size, strip), at_strip)] * count,
+        out_shape=[jax.ShapeDtypeStruct((size, model_width), jnp.bfloat16)] * count,
+        scratch_shapes=[
+            pltpu.VMEM((2, total, width), jnp.float32),
+            pltpu.VMEM((total, width), jnp.bfloat16),
+            pltpu.VMEM((total, 1), jnp.float32),
+        ],
+        cost_estimate=pl.CostEstimate(
+            flops=6 * total * model_width * width,
+            bytes_accessed=6 * model_width * width + 4 * total * model_width,
+            transcendentals=total * width,
+        ),
+        compiler_params=pltpu.CompilerParams(vmem_limit_bytes=40 * 1024 * 1024),
+        name="expert_layer",
+    )(own_expert, *rows, in_own, in_other, down_own, down_other)
+
+
 def across_chips(block, far):
     count = lax.axis_size("expert")
     return lax.ppermute(block, "expert", [(low, low ^ 2 * far) for low in range(count)])
@@ -190,65 +267,68 @@
     pad = jnp.zeros((token_count, extra - 2 * expert_count), jnp.bfloat16)
     payload = jnp.concatenate([tokens, high, low, pad], axis=1)
 
-    route = [0, *range(2, pair_count), 1][:pair_count]
-    order_of = {far: orders[place % 2] for place, far in enumerate(route)}
+    together = lax.optimization_barrier
     step = 2
-    blocks = {0: payload[None]}
-    for far in route[1:step]:
-        blocks[far] = across_chips(payload, far)[None]
-    blocks[0] = gather_groups(blocks[0], order_of[0][:1])
-
-    gate_own, up_own, payload = lax.optimization_barrier((gate_q[0], up_q[0], payload))
+    pairs = [range(first, min(first + step, pair_count)) for first in range(0, pair_count, step)]
+    near = {0: payload[None]}
+    for far in pairs[0][1:]:
+        near[far] = across_chips(payload, far)[None]
+
+    gate_own, up_own, payload = together((gate_q[0], up_q[0], payload))
     hidden_half = gate_q.shape[2]
     in_own = dequantize_in(gate_own, up_own, gate_scale.reshape(-1), up_scale.reshape(-1))
-    blocks, payload, in_own, down_half = lax.optimization_barrier(
-        (blocks, payload, in_own, down_q[0])
-    )
+    near, payload, in_own, down_half = together((near, payload, in_own, down_q[0]))
     in_other = from_partner(in_own, "expert", 0)
-    for far in route[step:]:
-        blocks[far] = across_chips(payload, far)[None]
     down_own = dequantize_down(down_half, down_scale.reshape(-1))
-    down_other = from_partner(down_own, "expert", 0)
-    down_both = jnp.concatenate([down_own, down_other], axis=0)
-
-    def ffn(rows):
-        inputs = rows[:, :model_width]
-        marks = rows[:, model_width:].astype(jnp.float32)
-        column = jnp.arange(extra, dtype=jnp.int32)[None, :]
-        chosen = (column == own_expert) | (column == own_expert + expert_count)
-        row_weight = jnp.sum(jnp.where(chosen, marks, 0.0), axis=1)
-        hidden = []
-        for w_in in (in_own, in_other):
-            parts = jnp.dot(inputs, w_in, preferred_element_type=jnp.float32)
-            hidden.append(
-                (jax.nn.silu(parts[:, :hidden_half]) * parts[:, hidden_half:]).astype(jnp.bfloat16)
-            )
-        hidden = jnp.concatenate(hidden, axis=1)
-        value = jnp.dot(hidden, down_both, preferred_element_type=jnp.float32)
-        return (value * row_weight[:, None]).astype(jnp.bfloat16)
-
-    outs = {}
-    for first in range(0, pair_count, step):
-        fars = route[first : first + step]
-        for far in fars:
-            blocks[far] = gather_groups(blocks[far], order_of[far][int(far == 0) : -1])
-        if outs:
-            tied = [blocks[far] for far in fars]
-            outs[0], tied = lax.optimization_barrier((outs[0], tied))
-            for far, block in zip(fars, tied):
-                blocks[far] = block
-        for far in fars:
-            blocks[far] = gather_groups(blocks[far], order_of[far][-1:])
-        for far in fars:
-            outs[far] = ffn(blocks[far].reshape(-1, blocks[far].shape[-1]))
-    outs[0], outs[1] = lax.optimization_barrier((outs[0], outs[1]))
+
+    place = jnp.reshape(own_expert, (1,)).astype(jnp.int32)
+    outs, weights = {}, None
+    for number, pair in enumerate(pairs):
+        following = list(pairs[number + 1]) if number + 1 < len(pairs) else []
+        later, rows_before = {}, None
+        for turn in range(len(bits)):
+            if turn == 0:
+                for far in following:
+                    low = far & -far
+                    block = payload if far == low else later[far ^ low][0]
+                    later[far] = across_chips(block, low)[None]
+            near = {far: gather_step(near[far], orders[far % 2][turn]) for far in pair}
+            if number == 0 and turn == 0:
+                near, down_own = together((near, down_own))
+            elif number == 0 and turn == len(bits) - 1:
+                near, later, in_other, down_own = together((near, later, in_other, down_own))
+            elif number == 1 and turn == 0:
+                down_other = from_partner(down_own, "expert", 0)
+                near, waiting, down_other = together((near, waiting, down_other))
+                weights = (in_own, in_other, down_own, down_other)
+        if number == 0:
+            waiting = near
+        else:
+            for held in ([waiting, near] if number == 1 else [near]):
+                if number == 1 and held is near:
+                    near, outs = together((near, outs))
+                rows = [held[far].reshape(-1, held[far].shape[-1]) for far in held]
+                for far, out in zip(held, expert_layer(rows, place, expert_count, *weights)):
+                    outs[far] = out
+        near = later
+
     total = tokens.astype(jnp.float32)
-    for far in route[1:] + route[:1]:
-        out = outs[far].reshape(group_count, token_count, model_width)
-        block = sum_groups(out, order_of[far])[0]
-        if far > 0:
-            block = across_chips(block, far)
-        total = total + block.astype(jnp.float32)
+    sums = {far: out.reshape(group_count, token_count, model_width) for far, out in outs.items()}
+    for pair in pairs[::-1]:
+        for turn in reversed(range(len(bits))):
+            for far in pair:
+                sums[far] = sum_step(sums[far], orders[far % 2][turn])
+            sums = together(sums)
+        for far in reversed(pair):
+            block, low = sums.pop(far), far & -far
+            if far == 0:
+                total = total + block[0].astype(jnp.float32)
+            elif far == low:
+                total = total + across_chips(block[0], low).astype(jnp.float32)
+            else:
+                arrived = across_chips(block, low)
+                block = sums[far ^ low]
+                sums[far ^ low] = (block.astype(jnp.float32) + arrived.astype(jnp.float32)).astype(jnp.bfloat16)
     return total.astype(jnp.bfloat16)
 
 
@@ -256,7 +336,10 @@
     expert_count = lax.axis_size("dp") * lax.axis_size("expert") // 2
     token_count, top_count = expert_ids.shape
     capacity = 2 * token_count * top_count // expert_count
-    plan = by_rows if capacity < token_count else by_sums
+    group_count, pair_count = lax.axis_size("dp"), lax.axis_size("expert") // 2
+    powers = all(count & (count - 1) == 0 for count in (group_count, pair_count))
+    dense = capacity >= token_count and powers and min(group_count, pair_count) >= 4
+    plan = by_sums if dense else by_rows
     return plan(tokens, expert_ids, *weights)
 
 

time: 139 us -> 143 us (1.029)
  matrix products: 27.5 us -> 0 us
  Pallas kernels: 10.8 us -> 37.4 us
  other arithmetic: 3.79 us -> 6.76 us
  starting transfers between devices: 24 us -> 25.9 us
    dot_general x12 -> x0, matrix products: 27.5 us -> none  [the longest x8 22.5 us: ffn(): parts = jnp.dot(inputs, w_in, preferred_element_type=jnp.float32)]
    pallas_call x0 -> x2, Pallas kernels: none -> 26.5 us  [expert_layer(): pl.pallas_call(functools.partial(ffn_kernel, count, experts, in_steps), g...]
    ppermute x18, waiting for transfers between devices: 52.9 us -> 43.2 us  [from_partner(): return lax.ppermute(block, axis, route)]
    ppermute x6, waiting for transfers between devices: 14 us -> 22.7 us  [across_chips(): lax.ppermute(block, 'expert', [(low, low ^ 2 * far) for low in range(coun...]
    concatenate x8 -> x6, other arithmetic: 0.7 us -> 4.37 us  [gather_step(): return jnp.concatenate([block, from_partner(block, 'dp', bit)], axis=0)]
  transfers between devices with their start and end apart: 24 -> 24, of which waited for: 14 -> 16; matrix products, arithmetic and copies ran while one was open for 23% -> 6% of each run, Pallas kernels for 8% -> 17%
where the time goes in v5:
time: 143 us; the launch traced here: 142 us
  waiting for transfers between devices  66 us (46%)
  Pallas kernels  37.4 us (26%)
  starting transfers between devices  25.9 us (18%)
  other arithmetic  6.76 us (5%)
  local copies, waits for them, and re-layouts  5.8 us (4%)
    ppermute x18, waiting for transfers between devices, from_partner(): return lax.ppermute(block, axis, route)  43.2 us
    pallas_call x2, Pallas kernels, expert_layer(): pl.pallas_call(functools.partial(ffn_kernel, count, experts, in_steps), g...  26.5 us
    ppermute x6, waiting for transfers between devices, across_chips(): lax.ppermute(block, 'expert', [(low, low ^ 2 * far) for low in range(coun...  22.7 us
    ppermute x18, starting transfers between devices, from_partner(): return lax.ppermute(block, axis, route)  17.7 us
    ppermute x6, starting transfers between devices, across_chips(): lax.ppermute(block, 'expert', [(low, low ^ 2 * far) for low in range(coun...  8.18 us
    pallas_call x1, Pallas kernels, dequantize_in(): pl.pallas_call(functools.partial(in_kernel, cols // BLOCK), grid=(rows //...  6.28 us
    pallas_call x1, Pallas kernels, dequantize_down(): pl.pallas_call(functools.partial(down_kernel, cols // BLOCK), grid=(cols...  4.56 us
    concatenate x6, other arithmetic, gather_step(): return jnp.concatenate([block, from_partner(block, 'dp', bit)], axis=0)  4.37 us
  transfers between devices with their start and end apart: 24, of which 16 were waited for; matrix products, arithmetic and copies ran while one was open for 6% of the time, Pallas kernels for 17%

profile of v5, /device:TPU:0, one launch (start us, length us, event | category | flops | bytes accessed | tf_op | source)
XLA Modules:
  0.0 142.0 jit_solution(17739989135474463074)
XLA Ops:
  2.0 3.1 %collective-permute-start = (bf16[32,4224]{1,0:T(8,128)(2,1)S(1)}, bf16[32,4224]{1,0:T(8,128)(2,1)S(1)}, u32[]{:S(2)}, u32[]{:S(2)}) collective-permute-start(bf16[32,4224]{1,0:T(8,128)(2,1)S(1)} %concatenate.27), channel_id=1, source_target_pairs={{0,2},{1,3},{2,0},{3,1},{4,6},{5,7},{6,4},{7,5},{8,10},{9,11},{10,... | collective-permute-start | bytes 811016 | tf_op jit(solution)/shard_map/ppermute | solution.py:250
  7.8 6.3 %dequantize_in.1.refs_3_ = bf16[4096,768]{1,0:T(8,128)(2,1)} custom-call(f32[96]{0:T(128)} %reshape.44.gate_scales, f32[96]{0:T(128)} %reshape.45.up_scales, bf16[4096,384]{1,0:T(8,128)(2,1)} %bitcast.35, bf16[4096,384]{1,0:T(8,128)(2,1)} %bitcast.36), custom_call_target="tpu_custom_call" | custom-call | flops 3145728 | bytes 12582912 | tf_op jit(solution)/shard_map/dequantize_in/pallas_call | solution.py:126
  14.1 1.6 %collective-permute-start.1 = (bf16[1,32,4224]{2,1,0:T(8,128)(2,1)S(1)}, bf16[1,32,4224]{2,1,0:T(8,128)(2,1)S(1)}, u32[]{:S(2)}, u32[]{:S(2)}) collective-permute-start(bf16[1,32,4224]{2,1,0:T(8,128)(2,1)S(1)} %bitcast.39), channel_id=1, source_target_pairs={{0,8},{8,0},{16,24},{24,16},{1,9},{9,1},{17,25},{25,17},{2,10},{10... | collective-permute-start | bytes 811016 | tf_op jit(solution)/shard_map/ppermute | solution.py:20
  16.3 1.5 %collective-permute-start.2 = (bf16[1,32,4224]{2,1,0:T(8,128)(2,1)S(1)}, bf16[1,32,4224]{2,1,0:T(8,128)(2,1)S(1)}, u32[]{:S(2)}, u32[]{:S(2)}) collective-permute-start(bf16[1,32,4224]{2,1,0:T(8,128)(2,1)S(1)} %bitcast.47), channel_id=1, source_target_pairs={{0,16},{16,0},{8,24},{24,8},{1,17},{17,1},{9,25},{25,9},{2,18},{18... | collective-permute-start | bytes 811016 | tf_op jit(solution)/shard_map/ppermute | solution.py:20
  17.8 4.6 %dequantize_down.1.refs_5_ = bf16[384,4096]{1,0:T(8,128)(2,1)} custom-call(f32[96]{0:T(128)} %reshape.46.scales, bf16[384,4096]{1,0:T(8,128)(2,1)} %bitcast.34), custom_call_target="tpu_custom_call" | custom-call | flops 1572864 | bytes 6291456 | tf_op jit(solution)/shard_map/dequantize_down/pallas_call | solution.py:154
  23.1 1.8 %collective-permute-done.2 = bf16[1,32,4224]{2,1,0:T(8,128)(2,1)S(1)} collective-permute-done((bf16[1,32,4224]{2,1,0:T(8,128)(2,1)S(1)}, bf16[1,32,4224]{2,1,0:T(8,128)(2,1)S(1)}, u32[]{:S(2)}, u32[]{:S(2)}) %collective-permute-start.2) | collective-permute-done | bytes 270368 | tf_op jit(solution)/shard_map/ppermute | solution.py:20
  24.9 1.6 %collective-permute-start.3 = (bf16[2,32,4224]{2,1,0:T(8,128)(2,1)S(1)}, bf16[2,32,4224]{2,1,0:T(8,128)(2,1)S(1)}, u32[]{:S(2)}, u32[]{:S(2)}) collective-permute-start(bf16[2,32,4224]{2,1,0:T(8,128)(2,1)S(1)} %pad_maximum_fusion.2), channel_id=1, source_target_pairs={{0,16},{16,0},{8,24},{24,8},{1,17},{17,1},{9,25},{25,9},{2,18},{18... | collective-permute-start | bytes 1622024 | tf_op jit(solution)/shard_map/ppermute | solution.py:20
  26.5 2.6 %collective-permute-start.5 = (bf16[32,4224]{1,0:T(8,128)(2,1)S(1)}, bf16[32,4224]{1,0:T(8,128)(2,1)S(1)}, u32[]{:S(2)}, u32[]{:S(2)}) collective-permute-start(bf16[32,4224]{1,0:T(8,128)(2,1)S(1)} %concatenate.27), channel_id=1, source_target_pairs={{0,4},{1,5},{2,6},{3,7},{4,0},{5,1},{6,2},{7,3},{8,12},{9,13},{10,... | collective-permute-start | bytes 811016 | tf_op jit(solution)/shard_map/ppermute | solution.py:250
  29.6 10.9 %collective-permute-done.5 = bf16[32,4224]{1,0:T(8,128)(2,1)S(1)} collective-permute-done((bf16[32,4224]{1,0:T(8,128)(2,1)S(1)}, bf16[32,4224]{1,0:T(8,128)(2,1)S(1)}, u32[]{:S(2)}, u32[]{:S(2)}) %collective-permute-start.5) | collective-permute-done | bytes 270368 | tf_op jit(solution)/shard_map/ppermute | solution.py:250
  40.5 1.1 pad_maximum_fusion
  42.0 1.1 pad_maximum_fusion.1
  43.1 5.8 %collective-permute-done.6 = bf16[32,4224]{1,0:T(8,128)(2,1)S(1)} collective-permute-done((bf16[32,4224]{1,0:T(8,128)(2,1)S(1)}, bf16[32,4224]{1,0:T(8,128)(2,1)S(1)}, u32[]{:S(2)}, u32[]{:S(2)}) %collective-permute-start.6) | collective-permute-done | bytes 270368 | tf_op jit(solution)/shard_map/ppermute | solution.py:250
  50.7 7.9 %collective-permute-done.8 = bf16[1,32,4224]{2,1,0:T(8,128)(2,1)} collective-permute-done((bf16[1,32,4224]{2,1,0:T(8,128)(2,1)S(1)}, bf16[1,32,4224]{2,1,0:T(8,128)(2,1)}, u32[]{:S(2)}, u32[]{:S(2)}) %collective-permute-start.8) | collective-permute-done | bytes 270368 | tf_op jit(solution)/shard_map/ppermute | solution.py:20
  62.1 13.3 %expert_layer.2 = (bf16[128,4096]{1,0:T(8,128)(2,1)S(1)}, bf16[128,4096]{1,0:T(8,128)(2,1)S(1)}) custom-call(s32[1]{0:T(128)} %bitcast.7.refs_0_, bf16[128,4224]{1,0:T(8,128)(2,1)S(1)} %bitcast.26, bf16[128,4224]{1,0:T(8,128)(2,1)S(1)} %bitcast.27, bf16[4096,768]{1,0:T(8,128)(2,1)} %dequantize_in.1.refs_3_, ...), custom_call_target="tpu_custom_call" | custom-call | flops 4831838208 | bytes 23068672 | tf_op jit(solution)/shard_map/expert_layer/pallas_call | solution.py:225
  75.6 13.3 %expert_layer.3 = (bf16[128,4096]{1,0:T(8,128)(2,1)S(1)}, bf16[128,4096]{1,0:T(8,128)(2,1)S(1)}) custom-call(s32[1]{0:T(128)} %bitcast.7.refs_0_, bf16[128,4224]{1,0:T(8,128)(2,1)S(1)} %bitcast.29, bf16[128,4224]{1,0:T(8,128)(2,1)S(1)} %bitcast.28, bf16[4096,768]{1,0:T(8,128)(2,1)} %dequantize_in.1.refs_3_, ...), custom_call_target="tpu_custom_call" | custom-call | flops 4831838208 | bytes 23068672 | tf_op jit(solution)/shard_map/expert_layer/pallas_call | solution.py:225
  88.9 1.6 %collective-permute-start.13 = (bf16[2,32,4096]{2,1,0:T(8,128)(2,1)S(1)}, bf16[2,32,4096]{2,1,0:T(8,128)(2,1)S(1)}, u32[]{:S(2)}, u32[]{:S(2)}) collective-permute-start(bf16[2,32,4096]{2,1,0:T(8,128)(2,1)S(1)} %bitcast.41), channel_id=1, source_target_pairs={{0,16},{16,0},{8,24},{24,8},{1,17},{17,1},{9,25},{25,9},{2,18},{18... | collective-permute-start | bytes 1572872 | tf_op jit(solution)/shard_map/ppermute | solution.py:20
  90.6 1.3 collective-permute-start.14
  91.9 9.8 %collective-permute-done.13 = bf16[2,32,4096]{2,1,0:T(8,128)(2,1)S(1)} collective-permute-done((bf16[2,32,4096]{2,1,0:T(8,128)(2,1)S(1)}, bf16[2,32,4096]{2,1,0:T(8,128)(2,1)S(1)}, u32[]{:S(2)}, u32[]{:S(2)}) %collective-permute-start.13) | collective-permute-done | bytes 524320 | tf_op jit(solution)/shard_map/ppermute | solution.py:20
  101.9 1.2 collective-permute-done.14
  103.9 1.5 %collective-permute-start.15 = (bf16[1,32,4096]{2,1,0:T(8,128)(2,1)S(1)}, bf16[1,32,4096]{2,1,0:T(8,128)(2,1)S(1)}, u32[]{:S(2)}, u32[]{:S(2)}) collective-permute-start(bf16[1,32,4096]{2,1,0:T(8,128)(2,1)S(1)} %split.59), channel_id=1, source_target_pairs={{0,8},{8,0},{16,24},{24,16},{1,9},{9,1},{17,25},{25,17},{2,10},{10... | collective-permute-start | bytes 786440 | tf_op jit(solution)/shard_map/ppermute | solution.py:20
  105.4 4.3 %collective-permute-done.16 = bf16[1,32,4096]{2,1,0:T(8,128)(2,1)S(1)} collective-permute-done((bf16[1,32,4096]{2,1,0:T(8,128)(2,1)S(1)}, bf16[1,32,4096]{2,1,0:T(8,128)(2,1)S(1)}, u32[]{:S(2)}, u32[]{:S(2)}) %collective-permute-start.16) | collective-permute-done | bytes 262176 | tf_op jit(solution)/shard_map/ppermute | solution.py:20
  109.8 1.1 collective-permute-done.15
  111.0 1.3 collective-permute-start.20
  112.6 1.6 %collective-permute-start.19 = (bf16[2,32,4096]{2,1,0:T(8,128)(2,1)S(1)}, bf16[2,32,4096]{2,1,0:T(8,128)(2,1)S(1)}, u32[]{:S(2)}, u32[]{:S(2)}) collective-permute-start(bf16[2,32,4096]{2,1,0:T(8,128)(2,1)S(1)} %split.63), channel_id=1, source_target_pairs={{0,16},{16,0},{8,24},{24,8},{1,17},{17,1},{9,25},{25,9},{2,18},{18... | collective-permute-start | bytes 1572872 | tf_op jit(solution)/shard_map/ppermute | solution.py:20
  114.2 7.3 %collective-permute-done.20 = bf16[2,32,4096]{2,1,0:T(8,128)(2,1)S(1)} collective-permute-done((bf16[2,32,4096]{2,1,0:T(8,128)(2,1)S(1)}, bf16[2,32,4096]{2,1,0:T(8,128)(2,1)S(1)}, u32[]{:S(2)}, u32[]{:S(2)}) %collective-permute-start.20) | collective-permute-done | bytes 524320 | tf_op jit(solution)/shard_map/ppermute | solution.py:20
  121.7 2.8 %collective-permute-done.19 = bf16[2,32,4096]{2,1,0:T(8,128)(2,1)S(1)} collective-permute-done((bf16[2,32,4096]{2,1,0:T(8,128)(2,1)S(1)}, bf16[2,32,4096]{2,1,0:T(8,128)(2,1)S(1)}, u32[]{:S(2)}, u32[]{:S(2)}) %collective-permute-start.19) | collective-permute-done | bytes 524320 | tf_op jit(solution)/shard_map/ppermute | solution.py:20
  124.7 1.6 %collective-permute-start.22 = (bf16[1,32,4096]{2,1,0:T(8,128)(2,1)S(1)}, bf16[1,32,4096]{2,1,0:T(8,128)(2,1)S(1)}, u32[]{:S(2)}, u32[]{:S(2)}) collective-permute-start(bf16[1,32,4096]{2,1,0:T(8,128)(2,1)S(1)} %split.69), channel_id=1, source_target_pairs={{0,16},{16,0},{8,24},{24,8},{1,17},{17,1},{9,25},{25,9},{2,18},{18... | collective-permute-start | bytes 786440 | tf_op jit(solution)/shard_map/ppermute | solution.py:20
  126.4 1.9 %collective-permute-start.18 = (bf16[32,4096]{1,0:T(8,128)(2,1)S(1)}, bf16[32,4096]{1,0:T(8,128)(2,1)S(1)}, u32[]{:S(2)}, u32[]{:S(2)}) collective-permute-start(bf16[32,4096]{1,0:T(8,128)(2,1)S(1)} %fusion.3), channel_id=1, source_target_pairs={{0,4},{1,5},{2,6},{3,7},{4,0},{5,1},{6,2},{7,3},{8,12},{9,13},{10,... | collective-permute-start | bytes 786440 | tf_op jit(solution)/shard_map/ppermute | solution.py:250
  128.8 2.3 %collective-permute-done.22 = bf16[1,32,4096]{2,1,0:T(8,128)(2,1)S(1)} collective-permute-done((bf16[1,32,4096]{2,1,0:T(8,128)(2,1)S(1)}, bf16[1,32,4096]{2,1,0:T(8,128)(2,1)S(1)}, u32[]{:S(2)}, u32[]{:S(2)}) %collective-permute-start.22) | collective-permute-done | bytes 262176 | tf_op jit(solution)/shard_map/ppermute | solution.py:20
  131.2 3.5 %collective-permute-done.21 = bf16[1,32,4096]{2,1,0:T(8,128)(2,1)S(1)} collective-permute-done((bf16[1,32,4096]{2,1,0:T(8,128)(2,1)S(1)}, bf16[1,32,4096]{2,1,0:T(8,128)(2,1)S(1)}, u32[]{:S(2)}, u32[]{:S(2)}) %collective-permute-start.21) | collective-permute-done | bytes 262176 | tf_op jit(solution)/shard_map/ppermute | solution.py:20
  135.1 1.5 %collective-permute-done.18 = bf16[32,4096]{1,0:T(8,128)(2,1)S(1)} collective-permute-done((bf16[32,4096]{1,0:T(8,128)(2,1)S(1)}, bf16[32,4096]{1,0:T(8,128)(2,1)S(1)}, u32[]{:S(2)}, u32[]{:S(2)}) %collective-permute-start.18) | collective-permute-done | bytes 262176 | tf_op jit(solution)/shard_map/ppermute | solution.py:250
  136.6 4.6 %collective-permute-done.23 = bf16[32,4096]{1,0:T(8,128)(2,1)S(1)} collective-permute-done((bf16[32,4096]{1,0:T(8,128)(2,1)S(1)}, bf16[32,4096]{1,0:T(8,128)(2,1)S(1)}, u32[]{:S(2)}, u32[]{:S(2)}) %collective-permute-start.23) | collective-permute-done | bytes 262176 | tf_op jit(solution)/shard_map/ppermute | solution.py:250
  (71 shorter events, 16.2 us)
Async XLA Ops:
  2.0 12.1 %collective-permute-start = (bf16[32,4224]{1,0:T(8,128)(2,1)S(1)}, bf16[32,4224]{1,0:T(8,128)(2,1)S(1)}, u32[]{:S(2)}, u32[]{:S(2)}) collective-permute-start(bf16[32,4224]{1,0:T(8,128)(2,1)S(1)} %concatenate.27), channel_id=1, source_target_pairs={{0,2},{1,3},{2,0},{3,1},{4,6},{5,7},{6,4},{7,5},{8,10},{9,11},{10,... | collective-permute-start | bytes 811016 | tf_op jit(solution)/shard_map/ppermute | solution.py:250
  7.8 7.9 %copy-start.5 = (f32[1,3,32]{2,0,1:T(1,128)S(1)}, f32[1,3,32]{2,0,1:T(1,128)}, u32[]{:S(2)}) copy-start(f32[1,3,32]{2,0,1:T(1,128)} %param.17) | copy-start | bytes 1156
  14.1 34.8 %collective-permute-start.7 = (bf16[4096,768]{1,0:T(8,128)(2,1)}, bf16[4096,768]{1,0:T(8,128)(2,1)}, u32[]{:S(2)}, u32[]{:S(2)}) collective-permute-start(bf16[4096,768]{1,0:T(8,128)(2,1)} %dequantize_in.1.refs_3_), channel_id=1, source_target_pairs={{0,1},{1,0},{2,3},{3,2},{4,5},{5,4},{6,7},{7,6},{8,9},{9,8},{10,11... | collective-permute-start | bytes 18874376 | tf_op jit(solution)/shard_map/ppermute | solution.py:20
  14.1 8.9 %collective-permute-start.1 = (bf16[1,32,4224]{2,1,0:T(8,128)(2,1)S(1)}, bf16[1,32,4224]{2,1,0:T(8,128)(2,1)S(1)}, u32[]{:S(2)}, u32[]{:S(2)}) collective-permute-start(bf16[1,32,4224]{2,1,0:T(8,128)(2,1)S(1)} %bitcast.39), channel_id=1, source_target_pairs={{0,8},{8,0},{16,24},{24,16},{1,9},{9,1},{17,25},{25,17},{2,10},{10... | collective-permute-start | bytes 811016 | tf_op jit(solution)/shard_map/ppermute | solution.py:20
  16.3 8.5 %collective-permute-start.2 = (bf16[1,32,4224]{2,1,0:T(8,128)(2,1)S(1)}, bf16[1,32,4224]{2,1,0:T(8,128)(2,1)S(1)}, u32[]{:S(2)}, u32[]{:S(2)}) collective-permute-start(bf16[1,32,4224]{2,1,0:T(8,128)(2,1)S(1)} %bitcast.47), channel_id=1, source_target_pairs={{0,16},{16,0},{8,24},{24,8},{1,17},{17,1},{9,25},{25,9},{2,18},{18... | collective-permute-start | bytes 811016 | tf_op jit(solution)/shard_map/ppermute | solution.py:20
  24.9 15.6 %collective-permute-start.3 = (bf16[2,32,4224]{2,1,0:T(8,128)(2,1)S(1)}, bf16[2,32,4224]{2,1,0:T(8,128)(2,1)S(1)}, u32[]{:S(2)}, u32[]{:S(2)}) collective-permute-start(bf16[2,32,4224]{2,1,0:T(8,128)(2,1)S(1)} %pad_maximum_fusion.2), channel_id=1, source_target_pairs={{0,16},{16,0},{8,24},{24,8},{1,17},{17,1},{9,25},{25,9},{2,18},{18... | collective-permute-start | bytes 1622024 | tf_op jit(solution)/shard_map/ppermute | solution.py:20
  26.5 14.0 %collective-permute-start.5 = (bf16[32,4224]{1,0:T(8,128)(2,1)S(1)}, bf16[32,4224]{1,0:T(8,128)(2,1)S(1)}, u32[]{:S(2)}, u32[]{:S(2)}) collective-permute-start(bf16[32,4224]{1,0:T(8,128)(2,1)S(1)} %concatenate.27), channel_id=1, source_target_pairs={{0,4},{1,5},{2,6},{3,7},{4,0},{5,1},{6,2},{7,3},{8,12},{9,13},{10,... | collective-permute-start | bytes 811016 | tf_op jit(solution)/shard_map/ppermute | solution.py:250
  29.1 12.9 %collective-permute-start.4 = (bf16[2,32,4224]{2,1,0:T(8,128)(2,1)S(1)}, bf16[2,32,4224]{2,1,0:T(8,128)(2,1)S(1)}, u32[]{:S(2)}, u32[]{:S(2)}) collective-permute-start(bf16[2,32,4224]{2,1,0:T(8,128)(2,1)S(1)} %pad_maximum_fusion.3), channel_id=1, source_target_pairs={{0,8},{8,0},{16,24},{24,16},{1,9},{9,1},{17,25},{25,17},{2,10},{10... | collective-permute-start | bytes 1622024 | tf_op jit(solution)/shard_map/ppermute | solution.py:20
  40.5 8.4 %collective-permute-start.6 = (bf16[32,4224]{1,0:T(8,128)(2,1)S(1)}, bf16[32,4224]{1,0:T(8,128)(2,1)S(1)}, u32[]{:S(2)}, u32[]{:S(2)}) collective-permute-start(bf16[32,4224]{1,0:T(8,128)(2,1)S(1)} %collective-permute-done.5), channel_id=1, source_target_pairs={{0,2},{1,3},{2,0},{3,1},{4,6},{5,7},{6,4},{7,5},{8,10},{9,11},{10,... | collective-permute-start | bytes 811016 | tf_op jit(solution)/shard_map/ppermute | solution.py:250
  40.5 9.1 %copy-start = (bf16[384,4096]{1,0:T(8,128)(2,1)S(1)}, bf16[384,4096]{1,0:T(8,128)(2,1)}, u32[]{:S(2)}) copy-start(bf16[384,4096]{1,0:T(8,128)(2,1)} %dequantize_down.1.refs_5_) | copy-start | bytes 9437188
  48.9 0.7 copy-start.4
  49.6 11.0 %collective-permute-start.10 = (bf16[384,4096]{1,0:T(8,128)(2,1)S(1)}, bf16[384,4096]{1,0:T(8,128)(2,1)}, u32[]{:S(2)}, u32[]{:S(2)}) collective-permute-start(bf16[384,4096]{1,0:T(8,128)(2,1)S(1)} %copy-done), channel_id=1, source_target_pairs={{0,1},{1,0},{2,3},{3,2},{4,5},{5,4},{6,7},{7,6},{8,9},{9,8},{10,11... | collective-permute-start | bytes 9437192 | tf_op jit(solution)/shard_map/ppermute | solution.py:20
  49.6 9.0 %collective-permute-start.8 = (bf16[1,32,4224]{2,1,0:T(8,128)(2,1)S(1)}, bf16[1,32,4224]{2,1,0:T(8,128)(2,1)}, u32[]{:S(2)}, u32[]{:S(2)}) collective-permute-start(bf16[1,32,4224]{2,1,0:T(8,128)(2,1)S(1)} %bitcast.43), channel_id=1, source_target_pairs={{0,8},{8,0},{16,24},{24,16},{1,9},{9,1},{17,25},{25,17},{2,10},{10... | collective-permute-start | bytes 811016 | tf_op jit(solution)/shard_map/ppermute | solution.py:20
  50.1 11.9 %copy-start.1 = (bf16[4,32,4224]{2,1,0:T(8,128)(2,1)S(1)}, bf16[4,32,4224]{2,1,0:T(8,128)(2,1)}, u32[]{:S(2)}) copy-start(bf16[4,32,4224]{2,1,0:T(8,128)(2,1)} %pad_maximum_fusion) | copy-start | bytes 3244036
  50.1 11.9 %copy-start.2 = (bf16[4,32,4224]{2,1,0:T(8,128)(2,1)S(1)}, bf16[4,32,4224]{2,1,0:T(8,128)(2,1)}, u32[]{:S(2)}) copy-start(bf16[4,32,4224]{2,1,0:T(8,128)(2,1)} %pad_maximum_fusion.1) | copy-start | bytes 3244036
  50.2 9.5 %collective-permute-start.9 = (bf16[1,32,4224]{2,1,0:T(8,128)(2,1)}, bf16[1,32,4224]{2,1,0:T(8,128)(2,1)S(1)}, u32[]{:S(2)}, u32[]{:S(2)}) collective-permute-start(bf16[1,32,4224]{2,1,0:T(8,128)(2,1)} %bitcast.45), channel_id=1, source_target_pairs={{0,16},{16,0},{8,24},{24,8},{1,17},{17,1},{9,25},{25,9},{2,18},{18... | collective-permute-start | bytes 811016 | tf_op jit(solution)/shard_map/ppermute | solution.py:20
  60.7 14.8 %collective-permute-start.11 = (bf16[2,32,4224]{2,1,0:T(8,128)(2,1)S(1)}, bf16[2,32,4224]{2,1,0:T(8,128)(2,1)S(1)}, u32[]{:S(2)}, u32[]{:S(2)}) collective-permute-start(bf16[2,32,4224]{2,1,0:T(8,128)(2,1)S(1)} %pad_maximum_fusion.4), channel_id=1, source_target_pairs={{0,16},{16,0},{8,24},{24,8},{1,17},{17,1},{9,25},{25,9},{2,18},{18... | collective-permute-start | bytes 1622024 | tf_op jit(solution)/shard_map/ppermute | solution.py:20
  61.2 14.3 %collective-permute-start.12 = (bf16[2,32,4224]{2,1,0:T(8,128)(2,1)S(1)}, bf16[2,32,4224]{2,1,0:T(8,128)(2,1)S(1)}, u32[]{:S(2)}, u32[]{:S(2)}) collective-permute-start(bf16[2,32,4224]{2,1,0:T(8,128)(2,1)S(1)} %pad_maximum_fusion.5), channel_id=1, source_target_pairs={{0,8},{8,0},{16,24},{24,16},{1,9},{9,1},{17,25},{25,17},{2,10},{10... | collective-permute-start | bytes 1622024 | tf_op jit(solution)/shard_map/ppermute | solution.py:20
  88.9 12.8 %collective-permute-start.13 = (bf16[2,32,4096]{2,1,0:T(8,128)(2,1)S(1)}, bf16[2,32,4096]{2,1,0:T(8,128)(2,1)S(1)}, u32[]{:S(2)}, u32[]{:S(2)}) collective-permute-start(bf16[2,32,4096]{2,1,0:T(8,128)(2,1)S(1)} %bitcast.41), channel_id=1, source_target_pairs={{0,16},{16,0},{8,24},{24,8},{1,17},{17,1},{9,25},{25,9},{2,18},{18... | collective-permute-start | bytes 1572872 | tf_op jit(solution)/shard_map/ppermute | solution.py:20
  90.6 12.5 %collective-permute-start.14 = (bf16[2,32,4096]{2,1,0:T(8,128)(2,1)S(1)}, bf16[2,32,4096]{2,1,0:T(8,128)(2,1)S(1)}, u32[]{:S(2)}, u32[]{:S(2)}) collective-permute-start(bf16[2,32,4096]{2,1,0:T(8,128)(2,1)S(1)} %bitcast.42), channel_id=1, source_target_pairs={{0,8},{8,0},{16,24},{24,16},{1,9},{9,1},{17,25},{25,17},{2,10},{10... | collective-permute-start | bytes 1572872 | tf_op jit(solution)/shard_map/ppermute | solution.py:20
  103.3 6.4 %collective-permute-start.16 = (bf16[1,32,4096]{2,1,0:T(8,128)(2,1)S(1)}, bf16[1,32,4096]{2,1,0:T(8,128)(2,1)S(1)}, u32[]{:S(2)}, u32[]{:S(2)}) collective-permute-start(bf16[1,32,4096]{2,1,0:T(8,128)(2,1)S(1)} %split.61), channel_id=1, source_target_pairs={{0,16},{16,0},{8,24},{24,8},{1,17},{17,1},{9,25},{25,9},{2,18},{18... | collective-permute-start | bytes 786440 | tf_op jit(solution)/shard_map/ppermute | solution.py:20
  103.9 7.0 %collective-permute-start.15 = (bf16[1,32,4096]{2,1,0:T(8,128)(2,1)S(1)}, bf16[1,32,4096]{2,1,0:T(8,128)(2,1)S(1)}, u32[]{:S(2)}, u32[]{:S(2)}) collective-permute-start(bf16[1,32,4096]{2,1,0:T(8,128)(2,1)S(1)} %split.59), channel_id=1, source_target_pairs={{0,8},{8,0},{16,24},{24,16},{1,9},{9,1},{17,25},{25,17},{2,10},{10... | collective-permute-start | bytes 786440 | tf_op jit(solution)/shard_map/ppermute | solution.py:20
  111.0 10.6 %collective-permute-start.20 = (bf16[2,32,4096]{2,1,0:T(8,128)(2,1)S(1)}, bf16[2,32,4096]{2,1,0:T(8,128)(2,1)S(1)}, u32[]{:S(2)}, u32[]{:S(2)}) collective-permute-start(bf16[2,32,4096]{2,1,0:T(8,128)(2,1)S(1)} %split.65), channel_id=1, source_target_pairs={{0,8},{8,0},{16,24},{24,16},{1,9},{9,1},{17,25},{25,17},{2,10},{10... | collective-permute-start | bytes 1572872 | tf_op jit(solution)/shard_map/ppermute | solution.py:20
  112.2 14.1 %collective-permute-start.17 = (bf16[1,32,4096]{2,1,0:T(8,128)(2,1)S(1)}, bf16[1,32,4096]{2,1,0:T(8,128)(2,1)S(1)}, u32[]{:S(2)}, u32[]{:S(2)}) collective-permute-start(bf16[1,32,4096]{2,1,0:T(8,128)(2,1)S(1)} %add_convert_fusion.5), channel_id=1, source_target_pairs={{0,2},{1,3},{2,0},{3,1},{4,6},{5,7},{6,4},{7,5},{8,10},{9,11},{10,... | collective-permute-start | bytes 786440 | tf_op jit(solution)/shard_map/ppermute | solution.py:250
  112.6 11.9 %collective-permute-start.19 = (bf16[2,32,4096]{2,1,0:T(8,128)(2,1)S(1)}, bf16[2,32,4096]{2,1,0:T(8,128)(2,1)S(1)}, u32[]{:S(2)}, u32[]{:S(2)}) collective-permute-start(bf16[2,32,4096]{2,1,0:T(8,128)(2,1)S(1)} %split.63), channel_id=1, source_target_pairs={{0,16},{16,0},{8,24},{24,8},{1,17},{17,1},{9,25},{25,9},{2,18},{18... | collective-permute-start | bytes 1572872 | tf_op jit(solution)/shard_map/ppermute | solution.py:20
  124.7 6.4 %collective-permute-start.22 = (bf16[1,32,4096]{2,1,0:T(8,128)(2,1)S(1)}, bf16[1,32,4096]{2,1,0:T(8,128)(2,1)S(1)}, u32[]{:S(2)}, u32[]{:S(2)}) collective-permute-start(bf16[1,32,4096]{2,1,0:T(8,128)(2,1)S(1)} %split.69), channel_id=1, source_target_pairs={{0,16},{16,0},{8,24},{24,8},{1,17},{17,1},{9,25},{25,9},{2,18},{18... | collective-permute-start | bytes 786440 | tf_op jit(solution)/shard_map/ppermute | solution.py:20
  126.4 14.8 %copy-start.3 = (bf16[32,4096]{1,0:T(8,128)(2,1)S(1)}, bf16[32,4096]{1,0:T(8,128)(2,1)}, u32[]{:S(2)}) copy-start(bf16[32,4096]{1,0:T(8,128)(2,1)} %param.9) | copy-start | bytes 786436
  126.4 10.2 %collective-permute-start.18 = (bf16[32,4096]{1,0:T(8,128)(2,1)S(1)}, bf16[32,4096]{1,0:T(8,128)(2,1)S(1)}, u32[]{:S(2)}, u32[]{:S(2)}) collective-permute-start(bf16[32,4096]{1,0:T(8,128)(2,1)S(1)} %fusion.3), channel_id=1, source_target_pairs={{0,4},{1,5},{2,6},{3,7},{4,0},{5,1},{6,2},{7,3},{8,12},{9,13},{10,... | collective-permute-start | bytes 786440 | tf_op jit(solution)/shard_map/ppermute | solution.py:250
  128.2 6.4 %collective-permute-start.21 = (bf16[1,32,4096]{2,1,0:T(8,128)(2,1)S(1)}, bf16[1,32,4096]{2,1,0:T(8,128)(2,1)S(1)}, u32[]{:S(2)}, u32[]{:S(2)}) collective-permute-start(bf16[1,32,4096]{2,1,0:T(8,128)(2,1)S(1)} %split.67), channel_id=1, source_target_pairs={{0,8},{8,0},{16,24},{24,16},{1,9},{9,1},{17,25},{25,17},{2,10},{10... | collective-permute-start | bytes 786440 | tf_op jit(solution)/shard_map/ppermute | solution.py:20
  134.8 6.4 %collective-permute-start.23 = (bf16[32,4096]{1,0:T(8,128)(2,1)S(1)}, bf16[32,4096]{1,0:T(8,128)(2,1)S(1)}, u32[]{:S(2)}, u32[]{:S(2)}) collective-permute-start(bf16[32,4096]{1,0:T(8,128)(2,1)S(1)} %bitcast.49), channel_id=1, source_target_pairs={{0,2},{1,3},{2,0},{3,1},{4,6},{5,7},{6,4},{7,5},{8,10},{9,11},{10,... | collective-permute-start | bytes 786440 | tf_op jit(solution)/shard_map/ppermute | solution.py:250

commit v6 on v1

--- a/solution.py
+++ b/solution.py
@@ -1,6 +1,10 @@
+import functools
+
 import jax
 import jax.numpy as jnp
 from jax import lax
+from jax.experimental import pallas as pl
+from jax.experimental.pallas import tpu as pltpu
 from jax.sharding import PartitionSpec as P
 
 BLOCK = 128
@@ -87,34 +91,252 @@
     return mixed.astype(jnp.bfloat16)
 
 
+def added(block, arrived):
+    return (block.astype(jnp.float32) + arrived.astype(jnp.float32)).astype(jnp.bfloat16)
+
+
+def scaled(block, scale):
+    return (block.astype(jnp.float32) * scale).astype(jnp.bfloat16)
+
+
+def in_kernel(gate_scales, up_scales, gate_ref, up_ref, out_ref):
+    strip, cols = gate_ref.shape
+    first = pl.program_id(0) * (strip // BLOCK)
+    for row in range(strip // BLOCK):
+        rows = slice(row * BLOCK, (row + 1) * BLOCK)
+        for col in range(cols // BLOCK):
+            at = slice(col * BLOCK, (col + 1) * BLOCK)
+            to = 2 * col * BLOCK
+            out_ref[rows, to : to + BLOCK] = scaled(gate_ref[rows, at], gate_scales[col, first + row])
+            to += BLOCK
+            out_ref[rows, to : to + BLOCK] = scaled(up_ref[rows, at], up_scales[col, first + row])
+
+
+def dequantize_in(gate, up, gate_scales, up_scales):
+    rows, cols = gate.shape
+    strip = min(rows, 8 * BLOCK)
+    block = pl.BlockSpec((strip, cols), lambda i: (i, 0))
+    smem = pl.BlockSpec(memory_space=pltpu.SMEM)
+    return pl.pallas_call(
+        in_kernel,
+        grid=(rows // strip,),
+        in_specs=[smem, smem, block, block],
+        out_specs=pl.BlockSpec((strip, 2 * cols), lambda i: (i, 0)),
+        out_shape=jax.ShapeDtypeStruct((rows, 2 * cols), jnp.bfloat16),
+        cost_estimate=pl.CostEstimate(
+            flops=2 * rows * cols, bytes_accessed=8 * rows * cols, transcendentals=0
+        ),
+        name="dequantize_in",
+    )(gate_scales.T, up_scales.T, gate, up)
+
+
+def down_kernel(scales, down_ref, out_ref):
+    strip = down_ref.shape[1] // BLOCK
+    first = pl.program_id(0) * strip
+    for row in range(down_ref.shape[0] // BLOCK):
+        rows = slice(row * BLOCK, (row + 1) * BLOCK)
+        for col in range(strip):
+            cols = slice(col * BLOCK, (col + 1) * BLOCK)
+            out_ref[rows, cols] = scaled(down_ref[rows, cols], scales[row, first + col])
+
+
+def dequantize_down(down, scales):
+    rows, cols = down.shape
+    strip = min(cols, 8 * BLOCK)
+    block = pl.BlockSpec((rows, strip), lambda i: (0, i))
+    return pl.pallas_call(
+        down_kernel,
+        grid=(cols // strip,),
+        in_specs=[pl.BlockSpec(memory_space=pltpu.SMEM), block],
+        out_specs=block,
+        out_shape=jax.ShapeDtypeStruct((rows, cols), jnp.bfloat16),
+        cost_estimate=pl.CostEstimate(
+            flops=rows * cols, bytes_accessed=4 * rows * cols, transcendentals=0
+        ),
+        name="dequantize_down",
+    )(scales, down)
+
+
+def silu(v):
+    return v / (1 + jnp.exp(-v))
+
+
+def expert_kernel(count, experts, own_expert, *refs):
+    pieces, refs = refs[:count], refs[count:]
+    in_refs, down_refs, refs = refs[:2], refs[2:4], refs[4:]
+    outs, (rows, w_in, w_down, hidden, in_sems, down_sems) = refs[:count], refs[count:]
+    size = pieces[0].shape[0]
+    model_width = rows.shape[1]
+    strips, full, strip = w_down.shape
+    half = full // 2
+    columns = range(half // BLOCK)
+
+    def in_copy(part, col):
+        source = in_refs[part].at[:, pl.ds(2 * col * BLOCK, 2 * BLOCK)]
+        return pltpu.make_async_copy(source, w_in.at[part, col], in_sems.at[part, col])
+
+    def down_copy(part, at):
+        source = down_refs[part].at[:, pl.ds(at * strip, strip)]
+        target = w_down.at[at, pl.ds(part * half, half)]
+        return pltpu.make_async_copy(source, target, down_sems.at[part, at])
+
+    for part in range(2):
+        for col in columns:
+            in_copy(part, col).start()
+    for at in range(strips):
+        for part in range(2):
+            down_copy(part, at).start()
+
+    weights = []
+    for place, piece in enumerate(pieces):
+        rows[place * size : (place + 1) * size, :] = piece[:, :model_width]
+        marks = piece[:, model_width:].astype(jnp.float32)
+        column = lax.broadcasted_iota(jnp.int32, marks.shape, 1)
+        chosen = (column == own_expert[0]) | (column == own_expert[0] + experts)
+        weights.append(jnp.sum(jnp.where(chosen, marks, 0.0), axis=1, keepdims=True))
+    for part in range(2):
+        for col in columns:
+            in_copy(part, col).wait()
+            both = jnp.dot(rows[...], w_in[part, col], preferred_element_type=jnp.float32)
+            value = (silu(both[:, :BLOCK]) * both[:, BLOCK:]).astype(jnp.bfloat16)
+            to = part * half + col * BLOCK
+            hidden[:, to : to + BLOCK] = value
+    for at in range(strips):
+        for part in range(2):
+            down_copy(part, at).wait()
+        value = jnp.dot(hidden[...], w_down[at], preferred_element_type=jnp.float32)
+        for place, out in enumerate(outs):
+            weighted = value[place * size : (place + 1) * size] * weights[place]
+            out[:, at * strip : (at + 1) * strip] = weighted.astype(jnp.bfloat16)
+
+
+def expert_layer(pieces, own_expert, experts, in_own, in_other, down_own, down_other):
+    count, size = len(pieces), pieces[0].shape[0]
+    model_width, width = in_own.shape
+    half = width // 2
+    strip = min(8 * BLOCK, model_width)
+    strips, columns = model_width // strip, half // BLOCK
+    total = count * size
+    whole = pl.BlockSpec(memory_space=pltpu.VMEM)
+    anywhere = pl.BlockSpec(memory_space=pl.ANY)
+    return pl.pallas_call(
+        functools.partial(expert_kernel, count, experts),
+        in_specs=[pl.BlockSpec(memory_space=pltpu.SMEM)] + [whole] * count + [anywhere] * 4,
+        out_specs=[whole] * count,
+        out_shape=[jax.ShapeDtypeStruct((size, model_width), jnp.bfloat16)] * count,
+        scratch_shapes=[
+            pltpu.VMEM((total, model_width), jnp.bfloat16),
+            pltpu.VMEM((2, columns, model_width, 2 * BLOCK), jnp.bfloat16),
+            pltpu.VMEM((strips, width, strip), jnp.bfloat16),
+            pltpu.VMEM((total, width), jnp.bfloat16),
+            pltpu.SemaphoreType.DMA((2, columns)),
+            pltpu.SemaphoreType.DMA((2, strips)),
+        ],
+        cost_estimate=pl.CostEstimate(
+            flops=6 * total * model_width * width,
+            bytes_accessed=6 * model_width * width + 4 * total * model_width,
+            transcendentals=total * width,
+        ),
+        compiler_params=pltpu.CompilerParams(vmem_limit_bytes=32 * 1024 * 1024),
+        name="expert_layer",
+    )(own_expert, *pieces, in_own, in_other, down_own, down_other)
+
+
+def across_chips(block, far):
+    count = lax.axis_size("expert")
+    return lax.ppermute(block, "expert", [(low, low ^ 2 * far) for low in range(count)])
+
+
 def by_sums(tokens, expert_ids, gate_vals, gate_q, up_q, down_q, gate_scale, up_scale, down_scale):
-    both = ("dp", "expert")
+    token_count, model_width = tokens.shape
+    group_count = lax.axis_size("dp")
     pair_count = lax.axis_size("expert") // 2
-    expert_count = lax.axis_size("dp") * pair_count
+    expert_count = group_count * pair_count
     own_expert = lax.axis_index("dp") * pair_count + lax.axis_index("expert") // 2
+    bits = list(range(group_count.bit_length() - 1))
+    orders = (bits, bits[::-1])
+
     named = expert_ids[:, :, None] == jnp.arange(expert_count, dtype=jnp.int32)[None, None, :]
     weight = jnp.sum(jnp.where(named, gate_vals[:, :, None], 0.0), axis=1)
-    all_weights = lax.all_gather(weight, both, axis=0, tiled=True)
-    own_weight = jnp.sum(
-        jnp.where(jnp.arange(expert_count)[None, :] == own_expert, all_weights, 0.0), axis=1
-    )
-    all_tokens = lax.all_gather(tokens, both, axis=0, tiled=True)
-    w_gate = dequantize(gate_q[0], gate_scale[0])
-    w_up = dequantize(up_q[0], up_scale[0])
-    w_down = dequantize(down_q[0], down_scale[0])
-    partial_value = expert_ffn(all_tokens, w_gate, w_up, w_down) * own_weight[:, None]
-    summed = lax.psum_scatter(
-        partial_value.astype(jnp.bfloat16), both, scatter_dimension=0, tiled=True
-    )
-    mixed = tokens.astype(jnp.float32) + summed.astype(jnp.float32)
-    return mixed.astype(jnp.bfloat16)
+    high = weight.astype(jnp.bfloat16)
+    low = (weight - high.astype(jnp.float32)).astype(jnp.bfloat16)
+    extra = -(-2 * expert_count // BLOCK) * BLOCK
+    pad = jnp.zeros((token_count, extra - 2 * expert_count), jnp.bfloat16)
+    payload = jnp.concatenate([tokens, high, low, pad], axis=1)
+
+    together = lax.optimization_barrier
+    place = jnp.reshape(own_expert, (1,)).astype(jnp.int32)
+    last = len(bits) - 1
+    pairs = [(first, first + 1) for first in range(0, pair_count, 2)]
+    came = {0: payload, 1: across_chips(payload, 1)}
+
+    def along_z(far):
+        low = far & -far
+        came[far] = across_chips(came[far ^ low], low)
+
+    gate_own, up_own, came = together((gate_q[0], up_q[0], came))
+    pieces, outs, in_other, down_other = {}, {}, None, None
+    for number, pair in enumerate(pairs):
+        following = pairs[number + 1] if number + 1 < len(pairs) else ()
+        blocks = {far: came[far] for far in pair}
+        for turn in range(len(bits)):
+            if turn < len(following):
+                along_z(following[turn])
+            arrived = {far: from_partner(blocks[far], "dp", orders[far % 2][turn]) for far in pair}
+            if turn == last:
+                pieces[pair] = [part for far in pair for part in (blocks[far], arrived[far])]
+            else:
+                blocks = {
+                    far: jnp.concatenate([blocks[far], arrived[far]], axis=0) for far in pair
+                }
+            if number == 0 and turn == 0:
+                in_own = dequantize_in(gate_own, up_own, gate_scale[0], up_scale[0])
+                blocks, came, in_own, down_own = together((blocks, came, in_own, down_q[0]))
+                in_other = from_partner(in_own, "expert", 0)
+                down_own = dequantize_down(down_own, down_scale[0])
+            elif number == 0 and turn == last:
+                tied = (pieces[pair], came, in_other, down_own)
+                pieces[pair], came, in_other, down_own = together(tied)
+                down_other = from_partner(down_own, "expert", 0)
+                weights = (in_own, in_other, down_own)
+            elif number == 1 and turn == 0:
+                blocks, pieces, down_other = together((blocks, pieces, down_other))
+                held = pieces[pairs[0]]
+                outs[pairs[0]] = expert_layer(held, place, expert_count, *weights, down_other)
+        if number > 0:
+            pieces[pair], outs = together((pieces[pair], outs))
+            outs[pair] = expert_layer(pieces[pair], place, expert_count, *weights, down_other)
+
+    total = tokens.astype(jnp.float32)
+    sums = {}
+    for pair in pairs[::-1]:
+        for turn in range(last, -1, -1):
+            for where, far in enumerate(pair):
+                if turn == last:
+                    kept, sent = outs[pair][2 * where : 2 * where + 2]
+                else:
+                    kept, sent = jnp.split(sums[far], 2, axis=0)
+                sums[far] = added(kept, from_partner(sent, "dp", orders[far % 2][turn]))
+            sums, outs = together((sums, outs))
+        for far in reversed(pair):
+            block, low = sums.pop(far), far & -far
+            if far == 0:
+                total = total + block.astype(jnp.float32)
+            elif far == low:
+                total = total + across_chips(block, low).astype(jnp.float32)
+            else:
+                sums[far ^ low] = added(sums[far ^ low], across_chips(block, low))
+    return total.astype(jnp.bfloat16)
 
 
 def shards(tokens, expert_ids, *weights):
     expert_count = lax.axis_size("dp") * lax.axis_size("expert") // 2
     token_count, top_count = expert_ids.shape
     capacity = 2 * token_count * top_count // expert_count
-    plan = by_rows if capacity < token_count else by_sums
+    group_count, pair_count = lax.axis_size("dp"), lax.axis_size("expert") // 2
+    powers = all(count & (count - 1) == 0 for count in (group_count, pair_count))
+    dense = capacity >= token_count and powers and min(group_count, pair_count) >= 4
+    plan = by_sums if dense else by_rows
     return plan(tokens, expert_ids, *weights)
 
 

time: 286 us -> 143 us (0.50)
  waiting for transfers between devices: 181 us -> 61.6 us
  blocking collectives: 45.1 us -> 0 us
  Pallas kernels: 0 us -> 34.6 us
  matrix products: 30.8 us -> 0 us
  starting transfers between devices: 0.04 us -> 28.6 us
  between operations: 13.5 us -> 0.2 us
    reduce_scatter x1 -> x0, waiting for transfers between devices: 151 us -> none  [by_sums(): lax.psum_scatter(partial_value.astype(jnp.bfloat16), both, scatter_dimens...]
    ppermute x0 -> x24, waiting for transfers between devices: none -> 61.6 us  [the longest x18 43 us: from_partner(): return lax.ppermute(block, axis, route)]
    all_gather x1 -> x0, blocking collectives: 45.1 us -> none  [by_sums(): all_weights = lax.all_gather(weight, both, axis=0, tiled=True)]
    pallas_call x0 -> x4, Pallas kernels: none -> 34.6 us  [the longest x2 23.8 us: expert_layer(): pl.pallas_call(functools.partial(expert_kernel, count, experts), in_specs...]
    dot_general x3 -> x0, matrix products: 30.8 us -> none  [the longest x1 11 us: expert_ffn(): return jnp.dot(hidden, w_down, preferred_element_type=jnp.float32)]
    all_gather x1 -> x0, waiting for transfers between devices: 29.8 us -> none  [by_sums(): all_tokens = lax.all_gather(tokens, both, axis=0, tiled=True)]
    ppermute x0 -> x24, starting transfers between devices: none -> 28.6 us  [the longest x18 17.3 us: from_partner(): return lax.ppermute(block, axis, route)]
    unnamed x24 -> x29, local copies, waits for them, and re-layouts: 10.8 us -> 11.1 us
  transfers between devices with their start and end apart: 2 -> 24, of which waited for: 2 -> 16; matrix products, arithmetic and copies ran while one was open for 3% -> 3% of each run, Pallas kernels for 0% -> 15%
where the time goes in v6:
time: 143 us
  waiting for transfers between devices  61.6 us (43%)
  Pallas kernels  34.6 us (24%)
  starting transfers between devices  28.6 us (20%)
  local copies, waits for them, and re-layouts  13.7 us (10%)
  other arithmetic  4.14 us (3%)
    ppermute x18, waiting for transfers between devices, from_partner(): return lax.ppermute(block, axis, route)  43 us
    pallas_call x2, Pallas kernels, expert_layer(): pl.pallas_call(functools.partial(expert_kernel, count, experts), in_specs...  23.8 us
    ppermute x6, waiting for transfers between devices, across_chips(): lax.ppermute(block, 'expert', [(low, low ^ 2 * far) for low in range(coun...  18.6 us
    ppermute x18, starting transfers between devices, from_partner(): return lax.ppermute(block, axis, route)  17.3 us
    ppermute x6, starting transfers between devices, across_chips(): lax.ppermute(block, 'expert', [(low, low ^ 2 * far) for low in range(coun...  11.3 us
    unnamed x29, local copies, waits for them, and re-layouts  11.1 us
    pallas_call x1, Pallas kernels, dequantize_in(): pl.pallas_call(in_kernel, grid=(rows // strip,), in_specs=[smem, smem, bl...  6.25 us
    pallas_call x1, Pallas kernels, dequantize_down(): pl.pallas_call(down_kernel, grid=(cols // strip,), in_specs=[pl.BlockSpec...  4.55 us
  transfers between devices with their start and end apart: 24, of which 16 were waited for; matrix products, arithmetic and copies ran while one was open for 3% of the time, Pallas kernels for 15%

profile of v6, /device:TPU:0, one launch (start us, length us, event | category | flops | bytes accessed | tf_op | source)
XLA Modules:
  0.0 142.8 jit_solution(7466791871985186356)
XLA Ops:
  0.9 1.0 concatenate.15
  2.0 3.1 %collective-permute-start = (bf16[32,4224]{1,0:T(8,128)(2,1)S(1)}, bf16[32,4224]{1,0:T(8,128)(2,1)S(1)}, u32[]{:S(2)}, u32[]{:S(2)}) collective-permute-start(bf16[32,4224]{1,0:T(8,128)(2,1)S(1)} %concatenate.15), channel_id=1, source_target_pairs={{0,2},{1,3},{2,0},{3,1},{4,6},{5,7},{6,4},{7,5},{8,10},{9,11},{10,... | collective-permute-start | bytes 811016 | tf_op jit(solution)/shard_map/ppermute | solution.py:247
  5.0 6.5 %collective-permute-done = bf16[32,4224]{1,0:T(8,128)(2,1)S(1)} collective-permute-done((bf16[32,4224]{1,0:T(8,128)(2,1)S(1)}, bf16[32,4224]{1,0:T(8,128)(2,1)S(1)}, u32[]{:S(2)}, u32[]{:S(2)}) %collective-permute-start) | collective-permute-done | bytes 270368 | tf_op jit(solution)/shard_map/ppermute | solution.py:247
  11.5 1.7 %collective-permute-start.2 = (bf16[32,4224]{1,0:T(8,128)(2,1)S(1)}, bf16[32,4224]{1,0:T(8,128)(2,1)S(1)}, u32[]{:S(2)}, u32[]{:S(2)}) collective-permute-start(bf16[32,4224]{1,0:T(8,128)(2,1)S(1)} %collective-permute-done), channel_id=1, source_target_pairs={{0,16},{16,0},{8,24},{24,8},{1,17},{17,1},{9,25},{25,9},{2,18},{18... | collective-permute-start | bytes 811016 | tf_op jit(solution)/shard_map/ppermute | solution.py:20
  13.2 1.3 copy_bitcast_fusion.1
  14.5 2.6 %collective-permute-start.3 = (bf16[32,4224]{1,0:T(8,128)(2,1)S(1)}, bf16[32,4224]{1,0:T(8,128)(2,1)S(1)}, u32[]{:S(2)}, u32[]{:S(2)}) collective-permute-start(bf16[32,4224]{1,0:T(8,128)(2,1)S(1)} %concatenate.15), channel_id=1, source_target_pairs={{0,4},{1,5},{2,6},{3,7},{4,0},{5,1},{6,2},{7,3},{8,12},{9,13},{10,... | collective-permute-start | bytes 811016 | tf_op jit(solution)/shard_map/ppermute | solution.py:247
  17.1 1.5 %collective-permute-start.1 = (bf16[32,4224]{1,0:T(8,128)(2,1)S(1)}, bf16[32,4224]{1,0:T(8,128)(2,1)S(1)}, u32[]{:S(2)}, u32[]{:S(2)}) collective-permute-start(bf16[32,4224]{1,0:T(8,128)(2,1)S(1)} %concatenate.15), channel_id=1, source_target_pairs={{0,8},{8,0},{16,24},{24,16},{1,9},{9,1},{17,25},{25,17},{2,10},{10... | collective-permute-start | bytes 811016 | tf_op jit(solution)/shard_map/ppermute | solution.py:20
  18.6 6.3 %dequantize_in.1.refs_4_ = bf16[4096,768]{1,0:T(8,128)(2,1)} custom-call(f32[3,32]{1,0:T(4,128)} %get-tuple-element.118.gate_scales, f32[3,32]{1,0:T(4,128)} %get-tuple-element.117.up_scales, bf16[4096,384]{1,0:T(8,128)(2,1)} %bitcast.16, bf16[4096,384]{1,0:T(8,128)(2,1)} %bitcast.17), custom_call_target="tpu_custom_call" | custom-call | flops 3145728 | bytes 12582912 | tf_op jit(solution)/shard_map/dequantize_in/pallas_call | solution.py:120
  25.0 3.3 %collective-permute-done.3 = bf16[32,4224]{1,0:T(8,128)(2,1)S(1)} collective-permute-done((bf16[32,4224]{1,0:T(8,128)(2,1)S(1)}, bf16[32,4224]{1,0:T(8,128)(2,1)S(1)}, u32[]{:S(2)}, u32[]{:S(2)}) %collective-permute-start.3) | collective-permute-done | bytes 270368 | tf_op jit(solution)/shard_map/ppermute | solution.py:247
  28.9 1.3 collective-permute-start.5
  31.5 4.6 %dequantize_down.1.refs_6_ = bf16[384,4096]{1,0:T(8,128)(2,1)} custom-call(f32[3,32]{1,0:T(4,128)} %bitcast.18, bf16[384,4096]{1,0:T(8,128)(2,1)} %bitcast.15), custom_call_target="tpu_custom_call" | custom-call | flops 1572864 | bytes 6291456 | tf_op jit(solution)/shard_map/dequantize_down/pallas_call | solution.py:147
  36.1 2.5 %collective-permute-done.6 = bf16[32,4224]{1,0:T(8,128)(2,1)S(1)} collective-permute-done((bf16[32,4224]{1,0:T(8,128)(2,1)S(1)}, bf16[32,4224]{1,0:T(8,128)(2,1)S(1)}, u32[]{:S(2)}, u32[]{:S(2)}) %collective-permute-start.6) | collective-permute-done | bytes 270368 | tf_op jit(solution)/shard_map/ppermute | solution.py:247
  38.6 4.4 %collective-permute-done.4.refs_1_ = bf16[64,4224]{1,0:T(8,128)(2,1)S(1)} collective-permute-done((bf16[64,4224]{1,0:T(8,128)(2,1)S(1)}, bf16[64,4224]{1,0:T(8,128)(2,1)S(1)}, u32[]{:S(2)}, u32[]{:S(2)}) %collective-permute-start.4) | collective-permute-done | bytes 540704 | tf_op jit(solution)/shard_map/ppermute | solution.py:20
  44.6 1.6 %collective-permute-start.8 = (bf16[32,4224]{1,0:T(8,128)(2,1)S(1)}, bf16[32,4224]{1,0:T(8,128)(2,1)S(1)}, u32[]{:S(2)}, u32[]{:S(2)}) collective-permute-start(bf16[32,4224]{1,0:T(8,128)(2,1)S(1)} %collective-permute-done.3), channel_id=1, source_target_pairs={{0,8},{8,0},{16,24},{24,16},{1,9},{9,1},{17,25},{25,17},{2,10},{10... | collective-permute-start | bytes 811016 | tf_op jit(solution)/shard_map/ppermute | solution.py:20
  47.1 6.4 %collective-permute-done.8 = bf16[32,4224]{1,0:T(8,128)(2,1)S(1)} collective-permute-done((bf16[32,4224]{1,0:T(8,128)(2,1)S(1)}, bf16[32,4224]{1,0:T(8,128)(2,1)S(1)}, u32[]{:S(2)}, u32[]{:S(2)}) %collective-permute-start.8) | collective-permute-done | bytes 270368 | tf_op jit(solution)/shard_map/ppermute | solution.py:20
  57.6 2.8 %copy-done = bf16[4096,768]{1,0:T(8,128)(2,1)S(1)} copy-done((bf16[4096,768]{1,0:T(8,128)(2,1)S(1)}, bf16[4096,768]{1,0:T(8,128)(2,1)}, u32[]{:S(2)}) %copy-start) | copy-done | bytes 6291480
  60.4 1.9 %copy-done.1 = bf16[384,4096]{1,0:T(8,128)(2,1)S(1)} copy-done((bf16[384,4096]{1,0:T(8,128)(2,1)S(1)}, bf16[384,4096]{1,0:T(8,128)(2,1)}, u32[]{:S(2)}) %copy-start.1) | copy-done | bytes 3145752
  62.3 1.0 copy-done.3
  63.3 1.0 copy-done.5
  64.4 1.0 copy-done.7
  65.4 1.0 copy-done.9
  66.5 11.0 %expert_layer.2 = (bf16[64,4096]{1,0:T(8,128)(2,1)S(1)}, bf16[64,4096]{1,0:T(8,128)(2,1)S(1)}, bf16[64,4096]{1,0:T(8,128)(2,1)S(1)}, bf16[64,4096]{1,0:T(8,128)(2,1)S(1)}) custom-call(s32[1]{0:T(128)} %bitcast.own_expert, bf16[64,4224]{1,0:T(8,128)(2,1)S(1)} %copy-done.5, bf16[64,4224]{1,0:T(8,128)(2,1)S(1)} %copy-done.7, bf16[64,4224]{1,0:T(8,128)(2,1)S(1)} %copy-done.3, ...), custom_call_target="tpu_custom_call" | custom-call | flops 4831838208 | bytes 23068672 | tf_op jit(solution)/shard_map/expert_layer/pallas_call | solution.py:222
  77.5 12.8 %expert_layer.3 = (bf16[64,4096]{1,0:T(8,128)(2,1)S(1)}, bf16[64,4096]{1,0:T(8,128)(2,1)S(1)}, bf16[64,4096]{1,0:T(8,128)(2,1)S(1)}, bf16[64,4096]{1,0:T(8,128)(2,1)S(1)}) custom-call(s32[1]{0:T(128)} %bitcast.own_expert, bf16[64,4224]{1,0:T(8,128)(2,1)} %pad_maximum_fusion.2.refs_0_, bf16[64,4224]{1,0:T(8,128)(2,1)} %collective-permute-done.11.refs_1_, ...), custom_call_target="tpu_custom_call" | custom-call | flops 4831838208 | bytes 23068672 | tf_op jit(solution)/shard_map/expert_layer/pallas_call | solution.py:222
  90.3 1.2 collective-permute-start.13
  91.5 1.1 collective-permute-start.14
  92.6 10.7 %collective-permute-done.13 = bf16[64,4096]{1,0:T(8,128)(2,1)S(1)} collective-permute-done((bf16[64,4096]{1,0:T(8,128)(2,1)S(1)}, bf16[64,4096]{1,0:T(8,128)(2,1)S(1)}, u32[]{:S(2)}, u32[]{:S(2)}) %collective-permute-start.13) | collective-permute-done | bytes 524320 | tf_op jit(solution)/shard_map/ppermute | solution.py:20
  106.1 4.6 %collective-permute-done.16 = bf16[32,4096]{1,0:T(8,128)(2,1)S(1)} collective-permute-done((bf16[32,4096]{1,0:T(8,128)(2,1)S(1)}, bf16[32,4096]{1,0:T(8,128)(2,1)S(1)}, u32[]{:S(2)}, u32[]{:S(2)}) %collective-permute-start.16) | collective-permute-done | bytes 262176 | tf_op jit(solution)/shard_map/ppermute | solution.py:20
  111.8 1.2 collective-permute-start.19
  114.4 8.6 %collective-permute-done.19 = bf16[64,4096]{1,0:T(8,128)(2,1)S(1)} collective-permute-done((bf16[64,4096]{1,0:T(8,128)(2,1)S(1)}, bf16[64,4096]{1,0:T(8,128)(2,1)S(1)}, u32[]{:S(2)}, u32[]{:S(2)}) %collective-permute-start.19) | collective-permute-done | bytes 524320 | tf_op jit(solution)/shard_map/ppermute | solution.py:20
  124.8 4.2 %collective-permute-start.18 = (bf16[32,4096]{1,0:T(8,128)(2,1)S(1)}, bf16[32,4096]{1,0:T(8,128)(2,1)S(1)}, u32[]{:S(2)}, u32[]{:S(2)}) collective-permute-start(bf16[32,4096]{1,0:T(8,128)(2,1)S(1)} %add_convert_fusion.7), channel_id=1, source_target_pairs={{0,4},{1,5},{2,6},{3,7},{4,0},{5,1},{6,2},{7,3},{8,12},{9,13},{10,... | collective-permute-start | bytes 786440 | tf_op jit(solution)/shard_map/ppermute | solution.py:247
  130.3 5.2 %collective-permute-done.21 = bf16[32,4096]{1,0:T(8,128)(2,1)S(1)} collective-permute-done((bf16[32,4096]{1,0:T(8,128)(2,1)S(1)}, bf16[32,4096]{1,0:T(8,128)(2,1)S(1)}, u32[]{:S(2)}, u32[]{:S(2)}) %collective-permute-start.21) | collective-permute-done | bytes 262176 | tf_op jit(solution)/shard_map/ppermute | solution.py:20
  135.9 6.1 %collective-permute-done.23 = bf16[32,4096]{1,0:T(8,128)(2,1)S(1)} collective-permute-done((bf16[32,4096]{1,0:T(8,128)(2,1)S(1)}, bf16[32,4096]{1,0:T(8,128)(2,1)S(1)}, u32[]{:S(2)}, u32[]{:S(2)}) %collective-permute-start.23) | collective-permute-done | bytes 262176 | tf_op jit(solution)/shard_map/ppermute | solution.py:247
  (75 shorter events, 19.2 us)
Async XLA Ops:
  2.0 9.6 %collective-permute-start = (bf16[32,4224]{1,0:T(8,128)(2,1)S(1)}, bf16[32,4224]{1,0:T(8,128)(2,1)S(1)}, u32[]{:S(2)}, u32[]{:S(2)}) collective-permute-start(bf16[32,4224]{1,0:T(8,128)(2,1)S(1)} %concatenate.15), channel_id=1, source_target_pairs={{0,2},{1,3},{2,0},{3,1},{4,6},{5,7},{6,4},{7,5},{8,10},{9,11},{10,... | collective-permute-start | bytes 811016 | tf_op jit(solution)/shard_map/ppermute | solution.py:247
  11.5 13.3 %collective-permute-start.2 = (bf16[32,4224]{1,0:T(8,128)(2,1)S(1)}, bf16[32,4224]{1,0:T(8,128)(2,1)S(1)}, u32[]{:S(2)}, u32[]{:S(2)}) collective-permute-start(bf16[32,4224]{1,0:T(8,128)(2,1)S(1)} %collective-permute-done), channel_id=1, source_target_pairs={{0,16},{16,0},{8,24},{24,8},{1,17},{17,1},{9,25},{25,9},{2,18},{18... | collective-permute-start | bytes 811016 | tf_op jit(solution)/shard_map/ppermute | solution.py:20
  14.5 13.8 %collective-permute-start.3 = (bf16[32,4224]{1,0:T(8,128)(2,1)S(1)}, bf16[32,4224]{1,0:T(8,128)(2,1)S(1)}, u32[]{:S(2)}, u32[]{:S(2)}) collective-permute-start(bf16[32,4224]{1,0:T(8,128)(2,1)S(1)} %concatenate.15), channel_id=1, source_target_pairs={{0,4},{1,5},{2,6},{3,7},{4,0},{5,1},{6,2},{7,3},{8,12},{9,13},{10,... | collective-permute-start | bytes 811016 | tf_op jit(solution)/shard_map/ppermute | solution.py:247
  17.1 7.8 %collective-permute-start.1 = (bf16[32,4224]{1,0:T(8,128)(2,1)S(1)}, bf16[32,4224]{1,0:T(8,128)(2,1)S(1)}, u32[]{:S(2)}, u32[]{:S(2)}) collective-permute-start(bf16[32,4224]{1,0:T(8,128)(2,1)S(1)} %concatenate.15), channel_id=1, source_target_pairs={{0,8},{8,0},{16,24},{24,16},{1,9},{9,1},{17,25},{25,17},{2,10},{10... | collective-permute-start | bytes 811016 | tf_op jit(solution)/shard_map/ppermute | solution.py:20
  24.8 6.1 %copy-start.13 = (f32[1,3,32]{2,0,1:T(1,128)S(1)}, f32[1,3,32]{2,0,1:T(1,128)}, u32[]{:S(2)}) copy-start(f32[1,3,32]{2,0,1:T(1,128)} %param.17) | copy-start | bytes 1156
  24.9 11.2 %copy-start.2 = (bf16[64,4224]{1,0:T(8,128)(2,1)}, bf16[64,4224]{1,0:T(8,128)(2,1)S(1)}, u32[]{:S(2)}) copy-start(bf16[64,4224]{1,0:T(8,128)(2,1)S(1)} %pad_maximum_fusion.1.refs_2_) | copy-start | bytes 1622020
  25.0 11.1 %copy-start.4 = (bf16[64,4224]{1,0:T(8,128)(2,1)}, bf16[64,4224]{1,0:T(8,128)(2,1)S(1)}, u32[]{:S(2)}) copy-start(bf16[64,4224]{1,0:T(8,128)(2,1)S(1)} %pad_maximum_fusion.refs_0_) | copy-start | bytes 1622020
  28.3 16.3 %collective-permute-start.7 = (bf16[4096,768]{1,0:T(8,128)(2,1)}, bf16[4096,768]{1,0:T(8,128)(2,1)}, u32[]{:S(2)}, u32[]{:S(2)}) collective-permute-start(bf16[4096,768]{1,0:T(8,128)(2,1)} %dequantize_in.1.refs_4_), channel_id=1, source_target_pairs={{0,1},{1,0},{2,3},{3,2},{4,5},{5,4},{6,7},{7,6},{8,9},{9,8},{10,11... | collective-permute-start | bytes 18874376 | tf_op jit(solution)/shard_map/ppermute | solution.py:20
  28.3 14.7 %collective-permute-start.4 = (bf16[64,4224]{1,0:T(8,128)(2,1)S(1)}, bf16[64,4224]{1,0:T(8,128)(2,1)S(1)}, u32[]{:S(2)}, u32[]{:S(2)}) collective-permute-start(bf16[64,4224]{1,0:T(8,128)(2,1)S(1)} %pad_maximum_fusion.refs_0_), channel_id=1, source_target_pairs={{0,16},{16,0},{8,24},{24,8},{1,17},{17,1},{9,25},{25,9},{2,18},{18... | collective-permute-start | bytes 1622024 | tf_op jit(solution)/shard_map/ppermute | solution.py:20
  28.9 14.9 %collective-permute-start.5 = (bf16[64,4224]{1,0:T(8,128)(2,1)S(1)}, bf16[64,4224]{1,0:T(8,128)(2,1)S(1)}, u32[]{:S(2)}, u32[]{:S(2)}) collective-permute-start(bf16[64,4224]{1,0:T(8,128)(2,1)S(1)} %pad_maximum_fusion.1.refs_2_), channel_id=1, source_target_pairs={{0,8},{8,0},{16,24},{24,16},{1,9},{9,1},{17,25},{25,17},{2,10},{10... | collective-permute-start | bytes 1622024 | tf_op jit(solution)/shard_map/ppermute | solution.py:20
  30.3 8.3 %collective-permute-start.6 = (bf16[32,4224]{1,0:T(8,128)(2,1)S(1)}, bf16[32,4224]{1,0:T(8,128)(2,1)S(1)}, u32[]{:S(2)}, u32[]{:S(2)}) collective-permute-start(bf16[32,4224]{1,0:T(8,128)(2,1)S(1)} %collective-permute-done.3), channel_id=1, source_target_pairs={{0,2},{1,3},{2,0},{3,1},{4,6},{5,7},{6,4},{7,5},{8,10},{9,11},{10,... | collective-permute-start | bytes 811016 | tf_op jit(solution)/shard_map/ppermute | solution.py:247
  38.6 5.2 %copy-start.11 = (bf16[32,4224]{1,0:T(8,128)(2,1)}, bf16[32,4224]{1,0:T(8,128)(2,1)S(1)}, u32[]{:S(2)}) copy-start(bf16[32,4224]{1,0:T(8,128)(2,1)S(1)} %collective-permute-done.6) | copy-start | bytes 811012
  44.6 10.3 %copy-start.12 = (bf16[32,4224]{1,0:T(8,128)(2,1)S(1)}, bf16[32,4224]{1,0:T(8,128)(2,1)}, u32[]{:S(2)}) copy-start(bf16[32,4224]{1,0:T(8,128)(2,1)} %copy-done.11) | copy-start | bytes 811012
  44.6 11.2 %collective-permute-start.10 = (bf16[384,4096]{1,0:T(8,128)(2,1)}, bf16[384,4096]{1,0:T(8,128)(2,1)S(1)}, u32[]{:S(2)}, u32[]{:S(2)}) collective-permute-start(bf16[384,4096]{1,0:T(8,128)(2,1)} %dequantize_down.1.refs_6_), channel_id=1, source_target_pairs={{0,1},{1,0},{2,3},{3,2},{4,5},{5,4},{6,7},{7,6},{8,9},{9,8},{10,11... | collective-permute-start | bytes 9437192 | tf_op jit(solution)/shard_map/ppermute | solution.py:20
  44.6 8.9 %collective-permute-start.8 = (bf16[32,4224]{1,0:T(8,128)(2,1)S(1)}, bf16[32,4224]{1,0:T(8,128)(2,1)S(1)}, u32[]{:S(2)}, u32[]{:S(2)}) collective-permute-start(bf16[32,4224]{1,0:T(8,128)(2,1)S(1)} %collective-permute-done.3), channel_id=1, source_target_pairs={{0,8},{8,0},{16,24},{24,16},{1,9},{9,1},{17,25},{25,17},{2,10},{10... | collective-permute-start | bytes 811016 | tf_op jit(solution)/shard_map/ppermute | solution.py:20
  46.2 8.8 %collective-permute-start.9 = (bf16[32,4224]{1,0:T(8,128)(2,1)}, bf16[32,4224]{1,0:T(8,128)(2,1)S(1)}, u32[]{:S(2)}, u32[]{:S(2)}) collective-permute-start(bf16[32,4224]{1,0:T(8,128)(2,1)} %copy-done.11), channel_id=1, source_target_pairs={{0,16},{16,0},{8,24},{24,8},{1,17},{17,1},{9,25},{25,9},{2,18},{18... | collective-permute-start | bytes 811016 | tf_op jit(solution)/shard_map/ppermute | solution.py:20
  55.8 21.7 %collective-permute-start.11 = (bf16[64,4224]{1,0:T(8,128)(2,1)}, bf16[64,4224]{1,0:T(8,128)(2,1)}, u32[]{:S(2)}, u32[]{:S(2)}) collective-permute-start(bf16[64,4224]{1,0:T(8,128)(2,1)} %pad_maximum_fusion.2.refs_0_), channel_id=1, source_target_pairs={{0,16},{16,0},{8,24},{24,8},{1,17},{17,1},{9,25},{25,9},{2,18},{18... | collective-permute-start | bytes 1622024 | tf_op jit(solution)/shard_map/ppermute | solution.py:20
  56.7 20.8 %collective-permute-start.12 = (bf16[64,4224]{1,0:T(8,128)(2,1)}, bf16[64,4224]{1,0:T(8,128)(2,1)}, u32[]{:S(2)}, u32[]{:S(2)}) collective-permute-start(bf16[64,4224]{1,0:T(8,128)(2,1)} %pad_maximum_fusion.3.refs_2_), channel_id=1, source_target_pairs={{0,8},{8,0},{16,24},{24,16},{1,9},{9,1},{17,25},{25,17},{2,10},{10... | collective-permute-start | bytes 1622024 | tf_op jit(solution)/shard_map/ppermute | solution.py:20
  57.6 2.8 %copy-start = (bf16[4096,768]{1,0:T(8,128)(2,1)S(1)}, bf16[4096,768]{1,0:T(8,128)(2,1)}, u32[]{:S(2)}) copy-start(bf16[4096,768]{1,0:T(8,128)(2,1)} %dequantize_in.1.refs_4_) | copy-start | bytes 18874372
  60.4 1.9 %copy-start.1 = (bf16[384,4096]{1,0:T(8,128)(2,1)S(1)}, bf16[384,4096]{1,0:T(8,128)(2,1)}, u32[]{:S(2)}) copy-start(bf16[384,4096]{1,0:T(8,128)(2,1)} %dequantize_down.1.refs_6_) | copy-start | bytes 9437188
  90.3 13.0 %collective-permute-start.13 = (bf16[64,4096]{1,0:T(8,128)(2,1)S(1)}, bf16[64,4096]{1,0:T(8,128)(2,1)S(1)}, u32[]{:S(2)}, u32[]{:S(2)}) collective-permute-start(bf16[64,4096]{1,0:T(8,128)(2,1)S(1)} %get-tuple-element.94), channel_id=1, source_target_pairs={{0,16},{16,0},{8,24},{24,8},{1,17},{17,1},{9,25},{25,9},{2,18},{18... | collective-permute-start | bytes 1572872 | tf_op jit(solution)/shard_map/ppermute | solution.py:20
  91.5 12.6 %collective-permute-start.14 = (bf16[64,4096]{1,0:T(8,128)(2,1)S(1)}, bf16[64,4096]{1,0:T(8,128)(2,1)S(1)}, u32[]{:S(2)}, u32[]{:S(2)}) collective-permute-start(bf16[64,4096]{1,0:T(8,128)(2,1)S(1)} %get-tuple-element.96), channel_id=1, source_target_pairs={{0,8},{8,0},{16,24},{24,16},{1,9},{9,1},{17,25},{25,17},{2,10},{10... | collective-permute-start | bytes 1572872 | tf_op jit(solution)/shard_map/ppermute | solution.py:20
  104.3 6.4 %collective-permute-start.16 = (bf16[32,4096]{1,0:T(8,128)(2,1)S(1)}, bf16[32,4096]{1,0:T(8,128)(2,1)S(1)}, u32[]{:S(2)}, u32[]{:S(2)}) collective-permute-start(bf16[32,4096]{1,0:T(8,128)(2,1)S(1)} %split.27), channel_id=1, source_target_pairs={{0,16},{16,0},{8,24},{24,8},{1,17},{17,1},{9,25},{25,9},{2,18},{18... | collective-permute-start | bytes 786440 | tf_op jit(solution)/shard_map/ppermute | solution.py:20
  105.3 6.4 %collective-permute-start.15 = (bf16[32,4096]{1,0:T(8,128)(2,1)S(1)}, bf16[32,4096]{1,0:T(8,128)(2,1)S(1)}, u32[]{:S(2)}, u32[]{:S(2)}) collective-permute-start(bf16[32,4096]{1,0:T(8,128)(2,1)S(1)} %split.25), channel_id=1, source_target_pairs={{0,8},{8,0},{16,24},{24,16},{1,9},{9,1},{17,25},{25,17},{2,10},{10... | collective-permute-start | bytes 786440 | tf_op jit(solution)/shard_map/ppermute | solution.py:20
  111.8 11.3 %collective-permute-start.19 = (bf16[64,4096]{1,0:T(8,128)(2,1)S(1)}, bf16[64,4096]{1,0:T(8,128)(2,1)S(1)}, u32[]{:S(2)}, u32[]{:S(2)}) collective-permute-start(bf16[64,4096]{1,0:T(8,128)(2,1)S(1)} %get-tuple-element.110), channel_id=1, source_target_pairs={{0,16},{16,0},{8,24},{24,8},{1,17},{17,1},{9,25},{25,9},{2,18},{18... | collective-permute-start | bytes 1572872 | tf_op jit(solution)/shard_map/ppermute | solution.py:20
  112.9 11.8 %collective-permute-start.17 = (bf16[32,4096]{1,0:T(8,128)(2,1)S(1)}, bf16[32,4096]{1,0:T(8,128)(2,1)S(1)}, u32[]{:S(2)}, u32[]{:S(2)}) collective-permute-start(bf16[32,4096]{1,0:T(8,128)(2,1)S(1)} %add_convert_fusion.8), channel_id=1, source_target_pairs={{0,2},{1,3},{2,0},{3,1},{4,6},{5,7},{6,4},{7,5},{8,10},{9,11},{10,... | collective-permute-start | bytes 786440 | tf_op jit(solution)/shard_map/ppermute | solution.py:247
  113.6 10.0 %collective-permute-start.20 = (bf16[64,4096]{1,0:T(8,128)(2,1)S(1)}, bf16[64,4096]{1,0:T(8,128)(2,1)S(1)}, u32[]{:S(2)}, u32[]{:S(2)}) collective-permute-start(bf16[64,4096]{1,0:T(8,128)(2,1)S(1)} %get-tuple-element.112), channel_id=1, source_target_pairs={{0,8},{8,0},{16,24},{24,16},{1,9},{9,1},{17,25},{25,17},{2,10},{10... | collective-permute-start | bytes 1572872 | tf_op jit(solution)/shard_map/ppermute | solution.py:20
  123.8 6.4 %collective-permute-start.22 = (bf16[32,4096]{1,0:T(8,128)(2,1)S(1)}, bf16[32,4096]{1,0:T(8,128)(2,1)S(1)}, u32[]{:S(2)}, u32[]{:S(2)}) collective-permute-start(bf16[32,4096]{1,0:T(8,128)(2,1)S(1)} %split.31), channel_id=1, source_target_pairs={{0,16},{16,0},{8,24},{24,8},{1,17},{17,1},{9,25},{25,9},{2,18},{18... | collective-permute-start | bytes 786440 | tf_op jit(solution)/shard_map/ppermute | solution.py:20
  124.8 17.2 %copy-start.10 = (bf16[32,4096]{1,0:T(8,128)(2,1)S(1)}, bf16[32,4096]{1,0:T(8,128)(2,1)}, u32[]{:S(2)}) copy-start(bf16[32,4096]{1,0:T(8,128)(2,1)} %param.9) | copy-start | bytes 786436
  124.8 11.1 %collective-permute-start.18 = (bf16[32,4096]{1,0:T(8,128)(2,1)S(1)}, bf16[32,4096]{1,0:T(8,128)(2,1)S(1)}, u32[]{:S(2)}, u32[]{:S(2)}) collective-permute-start(bf16[32,4096]{1,0:T(8,128)(2,1)S(1)} %add_convert_fusion.7), channel_id=1, source_target_pairs={{0,4},{1,5},{2,6},{3,7},{4,0},{5,1},{6,2},{7,3},{8,12},{9,13},{10,... | collective-permute-start | bytes 786440 | tf_op jit(solution)/shard_map/ppermute | solution.py:247
  129.1 6.4 %collective-permute-start.21 = (bf16[32,4096]{1,0:T(8,128)(2,1)S(1)}, bf16[32,4096]{1,0:T(8,128)(2,1)S(1)}, u32[]{:S(2)}, u32[]{:S(2)}) collective-permute-start(bf16[32,4096]{1,0:T(8,128)(2,1)S(1)} %split.29), channel_id=1, source_target_pairs={{0,8},{8,0},{16,24},{24,16},{1,9},{9,1},{17,25},{25,17},{2,10},{10... | collective-permute-start | bytes 786440 | tf_op jit(solution)/shard_map/ppermute | solution.py:20
  135.6 6.4 %collective-permute-start.23 = (bf16[32,4096]{1,0:T(8,128)(2,1)S(1)}, bf16[32,4096]{1,0:T(8,128)(2,1)S(1)}, u32[]{:S(2)}, u32[]{:S(2)}) collective-permute-start(bf16[32,4096]{1,0:T(8,128)(2,1)S(1)} %add_convert_fusion.5), channel_id=1, source_target_pairs={{0,2},{1,3},{2,0},{3,1},{4,6},{5,7},{6,4},{7,5},{8,10},{9,11},{10,... | collective-permute-start | bytes 786440 | tf_op jit(solution)/shard_map/ppermute | solution.py:247
  (6 other events, 5.8 us)

commit v7 on v6

--- a/solution.py
+++ b/solution.py
@@ -126,6 +126,7 @@
         cost_estimate=pl.CostEstimate(
             flops=2 * rows * cols, bytes_accessed=8 * rows * cols, transcendentals=0
         ),
+        compiler_params=pltpu.CompilerParams(vmem_limit_bytes=8 * 1024 * 1024),
         name="dequantize_in",
     )(gate_scales.T, up_scales.T, gate, up)
 
@@ -153,6 +154,7 @@
         cost_estimate=pl.CostEstimate(
             flops=rows * cols, bytes_accessed=4 * rows * cols, transcendentals=0
         ),
+        compiler_params=pltpu.CompilerParams(vmem_limit_bytes=8 * 1024 * 1024),
         name="dequantize_down",
     )(scales, down)
 
@@ -164,28 +166,9 @@
 def expert_kernel(count, experts, own_expert, *refs):
     pieces, refs = refs[:count], refs[count:]
     in_refs, down_refs, refs = refs[:2], refs[2:4], refs[4:]
-    outs, (rows, w_in, w_down, hidden, in_sems, down_sems) = refs[:count], refs[count:]
-    size = pieces[0].shape[0]
-    model_width = rows.shape[1]
-    strips, full, strip = w_down.shape
-    half = full // 2
-    columns = range(half // BLOCK)
-
-    def in_copy(part, col):
-        source = in_refs[part].at[:, pl.ds(2 * col * BLOCK, 2 * BLOCK)]
-        return pltpu.make_async_copy(source, w_in.at[part, col], in_sems.at[part, col])
-
-    def down_copy(part, at):
-        source = down_refs[part].at[:, pl.ds(at * strip, strip)]
-        target = w_down.at[at, pl.ds(part * half, half)]
-        return pltpu.make_async_copy(source, target, down_sems.at[part, at])
-
-    for part in range(2):
-        for col in columns:
-            in_copy(part, col).start()
-    for at in range(strips):
-        for part in range(2):
-            down_copy(part, at).start()
+    outs, (rows, hidden) = refs[:count], refs[count:]
+    size, (half, model_width) = pieces[0].shape[0], down_refs[0].shape
+    strip = min(4 * BLOCK, model_width)
 
     weights = []
     for place, piece in enumerate(pieces):
@@ -194,52 +177,45 @@
         column = lax.broadcasted_iota(jnp.int32, marks.shape, 1)
         chosen = (column == own_expert[0]) | (column == own_expert[0] + experts)
         weights.append(jnp.sum(jnp.where(chosen, marks, 0.0), axis=1, keepdims=True))
-    for part in range(2):
-        for col in columns:
-            in_copy(part, col).wait()
-            both = jnp.dot(rows[...], w_in[part, col], preferred_element_type=jnp.float32)
+    for part, in_ref in enumerate(in_refs):
+        for col in range(half // BLOCK):
+            at = slice(2 * col * BLOCK, 2 * (col + 1) * BLOCK)
+            both = jnp.dot(rows[...], in_ref[:, at], preferred_element_type=jnp.float32)
             value = (silu(both[:, :BLOCK]) * both[:, BLOCK:]).astype(jnp.bfloat16)
             to = part * half + col * BLOCK
             hidden[:, to : to + BLOCK] = value
-    for at in range(strips):
-        for part in range(2):
-            down_copy(part, at).wait()
-        value = jnp.dot(hidden[...], w_down[at], preferred_element_type=jnp.float32)
+    for first in range(0, model_width, strip):
+        at = slice(first, first + strip)
+        value = jnp.dot(hidden[:, :half], down_refs[0][:, at], preferred_element_type=jnp.float32)
+        value += jnp.dot(hidden[:, half:], down_refs[1][:, at], preferred_element_type=jnp.float32)
         for place, out in enumerate(outs):
             weighted = value[place * size : (place + 1) * size] * weights[place]
-            out[:, at * strip : (at + 1) * strip] = weighted.astype(jnp.bfloat16)
-
-
-def expert_layer(pieces, own_expert, experts, in_own, in_other, down_own, down_other):
+            out[:, at] = weighted.astype(jnp.bfloat16)
+
+
+def expert_layer(pieces, own_expert, experts, *weights):
     count, size = len(pieces), pieces[0].shape[0]
-    model_width, width = in_own.shape
-    half = width // 2
-    strip = min(8 * BLOCK, model_width)
-    strips, columns = model_width // strip, half // BLOCK
+    model_width, width = weights[0].shape
     total = count * size
     whole = pl.BlockSpec(memory_space=pltpu.VMEM)
-    anywhere = pl.BlockSpec(memory_space=pl.ANY)
+    weights = [pltpu.with_memory_space_constraint(weight, pltpu.VMEM) for weight in weights]
     return pl.pallas_call(
         functools.partial(expert_kernel, count, experts),
-        in_specs=[pl.BlockSpec(memory_space=pltpu.SMEM)] + [whole] * count + [anywhere] * 4,
+        in_specs=[pl.BlockSpec(memory_space=pltpu.SMEM)] + [whole] * (count + len(weights)),
         out_specs=[whole] * count,
         out_shape=[jax.ShapeDtypeStruct((size, model_width), jnp.bfloat16)] * count,
         scratch_shapes=[
             pltpu.VMEM((total, model_width), jnp.bfloat16),
-            pltpu.VMEM((2, columns, model_width, 2 * BLOCK), jnp.bfloat16),
-            pltpu.VMEM((strips, width, strip), jnp.bfloat16),
             pltpu.VMEM((total, width), jnp.bfloat16),
-            pltpu.SemaphoreType.DMA((2, columns)),
-            pltpu.SemaphoreType.DMA((2, strips)),
         ],
         cost_estimate=pl.CostEstimate(
             flops=6 * total * model_width * width,
             bytes_accessed=6 * model_width * width + 4 * total * model_width,
             transcendentals=total * width,
         ),
-        compiler_params=pltpu.CompilerParams(vmem_limit_bytes=32 * 1024 * 1024),
+        compiler_params=pltpu.CompilerParams(vmem_limit_bytes=16 * 1024 * 1024),
         name="expert_layer",
-    )(own_expert, *pieces, in_own, in_other, down_own, down_other)
+    )(own_expert, *pieces, *weights)
 
 
 def across_chips(block, far):

time: 143 us -> 143 us (level)
  Pallas kernels: 34.6 us -> 16.8 us
  local copies, waits for them, and re-layouts: 13.7 us -> 26.8 us
  waiting for transfers between devices: 61.6 us -> 65.8 us
    unnamed x29 -> x41, local copies, waits for them, and re-layouts: 11.1 us -> 24.9 us
    pallas_call x2, Pallas kernels: 23.8 us -> 13 us  [expert_layer(): pl.pallas_call(functools.partial(expert_kernel, count, experts), in_specs...]
    pallas_call x1, Pallas kernels: 6.25 us -> 1.93 us  [dequantize_in(): pl.pallas_call(in_kernel, grid=(rows // strip,), in_specs=[smem, smem, bl...]
    ppermute x6, waiting for transfers between devices: 18.6 us -> 22.4 us  [across_chips(): lax.ppermute(block, 'expert', [(low, low ^ 2 * far) for low in range(coun...]
    pallas_call x1, Pallas kernels: 4.55 us -> 1.85 us  [dequantize_down(): pl.pallas_call(down_kernel, grid=(cols // strip,), in_specs=[pl.BlockSpec...]
  transfers between devices with their start and end apart: 24 -> 24, of which waited for: 16 -> 16; matrix products, arithmetic and copies ran while one was open for 3% -> 2% of each run, Pallas kernels for 15% -> 7%
where the time goes in v7:
time: 143 us; the launch traced here: 142 us
  waiting for transfers between devices  65.8 us (46%)
  starting transfers between devices  28.6 us (20%)
  local copies, waits for them, and re-layouts  26.8 us (19%)
  Pallas kernels  16.8 us (12%)
  other arithmetic  4.16 us (3%)
    ppermute x18, waiting for transfers between devices, from_partner(): return lax.ppermute(block, axis, route)  43.3 us
    unnamed x41, local copies, waits for them, and re-layouts  24.9 us
    ppermute x6, waiting for transfers between devices, across_chips(): lax.ppermute(block, 'expert', [(low, low ^ 2 * far) for low in range(coun...  22.4 us
    ppermute x18, starting transfers between devices, from_partner(): return lax.ppermute(block, axis, route)  17.1 us
    pallas_call x2, Pallas kernels, expert_layer(): pl.pallas_call(functools.partial(expert_kernel, count, experts), in_specs...  13 us
    ppermute x6, starting transfers between devices, across_chips(): lax.ppermute(block, 'expert', [(low, low ^ 2 * far) for low in range(coun...  11.5 us
  transfers between devices with their start and end apart: 24, of which 16 were waited for; matrix products, arithmetic and copies ran while one was open for 2% of the time, Pallas kernels for 7%

profile of v7, /device:TPU:0, one launch (start us, length us, event | category | flops | bytes accessed | tf_op | source)
XLA Modules:
  0.0 142.4 jit_solution(13074323290265434228)
XLA Ops:
  2.0 3.1 %collective-permute-start = (bf16[32,4224]{1,0:T(8,128)(2,1)S(1)}, bf16[32,4224]{1,0:T(8,128)(2,1)S(1)}, u32[]{:S(2)}, u32[]{:S(2)}) collective-permute-start(bf16[32,4224]{1,0:T(8,128)(2,1)S(1)} %concatenate.15), channel_id=1, source_target_pairs={{0,2},{1,3},{2,0},{3,1},{4,6},{5,7},{6,4},{7,5},{8,10},{9,11},{10,... | collective-permute-start | bytes 811016 | tf_op jit(solution)/shard_map/ppermute | solution.py:223
  5.0 6.5 %collective-permute-done = bf16[32,4224]{1,0:T(8,128)(2,1)S(1)} collective-permute-done((bf16[32,4224]{1,0:T(8,128)(2,1)S(1)}, bf16[32,4224]{1,0:T(8,128)(2,1)S(1)}, u32[]{:S(2)}, u32[]{:S(2)}) %collective-permute-start) | collective-permute-done | bytes 270368 | tf_op jit(solution)/shard_map/ppermute | solution.py:223
  11.5 1.7 %collective-permute-start.2 = (bf16[32,4224]{1,0:T(8,128)(2,1)S(1)}, bf16[32,4224]{1,0:T(8,128)(2,1)S(1)}, u32[]{:S(2)}, u32[]{:S(2)}) collective-permute-start(bf16[32,4224]{1,0:T(8,128)(2,1)S(1)} %collective-permute-done), channel_id=1, source_target_pairs={{0,16},{16,0},{8,24},{24,8},{1,17},{17,1},{9,25},{25,9},{2,18},{18... | collective-permute-start | bytes 811016 | tf_op jit(solution)/shard_map/ppermute | solution.py:20
  13.9 2.6 %collective-permute-start.3 = (bf16[32,4224]{1,0:T(8,128)(2,1)S(1)}, bf16[32,4224]{1,0:T(8,128)(2,1)S(1)}, u32[]{:S(2)}, u32[]{:S(2)}) collective-permute-start(bf16[32,4224]{1,0:T(8,128)(2,1)S(1)} %concatenate.15), channel_id=1, source_target_pairs={{0,4},{1,5},{2,6},{3,7},{4,0},{5,1},{6,2},{7,3},{8,12},{9,13},{10,... | collective-permute-start | bytes 811016 | tf_op jit(solution)/shard_map/ppermute | solution.py:223
  16.5 1.5 %collective-permute-start.1 = (bf16[32,4224]{1,0:T(8,128)(2,1)S(1)}, bf16[32,4224]{1,0:T(8,128)(2,1)S(1)}, u32[]{:S(2)}, u32[]{:S(2)}) collective-permute-start(bf16[32,4224]{1,0:T(8,128)(2,1)S(1)} %concatenate.15), channel_id=1, source_target_pairs={{0,8},{8,0},{16,24},{24,16},{1,9},{9,1},{17,25},{25,17},{2,10},{10... | collective-permute-start | bytes 811016 | tf_op jit(solution)/shard_map/ppermute | solution.py:20
  18.0 1.9 %copy-done.8 = bf16[1,4096,384]{2,1,0:T(8,128)(2,1)S(1)} copy-done((bf16[1,4096,384]{2,1,0:T(8,128)(2,1)S(1)}, bf16[1,4096,384]{2,1,0:T(8,128)(2,1)}, u32[]{:S(2)}) %copy-start.8) | copy-done | bytes 3145752
  19.9 1.9 %copy-done.9 = bf16[1,4096,384]{2,1,0:T(8,128)(2,1)S(1)} copy-done((bf16[1,4096,384]{2,1,0:T(8,128)(2,1)S(1)}, bf16[1,4096,384]{2,1,0:T(8,128)(2,1)}, u32[]{:S(2)}) %copy-start.9) | copy-done | bytes 3145752
  21.8 1.9 %dequantize_in.1.refs_4_ = bf16[4096,768]{1,0:T(8,128)(2,1)S(1)} custom-call(f32[3,32]{1,0:T(4,128)S(1)} %get-tuple-element.118.gate_scales, f32[3,32]{1,0:T(4,128)S(1)} %get-tuple-element.117.up_scales, bf16[4096,384]{1,0:T(8,128)(2,1)S(1)} %bitcast.16, bf16[4096,384]{1,0:T(8,128)(2,1)S(1)} %bitcast.17), custom_call_target="tpu_custom_call" | custom-call | flops 3145728 | bytes 12582912 | tf_op jit(solution)/shard_map/dequantize_in/pallas_call | solution.py:120
  23.8 3.8 %collective-permute-done.3 = bf16[32,4224]{1,0:T(8,128)(2,1)S(1)} collective-permute-done((bf16[32,4224]{1,0:T(8,128)(2,1)S(1)}, bf16[32,4224]{1,0:T(8,128)(2,1)S(1)}, u32[]{:S(2)}, u32[]{:S(2)}) %collective-permute-start.3) | collective-permute-done | bytes 270368 | tf_op jit(solution)/shard_map/ppermute | solution.py:223
  27.7 2.6 %copy-done = bf16[4096,768]{1,0:T(8,128)(2,1)} copy-done((bf16[4096,768]{1,0:T(8,128)(2,1)}, bf16[4096,768]{1,0:T(8,128)(2,1)S(1)}, u32[]{:S(2)}) %copy-start) | copy-done | bytes 6291480
  31.8 1.3 collective-permute-start.5
  33.8 1.9 %dequantize_down.1.refs_6_ = bf16[384,4096]{1,0:T(8,128)(2,1)S(1)} custom-call(f32[3,32]{1,0:T(4,128)S(1)} %bitcast.18, bf16[384,4096]{1,0:T(8,128)(2,1)S(1)} %bitcast.15), custom_call_target="tpu_custom_call" | custom-call | flops 1572864 | bytes 6291456 | tf_op jit(solution)/shard_map/dequantize_down/pallas_call | solution.py:148
  35.7 5.8 %collective-permute-done.6 = bf16[32,4224]{1,0:T(8,128)(2,1)S(1)} collective-permute-done((bf16[32,4224]{1,0:T(8,128)(2,1)S(1)}, bf16[32,4224]{1,0:T(8,128)(2,1)S(1)}, u32[]{:S(2)}, u32[]{:S(2)}) %collective-permute-start.6) | collective-permute-done | bytes 270368 | tf_op jit(solution)/shard_map/ppermute | solution.py:223
  41.5 3.6 %collective-permute-done.4.refs_1_ = bf16[64,4224]{1,0:T(8,128)(2,1)S(1)} collective-permute-done((bf16[64,4224]{1,0:T(8,128)(2,1)S(1)}, bf16[64,4224]{1,0:T(8,128)(2,1)S(1)}, u32[]{:S(2)}, u32[]{:S(2)}) %collective-permute-start.4) | collective-permute-done | bytes 540704 | tf_op jit(solution)/shard_map/ppermute | solution.py:20
  47.0 2.7 %copy-done.2 = bf16[4096,768]{1,0:T(8,128)(2,1)} copy-done((bf16[4096,768]{1,0:T(8,128)(2,1)}, bf16[4096,768]{1,0:T(8,128)(2,1)S(1)}, u32[]{:S(2)}) %copy-start.2) | copy-done | bytes 6291480
  51.0 1.5 %collective-permute-start.9 = (bf16[32,4224]{1,0:T(8,128)(2,1)S(1)}, bf16[32,4224]{1,0:T(8,128)(2,1)S(1)}, u32[]{:S(2)}, u32[]{:S(2)}) collective-permute-start(bf16[32,4224]{1,0:T(8,128)(2,1)S(1)} %collective-permute-done.6), channel_id=1, source_target_pairs={{0,16},{16,0},{8,24},{24,8},{1,17},{17,1},{9,25},{25,9},{2,18},{18... | collective-permute-start | bytes 811016 | tf_op jit(solution)/shard_map/ppermute | solution.py:20
  52.6 6.0 %collective-permute-done.8 = bf16[32,4224]{1,0:T(8,128)(2,1)S(1)} collective-permute-done((bf16[32,4224]{1,0:T(8,128)(2,1)S(1)}, bf16[32,4224]{1,0:T(8,128)(2,1)S(1)}, u32[]{:S(2)}, u32[]{:S(2)}) %collective-permute-start.8) | collective-permute-done | bytes 270368 | tf_op jit(solution)/shard_map/ppermute | solution.py:20
  60.5 1.6 %copy-done.5 = bf16[384,4096]{1,0:T(8,128)(2,1)} copy-done((bf16[384,4096]{1,0:T(8,128)(2,1)}, bf16[384,4096]{1,0:T(8,128)(2,1)S(1)}, u32[]{:S(2)}) %copy-start.5) | copy-done | bytes 3145752
  62.2 1.5 %collective-permute-start.11 = (bf16[64,4224]{1,0:T(8,128)(2,1)}, bf16[64,4224]{1,0:T(8,128)(2,1)}, u32[]{:S(2)}, u32[]{:S(2)}) collective-permute-start(bf16[64,4224]{1,0:T(8,128)(2,1)} %pad_maximum_fusion.2.refs_0_), channel_id=1, source_target_pairs={{0,16},{16,0},{8,24},{24,8},{1,17},{17,1},{9,25},{25,9},{2,18},{18... | collective-permute-start | bytes 1622024 | tf_op jit(solution)/shard_map/ppermute | solution.py:20
  64.8 2.8 %copy-done.1 = bf16[4096,768]{1,0:T(8,128)(2,1)S(1)} copy-done((bf16[4096,768]{1,0:T(8,128)(2,1)S(1)}, bf16[4096,768]{1,0:T(8,128)(2,1)}, u32[]{:S(2)}) %copy-start.1) | copy-done | bytes 6291480
  67.6 2.8 %copy-done.3 = bf16[4096,768]{1,0:T(8,128)(2,1)S(1)} copy-done((bf16[4096,768]{1,0:T(8,128)(2,1)S(1)}, bf16[4096,768]{1,0:T(8,128)(2,1)}, u32[]{:S(2)}) %copy-start.3) | copy-done | bytes 6291480
  70.4 1.9 %copy-done.6 = bf16[384,4096]{1,0:T(8,128)(2,1)S(1)} copy-done((bf16[384,4096]{1,0:T(8,128)(2,1)S(1)}, bf16[384,4096]{1,0:T(8,128)(2,1)}, u32[]{:S(2)}) %copy-start.6) | copy-done | bytes 3145752
  76.5 5.7 %expert_layer.2 = (bf16[64,4096]{1,0:T(8,128)(2,1)S(1)}, bf16[64,4096]{1,0:T(8,128)(2,1)S(1)}, bf16[64,4096]{1,0:T(8,128)(2,1)S(1)}, bf16[64,4096]{1,0:T(8,128)(2,1)S(1)}) custom-call(s32[1]{0:T(128)} %bitcast.own_expert, bf16[64,4224]{1,0:T(8,128)(2,1)S(1)} %copy-done.13, bf16[64,4224]{1,0:T(8,128)(2,1)S(1)} %copy-done.15, bf16[64,4224]{1,0:T(8,128)(2,1)S(1)} %copy-done.11, ...), custom_call_target="tpu_custom_call" | custom-call | flops 4831838208 | bytes 23068672 | tf_op jit(solution)/shard_map/expert_layer/pallas_call | solution.py:202
  82.2 7.3 %expert_layer.3 = (bf16[64,4096]{1,0:T(8,128)(2,1)S(1)}, bf16[64,4096]{1,0:T(8,128)(2,1)S(1)}, bf16[64,4096]{1,0:T(8,128)(2,1)S(1)}, bf16[64,4096]{1,0:T(8,128)(2,1)S(1)}) custom-call(s32[1]{0:T(128)} %bitcast.own_expert, bf16[64,4224]{1,0:T(8,128)(2,1)} %pad_maximum_fusion.2.refs_0_, bf16[64,4224]{1,0:T(8,128)(2,1)} %collective-permute-done.11.refs_1_, ...), custom_call_target="tpu_custom_call" | custom-call | flops 4831838208 | bytes 23068672 | tf_op jit(solution)/shard_map/expert_layer/pallas_call | solution.py:202
  91.0 11.6 %collective-permute-done.13 = bf16[64,4096]{1,0:T(8,128)(2,1)S(1)} collective-permute-done((bf16[64,4096]{1,0:T(8,128)(2,1)S(1)}, bf16[64,4096]{1,0:T(8,128)(2,1)S(1)}, u32[]{:S(2)}, u32[]{:S(2)}) %collective-permute-start.13) | collective-permute-done | bytes 524320 | tf_op jit(solution)/shard_map/ppermute | solution.py:20
  102.9 1.6 %collective-permute-start.16 = (bf16[32,4096]{1,0:T(8,128)(2,1)S(1)}, bf16[32,4096]{1,0:T(8,128)(2,1)S(1)}, u32[]{:S(2)}, u32[]{:S(2)}) collective-permute-start(bf16[32,4096]{1,0:T(8,128)(2,1)S(1)} %split.27), channel_id=1, source_target_pairs={{0,16},{16,0},{8,24},{24,8},{1,17},{17,1},{9,25},{25,9},{2,18},{18... | collective-permute-start | bytes 786440 | tf_op jit(solution)/shard_map/ppermute | solution.py:20
  105.2 4.2 %collective-permute-done.16 = bf16[32,4096]{1,0:T(8,128)(2,1)S(1)} collective-permute-done((bf16[32,4096]{1,0:T(8,128)(2,1)S(1)}, bf16[32,4096]{1,0:T(8,128)(2,1)S(1)}, u32[]{:S(2)}, u32[]{:S(2)}) %collective-permute-start.16) | collective-permute-done | bytes 262176 | tf_op jit(solution)/shard_map/ppermute | solution.py:20
  109.4 1.5 %collective-permute-done.15 = bf16[32,4096]{1,0:T(8,128)(2,1)S(1)} collective-permute-done((bf16[32,4096]{1,0:T(8,128)(2,1)S(1)}, bf16[32,4096]{1,0:T(8,128)(2,1)S(1)}, u32[]{:S(2)}, u32[]{:S(2)}) %collective-permute-start.15) | collective-permute-done | bytes 262176 | tf_op jit(solution)/shard_map/ppermute | solution.py:20
  112.9 9.7 %collective-permute-done.19 = bf16[64,4096]{1,0:T(8,128)(2,1)S(1)} collective-permute-done((bf16[64,4096]{1,0:T(8,128)(2,1)S(1)}, bf16[64,4096]{1,0:T(8,128)(2,1)S(1)}, u32[]{:S(2)}, u32[]{:S(2)}) %collective-permute-start.19) | collective-permute-done | bytes 524320 | tf_op jit(solution)/shard_map/ppermute | solution.py:20
  124.2 4.4 %collective-permute-start.18 = (bf16[32,4096]{1,0:T(8,128)(2,1)S(1)}, bf16[32,4096]{1,0:T(8,128)(2,1)S(1)}, u32[]{:S(2)}, u32[]{:S(2)}) collective-permute-start(bf16[32,4096]{1,0:T(8,128)(2,1)S(1)} %add_convert_fusion.7), channel_id=1, source_target_pairs={{0,4},{1,5},{2,6},{3,7},{4,0},{5,1},{6,2},{7,3},{8,12},{9,13},{10,... | collective-permute-start | bytes 786440 | tf_op jit(solution)/shard_map/ppermute | solution.py:223
  129.4 5.7 %collective-permute-done.21 = bf16[32,4096]{1,0:T(8,128)(2,1)S(1)} collective-permute-done((bf16[32,4096]{1,0:T(8,128)(2,1)S(1)}, bf16[32,4096]{1,0:T(8,128)(2,1)S(1)}, u32[]{:S(2)}, u32[]{:S(2)}) %collective-permute-start.21) | collective-permute-done | bytes 262176 | tf_op jit(solution)/shard_map/ppermute | solution.py:20
  135.3 6.3 %collective-permute-done.23 = bf16[32,4096]{1,0:T(8,128)(2,1)S(1)} collective-permute-done((bf16[32,4096]{1,0:T(8,128)(2,1)S(1)}, bf16[32,4096]{1,0:T(8,128)(2,1)S(1)}, u32[]{:S(2)}, u32[]{:S(2)}) %collective-permute-start.23) | collective-permute-done | bytes 262176 | tf_op jit(solution)/shard_map/ppermute | solution.py:223
  (87 shorter events, 23.4 us)
Async XLA Ops:
  2.0 9.6 %collective-permute-start = (bf16[32,4224]{1,0:T(8,128)(2,1)S(1)}, bf16[32,4224]{1,0:T(8,128)(2,1)S(1)}, u32[]{:S(2)}, u32[]{:S(2)}) collective-permute-start(bf16[32,4224]{1,0:T(8,128)(2,1)S(1)} %concatenate.15), channel_id=1, source_target_pairs={{0,2},{1,3},{2,0},{3,1},{4,6},{5,7},{6,4},{7,5},{8,10},{9,11},{10,... | collective-permute-start | bytes 811016 | tf_op jit(solution)/shard_map/ppermute | solution.py:223
  11.5 12.2 %collective-permute-start.2 = (bf16[32,4224]{1,0:T(8,128)(2,1)S(1)}, bf16[32,4224]{1,0:T(8,128)(2,1)S(1)}, u32[]{:S(2)}, u32[]{:S(2)}) collective-permute-start(bf16[32,4224]{1,0:T(8,128)(2,1)S(1)} %collective-permute-done), channel_id=1, source_target_pairs={{0,16},{16,0},{8,24},{24,8},{1,17},{17,1},{9,25},{25,9},{2,18},{18... | collective-permute-start | bytes 811016 | tf_op jit(solution)/shard_map/ppermute | solution.py:20
  13.9 13.8 %collective-permute-start.3 = (bf16[32,4224]{1,0:T(8,128)(2,1)S(1)}, bf16[32,4224]{1,0:T(8,128)(2,1)S(1)}, u32[]{:S(2)}, u32[]{:S(2)}) collective-permute-start(bf16[32,4224]{1,0:T(8,128)(2,1)S(1)} %concatenate.15), channel_id=1, source_target_pairs={{0,4},{1,5},{2,6},{3,7},{4,0},{5,1},{6,2},{7,3},{8,12},{9,13},{10,... | collective-permute-start | bytes 811016 | tf_op jit(solution)/shard_map/ppermute | solution.py:223
  16.5 7.3 %collective-permute-start.1 = (bf16[32,4224]{1,0:T(8,128)(2,1)S(1)}, bf16[32,4224]{1,0:T(8,128)(2,1)S(1)}, u32[]{:S(2)}, u32[]{:S(2)}) collective-permute-start(bf16[32,4224]{1,0:T(8,128)(2,1)S(1)} %concatenate.15), channel_id=1, source_target_pairs={{0,8},{8,0},{16,24},{24,16},{1,9},{9,1},{17,25},{25,17},{2,10},{10... | collective-permute-start | bytes 811016 | tf_op jit(solution)/shard_map/ppermute | solution.py:20
  21.8 12.0 %copy-start.7 = (bf16[1,384,4096]{2,1,0:T(8,128)(2,1)S(1)}, bf16[1,384,4096]{2,1,0:T(8,128)(2,1)}, u32[]{:S(2)}) copy-start(bf16[1,384,4096]{2,1,0:T(8,128)(2,1)} %param.14) | copy-start | bytes 9437188
  23.7 10.1 %copy-start.19 = (f32[1,3,32]{2,0,1:T(1,128)S(1)}, f32[1,3,32]{2,0,1:T(1,128)}, u32[]{:S(2)}) copy-start(f32[1,3,32]{2,0,1:T(1,128)} %param.17) | copy-start | bytes 1156
  23.8 11.9 %copy-start.10 = (bf16[64,4224]{1,0:T(8,128)(2,1)}, bf16[64,4224]{1,0:T(8,128)(2,1)S(1)}, u32[]{:S(2)}) copy-start(bf16[64,4224]{1,0:T(8,128)(2,1)S(1)} %pad_maximum_fusion.1.refs_2_) | copy-start | bytes 1622020
  27.7 19.4 %collective-permute-start.7 = (bf16[4096,768]{1,0:T(8,128)(2,1)S(1)}, bf16[4096,768]{1,0:T(8,128)(2,1)S(1)}, u32[]{:S(2)}, u32[]{:S(2)}) collective-permute-start(bf16[4096,768]{1,0:T(8,128)(2,1)S(1)} %dequantize_in.1.refs_4_), channel_id=1, source_target_pairs={{0,1},{1,0},{2,3},{3,2},{4,5},{5,4},{6,7},{7,6},{8,9},{9,8},{10,11... | collective-permute-start | bytes 18874376 | tf_op jit(solution)/shard_map/ppermute | solution.py:20
  30.3 14.7 %collective-permute-start.4 = (bf16[64,4224]{1,0:T(8,128)(2,1)S(1)}, bf16[64,4224]{1,0:T(8,128)(2,1)S(1)}, u32[]{:S(2)}, u32[]{:S(2)}) collective-permute-start(bf16[64,4224]{1,0:T(8,128)(2,1)S(1)} %pad_maximum_fusion.refs_0_), channel_id=1, source_target_pairs={{0,16},{16,0},{8,24},{24,8},{1,17},{17,1},{9,25},{25,9},{2,18},{18... | collective-permute-start | bytes 1622024 | tf_op jit(solution)/shard_map/ppermute | solution.py:20
  31.8 14.4 %collective-permute-start.5 = (bf16[64,4224]{1,0:T(8,128)(2,1)S(1)}, bf16[64,4224]{1,0:T(8,128)(2,1)S(1)}, u32[]{:S(2)}, u32[]{:S(2)}) collective-permute-start(bf16[64,4224]{1,0:T(8,128)(2,1)S(1)} %pad_maximum_fusion.1.refs_2_), channel_id=1, source_target_pairs={{0,8},{8,0},{16,24},{24,16},{1,9},{9,1},{17,25},{25,17},{2,10},{10... | collective-permute-start | bytes 1622024 | tf_op jit(solution)/shard_map/ppermute | solution.py:20
  33.1 8.3 %collective-permute-start.6 = (bf16[32,4224]{1,0:T(8,128)(2,1)S(1)}, bf16[32,4224]{1,0:T(8,128)(2,1)S(1)}, u32[]{:S(2)}, u32[]{:S(2)}) collective-permute-start(bf16[32,4224]{1,0:T(8,128)(2,1)S(1)} %collective-permute-done.3), channel_id=1, source_target_pairs={{0,2},{1,3},{2,0},{3,1},{4,6},{5,7},{6,4},{7,5},{8,10},{9,11},{10,... | collective-permute-start | bytes 811016 | tf_op jit(solution)/shard_map/ppermute | solution.py:223
  47.0 2.7 %copy-start.2 = (bf16[4096,768]{1,0:T(8,128)(2,1)}, bf16[4096,768]{1,0:T(8,128)(2,1)S(1)}, u32[]{:S(2)}) copy-start(bf16[4096,768]{1,0:T(8,128)(2,1)S(1)} %collective-permute-done.7.refs_5_) | copy-start | bytes 18874372
  49.7 10.8 %collective-permute-start.10 = (bf16[384,4096]{1,0:T(8,128)(2,1)S(1)}, bf16[384,4096]{1,0:T(8,128)(2,1)S(1)}, u32[]{:S(2)}, u32[]{:S(2)}) collective-permute-start(bf16[384,4096]{1,0:T(8,128)(2,1)S(1)} %dequantize_down.1.refs_6_), channel_id=1, source_target_pairs={{0,1},{1,0},{2,3},{3,2},{4,5},{5,4},{6,7},{7,6},{8,9},{9,8},{10,11... | collective-permute-start | bytes 9437192 | tf_op jit(solution)/shard_map/ppermute | solution.py:20
  49.7 8.9 %collective-permute-start.8 = (bf16[32,4224]{1,0:T(8,128)(2,1)S(1)}, bf16[32,4224]{1,0:T(8,128)(2,1)S(1)}, u32[]{:S(2)}, u32[]{:S(2)}) collective-permute-start(bf16[32,4224]{1,0:T(8,128)(2,1)S(1)} %collective-permute-done.3), channel_id=1, source_target_pairs={{0,8},{8,0},{16,24},{24,16},{1,9},{9,1},{17,25},{25,17},{2,10},{10... | collective-permute-start | bytes 811016 | tf_op jit(solution)/shard_map/ppermute | solution.py:20
  51.0 8.6 %collective-permute-start.9 = (bf16[32,4224]{1,0:T(8,128)(2,1)S(1)}, bf16[32,4224]{1,0:T(8,128)(2,1)S(1)}, u32[]{:S(2)}, u32[]{:S(2)}) collective-permute-start(bf16[32,4224]{1,0:T(8,128)(2,1)S(1)} %collective-permute-done.6), channel_id=1, source_target_pairs={{0,16},{16,0},{8,24},{24,8},{1,17},{17,1},{9,25},{25,9},{2,18},{18... | collective-permute-start | bytes 811016 | tf_op jit(solution)/shard_map/ppermute | solution.py:20
  62.2 20.0 %collective-permute-start.11 = (bf16[64,4224]{1,0:T(8,128)(2,1)}, bf16[64,4224]{1,0:T(8,128)(2,1)}, u32[]{:S(2)}, u32[]{:S(2)}) collective-permute-start(bf16[64,4224]{1,0:T(8,128)(2,1)} %pad_maximum_fusion.2.refs_0_), channel_id=1, source_target_pairs={{0,16},{16,0},{8,24},{24,8},{1,17},{17,1},{9,25},{25,9},{2,18},{18... | collective-permute-start | bytes 1622024 | tf_op jit(solution)/shard_map/ppermute | solution.py:20
  63.7 18.5 %collective-permute-start.12 = (bf16[64,4224]{1,0:T(8,128)(2,1)}, bf16[64,4224]{1,0:T(8,128)(2,1)}, u32[]{:S(2)}, u32[]{:S(2)}) collective-permute-start(bf16[64,4224]{1,0:T(8,128)(2,1)} %pad_maximum_fusion.3.refs_2_), channel_id=1, source_target_pairs={{0,8},{8,0},{16,24},{24,16},{1,9},{9,1},{17,25},{25,17},{2,10},{10... | collective-permute-start | bytes 1622024 | tf_op jit(solution)/shard_map/ppermute | solution.py:20
  64.8 2.8 %copy-start.1 = (bf16[4096,768]{1,0:T(8,128)(2,1)S(1)}, bf16[4096,768]{1,0:T(8,128)(2,1)}, u32[]{:S(2)}) copy-start(bf16[4096,768]{1,0:T(8,128)(2,1)} %copy-done) | copy-start | bytes 18874372
  67.6 2.8 %copy-start.3 = (bf16[4096,768]{1,0:T(8,128)(2,1)S(1)}, bf16[4096,768]{1,0:T(8,128)(2,1)}, u32[]{:S(2)}) copy-start(bf16[4096,768]{1,0:T(8,128)(2,1)} %copy-done.2) | copy-start | bytes 18874372
  76.5 5.7 %copy-start.4 = (bf16[4096,768]{1,0:T(8,128)(2,1)S(1)}, bf16[4096,768]{1,0:T(8,128)(2,1)}, u32[]{:S(2)}) copy-start(bf16[4096,768]{1,0:T(8,128)(2,1)} %copy-done.2) | copy-start | bytes 18874372
  89.5 13.1 %collective-permute-start.13 = (bf16[64,4096]{1,0:T(8,128)(2,1)S(1)}, bf16[64,4096]{1,0:T(8,128)(2,1)S(1)}, u32[]{:S(2)}, u32[]{:S(2)}) collective-permute-start(bf16[64,4096]{1,0:T(8,128)(2,1)S(1)} %get-tuple-element.94), channel_id=1, source_target_pairs={{0,16},{16,0},{8,24},{24,8},{1,17},{17,1},{9,25},{25,9},{2,18},{18... | collective-permute-start | bytes 1572872 | tf_op jit(solution)/shard_map/ppermute | solution.py:20
  90.1 12.7 %collective-permute-start.14 = (bf16[64,4096]{1,0:T(8,128)(2,1)S(1)}, bf16[64,4096]{1,0:T(8,128)(2,1)S(1)}, u32[]{:S(2)}, u32[]{:S(2)}) collective-permute-start(bf16[64,4096]{1,0:T(8,128)(2,1)S(1)} %get-tuple-element.96), channel_id=1, source_target_pairs={{0,8},{8,0},{16,24},{24,16},{1,9},{9,1},{17,25},{25,17},{2,10},{10... | collective-permute-start | bytes 1572872 | tf_op jit(solution)/shard_map/ppermute | solution.py:20
  102.9 6.4 %collective-permute-start.16 = (bf16[32,4096]{1,0:T(8,128)(2,1)S(1)}, bf16[32,4096]{1,0:T(8,128)(2,1)S(1)}, u32[]{:S(2)}, u32[]{:S(2)}) collective-permute-start(bf16[32,4096]{1,0:T(8,128)(2,1)S(1)} %split.27), channel_id=1, source_target_pairs={{0,16},{16,0},{8,24},{24,8},{1,17},{17,1},{9,25},{25,9},{2,18},{18... | collective-permute-start | bytes 786440 | tf_op jit(solution)/shard_map/ppermute | solution.py:20
  104.5 6.4 %collective-permute-start.15 = (bf16[32,4096]{1,0:T(8,128)(2,1)S(1)}, bf16[32,4096]{1,0:T(8,128)(2,1)S(1)}, u32[]{:S(2)}, u32[]{:S(2)}) collective-permute-start(bf16[32,4096]{1,0:T(8,128)(2,1)S(1)} %split.25), channel_id=1, source_target_pairs={{0,8},{8,0},{16,24},{24,16},{1,9},{9,1},{17,25},{25,17},{2,10},{10... | collective-permute-start | bytes 786440 | tf_op jit(solution)/shard_map/ppermute | solution.py:20
  111.0 11.5 %collective-permute-start.19 = (bf16[64,4096]{1,0:T(8,128)(2,1)S(1)}, bf16[64,4096]{1,0:T(8,128)(2,1)S(1)}, u32[]{:S(2)}, u32[]{:S(2)}) collective-permute-start(bf16[64,4096]{1,0:T(8,128)(2,1)S(1)} %get-tuple-element.110), channel_id=1, source_target_pairs={{0,16},{16,0},{8,24},{24,8},{1,17},{17,1},{9,25},{25,9},{2,18},{18... | collective-permute-start | bytes 1572872 | tf_op jit(solution)/shard_map/ppermute | solution.py:20
  111.6 12.5 %collective-permute-start.17 = (bf16[32,4096]{1,0:T(8,128)(2,1)S(1)}, bf16[32,4096]{1,0:T(8,128)(2,1)S(1)}, u32[]{:S(2)}, u32[]{:S(2)}) collective-permute-start(bf16[32,4096]{1,0:T(8,128)(2,1)S(1)} %add_convert_fusion.8), channel_id=1, source_target_pairs={{0,2},{1,3},{2,0},{3,1},{4,6},{5,7},{6,4},{7,5},{8,10},{9,11},{10,... | collective-permute-start | bytes 786440 | tf_op jit(solution)/shard_map/ppermute | solution.py:223
  112.3 10.4 %collective-permute-start.20 = (bf16[64,4096]{1,0:T(8,128)(2,1)S(1)}, bf16[64,4096]{1,0:T(8,128)(2,1)S(1)}, u32[]{:S(2)}, u32[]{:S(2)}) collective-permute-start(bf16[64,4096]{1,0:T(8,128)(2,1)S(1)} %get-tuple-element.112), channel_id=1, source_target_pairs={{0,8},{8,0},{16,24},{24,16},{1,9},{9,1},{17,25},{25,17},{2,10},{10... | collective-permute-start | bytes 1572872 | tf_op jit(solution)/shard_map/ppermute | solution.py:20
  122.8 6.4 %collective-permute-start.22 = (bf16[32,4096]{1,0:T(8,128)(2,1)S(1)}, bf16[32,4096]{1,0:T(8,128)(2,1)S(1)}, u32[]{:S(2)}, u32[]{:S(2)}) collective-permute-start(bf16[32,4096]{1,0:T(8,128)(2,1)S(1)} %split.31), channel_id=1, source_target_pairs={{0,16},{16,0},{8,24},{24,8},{1,17},{17,1},{9,25},{25,9},{2,18},{18... | collective-permute-start | bytes 786440 | tf_op jit(solution)/shard_map/ppermute | solution.py:20
  124.2 17.3 %copy-start.18 = (bf16[32,4096]{1,0:T(8,128)(2,1)S(1)}, bf16[32,4096]{1,0:T(8,128)(2,1)}, u32[]{:S(2)}) copy-start(bf16[32,4096]{1,0:T(8,128)(2,1)} %param.9) | copy-start | bytes 786436
  124.2 11.1 %collective-permute-start.18 = (bf16[32,4096]{1,0:T(8,128)(2,1)S(1)}, bf16[32,4096]{1,0:T(8,128)(2,1)S(1)}, u32[]{:S(2)}, u32[]{:S(2)}) collective-permute-start(bf16[32,4096]{1,0:T(8,128)(2,1)S(1)} %add_convert_fusion.7), channel_id=1, source_target_pairs={{0,4},{1,5},{2,6},{3,7},{4,0},{5,1},{6,2},{7,3},{8,12},{9,13},{10,... | collective-permute-start | bytes 786440 | tf_op jit(solution)/shard_map/ppermute | solution.py:223
  128.6 6.4 %collective-permute-start.21 = (bf16[32,4096]{1,0:T(8,128)(2,1)S(1)}, bf16[32,4096]{1,0:T(8,128)(2,1)S(1)}, u32[]{:S(2)}, u32[]{:S(2)}) collective-permute-start(bf16[32,4096]{1,0:T(8,128)(2,1)S(1)} %split.29), channel_id=1, source_target_pairs={{0,8},{8,0},{16,24},{24,16},{1,9},{9,1},{17,25},{25,17},{2,10},{10... | collective-permute-start | bytes 786440 | tf_op jit(solution)/shard_map/ppermute | solution.py:20
  135.1 6.4 %collective-permute-start.23 = (bf16[32,4096]{1,0:T(8,128)(2,1)S(1)}, bf16[32,4096]{1,0:T(8,128)(2,1)S(1)}, u32[]{:S(2)}, u32[]{:S(2)}) collective-permute-start(bf16[32,4096]{1,0:T(8,128)(2,1)S(1)} %add_convert_fusion.5), channel_id=1, source_target_pairs={{0,2},{1,3},{2,0},{3,1},{4,6},{5,7},{6,4},{7,5},{8,10},{9,11},{10,... | collective-permute-start | bytes 786440 | tf_op jit(solution)/shard_map/ppermute | solution.py:223
  (12 other events, 16.6 us)

commit v8 on v7

--- a/solution.py
+++ b/solution.py
@@ -244,14 +244,18 @@
     place = jnp.reshape(own_expert, (1,)).astype(jnp.int32)
     last = len(bits) - 1
     pairs = [(first, first + 1) for first in range(0, pair_count, 2)]
+    place, payload = together((place, payload))
     came = {0: payload, 1: across_chips(payload, 1)}
 
     def along_z(far):
         low = far & -far
         came[far] = across_chips(came[far ^ low], low)
 
-    gate_own, up_own, came = together((gate_q[0], up_q[0], came))
-    pieces, outs, in_other, down_other = {}, {}, None, None
+    in_own = dequantize_in(gate_q[0], up_q[0], gate_scale[0], up_scale[0])
+    down_own = dequantize_down(down_q[0], down_scale[0])
+    came, in_own, down_own = together((came, in_own, down_own))
+    in_other, down_other = from_partner(in_own, "expert", 0), None
+    pieces, outs, weights = {}, {}, None
     for number, pair in enumerate(pairs):
         following = pairs[number + 1] if number + 1 < len(pairs) else ()
         blocks = {far: came[far] for far in pair}
@@ -265,23 +269,18 @@
                 blocks = {
                     far: jnp.concatenate([blocks[far], arrived[far]], axis=0) for far in pair
                 }
-            if number == 0 and turn == 0:
-                in_own = dequantize_in(gate_own, up_own, gate_scale[0], up_scale[0])
-                blocks, came, in_own, down_own = together((blocks, came, in_own, down_q[0]))
-                in_other = from_partner(in_own, "expert", 0)
-                down_own = dequantize_down(down_own, down_scale[0])
-            elif number == 0 and turn == last:
-                tied = (pieces[pair], came, in_other, down_own)
-                pieces[pair], came, in_other, down_own = together(tied)
-                down_other = from_partner(down_own, "expert", 0)
-                weights = (in_own, in_other, down_own)
-            elif number == 1 and turn == 0:
-                blocks, pieces, down_other = together((blocks, pieces, down_other))
-                held = pieces[pairs[0]]
-                outs[pairs[0]] = expert_layer(held, place, expert_count, *weights, down_other)
-        if number > 0:
+                if number == 0 and turn == 0:
+                    blocks, came, down_own = together((blocks, came, down_own))
+                    down_other = from_partner(down_own, "expert", 0)
+                elif number == 1 and turn == 0:
+                    blocks, outs = together((blocks, outs))
+        if number == 0:
+            tied = (pieces[pair], came, in_other, down_other)
+            pieces[pair], came, in_other, down_other = together(tied)
+            weights = (in_own, in_other, down_own, down_other)
+        else:
             pieces[pair], outs = together((pieces[pair], outs))
-            outs[pair] = expert_layer(pieces[pair], place, expert_count, *weights, down_other)
+        outs[pair] = expert_layer(pieces[pair], place, expert_count, *weights)
 
     total = tokens.astype(jnp.float32)
     sums = {}

time: 143 us -> 126 us (0.88)
  local copies, waits for them, and re-layouts: 26.8 us -> 4.85 us
  waiting for transfers between devices: 65.8 us -> 77.3 us
  starting transfers between devices: 28.6 us -> 25.8 us
  other arithmetic: 4.16 us -> 2.53 us
  Pallas kernels: 16.8 us -> 15.2 us
    unnamed x41 -> x13, local copies, waits for them, and re-layouts: 24.9 us -> 3.56 us
    ppermute x18, waiting for transfers between devices: 43.3 us -> 58.2 us  [from_partner(): return lax.ppermute(block, axis, route)]
    ppermute x6, waiting for transfers between devices: 22.4 us -> 19 us  [across_chips(): lax.ppermute(block, 'expert', [(low, low ^ 2 * far) for low in range(coun...]
    ppermute x6, starting transfers between devices: 11.5 us -> 9.26 us  [across_chips(): lax.ppermute(block, 'expert', [(low, low ^ 2 * far) for low in range(coun...]
    concatenate x4, other arithmetic: 1.79 us -> 0.16 us  [by_sums(): jnp.concatenate([blocks[far], arrived[far]], axis=0)]
    pallas_call x2, Pallas kernels: 13 us -> 11.5 us  [expert_layer(): pl.pallas_call(functools.partial(expert_kernel, count, experts), in_specs...]
  transfers between devices with their start and end apart: 24 -> 24, of which waited for: 16 -> 19; matrix products, arithmetic and copies ran while one was open for 2% -> 1% of each run, Pallas kernels for 7% -> 8%
where the time goes in v8:
time: 126 us
  waiting for transfers between devices  77.3 us (61%)
  starting transfers between devices  25.8 us (20%)
  Pallas kernels  15.2 us (12%)
  local copies, waits for them, and re-layouts  4.85 us (4%)
  other arithmetic  2.53 us (2%)
    ppermute x18, waiting for transfers between devices, from_partner(): return lax.ppermute(block, axis, route)  58.2 us
    ppermute x6, waiting for transfers between devices, across_chips(): lax.ppermute(block, 'expert', [(low, low ^ 2 * far) for low in range(coun...  19 us
    ppermute x18, starting transfers between devices, from_partner(): return lax.ppermute(block, axis, route)  16.5 us
    pallas_call x2, Pallas kernels, expert_layer(): pl.pallas_call(functools.partial(expert_kernel, count, experts), in_specs...  11.5 us
    ppermute x6, starting transfers between devices, across_chips(): lax.ppermute(block, 'expert', [(low, low ^ 2 * far) for low in range(coun...  9.26 us
    unnamed x13, local copies, waits for them, and re-layouts  3.56 us
  transfers between devices with their start and end apart: 24, of which 19 were waited for; matrix products, arithmetic and copies ran while one was open for 1% of the time, Pallas kernels for 8%

profile of v8, /device:TPU:0, one launch (start us, length us, event | category | flops | bytes accessed | tf_op | source)
XLA Modules:
  0.0 125.9 jit_solution(687690664688521563)
XLA Ops:
  0.9 1.0 concatenate.15
  2.0 3.1 %collective-permute-start = (bf16[32,4224]{1,0:T(8,128)(2,1)S(1)}, bf16[32,4224]{1,0:T(8,128)(2,1)S(1)}, u32[]{:S(2)}, u32[]{:S(2)}) collective-permute-start(bf16[32,4224]{1,0:T(8,128)(2,1)S(1)} %concatenate.15), channel_id=1, source_target_pairs={{0,2},{1,3},{2,0},{3,1},{4,6},{5,7},{6,4},{7,5},{8,10},{9,11},{10,... | collective-permute-start | bytes 811016 | tf_op jit(solution)/shard_map/ppermute | solution.py:223
  5.7 1.9 %copy-done = bf16[1,384,4096]{2,1,0:T(8,128)(2,1)S(1)} copy-done((bf16[1,384,4096]{2,1,0:T(8,128)(2,1)S(1)}, bf16[1,384,4096]{2,1,0:T(8,128)(2,1)}, u32[]{:S(2)}) %copy-start) | copy-done | bytes 3145752
  7.6 1.8 %dequantize_down.1.refs_6_ = bf16[384,4096]{1,0:T(8,128)(2,1)S(1)} custom-call(f32[3,32]{1,0:T(4,128)S(1)} %bitcast.18, bf16[384,4096]{1,0:T(8,128)(2,1)S(1)} %bitcast.15), custom_call_target="tpu_custom_call" | custom-call | flops 1572864 | bytes 6291456 | tf_op jit(solution)/shard_map/dequantize_down/pallas_call | solution.py:148
  9.5 1.0 copy-done.2
  10.5 1.9 %dequantize_in.1.refs_4_ = bf16[4096,768]{1,0:T(8,128)(2,1)S(1)} custom-call(f32[3,32]{1,0:T(4,128)S(1)} %get-tuple-element.118.gate_scales, f32[3,32]{1,0:T(4,128)S(1)} %get-tuple-element.117.up_scales, bf16[4096,384]{1,0:T(8,128)(2,1)S(1)} %bitcast.16, bf16[4096,384]{1,0:T(8,128)(2,1)S(1)} %bitcast.17), custom_call_target="tpu_custom_call" | custom-call | flops 3145728 | bytes 12582912 | tf_op jit(solution)/shard_map/dequantize_in/pallas_call | solution.py:120
  12.5 1.6 %collective-permute-start.2 = (bf16[32,4224]{1,0:T(8,128)(2,1)S(1)}, bf16[32,4224]{1,0:T(8,128)(2,1)S(1)}, u32[]{:S(2)}, u32[]{:S(2)}) collective-permute-start(bf16[32,4224]{1,0:T(8,128)(2,1)S(1)} %collective-permute-done), channel_id=1, source_target_pairs={{0,16},{16,0},{8,24},{24,8},{1,17},{17,1},{9,25},{25,9},{2,18},{18... | collective-permute-start | bytes 811016 | tf_op jit(solution)/shard_map/ppermute | solution.py:20
  14.1 2.6 %collective-permute-start.3 = (bf16[32,4224]{1,0:T(8,128)(2,1)S(1)}, bf16[32,4224]{1,0:T(8,128)(2,1)S(1)}, u32[]{:S(2)}, u32[]{:S(2)}) collective-permute-start(bf16[32,4224]{1,0:T(8,128)(2,1)S(1)} %concatenate.15), channel_id=1, source_target_pairs={{0,4},{1,5},{2,6},{3,7},{4,0},{5,1},{6,2},{7,3},{8,12},{9,13},{10,... | collective-permute-start | bytes 811016 | tf_op jit(solution)/shard_map/ppermute | solution.py:223
  16.7 1.5 %collective-permute-start.1 = (bf16[32,4224]{1,0:T(8,128)(2,1)S(1)}, bf16[32,4224]{1,0:T(8,128)(2,1)S(1)}, u32[]{:S(2)}, u32[]{:S(2)}) collective-permute-start(bf16[32,4224]{1,0:T(8,128)(2,1)S(1)} %concatenate.15), channel_id=1, source_target_pairs={{0,8},{8,0},{16,24},{24,16},{1,9},{9,1},{17,25},{25,17},{2,10},{10... | collective-permute-start | bytes 811016 | tf_op jit(solution)/shard_map/ppermute | solution.py:20
  18.2 3.2 %collective-permute-done.2 = bf16[32,4224]{1,0:T(8,128)(2,1)S(1)} collective-permute-done((bf16[32,4224]{1,0:T(8,128)(2,1)S(1)}, bf16[32,4224]{1,0:T(8,128)(2,1)S(1)}, u32[]{:S(2)}, u32[]{:S(2)}) %collective-permute-start.2) | collective-permute-done | bytes 270368 | tf_op jit(solution)/shard_map/ppermute | solution.py:20
  21.5 3.5 %collective-permute-done.1 = bf16[32,4224]{1,0:T(8,128)(2,1)S(1)} collective-permute-done((bf16[32,4224]{1,0:T(8,128)(2,1)S(1)}, bf16[32,4224]{1,0:T(8,128)(2,1)S(1)}, u32[]{:S(2)}, u32[]{:S(2)}) %collective-permute-start.1) | collective-permute-done | bytes 270368 | tf_op jit(solution)/shard_map/ppermute | solution.py:20
  25.0 4.3 %collective-permute-done.3 = bf16[32,4224]{1,0:T(8,128)(2,1)S(1)} collective-permute-done((bf16[32,4224]{1,0:T(8,128)(2,1)S(1)}, bf16[32,4224]{1,0:T(8,128)(2,1)S(1)}, u32[]{:S(2)}, u32[]{:S(2)}) %collective-permute-start.3) | collective-permute-done | bytes 270368 | tf_op jit(solution)/shard_map/ppermute | solution.py:223
  29.9 1.5 %collective-permute-start.5 = (bf16[64,4224]{1,0:T(8,128)(2,1)S(1)}, bf16[64,4224]{1,0:T(8,128)(2,1)S(1)}, u32[]{:S(2)}, u32[]{:S(2)}) collective-permute-start(bf16[64,4224]{1,0:T(8,128)(2,1)S(1)} %pad_maximum_fusion.1.refs_2_), channel_id=1, source_target_pairs={{0,8},{8,0},{16,24},{24,16},{1,9},{9,1},{17,25},{25,17},{2,10},{10... | collective-permute-start | bytes 1622024 | tf_op jit(solution)/shard_map/ppermute | solution.py:20
  31.4 8.3 %collective-permute-done.6 = bf16[32,4224]{1,0:T(8,128)(2,1)S(1)} collective-permute-done((bf16[32,4224]{1,0:T(8,128)(2,1)S(1)}, bf16[32,4224]{1,0:T(8,128)(2,1)S(1)}, u32[]{:S(2)}, u32[]{:S(2)}) %collective-permute-start.6) | collective-permute-done | bytes 270368 | tf_op jit(solution)/shard_map/ppermute | solution.py:223
  39.7 4.4 %collective-permute-done.4.refs_1_ = bf16[64,4224]{1,0:T(8,128)(2,1)S(1)} collective-permute-done((bf16[64,4224]{1,0:T(8,128)(2,1)S(1)}, bf16[64,4224]{1,0:T(8,128)(2,1)S(1)}, u32[]{:S(2)}, u32[]{:S(2)}) %collective-permute-start.4) | collective-permute-done | bytes 540704 | tf_op jit(solution)/shard_map/ppermute | solution.py:20
  44.3 1.5 %collective-permute-start.9 = (bf16[32,4224]{1,0:T(8,128)(2,1)S(1)}, bf16[32,4224]{1,0:T(8,128)(2,1)S(1)}, u32[]{:S(2)}, u32[]{:S(2)}) collective-permute-start(bf16[32,4224]{1,0:T(8,128)(2,1)S(1)} %collective-permute-done.3), channel_id=1, source_target_pairs={{0,8},{8,0},{16,24},{24,16},{1,9},{9,1},{17,25},{25,17},{2,10},{10... | collective-permute-start | bytes 811016 | tf_op jit(solution)/shard_map/ppermute | solution.py:20
  45.8 1.5 %collective-permute-start.10 = (bf16[32,4224]{1,0:T(8,128)(2,1)S(1)}, bf16[32,4224]{1,0:T(8,128)(2,1)S(1)}, u32[]{:S(2)}, u32[]{:S(2)}) collective-permute-start(bf16[32,4224]{1,0:T(8,128)(2,1)S(1)} %collective-permute-done.6), channel_id=1, source_target_pairs={{0,16},{16,0},{8,24},{24,8},{1,17},{17,1},{9,25},{25,9},{2,18},{18... | collective-permute-start | bytes 811016 | tf_op jit(solution)/shard_map/ppermute | solution.py:20
  47.3 5.7 %expert_layer.2 = (bf16[64,4096]{1,0:T(8,128)(2,1)S(1)}, bf16[64,4096]{1,0:T(8,128)(2,1)S(1)}, bf16[64,4096]{1,0:T(8,128)(2,1)S(1)}, bf16[64,4096]{1,0:T(8,128)(2,1)S(1)}) custom-call(s32[1]{0:T(128)} %bitcast.own_expert, bf16[64,4224]{1,0:T(8,128)(2,1)S(1)} %pad_maximum_fusion.refs_0_, bf16[64,4224]{1,0:T(8,128)(2,1)S(1)} %collective-permute-done.4.refs_1_, ...), custom_call_target="tpu_custom_call" | custom-call | flops 4831838208 | bytes 23068672 | tf_op jit(solution)/shard_map/expert_layer/pallas_call | solution.py:202
  53.5 1.4 %collective-permute-start.11 = (bf16[64,4224]{1,0:T(8,128)(2,1)S(1)}, bf16[64,4224]{1,0:T(8,128)(2,1)S(1)}, u32[]{:S(2)}, u32[]{:S(2)}) collective-permute-start(bf16[64,4224]{1,0:T(8,128)(2,1)S(1)} %pad_maximum_fusion.2.refs_0_), channel_id=1, source_target_pairs={{0,16},{16,0},{8,24},{24,8},{1,17},{17,1},{9,25},{25,9},{2,18},{18... | collective-permute-start | bytes 1622024 | tf_op jit(solution)/shard_map/ppermute | solution.py:20
  55.4 10.8 %collective-permute-done.11.refs_1_ = bf16[64,4224]{1,0:T(8,128)(2,1)S(1)} collective-permute-done((bf16[64,4224]{1,0:T(8,128)(2,1)S(1)}, bf16[64,4224]{1,0:T(8,128)(2,1)S(1)}, u32[]{:S(2)}, u32[]{:S(2)}) %collective-permute-start.11) | collective-permute-done | bytes 540704 | tf_op jit(solution)/shard_map/ppermute | solution.py:20
  67.0 5.7 %expert_layer.3 = (bf16[64,4096]{1,0:T(8,128)(2,1)S(1)}, bf16[64,4096]{1,0:T(8,128)(2,1)S(1)}, bf16[64,4096]{1,0:T(8,128)(2,1)S(1)}, bf16[64,4096]{1,0:T(8,128)(2,1)S(1)}) custom-call(s32[1]{0:T(128)} %bitcast.own_expert, bf16[64,4224]{1,0:T(8,128)(2,1)S(1)} %pad_maximum_fusion.2.refs_0_, bf16[64,4224]{1,0:T(8,128)(2,1)S(1)} %collective-permute-done.11.refs_1_, ...), custom_call_target="tpu_custom_call" | custom-call | flops 4831838208 | bytes 23068672 | tf_op jit(solution)/shard_map/expert_layer/pallas_call | solution.py:202
  72.8 1.0 collective-permute-start.13
  74.3 9.4 %collective-permute-done.13 = bf16[64,4096]{1,0:T(8,128)(2,1)S(1)} collective-permute-done((bf16[64,4096]{1,0:T(8,128)(2,1)S(1)}, bf16[64,4096]{1,0:T(8,128)(2,1)S(1)}, u32[]{:S(2)}, u32[]{:S(2)}) %collective-permute-start.13) | collective-permute-done | bytes 524320 | tf_op jit(solution)/shard_map/ppermute | solution.py:20
  83.8 1.3 %collective-permute-done.14 = bf16[64,4096]{1,0:T(8,128)(2,1)S(1)} collective-permute-done((bf16[64,4096]{1,0:T(8,128)(2,1)S(1)}, bf16[64,4096]{1,0:T(8,128)(2,1)S(1)}, u32[]{:S(2)}, u32[]{:S(2)}) %collective-permute-start.14) | collective-permute-done | bytes 524320 | tf_op jit(solution)/shard_map/ppermute | solution.py:20
  86.5 7.0 %collective-permute-done.16 = bf16[32,4096]{1,0:T(8,128)(2,1)S(1)} collective-permute-done((bf16[32,4096]{1,0:T(8,128)(2,1)S(1)}, bf16[32,4096]{1,0:T(8,128)(2,1)S(1)}, u32[]{:S(2)}, u32[]{:S(2)}) %collective-permute-start.16) | collective-permute-done | bytes 262176 | tf_op jit(solution)/shard_map/ppermute | solution.py:20
  94.3 1.9 %collective-permute-start.19 = (bf16[64,4096]{1,0:T(8,128)(2,1)S(1)}, bf16[64,4096]{1,0:T(8,128)(2,1)S(1)}, u32[]{:S(2)}, u32[]{:S(2)}) collective-permute-start(bf16[64,4096]{1,0:T(8,128)(2,1)S(1)} %get-tuple-element.110), channel_id=1, source_target_pairs={{0,16},{16,0},{8,24},{24,8},{1,17},{17,1},{9,25},{25,9},{2,18},{18... | collective-permute-start | bytes 1572872 | tf_op jit(solution)/shard_map/ppermute | solution.py:20
  96.7 9.4 %collective-permute-done.19 = bf16[64,4096]{1,0:T(8,128)(2,1)S(1)} collective-permute-done((bf16[64,4096]{1,0:T(8,128)(2,1)S(1)}, bf16[64,4096]{1,0:T(8,128)(2,1)S(1)}, u32[]{:S(2)}, u32[]{:S(2)}) %collective-permute-start.19) | collective-permute-done | bytes 524320 | tf_op jit(solution)/shard_map/ppermute | solution.py:20
  106.2 1.3 %collective-permute-done.20 = bf16[64,4096]{1,0:T(8,128)(2,1)S(1)} collective-permute-done((bf16[64,4096]{1,0:T(8,128)(2,1)S(1)}, bf16[64,4096]{1,0:T(8,128)(2,1)S(1)}, u32[]{:S(2)}, u32[]{:S(2)}) %collective-permute-start.20) | collective-permute-done | bytes 524320 | tf_op jit(solution)/shard_map/ppermute | solution.py:20
  108.6 3.5 %collective-permute-start.18 = (bf16[32,4096]{1,0:T(8,128)(2,1)S(1)}, bf16[32,4096]{1,0:T(8,128)(2,1)S(1)}, u32[]{:S(2)}, u32[]{:S(2)}) collective-permute-start(bf16[32,4096]{1,0:T(8,128)(2,1)S(1)} %add_convert_fusion.7), channel_id=1, source_target_pairs={{0,4},{1,5},{2,6},{3,7},{4,0},{5,1},{6,2},{7,3},{8,12},{9,13},{10,... | collective-permute-start | bytes 786440 | tf_op jit(solution)/shard_map/ppermute | solution.py:223
  112.5 1.6 %collective-permute-done.22 = bf16[32,4096]{1,0:T(8,128)(2,1)S(1)} collective-permute-done((bf16[32,4096]{1,0:T(8,128)(2,1)S(1)}, bf16[32,4096]{1,0:T(8,128)(2,1)S(1)}, u32[]{:S(2)}, u32[]{:S(2)}) %collective-permute-start.22) | collective-permute-done | bytes 262176 | tf_op jit(solution)/shard_map/ppermute | solution.py:20
  114.2 4.3 %collective-permute-done.21 = bf16[32,4096]{1,0:T(8,128)(2,1)S(1)} collective-permute-done((bf16[32,4096]{1,0:T(8,128)(2,1)S(1)}, bf16[32,4096]{1,0:T(8,128)(2,1)S(1)}, u32[]{:S(2)}, u32[]{:S(2)}) %collective-permute-start.21) | collective-permute-done | bytes 262176 | tf_op jit(solution)/shard_map/ppermute | solution.py:20
  119.2 5.8 %collective-permute-done.23 = bf16[32,4096]{1,0:T(8,128)(2,1)S(1)} collective-permute-done((bf16[32,4096]{1,0:T(8,128)(2,1)S(1)}, bf16[32,4096]{1,0:T(8,128)(2,1)S(1)}, u32[]{:S(2)}, u32[]{:S(2)}) %collective-permute-start.23) | collective-permute-done | bytes 262176 | tf_op jit(solution)/shard_map/ppermute | solution.py:223
  (59 shorter events, 10.8 us)
Async XLA Ops:
  0.9 8.6 %copy-start.5 = (f32[1,32,3]{1,0,2:T(1,128)S(1)}, f32[1,32,3]{1,0,2:T(1,128)}, u32[]{:S(2)}) copy-start(f32[1,32,3]{1,0,2:T(1,128)} %param.15) | copy-start | bytes 1156
  2.0 10.5 %collective-permute-start = (bf16[32,4224]{1,0:T(8,128)(2,1)S(1)}, bf16[32,4224]{1,0:T(8,128)(2,1)S(1)}, u32[]{:S(2)}, u32[]{:S(2)}) collective-permute-start(bf16[32,4224]{1,0:T(8,128)(2,1)S(1)} %concatenate.15), channel_id=1, source_target_pairs={{0,2},{1,3},{2,0},{3,1},{4,6},{5,7},{6,4},{7,5},{8,10},{9,11},{10,... | collective-permute-start | bytes 811016 | tf_op jit(solution)/shard_map/ppermute | solution.py:223
  5.7 1.9 %copy-start = (bf16[1,384,4096]{2,1,0:T(8,128)(2,1)S(1)}, bf16[1,384,4096]{2,1,0:T(8,128)(2,1)}, u32[]{:S(2)}) copy-start(bf16[1,384,4096]{2,1,0:T(8,128)(2,1)} %param.14) | copy-start | bytes 9437188
  7.6 1.9 %copy-start.4 = (f32[1,32,3]{1,0,2:T(1,128)S(1)}, f32[1,32,3]{1,0,2:T(1,128)}, u32[]{:S(2)}) copy-start(f32[1,32,3]{1,0,2:T(1,128)} %param.16) | copy-start | bytes 1156
  7.6 1.9 %copy-start.1 = (bf16[1,4096,384]{2,1,0:T(8,128)(2,1)S(1)}, bf16[1,4096,384]{2,1,0:T(8,128)(2,1)}, u32[]{:S(2)}) copy-start(bf16[1,4096,384]{2,1,0:T(8,128)(2,1)} %param.12) | copy-start | bytes 9437188
  7.6 2.9 %copy-start.2 = (bf16[1,4096,384]{2,1,0:T(8,128)(2,1)S(1)}, bf16[1,4096,384]{2,1,0:T(8,128)(2,1)}, u32[]{:S(2)}) copy-start(bf16[1,4096,384]{2,1,0:T(8,128)(2,1)} %param.13) | copy-start | bytes 9437188
  12.4 31.8 %collective-permute-start.7 = (bf16[4096,768]{1,0:T(8,128)(2,1)S(1)}, bf16[4096,768]{1,0:T(8,128)(2,1)S(1)}, u32[]{:S(2)}, u32[]{:S(2)}) collective-permute-start(bf16[4096,768]{1,0:T(8,128)(2,1)S(1)} %dequantize_in.1.refs_4_), channel_id=1, source_target_pairs={{0,1},{1,0},{2,3},{3,2},{4,5},{5,4},{6,7},{7,6},{8,9},{9,8},{10,11... | collective-permute-start | bytes 18874376 | tf_op jit(solution)/shard_map/ppermute | solution.py:20
  12.5 8.9 %collective-permute-start.2 = (bf16[32,4224]{1,0:T(8,128)(2,1)S(1)}, bf16[32,4224]{1,0:T(8,128)(2,1)S(1)}, u32[]{:S(2)}, u32[]{:S(2)}) collective-permute-start(bf16[32,4224]{1,0:T(8,128)(2,1)S(1)} %collective-permute-done), channel_id=1, source_target_pairs={{0,16},{16,0},{8,24},{24,8},{1,17},{17,1},{9,25},{25,9},{2,18},{18... | collective-permute-start | bytes 811016 | tf_op jit(solution)/shard_map/ppermute | solution.py:20
  14.1 15.2 %collective-permute-start.3 = (bf16[32,4224]{1,0:T(8,128)(2,1)S(1)}, bf16[32,4224]{1,0:T(8,128)(2,1)S(1)}, u32[]{:S(2)}, u32[]{:S(2)}) collective-permute-start(bf16[32,4224]{1,0:T(8,128)(2,1)S(1)} %concatenate.15), channel_id=1, source_target_pairs={{0,4},{1,5},{2,6},{3,7},{4,0},{5,1},{6,2},{7,3},{8,12},{9,13},{10,... | collective-permute-start | bytes 811016 | tf_op jit(solution)/shard_map/ppermute | solution.py:223
  16.7 8.3 %collective-permute-start.1 = (bf16[32,4224]{1,0:T(8,128)(2,1)S(1)}, bf16[32,4224]{1,0:T(8,128)(2,1)S(1)}, u32[]{:S(2)}, u32[]{:S(2)}) collective-permute-start(bf16[32,4224]{1,0:T(8,128)(2,1)S(1)} %concatenate.15), channel_id=1, source_target_pairs={{0,8},{8,0},{16,24},{24,16},{1,9},{9,1},{17,25},{25,17},{2,10},{10... | collective-permute-start | bytes 811016 | tf_op jit(solution)/shard_map/ppermute | solution.py:20
  29.3 14.9 %collective-permute-start.8 = (bf16[384,4096]{1,0:T(8,128)(2,1)S(1)}, bf16[384,4096]{1,0:T(8,128)(2,1)S(1)}, u32[]{:S(2)}, u32[]{:S(2)}) collective-permute-start(bf16[384,4096]{1,0:T(8,128)(2,1)S(1)} %dequantize_down.1.refs_6_), channel_id=1, source_target_pairs={{0,1},{1,0},{2,3},{3,2},{4,5},{5,4},{6,7},{7,6},{8,9},{9,8},{10,11... | collective-permute-start | bytes 9437192 | tf_op jit(solution)/shard_map/ppermute | solution.py:20
  29.4 14.7 %collective-permute-start.4 = (bf16[64,4224]{1,0:T(8,128)(2,1)S(1)}, bf16[64,4224]{1,0:T(8,128)(2,1)S(1)}, u32[]{:S(2)}, u32[]{:S(2)}) collective-permute-start(bf16[64,4224]{1,0:T(8,128)(2,1)S(1)} %pad_maximum_fusion.refs_0_), channel_id=1, source_target_pairs={{0,16},{16,0},{8,24},{24,8},{1,17},{17,1},{9,25},{25,9},{2,18},{18... | collective-permute-start | bytes 1622024 | tf_op jit(solution)/shard_map/ppermute | solution.py:20
  29.9 14.4 %collective-permute-start.5 = (bf16[64,4224]{1,0:T(8,128)(2,1)S(1)}, bf16[64,4224]{1,0:T(8,128)(2,1)S(1)}, u32[]{:S(2)}, u32[]{:S(2)}) collective-permute-start(bf16[64,4224]{1,0:T(8,128)(2,1)S(1)} %pad_maximum_fusion.1.refs_2_), channel_id=1, source_target_pairs={{0,8},{8,0},{16,24},{24,16},{1,9},{9,1},{17,25},{25,17},{2,10},{10... | collective-permute-start | bytes 1622024 | tf_op jit(solution)/shard_map/ppermute | solution.py:20
  31.4 8.3 %collective-permute-start.6 = (bf16[32,4224]{1,0:T(8,128)(2,1)S(1)}, bf16[32,4224]{1,0:T(8,128)(2,1)S(1)}, u32[]{:S(2)}, u32[]{:S(2)}) collective-permute-start(bf16[32,4224]{1,0:T(8,128)(2,1)S(1)} %collective-permute-done.3), channel_id=1, source_target_pairs={{0,2},{1,3},{2,0},{3,1},{4,6},{5,7},{6,4},{7,5},{8,10},{9,11},{10,... | collective-permute-start | bytes 811016 | tf_op jit(solution)/shard_map/ppermute | solution.py:223
  44.3 8.8 %collective-permute-start.9 = (bf16[32,4224]{1,0:T(8,128)(2,1)S(1)}, bf16[32,4224]{1,0:T(8,128)(2,1)S(1)}, u32[]{:S(2)}, u32[]{:S(2)}) collective-permute-start(bf16[32,4224]{1,0:T(8,128)(2,1)S(1)} %collective-permute-done.3), channel_id=1, source_target_pairs={{0,8},{8,0},{16,24},{24,16},{1,9},{9,1},{17,25},{25,17},{2,10},{10... | collective-permute-start | bytes 811016 | tf_op jit(solution)/shard_map/ppermute | solution.py:20
  45.8 7.7 %collective-permute-start.10 = (bf16[32,4224]{1,0:T(8,128)(2,1)S(1)}, bf16[32,4224]{1,0:T(8,128)(2,1)S(1)}, u32[]{:S(2)}, u32[]{:S(2)}) collective-permute-start(bf16[32,4224]{1,0:T(8,128)(2,1)S(1)} %collective-permute-done.6), channel_id=1, source_target_pairs={{0,16},{16,0},{8,24},{24,8},{1,17},{17,1},{9,25},{25,9},{2,18},{18... | collective-permute-start | bytes 811016 | tf_op jit(solution)/shard_map/ppermute | solution.py:20
  53.5 12.8 %collective-permute-start.11 = (bf16[64,4224]{1,0:T(8,128)(2,1)S(1)}, bf16[64,4224]{1,0:T(8,128)(2,1)S(1)}, u32[]{:S(2)}, u32[]{:S(2)}) collective-permute-start(bf16[64,4224]{1,0:T(8,128)(2,1)S(1)} %pad_maximum_fusion.2.refs_0_), channel_id=1, source_target_pairs={{0,16},{16,0},{8,24},{24,8},{1,17},{17,1},{9,25},{25,9},{2,18},{18... | collective-permute-start | bytes 1622024 | tf_op jit(solution)/shard_map/ppermute | solution.py:20
  54.9 12.1 %collective-permute-start.12 = (bf16[64,4224]{1,0:T(8,128)(2,1)S(1)}, bf16[64,4224]{1,0:T(8,128)(2,1)S(1)}, u32[]{:S(2)}, u32[]{:S(2)}) collective-permute-start(bf16[64,4224]{1,0:T(8,128)(2,1)S(1)} %pad_maximum_fusion.3.refs_2_), channel_id=1, source_target_pairs={{0,8},{8,0},{16,24},{24,16},{1,9},{9,1},{17,25},{25,17},{2,10},{10... | collective-permute-start | bytes 1622024 | tf_op jit(solution)/shard_map/ppermute | solution.py:20
  72.8 10.9 %collective-permute-start.13 = (bf16[64,4096]{1,0:T(8,128)(2,1)S(1)}, bf16[64,4096]{1,0:T(8,128)(2,1)S(1)}, u32[]{:S(2)}, u32[]{:S(2)}) collective-permute-start(bf16[64,4096]{1,0:T(8,128)(2,1)S(1)} %get-tuple-element.94), channel_id=1, source_target_pairs={{0,16},{16,0},{8,24},{24,8},{1,17},{17,1},{9,25},{25,9},{2,18},{18... | collective-permute-start | bytes 1572872 | tf_op jit(solution)/shard_map/ppermute | solution.py:20
  73.8 11.4 %collective-permute-start.14 = (bf16[64,4096]{1,0:T(8,128)(2,1)S(1)}, bf16[64,4096]{1,0:T(8,128)(2,1)S(1)}, u32[]{:S(2)}, u32[]{:S(2)}) collective-permute-start(bf16[64,4096]{1,0:T(8,128)(2,1)S(1)} %get-tuple-element.96), channel_id=1, source_target_pairs={{0,8},{8,0},{16,24},{24,16},{1,9},{9,1},{17,25},{25,17},{2,10},{10... | collective-permute-start | bytes 1572872 | tf_op jit(solution)/shard_map/ppermute | solution.py:20
  85.3 8.2 %collective-permute-start.16 = (bf16[32,4096]{1,0:T(8,128)(2,1)S(1)}, bf16[32,4096]{1,0:T(8,128)(2,1)S(1)}, u32[]{:S(2)}, u32[]{:S(2)}) collective-permute-start(bf16[32,4096]{1,0:T(8,128)(2,1)S(1)} %split.27), channel_id=1, source_target_pairs={{0,16},{16,0},{8,24},{24,8},{1,17},{17,1},{9,25},{25,9},{2,18},{18... | collective-permute-start | bytes 786440 | tf_op jit(solution)/shard_map/ppermute | solution.py:20
  85.9 8.3 %collective-permute-start.15 = (bf16[32,4096]{1,0:T(8,128)(2,1)S(1)}, bf16[32,4096]{1,0:T(8,128)(2,1)S(1)}, u32[]{:S(2)}, u32[]{:S(2)}) collective-permute-start(bf16[32,4096]{1,0:T(8,128)(2,1)S(1)} %split.25), channel_id=1, source_target_pairs={{0,8},{8,0},{16,24},{24,16},{1,9},{9,1},{17,25},{25,17},{2,10},{10... | collective-permute-start | bytes 786440 | tf_op jit(solution)/shard_map/ppermute | solution.py:20
  94.3 11.8 %collective-permute-start.19 = (bf16[64,4096]{1,0:T(8,128)(2,1)S(1)}, bf16[64,4096]{1,0:T(8,128)(2,1)S(1)}, u32[]{:S(2)}, u32[]{:S(2)}) collective-permute-start(bf16[64,4096]{1,0:T(8,128)(2,1)S(1)} %get-tuple-element.110), channel_id=1, source_target_pairs={{0,16},{16,0},{8,24},{24,8},{1,17},{17,1},{9,25},{25,9},{2,18},{18... | collective-permute-start | bytes 1572872 | tf_op jit(solution)/shard_map/ppermute | solution.py:20
  96.1 12.4 %collective-permute-start.17 = (bf16[32,4096]{1,0:T(8,128)(2,1)S(1)}, bf16[32,4096]{1,0:T(8,128)(2,1)S(1)}, u32[]{:S(2)}, u32[]{:S(2)}) collective-permute-start(bf16[32,4096]{1,0:T(8,128)(2,1)S(1)} %add_convert_fusion.8), channel_id=1, source_target_pairs={{0,2},{1,3},{2,0},{3,1},{4,6},{5,7},{6,4},{7,5},{8,10},{9,11},{10,... | collective-permute-start | bytes 786440 | tf_op jit(solution)/shard_map/ppermute | solution.py:223
  96.1 11.4 %collective-permute-start.20 = (bf16[64,4096]{1,0:T(8,128)(2,1)S(1)}, bf16[64,4096]{1,0:T(8,128)(2,1)S(1)}, u32[]{:S(2)}, u32[]{:S(2)}) collective-permute-start(bf16[64,4096]{1,0:T(8,128)(2,1)S(1)} %get-tuple-element.112), channel_id=1, source_target_pairs={{0,8},{8,0},{16,24},{24,16},{1,9},{9,1},{17,25},{25,17},{2,10},{10... | collective-permute-start | bytes 1572872 | tf_op jit(solution)/shard_map/ppermute | solution.py:20
  107.7 6.4 %collective-permute-start.22 = (bf16[32,4096]{1,0:T(8,128)(2,1)S(1)}, bf16[32,4096]{1,0:T(8,128)(2,1)S(1)}, u32[]{:S(2)}, u32[]{:S(2)}) collective-permute-start(bf16[32,4096]{1,0:T(8,128)(2,1)S(1)} %split.31), channel_id=1, source_target_pairs={{0,16},{16,0},{8,24},{24,8},{1,17},{17,1},{9,25},{25,9},{2,18},{18... | collective-permute-start | bytes 786440 | tf_op jit(solution)/shard_map/ppermute | solution.py:20
  108.6 16.5 %copy-start.3 = (bf16[32,4096]{1,0:T(8,128)(2,1)S(1)}, bf16[32,4096]{1,0:T(8,128)(2,1)}, u32[]{:S(2)}) copy-start(bf16[32,4096]{1,0:T(8,128)(2,1)} %param.9) | copy-start | bytes 786436
  108.6 10.7 %collective-permute-start.18 = (bf16[32,4096]{1,0:T(8,128)(2,1)S(1)}, bf16[32,4096]{1,0:T(8,128)(2,1)S(1)}, u32[]{:S(2)}, u32[]{:S(2)}) collective-permute-start(bf16[32,4096]{1,0:T(8,128)(2,1)S(1)} %add_convert_fusion.7), channel_id=1, source_target_pairs={{0,4},{1,5},{2,6},{3,7},{4,0},{5,1},{6,2},{7,3},{8,12},{9,13},{10,... | collective-permute-start | bytes 786440 | tf_op jit(solution)/shard_map/ppermute | solution.py:223
  112.1 6.4 %collective-permute-start.21 = (bf16[32,4096]{1,0:T(8,128)(2,1)S(1)}, bf16[32,4096]{1,0:T(8,128)(2,1)S(1)}, u32[]{:S(2)}, u32[]{:S(2)}) collective-permute-start(bf16[32,4096]{1,0:T(8,128)(2,1)S(1)} %split.29), channel_id=1, source_target_pairs={{0,8},{8,0},{16,24},{24,16},{1,9},{9,1},{17,25},{25,17},{2,10},{10... | collective-permute-start | bytes 786440 | tf_op jit(solution)/shard_map/ppermute | solution.py:20
  118.6 6.4 %collective-permute-start.23 = (bf16[32,4096]{1,0:T(8,128)(2,1)S(1)}, bf16[32,4096]{1,0:T(8,128)(2,1)S(1)}, u32[]{:S(2)}, u32[]{:S(2)}) collective-permute-start(bf16[32,4096]{1,0:T(8,128)(2,1)S(1)} %add_convert_fusion.5), channel_id=1, source_target_pairs={{0,2},{1,3},{2,0},{3,1},{4,6},{5,7},{6,4},{7,5},{8,10},{9,11},{10,... | collective-permute-start | bytes 786440 | tf_op jit(solution)/shard_map/ppermute | solution.py:223

commit v9 on v8

--- a/solution.py
+++ b/solution.py
@@ -238,70 +238,126 @@
     low = (weight - high.astype(jnp.float32)).astype(jnp.bfloat16)
     extra = -(-2 * expert_count // BLOCK) * BLOCK
     pad = jnp.zeros((token_count, extra - 2 * expert_count), jnp.bfloat16)
-    payload = jnp.concatenate([tokens, high, low, pad], axis=1)
+    half = token_count // 2
+    halves = [slice(0, half), slice(half, token_count)]
+    payload = [
+        jnp.concatenate([part[rows] for part in (tokens, high, low, pad)], axis=1)
+        for rows in halves
+    ]
 
     together = lax.optimization_barrier
     place = jnp.reshape(own_expert, (1,)).astype(jnp.int32)
-    last = len(bits) - 1
-    pairs = [(first, first + 1) for first in range(0, pair_count, 2)]
-    place, payload = together((place, payload))
-    came = {0: payload, 1: across_chips(payload, 1)}
+    turns = len(bits)
+    groups = [(0,), *((far, far + 1) for far in range(1, pair_count - 1, 2)), (pair_count - 1,)]
+
+    def lanes_of(group):
+        if len(group) == 2:
+            return [came[far] for far in group]
+        return [came[group[0]][:half], came[group[0]][half:]]
 
     def along_z(far):
         low = far & -far
         came[far] = across_chips(came[far ^ low], low)
 
-    in_own = dequantize_in(gate_q[0], up_q[0], gate_scale[0], up_scale[0])
-    down_own = dequantize_down(down_q[0], down_scale[0])
-    came, in_own, down_own = together((came, in_own, down_own))
-    in_other, down_other = from_partner(in_own, "expert", 0), None
-    pieces, outs, weights = {}, {}, None
-    for number, pair in enumerate(pairs):
-        following = pairs[number + 1] if number + 1 < len(pairs) else ()
-        blocks = {far: came[far] for far in pair}
-        for turn in range(len(bits)):
-            if turn < len(following):
-                along_z(following[turn])
-            arrived = {far: from_partner(blocks[far], "dp", orders[far % 2][turn]) for far in pair}
-            if turn == last:
-                pieces[pair] = [part for far in pair for part in (blocks[far], arrived[far])]
+    def gather_turn(number, turn):
+        blocks = lanes[number]
+        arrived = [from_partner(block, "dp", orders[lane][turn]) for lane, block in enumerate(blocks)]
+        if turn == turns - 1:
+            lanes[number] = [part for pair in zip(blocks, arrived) for part in pair]
+        else:
+            lanes[number] = [jnp.concatenate(pair, axis=0) for pair in zip(blocks, arrived)]
+
+    def layer(number):
+        return expert_layer(lanes[number], place, expert_count, *weights)
+
+    place, payload = together((place, payload))
+    lanes, outs = {0: payload}, {}
+    near = [{far: across_chips(payload[0], far) for far in groups[1]}]
+    gather_turn(0, 0)
+    lanes, near, payload, gate_own, up_own, down_own = together(
+        (lanes, near, payload, gate_q[0], up_q[0], down_q[0])
+    )
+    in_own = dequantize_in(gate_own, up_own, gate_scale[0], up_scale[0])
+    in_other = from_partner(in_own, "expert", 0)
+    down_own = dequantize_down(down_own, down_scale[0])
+    near.append({far: across_chips(payload[1], far) for far in groups[1]})
+    for turn in range(1, turns):
+        gather_turn(0, turn)
+    lanes, near, down_own = together((lanes, near, down_own))
+    came = {far: jnp.concatenate([part[far] for part in near], axis=0) for far in groups[1]}
+    down_other = from_partner(down_own, "expert", 0)
+    lanes[1] = lanes_of(groups[1])
+    for number in range(1, len(groups)):
+        following = groups[number + 1] if number + 1 < len(groups) else ()
+        for turn in range(int(number > 1), turns - 1):
+            gather_turn(number, turn)
+            if turn == int(number > 1):
+                for far in following:
+                    along_z(far)
+            tied = (lanes, came, outs, in_other, down_other)
+            lanes, came, outs, in_other, down_other = together(tied)
+        weights = (in_own, in_other, down_own, down_other)
+        gather_turn(number, turns - 1)
+        if following:
+            if turns - 1 == int(number > 1):
+                for far in following:
+                    along_z(far)
+            lanes[number + 1] = lanes_of(following)
+            gather_turn(number + 1, 0)
+        outs[number - 1] = layer(number - 1)
+        lanes, outs, came = together((lanes, outs, came))
+    final = len(groups) - 1
+    outs[final] = layer(final)
+
+    def sum_turn(number, turn):
+        result = []
+        for lane in range(2):
+            if turn == turns - 1:
+                kept, sent = outs[number][2 * lane : 2 * lane + 2]
             else:
-                blocks = {
-                    far: jnp.concatenate([blocks[far], arrived[far]], axis=0) for far in pair
-                }
-                if number == 0 and turn == 0:
-                    blocks, came, down_own = together((blocks, came, down_own))
-                    down_other = from_partner(down_own, "expert", 0)
-                elif number == 1 and turn == 0:
-                    blocks, outs = together((blocks, outs))
-        if number == 0:
-            tied = (pieces[pair], came, in_other, down_other)
-            pieces[pair], came, in_other, down_other = together(tied)
-            weights = (in_own, in_other, down_own, down_other)
-        else:
-            pieces[pair], outs = together((pieces[pair], outs))
-        outs[pair] = expert_layer(pieces[pair], place, expert_count, *weights)
-
-    total = tokens.astype(jnp.float32)
-    sums = {}
-    for pair in pairs[::-1]:
-        for turn in range(last, -1, -1):
-            for where, far in enumerate(pair):
-                if turn == last:
-                    kept, sent = outs[pair][2 * where : 2 * where + 2]
-                else:
-                    kept, sent = jnp.split(sums[far], 2, axis=0)
-                sums[far] = added(kept, from_partner(sent, "dp", orders[far % 2][turn]))
-            sums, outs = together((sums, outs))
-        for far in reversed(pair):
-            block, low = sums.pop(far), far & -far
-            if far == 0:
-                total = total + block.astype(jnp.float32)
-            elif far == low:
-                total = total + across_chips(block, low).astype(jnp.float32)
+                kept, sent = jnp.split(sums[number][lane], 2, axis=0)
+            result.append(added(kept, from_partner(sent, "dp", orders[lane][turn])))
+        sums[number] = result
+
+    def leave(number):
+        group, done = groups[number], sums.pop(number)
+        done = done if len(group) == 2 else [jnp.concatenate(done, axis=0)]
+        ready = dict(zip(group, done))
+        for far in reversed(group):
+            block, low = ready[far], far & -far
+            if far in merged:
+                block = added(block, merged.pop(far))
+            if far != low:
+                came_back = across_chips(block, low)
+                into = far ^ low
+                merged[into] = added(merged[into], came_back) if into in merged else came_back
+            elif number > 1:
+                whole = across_chips(block, low)
+                parts.append([whole[rows] for rows in halves])
             else:
-                sums[far ^ low] = added(sums[far ^ low], across_chips(block, low))
-    return total.astype(jnp.bfloat16)
+                leaving[far] = [block[rows] for rows in halves]
+
+    sums, merged, parts, leaving = {}, {}, [], {}
+    for number in range(final, 0, -1):
+        for turn in range(turns - 1 - int(number < final), -1, -1):
+            sum_turn(number, turn)
+            if turn == 0 and number > 1:
+                sum_turn(number - 1, turns - 1)
+            sums, outs, merged = together((sums, outs, merged))
+        leave(number)
+    back = [{far: across_chips(leaving[far][0], far) for far in groups[1]}]
+    for turn in range(turns - 1, 0, -1):
+        sum_turn(0, turn)
+    sums, back, leaving = together((sums, back, leaving))
+    back.append({far: across_chips(leaving[far][1], far) for far in groups[1]})
+    sum_turn(0, 0)
+    result = []
+    for lane, rows in enumerate(halves):
+        total = tokens[rows].astype(jnp.float32) + sums[0][lane].astype(jnp.float32)
+        for part in [*back[lane].values(), *(part[lane] for part in parts)]:
+            total = total + part.astype(jnp.float32)
+        result.append(total.astype(jnp.bfloat16))
+    return jnp.concatenate(result, axis=0)
 
 
 def shards(tokens, expert_ids, *weights):

time: 126 us -> 125 us (level)
  waiting for transfers between devices: 77.3 us -> 59.5 us
  starting transfers between devices: 25.8 us -> 41.7 us
    ppermute x18 -> x26, waiting for transfers between devices: 58.2 us -> 48.2 us  [from_partner(): return lax.ppermute(block, axis, route)]
    ppermute x18 -> x26, starting transfers between devices: 16.5 us -> 25.7 us  [from_partner(): return lax.ppermute(block, axis, route)]
    ppermute x6 -> x10, waiting for transfers between devices: 19 us -> 11.3 us  [across_chips(): lax.ppermute(block, 'expert', [(low, low ^ 2 * far) for low in range(coun...]
    ppermute x6 -> x10, starting transfers between devices: 9.26 us -> 16 us  [across_chips(): lax.ppermute(block, 'expert', [(low, low ^ 2 * far) for low in range(coun...]
    pallas_call x2 -> x3, Pallas kernels: 11.5 us -> 12 us  [expert_layer(): pl.pallas_call(functools.partial(expert_kernel, count, experts), in_specs...]
    unnamed x13 -> x17, local copies, waits for them, and re-layouts: 3.56 us -> 3.82 us
  transfers between devices with their start and end apart: 24 -> 36, of which waited for: 19 -> 22; matrix products, arithmetic and copies ran while one was open for 1% -> 1% of each run, Pallas kernels for 8% -> 9%
where the time goes in v9:
time: 125 us
  waiting for transfers between devices  59.5 us (48%)
  starting transfers between devices  41.7 us (33%)
  Pallas kernels  15.8 us (13%)
  local copies, waits for them, and re-layouts  5.25 us (4%)
  other arithmetic  2.6 us (2%)
    ppermute x26, waiting for transfers between devices, from_partner(): return lax.ppermute(block, axis, route)  48.2 us
    ppermute x26, starting transfers between devices, from_partner(): return lax.ppermute(block, axis, route)  25.7 us
    ppermute x10, starting transfers between devices, across_chips(): lax.ppermute(block, 'expert', [(low, low ^ 2 * far) for low in range(coun...  16 us
    pallas_call x3, Pallas kernels, expert_layer(): pl.pallas_call(functools.partial(expert_kernel, count, experts), in_specs...  12 us
    ppermute x10, waiting for transfers between devices, across_chips(): lax.ppermute(block, 'expert', [(low, low ^ 2 * far) for low in range(coun...  11.3 us
    unnamed x17, local copies, waits for them, and re-layouts  3.82 us
  transfers between devices with their start and end apart: 36, of which 22 were waited for; matrix products, arithmetic and copies ran while one was open for 1% of the time, Pallas kernels for 9%

profile of v9, /device:TPU:0, one launch (start us, length us, event | category | flops | bytes accessed | tf_op | source)
XLA Modules:
  0.0 125.2 jit_solution(10980905669091841678)
XLA Ops:
  2.1 4.0 %collective-permute-start.3 = (bf16[16,4224]{1,0:T(8,128)(2,1)S(1)}, bf16[16,4224]{1,0:T(8,128)(2,1)S(1)}, u32[]{:S(2)}, u32[]{:S(2)}) collective-permute-start(bf16[16,4224]{1,0:T(8,128)(2,1)S(1)} %concatenate.38), channel_id=1, source_target_pairs={{0,4},{1,5},{2,6},{3,7},{4,0},{5,1},{6,2},{7,3},{8,12},{9,13},{10,... | collective-permute-start | bytes 405512 | tf_op jit(solution)/shard_map/ppermute | solution.py:223
  6.1 1.6 %collective-permute-start.2 = (bf16[16,4224]{1,0:T(8,128)(2,1)S(1)}, bf16[16,4224]{1,0:T(8,128)(2,1)S(1)}, u32[]{:S(2)}, u32[]{:S(2)}) collective-permute-start(bf16[16,4224]{1,0:T(8,128)(2,1)S(1)} %concatenate.38), channel_id=1, source_target_pairs={{0,2},{1,3},{2,0},{3,1},{4,6},{5,7},{6,4},{7,5},{8,10},{9,11},{10,... | collective-permute-start | bytes 405512 | tf_op jit(solution)/shard_map/ppermute | solution.py:223
  7.7 1.5 %collective-permute-start = (bf16[16,4224]{1,0:T(8,128)(2,1)S(1)}, bf16[16,4224]{1,0:T(8,128)(2,1)S(1)}, u32[]{:S(2)}, u32[]{:S(2)}) collective-permute-start(bf16[16,4224]{1,0:T(8,128)(2,1)S(1)} %concatenate.38), channel_id=1, source_target_pairs={{0,8},{8,0},{16,24},{24,16},{1,9},{9,1},{17,25},{25,17},{2,10},{10... | collective-permute-start | bytes 405512 | tf_op jit(solution)/shard_map/ppermute | solution.py:20
  9.2 1.5 %collective-permute-start.1 = (bf16[16,4224]{1,0:T(8,128)(2,1)S(1)}, bf16[16,4224]{1,0:T(8,128)(2,1)S(1)}, u32[]{:S(2)}, u32[]{:S(2)}) collective-permute-start(bf16[16,4224]{1,0:T(8,128)(2,1)S(1)} %concatenate.39), channel_id=1, source_target_pairs={{0,16},{16,0},{8,24},{24,8},{1,17},{17,1},{9,25},{25,9},{2,18},{18... | collective-permute-start | bytes 405512 | tf_op jit(solution)/shard_map/ppermute | solution.py:20
  10.7 3.5 %collective-permute-done.1 = bf16[16,4224]{1,0:T(8,128)(2,1)S(1)} collective-permute-done((bf16[16,4224]{1,0:T(8,128)(2,1)S(1)}, bf16[16,4224]{1,0:T(8,128)(2,1)S(1)}, u32[]{:S(2)}, u32[]{:S(2)}) %collective-permute-start.1) | collective-permute-done | bytes 135200 | tf_op jit(solution)/shard_map/ppermute | solution.py:20
  14.3 1.9 %copy-done.1 = bf16[1,4096,384]{2,1,0:T(8,128)(2,1)S(1)} copy-done((bf16[1,4096,384]{2,1,0:T(8,128)(2,1)S(1)}, bf16[1,4096,384]{2,1,0:T(8,128)(2,1)}, u32[]{:S(2)}) %copy-start.1) | copy-done | bytes 3145752
  16.2 1.9 %copy-done.2 = bf16[1,4096,384]{2,1,0:T(8,128)(2,1)S(1)} copy-done((bf16[1,4096,384]{2,1,0:T(8,128)(2,1)S(1)}, bf16[1,4096,384]{2,1,0:T(8,128)(2,1)}, u32[]{:S(2)}) %copy-start.2) | copy-done | bytes 3145752
  18.1 1.9 %dequantize_in.1.refs_4_ = bf16[4096,768]{1,0:T(8,128)(2,1)S(1)} custom-call(f32[3,32]{1,0:T(4,128)S(1)} %get-tuple-element.212.gate_scales, f32[3,32]{1,0:T(4,128)S(1)} %get-tuple-element.211.up_scales, bf16[4096,384]{1,0:T(8,128)(2,1)S(1)} %bitcast.16, bf16[4096,384]{1,0:T(8,128)(2,1)S(1)} %bitcast.17), custom_call_target="tpu_custom_call" | custom-call | flops 3145728 | bytes 12582912 | tf_op jit(solution)/shard_map/dequantize_in/pallas_call | solution.py:120
  20.1 1.6 %collective-permute-start.4 = (bf16[32,4224]{1,0:T(8,128)(2,1)S(1)}, bf16[32,4224]{1,0:T(8,128)(2,1)S(1)}, u32[]{:S(2)}, u32[]{:S(2)}) collective-permute-start(bf16[32,4224]{1,0:T(8,128)(2,1)S(1)} %pad_maximum_fusion.2.refs_0_), channel_id=1, source_target_pairs={{0,16},{16,0},{8,24},{24,8},{1,17},{17,1},{9,25},{25,9},{2,18},{18... | collective-permute-start | bytes 811016 | tf_op jit(solution)/shard_map/ppermute | solution.py:20
  23.1 2.4 %collective-permute-start.6 = (bf16[16,4224]{1,0:T(8,128)(2,1)S(1)}, bf16[16,4224]{1,0:T(8,128)(2,1)S(1)}, u32[]{:S(2)}, u32[]{:S(2)}) collective-permute-start(bf16[16,4224]{1,0:T(8,128)(2,1)S(1)} %concatenate.39), channel_id=1, source_target_pairs={{0,2},{1,3},{2,0},{3,1},{4,6},{5,7},{6,4},{7,5},{8,10},{9,11},{10,... | collective-permute-start | bytes 405512 | tf_op jit(solution)/shard_map/ppermute | solution.py:223
  25.6 1.9 %dequantize_down.1.refs_6_ = bf16[384,4096]{1,0:T(8,128)(2,1)S(1)} custom-call(f32[3,32]{1,0:T(4,128)S(1)} %bitcast.18, bf16[384,4096]{1,0:T(8,128)(2,1)S(1)} %bitcast.15), custom_call_target="tpu_custom_call" | custom-call | flops 1572864 | bytes 6291456 | tf_op jit(solution)/shard_map/dequantize_down/pallas_call | solution.py:148
  27.4 3.9 %collective-permute-done.7 = bf16[16,4224]{1,0:T(8,128)(2,1)S(1)} collective-permute-done((bf16[16,4224]{1,0:T(8,128)(2,1)S(1)}, bf16[16,4224]{1,0:T(8,128)(2,1)S(1)}, u32[]{:S(2)}, u32[]{:S(2)}) %collective-permute-start.7) | collective-permute-done | bytes 135200 | tf_op jit(solution)/shard_map/ppermute | solution.py:223
  32.2 1.4 %collective-permute-start.8 = (bf16[32,4224]{1,0:T(8,128)(2,1)S(1)}, bf16[32,4224]{1,0:T(8,128)(2,1)S(1)}, u32[]{:S(2)}, u32[]{:S(2)}) collective-permute-start(bf16[32,4224]{1,0:T(8,128)(2,1)S(1)} %constant_dynamic-update-slice_fusion), channel_id=1, source_target_pairs={{0,8},{8,0},{16,24},{24,16},{1,9},{9,1},{17,25},{25,17},{2,10},{10... | collective-permute-start | bytes 811016 | tf_op jit(solution)/shard_map/ppermute | solution.py:20
  33.6 6.9 %collective-permute-done.9 = bf16[32,4224]{1,0:T(8,128)(2,1)S(1)} collective-permute-done((bf16[32,4224]{1,0:T(8,128)(2,1)S(1)}, bf16[32,4224]{1,0:T(8,128)(2,1)S(1)}, u32[]{:S(2)}, u32[]{:S(2)}) %collective-permute-start.9) | collective-permute-done | bytes 270368 | tf_op jit(solution)/shard_map/ppermute | solution.py:20
  41.0 1.6 %collective-permute-start.16 = (bf16[16,4224]{1,0:T(8,128)(2,1)S(1)}, bf16[16,4224]{1,0:T(8,128)(2,1)S(1)}, u32[]{:S(2)}, u32[]{:S(2)}) collective-permute-start(bf16[16,4224]{1,0:T(8,128)(2,1)S(1)} %get-tuple-element.195), channel_id=1, source_target_pairs={{0,16},{16,0},{8,24},{24,8},{1,17},{17,1},{9,25},{25,9},{2,18},{18... | collective-permute-start | bytes 405512 | tf_op jit(solution)/shard_map/ppermute | solution.py:20
  45.1 3.1 %expert_layer.3 = (bf16[32,4096]{1,0:T(8,128)(2,1)S(1)}, bf16[32,4096]{1,0:T(8,128)(2,1)S(1)}, bf16[32,4096]{1,0:T(8,128)(2,1)S(1)}, bf16[32,4096]{1,0:T(8,128)(2,1)S(1)}) custom-call(s32[1]{0:T(128)} %bitcast.own_expert, bf16[32,4224]{1,0:T(8,128)(2,1)S(1)} %pad_maximum_fusion.2.refs_0_, bf16[32,4224]{1,0:T(8,128)(2,1)S(1)} %collective-permute-done.4.refs_1_, ...), custom_call_target="tpu_custom_call" | custom-call | flops 2415919104 | bytes 20971520 | tf_op jit(solution)/shard_map/expert_layer/pallas_call | solution.py:202
  49.1 8.5 %collective-permute-done.13.refs_1_ = bf16[64,4224]{1,0:T(8,128)(2,1)S(1)} collective-permute-done((bf16[64,4224]{1,0:T(8,128)(2,1)S(1)}, bf16[64,4224]{1,0:T(8,128)(2,1)S(1)}, u32[]{:S(2)}, u32[]{:S(2)}) %collective-permute-start.13) | collective-permute-done | bytes 540704 | tf_op jit(solution)/shard_map/ppermute | solution.py:20
  60.8 5.7 %expert_layer.4 = (bf16[64,4096]{1,0:T(8,128)(2,1)S(1)}, bf16[64,4096]{1,0:T(8,128)(2,1)S(1)}, bf16[64,4096]{1,0:T(8,128)(2,1)S(1)}, bf16[64,4096]{1,0:T(8,128)(2,1)S(1)}) custom-call(s32[1]{0:T(128)} %bitcast.own_expert, bf16[64,4224]{1,0:T(8,128)(2,1)S(1)} %pad_maximum_fusion.refs_0_, bf16[64,4224]{1,0:T(8,128)(2,1)S(1)} %collective-permute-done.13.refs_1_, ...), custom_call_target="tpu_custom_call" | custom-call | flops 4831838208 | bytes 23068672 | tf_op jit(solution)/shard_map/expert_layer/pallas_call | solution.py:202
  66.5 3.2 %expert_layer.5 = (bf16[32,4096]{1,0:T(8,128)(2,1)S(1)}, bf16[32,4096]{1,0:T(8,128)(2,1)S(1)}, bf16[32,4096]{1,0:T(8,128)(2,1)S(1)}, bf16[32,4096]{1,0:T(8,128)(2,1)S(1)}) custom-call(s32[1]{0:T(128)} %bitcast.own_expert, bf16[32,4224]{1,0:T(8,128)(2,1)S(1)} %pad_maximum_fusion.4.refs_0_, bf16[32,4224]{1,0:T(8,128)(2,1)S(1)} %collective-permute-done.17.refs_1_, ...), custom_call_target="tpu_custom_call" | custom-call | flops 2415919104 | bytes 20971520 | tf_op jit(solution)/shard_map/expert_layer/pallas_call | solution.py:202
  69.7 1.4 %collective-permute-start.19 = (bf16[32,4096]{1,0:T(8,128)(2,1)S(1)}, bf16[32,4096]{1,0:T(8,128)(2,1)S(1)}, u32[]{:S(2)}, u32[]{:S(2)}) collective-permute-start(bf16[32,4096]{1,0:T(8,128)(2,1)S(1)} %get-tuple-element.151), channel_id=1, source_target_pairs={{0,16},{16,0},{8,24},{24,8},{1,17},{17,1},{9,25},{25,9},{2,18},{18... | collective-permute-start | bytes 786440 | tf_op jit(solution)/shard_map/ppermute | solution.py:20
  71.8 4.3 %collective-permute-done.19 = bf16[32,4096]{1,0:T(8,128)(2,1)S(1)} collective-permute-done((bf16[32,4096]{1,0:T(8,128)(2,1)S(1)}, bf16[32,4096]{1,0:T(8,128)(2,1)S(1)}, u32[]{:S(2)}, u32[]{:S(2)}) %collective-permute-start.19) | collective-permute-done | bytes 262176 | tf_op jit(solution)/shard_map/ppermute | solution.py:20
  81.8 2.3 %collective-permute-done.24 = bf16[16,4096]{1,0:T(8,128)(2,1)S(1)} collective-permute-done((bf16[16,4096]{1,0:T(8,128)(2,1)S(1)}, bf16[16,4096]{1,0:T(8,128)(2,1)S(1)}, u32[]{:S(2)}, u32[]{:S(2)}) %collective-permute-start.24) | collective-permute-done | bytes 131104 | tf_op jit(solution)/shard_map/ppermute | solution.py:20
  84.9 6.8 %collective-permute-done.21 = bf16[64,4096]{1,0:T(8,128)(2,1)S(1)} collective-permute-done((bf16[64,4096]{1,0:T(8,128)(2,1)S(1)}, bf16[64,4096]{1,0:T(8,128)(2,1)S(1)}, u32[]{:S(2)}, u32[]{:S(2)}) %collective-permute-start.21) | collective-permute-done | bytes 524320 | tf_op jit(solution)/shard_map/ppermute | solution.py:20
  94.2 1.9 %collective-permute-start.27 = (bf16[32,4096]{1,0:T(8,128)(2,1)S(1)}, bf16[32,4096]{1,0:T(8,128)(2,1)S(1)}, u32[]{:S(2)}, u32[]{:S(2)}) collective-permute-start(bf16[32,4096]{1,0:T(8,128)(2,1)S(1)} %pad_maximum_fusion.6), channel_id=1, source_target_pairs={{0,2},{1,3},{2,0},{3,1},{4,6},{5,7},{6,4},{7,5},{8,10},{9,11},{10,... | collective-permute-start | bytes 786440 | tf_op jit(solution)/shard_map/ppermute | solution.py:223
  96.1 3.3 %collective-permute-done.26 = bf16[32,4096]{1,0:T(8,128)(2,1)S(1)} collective-permute-done((bf16[32,4096]{1,0:T(8,128)(2,1)S(1)}, bf16[32,4096]{1,0:T(8,128)(2,1)S(1)}, u32[]{:S(2)}, u32[]{:S(2)}) %collective-permute-start.26) | collective-permute-done | bytes 262176 | tf_op jit(solution)/shard_map/ppermute | solution.py:20
  100.4 3.1 %collective-permute-done.27 = bf16[32,4096]{1,0:T(8,128)(2,1)S(1)} collective-permute-done((bf16[32,4096]{1,0:T(8,128)(2,1)S(1)}, bf16[32,4096]{1,0:T(8,128)(2,1)S(1)}, u32[]{:S(2)}, u32[]{:S(2)}) %collective-permute-start.27) | collective-permute-done | bytes 262176 | tf_op jit(solution)/shard_map/ppermute | solution.py:223
  103.5 1.5 %collective-permute-start.31 = (bf16[16,4096]{1,0:T(8,128)(2,1)S(1)}, bf16[16,4096]{1,0:T(8,128)(2,1)S(1)}, u32[]{:S(2)}, u32[]{:S(2)}) collective-permute-start(bf16[16,4096]{1,0:T(8,128)(2,1)S(1)} %get-tuple-element.200), channel_id=1, source_target_pairs={{0,4},{1,5},{2,6},{3,7},{4,0},{5,1},{6,2},{7,3},{8,12},{9,13},{10,... | collective-permute-start | bytes 393224 | tf_op jit(solution)/shard_map/ppermute | solution.py:223
  108.4 3.0 %collective-permute-done.28 = bf16[32,4096]{1,0:T(8,128)(2,1)S(1)} collective-permute-done((bf16[32,4096]{1,0:T(8,128)(2,1)S(1)}, bf16[32,4096]{1,0:T(8,128)(2,1)S(1)}, u32[]{:S(2)}, u32[]{:S(2)}) %collective-permute-start.28) | collective-permute-done | bytes 262176 | tf_op jit(solution)/shard_map/ppermute | solution.py:20
  111.5 2.0 %collective-permute-done.29 = bf16[32,4096]{1,0:T(8,128)(2,1)S(1)} collective-permute-done((bf16[32,4096]{1,0:T(8,128)(2,1)S(1)}, bf16[32,4096]{1,0:T(8,128)(2,1)S(1)}, u32[]{:S(2)}, u32[]{:S(2)}) %collective-permute-start.29) | collective-permute-done | bytes 262176 | tf_op jit(solution)/shard_map/ppermute | solution.py:20
  113.6 1.4 %collective-permute-start.33 = (bf16[16,4096]{1,0:T(8,128)(2,1)S(1)}, bf16[16,4096]{1,0:T(8,128)(2,1)S(1)}, u32[]{:S(2)}, u32[]{:S(2)}) collective-permute-start(bf16[16,4096]{1,0:T(8,128)(2,1)S(1)} %split.47), channel_id=1, source_target_pairs={{0,16},{16,0},{8,24},{24,8},{1,17},{17,1},{9,25},{25,9},{2,18},{18... | collective-permute-start | bytes 393224 | tf_op jit(solution)/shard_map/ppermute | solution.py:20
  117.1 1.4 %collective-permute-start.35 = (bf16[16,4096]{1,0:T(8,128)(2,1)S(1)}, bf16[16,4096]{1,0:T(8,128)(2,1)S(1)}, u32[]{:S(2)}, u32[]{:S(2)}) collective-permute-start(bf16[16,4096]{1,0:T(8,128)(2,1)S(1)} %get-tuple-element.192), channel_id=1, source_target_pairs={{0,4},{1,5},{2,6},{3,7},{4,0},{5,1},{6,2},{7,3},{8,12},{9,13},{10,... | collective-permute-start | bytes 393224 | tf_op jit(solution)/shard_map/ppermute | solution.py:223
  120.6 3.7 %collective-permute-done.35 = bf16[16,4096]{1,0:T(8,128)(2,1)S(1)} collective-permute-done((bf16[16,4096]{1,0:T(8,128)(2,1)S(1)}, bf16[16,4096]{1,0:T(8,128)(2,1)S(1)}, u32[]{:S(2)}, u32[]{:S(2)}) %collective-permute-start.35) | collective-permute-done | bytes 131104 | tf_op jit(solution)/shard_map/ppermute | solution.py:223
  (102 shorter events, 30.5 us)
Async XLA Ops:
  2.1 12.2 %collective-permute-start.3 = (bf16[16,4224]{1,0:T(8,128)(2,1)S(1)}, bf16[16,4224]{1,0:T(8,128)(2,1)S(1)}, u32[]{:S(2)}, u32[]{:S(2)}) collective-permute-start(bf16[16,4224]{1,0:T(8,128)(2,1)S(1)} %concatenate.38), channel_id=1, source_target_pairs={{0,4},{1,5},{2,6},{3,7},{4,0},{5,1},{6,2},{7,3},{8,12},{9,13},{10,... | collective-permute-start | bytes 405512 | tf_op jit(solution)/shard_map/ppermute | solution.py:223
  6.1 8.2 %collective-permute-start.2 = (bf16[16,4224]{1,0:T(8,128)(2,1)S(1)}, bf16[16,4224]{1,0:T(8,128)(2,1)S(1)}, u32[]{:S(2)}, u32[]{:S(2)}) collective-permute-start(bf16[16,4224]{1,0:T(8,128)(2,1)S(1)} %concatenate.38), channel_id=1, source_target_pairs={{0,2},{1,3},{2,0},{3,1},{4,6},{5,7},{6,4},{7,5},{8,10},{9,11},{10,... | collective-permute-start | bytes 405512 | tf_op jit(solution)/shard_map/ppermute | solution.py:223
  7.7 6.5 %collective-permute-start = (bf16[16,4224]{1,0:T(8,128)(2,1)S(1)}, bf16[16,4224]{1,0:T(8,128)(2,1)S(1)}, u32[]{:S(2)}, u32[]{:S(2)}) collective-permute-start(bf16[16,4224]{1,0:T(8,128)(2,1)S(1)} %concatenate.38), channel_id=1, source_target_pairs={{0,8},{8,0},{16,24},{24,16},{1,9},{9,1},{17,25},{25,17},{2,10},{10... | collective-permute-start | bytes 405512 | tf_op jit(solution)/shard_map/ppermute | solution.py:20
  20.0 20.9 %collective-permute-start.11 = (bf16[4096,768]{1,0:T(8,128)(2,1)S(1)}, bf16[4096,768]{1,0:T(8,128)(2,1)S(1)}, u32[]{:S(2)}, u32[]{:S(2)}) collective-permute-start(bf16[4096,768]{1,0:T(8,128)(2,1)S(1)} %dequantize_in.1.refs_4_), channel_id=1, source_target_pairs={{0,1},{1,0},{2,3},{3,2},{4,5},{5,4},{6,7},{7,6},{8,9},{9,8},{10,11... | collective-permute-start | bytes 18874376 | tf_op jit(solution)/shard_map/ppermute | solution.py:20
  20.1 11.3 %collective-permute-start.4 = (bf16[32,4224]{1,0:T(8,128)(2,1)S(1)}, bf16[32,4224]{1,0:T(8,128)(2,1)S(1)}, u32[]{:S(2)}, u32[]{:S(2)}) collective-permute-start(bf16[32,4224]{1,0:T(8,128)(2,1)S(1)} %pad_maximum_fusion.2.refs_0_), channel_id=1, source_target_pairs={{0,16},{16,0},{8,24},{24,8},{1,17},{17,1},{9,25},{25,9},{2,18},{18... | collective-permute-start | bytes 811016 | tf_op jit(solution)/shard_map/ppermute | solution.py:20
  21.7 9.7 %collective-permute-start.5 = (bf16[32,4224]{1,0:T(8,128)(2,1)S(1)}, bf16[32,4224]{1,0:T(8,128)(2,1)S(1)}, u32[]{:S(2)}, u32[]{:S(2)}) collective-permute-start(bf16[32,4224]{1,0:T(8,128)(2,1)S(1)} %pad_maximum_fusion.3.refs_2_), channel_id=1, source_target_pairs={{0,8},{8,0},{16,24},{24,16},{1,9},{9,1},{17,25},{25,17},{2,10},{10... | collective-permute-start | bytes 811016 | tf_op jit(solution)/shard_map/ppermute | solution.py:20
  22.2 9.2 %collective-permute-start.7 = (bf16[16,4224]{1,0:T(8,128)(2,1)S(1)}, bf16[16,4224]{1,0:T(8,128)(2,1)S(1)}, u32[]{:S(2)}, u32[]{:S(2)}) collective-permute-start(bf16[16,4224]{1,0:T(8,128)(2,1)S(1)} %concatenate.39), channel_id=1, source_target_pairs={{0,4},{1,5},{2,6},{3,7},{4,0},{5,1},{6,2},{7,3},{8,12},{9,13},{10,... | collective-permute-start | bytes 405512 | tf_op jit(solution)/shard_map/ppermute | solution.py:223
  23.1 8.2 %collective-permute-start.6 = (bf16[16,4224]{1,0:T(8,128)(2,1)S(1)}, bf16[16,4224]{1,0:T(8,128)(2,1)S(1)}, u32[]{:S(2)}, u32[]{:S(2)}) collective-permute-start(bf16[16,4224]{1,0:T(8,128)(2,1)S(1)} %concatenate.39), channel_id=1, source_target_pairs={{0,2},{1,3},{2,0},{3,1},{4,6},{5,7},{6,4},{7,5},{8,10},{9,11},{10,... | collective-permute-start | bytes 405512 | tf_op jit(solution)/shard_map/ppermute | solution.py:223
  31.4 9.5 %collective-permute-start.12 = (bf16[384,4096]{1,0:T(8,128)(2,1)S(1)}, bf16[384,4096]{1,0:T(8,128)(2,1)S(1)}, u32[]{:S(2)}, u32[]{:S(2)}) collective-permute-start(bf16[384,4096]{1,0:T(8,128)(2,1)S(1)} %dequantize_down.1.refs_6_), channel_id=1, source_target_pairs={{0,1},{1,0},{2,3},{3,2},{4,5},{5,4},{6,7},{7,6},{8,9},{9,8},{10,11... | collective-permute-start | bytes 9437192 | tf_op jit(solution)/shard_map/ppermute | solution.py:20
  31.5 9.4 %collective-permute-start.10 = (bf16[32,4224]{1,0:T(8,128)(2,1)S(1)}, bf16[32,4224]{1,0:T(8,128)(2,1)S(1)}, u32[]{:S(2)}, u32[]{:S(2)}) collective-permute-start(bf16[32,4224]{1,0:T(8,128)(2,1)S(1)} %constant_dynamic-update-slice_fusion.2), channel_id=1, source_target_pairs={{0,2},{1,3},{2,0},{3,1},{4,6},{5,7},{6,4},{7,5},{8,10},{9,11},{10,... | collective-permute-start | bytes 811016 | tf_op jit(solution)/shard_map/ppermute | solution.py:223
  31.6 8.9 %collective-permute-start.9 = (bf16[32,4224]{1,0:T(8,128)(2,1)S(1)}, bf16[32,4224]{1,0:T(8,128)(2,1)S(1)}, u32[]{:S(2)}, u32[]{:S(2)}) collective-permute-start(bf16[32,4224]{1,0:T(8,128)(2,1)S(1)} %constant_dynamic-update-slice_fusion.2), channel_id=1, source_target_pairs={{0,16},{16,0},{8,24},{24,8},{1,17},{17,1},{9,25},{25,9},{2,18},{18... | collective-permute-start | bytes 811016 | tf_op jit(solution)/shard_map/ppermute | solution.py:20
  32.2 8.7 %collective-permute-start.8 = (bf16[32,4224]{1,0:T(8,128)(2,1)S(1)}, bf16[32,4224]{1,0:T(8,128)(2,1)S(1)}, u32[]{:S(2)}, u32[]{:S(2)}) collective-permute-start(bf16[32,4224]{1,0:T(8,128)(2,1)S(1)} %constant_dynamic-update-slice_fusion), channel_id=1, source_target_pairs={{0,8},{8,0},{16,24},{24,16},{1,9},{9,1},{17,25},{25,17},{2,10},{10... | collective-permute-start | bytes 811016 | tf_op jit(solution)/shard_map/ppermute | solution.py:20
  41.0 7.3 %collective-permute-start.16 = (bf16[16,4224]{1,0:T(8,128)(2,1)S(1)}, bf16[16,4224]{1,0:T(8,128)(2,1)S(1)}, u32[]{:S(2)}, u32[]{:S(2)}) collective-permute-start(bf16[16,4224]{1,0:T(8,128)(2,1)S(1)} %get-tuple-element.195), channel_id=1, source_target_pairs={{0,16},{16,0},{8,24},{24,8},{1,17},{17,1},{9,25},{25,9},{2,18},{18... | collective-permute-start | bytes 405512 | tf_op jit(solution)/shard_map/ppermute | solution.py:20
  42.5 6.5 %collective-permute-start.15 = (bf16[16,4224]{1,0:T(8,128)(2,1)S(1)}, bf16[16,4224]{1,0:T(8,128)(2,1)S(1)}, u32[]{:S(2)}, u32[]{:S(2)}) collective-permute-start(bf16[16,4224]{1,0:T(8,128)(2,1)S(1)} %get-tuple-element.196), channel_id=1, source_target_pairs={{0,8},{8,0},{16,24},{24,16},{1,9},{9,1},{17,25},{25,17},{2,10},{10... | collective-permute-start | bytes 405512 | tf_op jit(solution)/shard_map/ppermute | solution.py:20
  43.9 13.7 %collective-permute-start.13 = (bf16[64,4224]{1,0:T(8,128)(2,1)S(1)}, bf16[64,4224]{1,0:T(8,128)(2,1)S(1)}, u32[]{:S(2)}, u32[]{:S(2)}) collective-permute-start(bf16[64,4224]{1,0:T(8,128)(2,1)S(1)} %pad_maximum_fusion.refs_0_), channel_id=1, source_target_pairs={{0,16},{16,0},{8,24},{24,8},{1,17},{17,1},{9,25},{25,9},{2,18},{18... | collective-permute-start | bytes 1622024 | tf_op jit(solution)/shard_map/ppermute | solution.py:20
  44.4 14.3 %collective-permute-start.14 = (bf16[64,4224]{1,0:T(8,128)(2,1)S(1)}, bf16[64,4224]{1,0:T(8,128)(2,1)S(1)}, u32[]{:S(2)}, u32[]{:S(2)}) collective-permute-start(bf16[64,4224]{1,0:T(8,128)(2,1)S(1)} %pad_maximum_fusion.1.refs_2_), channel_id=1, source_target_pairs={{0,8},{8,0},{16,24},{24,16},{1,9},{9,1},{17,25},{25,17},{2,10},{10... | collective-permute-start | bytes 1622024 | tf_op jit(solution)/shard_map/ppermute | solution.py:20
  58.7 7.8 %collective-permute-start.17 = (bf16[32,4224]{1,0:T(8,128)(2,1)S(1)}, bf16[32,4224]{1,0:T(8,128)(2,1)S(1)}, u32[]{:S(2)}, u32[]{:S(2)}) collective-permute-start(bf16[32,4224]{1,0:T(8,128)(2,1)S(1)} %pad_maximum_fusion.4.refs_0_), channel_id=1, source_target_pairs={{0,16},{16,0},{8,24},{24,8},{1,17},{17,1},{9,25},{25,9},{2,18},{18... | collective-permute-start | bytes 811016 | tf_op jit(solution)/shard_map/ppermute | solution.py:20
  59.6 6.9 %collective-permute-start.18 = (bf16[32,4224]{1,0:T(8,128)(2,1)S(1)}, bf16[32,4224]{1,0:T(8,128)(2,1)S(1)}, u32[]{:S(2)}, u32[]{:S(2)}) collective-permute-start(bf16[32,4224]{1,0:T(8,128)(2,1)S(1)} %pad_maximum_fusion.5.refs_2_), channel_id=1, source_target_pairs={{0,8},{8,0},{16,24},{24,16},{1,9},{9,1},{17,25},{25,17},{2,10},{10... | collective-permute-start | bytes 811016 | tf_op jit(solution)/shard_map/ppermute | solution.py:20
  69.7 6.4 %collective-permute-start.19 = (bf16[32,4096]{1,0:T(8,128)(2,1)S(1)}, bf16[32,4096]{1,0:T(8,128)(2,1)S(1)}, u32[]{:S(2)}, u32[]{:S(2)}) collective-permute-start(bf16[32,4096]{1,0:T(8,128)(2,1)S(1)} %get-tuple-element.151), channel_id=1, source_target_pairs={{0,16},{16,0},{8,24},{24,8},{1,17},{17,1},{9,25},{25,9},{2,18},{18... | collective-permute-start | bytes 786440 | tf_op jit(solution)/shard_map/ppermute | solution.py:20
  71.1 6.4 %collective-permute-start.20 = (bf16[32,4096]{1,0:T(8,128)(2,1)S(1)}, bf16[32,4096]{1,0:T(8,128)(2,1)S(1)}, u32[]{:S(2)}, u32[]{:S(2)}) collective-permute-start(bf16[32,4096]{1,0:T(8,128)(2,1)S(1)} %get-tuple-element.153), channel_id=1, source_target_pairs={{0,8},{8,0},{16,24},{24,16},{1,9},{9,1},{17,25},{25,17},{2,10},{10... | collective-permute-start | bytes 786440 | tf_op jit(solution)/shard_map/ppermute | solution.py:20
  77.6 6.5 %collective-permute-start.24 = (bf16[16,4096]{1,0:T(8,128)(2,1)S(1)}, bf16[16,4096]{1,0:T(8,128)(2,1)S(1)}, u32[]{:S(2)}, u32[]{:S(2)}) collective-permute-start(bf16[16,4096]{1,0:T(8,128)(2,1)S(1)} %split.39), channel_id=1, source_target_pairs={{0,16},{16,0},{8,24},{24,8},{1,17},{17,1},{9,25},{25,9},{2,18},{18... | collective-permute-start | bytes 393224 | tf_op jit(solution)/shard_map/ppermute | solution.py:20
  78.3 6.5 %collective-permute-start.23 = (bf16[16,4096]{1,0:T(8,128)(2,1)S(1)}, bf16[16,4096]{1,0:T(8,128)(2,1)S(1)}, u32[]{:S(2)}, u32[]{:S(2)}) collective-permute-start(bf16[16,4096]{1,0:T(8,128)(2,1)S(1)} %split.37), channel_id=1, source_target_pairs={{0,8},{8,0},{16,24},{24,16},{1,9},{9,1},{17,25},{25,17},{2,10},{10... | collective-permute-start | bytes 393224 | tf_op jit(solution)/shard_map/ppermute | solution.py:20
  79.3 12.4 %collective-permute-start.21 = (bf16[64,4096]{1,0:T(8,128)(2,1)S(1)}, bf16[64,4096]{1,0:T(8,128)(2,1)S(1)}, u32[]{:S(2)}, u32[]{:S(2)}) collective-permute-start(bf16[64,4096]{1,0:T(8,128)(2,1)S(1)} %get-tuple-element.163), channel_id=1, source_target_pairs={{0,16},{16,0},{8,24},{24,8},{1,17},{17,1},{9,25},{25,9},{2,18},{18... | collective-permute-start | bytes 1572872 | tf_op jit(solution)/shard_map/ppermute | solution.py:20
  80.4 12.2 %collective-permute-start.22 = (bf16[64,4096]{1,0:T(8,128)(2,1)S(1)}, bf16[64,4096]{1,0:T(8,128)(2,1)S(1)}, u32[]{:S(2)}, u32[]{:S(2)}) collective-permute-start(bf16[64,4096]{1,0:T(8,128)(2,1)S(1)} %get-tuple-element.165), channel_id=1, source_target_pairs={{0,8},{8,0},{16,24},{24,16},{1,9},{9,1},{17,25},{25,17},{2,10},{10... | collective-permute-start | bytes 1572872 | tf_op jit(solution)/shard_map/ppermute | solution.py:20
  92.8 6.6 %collective-permute-start.26 = (bf16[32,4096]{1,0:T(8,128)(2,1)S(1)}, bf16[32,4096]{1,0:T(8,128)(2,1)S(1)}, u32[]{:S(2)}, u32[]{:S(2)}) collective-permute-start(bf16[32,4096]{1,0:T(8,128)(2,1)S(1)} %split.43), channel_id=1, source_target_pairs={{0,16},{16,0},{8,24},{24,8},{1,17},{17,1},{9,25},{25,9},{2,18},{18... | collective-permute-start | bytes 786440 | tf_op jit(solution)/shard_map/ppermute | solution.py:20
  93.7 6.6 %collective-permute-start.25 = (bf16[32,4096]{1,0:T(8,128)(2,1)S(1)}, bf16[32,4096]{1,0:T(8,128)(2,1)S(1)}, u32[]{:S(2)}, u32[]{:S(2)}) collective-permute-start(bf16[32,4096]{1,0:T(8,128)(2,1)S(1)} %split.41), channel_id=1, source_target_pairs={{0,8},{8,0},{16,24},{24,16},{1,9},{9,1},{17,25},{25,17},{2,10},{10... | collective-permute-start | bytes 786440 | tf_op jit(solution)/shard_map/ppermute | solution.py:20
  94.2 9.2 %collective-permute-start.27 = (bf16[32,4096]{1,0:T(8,128)(2,1)S(1)}, bf16[32,4096]{1,0:T(8,128)(2,1)S(1)}, u32[]{:S(2)}, u32[]{:S(2)}) collective-permute-start(bf16[32,4096]{1,0:T(8,128)(2,1)S(1)} %pad_maximum_fusion.6), channel_id=1, source_target_pairs={{0,2},{1,3},{2,0},{3,1},{4,6},{5,7},{6,4},{7,5},{8,10},{9,11},{10,... | collective-permute-start | bytes 786440 | tf_op jit(solution)/shard_map/ppermute | solution.py:223
  103.5 10.1 %collective-permute-start.31 = (bf16[16,4096]{1,0:T(8,128)(2,1)S(1)}, bf16[16,4096]{1,0:T(8,128)(2,1)S(1)}, u32[]{:S(2)}, u32[]{:S(2)}) collective-permute-start(bf16[16,4096]{1,0:T(8,128)(2,1)S(1)} %get-tuple-element.200), channel_id=1, source_target_pairs={{0,4},{1,5},{2,6},{3,7},{4,0},{5,1},{6,2},{7,3},{8,12},{9,13},{10,... | collective-permute-start | bytes 393224 | tf_op jit(solution)/shard_map/ppermute | solution.py:223
  105.1 6.4 %collective-permute-start.28 = (bf16[32,4096]{1,0:T(8,128)(2,1)S(1)}, bf16[32,4096]{1,0:T(8,128)(2,1)S(1)}, u32[]{:S(2)}, u32[]{:S(2)}) collective-permute-start(bf16[32,4096]{1,0:T(8,128)(2,1)S(1)} %get-tuple-element.181), channel_id=1, source_target_pairs={{0,16},{16,0},{8,24},{24,8},{1,17},{17,1},{9,25},{25,9},{2,18},{18... | collective-permute-start | bytes 786440 | tf_op jit(solution)/shard_map/ppermute | solution.py:20
  106.4 7.2 %collective-permute-start.30 = (bf16[16,4096]{1,0:T(8,128)(2,1)S(1)}, bf16[16,4096]{1,0:T(8,128)(2,1)S(1)}, u32[]{:S(2)}, u32[]{:S(2)}) collective-permute-start(bf16[16,4096]{1,0:T(8,128)(2,1)S(1)} %get-tuple-element.202), channel_id=1, source_target_pairs={{0,2},{1,3},{2,0},{3,1},{4,6},{5,7},{6,4},{7,5},{8,10},{9,11},{10,... | collective-permute-start | bytes 393224 | tf_op jit(solution)/shard_map/ppermute | solution.py:223
  107.1 6.4 %collective-permute-start.29 = (bf16[32,4096]{1,0:T(8,128)(2,1)S(1)}, bf16[32,4096]{1,0:T(8,128)(2,1)S(1)}, u32[]{:S(2)}, u32[]{:S(2)}) collective-permute-start(bf16[32,4096]{1,0:T(8,128)(2,1)S(1)} %get-tuple-element.183), channel_id=1, source_target_pairs={{0,8},{8,0},{16,24},{24,16},{1,9},{9,1},{17,25},{25,17},{2,10},{10... | collective-permute-start | bytes 786440 | tf_op jit(solution)/shard_map/ppermute | solution.py:20
  117.1 7.3 %collective-permute-start.35 = (bf16[16,4096]{1,0:T(8,128)(2,1)S(1)}, bf16[16,4096]{1,0:T(8,128)(2,1)S(1)}, u32[]{:S(2)}, u32[]{:S(2)}) collective-permute-start(bf16[16,4096]{1,0:T(8,128)(2,1)S(1)} %get-tuple-element.192), channel_id=1, source_target_pairs={{0,4},{1,5},{2,6},{3,7},{4,0},{5,1},{6,2},{7,3},{8,12},{9,13},{10,... | collective-permute-start | bytes 393224 | tf_op jit(solution)/shard_map/ppermute | solution.py:223
  (11 other events, 78.1 us)

commit v10 on v9

--- a/solution.py
+++ b/solution.py
@@ -274,12 +274,10 @@
     lanes, outs = {0: payload}, {}
     near = [{far: across_chips(payload[0], far) for far in groups[1]}]
     gather_turn(0, 0)
-    lanes, near, payload, gate_own, up_own, down_own = together(
-        (lanes, near, payload, gate_q[0], up_q[0], down_q[0])
-    )
-    in_own = dequantize_in(gate_own, up_own, gate_scale[0], up_scale[0])
+    in_own = dequantize_in(gate_q[0], up_q[0], gate_scale[0], up_scale[0])
+    down_own = dequantize_down(down_q[0], down_scale[0])
+    lanes, near, payload, in_own, down_own = together((lanes, near, payload, in_own, down_own))
     in_other = from_partner(in_own, "expert", 0)
-    down_own = dequantize_down(down_own, down_scale[0])
     near.append({far: across_chips(payload[1], far) for far in groups[1]})
     for turn in range(1, turns):
         gather_turn(0, turn)
@@ -343,8 +341,10 @@
             sum_turn(number, turn)
             if turn == 0 and number > 1:
                 sum_turn(number - 1, turns - 1)
+            if turn == 0 and number > 1:
+                leave(number)
             sums, outs, merged = together((sums, outs, merged))
-        leave(number)
+    leave(1)
     back = [{far: across_chips(leaving[far][0], far) for far in groups[1]}]
     for turn in range(turns - 1, 0, -1):
         sum_turn(0, turn)

time: 125 us -> 118 us (0.944)
  waiting for transfers between devices: 59.5 us -> 55.4 us
  starting transfers between devices: 41.7 us -> 39.8 us
    ppermute x26, waiting for transfers between devices: 48.2 us -> 44.7 us  [from_partner(): return lax.ppermute(block, axis, route)]
    ppermute x10, starting transfers between devices: 16 us -> 12.6 us  [across_chips(): lax.ppermute(block, 'expert', [(low, low ^ 2 * far) for low in range(coun...]
    ppermute x26, starting transfers between devices: 25.7 us -> 27.2 us  [from_partner(): return lax.ppermute(block, axis, route)]
  transfers between devices with their start and end apart: 36 -> 36, of which waited for: 22 -> 19; matrix products, arithmetic and copies ran while one was open for 1% -> 1% of each run, Pallas kernels for 9% -> 11%
where the time goes in v10:
time: 118 us
  waiting for transfers between devices  55.4 us (47%)
  starting transfers between devices  39.8 us (34%)
  Pallas kernels  15.8 us (13%)
  local copies, waits for them, and re-layouts  4.33 us (4%)
  other arithmetic  2.58 us (2%)
    ppermute x26, waiting for transfers between devices, from_partner(): return lax.ppermute(block, axis, route)  44.7 us
    ppermute x26, starting transfers between devices, from_partner(): return lax.ppermute(block, axis, route)  27.2 us
    ppermute x10, starting transfers between devices, across_chips(): lax.ppermute(block, 'expert', [(low, low ^ 2 * far) for low in range(coun...  12.6 us
    pallas_call x3, Pallas kernels, expert_layer(): pl.pallas_call(functools.partial(expert_kernel, count, experts), in_specs...  12 us
    ppermute x10, waiting for transfers between devices, across_chips(): lax.ppermute(block, 'expert', [(low, low ^ 2 * far) for low in range(coun...  10.7 us
    unnamed x17, local copies, waits for them, and re-layouts  2.9 us
  transfers between devices with their start and end apart: 36, of which 19 were waited for; matrix products, arithmetic and copies ran while one was open for 1% of the time, Pallas kernels for 11%

profile of v10, /device:TPU:0, one launch (start us, length us, event | category | flops | bytes accessed | tf_op | source)
XLA Modules:
  0.0 118.3 jit_solution(10440322668476959018)
XLA Ops:
  2.0 4.0 %collective-permute-start.3 = (bf16[16,4224]{1,0:T(8,128)(2,1)S(1)}, bf16[16,4224]{1,0:T(8,128)(2,1)S(1)}, u32[]{:S(2)}, u32[]{:S(2)}) collective-permute-start(bf16[16,4224]{1,0:T(8,128)(2,1)S(1)} %concatenate.38), channel_id=1, source_target_pairs={{0,4},{1,5},{2,6},{3,7},{4,0},{5,1},{6,2},{7,3},{8,12},{9,13},{10,... | collective-permute-start | bytes 405512 | tf_op jit(solution)/shard_map/ppermute | solution.py:223
  6.1 1.6 %collective-permute-start.2 = (bf16[16,4224]{1,0:T(8,128)(2,1)S(1)}, bf16[16,4224]{1,0:T(8,128)(2,1)S(1)}, u32[]{:S(2)}, u32[]{:S(2)}) collective-permute-start(bf16[16,4224]{1,0:T(8,128)(2,1)S(1)} %concatenate.38), channel_id=1, source_target_pairs={{0,2},{1,3},{2,0},{3,1},{4,6},{5,7},{6,4},{7,5},{8,10},{9,11},{10,... | collective-permute-start | bytes 405512 | tf_op jit(solution)/shard_map/ppermute | solution.py:223
  7.7 1.5 %collective-permute-start = (bf16[16,4224]{1,0:T(8,128)(2,1)S(1)}, bf16[16,4224]{1,0:T(8,128)(2,1)S(1)}, u32[]{:S(2)}, u32[]{:S(2)}) collective-permute-start(bf16[16,4224]{1,0:T(8,128)(2,1)S(1)} %concatenate.38), channel_id=1, source_target_pairs={{0,8},{8,0},{16,24},{24,16},{1,9},{9,1},{17,25},{25,17},{2,10},{10... | collective-permute-start | bytes 405512 | tf_op jit(solution)/shard_map/ppermute | solution.py:20
  9.2 1.5 %collective-permute-start.1 = (bf16[16,4224]{1,0:T(8,128)(2,1)S(1)}, bf16[16,4224]{1,0:T(8,128)(2,1)S(1)}, u32[]{:S(2)}, u32[]{:S(2)}) collective-permute-start(bf16[16,4224]{1,0:T(8,128)(2,1)S(1)} %concatenate.39), channel_id=1, source_target_pairs={{0,16},{16,0},{8,24},{24,8},{1,17},{17,1},{9,25},{25,9},{2,18},{18... | collective-permute-start | bytes 405512 | tf_op jit(solution)/shard_map/ppermute | solution.py:20
  10.7 1.9 %copy-done = bf16[1,384,4096]{2,1,0:T(8,128)(2,1)S(1)} copy-done((bf16[1,384,4096]{2,1,0:T(8,128)(2,1)S(1)}, bf16[1,384,4096]{2,1,0:T(8,128)(2,1)}, u32[]{:S(2)}) %copy-start) | copy-done | bytes 3145752
  12.6 1.8 %dequantize_down.1.refs_6_ = bf16[384,4096]{1,0:T(8,128)(2,1)S(1)} custom-call(f32[3,32]{1,0:T(4,128)S(1)} %bitcast.18, bf16[384,4096]{1,0:T(8,128)(2,1)S(1)} %bitcast.15), custom_call_target="tpu_custom_call" | custom-call | flops 1572864 | bytes 6291456 | tf_op jit(solution)/shard_map/dequantize_down/pallas_call | solution.py:148
  15.4 1.9 %dequantize_in.1.refs_4_ = bf16[4096,768]{1,0:T(8,128)(2,1)S(1)} custom-call(f32[3,32]{1,0:T(4,128)S(1)} %get-tuple-element.208.gate_scales, f32[3,32]{1,0:T(4,128)S(1)} %get-tuple-element.207.up_scales, bf16[4096,384]{1,0:T(8,128)(2,1)S(1)} %bitcast.16, bf16[4096,384]{1,0:T(8,128)(2,1)S(1)} %bitcast.17), custom_call_target="tpu_custom_call" | custom-call | flops 3145728 | bytes 12582912 | tf_op jit(solution)/shard_map/dequantize_in/pallas_call | solution.py:120
  19.7 8.0 %collective-permute-done.7 = bf16[16,4224]{1,0:T(8,128)(2,1)S(1)} collective-permute-done((bf16[16,4224]{1,0:T(8,128)(2,1)S(1)}, bf16[16,4224]{1,0:T(8,128)(2,1)S(1)}, u32[]{:S(2)}, u32[]{:S(2)}) %collective-permute-start.7) | collective-permute-done | bytes 135200 | tf_op jit(solution)/shard_map/ppermute | solution.py:223
  27.9 1.6 %collective-permute-start.9 = (bf16[32,4224]{1,0:T(8,128)(2,1)S(1)}, bf16[32,4224]{1,0:T(8,128)(2,1)S(1)}, u32[]{:S(2)}, u32[]{:S(2)}) collective-permute-start(bf16[32,4224]{1,0:T(8,128)(2,1)S(1)} %constant_dynamic-update-slice_fusion.2), channel_id=1, source_target_pairs={{0,16},{16,0},{8,24},{24,8},{1,17},{17,1},{9,25},{25,9},{2,18},{18... | collective-permute-start | bytes 811016 | tf_op jit(solution)/shard_map/ppermute | solution.py:20
  29.5 1.6 %collective-permute-start.8 = (bf16[32,4224]{1,0:T(8,128)(2,1)S(1)}, bf16[32,4224]{1,0:T(8,128)(2,1)S(1)}, u32[]{:S(2)}, u32[]{:S(2)}) collective-permute-start(bf16[32,4224]{1,0:T(8,128)(2,1)S(1)} %constant_dynamic-update-slice_fusion), channel_id=1, source_target_pairs={{0,8},{8,0},{16,24},{24,16},{1,9},{9,1},{17,25},{25,17},{2,10},{10... | collective-permute-start | bytes 811016 | tf_op jit(solution)/shard_map/ppermute | solution.py:20
  31.1 5.8 %collective-permute-done.9 = bf16[32,4224]{1,0:T(8,128)(2,1)S(1)} collective-permute-done((bf16[32,4224]{1,0:T(8,128)(2,1)S(1)}, bf16[32,4224]{1,0:T(8,128)(2,1)S(1)}, u32[]{:S(2)}, u32[]{:S(2)}) %collective-permute-start.9) | collective-permute-done | bytes 270368 | tf_op jit(solution)/shard_map/ppermute | solution.py:20
  38.9 1.5 %collective-permute-start.15 = (bf16[16,4224]{1,0:T(8,128)(2,1)S(1)}, bf16[16,4224]{1,0:T(8,128)(2,1)S(1)}, u32[]{:S(2)}, u32[]{:S(2)}) collective-permute-start(bf16[16,4224]{1,0:T(8,128)(2,1)S(1)} %get-tuple-element.192), channel_id=1, source_target_pairs={{0,8},{8,0},{16,24},{24,16},{1,9},{9,1},{17,25},{25,17},{2,10},{10... | collective-permute-start | bytes 405512 | tf_op jit(solution)/shard_map/ppermute | solution.py:20
  40.4 1.5 %collective-permute-start.13 = (bf16[64,4224]{1,0:T(8,128)(2,1)S(1)}, bf16[64,4224]{1,0:T(8,128)(2,1)S(1)}, u32[]{:S(2)}, u32[]{:S(2)}) collective-permute-start(bf16[64,4224]{1,0:T(8,128)(2,1)S(1)} %pad_maximum_fusion.refs_0_), channel_id=1, source_target_pairs={{0,16},{16,0},{8,24},{24,8},{1,17},{17,1},{9,25},{25,9},{2,18},{18... | collective-permute-start | bytes 1622024 | tf_op jit(solution)/shard_map/ppermute | solution.py:20
  42.4 3.1 %expert_layer.3 = (bf16[32,4096]{1,0:T(8,128)(2,1)S(1)}, bf16[32,4096]{1,0:T(8,128)(2,1)S(1)}, bf16[32,4096]{1,0:T(8,128)(2,1)S(1)}, bf16[32,4096]{1,0:T(8,128)(2,1)S(1)}) custom-call(s32[1]{0:T(128)} %bitcast.own_expert, bf16[32,4224]{1,0:T(8,128)(2,1)S(1)} %pad_maximum_fusion.2.refs_0_, bf16[32,4224]{1,0:T(8,128)(2,1)S(1)} %collective-permute-done.4.refs_1_, ...), custom_call_target="tpu_custom_call" | custom-call | flops 2415919104 | bytes 20971520 | tf_op jit(solution)/shard_map/expert_layer/pallas_call | solution.py:202
  45.6 9.3 %collective-permute-done.13.refs_1_ = bf16[64,4224]{1,0:T(8,128)(2,1)S(1)} collective-permute-done((bf16[64,4224]{1,0:T(8,128)(2,1)S(1)}, bf16[64,4224]{1,0:T(8,128)(2,1)S(1)}, u32[]{:S(2)}, u32[]{:S(2)}) %collective-permute-start.13) | collective-permute-done | bytes 540704 | tf_op jit(solution)/shard_map/ppermute | solution.py:20
  56.6 1.5 %collective-permute-start.18 = (bf16[32,4224]{1,0:T(8,128)(2,1)S(1)}, bf16[32,4224]{1,0:T(8,128)(2,1)S(1)}, u32[]{:S(2)}, u32[]{:S(2)}) collective-permute-start(bf16[32,4224]{1,0:T(8,128)(2,1)S(1)} %pad_maximum_fusion.5.refs_2_), channel_id=1, source_target_pairs={{0,8},{8,0},{16,24},{24,16},{1,9},{9,1},{17,25},{25,17},{2,10},{10... | collective-permute-start | bytes 811016 | tf_op jit(solution)/shard_map/ppermute | solution.py:20
  58.1 5.7 %expert_layer.4 = (bf16[64,4096]{1,0:T(8,128)(2,1)S(1)}, bf16[64,4096]{1,0:T(8,128)(2,1)S(1)}, bf16[64,4096]{1,0:T(8,128)(2,1)S(1)}, bf16[64,4096]{1,0:T(8,128)(2,1)S(1)}) custom-call(s32[1]{0:T(128)} %bitcast.own_expert, bf16[64,4224]{1,0:T(8,128)(2,1)S(1)} %pad_maximum_fusion.refs_0_, bf16[64,4224]{1,0:T(8,128)(2,1)S(1)} %collective-permute-done.13.refs_1_, ...), custom_call_target="tpu_custom_call" | custom-call | flops 4831838208 | bytes 23068672 | tf_op jit(solution)/shard_map/expert_layer/pallas_call | solution.py:202
  63.9 3.1 %expert_layer.5 = (bf16[32,4096]{1,0:T(8,128)(2,1)S(1)}, bf16[32,4096]{1,0:T(8,128)(2,1)S(1)}, bf16[32,4096]{1,0:T(8,128)(2,1)S(1)}, bf16[32,4096]{1,0:T(8,128)(2,1)S(1)}) custom-call(s32[1]{0:T(128)} %bitcast.own_expert, bf16[32,4224]{1,0:T(8,128)(2,1)S(1)} %pad_maximum_fusion.4.refs_0_, bf16[32,4224]{1,0:T(8,128)(2,1)S(1)} %collective-permute-done.17.refs_1_, ...), custom_call_target="tpu_custom_call" | custom-call | flops 2415919104 | bytes 20971520 | tf_op jit(solution)/shard_map/expert_layer/pallas_call | solution.py:202
  68.5 5.3 %collective-permute-done.19 = bf16[32,4096]{1,0:T(8,128)(2,1)S(1)} collective-permute-done((bf16[32,4096]{1,0:T(8,128)(2,1)S(1)}, bf16[32,4096]{1,0:T(8,128)(2,1)S(1)}, u32[]{:S(2)}, u32[]{:S(2)}) %collective-permute-start.19) | collective-permute-done | bytes 262176 | tf_op jit(solution)/shard_map/ppermute | solution.py:20
  74.1 2.1 %collective-permute-start.24 = (bf16[16,4096]{1,0:T(8,128)(2,1)S(1)}, bf16[16,4096]{1,0:T(8,128)(2,1)S(1)}, u32[]{:S(2)}, u32[]{:S(2)}) collective-permute-start(bf16[16,4096]{1,0:T(8,128)(2,1)S(1)} %split.39), channel_id=1, source_target_pairs={{0,16},{16,0},{8,24},{24,8},{1,17},{17,1},{9,25},{25,9},{2,18},{18... | collective-permute-start | bytes 393224 | tf_op jit(solution)/shard_map/ppermute | solution.py:20
  78.3 2.3 %collective-permute-done.24 = bf16[16,4096]{1,0:T(8,128)(2,1)S(1)} collective-permute-done((bf16[16,4096]{1,0:T(8,128)(2,1)S(1)}, bf16[16,4096]{1,0:T(8,128)(2,1)S(1)}, u32[]{:S(2)}, u32[]{:S(2)}) %collective-permute-start.24) | collective-permute-done | bytes 131104 | tf_op jit(solution)/shard_map/ppermute | solution.py:20
  80.7 2.1 %collective-permute-done.23 = bf16[16,4096]{1,0:T(8,128)(2,1)S(1)} collective-permute-done((bf16[16,4096]{1,0:T(8,128)(2,1)S(1)}, bf16[16,4096]{1,0:T(8,128)(2,1)S(1)}, u32[]{:S(2)}, u32[]{:S(2)}) %collective-permute-start.23) | collective-permute-done | bytes 131104 | tf_op jit(solution)/shard_map/ppermute | solution.py:20
  84.2 4.6 %collective-permute-done.21 = bf16[64,4096]{1,0:T(8,128)(2,1)S(1)} collective-permute-done((bf16[64,4096]{1,0:T(8,128)(2,1)S(1)}, bf16[64,4096]{1,0:T(8,128)(2,1)S(1)}, u32[]{:S(2)}, u32[]{:S(2)}) %collective-permute-start.21) | collective-permute-done | bytes 524320 | tf_op jit(solution)/shard_map/ppermute | solution.py:20
  89.4 1.5 %collective-permute-start.27 = (bf16[32,4096]{1,0:T(8,128)(2,1)S(1)}, bf16[32,4096]{1,0:T(8,128)(2,1)S(1)}, u32[]{:S(2)}, u32[]{:S(2)}) collective-permute-start(bf16[32,4096]{1,0:T(8,128)(2,1)S(1)} %split.43), channel_id=1, source_target_pairs={{0,16},{16,0},{8,24},{24,8},{1,17},{17,1},{9,25},{25,9},{2,18},{18... | collective-permute-start | bytes 786440 | tf_op jit(solution)/shard_map/ppermute | solution.py:20
  92.0 5.0 %collective-permute-done.27 = bf16[32,4096]{1,0:T(8,128)(2,1)S(1)} collective-permute-done((bf16[32,4096]{1,0:T(8,128)(2,1)S(1)}, bf16[32,4096]{1,0:T(8,128)(2,1)S(1)}, u32[]{:S(2)}, u32[]{:S(2)}) %collective-permute-start.27) | collective-permute-done | bytes 262176 | tf_op jit(solution)/shard_map/ppermute | solution.py:20
  97.1 1.5 %collective-permute-done.26 = bf16[32,4096]{1,0:T(8,128)(2,1)S(1)} collective-permute-done((bf16[32,4096]{1,0:T(8,128)(2,1)S(1)}, bf16[32,4096]{1,0:T(8,128)(2,1)S(1)}, u32[]{:S(2)}, u32[]{:S(2)}) %collective-permute-start.26) | collective-permute-done | bytes 262176 | tf_op jit(solution)/shard_map/ppermute | solution.py:20
  99.9 1.5 %collective-permute-start.30 = (bf16[16,4096]{1,0:T(8,128)(2,1)S(1)}, bf16[16,4096]{1,0:T(8,128)(2,1)S(1)}, u32[]{:S(2)}, u32[]{:S(2)}) collective-permute-start(bf16[16,4096]{1,0:T(8,128)(2,1)S(1)} %get-tuple-element.198), channel_id=1, source_target_pairs={{0,2},{1,3},{2,0},{3,1},{4,6},{5,7},{6,4},{7,5},{8,10},{9,11},{10,... | collective-permute-start | bytes 393224 | tf_op jit(solution)/shard_map/ppermute | solution.py:223
  102.6 4.0 %collective-permute-done.28 = bf16[32,4096]{1,0:T(8,128)(2,1)S(1)} collective-permute-done((bf16[32,4096]{1,0:T(8,128)(2,1)S(1)}, bf16[32,4096]{1,0:T(8,128)(2,1)S(1)}, u32[]{:S(2)}, u32[]{:S(2)}) %collective-permute-start.28) | collective-permute-done | bytes 262176 | tf_op jit(solution)/shard_map/ppermute | solution.py:20
  108.2 1.8 %collective-permute-start.33 = (bf16[16,4096]{1,0:T(8,128)(2,1)S(1)}, bf16[16,4096]{1,0:T(8,128)(2,1)S(1)}, u32[]{:S(2)}, u32[]{:S(2)}) collective-permute-start(bf16[16,4096]{1,0:T(8,128)(2,1)S(1)} %split.47), channel_id=1, source_target_pairs={{0,16},{16,0},{8,24},{24,8},{1,17},{17,1},{9,25},{25,9},{2,18},{18... | collective-permute-start | bytes 393224 | tf_op jit(solution)/shard_map/ppermute | solution.py:20
  111.5 2.1 %collective-permute-start.35 = (bf16[16,4096]{1,0:T(8,128)(2,1)S(1)}, bf16[16,4096]{1,0:T(8,128)(2,1)S(1)}, u32[]{:S(2)}, u32[]{:S(2)}) collective-permute-start(bf16[16,4096]{1,0:T(8,128)(2,1)S(1)} %get-tuple-element.188), channel_id=1, source_target_pairs={{0,4},{1,5},{2,6},{3,7},{4,0},{5,1},{6,2},{7,3},{8,12},{9,13},{10,... | collective-permute-start | bytes 393224 | tf_op jit(solution)/shard_map/ppermute | solution.py:223
  113.6 1.4 %collective-permute-done.32 = bf16[16,4096]{1,0:T(8,128)(2,1)S(1)} collective-permute-done((bf16[16,4096]{1,0:T(8,128)(2,1)S(1)}, bf16[16,4096]{1,0:T(8,128)(2,1)S(1)}, u32[]{:S(2)}, u32[]{:S(2)}) %collective-permute-start.32) | collective-permute-done | bytes 131104 | tf_op jit(solution)/shard_map/ppermute | solution.py:20
  115.6 1.8 %collective-permute-done.35 = bf16[16,4096]{1,0:T(8,128)(2,1)S(1)} collective-permute-done((bf16[16,4096]{1,0:T(8,128)(2,1)S(1)}, bf16[16,4096]{1,0:T(8,128)(2,1)S(1)}, u32[]{:S(2)}, u32[]{:S(2)}) %collective-permute-start.35) | collective-permute-done | bytes 131104 | tf_op jit(solution)/shard_map/ppermute | solution.py:223
  (102 shorter events, 24.0 us)
Async XLA Ops:
  2.0 15.4 %collective-permute-start.3 = (bf16[16,4224]{1,0:T(8,128)(2,1)S(1)}, bf16[16,4224]{1,0:T(8,128)(2,1)S(1)}, u32[]{:S(2)}, u32[]{:S(2)}) collective-permute-start(bf16[16,4224]{1,0:T(8,128)(2,1)S(1)} %concatenate.38), channel_id=1, source_target_pairs={{0,4},{1,5},{2,6},{3,7},{4,0},{5,1},{6,2},{7,3},{8,12},{9,13},{10,... | collective-permute-start | bytes 405512 | tf_op jit(solution)/shard_map/ppermute | solution.py:223
  6.1 11.4 %collective-permute-start.2 = (bf16[16,4224]{1,0:T(8,128)(2,1)S(1)}, bf16[16,4224]{1,0:T(8,128)(2,1)S(1)}, u32[]{:S(2)}, u32[]{:S(2)}) collective-permute-start(bf16[16,4224]{1,0:T(8,128)(2,1)S(1)} %concatenate.38), channel_id=1, source_target_pairs={{0,2},{1,3},{2,0},{3,1},{4,6},{5,7},{6,4},{7,5},{8,10},{9,11},{10,... | collective-permute-start | bytes 405512 | tf_op jit(solution)/shard_map/ppermute | solution.py:223
  7.7 9.7 %collective-permute-start = (bf16[16,4224]{1,0:T(8,128)(2,1)S(1)}, bf16[16,4224]{1,0:T(8,128)(2,1)S(1)}, u32[]{:S(2)}, u32[]{:S(2)}) collective-permute-start(bf16[16,4224]{1,0:T(8,128)(2,1)S(1)} %concatenate.38), channel_id=1, source_target_pairs={{0,8},{8,0},{16,24},{24,16},{1,9},{9,1},{17,25},{25,17},{2,10},{10... | collective-permute-start | bytes 405512 | tf_op jit(solution)/shard_map/ppermute | solution.py:20
  9.2 8.2 %collective-permute-start.1 = (bf16[16,4224]{1,0:T(8,128)(2,1)S(1)}, bf16[16,4224]{1,0:T(8,128)(2,1)S(1)}, u32[]{:S(2)}, u32[]{:S(2)}) collective-permute-start(bf16[16,4224]{1,0:T(8,128)(2,1)S(1)} %concatenate.39), channel_id=1, source_target_pairs={{0,16},{16,0},{8,24},{24,8},{1,17},{17,1},{9,25},{25,9},{2,18},{18... | collective-permute-start | bytes 405512 | tf_op jit(solution)/shard_map/ppermute | solution.py:20
  17.5 20.8 %collective-permute-start.11 = (bf16[4096,768]{1,0:T(8,128)(2,1)S(1)}, bf16[4096,768]{1,0:T(8,128)(2,1)S(1)}, u32[]{:S(2)}, u32[]{:S(2)}) collective-permute-start(bf16[4096,768]{1,0:T(8,128)(2,1)S(1)} %dequantize_in.1.refs_4_), channel_id=1, source_target_pairs={{0,1},{1,0},{2,3},{3,2},{4,5},{5,4},{6,7},{7,6},{8,9},{9,8},{10,11... | collective-permute-start | bytes 18874376 | tf_op jit(solution)/shard_map/ppermute | solution.py:20
  17.5 10.2 %collective-permute-start.4 = (bf16[32,4224]{1,0:T(8,128)(2,1)S(1)}, bf16[32,4224]{1,0:T(8,128)(2,1)S(1)}, u32[]{:S(2)}, u32[]{:S(2)}) collective-permute-start(bf16[32,4224]{1,0:T(8,128)(2,1)S(1)} %pad_maximum_fusion.2.refs_0_), channel_id=1, source_target_pairs={{0,16},{16,0},{8,24},{24,8},{1,17},{17,1},{9,25},{25,9},{2,18},{18... | collective-permute-start | bytes 811016 | tf_op jit(solution)/shard_map/ppermute | solution.py:20
  18.1 9.6 %collective-permute-start.5 = (bf16[32,4224]{1,0:T(8,128)(2,1)S(1)}, bf16[32,4224]{1,0:T(8,128)(2,1)S(1)}, u32[]{:S(2)}, u32[]{:S(2)}) collective-permute-start(bf16[32,4224]{1,0:T(8,128)(2,1)S(1)} %pad_maximum_fusion.3.refs_2_), channel_id=1, source_target_pairs={{0,8},{8,0},{16,24},{24,16},{1,9},{9,1},{17,25},{25,17},{2,10},{10... | collective-permute-start | bytes 811016 | tf_op jit(solution)/shard_map/ppermute | solution.py:20
  18.7 9.1 %collective-permute-start.7 = (bf16[16,4224]{1,0:T(8,128)(2,1)S(1)}, bf16[16,4224]{1,0:T(8,128)(2,1)S(1)}, u32[]{:S(2)}, u32[]{:S(2)}) collective-permute-start(bf16[16,4224]{1,0:T(8,128)(2,1)S(1)} %concatenate.39), channel_id=1, source_target_pairs={{0,4},{1,5},{2,6},{3,7},{4,0},{5,1},{6,2},{7,3},{8,12},{9,13},{10,... | collective-permute-start | bytes 405512 | tf_op jit(solution)/shard_map/ppermute | solution.py:223
  19.0 8.7 %collective-permute-start.6 = (bf16[16,4224]{1,0:T(8,128)(2,1)S(1)}, bf16[16,4224]{1,0:T(8,128)(2,1)S(1)}, u32[]{:S(2)}, u32[]{:S(2)}) collective-permute-start(bf16[16,4224]{1,0:T(8,128)(2,1)S(1)} %concatenate.39), channel_id=1, source_target_pairs={{0,2},{1,3},{2,0},{3,1},{4,6},{5,7},{6,4},{7,5},{8,10},{9,11},{10,... | collective-permute-start | bytes 405512 | tf_op jit(solution)/shard_map/ppermute | solution.py:223
  27.7 10.5 %collective-permute-start.12 = (bf16[384,4096]{1,0:T(8,128)(2,1)S(1)}, bf16[384,4096]{1,0:T(8,128)(2,1)S(1)}, u32[]{:S(2)}, u32[]{:S(2)}) collective-permute-start(bf16[384,4096]{1,0:T(8,128)(2,1)S(1)} %dequantize_down.1.refs_6_), channel_id=1, source_target_pairs={{0,1},{1,0},{2,3},{3,2},{4,5},{5,4},{6,7},{7,6},{8,9},{9,8},{10,11... | collective-permute-start | bytes 9437192 | tf_op jit(solution)/shard_map/ppermute | solution.py:20
  27.8 10.4 %collective-permute-start.10 = (bf16[32,4224]{1,0:T(8,128)(2,1)S(1)}, bf16[32,4224]{1,0:T(8,128)(2,1)S(1)}, u32[]{:S(2)}, u32[]{:S(2)}) collective-permute-start(bf16[32,4224]{1,0:T(8,128)(2,1)S(1)} %constant_dynamic-update-slice_fusion.2), channel_id=1, source_target_pairs={{0,2},{1,3},{2,0},{3,1},{4,6},{5,7},{6,4},{7,5},{8,10},{9,11},{10,... | collective-permute-start | bytes 811016 | tf_op jit(solution)/shard_map/ppermute | solution.py:223
  27.9 8.9 %collective-permute-start.9 = (bf16[32,4224]{1,0:T(8,128)(2,1)S(1)}, bf16[32,4224]{1,0:T(8,128)(2,1)S(1)}, u32[]{:S(2)}, u32[]{:S(2)}) collective-permute-start(bf16[32,4224]{1,0:T(8,128)(2,1)S(1)} %constant_dynamic-update-slice_fusion.2), channel_id=1, source_target_pairs={{0,16},{16,0},{8,24},{24,8},{1,17},{17,1},{9,25},{25,9},{2,18},{18... | collective-permute-start | bytes 811016 | tf_op jit(solution)/shard_map/ppermute | solution.py:20
  29.5 8.7 %collective-permute-start.8 = (bf16[32,4224]{1,0:T(8,128)(2,1)S(1)}, bf16[32,4224]{1,0:T(8,128)(2,1)S(1)}, u32[]{:S(2)}, u32[]{:S(2)}) collective-permute-start(bf16[32,4224]{1,0:T(8,128)(2,1)S(1)} %constant_dynamic-update-slice_fusion), channel_id=1, source_target_pairs={{0,8},{8,0},{16,24},{24,16},{1,9},{9,1},{17,25},{25,17},{2,10},{10... | collective-permute-start | bytes 811016 | tf_op jit(solution)/shard_map/ppermute | solution.py:20
  38.3 7.2 %collective-permute-start.16 = (bf16[16,4224]{1,0:T(8,128)(2,1)S(1)}, bf16[16,4224]{1,0:T(8,128)(2,1)S(1)}, u32[]{:S(2)}, u32[]{:S(2)}) collective-permute-start(bf16[16,4224]{1,0:T(8,128)(2,1)S(1)} %get-tuple-element.191), channel_id=1, source_target_pairs={{0,16},{16,0},{8,24},{24,8},{1,17},{17,1},{9,25},{25,9},{2,18},{18... | collective-permute-start | bytes 405512 | tf_op jit(solution)/shard_map/ppermute | solution.py:20
  38.9 6.7 %collective-permute-start.15 = (bf16[16,4224]{1,0:T(8,128)(2,1)S(1)}, bf16[16,4224]{1,0:T(8,128)(2,1)S(1)}, u32[]{:S(2)}, u32[]{:S(2)}) collective-permute-start(bf16[16,4224]{1,0:T(8,128)(2,1)S(1)} %get-tuple-element.192), channel_id=1, source_target_pairs={{0,8},{8,0},{16,24},{24,16},{1,9},{9,1},{17,25},{25,17},{2,10},{10... | collective-permute-start | bytes 405512 | tf_op jit(solution)/shard_map/ppermute | solution.py:20
  40.4 14.5 %collective-permute-start.13 = (bf16[64,4224]{1,0:T(8,128)(2,1)S(1)}, bf16[64,4224]{1,0:T(8,128)(2,1)S(1)}, u32[]{:S(2)}, u32[]{:S(2)}) collective-permute-start(bf16[64,4224]{1,0:T(8,128)(2,1)S(1)} %pad_maximum_fusion.refs_0_), channel_id=1, source_target_pairs={{0,16},{16,0},{8,24},{24,8},{1,17},{17,1},{9,25},{25,9},{2,18},{18... | collective-permute-start | bytes 1622024 | tf_op jit(solution)/shard_map/ppermute | solution.py:20
  41.9 13.6 %collective-permute-start.14 = (bf16[64,4224]{1,0:T(8,128)(2,1)S(1)}, bf16[64,4224]{1,0:T(8,128)(2,1)S(1)}, u32[]{:S(2)}, u32[]{:S(2)}) collective-permute-start(bf16[64,4224]{1,0:T(8,128)(2,1)S(1)} %pad_maximum_fusion.1.refs_2_), channel_id=1, source_target_pairs={{0,8},{8,0},{16,24},{24,16},{1,9},{9,1},{17,25},{25,17},{2,10},{10... | collective-permute-start | bytes 1622024 | tf_op jit(solution)/shard_map/ppermute | solution.py:20
  55.5 8.4 %collective-permute-start.17 = (bf16[32,4224]{1,0:T(8,128)(2,1)S(1)}, bf16[32,4224]{1,0:T(8,128)(2,1)S(1)}, u32[]{:S(2)}, u32[]{:S(2)}) collective-permute-start(bf16[32,4224]{1,0:T(8,128)(2,1)S(1)} %pad_maximum_fusion.4.refs_0_), channel_id=1, source_target_pairs={{0,16},{16,0},{8,24},{24,8},{1,17},{17,1},{9,25},{25,9},{2,18},{18... | collective-permute-start | bytes 811016 | tf_op jit(solution)/shard_map/ppermute | solution.py:20
  56.6 7.2 %collective-permute-start.18 = (bf16[32,4224]{1,0:T(8,128)(2,1)S(1)}, bf16[32,4224]{1,0:T(8,128)(2,1)S(1)}, u32[]{:S(2)}, u32[]{:S(2)}) collective-permute-start(bf16[32,4224]{1,0:T(8,128)(2,1)S(1)} %pad_maximum_fusion.5.refs_2_), channel_id=1, source_target_pairs={{0,8},{8,0},{16,24},{24,16},{1,9},{9,1},{17,25},{25,17},{2,10},{10... | collective-permute-start | bytes 811016 | tf_op jit(solution)/shard_map/ppermute | solution.py:20
  67.0 6.8 %collective-permute-start.19 = (bf16[32,4096]{1,0:T(8,128)(2,1)S(1)}, bf16[32,4096]{1,0:T(8,128)(2,1)S(1)}, u32[]{:S(2)}, u32[]{:S(2)}) collective-permute-start(bf16[32,4096]{1,0:T(8,128)(2,1)S(1)} %get-tuple-element.148), channel_id=1, source_target_pairs={{0,16},{16,0},{8,24},{24,8},{1,17},{17,1},{9,25},{25,9},{2,18},{18... | collective-permute-start | bytes 786440 | tf_op jit(solution)/shard_map/ppermute | solution.py:20
  67.6 6.4 %collective-permute-start.20 = (bf16[32,4096]{1,0:T(8,128)(2,1)S(1)}, bf16[32,4096]{1,0:T(8,128)(2,1)S(1)}, u32[]{:S(2)}, u32[]{:S(2)}) collective-permute-start(bf16[32,4096]{1,0:T(8,128)(2,1)S(1)} %get-tuple-element.150), channel_id=1, source_target_pairs={{0,8},{8,0},{16,24},{24,16},{1,9},{9,1},{17,25},{25,17},{2,10},{10... | collective-permute-start | bytes 786440 | tf_op jit(solution)/shard_map/ppermute | solution.py:20
  74.1 6.5 %collective-permute-start.24 = (bf16[16,4096]{1,0:T(8,128)(2,1)S(1)}, bf16[16,4096]{1,0:T(8,128)(2,1)S(1)}, u32[]{:S(2)}, u32[]{:S(2)}) collective-permute-start(bf16[16,4096]{1,0:T(8,128)(2,1)S(1)} %split.39), channel_id=1, source_target_pairs={{0,16},{16,0},{8,24},{24,8},{1,17},{17,1},{9,25},{25,9},{2,18},{18... | collective-permute-start | bytes 393224 | tf_op jit(solution)/shard_map/ppermute | solution.py:20
  76.2 6.5 %collective-permute-start.23 = (bf16[16,4096]{1,0:T(8,128)(2,1)S(1)}, bf16[16,4096]{1,0:T(8,128)(2,1)S(1)}, u32[]{:S(2)}, u32[]{:S(2)}) collective-permute-start(bf16[16,4096]{1,0:T(8,128)(2,1)S(1)} %split.37), channel_id=1, source_target_pairs={{0,8},{8,0},{16,24},{24,16},{1,9},{9,1},{17,25},{25,17},{2,10},{10... | collective-permute-start | bytes 393224 | tf_op jit(solution)/shard_map/ppermute | solution.py:20
  76.4 12.4 %collective-permute-start.21 = (bf16[64,4096]{1,0:T(8,128)(2,1)S(1)}, bf16[64,4096]{1,0:T(8,128)(2,1)S(1)}, u32[]{:S(2)}, u32[]{:S(2)}) collective-permute-start(bf16[64,4096]{1,0:T(8,128)(2,1)S(1)} %get-tuple-element.160), channel_id=1, source_target_pairs={{0,16},{16,0},{8,24},{24,8},{1,17},{17,1},{9,25},{25,9},{2,18},{18... | collective-permute-start | bytes 1572872 | tf_op jit(solution)/shard_map/ppermute | solution.py:20
  77.2 12.1 %collective-permute-start.22 = (bf16[64,4096]{1,0:T(8,128)(2,1)S(1)}, bf16[64,4096]{1,0:T(8,128)(2,1)S(1)}, u32[]{:S(2)}, u32[]{:S(2)}) collective-permute-start(bf16[64,4096]{1,0:T(8,128)(2,1)S(1)} %get-tuple-element.162), channel_id=1, source_target_pairs={{0,8},{8,0},{16,24},{24,16},{1,9},{9,1},{17,25},{25,17},{2,10},{10... | collective-permute-start | bytes 1572872 | tf_op jit(solution)/shard_map/ppermute | solution.py:20
  82.8 6.6 %collective-permute-start.25 = (bf16[32,4096]{1,0:T(8,128)(2,1)S(1)}, bf16[32,4096]{1,0:T(8,128)(2,1)S(1)}, u32[]{:S(2)}, u32[]{:S(2)}) collective-permute-start(bf16[32,4096]{1,0:T(8,128)(2,1)S(1)} %pad_maximum_fusion.6), channel_id=1, source_target_pairs={{0,2},{1,3},{2,0},{3,1},{4,6},{5,7},{6,4},{7,5},{8,10},{9,11},{10,... | collective-permute-start | bytes 786440 | tf_op jit(solution)/shard_map/ppermute | solution.py:223
  89.4 7.6 %collective-permute-start.27 = (bf16[32,4096]{1,0:T(8,128)(2,1)S(1)}, bf16[32,4096]{1,0:T(8,128)(2,1)S(1)}, u32[]{:S(2)}, u32[]{:S(2)}) collective-permute-start(bf16[32,4096]{1,0:T(8,128)(2,1)S(1)} %split.43), channel_id=1, source_target_pairs={{0,16},{16,0},{8,24},{24,8},{1,17},{17,1},{9,25},{25,9},{2,18},{18... | collective-permute-start | bytes 786440 | tf_op jit(solution)/shard_map/ppermute | solution.py:20
  90.9 7.6 %collective-permute-start.26 = (bf16[32,4096]{1,0:T(8,128)(2,1)S(1)}, bf16[32,4096]{1,0:T(8,128)(2,1)S(1)}, u32[]{:S(2)}, u32[]{:S(2)}) collective-permute-start(bf16[32,4096]{1,0:T(8,128)(2,1)S(1)} %split.41), channel_id=1, source_target_pairs={{0,8},{8,0},{16,24},{24,16},{1,9},{9,1},{17,25},{25,17},{2,10},{10... | collective-permute-start | bytes 786440 | tf_op jit(solution)/shard_map/ppermute | solution.py:20
  98.8 9.2 %collective-permute-start.31 = (bf16[16,4096]{1,0:T(8,128)(2,1)S(1)}, bf16[16,4096]{1,0:T(8,128)(2,1)S(1)}, u32[]{:S(2)}, u32[]{:S(2)}) collective-permute-start(bf16[16,4096]{1,0:T(8,128)(2,1)S(1)} %get-tuple-element.196), channel_id=1, source_target_pairs={{0,4},{1,5},{2,6},{3,7},{4,0},{5,1},{6,2},{7,3},{8,12},{9,13},{10,... | collective-permute-start | bytes 393224 | tf_op jit(solution)/shard_map/ppermute | solution.py:223
  98.8 7.8 %collective-permute-start.28 = (bf16[32,4096]{1,0:T(8,128)(2,1)S(1)}, bf16[32,4096]{1,0:T(8,128)(2,1)S(1)}, u32[]{:S(2)}, u32[]{:S(2)}) collective-permute-start(bf16[32,4096]{1,0:T(8,128)(2,1)S(1)} %get-tuple-element.177), channel_id=1, source_target_pairs={{0,16},{16,0},{8,24},{24,8},{1,17},{17,1},{9,25},{25,9},{2,18},{18... | collective-permute-start | bytes 786440 | tf_op jit(solution)/shard_map/ppermute | solution.py:20
  99.9 8.2 %collective-permute-start.30 = (bf16[16,4096]{1,0:T(8,128)(2,1)S(1)}, bf16[16,4096]{1,0:T(8,128)(2,1)S(1)}, u32[]{:S(2)}, u32[]{:S(2)}) collective-permute-start(bf16[16,4096]{1,0:T(8,128)(2,1)S(1)} %get-tuple-element.198), channel_id=1, source_target_pairs={{0,2},{1,3},{2,0},{3,1},{4,6},{5,7},{6,4},{7,5},{8,10},{9,11},{10,... | collective-permute-start | bytes 393224 | tf_op jit(solution)/shard_map/ppermute | solution.py:223
  101.5 6.4 %collective-permute-start.29 = (bf16[32,4096]{1,0:T(8,128)(2,1)S(1)}, bf16[32,4096]{1,0:T(8,128)(2,1)S(1)}, u32[]{:S(2)}, u32[]{:S(2)}) collective-permute-start(bf16[32,4096]{1,0:T(8,128)(2,1)S(1)} %get-tuple-element.179), channel_id=1, source_target_pairs={{0,8},{8,0},{16,24},{24,16},{1,9},{9,1},{17,25},{25,17},{2,10},{10... | collective-permute-start | bytes 786440 | tf_op jit(solution)/shard_map/ppermute | solution.py:20
  (11 other events, 70.4 us)

commit v11 on v8

--- a/solution.py
+++ b/solution.py
@@ -166,17 +166,20 @@
 def expert_kernel(count, experts, own_expert, *refs):
     pieces, refs = refs[:count], refs[count:]
     in_refs, down_refs, refs = refs[:2], refs[2:4], refs[4:]
-    outs, (rows, hidden) = refs[:count], refs[count:]
-    size, (half, model_width) = pieces[0].shape[0], down_refs[0].shape
+    outs, (rows, hidden) = refs[:-2], refs[-2:]
+    half, model_width = down_refs[0].shape
     strip = min(4 * BLOCK, model_width)
 
-    weights = []
-    for place, piece in enumerate(pieces):
-        rows[place * size : (place + 1) * size, :] = piece[:, :model_width]
+    weights, first = [], 0
+    for piece in pieces:
+        size = piece.shape[0]
+        rows[first : first + size, :] = piece[:, :model_width]
         marks = piece[:, model_width:].astype(jnp.float32)
         column = lax.broadcasted_iota(jnp.int32, marks.shape, 1)
         chosen = (column == own_expert[0]) | (column == own_expert[0] + experts)
         weights.append(jnp.sum(jnp.where(chosen, marks, 0.0), axis=1, keepdims=True))
+        first += size
+    weights = jnp.concatenate(weights, axis=0)
     for part, in_ref in enumerate(in_refs):
         for col in range(half // BLOCK):
             at = slice(2 * col * BLOCK, 2 * (col + 1) * BLOCK)
@@ -184,26 +187,26 @@
             value = (silu(both[:, :BLOCK]) * both[:, BLOCK:]).astype(jnp.bfloat16)
             to = part * half + col * BLOCK
             hidden[:, to : to + BLOCK] = value
-    for first in range(0, model_width, strip):
-        at = slice(first, first + strip)
+    for start in range(0, model_width, strip):
+        at = slice(start, start + strip)
         value = jnp.dot(hidden[:, :half], down_refs[0][:, at], preferred_element_type=jnp.float32)
         value += jnp.dot(hidden[:, half:], down_refs[1][:, at], preferred_element_type=jnp.float32)
-        for place, out in enumerate(outs):
-            weighted = value[place * size : (place + 1) * size] * weights[place]
-            out[:, at] = weighted.astype(jnp.bfloat16)
-
-
-def expert_layer(pieces, own_expert, experts, *weights):
-    count, size = len(pieces), pieces[0].shape[0]
+        value, first = (value * weights).astype(jnp.bfloat16), 0
+        for out in outs:
+            out[:, at] = value[first : first + out.shape[0]]
+            first += out.shape[0]
+
+
+def expert_layer(pieces, out_sizes, own_expert, experts, *weights):
+    count, total = len(pieces), sum(out_sizes)
     model_width, width = weights[0].shape
-    total = count * size
     whole = pl.BlockSpec(memory_space=pltpu.VMEM)
     weights = [pltpu.with_memory_space_constraint(weight, pltpu.VMEM) for weight in weights]
     return pl.pallas_call(
         functools.partial(expert_kernel, count, experts),
         in_specs=[pl.BlockSpec(memory_space=pltpu.SMEM)] + [whole] * (count + len(weights)),
-        out_specs=[whole] * count,
-        out_shape=[jax.ShapeDtypeStruct((size, model_width), jnp.bfloat16)] * count,
+        out_specs=[whole] * len(out_sizes),
+        out_shape=[jax.ShapeDtypeStruct((size, model_width), jnp.bfloat16) for size in out_sizes],
         scratch_shapes=[
             pltpu.VMEM((total, model_width), jnp.bfloat16),
             pltpu.VMEM((total, width), jnp.bfloat16),
@@ -238,70 +241,136 @@
     low = (weight - high.astype(jnp.float32)).astype(jnp.bfloat16)
     extra = -(-2 * expert_count // BLOCK) * BLOCK
     pad = jnp.zeros((token_count, extra - 2 * expert_count), jnp.bfloat16)
-    payload = jnp.concatenate([tokens, high, low, pad], axis=1)
+    half = token_count // 2
+    halves = [slice(0, half), slice(half, token_count)]
+    payload = [
+        jnp.concatenate([part[rows] for part in (tokens, high, low, pad)], axis=1)
+        for rows in halves
+    ]
 
     together = lax.optimization_barrier
     place = jnp.reshape(own_expert, (1,)).astype(jnp.int32)
-    last = len(bits) - 1
-    pairs = [(first, first + 1) for first in range(0, pair_count, 2)]
     place, payload = together((place, payload))
-    came = {0: payload, 1: across_chips(payload, 1)}
-
-    def along_z(far):
-        low = far & -far
-        came[far] = across_chips(came[far ^ low], low)
-
-    in_own = dequantize_in(gate_q[0], up_q[0], gate_scale[0], up_scale[0])
-    down_own = dequantize_down(down_q[0], down_scale[0])
-    came, in_own, down_own = together((came, in_own, down_own))
-    in_other, down_other = from_partner(in_own, "expert", 0), None
-    pieces, outs, weights = {}, {}, None
-    for number, pair in enumerate(pairs):
-        following = pairs[number + 1] if number + 1 < len(pairs) else ()
-        blocks = {far: came[far] for far in pair}
-        for turn in range(len(bits)):
-            if turn < len(following):
-                along_z(following[turn])
-            arrived = {far: from_partner(blocks[far], "dp", orders[far % 2][turn]) for far in pair}
-            if turn == last:
-                pieces[pair] = [part for far in pair for part in (blocks[far], arrived[far])]
+    own = jnp.concatenate(payload, axis=0)
+    fars, turns = range(2, pair_count), len(bits)
+    steps = [[(0, turn)] for turn in range(turns)]
+    for far in fars:
+        for turn in range(turns):
+            if turn == 0 and far > 2:
+                steps[-1].append((far, turn))
             else:
-                blocks = {
-                    far: jnp.concatenate([blocks[far], arrived[far]], axis=0) for far in pair
-                }
-                if number == 0 and turn == 0:
-                    blocks, came, down_own = together((blocks, came, down_own))
-                    down_other = from_partner(down_own, "expert", 0)
-                elif number == 1 and turn == 0:
-                    blocks, outs = together((blocks, outs))
+                steps.append([(far, turn)])
+
+    def gather_turn(far, turn):
+        blocks = lanes[far]
+        arrived = [from_partner(block, "dp", orders[lane][turn]) for lane, block in enumerate(blocks)]
+        if turn == turns - 1:
+            lanes[far] = [part for pair in zip(blocks, arrived) for part in pair]
+            gathered.append(far)
+        else:
+            lanes[far] = [jnp.concatenate(pair, axis=0) for pair in zip(blocks, arrived)]
+
+    def layer(pieces, sizes):
+        return expert_layer(pieces, sizes, place, expert_count, *weights)
+
+    def halved_layer(far):
+        return layer(lanes[far], [piece.shape[0] for piece in lanes[far]])
+
+    lanes, outs, gathered, came = {0: payload}, {}, [], {}
+    kept_rows = half * group_count // 2
+    beside = across_chips(own, 1)
+    second = [across_chips(payload[0], 2)]
+    for number, step in enumerate(steps):
+        for far, turn in step:
+            if turn == 0 and far > 0:
+                lanes[far] = [came[far][rows] for rows in halves]
+                if far + 1 in fars:
+                    low = (far + 1) & -(far + 1)
+                    block = own if low == far + 1 else came[(far + 1) ^ low]
+                    came[far + 1] = across_chips(block, low)
+        if number == turns + 1:
+            kept, other = lanes[0][0::2], lanes[0][1::2]
+            rest = jnp.concatenate([*(block[half:] for block in kept), *other], axis=0)
+            rest = across_chips(rest, 1)
+        if number > turns and gathered:
+            ready = gathered.pop(0)
+            outs[ready] = halved_layer(ready)
+        for far, turn in step:
+            gather_turn(far, turn)
         if number == 0:
-            tied = (pieces[pair], came, in_other, down_other)
-            pieces[pair], came, in_other, down_other = together(tied)
+            in_own = dequantize_in(gate_q[0], up_q[0], gate_scale[0], up_scale[0])
+            down_own = dequantize_down(down_q[0], down_scale[0])
+            tied = (lanes, own, payload, beside, second, in_own, down_own)
+            lanes, own, payload, beside, second, in_own, down_own = together(tied)
+            second.append(across_chips(payload[1], 2))
+            in_other = from_partner(in_own, "expert", 0)
+        elif number == 1:
+            lanes, second, down_own = together((lanes, second, down_own))
+            came[2] = jnp.concatenate(second, axis=0)
+            down_other = from_partner(down_own, "expert", 0)
+        elif number == turns:
+            tied = (lanes, came, in_other, down_other)
+            lanes, came, in_other, down_other = together(tied)
             weights = (in_own, in_other, down_own, down_other)
+        elif number < len(steps) - 1:
+            lanes, came, outs = together((lanes, came, outs))
         else:
-            pieces[pair], outs = together((pieces[pair], outs))
-        outs[pair] = expert_layer(pieces[pair], place, expert_count, *weights)
-
-    total = tokens.astype(jnp.float32)
-    sums = {}
-    for pair in pairs[::-1]:
-        for turn in range(last, -1, -1):
-            for where, far in enumerate(pair):
-                if turn == last:
-                    kept, sent = outs[pair][2 * where : 2 * where + 2]
-                else:
-                    kept, sent = jnp.split(sums[far], 2, axis=0)
-                sums[far] = added(kept, from_partner(sent, "dp", orders[far % 2][turn]))
-            sums, outs = together((sums, outs))
-        for far in reversed(pair):
-            block, low = sums.pop(far), far & -far
-            if far == 0:
-                total = total + block.astype(jnp.float32)
-            elif far == low:
-                total = total + across_chips(block, low).astype(jnp.float32)
+            lanes, rest, outs = together((lanes, rest, outs))
+    final = gathered.pop()
+    sizes = [piece.shape[0] for piece in lanes[final]]
+    returned, *outs[final] = layer([beside, rest, *lanes[final]], [4 * kept_rows, *sizes])
+
+    def sum_turn(far, turn):
+        result = []
+        for lane in range(2):
+            if turn == turns - 1:
+                kept, sent = outs[far][2 * lane : 2 * lane + 2]
             else:
-                sums[far ^ low] = added(sums[far ^ low], across_chips(block, low))
-    return total.astype(jnp.bfloat16)
+                kept, sent = jnp.split(sums[far][lane], 2, axis=0)
+            result.append(added(kept, from_partner(sent, "dp", orders[lane][turn])))
+        sums[far] = result
+
+    returned = across_chips(returned, 1)
+    sums, merged, parts = {}, {}, []
+    for step in steps[:turns - 1:-1]:
+        for far, turn in reversed(step):
+            sum_turn(far, turn)
+        far, turn = step[0] if len(step) == 1 else step[1]
+        if turn == 0 and far > 2:
+            low = far & -far
+            block = jnp.concatenate(sums.pop(far), axis=0)
+            block = added(block, merged.pop(far)) if far in merged else block
+            block = across_chips(block, low)
+            if far == low:
+                parts.append([block[rows] for rows in halves])
+            else:
+                into = far ^ low
+                merged[into] = added(merged[into], block) if into in merged else block
+    sums, outs, merged, returned = together((sums, outs, merged, returned))
+    lower = kept_rows - half
+    own_parts = [
+        jnp.concatenate([returned[:half], returned[2 * half : 2 * half + lower]], axis=0),
+        returned[2 * kept_rows : 3 * kept_rows],
+        jnp.concatenate([returned[half : 2 * half], returned[2 * half + lower : 2 * kept_rows]], axis=0),
+        returned[3 * kept_rows :],
+    ]
+    outs[0] = [added(block, part) for block, part in zip(outs[0], own_parts)]
+    leaving = sums.pop(2)
+    if 2 in merged:
+        leaving = [added(block, merged[2][rows]) for block, rows in zip(leaving, halves)]
+    back = [across_chips(leaving[0], 2)]
+    for turn in range(turns - 1, 0, -1):
+        sum_turn(0, turn)
+    sums, back, leaving = together((sums, back, leaving))
+    back.append(across_chips(leaving[1], 2))
+    sum_turn(0, 0)
+    result = []
+    for lane, rows in enumerate(halves):
+        total = tokens[rows].astype(jnp.float32) + sums[0][lane].astype(jnp.float32)
+        for part in [back[lane], *(part[lane] for part in parts)]:
+            total = total + part.astype(jnp.float32)
+        result.append(total.astype(jnp.bfloat16))
+    return jnp.concatenate(result, axis=0)
 
 
 def shards(tokens, expert_ids, *weights):

time: 126 us -> 120 us (0.952)
  waiting for transfers between devices: 77.3 us -> 62.6 us
  starting transfers between devices: 25.8 us -> 33.1 us
    ppermute x18 -> x26, waiting for transfers between devices: 58.2 us -> 28.7 us  [from_partner(): return lax.ppermute(block, axis, route)]
    ppermute x6 -> x9, waiting for transfers between devices: 19 us -> 33.8 us  [across_chips(): lax.ppermute(block, 'expert', [(low, low ^ 2 * far) for low in range(coun...]
    ppermute x18 -> x26, starting transfers between devices: 16.5 us -> 24.4 us  [from_partner(): return lax.ppermute(block, axis, route)]
    ppermute x6 -> x9, starting transfers between devices: 9.26 us -> 8.68 us  [across_chips(): lax.ppermute(block, 'expert', [(low, low ^ 2 * far) for low in range(coun...]
    pallas_call x2 -> x3, Pallas kernels: 11.5 us -> 12 us  [expert_layer(): pl.pallas_call(functools.partial(expert_kernel, count, experts), in_specs...]
    unnamed x13 -> x15, local copies, waits for them, and re-layouts: 3.56 us -> 3.58 us
  transfers between devices with their start and end apart: 24 -> 35, of which waited for: 19 -> 20; matrix products, arithmetic and copies ran while one was open for 1% -> 1% of each run, Pallas kernels for 8% -> 8%
where the time goes in v11:
time: 120 us; the launch traced here: 119 us
  waiting for transfers between devices  62.6 us (52%)
  starting transfers between devices  33.1 us (28%)
  Pallas kernels  15.7 us (13%)
  local copies, waits for them, and re-layouts  5.01 us (4%)
  other arithmetic  2.61 us (2%)
    ppermute x9, waiting for transfers between devices, across_chips(): lax.ppermute(block, 'expert', [(low, low ^ 2 * far) for low in range(coun...  33.8 us
    ppermute x26, waiting for transfers between devices, from_partner(): return lax.ppermute(block, axis, route)  28.7 us
    ppermute x26, starting transfers between devices, from_partner(): return lax.ppermute(block, axis, route)  24.4 us
    pallas_call x3, Pallas kernels, expert_layer(): pl.pallas_call(functools.partial(expert_kernel, count, experts), in_specs...  12 us
    ppermute x9, starting transfers between devices, across_chips(): lax.ppermute(block, 'expert', [(low, low ^ 2 * far) for low in range(coun...  8.68 us
    unnamed x15, local copies, waits for them, and re-layouts  3.58 us
  transfers between devices with their start and end apart: 35, of which 20 were waited for; matrix products, arithmetic and copies ran while one was open for 1% of the time, Pallas kernels for 8%

profile of v11, /device:TPU:0, one launch (start us, length us, event | category | flops | bytes accessed | tf_op | source)
XLA Modules:
  0.0 119.4 jit_solution(659235397990882718)
XLA Ops:
  2.0 4.0 %collective-permute-start.3 = (bf16[16,4224]{1,0:T(8,128)(2,1)S(1)}, bf16[16,4224]{1,0:T(8,128)(2,1)S(1)}, u32[]{:S(2)}, u32[]{:S(2)}) collective-permute-start(bf16[16,4224]{1,0:T(8,128)(2,1)S(1)} %concatenate.45), channel_id=1, source_target_pairs={{0,4},{1,5},{2,6},{3,7},{4,0},{5,1},{6,2},{7,3},{8,12},{9,13},{10,... | collective-permute-start | bytes 405512 | tf_op jit(solution)/shard_map/ppermute | solution.py:226
  6.1 1.5 %collective-permute-start = (bf16[16,4224]{1,0:T(8,128)(2,1)S(1)}, bf16[16,4224]{1,0:T(8,128)(2,1)S(1)}, u32[]{:S(2)}, u32[]{:S(2)}) collective-permute-start(bf16[16,4224]{1,0:T(8,128)(2,1)S(1)} %concatenate.45), channel_id=1, source_target_pairs={{0,8},{8,0},{16,24},{24,16},{1,9},{9,1},{17,25},{25,17},{2,10},{10... | collective-permute-start | bytes 405512 | tf_op jit(solution)/shard_map/ppermute | solution.py:20
  7.6 1.5 %collective-permute-start.1 = (bf16[16,4224]{1,0:T(8,128)(2,1)S(1)}, bf16[16,4224]{1,0:T(8,128)(2,1)S(1)}, u32[]{:S(2)}, u32[]{:S(2)}) collective-permute-start(bf16[16,4224]{1,0:T(8,128)(2,1)S(1)} %concatenate.46), channel_id=1, source_target_pairs={{0,16},{16,0},{8,24},{24,8},{1,17},{17,1},{9,25},{25,9},{2,18},{18... | collective-permute-start | bytes 405512 | tf_op jit(solution)/shard_map/ppermute | solution.py:20
  9.1 1.6 %collective-permute-start.2 = (bf16[32,4224]{1,0:T(8,128)(2,1)S(1)}, bf16[32,4224]{1,0:T(8,128)(2,1)S(1)}, u32[]{:S(2)}, u32[]{:S(2)}) collective-permute-start(bf16[32,4224]{1,0:T(8,128)(2,1)S(1)} %constant_dynamic-update-slice_fusion), channel_id=1, source_target_pairs={{0,2},{1,3},{2,0},{3,1},{4,6},{5,7},{6,4},{7,5},{8,10},{9,11},{10,... | collective-permute-start | bytes 811016 | tf_op jit(solution)/shard_map/ppermute | solution.py:226
  11.5 1.9 %copy-done = bf16[1,384,4096]{2,1,0:T(8,128)(2,1)S(1)} copy-done((bf16[1,384,4096]{2,1,0:T(8,128)(2,1)S(1)}, bf16[1,384,4096]{2,1,0:T(8,128)(2,1)}, u32[]{:S(2)}) %copy-start) | copy-done | bytes 3145752
  13.3 1.8 %dequantize_down.1.refs_6_.refs_8_ = bf16[384,4096]{1,0:T(8,128)(2,1)S(1)} custom-call(f32[3,32]{1,0:T(4,128)S(1)} %bitcast.18, bf16[384,4096]{1,0:T(8,128)(2,1)S(1)} %bitcast.15), custom_call_target="tpu_custom_call" | custom-call | flops 1572864 | bytes 6291456 | tf_op jit(solution)/shard_map/dequantize_down/pallas_call | solution.py:148
  16.2 1.9 %dequantize_in.1.refs_4_.refs_6_ = bf16[4096,768]{1,0:T(8,128)(2,1)S(1)} custom-call(f32[3,32]{1,0:T(4,128)S(1)} %get-tuple-element.176.gate_scales, f32[3,32]{1,0:T(4,128)S(1)} %get-tuple-element.175.up_scales, bf16[4096,384]{1,0:T(8,128)(2,1)S(1)} %bitcast.16, bf16[4096,384]{1,0:T(8,128)(2,1)S(1)} %bitcast.17), custom_call_target="tpu_custom_call" | custom-call | flops 3145728 | bytes 12582912 | tf_op jit(solution)/shard_map/dequantize_in/pallas_call | solution.py:120
  20.1 8.5 %collective-permute-done.6 = bf16[16,4224]{1,0:T(8,128)(2,1)S(1)} collective-permute-done((bf16[16,4224]{1,0:T(8,128)(2,1)S(1)}, bf16[16,4224]{1,0:T(8,128)(2,1)S(1)}, u32[]{:S(2)}, u32[]{:S(2)}) %collective-permute-start.6) | collective-permute-done | bytes 135200 | tf_op jit(solution)/shard_map/ppermute | solution.py:226
  28.7 1.4 %collective-permute-start.7 = (bf16[16,4224]{1,0:T(8,128)(2,1)S(1)}, bf16[16,4224]{1,0:T(8,128)(2,1)S(1)}, u32[]{:S(2)}, u32[]{:S(2)}) collective-permute-start(bf16[16,4224]{1,0:T(8,128)(2,1)S(1)} %collective-permute-done.3), channel_id=1, source_target_pairs={{0,8},{8,0},{16,24},{24,16},{1,9},{9,1},{17,25},{25,17},{2,10},{10... | collective-permute-start | bytes 405512 | tf_op jit(solution)/shard_map/ppermute | solution.py:20
  30.1 1.5 %collective-permute-start.8 = (bf16[16,4224]{1,0:T(8,128)(2,1)S(1)}, bf16[16,4224]{1,0:T(8,128)(2,1)S(1)}, u32[]{:S(2)}, u32[]{:S(2)}) collective-permute-start(bf16[16,4224]{1,0:T(8,128)(2,1)S(1)} %collective-permute-done.6), channel_id=1, source_target_pairs={{0,16},{16,0},{8,24},{24,8},{1,17},{17,1},{9,25},{25,9},{2,18},{18... | collective-permute-start | bytes 405512 | tf_op jit(solution)/shard_map/ppermute | solution.py:20
  31.7 3.0 %collective-permute-done.7 = bf16[16,4224]{1,0:T(8,128)(2,1)S(1)} collective-permute-done((bf16[16,4224]{1,0:T(8,128)(2,1)S(1)}, bf16[16,4224]{1,0:T(8,128)(2,1)S(1)}, u32[]{:S(2)}, u32[]{:S(2)}) %collective-permute-start.7) | collective-permute-done | bytes 135200 | tf_op jit(solution)/shard_map/ppermute | solution.py:20
  35.7 4.2 %collective-permute-done.9 = bf16[32,4224]{1,0:T(8,128)(2,1)S(1)} collective-permute-done((bf16[32,4224]{1,0:T(8,128)(2,1)S(1)}, bf16[32,4224]{1,0:T(8,128)(2,1)S(1)}, u32[]{:S(2)}, u32[]{:S(2)}) %collective-permute-start.9) | collective-permute-done | bytes 270368 | tf_op jit(solution)/shard_map/ppermute | solution.py:226
  42.6 1.5 %collective-permute-start.13 = (bf16[32,4224]{1,0:T(8,128)(2,1)S(1)}, bf16[32,4224]{1,0:T(8,128)(2,1)S(1)}, u32[]{:S(2)}, u32[]{:S(2)}) collective-permute-start(bf16[32,4224]{1,0:T(8,128)(2,1)S(1)} %pad_maximum_fusion.4.refs_2_), channel_id=1, source_target_pairs={{0,8},{8,0},{16,24},{24,16},{1,9},{9,1},{17,25},{25,17},{2,10},{10... | collective-permute-start | bytes 811016 | tf_op jit(solution)/shard_map/ppermute | solution.py:20
  44.5 3.1 %expert_layer.3 = (bf16[32,4096]{1,0:T(8,128)(2,1)S(1)}, bf16[32,4096]{1,0:T(8,128)(2,1)S(1)}, bf16[32,4096]{1,0:T(8,128)(2,1)S(1)}, bf16[32,4096]{1,0:T(8,128)(2,1)S(1)}) custom-call(s32[1]{0:T(128)} %bitcast.own_expert, bf16[32,4224]{1,0:T(8,128)(2,1)S(1)} %pad_maximum_fusion.1.refs_0_, bf16[32,4224]{1,0:T(8,128)(2,1)S(1)} %collective-permute-done.4.refs_1_, ...), custom_call_target="tpu_custom_call" | custom-call | flops 2415919104 | bytes 20971520 | tf_op jit(solution)/shard_map/expert_layer/pallas_call | solution.py:205
  47.7 2.6 %collective-permute-done.12.refs_1_ = bf16[32,4224]{1,0:T(8,128)(2,1)S(1)} collective-permute-done((bf16[32,4224]{1,0:T(8,128)(2,1)S(1)}, bf16[32,4224]{1,0:T(8,128)(2,1)S(1)}, u32[]{:S(2)}, u32[]{:S(2)}) %collective-permute-start.12) | collective-permute-done | bytes 270368 | tf_op jit(solution)/shard_map/ppermute | solution.py:20
  50.6 1.5 %collective-permute-start.16 = (bf16[32,4224]{1,0:T(8,128)(2,1)S(1)}, bf16[32,4224]{1,0:T(8,128)(2,1)S(1)}, u32[]{:S(2)}, u32[]{:S(2)}) collective-permute-start(bf16[32,4224]{1,0:T(8,128)(2,1)S(1)} %pad_maximum_fusion.5.refs_2_), channel_id=1, source_target_pairs={{0,16},{16,0},{8,24},{24,8},{1,17},{17,1},{9,25},{25,9},{2,18},{18... | collective-permute-start | bytes 811016 | tf_op jit(solution)/shard_map/ppermute | solution.py:20
  52.6 3.1 %expert_layer.4 = (bf16[32,4096]{1,0:T(8,128)(2,1)S(1)}, bf16[32,4096]{1,0:T(8,128)(2,1)S(1)}, bf16[32,4096]{1,0:T(8,128)(2,1)S(1)}, bf16[32,4096]{1,0:T(8,128)(2,1)S(1)}) custom-call(s32[1]{0:T(128)} %bitcast.own_expert, bf16[32,4224]{1,0:T(8,128)(2,1)S(1)} %pad_maximum_fusion.3.refs_0_, bf16[32,4224]{1,0:T(8,128)(2,1)S(1)} %collective-permute-done.12.refs_1_, ...), custom_call_target="tpu_custom_call" | custom-call | flops 2415919104 | bytes 20971520 | tf_op jit(solution)/shard_map/expert_layer/pallas_call | solution.py:205
  57.1 1.5 %collective-permute-done.17.refs_5_ = bf16[32,4224]{1,0:T(8,128)(2,1)S(1)} collective-permute-done((bf16[32,4224]{1,0:T(8,128)(2,1)S(1)}, bf16[32,4224]{1,0:T(8,128)(2,1)S(1)}, u32[]{:S(2)}, u32[]{:S(2)}) %collective-permute-start.17) | collective-permute-done | bytes 270368 | tf_op jit(solution)/shard_map/ppermute | solution.py:20
  58.6 3.6 %collective-permute-done.18.refs_1_ = bf16[96,4224]{1,0:T(8,128)(2,1)S(1)} collective-permute-done((bf16[96,4224]{1,0:T(8,128)(2,1)S(1)}, bf16[96,4224]{1,0:T(8,128)(2,1)S(1)}, u32[]{:S(2)}, u32[]{:S(2)}) %collective-permute-start.18) | collective-permute-done | bytes 811040 | tf_op jit(solution)/shard_map/ppermute | solution.py:226
  62.1 5.7 %expert_layer.5 = (bf16[128,4096]{1,0:T(8,128)(2,1)S(1)}, bf16[32,4096]{1,0:T(8,128)(2,1)S(1)}, bf16[32,4096]{1,0:T(8,128)(2,1)S(1)}, bf16[32,4096]{1,0:T(8,128)(2,1)S(1)}, bf16[32,4096]{1,0:T(8,128)(2,1)S(1)}) custom-call(s32[1]{0:T(128)} %bitcast.own_expert, bf16[32,4224]{1,0:T(8,128)(2,1)S(1)} %collective-permute-done.2.refs_0_, ...), custom_call_target="tpu_custom_call" | custom-call | flops 4831838208 | bytes 23068672 | tf_op jit(solution)/shard_map/expert_layer/pallas_call | solution.py:205
  69.1 1.4 %collective-permute-start.19 = (bf16[32,4096]{1,0:T(8,128)(2,1)S(1)}, bf16[32,4096]{1,0:T(8,128)(2,1)S(1)}, u32[]{:S(2)}, u32[]{:S(2)}) collective-permute-start(bf16[32,4096]{1,0:T(8,128)(2,1)S(1)} %get-tuple-element.123), channel_id=1, source_target_pairs={{0,16},{16,0},{8,24},{24,8},{1,17},{17,1},{9,25},{25,9},{2,18},{18... | collective-permute-start | bytes 786440 | tf_op jit(solution)/shard_map/ppermute | solution.py:20
  70.5 1.5 %collective-permute-start.21 = (bf16[32,4096]{1,0:T(8,128)(2,1)S(1)}, bf16[32,4096]{1,0:T(8,128)(2,1)S(1)}, u32[]{:S(2)}, u32[]{:S(2)}) collective-permute-start(bf16[32,4096]{1,0:T(8,128)(2,1)S(1)} %get-tuple-element.125), channel_id=1, source_target_pairs={{0,8},{8,0},{16,24},{24,16},{1,9},{9,1},{17,25},{25,17},{2,10},{10... | collective-permute-start | bytes 786440 | tf_op jit(solution)/shard_map/ppermute | solution.py:20
  72.6 4.6 %collective-permute-done.23 = bf16[32,4096]{1,0:T(8,128)(2,1)S(1)} collective-permute-done((bf16[32,4096]{1,0:T(8,128)(2,1)S(1)}, bf16[32,4096]{1,0:T(8,128)(2,1)S(1)}, u32[]{:S(2)}, u32[]{:S(2)}) %collective-permute-start.23) | collective-permute-done | bytes 262176 | tf_op jit(solution)/shard_map/ppermute | solution.py:20
  78.0 1.4 %collective-permute-start.26 = (bf16[16,4096]{1,0:T(8,128)(2,1)S(1)}, bf16[16,4096]{1,0:T(8,128)(2,1)S(1)}, u32[]{:S(2)}, u32[]{:S(2)}) collective-permute-start(bf16[16,4096]{1,0:T(8,128)(2,1)S(1)} %split.55), channel_id=1, source_target_pairs={{0,16},{16,0},{8,24},{24,8},{1,17},{17,1},{9,25},{25,9},{2,18},{18... | collective-permute-start | bytes 393224 | tf_op jit(solution)/shard_map/ppermute | solution.py:20
  79.4 2.2 %collective-permute-done.19 = bf16[32,4096]{1,0:T(8,128)(2,1)S(1)} collective-permute-done((bf16[32,4096]{1,0:T(8,128)(2,1)S(1)}, bf16[32,4096]{1,0:T(8,128)(2,1)S(1)}, u32[]{:S(2)}, u32[]{:S(2)}) %collective-permute-start.19) | collective-permute-done | bytes 262176 | tf_op jit(solution)/shard_map/ppermute | solution.py:20
  84.6 2.1 %collective-permute-done.20 = bf16[16,4096]{1,0:T(8,128)(2,1)S(1)} collective-permute-done((bf16[16,4096]{1,0:T(8,128)(2,1)S(1)}, bf16[16,4096]{1,0:T(8,128)(2,1)S(1)}, u32[]{:S(2)}, u32[]{:S(2)}) %collective-permute-start.20) | collective-permute-done | bytes 131104 | tf_op jit(solution)/shard_map/ppermute | solution.py:20
  87.2 12.8 %collective-permute-done.27 = bf16[32,4096]{1,0:T(8,128)(2,1)S(1)} collective-permute-done((bf16[32,4096]{1,0:T(8,128)(2,1)S(1)}, bf16[32,4096]{1,0:T(8,128)(2,1)S(1)}, u32[]{:S(2)}, u32[]{:S(2)}) %collective-permute-start.27) | collective-permute-done | bytes 262176 | tf_op jit(solution)/shard_map/ppermute | solution.py:226
  101.2 6.6 %collective-permute-done.30 = bf16[32,4096]{1,0:T(8,128)(2,1)S(1)} collective-permute-done((bf16[32,4096]{1,0:T(8,128)(2,1)S(1)}, bf16[32,4096]{1,0:T(8,128)(2,1)S(1)}, u32[]{:S(2)}, u32[]{:S(2)}) %collective-permute-start.30) | collective-permute-done | bytes 262176 | tf_op jit(solution)/shard_map/ppermute | solution.py:20
  108.1 2.0 %collective-permute-done.31 = bf16[16,4096]{1,0:T(8,128)(2,1)S(1)} collective-permute-done((bf16[16,4096]{1,0:T(8,128)(2,1)S(1)}, bf16[16,4096]{1,0:T(8,128)(2,1)S(1)}, u32[]{:S(2)}, u32[]{:S(2)}) %collective-permute-start.31) | collective-permute-done | bytes 131104 | tf_op jit(solution)/shard_map/ppermute | solution.py:226
  110.8 1.9 %collective-permute-start.32 = (bf16[16,4096]{1,0:T(8,128)(2,1)S(1)}, bf16[16,4096]{1,0:T(8,128)(2,1)S(1)}, u32[]{:S(2)}, u32[]{:S(2)}) collective-permute-start(bf16[16,4096]{1,0:T(8,128)(2,1)S(1)} %split.45), channel_id=1, source_target_pairs={{0,8},{8,0},{16,24},{24,16},{1,9},{9,1},{17,25},{25,17},{2,10},{10... | collective-permute-start | bytes 393224 | tf_op jit(solution)/shard_map/ppermute | solution.py:20
  112.7 2.4 %collective-permute-done.33 = bf16[16,4096]{1,0:T(8,128)(2,1)S(1)} collective-permute-done((bf16[16,4096]{1,0:T(8,128)(2,1)S(1)}, bf16[16,4096]{1,0:T(8,128)(2,1)S(1)}, u32[]{:S(2)}, u32[]{:S(2)}) %collective-permute-start.33) | collective-permute-done | bytes 131104 | tf_op jit(solution)/shard_map/ppermute | solution.py:20
  115.8 2.8 %collective-permute-done.34 = bf16[16,4096]{1,0:T(8,128)(2,1)S(1)} collective-permute-done((bf16[16,4096]{1,0:T(8,128)(2,1)S(1)}, bf16[16,4096]{1,0:T(8,128)(2,1)S(1)}, u32[]{:S(2)}, u32[]{:S(2)}) %collective-permute-start.34) | collective-permute-done | bytes 131104 | tf_op jit(solution)/shard_map/ppermute | solution.py:226
  (101 shorter events, 21.9 us)
Async XLA Ops:
  2.0 16.2 %collective-permute-start.3 = (bf16[16,4224]{1,0:T(8,128)(2,1)S(1)}, bf16[16,4224]{1,0:T(8,128)(2,1)S(1)}, u32[]{:S(2)}, u32[]{:S(2)}) collective-permute-start(bf16[16,4224]{1,0:T(8,128)(2,1)S(1)} %concatenate.45), channel_id=1, source_target_pairs={{0,4},{1,5},{2,6},{3,7},{4,0},{5,1},{6,2},{7,3},{8,12},{9,13},{10,... | collective-permute-start | bytes 405512 | tf_op jit(solution)/shard_map/ppermute | solution.py:226
  6.1 12.1 %collective-permute-start = (bf16[16,4224]{1,0:T(8,128)(2,1)S(1)}, bf16[16,4224]{1,0:T(8,128)(2,1)S(1)}, u32[]{:S(2)}, u32[]{:S(2)}) collective-permute-start(bf16[16,4224]{1,0:T(8,128)(2,1)S(1)} %concatenate.45), channel_id=1, source_target_pairs={{0,8},{8,0},{16,24},{24,16},{1,9},{9,1},{17,25},{25,17},{2,10},{10... | collective-permute-start | bytes 405512 | tf_op jit(solution)/shard_map/ppermute | solution.py:20
  7.6 10.6 %collective-permute-start.1 = (bf16[16,4224]{1,0:T(8,128)(2,1)S(1)}, bf16[16,4224]{1,0:T(8,128)(2,1)S(1)}, u32[]{:S(2)}, u32[]{:S(2)}) collective-permute-start(bf16[16,4224]{1,0:T(8,128)(2,1)S(1)} %concatenate.46), channel_id=1, source_target_pairs={{0,16},{16,0},{8,24},{24,8},{1,17},{17,1},{9,25},{25,9},{2,18},{18... | collective-permute-start | bytes 405512 | tf_op jit(solution)/shard_map/ppermute | solution.py:20
  9.1 9.2 %collective-permute-start.2 = (bf16[32,4224]{1,0:T(8,128)(2,1)S(1)}, bf16[32,4224]{1,0:T(8,128)(2,1)S(1)}, u32[]{:S(2)}, u32[]{:S(2)}) collective-permute-start(bf16[32,4224]{1,0:T(8,128)(2,1)S(1)} %constant_dynamic-update-slice_fusion), channel_id=1, source_target_pairs={{0,2},{1,3},{2,0},{3,1},{4,6},{5,7},{6,4},{7,5},{8,10},{9,11},{10,... | collective-permute-start | bytes 811016 | tf_op jit(solution)/shard_map/ppermute | solution.py:226
  18.3 21.6 %collective-permute-start.10 = (bf16[4096,768]{1,0:T(8,128)(2,1)S(1)}, bf16[4096,768]{1,0:T(8,128)(2,1)S(1)}, u32[]{:S(2)}, u32[]{:S(2)}) collective-permute-start(bf16[4096,768]{1,0:T(8,128)(2,1)S(1)} %dequantize_in.1.refs_4_.refs_6_), channel_id=1, source_target_pairs={{0,1},{1,0},{2,3},{3,2},{4,5},{5,4},{6,7},{7,6},{8,9},{9,8},{10,11... | collective-permute-start | bytes 18874376 | tf_op jit(solution)/shard_map/ppermute | solution.py:20
  18.3 10.3 %collective-permute-start.4 = (bf16[32,4224]{1,0:T(8,128)(2,1)S(1)}, bf16[32,4224]{1,0:T(8,128)(2,1)S(1)}, u32[]{:S(2)}, u32[]{:S(2)}) collective-permute-start(bf16[32,4224]{1,0:T(8,128)(2,1)S(1)} %pad_maximum_fusion.1.refs_0_), channel_id=1, source_target_pairs={{0,16},{16,0},{8,24},{24,8},{1,17},{17,1},{9,25},{25,9},{2,18},{18... | collective-permute-start | bytes 811016 | tf_op jit(solution)/shard_map/ppermute | solution.py:20
  18.9 9.8 %collective-permute-start.5 = (bf16[32,4224]{1,0:T(8,128)(2,1)S(1)}, bf16[32,4224]{1,0:T(8,128)(2,1)S(1)}, u32[]{:S(2)}, u32[]{:S(2)}) collective-permute-start(bf16[32,4224]{1,0:T(8,128)(2,1)S(1)} %pad_maximum_fusion.2.refs_2_), channel_id=1, source_target_pairs={{0,8},{8,0},{16,24},{24,16},{1,9},{9,1},{17,25},{25,17},{2,10},{10... | collective-permute-start | bytes 811016 | tf_op jit(solution)/shard_map/ppermute | solution.py:20
  19.4 9.2 %collective-permute-start.6 = (bf16[16,4224]{1,0:T(8,128)(2,1)S(1)}, bf16[16,4224]{1,0:T(8,128)(2,1)S(1)}, u32[]{:S(2)}, u32[]{:S(2)}) collective-permute-start(bf16[16,4224]{1,0:T(8,128)(2,1)S(1)} %concatenate.46), channel_id=1, source_target_pairs={{0,4},{1,5},{2,6},{3,7},{4,0},{5,1},{6,2},{7,3},{8,12},{9,13},{10,... | collective-permute-start | bytes 405512 | tf_op jit(solution)/shard_map/ppermute | solution.py:226
  28.6 11.3 %collective-permute-start.11 = (bf16[384,4096]{1,0:T(8,128)(2,1)S(1)}, bf16[384,4096]{1,0:T(8,128)(2,1)S(1)}, u32[]{:S(2)}, u32[]{:S(2)}) collective-permute-start(bf16[384,4096]{1,0:T(8,128)(2,1)S(1)} %dequantize_down.1.refs_6_.refs_8_), channel_id=1, source_target_pairs={{0,1},{1,0},{2,3},{3,2},{4,5},{5,4},{6,7},{7,6},{8,9},{9,8},{10,11... | collective-permute-start | bytes 9437192 | tf_op jit(solution)/shard_map/ppermute | solution.py:20
  28.7 6.0 %collective-permute-start.7 = (bf16[16,4224]{1,0:T(8,128)(2,1)S(1)}, bf16[16,4224]{1,0:T(8,128)(2,1)S(1)}, u32[]{:S(2)}, u32[]{:S(2)}) collective-permute-start(bf16[16,4224]{1,0:T(8,128)(2,1)S(1)} %collective-permute-done.3), channel_id=1, source_target_pairs={{0,8},{8,0},{16,24},{24,16},{1,9},{9,1},{17,25},{25,17},{2,10},{10... | collective-permute-start | bytes 405512 | tf_op jit(solution)/shard_map/ppermute | solution.py:20
  30.1 5.6 %collective-permute-start.8 = (bf16[16,4224]{1,0:T(8,128)(2,1)S(1)}, bf16[16,4224]{1,0:T(8,128)(2,1)S(1)}, u32[]{:S(2)}, u32[]{:S(2)}) collective-permute-start(bf16[16,4224]{1,0:T(8,128)(2,1)S(1)} %collective-permute-done.6), channel_id=1, source_target_pairs={{0,16},{16,0},{8,24},{24,8},{1,17},{17,1},{9,25},{25,9},{2,18},{18... | collective-permute-start | bytes 405512 | tf_op jit(solution)/shard_map/ppermute | solution.py:20
  31.6 8.3 %collective-permute-start.9 = (bf16[32,4224]{1,0:T(8,128)(2,1)S(1)}, bf16[32,4224]{1,0:T(8,128)(2,1)S(1)}, u32[]{:S(2)}, u32[]{:S(2)}) collective-permute-start(bf16[32,4224]{1,0:T(8,128)(2,1)S(1)} %constant_dynamic-update-slice_fusion.2), channel_id=1, source_target_pairs={{0,2},{1,3},{2,0},{3,1},{4,6},{5,7},{6,4},{7,5},{8,10},{9,11},{10,... | collective-permute-start | bytes 811016 | tf_op jit(solution)/shard_map/ppermute | solution.py:226
  40.0 7.6 %collective-permute-start.15 = (bf16[16,4224]{1,0:T(8,128)(2,1)S(1)}, bf16[16,4224]{1,0:T(8,128)(2,1)S(1)}, u32[]{:S(2)}, u32[]{:S(2)}) collective-permute-start(bf16[16,4224]{1,0:T(8,128)(2,1)S(1)} %get-tuple-element.161), channel_id=1, source_target_pairs={{0,16},{16,0},{8,24},{24,8},{1,17},{17,1},{9,25},{25,9},{2,18},{18... | collective-permute-start | bytes 405512 | tf_op jit(solution)/shard_map/ppermute | solution.py:20
  40.6 7.1 %collective-permute-start.14 = (bf16[16,4224]{1,0:T(8,128)(2,1)S(1)}, bf16[16,4224]{1,0:T(8,128)(2,1)S(1)}, u32[]{:S(2)}, u32[]{:S(2)}) collective-permute-start(bf16[16,4224]{1,0:T(8,128)(2,1)S(1)} %get-tuple-element.162), channel_id=1, source_target_pairs={{0,8},{8,0},{16,24},{24,16},{1,9},{9,1},{17,25},{25,17},{2,10},{10... | collective-permute-start | bytes 405512 | tf_op jit(solution)/shard_map/ppermute | solution.py:20
  41.3 9.1 %collective-permute-start.12 = (bf16[32,4224]{1,0:T(8,128)(2,1)S(1)}, bf16[32,4224]{1,0:T(8,128)(2,1)S(1)}, u32[]{:S(2)}, u32[]{:S(2)}) collective-permute-start(bf16[32,4224]{1,0:T(8,128)(2,1)S(1)} %pad_maximum_fusion.3.refs_0_), channel_id=1, source_target_pairs={{0,16},{16,0},{8,24},{24,8},{1,17},{17,1},{9,25},{25,9},{2,18},{18... | collective-permute-start | bytes 811016 | tf_op jit(solution)/shard_map/ppermute | solution.py:20
  42.6 8.0 %collective-permute-start.13 = (bf16[32,4224]{1,0:T(8,128)(2,1)S(1)}, bf16[32,4224]{1,0:T(8,128)(2,1)S(1)}, u32[]{:S(2)}, u32[]{:S(2)}) collective-permute-start(bf16[32,4224]{1,0:T(8,128)(2,1)S(1)} %pad_maximum_fusion.4.refs_2_), channel_id=1, source_target_pairs={{0,8},{8,0},{16,24},{24,16},{1,9},{9,1},{17,25},{25,17},{2,10},{10... | collective-permute-start | bytes 811016 | tf_op jit(solution)/shard_map/ppermute | solution.py:20
  44.2 17.9 %collective-permute-start.18 = (bf16[96,4224]{1,0:T(8,128)(2,1)S(1)}, bf16[96,4224]{1,0:T(8,128)(2,1)S(1)}, u32[]{:S(2)}, u32[]{:S(2)}) collective-permute-start(bf16[96,4224]{1,0:T(8,128)(2,1)S(1)} %pad_maximum_fusion), channel_id=1, source_target_pairs={{0,2},{1,3},{2,0},{3,1},{4,6},{5,7},{6,4},{7,5},{8,10},{9,11},{10,... | collective-permute-start | bytes 2433032 | tf_op jit(solution)/shard_map/ppermute | solution.py:226
  50.6 6.5 %collective-permute-start.16 = (bf16[32,4224]{1,0:T(8,128)(2,1)S(1)}, bf16[32,4224]{1,0:T(8,128)(2,1)S(1)}, u32[]{:S(2)}, u32[]{:S(2)}) collective-permute-start(bf16[32,4224]{1,0:T(8,128)(2,1)S(1)} %pad_maximum_fusion.5.refs_2_), channel_id=1, source_target_pairs={{0,16},{16,0},{8,24},{24,8},{1,17},{17,1},{9,25},{25,9},{2,18},{18... | collective-permute-start | bytes 811016 | tf_op jit(solution)/shard_map/ppermute | solution.py:20
  52.1 6.5 %collective-permute-start.17 = (bf16[32,4224]{1,0:T(8,128)(2,1)S(1)}, bf16[32,4224]{1,0:T(8,128)(2,1)S(1)}, u32[]{:S(2)}, u32[]{:S(2)}) collective-permute-start(bf16[32,4224]{1,0:T(8,128)(2,1)S(1)} %pad_maximum_fusion.6.refs_4_), channel_id=1, source_target_pairs={{0,8},{8,0},{16,24},{24,16},{1,9},{9,1},{17,25},{25,17},{2,10},{10... | collective-permute-start | bytes 811016 | tf_op jit(solution)/shard_map/ppermute | solution.py:20
  67.9 9.3 %collective-permute-start.23 = (bf16[32,4096]{1,0:T(8,128)(2,1)S(1)}, bf16[32,4096]{1,0:T(8,128)(2,1)S(1)}, u32[]{:S(2)}, u32[]{:S(2)}) collective-permute-start(bf16[32,4096]{1,0:T(8,128)(2,1)S(1)} %get-tuple-element.137), channel_id=1, source_target_pairs={{0,16},{16,0},{8,24},{24,8},{1,17},{17,1},{9,25},{25,9},{2,18},{18... | collective-permute-start | bytes 786440 | tf_op jit(solution)/shard_map/ppermute | solution.py:20
  68.5 9.4 %collective-permute-start.25 = (bf16[32,4096]{1,0:T(8,128)(2,1)S(1)}, bf16[32,4096]{1,0:T(8,128)(2,1)S(1)}, u32[]{:S(2)}, u32[]{:S(2)}) collective-permute-start(bf16[32,4096]{1,0:T(8,128)(2,1)S(1)} %get-tuple-element.139), channel_id=1, source_target_pairs={{0,8},{8,0},{16,24},{24,16},{1,9},{9,1},{17,25},{25,17},{2,10},{10... | collective-permute-start | bytes 786440 | tf_op jit(solution)/shard_map/ppermute | solution.py:20
  69.1 12.4 %collective-permute-start.19 = (bf16[32,4096]{1,0:T(8,128)(2,1)S(1)}, bf16[32,4096]{1,0:T(8,128)(2,1)S(1)}, u32[]{:S(2)}, u32[]{:S(2)}) collective-permute-start(bf16[32,4096]{1,0:T(8,128)(2,1)S(1)} %get-tuple-element.123), channel_id=1, source_target_pairs={{0,16},{16,0},{8,24},{24,8},{1,17},{17,1},{9,25},{25,9},{2,18},{18... | collective-permute-start | bytes 786440 | tf_op jit(solution)/shard_map/ppermute | solution.py:20
  70.5 11.5 %collective-permute-start.21 = (bf16[32,4096]{1,0:T(8,128)(2,1)S(1)}, bf16[32,4096]{1,0:T(8,128)(2,1)S(1)}, u32[]{:S(2)}, u32[]{:S(2)}) collective-permute-start(bf16[32,4096]{1,0:T(8,128)(2,1)S(1)} %get-tuple-element.125), channel_id=1, source_target_pairs={{0,8},{8,0},{16,24},{24,16},{1,9},{9,1},{17,25},{25,17},{2,10},{10... | collective-permute-start | bytes 786440 | tf_op jit(solution)/shard_map/ppermute | solution.py:20
  72.0 27.9 %collective-permute-start.28 = (bf16[128,4096]{1,0:T(8,128)(2,1)S(1)}, bf16[128,4096]{1,0:T(8,128)(2,1)S(1)}, u32[]{:S(2)}, u32[]{:S(2)}) collective-permute-start(bf16[128,4096]{1,0:T(8,128)(2,1)S(1)} %get-tuple-element.140), channel_id=1, source_target_pairs={{0,2},{1,3},{2,0},{3,1},{4,6},{5,7},{6,4},{7,5},{8,10},{9,11},{10,... | collective-permute-start | bytes 3145736 | tf_op jit(solution)/shard_map/ppermute | solution.py:226
  77.3 6.2 %collective-permute-start.24 = (bf16[16,4096]{1,0:T(8,128)(2,1)S(1)}, bf16[16,4096]{1,0:T(8,128)(2,1)S(1)}, u32[]{:S(2)}, u32[]{:S(2)}) collective-permute-start(bf16[16,4096]{1,0:T(8,128)(2,1)S(1)} %split.53), channel_id=1, source_target_pairs={{0,8},{8,0},{16,24},{24,16},{1,9},{9,1},{17,25},{25,17},{2,10},{10... | collective-permute-start | bytes 393224 | tf_op jit(solution)/shard_map/ppermute | solution.py:20
  78.0 5.5 %collective-permute-start.26 = (bf16[16,4096]{1,0:T(8,128)(2,1)S(1)}, bf16[16,4096]{1,0:T(8,128)(2,1)S(1)}, u32[]{:S(2)}, u32[]{:S(2)}) collective-permute-start(bf16[16,4096]{1,0:T(8,128)(2,1)S(1)} %split.55), channel_id=1, source_target_pairs={{0,16},{16,0},{8,24},{24,8},{1,17},{17,1},{9,25},{25,9},{2,18},{18... | collective-permute-start | bytes 393224 | tf_op jit(solution)/shard_map/ppermute | solution.py:20
  82.1 5.0 %collective-permute-start.22 = (bf16[16,4096]{1,0:T(8,128)(2,1)S(1)}, bf16[16,4096]{1,0:T(8,128)(2,1)S(1)}, u32[]{:S(2)}, u32[]{:S(2)}) collective-permute-start(bf16[16,4096]{1,0:T(8,128)(2,1)S(1)} %split.51), channel_id=1, source_target_pairs={{0,16},{16,0},{8,24},{24,8},{1,17},{17,1},{9,25},{25,9},{2,18},{18... | collective-permute-start | bytes 393224 | tf_op jit(solution)/shard_map/ppermute | solution.py:20
  83.6 16.4 %collective-permute-start.27 = (bf16[32,4096]{1,0:T(8,128)(2,1)S(1)}, bf16[32,4096]{1,0:T(8,128)(2,1)S(1)}, u32[]{:S(2)}, u32[]{:S(2)}) collective-permute-start(bf16[32,4096]{1,0:T(8,128)(2,1)S(1)} %pad_maximum_fusion.7), channel_id=1, source_target_pairs={{0,2},{1,3},{2,0},{3,1},{4,6},{5,7},{6,4},{7,5},{8,10},{9,11},{10,... | collective-permute-start | bytes 786440 | tf_op jit(solution)/shard_map/ppermute | solution.py:226
  100.1 7.7 %collective-permute-start.30 = (bf16[32,4096]{1,0:T(8,128)(2,1)S(1)}, bf16[32,4096]{1,0:T(8,128)(2,1)S(1)}, u32[]{:S(2)}, u32[]{:S(2)}) collective-permute-start(bf16[32,4096]{1,0:T(8,128)(2,1)S(1)} %get-tuple-element.159), channel_id=1, source_target_pairs={{0,8},{8,0},{16,24},{24,16},{1,9},{9,1},{17,25},{25,17},{2,10},{10... | collective-permute-start | bytes 786440 | tf_op jit(solution)/shard_map/ppermute | solution.py:20
  100.3 9.7 %collective-permute-start.31 = (bf16[16,4096]{1,0:T(8,128)(2,1)S(1)}, bf16[16,4096]{1,0:T(8,128)(2,1)S(1)}, u32[]{:S(2)}, u32[]{:S(2)}) collective-permute-start(bf16[16,4096]{1,0:T(8,128)(2,1)S(1)} %get-tuple-element.166), channel_id=1, source_target_pairs={{0,4},{1,5},{2,6},{3,7},{4,0},{5,1},{6,2},{7,3},{8,12},{9,13},{10,... | collective-permute-start | bytes 393224 | tf_op jit(solution)/shard_map/ppermute | solution.py:226
  100.5 7.4 %collective-permute-start.29 = (bf16[32,4096]{1,0:T(8,128)(2,1)S(1)}, bf16[32,4096]{1,0:T(8,128)(2,1)S(1)}, u32[]{:S(2)}, u32[]{:S(2)}) collective-permute-start(bf16[32,4096]{1,0:T(8,128)(2,1)S(1)} %get-tuple-element.160), channel_id=1, source_target_pairs={{0,16},{16,0},{8,24},{24,8},{1,17},{17,1},{9,25},{25,9},{2,18},{18... | collective-permute-start | bytes 786440 | tf_op jit(solution)/shard_map/ppermute | solution.py:20
  112.7 5.9 %collective-permute-start.34 = (bf16[16,4096]{1,0:T(8,128)(2,1)S(1)}, bf16[16,4096]{1,0:T(8,128)(2,1)S(1)}, u32[]{:S(2)}, u32[]{:S(2)}) collective-permute-start(bf16[16,4096]{1,0:T(8,128)(2,1)S(1)} %get-tuple-element.152), channel_id=1, source_target_pairs={{0,4},{1,5},{2,6},{3,7},{4,0},{5,1},{6,2},{7,3},{8,12},{9,13},{10,... | collective-permute-start | bytes 393224 | tf_op jit(solution)/shard_map/ppermute | solution.py:226
  (9 other events, 61.5 us)

commit v12 on v10

--- a/solution.py
+++ b/solution.py
@@ -218,6 +218,38 @@
     )(own_expert, *pieces, *weights)
 
 
+def payload_kernel(expert_count, tokens, ids, vals, *outs):
+    token_count, model_width = tokens.shape
+    extra = outs[0].shape[1] - model_width
+    column = lax.broadcasted_iota(jnp.int32, (token_count, extra), 1)
+    weight = jnp.zeros((token_count, extra), jnp.float32)
+    for choice in range(ids.shape[1]):
+        expert = ids[:, choice : choice + 1]
+        named = (column == expert) | (column == expert + expert_count)
+        weight += jnp.where(named, vals[:, choice : choice + 1], 0.0)
+    high = weight.astype(jnp.bfloat16).astype(jnp.float32)
+    marks = jnp.where(column < expert_count, high, weight - high).astype(jnp.bfloat16)
+    half = token_count // 2
+    for place, out in enumerate(outs):
+        rows = slice(place * half, (place + 1) * half)
+        out[:, :model_width] = tokens[rows, :]
+        out[:, model_width:] = marks[rows]
+
+
+def build_payload(tokens, ids, vals, expert_count):
+    token_count, model_width = tokens.shape
+    width = model_width + -(-2 * expert_count // BLOCK) * BLOCK
+    whole = pl.BlockSpec(memory_space=pltpu.VMEM)
+    return pl.pallas_call(
+        functools.partial(payload_kernel, expert_count),
+        in_specs=[whole] * 3,
+        out_specs=[whole] * 2,
+        out_shape=[jax.ShapeDtypeStruct((token_count // 2, width), jnp.bfloat16)] * 2,
+        compiler_params=pltpu.CompilerParams(vmem_limit_bytes=4 * 1024 * 1024),
+        name="build_payload",
+    )(tokens, ids, vals)
+
+
 def across_chips(block, far):
     count = lax.axis_size("expert")
     return lax.ppermute(block, "expert", [(low, low ^ 2 * far) for low in range(count)])
@@ -232,18 +264,9 @@
     bits = list(range(group_count.bit_length() - 1))
     orders = (bits, bits[::-1])
 
-    named = expert_ids[:, :, None] == jnp.arange(expert_count, dtype=jnp.int32)[None, None, :]
-    weight = jnp.sum(jnp.where(named, gate_vals[:, :, None], 0.0), axis=1)
-    high = weight.astype(jnp.bfloat16)
-    low = (weight - high.astype(jnp.float32)).astype(jnp.bfloat16)
-    extra = -(-2 * expert_count // BLOCK) * BLOCK
-    pad = jnp.zeros((token_count, extra - 2 * expert_count), jnp.bfloat16)
     half = token_count // 2
     halves = [slice(0, half), slice(half, token_count)]
-    payload = [
-        jnp.concatenate([part[rows] for part in (tokens, high, low, pad)], axis=1)
-        for rows in halves
-    ]
+    payload = build_payload(tokens, expert_ids, gate_vals, expert_count)
 
     together = lax.optimization_barrier
     place = jnp.reshape(own_expert, (1,)).astype(jnp.int32)
@@ -329,33 +352,24 @@
                 came_back = across_chips(block, low)
                 into = far ^ low
                 merged[into] = added(merged[into], came_back) if into in merged else came_back
-            elif number > 1:
+            else:
                 whole = across_chips(block, low)
                 parts.append([whole[rows] for rows in halves])
-            else:
-                leaving[far] = [block[rows] for rows in halves]
-
-    sums, merged, parts, leaving = {}, {}, [], {}
+
+    sums, merged, parts = {}, {}, []
     for number in range(final, 0, -1):
         for turn in range(turns - 1 - int(number < final), -1, -1):
             sum_turn(number, turn)
             if turn == 0 and number > 1:
                 sum_turn(number - 1, turns - 1)
-            if turn == 0 and number > 1:
-                leave(number)
-            sums, outs, merged = together((sums, outs, merged))
-    leave(1)
-    back = [{far: across_chips(leaving[far][0], far) for far in groups[1]}]
-    for turn in range(turns - 1, 0, -1):
+        leave(number)
+    for turn in range(turns - 1, -1, -1):
         sum_turn(0, turn)
-    sums, back, leaving = together((sums, back, leaving))
-    back.append({far: across_chips(leaving[far][1], far) for far in groups[1]})
-    sum_turn(0, 0)
     result = []
     for lane, rows in enumerate(halves):
         total = tokens[rows].astype(jnp.float32) + sums[0][lane].astype(jnp.float32)
-        for part in [*back[lane].values(), *(part[lane] for part in parts)]:
-            total = total + part.astype(jnp.float32)
+        for part in parts:
+            total = total + part[lane].astype(jnp.float32)
         result.append(total.astype(jnp.bfloat16))
     return jnp.concatenate(result, axis=0)
 

time: 118 us -> 127 us (1.076)
  waiting for transfers between devices: 55.4 us -> 69.5 us
  starting transfers between devices: 39.8 us -> 32.8 us
  local copies, waits for them, and re-layouts: 4.33 us -> 6.19 us
    ppermute x10 -> x8, waiting for transfers between devices: 10.7 us -> 20 us  [across_chips(): lax.ppermute(block, 'expert', [(low, low ^ 2 * far) for low in range(coun...]
    ppermute x10 -> x8, starting transfers between devices: 12.6 us -> 7.55 us  [across_chips(): lax.ppermute(block, 'expert', [(low, low ^ 2 * far) for low in range(coun...]
    ppermute x26, waiting for transfers between devices: 44.7 us -> 49.5 us  [from_partner(): return lax.ppermute(block, axis, route)]
    unnamed x17 -> x19, local copies, waits for them, and re-layouts: 2.9 us -> 6.05 us
    ppermute x26, starting transfers between devices: 27.2 us -> 25.3 us  [from_partner(): return lax.ppermute(block, axis, route)]
  transfers between devices with their start and end apart: 36 -> 34, of which waited for: 19 -> 13; matrix products, arithmetic and copies ran while one was open for 1% -> 1% of each run, Pallas kernels for 11% -> 12%
where the time goes in v12:
time: 127 us
  waiting for transfers between devices  69.5 us (55%)
  starting transfers between devices  32.8 us (26%)
  Pallas kernels  15.9 us (13%)
  local copies, waits for them, and re-layouts  6.19 us (5%)
  other arithmetic  1.82 us (1%)
    ppermute x26, waiting for transfers between devices, from_partner(): return lax.ppermute(block, axis, route)  49.5 us
    ppermute x26, starting transfers between devices, from_partner(): return lax.ppermute(block, axis, route)  25.3 us
    ppermute x8, waiting for transfers between devices, across_chips(): lax.ppermute(block, 'expert', [(low, low ^ 2 * far) for low in range(coun...  20 us
    pallas_call x3, Pallas kernels, expert_layer(): pl.pallas_call(functools.partial(expert_kernel, count, experts), in_specs...  12 us
    ppermute x8, starting transfers between devices, across_chips(): lax.ppermute(block, 'expert', [(low, low ^ 2 * far) for low in range(coun...  7.55 us
    unnamed x19, local copies, waits for them, and re-layouts  6.05 us
  transfers between devices with their start and end apart: 34, of which 13 were waited for; matrix products, arithmetic and copies ran while one was open for 1% of the time, Pallas kernels for 12%

profile of v12, /device:TPU:0, one launch (start us, length us, event | category | flops | bytes accessed | tf_op | source)
XLA Modules:
  0.0 126.6 jit_solution(14305338316972402215)
XLA Ops:
  2.7 4.1 %collective-permute-start.3 = (bf16[16,4224]{1,0:T(8,128)(2,1)S(1)}, bf16[16,4224]{1,0:T(8,128)(2,1)S(1)}, u32[]{:S(2)}, u32[]{:S(2)}) collective-permute-start(bf16[16,4224]{1,0:T(8,128)(2,1)S(1)} %get-tuple-element.71), channel_id=1, source_target_pairs={{0,4},{1,5},{2,6},{3,7},{4,0},{5,1},{6,2},{7,3},{8,12},{9,13},{10,... | collective-permute-start | bytes 405512 | tf_op jit(solution)/shard_map/ppermute | solution.py:255
  6.8 1.6 %collective-permute-start.2 = (bf16[16,4224]{1,0:T(8,128)(2,1)S(1)}, bf16[16,4224]{1,0:T(8,128)(2,1)S(1)}, u32[]{:S(2)}, u32[]{:S(2)}) collective-permute-start(bf16[16,4224]{1,0:T(8,128)(2,1)S(1)} %get-tuple-element.71), channel_id=1, source_target_pairs={{0,2},{1,3},{2,0},{3,1},{4,6},{5,7},{6,4},{7,5},{8,10},{9,11},{10,... | collective-permute-start | bytes 405512 | tf_op jit(solution)/shard_map/ppermute | solution.py:255
  8.3 1.5 %collective-permute-start = (bf16[16,4224]{1,0:T(8,128)(2,1)S(1)}, bf16[16,4224]{1,0:T(8,128)(2,1)S(1)}, u32[]{:S(2)}, u32[]{:S(2)}) collective-permute-start(bf16[16,4224]{1,0:T(8,128)(2,1)S(1)} %get-tuple-element.71), channel_id=1, source_target_pairs={{0,8},{8,0},{16,24},{24,16},{1,9},{9,1},{17,25},{25,17},{2,10},{10... | collective-permute-start | bytes 405512 | tf_op jit(solution)/shard_map/ppermute | solution.py:20
  9.8 1.5 %collective-permute-start.1 = (bf16[16,4224]{1,0:T(8,128)(2,1)S(1)}, bf16[16,4224]{1,0:T(8,128)(2,1)S(1)}, u32[]{:S(2)}, u32[]{:S(2)}) collective-permute-start(bf16[16,4224]{1,0:T(8,128)(2,1)S(1)} %get-tuple-element.77), channel_id=1, source_target_pairs={{0,16},{16,0},{8,24},{24,8},{1,17},{17,1},{9,25},{25,9},{2,18},{18... | collective-permute-start | bytes 405512 | tf_op jit(solution)/shard_map/ppermute | solution.py:20
  12.0 1.9 %copy-done = bf16[1,384,4096]{2,1,0:T(8,128)(2,1)S(1)} copy-done((bf16[1,384,4096]{2,1,0:T(8,128)(2,1)S(1)}, bf16[1,384,4096]{2,1,0:T(8,128)(2,1)}, u32[]{:S(2)}) %copy-start) | copy-done | bytes 3145752
  13.9 1.8 %dequantize_down.1.refs_6_ = bf16[384,4096]{1,0:T(8,128)(2,1)S(1)} custom-call(f32[3,32]{1,0:T(4,128)S(1)} %bitcast.18, bf16[384,4096]{1,0:T(8,128)(2,1)S(1)} %bitcast.15), custom_call_target="tpu_custom_call" | custom-call | flops 1572864 | bytes 6291456 | tf_op jit(solution)/shard_map/dequantize_down/pallas_call | solution.py:148
  16.8 1.9 %dequantize_in.1.refs_4_ = bf16[4096,768]{1,0:T(8,128)(2,1)S(1)} custom-call(f32[3,32]{1,0:T(4,128)S(1)} %get-tuple-element.138.gate_scales, f32[3,32]{1,0:T(4,128)S(1)} %get-tuple-element.137.up_scales, bf16[4096,384]{1,0:T(8,128)(2,1)S(1)} %bitcast.16, bf16[4096,384]{1,0:T(8,128)(2,1)S(1)} %bitcast.17), custom_call_target="tpu_custom_call" | custom-call | flops 3145728 | bytes 12582912 | tf_op jit(solution)/shard_map/dequantize_in/pallas_call | solution.py:120
  20.5 8.5 %collective-permute-done.7 = bf16[16,4224]{1,0:T(8,128)(2,1)S(1)} collective-permute-done((bf16[16,4224]{1,0:T(8,128)(2,1)S(1)}, bf16[16,4224]{1,0:T(8,128)(2,1)S(1)}, u32[]{:S(2)}, u32[]{:S(2)}) %collective-permute-start.7) | collective-permute-done | bytes 135200 | tf_op jit(solution)/shard_map/ppermute | solution.py:255
  29.3 1.6 %collective-permute-start.9 = (bf16[32,4224]{1,0:T(8,128)(2,1)S(1)}, bf16[32,4224]{1,0:T(8,128)(2,1)S(1)}, u32[]{:S(2)}, u32[]{:S(2)}) collective-permute-start(bf16[32,4224]{1,0:T(8,128)(2,1)S(1)} %constant_dynamic-update-slice_fusion.2), channel_id=1, source_target_pairs={{0,16},{16,0},{8,24},{24,8},{1,17},{17,1},{9,25},{25,9},{2,18},{18... | collective-permute-start | bytes 811016 | tf_op jit(solution)/shard_map/ppermute | solution.py:20
  30.9 1.6 %collective-permute-start.8 = (bf16[32,4224]{1,0:T(8,128)(2,1)S(1)}, bf16[32,4224]{1,0:T(8,128)(2,1)S(1)}, u32[]{:S(2)}, u32[]{:S(2)}) collective-permute-start(bf16[32,4224]{1,0:T(8,128)(2,1)S(1)} %constant_dynamic-update-slice_fusion), channel_id=1, source_target_pairs={{0,8},{8,0},{16,24},{24,16},{1,9},{9,1},{17,25},{25,17},{2,10},{10... | collective-permute-start | bytes 811016 | tf_op jit(solution)/shard_map/ppermute | solution.py:20
  32.5 5.8 %collective-permute-done.9 = bf16[32,4224]{1,0:T(8,128)(2,1)S(1)} collective-permute-done((bf16[32,4224]{1,0:T(8,128)(2,1)S(1)}, bf16[32,4224]{1,0:T(8,128)(2,1)S(1)}, u32[]{:S(2)}, u32[]{:S(2)}) %collective-permute-start.9) | collective-permute-done | bytes 270368 | tf_op jit(solution)/shard_map/ppermute | solution.py:20
  38.3 1.3 %collective-permute-done.8 = bf16[32,4224]{1,0:T(8,128)(2,1)S(1)} collective-permute-done((bf16[32,4224]{1,0:T(8,128)(2,1)S(1)}, bf16[32,4224]{1,0:T(8,128)(2,1)S(1)}, u32[]{:S(2)}, u32[]{:S(2)}) %collective-permute-start.8) | collective-permute-done | bytes 270368 | tf_op jit(solution)/shard_map/ppermute | solution.py:20
  40.2 1.5 %collective-permute-start.15 = (bf16[16,4224]{1,0:T(8,128)(2,1)S(1)}, bf16[16,4224]{1,0:T(8,128)(2,1)S(1)}, u32[]{:S(2)}, u32[]{:S(2)}) collective-permute-start(bf16[16,4224]{1,0:T(8,128)(2,1)S(1)} %get-tuple-element.136), channel_id=1, source_target_pairs={{0,8},{8,0},{16,24},{24,16},{1,9},{9,1},{17,25},{25,17},{2,10},{10... | collective-permute-start | bytes 405512 | tf_op jit(solution)/shard_map/ppermute | solution.py:20
  41.7 1.5 %collective-permute-start.13 = (bf16[64,4224]{1,0:T(8,128)(2,1)S(1)}, bf16[64,4224]{1,0:T(8,128)(2,1)S(1)}, u32[]{:S(2)}, u32[]{:S(2)}) collective-permute-start(bf16[64,4224]{1,0:T(8,128)(2,1)S(1)} %pad_maximum_fusion.refs_0_), channel_id=1, source_target_pairs={{0,16},{16,0},{8,24},{24,8},{1,17},{17,1},{9,25},{25,9},{2,18},{18... | collective-permute-start | bytes 1622024 | tf_op jit(solution)/shard_map/ppermute | solution.py:20
  43.8 3.1 %expert_layer.3 = (bf16[32,4096]{1,0:T(8,128)(2,1)S(1)}, bf16[32,4096]{1,0:T(8,128)(2,1)S(1)}, bf16[32,4096]{1,0:T(8,128)(2,1)S(1)}, bf16[32,4096]{1,0:T(8,128)(2,1)S(1)}) custom-call(s32[1]{0:T(128)} %bitcast.own_expert, bf16[32,4224]{1,0:T(8,128)(2,1)S(1)} %pad_maximum_fusion.2.refs_0_, bf16[32,4224]{1,0:T(8,128)(2,1)S(1)} %collective-permute-done.4.refs_1_, ...), custom_call_target="tpu_custom_call" | custom-call | flops 2415919104 | bytes 20971520 | tf_op jit(solution)/shard_map/expert_layer/pallas_call | solution.py:202
  47.0 9.3 %collective-permute-done.13.refs_1_ = bf16[64,4224]{1,0:T(8,128)(2,1)S(1)} collective-permute-done((bf16[64,4224]{1,0:T(8,128)(2,1)S(1)}, bf16[64,4224]{1,0:T(8,128)(2,1)S(1)}, u32[]{:S(2)}, u32[]{:S(2)}) %collective-permute-start.13) | collective-permute-done | bytes 540704 | tf_op jit(solution)/shard_map/ppermute | solution.py:20
  56.8 1.2 collective-permute-start.17
  58.0 1.4 %collective-permute-start.18 = (bf16[32,4224]{1,0:T(8,128)(2,1)S(1)}, bf16[32,4224]{1,0:T(8,128)(2,1)S(1)}, u32[]{:S(2)}, u32[]{:S(2)}) collective-permute-start(bf16[32,4224]{1,0:T(8,128)(2,1)S(1)} %pad_maximum_fusion.5.refs_2_), channel_id=1, source_target_pairs={{0,8},{8,0},{16,24},{24,16},{1,9},{9,1},{17,25},{25,17},{2,10},{10... | collective-permute-start | bytes 811016 | tf_op jit(solution)/shard_map/ppermute | solution.py:20
  59.4 5.7 %expert_layer.4 = (bf16[64,4096]{1,0:T(8,128)(2,1)S(1)}, bf16[64,4096]{1,0:T(8,128)(2,1)S(1)}, bf16[64,4096]{1,0:T(8,128)(2,1)S(1)}, bf16[64,4096]{1,0:T(8,128)(2,1)S(1)}) custom-call(s32[1]{0:T(128)} %bitcast.own_expert, bf16[64,4224]{1,0:T(8,128)(2,1)S(1)} %pad_maximum_fusion.refs_0_, bf16[64,4224]{1,0:T(8,128)(2,1)S(1)} %collective-permute-done.13.refs_1_, ...), custom_call_target="tpu_custom_call" | custom-call | flops 4831838208 | bytes 23068672 | tf_op jit(solution)/shard_map/expert_layer/pallas_call | solution.py:202
  65.8 3.1 %expert_layer.5 = (bf16[32,4096]{1,0:T(8,128)(2,1)S(1)}, bf16[32,4096]{1,0:T(8,128)(2,1)S(1)}, bf16[32,4096]{1,0:T(8,128)(2,1)S(1)}, bf16[32,4096]{1,0:T(8,128)(2,1)S(1)}) custom-call(s32[1]{0:T(128)} %bitcast.own_expert, bf16[32,4224]{1,0:T(8,128)(2,1)S(1)} %pad_maximum_fusion.4.refs_0_, bf16[32,4224]{1,0:T(8,128)(2,1)S(1)} %collective-permute-done.17.refs_1_, ...), custom_call_target="tpu_custom_call" | custom-call | flops 2415919104 | bytes 20971520 | tf_op jit(solution)/shard_map/expert_layer/pallas_call | solution.py:202
  69.0 1.5 %collective-permute-start.23 = (bf16[32,4096]{1,0:T(8,128)(2,1)S(1)}, bf16[32,4096]{1,0:T(8,128)(2,1)S(1)}, u32[]{:S(2)}, u32[]{:S(2)}) collective-permute-start(bf16[32,4096]{1,0:T(8,128)(2,1)S(1)} %get-tuple-element.126), channel_id=1, source_target_pairs={{0,16},{16,0},{8,24},{24,8},{1,17},{17,1},{9,25},{25,9},{2,18},{18... | collective-permute-start | bytes 786440 | tf_op jit(solution)/shard_map/ppermute | solution.py:20
  71.1 1.4 %collective-permute-start.32 = (bf16[32,4096]{1,0:T(8,128)(2,1)S(1)}, bf16[32,4096]{1,0:T(8,128)(2,1)S(1)}, u32[]{:S(2)}, u32[]{:S(2)}) collective-permute-start(bf16[32,4096]{1,0:T(8,128)(2,1)S(1)} %get-tuple-element.132), channel_id=1, source_target_pairs={{0,8},{8,0},{16,24},{24,16},{1,9},{9,1},{17,25},{25,17},{2,10},{10... | collective-permute-start | bytes 786440 | tf_op jit(solution)/shard_map/ppermute | solution.py:20
  73.2 1.1 collective-permute-done.19
  74.3 5.5 %collective-permute-done.23 = bf16[32,4096]{1,0:T(8,128)(2,1)S(1)} collective-permute-done((bf16[32,4096]{1,0:T(8,128)(2,1)S(1)}, bf16[32,4096]{1,0:T(8,128)(2,1)S(1)}, u32[]{:S(2)}, u32[]{:S(2)}) %collective-permute-start.23) | collective-permute-done | bytes 262176 | tf_op jit(solution)/shard_map/ppermute | solution.py:20
  80.1 1.9 %collective-permute-start.24 = (bf16[16,4096]{1,0:T(8,128)(2,1)S(1)}, bf16[16,4096]{1,0:T(8,128)(2,1)S(1)}, u32[]{:S(2)}, u32[]{:S(2)}) collective-permute-start(bf16[16,4096]{1,0:T(8,128)(2,1)S(1)} %split.53), channel_id=1, source_target_pairs={{0,8},{8,0},{16,24},{24,16},{1,9},{9,1},{17,25},{25,17},{2,10},{10... | collective-permute-start | bytes 393224 | tf_op jit(solution)/shard_map/ppermute | solution.py:20
  82.1 16.1 %collective-permute-done.24 = bf16[16,4096]{1,0:T(8,128)(2,1)S(1)} collective-permute-done((bf16[16,4096]{1,0:T(8,128)(2,1)S(1)}, bf16[16,4096]{1,0:T(8,128)(2,1)S(1)}, u32[]{:S(2)}, u32[]{:S(2)}) %collective-permute-start.24) | collective-permute-done | bytes 131104 | tf_op jit(solution)/shard_map/ppermute | solution.py:20
  98.9 5.6 %collective-permute-done.26 = bf16[16,4096]{1,0:T(8,128)(2,1)S(1)} collective-permute-done((bf16[16,4096]{1,0:T(8,128)(2,1)S(1)}, bf16[16,4096]{1,0:T(8,128)(2,1)S(1)}, u32[]{:S(2)}, u32[]{:S(2)}) %collective-permute-start.26) | collective-permute-done | bytes 131104 | tf_op jit(solution)/shard_map/ppermute | solution.py:20
  104.6 1.0 collective-permute-start.27
  106.6 2.0 %collective-permute-start.30 = (bf16[32,4096]{1,0:T(8,128)(2,1)S(1)}, bf16[32,4096]{1,0:T(8,128)(2,1)S(1)}, u32[]{:S(2)}, u32[]{:S(2)}) collective-permute-start(bf16[32,4096]{1,0:T(8,128)(2,1)S(1)} %split.57), channel_id=1, source_target_pairs={{0,8},{8,0},{16,24},{24,16},{1,9},{9,1},{17,25},{25,17},{2,10},{10... | collective-permute-start | bytes 786440 | tf_op jit(solution)/shard_map/ppermute | solution.py:20
  108.6 7.6 %collective-permute-done.27 = bf16[32,4096]{1,0:T(8,128)(2,1)S(1)} collective-permute-done((bf16[32,4096]{1,0:T(8,128)(2,1)S(1)}, bf16[32,4096]{1,0:T(8,128)(2,1)S(1)}, u32[]{:S(2)}, u32[]{:S(2)}) %collective-permute-start.27) | collective-permute-done | bytes 262176 | tf_op jit(solution)/shard_map/ppermute | solution.py:255
  117.6 4.2 %collective-permute-done.33 = bf16[16,4096]{1,0:T(8,128)(2,1)S(1)} collective-permute-done((bf16[16,4096]{1,0:T(8,128)(2,1)S(1)}, bf16[16,4096]{1,0:T(8,128)(2,1)S(1)}, u32[]{:S(2)}, u32[]{:S(2)}) %collective-permute-start.33) | collective-permute-done | bytes 131104 | tf_op jit(solution)/shard_map/ppermute | solution.py:20
  121.8 3.7 %collective-permute-done.28 = bf16[32,4096]{1,0:T(8,128)(2,1)S(1)} collective-permute-done((bf16[32,4096]{1,0:T(8,128)(2,1)S(1)}, bf16[32,4096]{1,0:T(8,128)(2,1)S(1)}, u32[]{:S(2)}, u32[]{:S(2)}) %collective-permute-start.28) | collective-permute-done | bytes 262176 | tf_op jit(solution)/shard_map/ppermute | solution.py:255
  (90 shorter events, 14.7 us)
Async XLA Ops:
  2.7 16.1 %collective-permute-start.3 = (bf16[16,4224]{1,0:T(8,128)(2,1)S(1)}, bf16[16,4224]{1,0:T(8,128)(2,1)S(1)}, u32[]{:S(2)}, u32[]{:S(2)}) collective-permute-start(bf16[16,4224]{1,0:T(8,128)(2,1)S(1)} %get-tuple-element.71), channel_id=1, source_target_pairs={{0,4},{1,5},{2,6},{3,7},{4,0},{5,1},{6,2},{7,3},{8,12},{9,13},{10,... | collective-permute-start | bytes 405512 | tf_op jit(solution)/shard_map/ppermute | solution.py:255
  6.8 12.0 %collective-permute-start.2 = (bf16[16,4224]{1,0:T(8,128)(2,1)S(1)}, bf16[16,4224]{1,0:T(8,128)(2,1)S(1)}, u32[]{:S(2)}, u32[]{:S(2)}) collective-permute-start(bf16[16,4224]{1,0:T(8,128)(2,1)S(1)} %get-tuple-element.71), channel_id=1, source_target_pairs={{0,2},{1,3},{2,0},{3,1},{4,6},{5,7},{6,4},{7,5},{8,10},{9,11},{10,... | collective-permute-start | bytes 405512 | tf_op jit(solution)/shard_map/ppermute | solution.py:255
  8.3 10.4 %collective-permute-start = (bf16[16,4224]{1,0:T(8,128)(2,1)S(1)}, bf16[16,4224]{1,0:T(8,128)(2,1)S(1)}, u32[]{:S(2)}, u32[]{:S(2)}) collective-permute-start(bf16[16,4224]{1,0:T(8,128)(2,1)S(1)} %get-tuple-element.71), channel_id=1, source_target_pairs={{0,8},{8,0},{16,24},{24,16},{1,9},{9,1},{17,25},{25,17},{2,10},{10... | collective-permute-start | bytes 405512 | tf_op jit(solution)/shard_map/ppermute | solution.py:20
  9.8 8.9 %collective-permute-start.1 = (bf16[16,4224]{1,0:T(8,128)(2,1)S(1)}, bf16[16,4224]{1,0:T(8,128)(2,1)S(1)}, u32[]{:S(2)}, u32[]{:S(2)}) collective-permute-start(bf16[16,4224]{1,0:T(8,128)(2,1)S(1)} %get-tuple-element.77), channel_id=1, source_target_pairs={{0,16},{16,0},{8,24},{24,8},{1,17},{17,1},{9,25},{25,9},{2,18},{18... | collective-permute-start | bytes 405512 | tf_op jit(solution)/shard_map/ppermute | solution.py:20
  18.8 20.8 %collective-permute-start.11 = (bf16[4096,768]{1,0:T(8,128)(2,1)S(1)}, bf16[4096,768]{1,0:T(8,128)(2,1)S(1)}, u32[]{:S(2)}, u32[]{:S(2)}) collective-permute-start(bf16[4096,768]{1,0:T(8,128)(2,1)S(1)} %dequantize_in.1.refs_4_), channel_id=1, source_target_pairs={{0,1},{1,0},{2,3},{3,2},{4,5},{5,4},{6,7},{7,6},{8,9},{9,8},{10,11... | collective-permute-start | bytes 18874376 | tf_op jit(solution)/shard_map/ppermute | solution.py:20
  18.9 10.2 %collective-permute-start.4 = (bf16[32,4224]{1,0:T(8,128)(2,1)S(1)}, bf16[32,4224]{1,0:T(8,128)(2,1)S(1)}, u32[]{:S(2)}, u32[]{:S(2)}) collective-permute-start(bf16[32,4224]{1,0:T(8,128)(2,1)S(1)} %pad_maximum_fusion.2.refs_0_), channel_id=1, source_target_pairs={{0,16},{16,0},{8,24},{24,8},{1,17},{17,1},{9,25},{25,9},{2,18},{18... | collective-permute-start | bytes 811016 | tf_op jit(solution)/shard_map/ppermute | solution.py:20
  19.5 9.6 %collective-permute-start.5 = (bf16[32,4224]{1,0:T(8,128)(2,1)S(1)}, bf16[32,4224]{1,0:T(8,128)(2,1)S(1)}, u32[]{:S(2)}, u32[]{:S(2)}) collective-permute-start(bf16[32,4224]{1,0:T(8,128)(2,1)S(1)} %pad_maximum_fusion.3.refs_2_), channel_id=1, source_target_pairs={{0,8},{8,0},{16,24},{24,16},{1,9},{9,1},{17,25},{25,17},{2,10},{10... | collective-permute-start | bytes 811016 | tf_op jit(solution)/shard_map/ppermute | solution.py:20
  20.0 9.1 %collective-permute-start.7 = (bf16[16,4224]{1,0:T(8,128)(2,1)S(1)}, bf16[16,4224]{1,0:T(8,128)(2,1)S(1)}, u32[]{:S(2)}, u32[]{:S(2)}) collective-permute-start(bf16[16,4224]{1,0:T(8,128)(2,1)S(1)} %get-tuple-element.77), channel_id=1, source_target_pairs={{0,4},{1,5},{2,6},{3,7},{4,0},{5,1},{6,2},{7,3},{8,12},{9,13},{10,... | collective-permute-start | bytes 405512 | tf_op jit(solution)/shard_map/ppermute | solution.py:255
  20.3 8.7 %collective-permute-start.6 = (bf16[16,4224]{1,0:T(8,128)(2,1)S(1)}, bf16[16,4224]{1,0:T(8,128)(2,1)S(1)}, u32[]{:S(2)}, u32[]{:S(2)}) collective-permute-start(bf16[16,4224]{1,0:T(8,128)(2,1)S(1)} %get-tuple-element.77), channel_id=1, source_target_pairs={{0,2},{1,3},{2,0},{3,1},{4,6},{5,7},{6,4},{7,5},{8,10},{9,11},{10,... | collective-permute-start | bytes 405512 | tf_op jit(solution)/shard_map/ppermute | solution.py:255
  29.1 10.5 %collective-permute-start.12 = (bf16[384,4096]{1,0:T(8,128)(2,1)S(1)}, bf16[384,4096]{1,0:T(8,128)(2,1)S(1)}, u32[]{:S(2)}, u32[]{:S(2)}) collective-permute-start(bf16[384,4096]{1,0:T(8,128)(2,1)S(1)} %dequantize_down.1.refs_6_), channel_id=1, source_target_pairs={{0,1},{1,0},{2,3},{3,2},{4,5},{5,4},{6,7},{7,6},{8,9},{9,8},{10,11... | collective-permute-start | bytes 9437192 | tf_op jit(solution)/shard_map/ppermute | solution.py:20
  29.2 10.4 %collective-permute-start.10 = (bf16[32,4224]{1,0:T(8,128)(2,1)S(1)}, bf16[32,4224]{1,0:T(8,128)(2,1)S(1)}, u32[]{:S(2)}, u32[]{:S(2)}) collective-permute-start(bf16[32,4224]{1,0:T(8,128)(2,1)S(1)} %constant_dynamic-update-slice_fusion.2), channel_id=1, source_target_pairs={{0,2},{1,3},{2,0},{3,1},{4,6},{5,7},{6,4},{7,5},{8,10},{9,11},{10,... | collective-permute-start | bytes 811016 | tf_op jit(solution)/shard_map/ppermute | solution.py:255
  29.3 8.9 %collective-permute-start.9 = (bf16[32,4224]{1,0:T(8,128)(2,1)S(1)}, bf16[32,4224]{1,0:T(8,128)(2,1)S(1)}, u32[]{:S(2)}, u32[]{:S(2)}) collective-permute-start(bf16[32,4224]{1,0:T(8,128)(2,1)S(1)} %constant_dynamic-update-slice_fusion.2), channel_id=1, source_target_pairs={{0,16},{16,0},{8,24},{24,8},{1,17},{17,1},{9,25},{25,9},{2,18},{18... | collective-permute-start | bytes 811016 | tf_op jit(solution)/shard_map/ppermute | solution.py:20
  30.9 8.7 %collective-permute-start.8 = (bf16[32,4224]{1,0:T(8,128)(2,1)S(1)}, bf16[32,4224]{1,0:T(8,128)(2,1)S(1)}, u32[]{:S(2)}, u32[]{:S(2)}) collective-permute-start(bf16[32,4224]{1,0:T(8,128)(2,1)S(1)} %constant_dynamic-update-slice_fusion), channel_id=1, source_target_pairs={{0,8},{8,0},{16,24},{24,16},{1,9},{9,1},{17,25},{25,17},{2,10},{10... | collective-permute-start | bytes 811016 | tf_op jit(solution)/shard_map/ppermute | solution.py:20
  39.7 7.2 %collective-permute-start.16 = (bf16[16,4224]{1,0:T(8,128)(2,1)S(1)}, bf16[16,4224]{1,0:T(8,128)(2,1)S(1)}, u32[]{:S(2)}, u32[]{:S(2)}) collective-permute-start(bf16[16,4224]{1,0:T(8,128)(2,1)S(1)} %get-tuple-element.135), channel_id=1, source_target_pairs={{0,16},{16,0},{8,24},{24,8},{1,17},{17,1},{9,25},{25,9},{2,18},{18... | collective-permute-start | bytes 405512 | tf_op jit(solution)/shard_map/ppermute | solution.py:20
  40.2 6.7 %collective-permute-start.15 = (bf16[16,4224]{1,0:T(8,128)(2,1)S(1)}, bf16[16,4224]{1,0:T(8,128)(2,1)S(1)}, u32[]{:S(2)}, u32[]{:S(2)}) collective-permute-start(bf16[16,4224]{1,0:T(8,128)(2,1)S(1)} %get-tuple-element.136), channel_id=1, source_target_pairs={{0,8},{8,0},{16,24},{24,16},{1,9},{9,1},{17,25},{25,17},{2,10},{10... | collective-permute-start | bytes 405512 | tf_op jit(solution)/shard_map/ppermute | solution.py:20
  41.7 14.5 %collective-permute-start.13 = (bf16[64,4224]{1,0:T(8,128)(2,1)S(1)}, bf16[64,4224]{1,0:T(8,128)(2,1)S(1)}, u32[]{:S(2)}, u32[]{:S(2)}) collective-permute-start(bf16[64,4224]{1,0:T(8,128)(2,1)S(1)} %pad_maximum_fusion.refs_0_), channel_id=1, source_target_pairs={{0,16},{16,0},{8,24},{24,8},{1,17},{17,1},{9,25},{25,9},{2,18},{18... | collective-permute-start | bytes 1622024 | tf_op jit(solution)/shard_map/ppermute | solution.py:20
  43.3 13.6 %collective-permute-start.14 = (bf16[64,4224]{1,0:T(8,128)(2,1)S(1)}, bf16[64,4224]{1,0:T(8,128)(2,1)S(1)}, u32[]{:S(2)}, u32[]{:S(2)}) collective-permute-start(bf16[64,4224]{1,0:T(8,128)(2,1)S(1)} %pad_maximum_fusion.1.refs_2_), channel_id=1, source_target_pairs={{0,8},{8,0},{16,24},{24,16},{1,9},{9,1},{17,25},{25,17},{2,10},{10... | collective-permute-start | bytes 1622024 | tf_op jit(solution)/shard_map/ppermute | solution.py:20
  56.8 8.4 %collective-permute-start.17 = (bf16[32,4224]{1,0:T(8,128)(2,1)S(1)}, bf16[32,4224]{1,0:T(8,128)(2,1)S(1)}, u32[]{:S(2)}, u32[]{:S(2)}) collective-permute-start(bf16[32,4224]{1,0:T(8,128)(2,1)S(1)} %pad_maximum_fusion.4.refs_0_), channel_id=1, source_target_pairs={{0,16},{16,0},{8,24},{24,8},{1,17},{17,1},{9,25},{25,9},{2,18},{18... | collective-permute-start | bytes 811016 | tf_op jit(solution)/shard_map/ppermute | solution.py:20
  58.0 7.2 %collective-permute-start.18 = (bf16[32,4224]{1,0:T(8,128)(2,1)S(1)}, bf16[32,4224]{1,0:T(8,128)(2,1)S(1)}, u32[]{:S(2)}, u32[]{:S(2)}) collective-permute-start(bf16[32,4224]{1,0:T(8,128)(2,1)S(1)} %pad_maximum_fusion.5.refs_2_), channel_id=1, source_target_pairs={{0,8},{8,0},{16,24},{24,16},{1,9},{9,1},{17,25},{25,17},{2,10},{10... | collective-permute-start | bytes 811016 | tf_op jit(solution)/shard_map/ppermute | solution.py:20
  65.2 9.0 %collective-permute-start.19 = (bf16[32,4096]{1,0:T(8,128)(2,1)S(1)}, bf16[32,4096]{1,0:T(8,128)(2,1)S(1)}, u32[]{:S(2)}, u32[]{:S(2)}) collective-permute-start(bf16[32,4096]{1,0:T(8,128)(2,1)S(1)} %get-tuple-element.118), channel_id=1, source_target_pairs={{0,16},{16,0},{8,24},{24,8},{1,17},{17,1},{9,25},{25,9},{2,18},{18... | collective-permute-start | bytes 786440 | tf_op jit(solution)/shard_map/ppermute | solution.py:20
  69.0 10.9 %collective-permute-start.23 = (bf16[32,4096]{1,0:T(8,128)(2,1)S(1)}, bf16[32,4096]{1,0:T(8,128)(2,1)S(1)}, u32[]{:S(2)}, u32[]{:S(2)}) collective-permute-start(bf16[32,4096]{1,0:T(8,128)(2,1)S(1)} %get-tuple-element.126), channel_id=1, source_target_pairs={{0,16},{16,0},{8,24},{24,8},{1,17},{17,1},{9,25},{25,9},{2,18},{18... | collective-permute-start | bytes 786440 | tf_op jit(solution)/shard_map/ppermute | solution.py:20
  70.5 9.6 %collective-permute-start.25 = (bf16[32,4096]{1,0:T(8,128)(2,1)S(1)}, bf16[32,4096]{1,0:T(8,128)(2,1)S(1)}, u32[]{:S(2)}, u32[]{:S(2)}) collective-permute-start(bf16[32,4096]{1,0:T(8,128)(2,1)S(1)} %get-tuple-element.128), channel_id=1, source_target_pairs={{0,8},{8,0},{16,24},{24,16},{1,9},{9,1},{17,25},{25,17},{2,10},{10... | collective-permute-start | bytes 786440 | tf_op jit(solution)/shard_map/ppermute | solution.py:20
  71.1 45.6 %collective-permute-start.32 = (bf16[32,4096]{1,0:T(8,128)(2,1)S(1)}, bf16[32,4096]{1,0:T(8,128)(2,1)S(1)}, u32[]{:S(2)}, u32[]{:S(2)}) collective-permute-start(bf16[32,4096]{1,0:T(8,128)(2,1)S(1)} %get-tuple-element.132), channel_id=1, source_target_pairs={{0,8},{8,0},{16,24},{24,16},{1,9},{9,1},{17,25},{25,17},{2,10},{10... | collective-permute-start | bytes 786440 | tf_op jit(solution)/shard_map/ppermute | solution.py:20
  72.5 33.0 %collective-permute-start.21 = (bf16[64,4096]{1,0:T(8,128)(2,1)S(1)}, bf16[64,4096]{1,0:T(8,128)(2,1)S(1)}, u32[]{:S(2)}, u32[]{:S(2)}) collective-permute-start(bf16[64,4096]{1,0:T(8,128)(2,1)S(1)} %get-tuple-element.120), channel_id=1, source_target_pairs={{0,8},{8,0},{16,24},{24,16},{1,9},{9,1},{17,25},{25,17},{2,10},{10... | collective-permute-start | bytes 1572872 | tf_op jit(solution)/shard_map/ppermute | solution.py:20
  74.3 32.2 %collective-permute-start.29 = (bf16[64,4096]{1,0:T(8,128)(2,1)S(1)}, bf16[64,4096]{1,0:T(8,128)(2,1)S(1)}, u32[]{:S(2)}, u32[]{:S(2)}) collective-permute-start(bf16[64,4096]{1,0:T(8,128)(2,1)S(1)} %get-tuple-element.130), channel_id=1, source_target_pairs={{0,16},{16,0},{8,24},{24,8},{1,17},{17,1},{9,25},{25,9},{2,18},{18... | collective-permute-start | bytes 1572872 | tf_op jit(solution)/shard_map/ppermute | solution.py:20
  79.9 37.8 %collective-permute-start.20 = (bf16[16,4096]{1,0:T(8,128)(2,1)S(1)}, bf16[16,4096]{1,0:T(8,128)(2,1)S(1)}, u32[]{:S(2)}, u32[]{:S(2)}) collective-permute-start(bf16[16,4096]{1,0:T(8,128)(2,1)S(1)} %split.49), channel_id=1, source_target_pairs={{0,8},{8,0},{16,24},{24,16},{1,9},{9,1},{17,25},{25,17},{2,10},{10... | collective-permute-start | bytes 393224 | tf_op jit(solution)/shard_map/ppermute | solution.py:20
  80.1 18.1 %collective-permute-start.24 = (bf16[16,4096]{1,0:T(8,128)(2,1)S(1)}, bf16[16,4096]{1,0:T(8,128)(2,1)S(1)}, u32[]{:S(2)}, u32[]{:S(2)}) collective-permute-start(bf16[16,4096]{1,0:T(8,128)(2,1)S(1)} %split.53), channel_id=1, source_target_pairs={{0,8},{8,0},{16,24},{24,16},{1,9},{9,1},{17,25},{25,17},{2,10},{10... | collective-permute-start | bytes 393224 | tf_op jit(solution)/shard_map/ppermute | solution.py:20
  104.6 11.6 %collective-permute-start.27 = (bf16[32,4096]{1,0:T(8,128)(2,1)S(1)}, bf16[32,4096]{1,0:T(8,128)(2,1)S(1)}, u32[]{:S(2)}, u32[]{:S(2)}) collective-permute-start(bf16[32,4096]{1,0:T(8,128)(2,1)S(1)} %pad_maximum_fusion.6), channel_id=1, source_target_pairs={{0,2},{1,3},{2,0},{3,1},{4,6},{5,7},{6,4},{7,5},{8,10},{9,11},{10,... | collective-permute-start | bytes 786440 | tf_op jit(solution)/shard_map/ppermute | solution.py:255
  105.7 10.4 %collective-permute-start.22 = (bf16[32,4096]{1,0:T(8,128)(2,1)S(1)}, bf16[32,4096]{1,0:T(8,128)(2,1)S(1)}, u32[]{:S(2)}, u32[]{:S(2)}) collective-permute-start(bf16[32,4096]{1,0:T(8,128)(2,1)S(1)} %split.51), channel_id=1, source_target_pairs={{0,16},{16,0},{8,24},{24,8},{1,17},{17,1},{9,25},{25,9},{2,18},{18... | collective-permute-start | bytes 786440 | tf_op jit(solution)/shard_map/ppermute | solution.py:20
  106.6 9.7 %collective-permute-start.30 = (bf16[32,4096]{1,0:T(8,128)(2,1)S(1)}, bf16[32,4096]{1,0:T(8,128)(2,1)S(1)}, u32[]{:S(2)}, u32[]{:S(2)}) collective-permute-start(bf16[32,4096]{1,0:T(8,128)(2,1)S(1)} %split.57), channel_id=1, source_target_pairs={{0,8},{8,0},{16,24},{24,16},{1,9},{9,1},{17,25},{25,17},{2,10},{10... | collective-permute-start | bytes 786440 | tf_op jit(solution)/shard_map/ppermute | solution.py:20
  116.3 9.2 %collective-permute-start.28 = (bf16[32,4096]{1,0:T(8,128)(2,1)S(1)}, bf16[32,4096]{1,0:T(8,128)(2,1)S(1)}, u32[]{:S(2)}, u32[]{:S(2)}) collective-permute-start(bf16[32,4096]{1,0:T(8,128)(2,1)S(1)} %add_convert_fusion.4), channel_id=1, source_target_pairs={{0,4},{1,5},{2,6},{3,7},{4,0},{5,1},{6,2},{7,3},{8,12},{9,13},{10,... | collective-permute-start | bytes 786440 | tf_op jit(solution)/shard_map/ppermute | solution.py:255
  116.5 9.2 %collective-permute-start.31 = (bf16[32,4096]{1,0:T(8,128)(2,1)S(1)}, bf16[32,4096]{1,0:T(8,128)(2,1)S(1)}, u32[]{:S(2)}, u32[]{:S(2)}) collective-permute-start(bf16[32,4096]{1,0:T(8,128)(2,1)S(1)} %add_convert_fusion.3), channel_id=1, source_target_pairs={{0,2},{1,3},{2,0},{3,1},{4,6},{5,7},{6,4},{7,5},{8,10},{9,11},{10,... | collective-permute-start | bytes 786440 | tf_op jit(solution)/shard_map/ppermute | solution.py:255
  (9 other events, 43.5 us)

commit v13 on v10

--- a/solution.py
+++ b/solution.py
@@ -272,17 +272,17 @@
 
     place, payload = together((place, payload))
     lanes, outs = {0: payload}, {}
-    near = [{far: across_chips(payload[0], far) for far in groups[1]}]
+    came = {0: jnp.concatenate(payload, axis=0)}
+    for far in groups[1]:
+        along_z(far)
     gather_turn(0, 0)
     in_own = dequantize_in(gate_q[0], up_q[0], gate_scale[0], up_scale[0])
     down_own = dequantize_down(down_q[0], down_scale[0])
-    lanes, near, payload, in_own, down_own = together((lanes, near, payload, in_own, down_own))
+    lanes, came, in_own, down_own = together((lanes, came, in_own, down_own))
     in_other = from_partner(in_own, "expert", 0)
-    near.append({far: across_chips(payload[1], far) for far in groups[1]})
     for turn in range(1, turns):
         gather_turn(0, turn)
-    lanes, near, down_own = together((lanes, near, down_own))
-    came = {far: jnp.concatenate([part[far] for part in near], axis=0) for far in groups[1]}
+    lanes, came, down_own = together((lanes, came, down_own))
     down_other = from_partner(down_own, "expert", 0)
     lanes[1] = lanes_of(groups[1])
     for number in range(1, len(groups)):
@@ -329,33 +329,28 @@
                 came_back = across_chips(block, low)
                 into = far ^ low
                 merged[into] = added(merged[into], came_back) if into in merged else came_back
-            elif number > 1:
+            else:
                 whole = across_chips(block, low)
                 parts.append([whole[rows] for rows in halves])
-            else:
-                leaving[far] = [block[rows] for rows in halves]
-
-    sums, merged, parts, leaving = {}, {}, [], {}
+
+    sums, merged, parts = {}, {}, []
     for number in range(final, 0, -1):
         for turn in range(turns - 1 - int(number < final), -1, -1):
             sum_turn(number, turn)
             if turn == 0 and number > 1:
                 sum_turn(number - 1, turns - 1)
-            if turn == 0 and number > 1:
-                leave(number)
-            sums, outs, merged = together((sums, outs, merged))
+        if number > 1:
+            leave(number)
+        sums, outs = together((sums, outs))
+    sums, merged = together((sums, merged))
     leave(1)
-    back = [{far: across_chips(leaving[far][0], far) for far in groups[1]}]
-    for turn in range(turns - 1, 0, -1):
+    for turn in range(turns - 1, -1, -1):
         sum_turn(0, turn)
-    sums, back, leaving = together((sums, back, leaving))
-    back.append({far: across_chips(leaving[far][1], far) for far in groups[1]})
-    sum_turn(0, 0)
     result = []
     for lane, rows in enumerate(halves):
         total = tokens[rows].astype(jnp.float32) + sums[0][lane].astype(jnp.float32)
-        for part in [*back[lane].values(), *(part[lane] for part in parts)]:
-            total = total + part.astype(jnp.float32)
+        for part in parts:
+            total = total + part[lane].astype(jnp.float32)
         result.append(total.astype(jnp.bfloat16))
     return jnp.concatenate(result, axis=0)
 

time: 118 us -> 117 us (level)
  waiting for transfers between devices: 55.4 us -> 54.2 us
    ppermute x10 -> x6, waiting for transfers between devices: 10.7 us -> 3.05 us  [across_chips(): lax.ppermute(block, 'expert', [(low, low ^ 2 * far) for low in range(coun...]
    ppermute x26, waiting for transfers between devices: 44.7 us -> 51.1 us  [from_partner(): return lax.ppermute(block, axis, route)]
    ppermute x10 -> x6, starting transfers between devices: 12.6 us -> 11.2 us  [across_chips(): lax.ppermute(block, 'expert', [(low, low ^ 2 * far) for low in range(coun...]
    unnamed x17 -> x14, local copies, waits for them, and re-layouts: 2.9 us -> 3.57 us
  transfers between devices with their start and end apart: 36 -> 32, of which waited for: 19 -> 17; matrix products, arithmetic and copies ran while one was open for 1% -> 1% of each run, Pallas kernels for 11% -> 11%
where the time goes in v13:
time: 117 us
  waiting for transfers between devices  54.2 us (46%)
  starting transfers between devices  39 us (33%)
  Pallas kernels  15.8 us (14%)
  local copies, waits for them, and re-layouts  4.95 us (4%)
  other arithmetic  2.55 us (2%)
    ppermute x26, waiting for transfers between devices, from_partner(): return lax.ppermute(block, axis, route)  51.1 us
    ppermute x26, starting transfers between devices, from_partner(): return lax.ppermute(block, axis, route)  27.8 us
    pallas_call x3, Pallas kernels, expert_layer(): pl.pallas_call(functools.partial(expert_kernel, count, experts), in_specs...  12 us
    ppermute x6, starting transfers between devices, across_chips(): lax.ppermute(block, 'expert', [(low, low ^ 2 * far) for low in range(coun...  11.2 us
    unnamed x14, local copies, waits for them, and re-layouts  3.57 us
    ppermute x6, waiting for transfers between devices, across_chips(): lax.ppermute(block, 'expert', [(low, low ^ 2 * far) for low in range(coun...  3.05 us
  transfers between devices with their start and end apart: 32, of which 17 were waited for; matrix products, arithmetic and copies ran while one was open for 1% of the time, Pallas kernels for 11%

profile of v13, /device:TPU:0, one launch (start us, length us, event | category | flops | bytes accessed | tf_op | source)
XLA Modules:
  0.0 116.9 jit_solution(17925709254066578027)
XLA Ops:
  2.0 2.9 %collective-permute-start = (bf16[16,4224]{1,0:T(8,128)(2,1)S(1)}, bf16[16,4224]{1,0:T(8,128)(2,1)S(1)}, u32[]{:S(2)}, u32[]{:S(2)}) collective-permute-start(bf16[16,4224]{1,0:T(8,128)(2,1)S(1)} %concatenate.33), channel_id=1, source_target_pairs={{0,8},{8,0},{16,24},{24,16},{1,9},{9,1},{17,25},{25,17},{2,10},{10... | collective-permute-start | bytes 405512 | tf_op jit(solution)/shard_map/ppermute | solution.py:20
  5.0 1.5 %collective-permute-start.1 = (bf16[16,4224]{1,0:T(8,128)(2,1)S(1)}, bf16[16,4224]{1,0:T(8,128)(2,1)S(1)}, u32[]{:S(2)}, u32[]{:S(2)}) collective-permute-start(bf16[16,4224]{1,0:T(8,128)(2,1)S(1)} %concatenate.34), channel_id=1, source_target_pairs={{0,16},{16,0},{8,24},{24,8},{1,17},{17,1},{9,25},{25,9},{2,18},{18... | collective-permute-start | bytes 405512 | tf_op jit(solution)/shard_map/ppermute | solution.py:20
  6.5 2.7 %collective-permute-start.3 = (bf16[32,4224]{1,0:T(8,128)(2,1)S(1)}, bf16[32,4224]{1,0:T(8,128)(2,1)S(1)}, u32[]{:S(2)}, u32[]{:S(2)}) collective-permute-start(bf16[32,4224]{1,0:T(8,128)(2,1)S(1)} %constant_dynamic-update-slice_fusion), channel_id=1, source_target_pairs={{0,4},{1,5},{2,6},{3,7},{4,0},{5,1},{6,2},{7,3},{8,12},{9,13},{10,... | collective-permute-start | bytes 811016 | tf_op jit(solution)/shard_map/ppermute | solution.py:223
  9.2 1.6 %collective-permute-start.2 = (bf16[32,4224]{1,0:T(8,128)(2,1)S(1)}, bf16[32,4224]{1,0:T(8,128)(2,1)S(1)}, u32[]{:S(2)}, u32[]{:S(2)}) collective-permute-start(bf16[32,4224]{1,0:T(8,128)(2,1)S(1)} %constant_dynamic-update-slice_fusion), channel_id=1, source_target_pairs={{0,2},{1,3},{2,0},{3,1},{4,6},{5,7},{6,4},{7,5},{8,10},{9,11},{10,... | collective-permute-start | bytes 811016 | tf_op jit(solution)/shard_map/ppermute | solution.py:223
  11.5 1.9 %copy-done = bf16[1,384,4096]{2,1,0:T(8,128)(2,1)S(1)} copy-done((bf16[1,384,4096]{2,1,0:T(8,128)(2,1)S(1)}, bf16[1,384,4096]{2,1,0:T(8,128)(2,1)}, u32[]{:S(2)}) %copy-start) | copy-done | bytes 3145752
  13.3 1.8 %dequantize_down.1.refs_6_ = bf16[384,4096]{1,0:T(8,128)(2,1)S(1)} custom-call(f32[3,32]{1,0:T(4,128)S(1)} %bitcast.18, bf16[384,4096]{1,0:T(8,128)(2,1)S(1)} %bitcast.15), custom_call_target="tpu_custom_call" | custom-call | flops 1572864 | bytes 6291456 | tf_op jit(solution)/shard_map/dequantize_down/pallas_call | solution.py:148
  16.2 1.9 %dequantize_in.1.refs_4_ = bf16[4096,768]{1,0:T(8,128)(2,1)S(1)} custom-call(f32[3,32]{1,0:T(4,128)S(1)} %get-tuple-element.168.gate_scales, f32[3,32]{1,0:T(4,128)S(1)} %get-tuple-element.167.up_scales, bf16[4096,384]{1,0:T(8,128)(2,1)S(1)} %bitcast.16, bf16[4096,384]{1,0:T(8,128)(2,1)S(1)} %bitcast.17), custom_call_target="tpu_custom_call" | custom-call | flops 3145728 | bytes 12582912 | tf_op jit(solution)/shard_map/dequantize_in/pallas_call | solution.py:120
  18.2 2.8 %collective-permute-done.3 = bf16[32,4224]{1,0:T(8,128)(2,1)S(1)} collective-permute-done((bf16[32,4224]{1,0:T(8,128)(2,1)S(1)}, bf16[32,4224]{1,0:T(8,128)(2,1)S(1)}, u32[]{:S(2)}, u32[]{:S(2)}) %collective-permute-start.3) | collective-permute-done | bytes 270368 | tf_op jit(solution)/shard_map/ppermute | solution.py:223
  22.2 7.9 %collective-permute-done.4.refs_1_ = bf16[32,4224]{1,0:T(8,128)(2,1)S(1)} collective-permute-done((bf16[32,4224]{1,0:T(8,128)(2,1)S(1)}, bf16[32,4224]{1,0:T(8,128)(2,1)S(1)}, u32[]{:S(2)}, u32[]{:S(2)}) %collective-permute-start.4) | collective-permute-done | bytes 270368 | tf_op jit(solution)/shard_map/ppermute | solution.py:20
  30.9 1.5 %collective-permute-start.8 = (bf16[32,4224]{1,0:T(8,128)(2,1)S(1)}, bf16[32,4224]{1,0:T(8,128)(2,1)S(1)}, u32[]{:S(2)}, u32[]{:S(2)}) collective-permute-start(bf16[32,4224]{1,0:T(8,128)(2,1)S(1)} %collective-permute-done.3), channel_id=1, source_target_pairs={{0,2},{1,3},{2,0},{3,1},{4,6},{5,7},{6,4},{7,5},{8,10},{9,11},{10,... | collective-permute-start | bytes 811016 | tf_op jit(solution)/shard_map/ppermute | solution.py:223
  32.4 1.5 %collective-permute-start.7 = (bf16[32,4224]{1,0:T(8,128)(2,1)S(1)}, bf16[32,4224]{1,0:T(8,128)(2,1)S(1)}, u32[]{:S(2)}, u32[]{:S(2)}) collective-permute-start(bf16[32,4224]{1,0:T(8,128)(2,1)S(1)} %collective-permute-done.3), channel_id=1, source_target_pairs={{0,16},{16,0},{8,24},{24,8},{1,17},{17,1},{9,25},{25,9},{2,18},{18... | collective-permute-start | bytes 811016 | tf_op jit(solution)/shard_map/ppermute | solution.py:20
  33.9 5.4 %collective-permute-done.6 = bf16[32,4224]{1,0:T(8,128)(2,1)S(1)} collective-permute-done((bf16[32,4224]{1,0:T(8,128)(2,1)S(1)}, bf16[32,4224]{1,0:T(8,128)(2,1)S(1)}, u32[]{:S(2)}, u32[]{:S(2)}) %collective-permute-start.6) | collective-permute-done | bytes 270368 | tf_op jit(solution)/shard_map/ppermute | solution.py:20
  39.3 1.4 %collective-permute-done.7 = bf16[32,4224]{1,0:T(8,128)(2,1)S(1)} collective-permute-done((bf16[32,4224]{1,0:T(8,128)(2,1)S(1)}, bf16[32,4224]{1,0:T(8,128)(2,1)S(1)}, u32[]{:S(2)}, u32[]{:S(2)}) %collective-permute-start.7) | collective-permute-done | bytes 270368 | tf_op jit(solution)/shard_map/ppermute | solution.py:20
  40.8 1.6 %collective-permute-start.14 = (bf16[16,4224]{1,0:T(8,128)(2,1)S(1)}, bf16[16,4224]{1,0:T(8,128)(2,1)S(1)}, u32[]{:S(2)}, u32[]{:S(2)}) collective-permute-start(bf16[16,4224]{1,0:T(8,128)(2,1)S(1)} %get-tuple-element.157), channel_id=1, source_target_pairs={{0,16},{16,0},{8,24},{24,8},{1,17},{17,1},{9,25},{25,9},{2,18},{18... | collective-permute-start | bytes 405512 | tf_op jit(solution)/shard_map/ppermute | solution.py:20
  42.4 1.5 %collective-permute-start.13 = (bf16[16,4224]{1,0:T(8,128)(2,1)S(1)}, bf16[16,4224]{1,0:T(8,128)(2,1)S(1)}, u32[]{:S(2)}, u32[]{:S(2)}) collective-permute-start(bf16[16,4224]{1,0:T(8,128)(2,1)S(1)} %get-tuple-element.158), channel_id=1, source_target_pairs={{0,8},{8,0},{16,24},{24,16},{1,9},{9,1},{17,25},{25,17},{2,10},{10... | collective-permute-start | bytes 405512 | tf_op jit(solution)/shard_map/ppermute | solution.py:20
  44.9 3.1 %expert_layer.3 = (bf16[32,4096]{1,0:T(8,128)(2,1)S(1)}, bf16[32,4096]{1,0:T(8,128)(2,1)S(1)}, bf16[32,4096]{1,0:T(8,128)(2,1)S(1)}, bf16[32,4096]{1,0:T(8,128)(2,1)S(1)}) custom-call(s32[1]{0:T(128)} %bitcast.own_expert, bf16[32,4224]{1,0:T(8,128)(2,1)S(1)} %pad_maximum_fusion.2.refs_0_, bf16[32,4224]{1,0:T(8,128)(2,1)S(1)} %collective-permute-done.4.refs_1_, ...), custom_call_target="tpu_custom_call" | custom-call | flops 2415919104 | bytes 20971520 | tf_op jit(solution)/shard_map/expert_layer/pallas_call | solution.py:202
  48.9 8.5 %collective-permute-done.11.refs_1_ = bf16[64,4224]{1,0:T(8,128)(2,1)S(1)} collective-permute-done((bf16[64,4224]{1,0:T(8,128)(2,1)S(1)}, bf16[64,4224]{1,0:T(8,128)(2,1)S(1)}, u32[]{:S(2)}, u32[]{:S(2)}) %collective-permute-start.11) | collective-permute-done | bytes 540704 | tf_op jit(solution)/shard_map/ppermute | solution.py:20
  58.3 1.2 %collective-permute-start.15 = (bf16[32,4224]{1,0:T(8,128)(2,1)S(1)}, bf16[32,4224]{1,0:T(8,128)(2,1)S(1)}, u32[]{:S(2)}, u32[]{:S(2)}) collective-permute-start(bf16[32,4224]{1,0:T(8,128)(2,1)S(1)} %pad_maximum_fusion.4.refs_0_), channel_id=1, source_target_pairs={{0,16},{16,0},{8,24},{24,8},{1,17},{17,1},{9,25},{25,9},{2,18},{18... | collective-permute-start | bytes 811016 | tf_op jit(solution)/shard_map/ppermute | solution.py:20
  60.3 5.7 %expert_layer.4 = (bf16[64,4096]{1,0:T(8,128)(2,1)S(1)}, bf16[64,4096]{1,0:T(8,128)(2,1)S(1)}, bf16[64,4096]{1,0:T(8,128)(2,1)S(1)}, bf16[64,4096]{1,0:T(8,128)(2,1)S(1)}) custom-call(s32[1]{0:T(128)} %bitcast.own_expert, bf16[64,4224]{1,0:T(8,128)(2,1)S(1)} %pad_maximum_fusion.refs_0_, bf16[64,4224]{1,0:T(8,128)(2,1)S(1)} %collective-permute-done.11.refs_1_, ...), custom_call_target="tpu_custom_call" | custom-call | flops 4831838208 | bytes 23068672 | tf_op jit(solution)/shard_map/expert_layer/pallas_call | solution.py:202
  66.1 3.1 %expert_layer.5 = (bf16[32,4096]{1,0:T(8,128)(2,1)S(1)}, bf16[32,4096]{1,0:T(8,128)(2,1)S(1)}, bf16[32,4096]{1,0:T(8,128)(2,1)S(1)}, bf16[32,4096]{1,0:T(8,128)(2,1)S(1)}) custom-call(s32[1]{0:T(128)} %bitcast.own_expert, bf16[32,4224]{1,0:T(8,128)(2,1)S(1)} %pad_maximum_fusion.4.refs_0_, bf16[32,4224]{1,0:T(8,128)(2,1)S(1)} %collective-permute-done.15.refs_1_, ...), custom_call_target="tpu_custom_call" | custom-call | flops 2415919104 | bytes 20971520 | tf_op jit(solution)/shard_map/expert_layer/pallas_call | solution.py:202
  69.2 1.5 %collective-permute-start.23 = (bf16[32,4096]{1,0:T(8,128)(2,1)S(1)}, bf16[32,4096]{1,0:T(8,128)(2,1)S(1)}, u32[]{:S(2)}, u32[]{:S(2)}) collective-permute-start(bf16[32,4096]{1,0:T(8,128)(2,1)S(1)} %get-tuple-element.135), channel_id=1, source_target_pairs={{0,16},{16,0},{8,24},{24,8},{1,17},{17,1},{9,25},{25,9},{2,18},{18... | collective-permute-start | bytes 786440 | tf_op jit(solution)/shard_map/ppermute | solution.py:20
  73.3 5.2 %collective-permute-done.23 = bf16[32,4096]{1,0:T(8,128)(2,1)S(1)} collective-permute-done((bf16[32,4096]{1,0:T(8,128)(2,1)S(1)}, bf16[32,4096]{1,0:T(8,128)(2,1)S(1)}, u32[]{:S(2)}, u32[]{:S(2)}) %collective-permute-start.23) | collective-permute-done | bytes 262176 | tf_op jit(solution)/shard_map/ppermute | solution.py:20
  78.6 1.3 %collective-permute-start.24 = (bf16[16,4096]{1,0:T(8,128)(2,1)S(1)}, bf16[16,4096]{1,0:T(8,128)(2,1)S(1)}, u32[]{:S(2)}, u32[]{:S(2)}) collective-permute-start(bf16[16,4096]{1,0:T(8,128)(2,1)S(1)} %split.51), channel_id=1, source_target_pairs={{0,8},{8,0},{16,24},{24,16},{1,9},{9,1},{17,25},{25,17},{2,10},{10... | collective-permute-start | bytes 393224 | tf_op jit(solution)/shard_map/ppermute | solution.py:20
  81.0 9.1 %collective-permute-done.24 = bf16[16,4096]{1,0:T(8,128)(2,1)S(1)} collective-permute-done((bf16[16,4096]{1,0:T(8,128)(2,1)S(1)}, bf16[16,4096]{1,0:T(8,128)(2,1)S(1)}, u32[]{:S(2)}, u32[]{:S(2)}) %collective-permute-start.24) | collective-permute-done | bytes 131104 | tf_op jit(solution)/shard_map/ppermute | solution.py:20
  92.2 1.3 %collective-permute-start.19 = (bf16[32,4096]{1,0:T(8,128)(2,1)S(1)}, bf16[32,4096]{1,0:T(8,128)(2,1)S(1)}, u32[]{:S(2)}, u32[]{:S(2)}) collective-permute-start(bf16[32,4096]{1,0:T(8,128)(2,1)S(1)} %split.37), channel_id=1, source_target_pairs={{0,8},{8,0},{16,24},{24,16},{1,9},{9,1},{17,25},{25,17},{2,10},{10... | collective-permute-start | bytes 786440 | tf_op jit(solution)/shard_map/ppermute | solution.py:20
  93.6 4.0 %collective-permute-done.20 = bf16[32,4096]{1,0:T(8,128)(2,1)S(1)} collective-permute-done((bf16[32,4096]{1,0:T(8,128)(2,1)S(1)}, bf16[32,4096]{1,0:T(8,128)(2,1)S(1)}, u32[]{:S(2)}, u32[]{:S(2)}) %collective-permute-start.20) | collective-permute-done | bytes 262176 | tf_op jit(solution)/shard_map/ppermute | solution.py:20
  98.7 1.1 collective-permute-start.21
  99.9 3.0 %collective-permute-start.28 = (bf16[32,4096]{1,0:T(8,128)(2,1)S(1)}, bf16[32,4096]{1,0:T(8,128)(2,1)S(1)}, u32[]{:S(2)}, u32[]{:S(2)}) collective-permute-start(bf16[32,4096]{1,0:T(8,128)(2,1)S(1)} %add_convert_fusion.3), channel_id=1, source_target_pairs={{0,4},{1,5},{2,6},{3,7},{4,0},{5,1},{6,2},{7,3},{8,12},{9,13},{10,... | collective-permute-start | bytes 786440 | tf_op jit(solution)/shard_map/ppermute | solution.py:223
  102.9 1.6 %collective-permute-start.29 = (bf16[32,4096]{1,0:T(8,128)(2,1)S(1)}, bf16[32,4096]{1,0:T(8,128)(2,1)S(1)}, u32[]{:S(2)}, u32[]{:S(2)}) collective-permute-start(bf16[32,4096]{1,0:T(8,128)(2,1)S(1)} %add_convert_fusion.8), channel_id=1, source_target_pairs={{0,2},{1,3},{2,0},{3,1},{4,6},{5,7},{6,4},{7,5},{8,10},{9,11},{10,... | collective-permute-start | bytes 786440 | tf_op jit(solution)/shard_map/ppermute | solution.py:223
  105.3 3.1 %collective-permute-start.22 = (bf16[16,4096]{1,0:T(8,128)(2,1)S(1)}, bf16[16,4096]{1,0:T(8,128)(2,1)S(1)}, u32[]{:S(2)}, u32[]{:S(2)}) collective-permute-start(bf16[16,4096]{1,0:T(8,128)(2,1)S(1)} %split.49), channel_id=1, source_target_pairs={{0,8},{8,0},{16,24},{24,16},{1,9},{9,1},{17,25},{25,17},{2,10},{10... | collective-permute-start | bytes 393224 | tf_op jit(solution)/shard_map/ppermute | solution.py:20
  108.4 2.4 %collective-permute-done.30 = bf16[32,4096]{1,0:T(8,128)(2,1)S(1)} collective-permute-done((bf16[32,4096]{1,0:T(8,128)(2,1)S(1)}, bf16[32,4096]{1,0:T(8,128)(2,1)S(1)}, u32[]{:S(2)}, u32[]{:S(2)}) %collective-permute-start.30) | collective-permute-done | bytes 262176 | tf_op jit(solution)/shard_map/ppermute | solution.py:20
  112.2 3.7 %collective-permute-done.31 = bf16[16,4096]{1,0:T(8,128)(2,1)S(1)} collective-permute-done((bf16[16,4096]{1,0:T(8,128)(2,1)S(1)}, bf16[16,4096]{1,0:T(8,128)(2,1)S(1)}, u32[]{:S(2)}, u32[]{:S(2)}) %collective-permute-start.31) | collective-permute-done | bytes 131104 | tf_op jit(solution)/shard_map/ppermute | solution.py:20
  (88 shorter events, 19.4 us)
Async XLA Ops:
  2.0 16.1 %collective-permute-start = (bf16[16,4224]{1,0:T(8,128)(2,1)S(1)}, bf16[16,4224]{1,0:T(8,128)(2,1)S(1)}, u32[]{:S(2)}, u32[]{:S(2)}) collective-permute-start(bf16[16,4224]{1,0:T(8,128)(2,1)S(1)} %concatenate.33), channel_id=1, source_target_pairs={{0,8},{8,0},{16,24},{24,16},{1,9},{9,1},{17,25},{25,17},{2,10},{10... | collective-permute-start | bytes 405512 | tf_op jit(solution)/shard_map/ppermute | solution.py:20
  5.0 13.2 %collective-permute-start.1 = (bf16[16,4224]{1,0:T(8,128)(2,1)S(1)}, bf16[16,4224]{1,0:T(8,128)(2,1)S(1)}, u32[]{:S(2)}, u32[]{:S(2)}) collective-permute-start(bf16[16,4224]{1,0:T(8,128)(2,1)S(1)} %concatenate.34), channel_id=1, source_target_pairs={{0,16},{16,0},{8,24},{24,8},{1,17},{17,1},{9,25},{25,9},{2,18},{18... | collective-permute-start | bytes 405512 | tf_op jit(solution)/shard_map/ppermute | solution.py:20
  6.5 14.5 %collective-permute-start.3 = (bf16[32,4224]{1,0:T(8,128)(2,1)S(1)}, bf16[32,4224]{1,0:T(8,128)(2,1)S(1)}, u32[]{:S(2)}, u32[]{:S(2)}) collective-permute-start(bf16[32,4224]{1,0:T(8,128)(2,1)S(1)} %constant_dynamic-update-slice_fusion), channel_id=1, source_target_pairs={{0,4},{1,5},{2,6},{3,7},{4,0},{5,1},{6,2},{7,3},{8,12},{9,13},{10,... | collective-permute-start | bytes 811016 | tf_op jit(solution)/shard_map/ppermute | solution.py:223
  9.2 12.1 %collective-permute-start.2 = (bf16[32,4224]{1,0:T(8,128)(2,1)S(1)}, bf16[32,4224]{1,0:T(8,128)(2,1)S(1)}, u32[]{:S(2)}, u32[]{:S(2)}) collective-permute-start(bf16[32,4224]{1,0:T(8,128)(2,1)S(1)} %constant_dynamic-update-slice_fusion), channel_id=1, source_target_pairs={{0,2},{1,3},{2,0},{3,1},{4,6},{5,7},{6,4},{7,5},{8,10},{9,11},{10,... | collective-permute-start | bytes 811016 | tf_op jit(solution)/shard_map/ppermute | solution.py:223
  21.3 19.5 %collective-permute-start.9 = (bf16[4096,768]{1,0:T(8,128)(2,1)S(1)}, bf16[4096,768]{1,0:T(8,128)(2,1)S(1)}, u32[]{:S(2)}, u32[]{:S(2)}) collective-permute-start(bf16[4096,768]{1,0:T(8,128)(2,1)S(1)} %dequantize_in.1.refs_4_), channel_id=1, source_target_pairs={{0,1},{1,0},{2,3},{3,2},{4,5},{5,4},{6,7},{7,6},{8,9},{9,8},{10,11... | collective-permute-start | bytes 18874376 | tf_op jit(solution)/shard_map/ppermute | solution.py:20
  21.3 8.9 %collective-permute-start.4 = (bf16[32,4224]{1,0:T(8,128)(2,1)S(1)}, bf16[32,4224]{1,0:T(8,128)(2,1)S(1)}, u32[]{:S(2)}, u32[]{:S(2)}) collective-permute-start(bf16[32,4224]{1,0:T(8,128)(2,1)S(1)} %pad_maximum_fusion.2.refs_0_), channel_id=1, source_target_pairs={{0,16},{16,0},{8,24},{24,8},{1,17},{17,1},{9,25},{25,9},{2,18},{18... | collective-permute-start | bytes 811016 | tf_op jit(solution)/shard_map/ppermute | solution.py:20
  21.8 8.6 %collective-permute-start.5 = (bf16[32,4224]{1,0:T(8,128)(2,1)S(1)}, bf16[32,4224]{1,0:T(8,128)(2,1)S(1)}, u32[]{:S(2)}, u32[]{:S(2)}) collective-permute-start(bf16[32,4224]{1,0:T(8,128)(2,1)S(1)} %pad_maximum_fusion.3.refs_2_), channel_id=1, source_target_pairs={{0,8},{8,0},{16,24},{24,16},{1,9},{9,1},{17,25},{25,17},{2,10},{10... | collective-permute-start | bytes 811016 | tf_op jit(solution)/shard_map/ppermute | solution.py:20
  30.4 10.4 %collective-permute-start.10 = (bf16[384,4096]{1,0:T(8,128)(2,1)S(1)}, bf16[384,4096]{1,0:T(8,128)(2,1)S(1)}, u32[]{:S(2)}, u32[]{:S(2)}) collective-permute-start(bf16[384,4096]{1,0:T(8,128)(2,1)S(1)} %dequantize_down.1.refs_6_), channel_id=1, source_target_pairs={{0,1},{1,0},{2,3},{3,2},{4,5},{5,4},{6,7},{7,6},{8,9},{9,8},{10,11... | collective-permute-start | bytes 9437192 | tf_op jit(solution)/shard_map/ppermute | solution.py:20
  30.4 8.9 %collective-permute-start.6 = (bf16[32,4224]{1,0:T(8,128)(2,1)S(1)}, bf16[32,4224]{1,0:T(8,128)(2,1)S(1)}, u32[]{:S(2)}, u32[]{:S(2)}) collective-permute-start(bf16[32,4224]{1,0:T(8,128)(2,1)S(1)} %collective-permute-done.2), channel_id=1, source_target_pairs={{0,8},{8,0},{16,24},{24,16},{1,9},{9,1},{17,25},{25,17},{2,10},{10... | collective-permute-start | bytes 811016 | tf_op jit(solution)/shard_map/ppermute | solution.py:20
  30.9 9.9 %collective-permute-start.8 = (bf16[32,4224]{1,0:T(8,128)(2,1)S(1)}, bf16[32,4224]{1,0:T(8,128)(2,1)S(1)}, u32[]{:S(2)}, u32[]{:S(2)}) collective-permute-start(bf16[32,4224]{1,0:T(8,128)(2,1)S(1)} %collective-permute-done.3), channel_id=1, source_target_pairs={{0,2},{1,3},{2,0},{3,1},{4,6},{5,7},{6,4},{7,5},{8,10},{9,11},{10,... | collective-permute-start | bytes 811016 | tf_op jit(solution)/shard_map/ppermute | solution.py:223
  32.4 8.3 %collective-permute-start.7 = (bf16[32,4224]{1,0:T(8,128)(2,1)S(1)}, bf16[32,4224]{1,0:T(8,128)(2,1)S(1)}, u32[]{:S(2)}, u32[]{:S(2)}) collective-permute-start(bf16[32,4224]{1,0:T(8,128)(2,1)S(1)} %collective-permute-done.3), channel_id=1, source_target_pairs={{0,16},{16,0},{8,24},{24,8},{1,17},{17,1},{9,25},{25,9},{2,18},{18... | collective-permute-start | bytes 811016 | tf_op jit(solution)/shard_map/ppermute | solution.py:20
  40.8 7.3 %collective-permute-start.14 = (bf16[16,4224]{1,0:T(8,128)(2,1)S(1)}, bf16[16,4224]{1,0:T(8,128)(2,1)S(1)}, u32[]{:S(2)}, u32[]{:S(2)}) collective-permute-start(bf16[16,4224]{1,0:T(8,128)(2,1)S(1)} %get-tuple-element.157), channel_id=1, source_target_pairs={{0,16},{16,0},{8,24},{24,8},{1,17},{17,1},{9,25},{25,9},{2,18},{18... | collective-permute-start | bytes 405512 | tf_op jit(solution)/shard_map/ppermute | solution.py:20
  42.4 6.5 %collective-permute-start.13 = (bf16[16,4224]{1,0:T(8,128)(2,1)S(1)}, bf16[16,4224]{1,0:T(8,128)(2,1)S(1)}, u32[]{:S(2)}, u32[]{:S(2)}) collective-permute-start(bf16[16,4224]{1,0:T(8,128)(2,1)S(1)} %get-tuple-element.158), channel_id=1, source_target_pairs={{0,8},{8,0},{16,24},{24,16},{1,9},{9,1},{17,25},{25,17},{2,10},{10... | collective-permute-start | bytes 405512 | tf_op jit(solution)/shard_map/ppermute | solution.py:20
  43.9 13.6 %collective-permute-start.11 = (bf16[64,4224]{1,0:T(8,128)(2,1)S(1)}, bf16[64,4224]{1,0:T(8,128)(2,1)S(1)}, u32[]{:S(2)}, u32[]{:S(2)}) collective-permute-start(bf16[64,4224]{1,0:T(8,128)(2,1)S(1)} %pad_maximum_fusion.refs_0_), channel_id=1, source_target_pairs={{0,16},{16,0},{8,24},{24,8},{1,17},{17,1},{9,25},{25,9},{2,18},{18... | collective-permute-start | bytes 1622024 | tf_op jit(solution)/shard_map/ppermute | solution.py:20
  44.4 13.9 %collective-permute-start.12 = (bf16[64,4224]{1,0:T(8,128)(2,1)S(1)}, bf16[64,4224]{1,0:T(8,128)(2,1)S(1)}, u32[]{:S(2)}, u32[]{:S(2)}) collective-permute-start(bf16[64,4224]{1,0:T(8,128)(2,1)S(1)} %pad_maximum_fusion.1.refs_2_), channel_id=1, source_target_pairs={{0,8},{8,0},{16,24},{24,16},{1,9},{9,1},{17,25},{25,17},{2,10},{10... | collective-permute-start | bytes 1622024 | tf_op jit(solution)/shard_map/ppermute | solution.py:20
  58.3 7.8 %collective-permute-start.15 = (bf16[32,4224]{1,0:T(8,128)(2,1)S(1)}, bf16[32,4224]{1,0:T(8,128)(2,1)S(1)}, u32[]{:S(2)}, u32[]{:S(2)}) collective-permute-start(bf16[32,4224]{1,0:T(8,128)(2,1)S(1)} %pad_maximum_fusion.4.refs_0_), channel_id=1, source_target_pairs={{0,16},{16,0},{8,24},{24,8},{1,17},{17,1},{9,25},{25,9},{2,18},{18... | collective-permute-start | bytes 811016 | tf_op jit(solution)/shard_map/ppermute | solution.py:20
  59.5 6.6 %collective-permute-start.16 = (bf16[32,4224]{1,0:T(8,128)(2,1)S(1)}, bf16[32,4224]{1,0:T(8,128)(2,1)S(1)}, u32[]{:S(2)}, u32[]{:S(2)}) collective-permute-start(bf16[32,4224]{1,0:T(8,128)(2,1)S(1)} %pad_maximum_fusion.5.refs_2_), channel_id=1, source_target_pairs={{0,8},{8,0},{16,24},{24,16},{1,9},{9,1},{17,25},{25,17},{2,10},{10... | collective-permute-start | bytes 811016 | tf_op jit(solution)/shard_map/ppermute | solution.py:20
  69.2 9.3 %collective-permute-start.23 = (bf16[32,4096]{1,0:T(8,128)(2,1)S(1)}, bf16[32,4096]{1,0:T(8,128)(2,1)S(1)}, u32[]{:S(2)}, u32[]{:S(2)}) collective-permute-start(bf16[32,4096]{1,0:T(8,128)(2,1)S(1)} %get-tuple-element.135), channel_id=1, source_target_pairs={{0,16},{16,0},{8,24},{24,8},{1,17},{17,1},{9,25},{25,9},{2,18},{18... | collective-permute-start | bytes 786440 | tf_op jit(solution)/shard_map/ppermute | solution.py:20
  70.7 9.2 %collective-permute-start.25 = (bf16[32,4096]{1,0:T(8,128)(2,1)S(1)}, bf16[32,4096]{1,0:T(8,128)(2,1)S(1)}, u32[]{:S(2)}, u32[]{:S(2)}) collective-permute-start(bf16[32,4096]{1,0:T(8,128)(2,1)S(1)} %get-tuple-element.137), channel_id=1, source_target_pairs={{0,8},{8,0},{16,24},{24,16},{1,9},{9,1},{17,25},{25,17},{2,10},{10... | collective-permute-start | bytes 786440 | tf_op jit(solution)/shard_map/ppermute | solution.py:20
  71.4 18.7 %collective-permute-start.17 = (bf16[64,4096]{1,0:T(8,128)(2,1)S(1)}, bf16[64,4096]{1,0:T(8,128)(2,1)S(1)}, u32[]{:S(2)}, u32[]{:S(2)}) collective-permute-start(bf16[64,4096]{1,0:T(8,128)(2,1)S(1)} %get-tuple-element.123), channel_id=1, source_target_pairs={{0,16},{16,0},{8,24},{24,8},{1,17},{17,1},{9,25},{25,9},{2,18},{18... | collective-permute-start | bytes 1572872 | tf_op jit(solution)/shard_map/ppermute | solution.py:20
  72.5 17.8 %collective-permute-start.18 = (bf16[64,4096]{1,0:T(8,128)(2,1)S(1)}, bf16[64,4096]{1,0:T(8,128)(2,1)S(1)}, u32[]{:S(2)}, u32[]{:S(2)}) collective-permute-start(bf16[64,4096]{1,0:T(8,128)(2,1)S(1)} %get-tuple-element.125), channel_id=1, source_target_pairs={{0,8},{8,0},{16,24},{24,16},{1,9},{9,1},{17,25},{25,17},{2,10},{10... | collective-permute-start | bytes 1572872 | tf_op jit(solution)/shard_map/ppermute | solution.py:20
  78.6 11.4 %collective-permute-start.24 = (bf16[16,4096]{1,0:T(8,128)(2,1)S(1)}, bf16[16,4096]{1,0:T(8,128)(2,1)S(1)}, u32[]{:S(2)}, u32[]{:S(2)}) collective-permute-start(bf16[16,4096]{1,0:T(8,128)(2,1)S(1)} %split.51), channel_id=1, source_target_pairs={{0,8},{8,0},{16,24},{24,16},{1,9},{9,1},{17,25},{25,17},{2,10},{10... | collective-permute-start | bytes 393224 | tf_op jit(solution)/shard_map/ppermute | solution.py:20
  80.1 10.0 %collective-permute-start.26 = (bf16[16,4096]{1,0:T(8,128)(2,1)S(1)}, bf16[16,4096]{1,0:T(8,128)(2,1)S(1)}, u32[]{:S(2)}, u32[]{:S(2)}) collective-permute-start(bf16[16,4096]{1,0:T(8,128)(2,1)S(1)} %split.53), channel_id=1, source_target_pairs={{0,16},{16,0},{8,24},{24,8},{1,17},{17,1},{9,25},{25,9},{2,18},{18... | collective-permute-start | bytes 393224 | tf_op jit(solution)/shard_map/ppermute | solution.py:20
  90.5 7.2 %collective-permute-start.20 = (bf16[32,4096]{1,0:T(8,128)(2,1)S(1)}, bf16[32,4096]{1,0:T(8,128)(2,1)S(1)}, u32[]{:S(2)}, u32[]{:S(2)}) collective-permute-start(bf16[32,4096]{1,0:T(8,128)(2,1)S(1)} %split.39), channel_id=1, source_target_pairs={{0,16},{16,0},{8,24},{24,8},{1,17},{17,1},{9,25},{25,9},{2,18},{18... | collective-permute-start | bytes 786440 | tf_op jit(solution)/shard_map/ppermute | solution.py:20
  91.3 7.5 %collective-permute-start.27 = (bf16[32,4096]{1,0:T(8,128)(2,1)S(1)}, bf16[32,4096]{1,0:T(8,128)(2,1)S(1)}, u32[]{:S(2)}, u32[]{:S(2)}) collective-permute-start(bf16[32,4096]{1,0:T(8,128)(2,1)S(1)} %pad_maximum_fusion.6), channel_id=1, source_target_pairs={{0,2},{1,3},{2,0},{3,1},{4,6},{5,7},{6,4},{7,5},{8,10},{9,11},{10,... | collective-permute-start | bytes 786440 | tf_op jit(solution)/shard_map/ppermute | solution.py:223
  92.2 6.4 %collective-permute-start.19 = (bf16[32,4096]{1,0:T(8,128)(2,1)S(1)}, bf16[32,4096]{1,0:T(8,128)(2,1)S(1)}, u32[]{:S(2)}, u32[]{:S(2)}) collective-permute-start(bf16[32,4096]{1,0:T(8,128)(2,1)S(1)} %split.37), channel_id=1, source_target_pairs={{0,8},{8,0},{16,24},{24,16},{1,9},{9,1},{17,25},{25,17},{2,10},{10... | collective-permute-start | bytes 786440 | tf_op jit(solution)/shard_map/ppermute | solution.py:20
  98.7 6.5 %collective-permute-start.21 = (bf16[32,4096]{1,0:T(8,128)(2,1)S(1)}, bf16[32,4096]{1,0:T(8,128)(2,1)S(1)}, u32[]{:S(2)}, u32[]{:S(2)}) collective-permute-start(bf16[32,4096]{1,0:T(8,128)(2,1)S(1)} %get-tuple-element.145), channel_id=1, source_target_pairs={{0,16},{16,0},{8,24},{24,8},{1,17},{17,1},{9,25},{25,9},{2,18},{18... | collective-permute-start | bytes 786440 | tf_op jit(solution)/shard_map/ppermute | solution.py:20
  99.9 11.8 %collective-permute-start.28 = (bf16[32,4096]{1,0:T(8,128)(2,1)S(1)}, bf16[32,4096]{1,0:T(8,128)(2,1)S(1)}, u32[]{:S(2)}, u32[]{:S(2)}) collective-permute-start(bf16[32,4096]{1,0:T(8,128)(2,1)S(1)} %add_convert_fusion.3), channel_id=1, source_target_pairs={{0,4},{1,5},{2,6},{3,7},{4,0},{5,1},{6,2},{7,3},{8,12},{9,13},{10,... | collective-permute-start | bytes 786440 | tf_op jit(solution)/shard_map/ppermute | solution.py:223
  102.9 8.9 %collective-permute-start.29 = (bf16[32,4096]{1,0:T(8,128)(2,1)S(1)}, bf16[32,4096]{1,0:T(8,128)(2,1)S(1)}, u32[]{:S(2)}, u32[]{:S(2)}) collective-permute-start(bf16[32,4096]{1,0:T(8,128)(2,1)S(1)} %add_convert_fusion.8), channel_id=1, source_target_pairs={{0,2},{1,3},{2,0},{3,1},{4,6},{5,7},{6,4},{7,5},{8,10},{9,11},{10,... | collective-permute-start | bytes 786440 | tf_op jit(solution)/shard_map/ppermute | solution.py:223
  104.5 6.4 %collective-permute-start.30 = (bf16[32,4096]{1,0:T(8,128)(2,1)S(1)}, bf16[32,4096]{1,0:T(8,128)(2,1)S(1)}, u32[]{:S(2)}, u32[]{:S(2)}) collective-permute-start(bf16[32,4096]{1,0:T(8,128)(2,1)S(1)} %get-tuple-element.152), channel_id=1, source_target_pairs={{0,8},{8,0},{16,24},{24,16},{1,9},{9,1},{17,25},{25,17},{2,10},{10... | collective-permute-start | bytes 786440 | tf_op jit(solution)/shard_map/ppermute | solution.py:20
  105.3 6.9 %collective-permute-start.22 = (bf16[16,4096]{1,0:T(8,128)(2,1)S(1)}, bf16[16,4096]{1,0:T(8,128)(2,1)S(1)}, u32[]{:S(2)}, u32[]{:S(2)}) collective-permute-start(bf16[16,4096]{1,0:T(8,128)(2,1)S(1)} %split.49), channel_id=1, source_target_pairs={{0,8},{8,0},{16,24},{24,16},{1,9},{9,1},{17,25},{25,17},{2,10},{10... | collective-permute-start | bytes 393224 | tf_op jit(solution)/shard_map/ppermute | solution.py:20
  110.9 5.0 %collective-permute-start.31 = (bf16[16,4096]{1,0:T(8,128)(2,1)S(1)}, bf16[16,4096]{1,0:T(8,128)(2,1)S(1)}, u32[]{:S(2)}, u32[]{:S(2)}) collective-permute-start(bf16[16,4096]{1,0:T(8,128)(2,1)S(1)} %split.55), channel_id=1, source_target_pairs={{0,16},{16,0},{8,24},{24,8},{1,17},{17,1},{9,25},{25,9},{2,18},{18... | collective-permute-start | bytes 393224 | tf_op jit(solution)/shard_map/ppermute | solution.py:20
  (6 other events, 42.8 us)

commit v14 on v13

--- a/solution.py
+++ b/solution.py
@@ -99,64 +99,78 @@
     return (block.astype(jnp.float32) * scale).astype(jnp.bfloat16)
 
 
-def in_kernel(gate_scales, up_scales, gate_ref, up_ref, out_ref):
-    strip, cols = gate_ref.shape
-    first = pl.program_id(0) * (strip // BLOCK)
-    for row in range(strip // BLOCK):
-        rows = slice(row * BLOCK, (row + 1) * BLOCK)
-        for col in range(cols // BLOCK):
-            at = slice(col * BLOCK, (col + 1) * BLOCK)
-            to = 2 * col * BLOCK
-            out_ref[rows, to : to + BLOCK] = scaled(gate_ref[rows, at], gate_scales[col, first + row])
-            to += BLOCK
-            out_ref[rows, to : to + BLOCK] = scaled(up_ref[rows, at], up_scales[col, first + row])
-
-
-def dequantize_in(gate, up, gate_scales, up_scales):
+def dequantize_kernel(gate_scales, up_scales, down_scales, gate, up, down, in_out, down_out, *scratch):
+    gate_raw, up_raw, down_raw, in_sems, down_sems = scratch
     rows, cols = gate.shape
-    strip = min(rows, 8 * BLOCK)
-    block = pl.BlockSpec((strip, cols), lambda i: (i, 0))
-    smem = pl.BlockSpec(memory_space=pltpu.SMEM)
+    chunks, down_chunks = in_sems.shape[1], down_sems.shape[0]
+    depth, down_depth = rows // chunks, down.shape[0] // down_chunks
+
+    def in_copy(part, chunk):
+        source, target = ((gate, gate_raw), (up, up_raw))[part]
+        at = pl.ds(pl.multiple_of(chunk * depth, depth), depth)
+        return pltpu.make_async_copy(source.at[at], target.at[at], in_sems.at[part, chunk])
+
+    def down_copy(chunk):
+        at = pl.ds(pl.multiple_of(chunk * down_depth, down_depth), down_depth)
+        return pltpu.make_async_copy(down.at[at], down_raw.at[at], down_sems.at[chunk])
+
+    for chunk in range(chunks):
+        for part in range(2):
+            in_copy(part, chunk).start()
+    for chunk in range(down_chunks):
+        down_copy(chunk).start()
+
+    @pl.loop(0, chunks)
+    def _(chunk):
+        in_copy(0, chunk).wait()
+        in_copy(1, chunk).wait()
+        for block in range(depth // BLOCK):
+            row = chunk * (depth // BLOCK) + block
+            at = pl.ds(pl.multiple_of(row * BLOCK, BLOCK), BLOCK)
+            for col in range(cols // BLOCK):
+                from_cols = slice(col * BLOCK, (col + 1) * BLOCK)
+                to = 2 * col * BLOCK
+                value = scaled(gate_raw[at, from_cols], gate_scales[col, row])
+                in_out[at, to : to + BLOCK] = value
+                to += BLOCK
+                value = scaled(up_raw[at, from_cols], up_scales[col, row])
+                in_out[at, to : to + BLOCK] = value
+
+    @pl.loop(0, down_chunks)
+    def _(chunk):
+        down_copy(chunk).wait()
+        for block in range(down_depth // BLOCK):
+            row = chunk * (down_depth // BLOCK) + block
+            at = pl.ds(pl.multiple_of(row * BLOCK, BLOCK), BLOCK)
+            for col in range(down.shape[1] // BLOCK):
+                cols_at = slice(col * BLOCK, (col + 1) * BLOCK)
+                down_out[at, cols_at] = scaled(down_raw[at, cols_at], down_scales[row, col])
+
+
+def dequantize_half(quants, scales):
+    rows, cols = quants[0].shape
+    chunks, down_chunks = max(1, rows // (4 * BLOCK)), max(1, cols // BLOCK)
+    quants = [pltpu.with_memory_space_constraint(quant, pltpu.HBM) for quant in quants]
+    whole = pl.BlockSpec(memory_space=pltpu.VMEM)
     return pl.pallas_call(
-        in_kernel,
-        grid=(rows // strip,),
-        in_specs=[smem, smem, block, block],
-        out_specs=pl.BlockSpec((strip, 2 * cols), lambda i: (i, 0)),
-        out_shape=jax.ShapeDtypeStruct((rows, 2 * cols), jnp.bfloat16),
+        dequantize_kernel,
+        in_specs=[pl.BlockSpec(memory_space=pltpu.SMEM)] * 3 + [pl.BlockSpec(memory_space=pl.ANY)] * 3,
+        out_specs=[whole] * 2,
+        out_shape=[
+            jax.ShapeDtypeStruct((rows, 2 * cols), jnp.bfloat16),
+            jax.ShapeDtypeStruct(quants[2].shape, jnp.bfloat16),
+        ],
+        scratch_shapes=[
+            *(pltpu.VMEM(quant.shape, jnp.bfloat16) for quant in quants),
+            pltpu.SemaphoreType.DMA((2, chunks)),
+            pltpu.SemaphoreType.DMA((down_chunks,)),
+        ],
         cost_estimate=pl.CostEstimate(
-            flops=2 * rows * cols, bytes_accessed=8 * rows * cols, transcendentals=0
+            flops=3 * rows * cols, bytes_accessed=12 * rows * cols, transcendentals=0
         ),
-        compiler_params=pltpu.CompilerParams(vmem_limit_bytes=8 * 1024 * 1024),
-        name="dequantize_in",
-    )(gate_scales.T, up_scales.T, gate, up)
-
-
-def down_kernel(scales, down_ref, out_ref):
-    strip = down_ref.shape[1] // BLOCK
-    first = pl.program_id(0) * strip
-    for row in range(down_ref.shape[0] // BLOCK):
-        rows = slice(row * BLOCK, (row + 1) * BLOCK)
-        for col in range(strip):
-            cols = slice(col * BLOCK, (col + 1) * BLOCK)
-            out_ref[rows, cols] = scaled(down_ref[rows, cols], scales[row, first + col])
-
-
-def dequantize_down(down, scales):
-    rows, cols = down.shape
-    strip = min(cols, 8 * BLOCK)
-    block = pl.BlockSpec((rows, strip), lambda i: (0, i))
-    return pl.pallas_call(
-        down_kernel,
-        grid=(cols // strip,),
-        in_specs=[pl.BlockSpec(memory_space=pltpu.SMEM), block],
-        out_specs=block,
-        out_shape=jax.ShapeDtypeStruct((rows, cols), jnp.bfloat16),
-        cost_estimate=pl.CostEstimate(
-            flops=rows * cols, bytes_accessed=4 * rows * cols, transcendentals=0
-        ),
-        compiler_params=pltpu.CompilerParams(vmem_limit_bytes=8 * 1024 * 1024),
-        name="dequantize_down",
-    )(scales, down)
+        compiler_params=pltpu.CompilerParams(vmem_limit_bytes=24 * 1024 * 1024),
+        name="dequantize_half",
+    )(*scales, *quants)
 
 
 def silu(v):
@@ -272,17 +286,18 @@
 
     place, payload = together((place, payload))
     lanes, outs = {0: payload}, {}
-    came = {0: jnp.concatenate(payload, axis=0)}
-    for far in groups[1]:
-        along_z(far)
+    near = [{far: across_chips(payload[0], far) for far in groups[1]}]
     gather_turn(0, 0)
-    in_own = dequantize_in(gate_q[0], up_q[0], gate_scale[0], up_scale[0])
-    down_own = dequantize_down(down_q[0], down_scale[0])
-    lanes, came, in_own, down_own = together((lanes, came, in_own, down_own))
+    in_own, down_own = dequantize_half(
+        (gate_q[0], up_q[0], down_q[0]), (gate_scale[0].T, up_scale[0].T, down_scale[0])
+    )
+    lanes, near, payload, in_own, down_own = together((lanes, near, payload, in_own, down_own))
     in_other = from_partner(in_own, "expert", 0)
+    near.append({far: across_chips(payload[1], far) for far in groups[1]})
     for turn in range(1, turns):
         gather_turn(0, turn)
-    lanes, came, down_own = together((lanes, came, down_own))
+    lanes, near, down_own = together((lanes, near, down_own))
+    came = {far: jnp.concatenate([part[far] for part in near], axis=0) for far in groups[1]}
     down_other = from_partner(down_own, "expert", 0)
     lanes[1] = lanes_of(groups[1])
     for number in range(1, len(groups)):
@@ -303,7 +318,8 @@
             lanes[number + 1] = lanes_of(following)
             gather_turn(number + 1, 0)
         outs[number - 1] = layer(number - 1)
-        lanes, outs, came = together((lanes, outs, came))
+        if number + 2 != len(groups):
+            lanes, outs, came = together((lanes, outs, came))
     final = len(groups) - 1
     outs[final] = layer(final)
 

time: 117 us -> 112 us (0.957)
  waiting for transfers between devices: 54.2 us -> 49.5 us
  local copies, waits for them, and re-layouts: 4.95 us -> 1.44 us
  starting transfers between devices: 39 us -> 40.9 us
  Pallas kernels: 15.8 us -> 17.3 us
    ppermute x26, waiting for transfers between devices: 51.1 us -> 42.8 us  [from_partner(): return lax.ppermute(block, axis, route)]
    ppermute x6 -> x8, waiting for transfers between devices: 3.05 us -> 6.65 us  [across_chips(): lax.ppermute(block, 'expert', [(low, low ^ 2 * far) for low in range(coun...]
    unnamed x14 -> x11, local copies, waits for them, and re-layouts: 3.57 us -> 0.04 us
    pallas_call x2 -> x1, Pallas kernels: 3.78 us -> 5.28 us  [dequantize_half(): pl.pallas_call(dequantize_kernel, in_specs=[pl.BlockSpec(memory_space=plt...]
    ppermute x6 -> x8, starting transfers between devices: 11.2 us -> 12.1 us  [across_chips(): lax.ppermute(block, 'expert', [(low, low ^ 2 * far) for low in range(coun...]
  transfers between devices with their start and end apart: 32 -> 34, of which waited for: 17 -> 13; matrix products, arithmetic and copies ran while one was open for 1% -> 1% of each run, Pallas kernels for 11% -> 13%
where the time goes in v14:
time: 112 us
  waiting for transfers between devices  49.5 us (44%)
  starting transfers between devices  40.9 us (37%)
  Pallas kernels  17.3 us (15%)
  other arithmetic  2.6 us (2%)
  local copies, waits for them, and re-layouts  1.44 us (1%)
    ppermute x26, waiting for transfers between devices, from_partner(): return lax.ppermute(block, axis, route)  42.8 us
    ppermute x26, starting transfers between devices, from_partner(): return lax.ppermute(block, axis, route)  28.9 us
    ppermute x8, starting transfers between devices, across_chips(): lax.ppermute(block, 'expert', [(low, low ^ 2 * far) for low in range(coun...  12.1 us
    pallas_call x3, Pallas kernels, expert_layer(): pl.pallas_call(functools.partial(expert_kernel, count, experts), in_specs...  12 us
    ppermute x8, waiting for transfers between devices, across_chips(): lax.ppermute(block, 'expert', [(low, low ^ 2 * far) for low in range(coun...  6.65 us
    pallas_call x1, Pallas kernels, dequantize_half(): pl.pallas_call(dequantize_kernel, in_specs=[pl.BlockSpec(memory_space=plt...  5.28 us
  transfers between devices with their start and end apart: 34, of which 13 were waited for; matrix products, arithmetic and copies ran while one was open for 1% of the time, Pallas kernels for 13%

profile of v14, /device:TPU:0, one launch (start us, length us, event | category | flops | bytes accessed | tf_op | source)
XLA Modules:
  0.0 112.1 jit_solution(16922270099655137607)
XLA Ops:
  2.1 4.0 %collective-permute-start.3 = (bf16[16,4224]{1,0:T(8,128)(2,1)S(1)}, bf16[16,4224]{1,0:T(8,128)(2,1)S(1)}, u32[]{:S(2)}, u32[]{:S(2)}) collective-permute-start(bf16[16,4224]{1,0:T(8,128)(2,1)S(1)} %concatenate.38), channel_id=1, source_target_pairs={{0,4},{1,5},{2,6},{3,7},{4,0},{5,1},{6,2},{7,3},{8,12},{9,13},{10,... | collective-permute-start | bytes 405512 | tf_op jit(solution)/shard_map/ppermute | solution.py:237
  6.1 1.6 %collective-permute-start.2 = (bf16[16,4224]{1,0:T(8,128)(2,1)S(1)}, bf16[16,4224]{1,0:T(8,128)(2,1)S(1)}, u32[]{:S(2)}, u32[]{:S(2)}) collective-permute-start(bf16[16,4224]{1,0:T(8,128)(2,1)S(1)} %concatenate.38), channel_id=1, source_target_pairs={{0,2},{1,3},{2,0},{3,1},{4,6},{5,7},{6,4},{7,5},{8,10},{9,11},{10,... | collective-permute-start | bytes 405512 | tf_op jit(solution)/shard_map/ppermute | solution.py:237
  7.7 1.5 %collective-permute-start = (bf16[16,4224]{1,0:T(8,128)(2,1)S(1)}, bf16[16,4224]{1,0:T(8,128)(2,1)S(1)}, u32[]{:S(2)}, u32[]{:S(2)}) collective-permute-start(bf16[16,4224]{1,0:T(8,128)(2,1)S(1)} %concatenate.38), channel_id=1, source_target_pairs={{0,8},{8,0},{16,24},{24,16},{1,9},{9,1},{17,25},{25,17},{2,10},{10... | collective-permute-start | bytes 405512 | tf_op jit(solution)/shard_map/ppermute | solution.py:20
  9.2 1.5 %collective-permute-start.1 = (bf16[16,4224]{1,0:T(8,128)(2,1)S(1)}, bf16[16,4224]{1,0:T(8,128)(2,1)S(1)}, u32[]{:S(2)}, u32[]{:S(2)}) collective-permute-start(bf16[16,4224]{1,0:T(8,128)(2,1)S(1)} %concatenate.39), channel_id=1, source_target_pairs={{0,16},{16,0},{8,24},{24,8},{1,17},{17,1},{9,25},{25,9},{2,18},{18... | collective-permute-start | bytes 405512 | tf_op jit(solution)/shard_map/ppermute | solution.py:20
  10.7 5.3 %dequantize_half.1 = (bf16[4096,768]{1,0:T(8,128)(2,1)S(1)}, bf16[384,4096]{1,0:T(8,128)(2,1)S(1)}) custom-call(f32[3,32]{1,0:T(4,128)S(1)} %get-tuple-element.158.gate_scales, f32[3,32]{1,0:T(4,128)S(1)} %get-tuple-element.157.up_scales, f32[3,32]{1,0:T(4,128)S(1)} %bitcast.15, bf16[4096,384]{1,0:T(8,128)(2,1)} %bitcast.16, bf16[4096,384]{1,0:T(8,128)(2,1)} %bitcast.17, ...), custom_call_target="tpu_custom_call" | custom-call | flops 4718592 | bytes 18874368 | tf_op jit(solution)/shard_map/dequantize_half/pallas_call | solution.py:155
  17.6 2.1 %collective-permute-start.6 = (bf16[16,4224]{1,0:T(8,128)(2,1)S(1)}, bf16[16,4224]{1,0:T(8,128)(2,1)S(1)}, u32[]{:S(2)}, u32[]{:S(2)}) collective-permute-start(bf16[16,4224]{1,0:T(8,128)(2,1)S(1)} %concatenate.39), channel_id=1, source_target_pairs={{0,2},{1,3},{2,0},{3,1},{4,6},{5,7},{6,4},{7,5},{8,10},{9,11},{10,... | collective-permute-start | bytes 405512 | tf_op jit(solution)/shard_map/ppermute | solution.py:237
  19.7 6.6 %collective-permute-done.7 = bf16[16,4224]{1,0:T(8,128)(2,1)S(1)} collective-permute-done((bf16[16,4224]{1,0:T(8,128)(2,1)S(1)}, bf16[16,4224]{1,0:T(8,128)(2,1)S(1)}, u32[]{:S(2)}, u32[]{:S(2)}) %collective-permute-start.7) | collective-permute-done | bytes 135200 | tf_op jit(solution)/shard_map/ppermute | solution.py:237
  26.6 1.6 %collective-permute-start.9 = (bf16[32,4224]{1,0:T(8,128)(2,1)S(1)}, bf16[32,4224]{1,0:T(8,128)(2,1)S(1)}, u32[]{:S(2)}, u32[]{:S(2)}) collective-permute-start(bf16[32,4224]{1,0:T(8,128)(2,1)S(1)} %constant_dynamic-update-slice_fusion.2), channel_id=1, source_target_pairs={{0,16},{16,0},{8,24},{24,8},{1,17},{17,1},{9,25},{25,9},{2,18},{18... | collective-permute-start | bytes 811016 | tf_op jit(solution)/shard_map/ppermute | solution.py:20
  28.2 1.6 %collective-permute-start.8 = (bf16[32,4224]{1,0:T(8,128)(2,1)S(1)}, bf16[32,4224]{1,0:T(8,128)(2,1)S(1)}, u32[]{:S(2)}, u32[]{:S(2)}) collective-permute-start(bf16[32,4224]{1,0:T(8,128)(2,1)S(1)} %constant_dynamic-update-slice_fusion), channel_id=1, source_target_pairs={{0,8},{8,0},{16,24},{24,16},{1,9},{9,1},{17,25},{25,17},{2,10},{10... | collective-permute-start | bytes 811016 | tf_op jit(solution)/shard_map/ppermute | solution.py:20
  29.7 5.8 %collective-permute-done.9 = bf16[32,4224]{1,0:T(8,128)(2,1)S(1)} collective-permute-done((bf16[32,4224]{1,0:T(8,128)(2,1)S(1)}, bf16[32,4224]{1,0:T(8,128)(2,1)S(1)}, u32[]{:S(2)}, u32[]{:S(2)}) %collective-permute-start.9) | collective-permute-done | bytes 270368 | tf_op jit(solution)/shard_map/ppermute | solution.py:20
  37.5 1.5 %collective-permute-start.15 = (bf16[16,4224]{1,0:T(8,128)(2,1)S(1)}, bf16[16,4224]{1,0:T(8,128)(2,1)S(1)}, u32[]{:S(2)}, u32[]{:S(2)}) collective-permute-start(bf16[16,4224]{1,0:T(8,128)(2,1)S(1)} %get-tuple-element.148), channel_id=1, source_target_pairs={{0,8},{8,0},{16,24},{24,16},{1,9},{9,1},{17,25},{25,17},{2,10},{10... | collective-permute-start | bytes 405512 | tf_op jit(solution)/shard_map/ppermute | solution.py:20
  39.0 1.5 %collective-permute-start.13 = (bf16[64,4224]{1,0:T(8,128)(2,1)S(1)}, bf16[64,4224]{1,0:T(8,128)(2,1)S(1)}, u32[]{:S(2)}, u32[]{:S(2)}) collective-permute-start(bf16[64,4224]{1,0:T(8,128)(2,1)S(1)} %pad_maximum_fusion.refs_0_), channel_id=1, source_target_pairs={{0,16},{16,0},{8,24},{24,8},{1,17},{17,1},{9,25},{25,9},{2,18},{18... | collective-permute-start | bytes 1622024 | tf_op jit(solution)/shard_map/ppermute | solution.py:20
  41.1 3.1 %expert_layer.3 = (bf16[32,4096]{1,0:T(8,128)(2,1)S(1)}, bf16[32,4096]{1,0:T(8,128)(2,1)S(1)}, bf16[32,4096]{1,0:T(8,128)(2,1)S(1)}, bf16[32,4096]{1,0:T(8,128)(2,1)S(1)}) custom-call(s32[1]{0:T(128)} %bitcast.own_expert, bf16[32,4224]{1,0:T(8,128)(2,1)S(1)} %pad_maximum_fusion.2.refs_0_, bf16[32,4224]{1,0:T(8,128)(2,1)S(1)} %collective-permute-done.4.refs_1_, ...), custom_call_target="tpu_custom_call" | custom-call | flops 2415919104 | bytes 20971520 | tf_op jit(solution)/shard_map/expert_layer/pallas_call | solution.py:216
  45.5 1.7 %collective-permute-start.18 = (bf16[32,4224]{1,0:T(8,128)(2,1)S(1)}, bf16[32,4224]{1,0:T(8,128)(2,1)S(1)}, u32[]{:S(2)}, u32[]{:S(2)}) collective-permute-start(bf16[32,4224]{1,0:T(8,128)(2,1)S(1)} %pad_maximum_fusion.5.refs_2_), channel_id=1, source_target_pairs={{0,8},{8,0},{16,24},{24,16},{1,9},{9,1},{17,25},{25,17},{2,10},{10... | collective-permute-start | bytes 811016 | tf_op jit(solution)/shard_map/ppermute | solution.py:20
  47.2 7.8 %collective-permute-done.13.refs_1_ = bf16[64,4224]{1,0:T(8,128)(2,1)S(1)} collective-permute-done((bf16[64,4224]{1,0:T(8,128)(2,1)S(1)}, bf16[64,4224]{1,0:T(8,128)(2,1)S(1)}, u32[]{:S(2)}, u32[]{:S(2)}) %collective-permute-start.13) | collective-permute-done | bytes 540704 | tf_op jit(solution)/shard_map/ppermute | solution.py:20
  55.8 5.7 %expert_layer.4 = (bf16[64,4096]{1,0:T(8,128)(2,1)S(1)}, bf16[64,4096]{1,0:T(8,128)(2,1)S(1)}, bf16[64,4096]{1,0:T(8,128)(2,1)S(1)}, bf16[64,4096]{1,0:T(8,128)(2,1)S(1)}) custom-call(s32[1]{0:T(128)} %bitcast.own_expert, bf16[64,4224]{1,0:T(8,128)(2,1)S(1)} %pad_maximum_fusion.refs_0_, bf16[64,4224]{1,0:T(8,128)(2,1)S(1)} %collective-permute-done.13.refs_1_, ...), custom_call_target="tpu_custom_call" | custom-call | flops 4831838208 | bytes 23068672 | tf_op jit(solution)/shard_map/expert_layer/pallas_call | solution.py:216
  61.5 3.1 %expert_layer.5 = (bf16[32,4096]{1,0:T(8,128)(2,1)S(1)}, bf16[32,4096]{1,0:T(8,128)(2,1)S(1)}, bf16[32,4096]{1,0:T(8,128)(2,1)S(1)}, bf16[32,4096]{1,0:T(8,128)(2,1)S(1)}) custom-call(s32[1]{0:T(128)} %bitcast.own_expert, bf16[32,4224]{1,0:T(8,128)(2,1)S(1)} %pad_maximum_fusion.4.refs_0_, bf16[32,4224]{1,0:T(8,128)(2,1)S(1)} %collective-permute-done.16.refs_1_, ...), custom_call_target="tpu_custom_call" | custom-call | flops 2415919104 | bytes 20971520 | tf_op jit(solution)/shard_map/expert_layer/pallas_call | solution.py:216
  64.7 1.3 %collective-permute-start.25 = (bf16[32,4096]{1,0:T(8,128)(2,1)S(1)}, bf16[32,4096]{1,0:T(8,128)(2,1)S(1)}, u32[]{:S(2)}, u32[]{:S(2)}) collective-permute-start(bf16[32,4096]{1,0:T(8,128)(2,1)S(1)} %get-tuple-element.125), channel_id=1, source_target_pairs={{0,16},{16,0},{8,24},{24,8},{1,17},{17,1},{9,25},{25,9},{2,18},{18... | collective-permute-start | bytes 786440 | tf_op jit(solution)/shard_map/ppermute | solution.py:20
  66.0 1.6 %collective-permute-start.27 = (bf16[32,4096]{1,0:T(8,128)(2,1)S(1)}, bf16[32,4096]{1,0:T(8,128)(2,1)S(1)}, u32[]{:S(2)}, u32[]{:S(2)}) collective-permute-start(bf16[32,4096]{1,0:T(8,128)(2,1)S(1)} %get-tuple-element.127), channel_id=1, source_target_pairs={{0,8},{8,0},{16,24},{24,16},{1,9},{9,1},{17,25},{25,17},{2,10},{10... | collective-permute-start | bytes 786440 | tf_op jit(solution)/shard_map/ppermute | solution.py:20
  68.8 5.2 %collective-permute-done.25 = bf16[32,4096]{1,0:T(8,128)(2,1)S(1)} collective-permute-done((bf16[32,4096]{1,0:T(8,128)(2,1)S(1)}, bf16[32,4096]{1,0:T(8,128)(2,1)S(1)}, u32[]{:S(2)}, u32[]{:S(2)}) %collective-permute-start.25) | collective-permute-done | bytes 262176 | tf_op jit(solution)/shard_map/ppermute | solution.py:20
  74.1 1.4 %collective-permute-start.26 = (bf16[16,4096]{1,0:T(8,128)(2,1)S(1)}, bf16[16,4096]{1,0:T(8,128)(2,1)S(1)}, u32[]{:S(2)}, u32[]{:S(2)}) collective-permute-start(bf16[16,4096]{1,0:T(8,128)(2,1)S(1)} %split.51), channel_id=1, source_target_pairs={{0,8},{8,0},{16,24},{24,16},{1,9},{9,1},{17,25},{25,17},{2,10},{10... | collective-permute-start | bytes 393224 | tf_op jit(solution)/shard_map/ppermute | solution.py:20
  75.6 1.6 %collective-permute-start.28 = (bf16[16,4096]{1,0:T(8,128)(2,1)S(1)}, bf16[16,4096]{1,0:T(8,128)(2,1)S(1)}, u32[]{:S(2)}, u32[]{:S(2)}) collective-permute-start(bf16[16,4096]{1,0:T(8,128)(2,1)S(1)} %split.53), channel_id=1, source_target_pairs={{0,16},{16,0},{8,24},{24,8},{1,17},{17,1},{9,25},{25,9},{2,18},{18... | collective-permute-start | bytes 393224 | tf_op jit(solution)/shard_map/ppermute | solution.py:20
  77.2 7.5 %collective-permute-done.26 = bf16[16,4096]{1,0:T(8,128)(2,1)S(1)} collective-permute-done((bf16[16,4096]{1,0:T(8,128)(2,1)S(1)}, bf16[16,4096]{1,0:T(8,128)(2,1)S(1)}, u32[]{:S(2)}, u32[]{:S(2)}) %collective-permute-start.26) | collective-permute-done | bytes 131104 | tf_op jit(solution)/shard_map/ppermute | solution.py:20
  86.1 2.1 %collective-permute-start.29 = (bf16[32,4096]{1,0:T(8,128)(2,1)S(1)}, bf16[32,4096]{1,0:T(8,128)(2,1)S(1)}, u32[]{:S(2)}, u32[]{:S(2)}) collective-permute-start(bf16[32,4096]{1,0:T(8,128)(2,1)S(1)} %pad_maximum_fusion.6), channel_id=1, source_target_pairs={{0,2},{1,3},{2,0},{3,1},{4,6},{5,7},{6,4},{7,5},{8,10},{9,11},{10,... | collective-permute-start | bytes 786440 | tf_op jit(solution)/shard_map/ppermute | solution.py:237
  89.3 2.6 %collective-permute-done.22 = bf16[32,4096]{1,0:T(8,128)(2,1)S(1)} collective-permute-done((bf16[32,4096]{1,0:T(8,128)(2,1)S(1)}, bf16[32,4096]{1,0:T(8,128)(2,1)S(1)}, u32[]{:S(2)}, u32[]{:S(2)}) %collective-permute-start.22) | collective-permute-done | bytes 262176 | tf_op jit(solution)/shard_map/ppermute | solution.py:20
  92.0 4.7 %collective-permute-done.21 = bf16[32,4096]{1,0:T(8,128)(2,1)S(1)} collective-permute-done((bf16[32,4096]{1,0:T(8,128)(2,1)S(1)}, bf16[32,4096]{1,0:T(8,128)(2,1)S(1)}, u32[]{:S(2)}, u32[]{:S(2)}) %collective-permute-start.21) | collective-permute-done | bytes 262176 | tf_op jit(solution)/shard_map/ppermute | solution.py:20
  97.9 1.8 %collective-permute-start.31 = (bf16[32,4096]{1,0:T(8,128)(2,1)S(1)}, bf16[32,4096]{1,0:T(8,128)(2,1)S(1)}, u32[]{:S(2)}, u32[]{:S(2)}) collective-permute-start(bf16[32,4096]{1,0:T(8,128)(2,1)S(1)} %add_convert_fusion.8), channel_id=1, source_target_pairs={{0,2},{1,3},{2,0},{3,1},{4,6},{5,7},{6,4},{7,5},{8,10},{9,11},{10,... | collective-permute-start | bytes 786440 | tf_op jit(solution)/shard_map/ppermute | solution.py:237
  100.4 3.9 %collective-permute-done.23 = bf16[32,4096]{1,0:T(8,128)(2,1)S(1)} collective-permute-done((bf16[32,4096]{1,0:T(8,128)(2,1)S(1)}, bf16[32,4096]{1,0:T(8,128)(2,1)S(1)}, u32[]{:S(2)}, u32[]{:S(2)}) %collective-permute-start.23) | collective-permute-done | bytes 262176 | tf_op jit(solution)/shard_map/ppermute | solution.py:20
  104.3 1.7 %collective-permute-start.24 = (bf16[16,4096]{1,0:T(8,128)(2,1)S(1)}, bf16[16,4096]{1,0:T(8,128)(2,1)S(1)}, u32[]{:S(2)}, u32[]{:S(2)}) collective-permute-start(bf16[16,4096]{1,0:T(8,128)(2,1)S(1)} %split.49), channel_id=1, source_target_pairs={{0,8},{8,0},{16,24},{24,16},{1,9},{9,1},{17,25},{25,17},{2,10},{10... | collective-permute-start | bytes 393224 | tf_op jit(solution)/shard_map/ppermute | solution.py:20
  106.2 1.8 %collective-permute-start.33 = (bf16[16,4096]{1,0:T(8,128)(2,1)S(1)}, bf16[16,4096]{1,0:T(8,128)(2,1)S(1)}, u32[]{:S(2)}, u32[]{:S(2)}) collective-permute-start(bf16[16,4096]{1,0:T(8,128)(2,1)S(1)} %split.55), channel_id=1, source_target_pairs={{0,16},{16,0},{8,24},{24,8},{1,17},{17,1},{9,25},{25,9},{2,18},{18... | collective-permute-start | bytes 393224 | tf_op jit(solution)/shard_map/ppermute | solution.py:20
  108.0 1.3 %collective-permute-done.24 = bf16[16,4096]{1,0:T(8,128)(2,1)S(1)} collective-permute-done((bf16[16,4096]{1,0:T(8,128)(2,1)S(1)}, bf16[16,4096]{1,0:T(8,128)(2,1)S(1)}, u32[]{:S(2)}, u32[]{:S(2)}) %collective-permute-start.24) | collective-permute-done | bytes 131104 | tf_op jit(solution)/shard_map/ppermute | solution.py:20
  109.3 1.9 %collective-permute-done.33 = bf16[16,4096]{1,0:T(8,128)(2,1)S(1)} collective-permute-done((bf16[16,4096]{1,0:T(8,128)(2,1)S(1)}, bf16[16,4096]{1,0:T(8,128)(2,1)S(1)}, u32[]{:S(2)}, u32[]{:S(2)}) %collective-permute-start.33) | collective-permute-done | bytes 131104 | tf_op jit(solution)/shard_map/ppermute | solution.py:20
  (89 shorter events, 15.3 us)
Async XLA Ops:
  2.1 14.0 %collective-permute-start.3 = (bf16[16,4224]{1,0:T(8,128)(2,1)S(1)}, bf16[16,4224]{1,0:T(8,128)(2,1)S(1)}, u32[]{:S(2)}, u32[]{:S(2)}) collective-permute-start(bf16[16,4224]{1,0:T(8,128)(2,1)S(1)} %concatenate.38), channel_id=1, source_target_pairs={{0,4},{1,5},{2,6},{3,7},{4,0},{5,1},{6,2},{7,3},{8,12},{9,13},{10,... | collective-permute-start | bytes 405512 | tf_op jit(solution)/shard_map/ppermute | solution.py:237
  6.1 10.0 %collective-permute-start.2 = (bf16[16,4224]{1,0:T(8,128)(2,1)S(1)}, bf16[16,4224]{1,0:T(8,128)(2,1)S(1)}, u32[]{:S(2)}, u32[]{:S(2)}) collective-permute-start(bf16[16,4224]{1,0:T(8,128)(2,1)S(1)} %concatenate.38), channel_id=1, source_target_pairs={{0,2},{1,3},{2,0},{3,1},{4,6},{5,7},{6,4},{7,5},{8,10},{9,11},{10,... | collective-permute-start | bytes 405512 | tf_op jit(solution)/shard_map/ppermute | solution.py:237
  7.7 8.4 %collective-permute-start = (bf16[16,4224]{1,0:T(8,128)(2,1)S(1)}, bf16[16,4224]{1,0:T(8,128)(2,1)S(1)}, u32[]{:S(2)}, u32[]{:S(2)}) collective-permute-start(bf16[16,4224]{1,0:T(8,128)(2,1)S(1)} %concatenate.38), channel_id=1, source_target_pairs={{0,8},{8,0},{16,24},{24,16},{1,9},{9,1},{17,25},{25,17},{2,10},{10... | collective-permute-start | bytes 405512 | tf_op jit(solution)/shard_map/ppermute | solution.py:20
  9.2 6.8 %collective-permute-start.1 = (bf16[16,4224]{1,0:T(8,128)(2,1)S(1)}, bf16[16,4224]{1,0:T(8,128)(2,1)S(1)}, u32[]{:S(2)}, u32[]{:S(2)}) collective-permute-start(bf16[16,4224]{1,0:T(8,128)(2,1)S(1)} %concatenate.39), channel_id=1, source_target_pairs={{0,16},{16,0},{8,24},{24,8},{1,17},{17,1},{9,25},{25,9},{2,18},{18... | collective-permute-start | bytes 405512 | tf_op jit(solution)/shard_map/ppermute | solution.py:20
  16.1 20.8 %collective-permute-start.11 = (bf16[4096,768]{1,0:T(8,128)(2,1)S(1)}, bf16[4096,768]{1,0:T(8,128)(2,1)S(1)}, u32[]{:S(2)}, u32[]{:S(2)}) collective-permute-start(bf16[4096,768]{1,0:T(8,128)(2,1)S(1)} %get-tuple-element.92.refs_4_), channel_id=1, source_target_pairs={{0,1},{1,0},{2,3},{3,2},{4,5},{5,4},{6,7},{7,6},{8,9},{9,8},{10,11... | collective-permute-start | bytes 18874376 | tf_op jit(solution)/shard_map/ppermute | solution.py:20
  16.2 10.2 %collective-permute-start.4 = (bf16[32,4224]{1,0:T(8,128)(2,1)S(1)}, bf16[32,4224]{1,0:T(8,128)(2,1)S(1)}, u32[]{:S(2)}, u32[]{:S(2)}) collective-permute-start(bf16[32,4224]{1,0:T(8,128)(2,1)S(1)} %pad_maximum_fusion.2.refs_0_), channel_id=1, source_target_pairs={{0,16},{16,0},{8,24},{24,8},{1,17},{17,1},{9,25},{25,9},{2,18},{18... | collective-permute-start | bytes 811016 | tf_op jit(solution)/shard_map/ppermute | solution.py:20
  16.8 9.6 %collective-permute-start.5 = (bf16[32,4224]{1,0:T(8,128)(2,1)S(1)}, bf16[32,4224]{1,0:T(8,128)(2,1)S(1)}, u32[]{:S(2)}, u32[]{:S(2)}) collective-permute-start(bf16[32,4224]{1,0:T(8,128)(2,1)S(1)} %pad_maximum_fusion.3.refs_2_), channel_id=1, source_target_pairs={{0,8},{8,0},{16,24},{24,16},{1,9},{9,1},{17,25},{25,17},{2,10},{10... | collective-permute-start | bytes 811016 | tf_op jit(solution)/shard_map/ppermute | solution.py:20
  17.3 9.1 %collective-permute-start.7 = (bf16[16,4224]{1,0:T(8,128)(2,1)S(1)}, bf16[16,4224]{1,0:T(8,128)(2,1)S(1)}, u32[]{:S(2)}, u32[]{:S(2)}) collective-permute-start(bf16[16,4224]{1,0:T(8,128)(2,1)S(1)} %concatenate.39), channel_id=1, source_target_pairs={{0,4},{1,5},{2,6},{3,7},{4,0},{5,1},{6,2},{7,3},{8,12},{9,13},{10,... | collective-permute-start | bytes 405512 | tf_op jit(solution)/shard_map/ppermute | solution.py:237
  17.6 8.7 %collective-permute-start.6 = (bf16[16,4224]{1,0:T(8,128)(2,1)S(1)}, bf16[16,4224]{1,0:T(8,128)(2,1)S(1)}, u32[]{:S(2)}, u32[]{:S(2)}) collective-permute-start(bf16[16,4224]{1,0:T(8,128)(2,1)S(1)} %concatenate.39), channel_id=1, source_target_pairs={{0,2},{1,3},{2,0},{3,1},{4,6},{5,7},{6,4},{7,5},{8,10},{9,11},{10,... | collective-permute-start | bytes 405512 | tf_op jit(solution)/shard_map/ppermute | solution.py:237
  26.4 10.5 %collective-permute-start.12 = (bf16[384,4096]{1,0:T(8,128)(2,1)S(1)}, bf16[384,4096]{1,0:T(8,128)(2,1)S(1)}, u32[]{:S(2)}, u32[]{:S(2)}) collective-permute-start(bf16[384,4096]{1,0:T(8,128)(2,1)S(1)} %get-tuple-element.93.refs_6_), channel_id=1, source_target_pairs={{0,1},{1,0},{2,3},{3,2},{4,5},{5,4},{6,7},{7,6},{8,9},{9,8},{10,11... | collective-permute-start | bytes 9437192 | tf_op jit(solution)/shard_map/ppermute | solution.py:20
  26.5 10.4 %collective-permute-start.10 = (bf16[32,4224]{1,0:T(8,128)(2,1)S(1)}, bf16[32,4224]{1,0:T(8,128)(2,1)S(1)}, u32[]{:S(2)}, u32[]{:S(2)}) collective-permute-start(bf16[32,4224]{1,0:T(8,128)(2,1)S(1)} %constant_dynamic-update-slice_fusion.2), channel_id=1, source_target_pairs={{0,2},{1,3},{2,0},{3,1},{4,6},{5,7},{6,4},{7,5},{8,10},{9,11},{10,... | collective-permute-start | bytes 811016 | tf_op jit(solution)/shard_map/ppermute | solution.py:237
  26.6 8.9 %collective-permute-start.9 = (bf16[32,4224]{1,0:T(8,128)(2,1)S(1)}, bf16[32,4224]{1,0:T(8,128)(2,1)S(1)}, u32[]{:S(2)}, u32[]{:S(2)}) collective-permute-start(bf16[32,4224]{1,0:T(8,128)(2,1)S(1)} %constant_dynamic-update-slice_fusion.2), channel_id=1, source_target_pairs={{0,16},{16,0},{8,24},{24,8},{1,17},{17,1},{9,25},{25,9},{2,18},{18... | collective-permute-start | bytes 811016 | tf_op jit(solution)/shard_map/ppermute | solution.py:20
  28.2 8.7 %collective-permute-start.8 = (bf16[32,4224]{1,0:T(8,128)(2,1)S(1)}, bf16[32,4224]{1,0:T(8,128)(2,1)S(1)}, u32[]{:S(2)}, u32[]{:S(2)}) collective-permute-start(bf16[32,4224]{1,0:T(8,128)(2,1)S(1)} %constant_dynamic-update-slice_fusion), channel_id=1, source_target_pairs={{0,8},{8,0},{16,24},{24,16},{1,9},{9,1},{17,25},{25,17},{2,10},{10... | collective-permute-start | bytes 811016 | tf_op jit(solution)/shard_map/ppermute | solution.py:20
  37.0 8.5 %collective-permute-start.17 = (bf16[16,4224]{1,0:T(8,128)(2,1)S(1)}, bf16[16,4224]{1,0:T(8,128)(2,1)S(1)}, u32[]{:S(2)}, u32[]{:S(2)}) collective-permute-start(bf16[16,4224]{1,0:T(8,128)(2,1)S(1)} %get-tuple-element.147), channel_id=1, source_target_pairs={{0,16},{16,0},{8,24},{24,8},{1,17},{17,1},{9,25},{25,9},{2,18},{18... | collective-permute-start | bytes 405512 | tf_op jit(solution)/shard_map/ppermute | solution.py:20
  37.5 6.7 %collective-permute-start.15 = (bf16[16,4224]{1,0:T(8,128)(2,1)S(1)}, bf16[16,4224]{1,0:T(8,128)(2,1)S(1)}, u32[]{:S(2)}, u32[]{:S(2)}) collective-permute-start(bf16[16,4224]{1,0:T(8,128)(2,1)S(1)} %get-tuple-element.148), channel_id=1, source_target_pairs={{0,8},{8,0},{16,24},{24,16},{1,9},{9,1},{17,25},{25,17},{2,10},{10... | collective-permute-start | bytes 405512 | tf_op jit(solution)/shard_map/ppermute | solution.py:20
  39.0 16.0 %collective-permute-start.13 = (bf16[64,4224]{1,0:T(8,128)(2,1)S(1)}, bf16[64,4224]{1,0:T(8,128)(2,1)S(1)}, u32[]{:S(2)}, u32[]{:S(2)}) collective-permute-start(bf16[64,4224]{1,0:T(8,128)(2,1)S(1)} %pad_maximum_fusion.refs_0_), channel_id=1, source_target_pairs={{0,16},{16,0},{8,24},{24,8},{1,17},{17,1},{9,25},{25,9},{2,18},{18... | collective-permute-start | bytes 1622024 | tf_op jit(solution)/shard_map/ppermute | solution.py:20
  40.5 15.2 %collective-permute-start.14 = (bf16[64,4224]{1,0:T(8,128)(2,1)S(1)}, bf16[64,4224]{1,0:T(8,128)(2,1)S(1)}, u32[]{:S(2)}, u32[]{:S(2)}) collective-permute-start(bf16[64,4224]{1,0:T(8,128)(2,1)S(1)} %pad_maximum_fusion.1.refs_2_), channel_id=1, source_target_pairs={{0,8},{8,0},{16,24},{24,16},{1,9},{9,1},{17,25},{25,17},{2,10},{10... | collective-permute-start | bytes 1622024 | tf_op jit(solution)/shard_map/ppermute | solution.py:20
  44.2 17.3 %collective-permute-start.16 = (bf16[32,4224]{1,0:T(8,128)(2,1)S(1)}, bf16[32,4224]{1,0:T(8,128)(2,1)S(1)}, u32[]{:S(2)}, u32[]{:S(2)}) collective-permute-start(bf16[32,4224]{1,0:T(8,128)(2,1)S(1)} %pad_maximum_fusion.4.refs_0_), channel_id=1, source_target_pairs={{0,16},{16,0},{8,24},{24,8},{1,17},{17,1},{9,25},{25,9},{2,18},{18... | collective-permute-start | bytes 811016 | tf_op jit(solution)/shard_map/ppermute | solution.py:20
  45.5 16.0 %collective-permute-start.18 = (bf16[32,4224]{1,0:T(8,128)(2,1)S(1)}, bf16[32,4224]{1,0:T(8,128)(2,1)S(1)}, u32[]{:S(2)}, u32[]{:S(2)}) collective-permute-start(bf16[32,4224]{1,0:T(8,128)(2,1)S(1)} %pad_maximum_fusion.5.refs_2_), channel_id=1, source_target_pairs={{0,8},{8,0},{16,24},{24,16},{1,9},{9,1},{17,25},{25,17},{2,10},{10... | collective-permute-start | bytes 811016 | tf_op jit(solution)/shard_map/ppermute | solution.py:20
  64.7 9.3 %collective-permute-start.25 = (bf16[32,4096]{1,0:T(8,128)(2,1)S(1)}, bf16[32,4096]{1,0:T(8,128)(2,1)S(1)}, u32[]{:S(2)}, u32[]{:S(2)}) collective-permute-start(bf16[32,4096]{1,0:T(8,128)(2,1)S(1)} %get-tuple-element.125), channel_id=1, source_target_pairs={{0,16},{16,0},{8,24},{24,8},{1,17},{17,1},{9,25},{25,9},{2,18},{18... | collective-permute-start | bytes 786440 | tf_op jit(solution)/shard_map/ppermute | solution.py:20
  66.0 9.5 %collective-permute-start.27 = (bf16[32,4096]{1,0:T(8,128)(2,1)S(1)}, bf16[32,4096]{1,0:T(8,128)(2,1)S(1)}, u32[]{:S(2)}, u32[]{:S(2)}) collective-permute-start(bf16[32,4096]{1,0:T(8,128)(2,1)S(1)} %get-tuple-element.127), channel_id=1, source_target_pairs={{0,8},{8,0},{16,24},{24,16},{1,9},{9,1},{17,25},{25,17},{2,10},{10... | collective-permute-start | bytes 786440 | tf_op jit(solution)/shard_map/ppermute | solution.py:20
  67.6 17.1 %collective-permute-start.19 = (bf16[64,4096]{1,0:T(8,128)(2,1)S(1)}, bf16[64,4096]{1,0:T(8,128)(2,1)S(1)}, u32[]{:S(2)}, u32[]{:S(2)}) collective-permute-start(bf16[64,4096]{1,0:T(8,128)(2,1)S(1)} %get-tuple-element.113), channel_id=1, source_target_pairs={{0,16},{16,0},{8,24},{24,8},{1,17},{17,1},{9,25},{25,9},{2,18},{18... | collective-permute-start | bytes 1572872 | tf_op jit(solution)/shard_map/ppermute | solution.py:20
  68.1 16.8 %collective-permute-start.20 = (bf16[64,4096]{1,0:T(8,128)(2,1)S(1)}, bf16[64,4096]{1,0:T(8,128)(2,1)S(1)}, u32[]{:S(2)}, u32[]{:S(2)}) collective-permute-start(bf16[64,4096]{1,0:T(8,128)(2,1)S(1)} %get-tuple-element.115), channel_id=1, source_target_pairs={{0,8},{8,0},{16,24},{24,16},{1,9},{9,1},{17,25},{25,17},{2,10},{10... | collective-permute-start | bytes 1572872 | tf_op jit(solution)/shard_map/ppermute | solution.py:20
  74.1 10.6 %collective-permute-start.26 = (bf16[16,4096]{1,0:T(8,128)(2,1)S(1)}, bf16[16,4096]{1,0:T(8,128)(2,1)S(1)}, u32[]{:S(2)}, u32[]{:S(2)}) collective-permute-start(bf16[16,4096]{1,0:T(8,128)(2,1)S(1)} %split.51), channel_id=1, source_target_pairs={{0,8},{8,0},{16,24},{24,16},{1,9},{9,1},{17,25},{25,17},{2,10},{10... | collective-permute-start | bytes 393224 | tf_op jit(solution)/shard_map/ppermute | solution.py:20
  75.6 9.1 %collective-permute-start.28 = (bf16[16,4096]{1,0:T(8,128)(2,1)S(1)}, bf16[16,4096]{1,0:T(8,128)(2,1)S(1)}, u32[]{:S(2)}, u32[]{:S(2)}) collective-permute-start(bf16[16,4096]{1,0:T(8,128)(2,1)S(1)} %split.53), channel_id=1, source_target_pairs={{0,16},{16,0},{8,24},{24,8},{1,17},{17,1},{9,25},{25,9},{2,18},{18... | collective-permute-start | bytes 393224 | tf_op jit(solution)/shard_map/ppermute | solution.py:20
  85.1 6.9 %collective-permute-start.22 = (bf16[32,4096]{1,0:T(8,128)(2,1)S(1)}, bf16[32,4096]{1,0:T(8,128)(2,1)S(1)}, u32[]{:S(2)}, u32[]{:S(2)}) collective-permute-start(bf16[32,4096]{1,0:T(8,128)(2,1)S(1)} %split.39), channel_id=1, source_target_pairs={{0,16},{16,0},{8,24},{24,8},{1,17},{17,1},{9,25},{25,9},{2,18},{18... | collective-permute-start | bytes 786440 | tf_op jit(solution)/shard_map/ppermute | solution.py:20
  86.1 10.7 %collective-permute-start.29 = (bf16[32,4096]{1,0:T(8,128)(2,1)S(1)}, bf16[32,4096]{1,0:T(8,128)(2,1)S(1)}, u32[]{:S(2)}, u32[]{:S(2)}) collective-permute-start(bf16[32,4096]{1,0:T(8,128)(2,1)S(1)} %pad_maximum_fusion.6), channel_id=1, source_target_pairs={{0,2},{1,3},{2,0},{3,1},{4,6},{5,7},{6,4},{7,5},{8,10},{9,11},{10,... | collective-permute-start | bytes 786440 | tf_op jit(solution)/shard_map/ppermute | solution.py:237
  88.2 8.5 %collective-permute-start.21 = (bf16[32,4096]{1,0:T(8,128)(2,1)S(1)}, bf16[32,4096]{1,0:T(8,128)(2,1)S(1)}, u32[]{:S(2)}, u32[]{:S(2)}) collective-permute-start(bf16[32,4096]{1,0:T(8,128)(2,1)S(1)} %split.37), channel_id=1, source_target_pairs={{0,8},{8,0},{16,24},{24,16},{1,9},{9,1},{17,25},{25,17},{2,10},{10... | collective-permute-start | bytes 786440 | tf_op jit(solution)/shard_map/ppermute | solution.py:20
  96.8 7.4 %collective-permute-start.23 = (bf16[32,4096]{1,0:T(8,128)(2,1)S(1)}, bf16[32,4096]{1,0:T(8,128)(2,1)S(1)}, u32[]{:S(2)}, u32[]{:S(2)}) collective-permute-start(bf16[32,4096]{1,0:T(8,128)(2,1)S(1)} %get-tuple-element.135), channel_id=1, source_target_pairs={{0,16},{16,0},{8,24},{24,8},{1,17},{17,1},{9,25},{25,9},{2,18},{18... | collective-permute-start | bytes 786440 | tf_op jit(solution)/shard_map/ppermute | solution.py:20
  97.9 10.1 %collective-permute-start.30 = (bf16[32,4096]{1,0:T(8,128)(2,1)S(1)}, bf16[32,4096]{1,0:T(8,128)(2,1)S(1)}, u32[]{:S(2)}, u32[]{:S(2)}) collective-permute-start(bf16[32,4096]{1,0:T(8,128)(2,1)S(1)} %add_convert_fusion.3), channel_id=1, source_target_pairs={{0,4},{1,5},{2,6},{3,7},{4,0},{5,1},{6,2},{7,3},{8,12},{9,13},{10,... | collective-permute-start | bytes 786440 | tf_op jit(solution)/shard_map/ppermute | solution.py:237
  97.9 10.0 %collective-permute-start.31 = (bf16[32,4096]{1,0:T(8,128)(2,1)S(1)}, bf16[32,4096]{1,0:T(8,128)(2,1)S(1)}, u32[]{:S(2)}, u32[]{:S(2)}) collective-permute-start(bf16[32,4096]{1,0:T(8,128)(2,1)S(1)} %add_convert_fusion.8), channel_id=1, source_target_pairs={{0,2},{1,3},{2,0},{3,1},{4,6},{5,7},{6,4},{7,5},{8,10},{9,11},{10,... | collective-permute-start | bytes 786440 | tf_op jit(solution)/shard_map/ppermute | solution.py:237
  99.8 6.4 %collective-permute-start.32 = (bf16[32,4096]{1,0:T(8,128)(2,1)S(1)}, bf16[32,4096]{1,0:T(8,128)(2,1)S(1)}, u32[]{:S(2)}, u32[]{:S(2)}) collective-permute-start(bf16[32,4096]{1,0:T(8,128)(2,1)S(1)} %get-tuple-element.142), channel_id=1, source_target_pairs={{0,8},{8,0},{16,24},{24,16},{1,9},{9,1},{17,25},{25,17},{2,10},{10... | collective-permute-start | bytes 786440 | tf_op jit(solution)/shard_map/ppermute | solution.py:20
  (6 other events, 55.6 us)

commit v15 on v14

--- a/solution.py
+++ b/solution.py
@@ -317,11 +317,13 @@
                     along_z(far)
             lanes[number + 1] = lanes_of(following)
             gather_turn(number + 1, 0)
+        if number + 1 == len(groups):
+            break
         outs[number - 1] = layer(number - 1)
         if number + 2 != len(groups):
             lanes, outs, came = together((lanes, outs, came))
     final = len(groups) - 1
-    outs[final] = layer(final)
+    sums, merged, parts = {}, {}, []
 
     def sum_turn(number, turn):
         result = []
@@ -349,7 +351,11 @@
                 whole = across_chips(block, low)
                 parts.append([whole[rows] for rows in halves])
 
-    sums, merged, parts = {}, {}, []
+    lanes, outs = together((lanes, outs))
+    sum_turn(0, turns - 1)
+    outs[final - 1] = layer(final - 1)
+    lanes, outs, sums = together((lanes, outs, sums))
+    outs[final] = layer(final)
     for number in range(final, 0, -1):
         for turn in range(turns - 1 - int(number < final), -1, -1):
             sum_turn(number, turn)
@@ -358,9 +364,8 @@
         if number > 1:
             leave(number)
         sums, outs = together((sums, outs))
-    sums, merged = together((sums, merged))
     leave(1)
-    for turn in range(turns - 1, -1, -1):
+    for turn in range(turns - 2, -1, -1):
         sum_turn(0, turn)
     result = []
     for lane, rows in enumerate(halves):

time: 112 us -> 112 us (level)
  waiting for transfers between devices: 49.5 us -> 54 us
  starting transfers between devices: 40.9 us -> 36.5 us
    ppermute x26, starting transfers between devices: 28.9 us -> 25.1 us  [from_partner(): return lax.ppermute(block, axis, route)]
    ppermute x8, waiting for transfers between devices: 6.65 us -> 8.97 us  [across_chips(): lax.ppermute(block, 'expert', [(low, low ^ 2 * far) for low in range(coun...]
    ppermute x26, waiting for transfers between devices: 42.8 us -> 45.1 us  [from_partner(): return lax.ppermute(block, axis, route)]
where the time goes in v15:
time: 112 us
  waiting for transfers between devices  54 us (48%)
  starting transfers between devices  36.5 us (33%)
  Pallas kernels  17.3 us (15%)
  other arithmetic  2.63 us (2%)
  local copies, waits for them, and re-layouts  1.44 us (1%)
    ppermute x26, waiting for transfers between devices, from_partner(): return lax.ppermute(block, axis, route)  45.1 us
    ppermute x26, starting transfers between devices, from_partner(): return lax.ppermute(block, axis, route)  25.1 us
    pallas_call x3, Pallas kernels, expert_layer(): pl.pallas_call(functools.partial(expert_kernel, count, experts), in_specs...  12 us
    ppermute x8, starting transfers between devices, across_chips(): lax.ppermute(block, 'expert', [(low, low ^ 2 * far) for low in range(coun...  11.4 us
    ppermute x8, waiting for transfers between devices, across_chips(): lax.ppermute(block, 'expert', [(low, low ^ 2 * far) for low in range(coun...  8.97 us
    pallas_call x1, Pallas kernels, dequantize_half(): pl.pallas_call(dequantize_kernel, in_specs=[pl.BlockSpec(memory_space=plt...  5.28 us
  transfers between devices with their start and end apart: 34, of which 13 were waited for; matrix products, arithmetic and copies ran while one was open for 1% of the time, Pallas kernels for 13%

profile of v15, /device:TPU:0, one launch (start us, length us, event | category | flops | bytes accessed | tf_op | source)
XLA Modules:
  0.0 112.3 jit_solution(11671129620588310264)
XLA Ops:
  2.1 4.0 %collective-permute-start.3 = (bf16[16,4224]{1,0:T(8,128)(2,1)S(1)}, bf16[16,4224]{1,0:T(8,128)(2,1)S(1)}, u32[]{:S(2)}, u32[]{:S(2)}) collective-permute-start(bf16[16,4224]{1,0:T(8,128)(2,1)S(1)} %concatenate.38), channel_id=1, source_target_pairs={{0,4},{1,5},{2,6},{3,7},{4,0},{5,1},{6,2},{7,3},{8,12},{9,13},{10,... | collective-permute-start | bytes 405512 | tf_op jit(solution)/shard_map/ppermute | solution.py:237
  6.1 1.6 %collective-permute-start.2 = (bf16[16,4224]{1,0:T(8,128)(2,1)S(1)}, bf16[16,4224]{1,0:T(8,128)(2,1)S(1)}, u32[]{:S(2)}, u32[]{:S(2)}) collective-permute-start(bf16[16,4224]{1,0:T(8,128)(2,1)S(1)} %concatenate.38), channel_id=1, source_target_pairs={{0,2},{1,3},{2,0},{3,1},{4,6},{5,7},{6,4},{7,5},{8,10},{9,11},{10,... | collective-permute-start | bytes 405512 | tf_op jit(solution)/shard_map/ppermute | solution.py:237
  7.7 1.5 %collective-permute-start = (bf16[16,4224]{1,0:T(8,128)(2,1)S(1)}, bf16[16,4224]{1,0:T(8,128)(2,1)S(1)}, u32[]{:S(2)}, u32[]{:S(2)}) collective-permute-start(bf16[16,4224]{1,0:T(8,128)(2,1)S(1)} %concatenate.38), channel_id=1, source_target_pairs={{0,8},{8,0},{16,24},{24,16},{1,9},{9,1},{17,25},{25,17},{2,10},{10... | collective-permute-start | bytes 405512 | tf_op jit(solution)/shard_map/ppermute | solution.py:20
  9.2 1.5 %collective-permute-start.1 = (bf16[16,4224]{1,0:T(8,128)(2,1)S(1)}, bf16[16,4224]{1,0:T(8,128)(2,1)S(1)}, u32[]{:S(2)}, u32[]{:S(2)}) collective-permute-start(bf16[16,4224]{1,0:T(8,128)(2,1)S(1)} %concatenate.39), channel_id=1, source_target_pairs={{0,16},{16,0},{8,24},{24,8},{1,17},{17,1},{9,25},{25,9},{2,18},{18... | collective-permute-start | bytes 405512 | tf_op jit(solution)/shard_map/ppermute | solution.py:20
  10.7 5.3 %dequantize_half.1 = (bf16[4096,768]{1,0:T(8,128)(2,1)S(1)}, bf16[384,4096]{1,0:T(8,128)(2,1)S(1)}) custom-call(f32[3,32]{1,0:T(4,128)S(1)} %get-tuple-element.164.gate_scales, f32[3,32]{1,0:T(4,128)S(1)} %get-tuple-element.163.up_scales, f32[3,32]{1,0:T(4,128)S(1)} %bitcast.15, bf16[4096,384]{1,0:T(8,128)(2,1)} %bitcast.16, bf16[4096,384]{1,0:T(8,128)(2,1)} %bitcast.17, ...), custom_call_target="tpu_custom_call" | custom-call | flops 4718592 | bytes 18874368 | tf_op jit(solution)/shard_map/dequantize_half/pallas_call | solution.py:155
  17.6 2.1 %collective-permute-start.6 = (bf16[16,4224]{1,0:T(8,128)(2,1)S(1)}, bf16[16,4224]{1,0:T(8,128)(2,1)S(1)}, u32[]{:S(2)}, u32[]{:S(2)}) collective-permute-start(bf16[16,4224]{1,0:T(8,128)(2,1)S(1)} %concatenate.39), channel_id=1, source_target_pairs={{0,2},{1,3},{2,0},{3,1},{4,6},{5,7},{6,4},{7,5},{8,10},{9,11},{10,... | collective-permute-start | bytes 405512 | tf_op jit(solution)/shard_map/ppermute | solution.py:237
  19.7 6.6 %collective-permute-done.7 = bf16[16,4224]{1,0:T(8,128)(2,1)S(1)} collective-permute-done((bf16[16,4224]{1,0:T(8,128)(2,1)S(1)}, bf16[16,4224]{1,0:T(8,128)(2,1)S(1)}, u32[]{:S(2)}, u32[]{:S(2)}) %collective-permute-start.7) | collective-permute-done | bytes 135200 | tf_op jit(solution)/shard_map/ppermute | solution.py:237
  26.6 1.6 %collective-permute-start.9 = (bf16[32,4224]{1,0:T(8,128)(2,1)S(1)}, bf16[32,4224]{1,0:T(8,128)(2,1)S(1)}, u32[]{:S(2)}, u32[]{:S(2)}) collective-permute-start(bf16[32,4224]{1,0:T(8,128)(2,1)S(1)} %constant_dynamic-update-slice_fusion.2), channel_id=1, source_target_pairs={{0,16},{16,0},{8,24},{24,8},{1,17},{17,1},{9,25},{25,9},{2,18},{18... | collective-permute-start | bytes 811016 | tf_op jit(solution)/shard_map/ppermute | solution.py:20
  28.2 1.6 %collective-permute-start.8 = (bf16[32,4224]{1,0:T(8,128)(2,1)S(1)}, bf16[32,4224]{1,0:T(8,128)(2,1)S(1)}, u32[]{:S(2)}, u32[]{:S(2)}) collective-permute-start(bf16[32,4224]{1,0:T(8,128)(2,1)S(1)} %constant_dynamic-update-slice_fusion), channel_id=1, source_target_pairs={{0,8},{8,0},{16,24},{24,16},{1,9},{9,1},{17,25},{25,17},{2,10},{10... | collective-permute-start | bytes 811016 | tf_op jit(solution)/shard_map/ppermute | solution.py:20
  29.7 5.8 %collective-permute-done.9 = bf16[32,4224]{1,0:T(8,128)(2,1)S(1)} collective-permute-done((bf16[32,4224]{1,0:T(8,128)(2,1)S(1)}, bf16[32,4224]{1,0:T(8,128)(2,1)S(1)}, u32[]{:S(2)}, u32[]{:S(2)}) %collective-permute-start.9) | collective-permute-done | bytes 270368 | tf_op jit(solution)/shard_map/ppermute | solution.py:20
  35.6 1.3 %collective-permute-done.8 = bf16[32,4224]{1,0:T(8,128)(2,1)S(1)} collective-permute-done((bf16[32,4224]{1,0:T(8,128)(2,1)S(1)}, bf16[32,4224]{1,0:T(8,128)(2,1)S(1)}, u32[]{:S(2)}, u32[]{:S(2)}) %collective-permute-start.8) | collective-permute-done | bytes 270368 | tf_op jit(solution)/shard_map/ppermute | solution.py:20
  37.0 1.6 %collective-permute-start.15 = (bf16[16,4224]{1,0:T(8,128)(2,1)S(1)}, bf16[16,4224]{1,0:T(8,128)(2,1)S(1)}, u32[]{:S(2)}, u32[]{:S(2)}) collective-permute-start(bf16[16,4224]{1,0:T(8,128)(2,1)S(1)} %get-tuple-element.154), channel_id=1, source_target_pairs={{0,8},{8,0},{16,24},{24,16},{1,9},{9,1},{17,25},{25,17},{2,10},{10... | collective-permute-start | bytes 405512 | tf_op jit(solution)/shard_map/ppermute | solution.py:20
  39.0 1.5 %collective-permute-start.13 = (bf16[64,4224]{1,0:T(8,128)(2,1)S(1)}, bf16[64,4224]{1,0:T(8,128)(2,1)S(1)}, u32[]{:S(2)}, u32[]{:S(2)}) collective-permute-start(bf16[64,4224]{1,0:T(8,128)(2,1)S(1)} %pad_maximum_fusion.refs_0_), channel_id=1, source_target_pairs={{0,16},{16,0},{8,24},{24,8},{1,17},{17,1},{9,25},{25,9},{2,18},{18... | collective-permute-start | bytes 1622024 | tf_op jit(solution)/shard_map/ppermute | solution.py:20
  41.1 1.3 %collective-permute-done.15 = bf16[16,4224]{1,0:T(8,128)(2,1)S(1)} collective-permute-done((bf16[16,4224]{1,0:T(8,128)(2,1)S(1)}, bf16[16,4224]{1,0:T(8,128)(2,1)S(1)}, u32[]{:S(2)}, u32[]{:S(2)}) %collective-permute-start.15) | collective-permute-done | bytes 135200 | tf_op jit(solution)/shard_map/ppermute | solution.py:20
  42.9 2.1 %collective-permute-done.17 = bf16[16,4224]{1,0:T(8,128)(2,1)S(1)} collective-permute-done((bf16[16,4224]{1,0:T(8,128)(2,1)S(1)}, bf16[16,4224]{1,0:T(8,128)(2,1)S(1)}, u32[]{:S(2)}, u32[]{:S(2)}) %collective-permute-start.17) | collective-permute-done | bytes 135200 | tf_op jit(solution)/shard_map/ppermute | solution.py:20
  45.7 3.1 %expert_layer.3 = (bf16[32,4096]{1,0:T(8,128)(2,1)S(1)}, bf16[32,4096]{1,0:T(8,128)(2,1)S(1)}, bf16[32,4096]{1,0:T(8,128)(2,1)S(1)}, bf16[32,4096]{1,0:T(8,128)(2,1)S(1)}) custom-call(s32[1]{0:T(128)} %bitcast.own_expert, bf16[32,4224]{1,0:T(8,128)(2,1)S(1)} %pad_maximum_fusion.2.refs_0_, bf16[32,4224]{1,0:T(8,128)(2,1)S(1)} %collective-permute-done.4.refs_1_, ...), custom_call_target="tpu_custom_call" | custom-call | flops 2415919104 | bytes 20971520 | tf_op jit(solution)/shard_map/expert_layer/pallas_call | solution.py:216
  48.8 11.7 %collective-permute-done.16.refs_1_ = bf16[32,4224]{1,0:T(8,128)(2,1)S(1)} collective-permute-done((bf16[32,4224]{1,0:T(8,128)(2,1)S(1)}, bf16[32,4224]{1,0:T(8,128)(2,1)S(1)}, u32[]{:S(2)}, u32[]{:S(2)}) %collective-permute-start.16) | collective-permute-done | bytes 270368 | tf_op jit(solution)/shard_map/ppermute | solution.py:20
  61.7 5.8 %expert_layer.4 = (bf16[64,4096]{1,0:T(8,128)(2,1)S(1)}, bf16[64,4096]{1,0:T(8,128)(2,1)S(1)}, bf16[64,4096]{1,0:T(8,128)(2,1)S(1)}, bf16[64,4096]{1,0:T(8,128)(2,1)S(1)}) custom-call(s32[1]{0:T(128)} %bitcast.own_expert, bf16[64,4224]{1,0:T(8,128)(2,1)S(1)} %pad_maximum_fusion.refs_0_, bf16[64,4224]{1,0:T(8,128)(2,1)S(1)} %collective-permute-done.13.refs_1_, ...), custom_call_target="tpu_custom_call" | custom-call | flops 4831838208 | bytes 23068672 | tf_op jit(solution)/shard_map/expert_layer/pallas_call | solution.py:216
  67.6 3.1 %expert_layer.5 = (bf16[32,4096]{1,0:T(8,128)(2,1)S(1)}, bf16[32,4096]{1,0:T(8,128)(2,1)S(1)}, bf16[32,4096]{1,0:T(8,128)(2,1)S(1)}, bf16[32,4096]{1,0:T(8,128)(2,1)S(1)}) custom-call(s32[1]{0:T(128)} %bitcast.own_expert, bf16[32,4224]{1,0:T(8,128)(2,1)S(1)} %pad_maximum_fusion.4.refs_0_, bf16[32,4224]{1,0:T(8,128)(2,1)S(1)} %collective-permute-done.16.refs_1_, ...), custom_call_target="tpu_custom_call" | custom-call | flops 2415919104 | bytes 20971520 | tf_op jit(solution)/shard_map/expert_layer/pallas_call | solution.py:216
  70.8 1.5 %collective-permute-start.26 = (bf16[32,4096]{1,0:T(8,128)(2,1)S(1)}, bf16[32,4096]{1,0:T(8,128)(2,1)S(1)}, u32[]{:S(2)}, u32[]{:S(2)}) collective-permute-start(bf16[32,4096]{1,0:T(8,128)(2,1)S(1)} %get-tuple-element.138), channel_id=1, source_target_pairs={{0,16},{16,0},{8,24},{24,8},{1,17},{17,1},{9,25},{25,9},{2,18},{18... | collective-permute-start | bytes 786440 | tf_op jit(solution)/shard_map/ppermute | solution.py:20
  72.3 1.5 %collective-permute-start.28 = (bf16[32,4096]{1,0:T(8,128)(2,1)S(1)}, bf16[32,4096]{1,0:T(8,128)(2,1)S(1)}, u32[]{:S(2)}, u32[]{:S(2)}) collective-permute-start(bf16[32,4096]{1,0:T(8,128)(2,1)S(1)} %get-tuple-element.140), channel_id=1, source_target_pairs={{0,8},{8,0},{16,24},{24,16},{1,9},{9,1},{17,25},{25,17},{2,10},{10... | collective-permute-start | bytes 786440 | tf_op jit(solution)/shard_map/ppermute | solution.py:20
  74.9 5.2 %collective-permute-done.26 = bf16[32,4096]{1,0:T(8,128)(2,1)S(1)} collective-permute-done((bf16[32,4096]{1,0:T(8,128)(2,1)S(1)}, bf16[32,4096]{1,0:T(8,128)(2,1)S(1)}, u32[]{:S(2)}, u32[]{:S(2)}) %collective-permute-start.26) | collective-permute-done | bytes 262176 | tf_op jit(solution)/shard_map/ppermute | solution.py:20
  80.2 1.5 %collective-permute-start.27 = (bf16[16,4096]{1,0:T(8,128)(2,1)S(1)}, bf16[16,4096]{1,0:T(8,128)(2,1)S(1)}, u32[]{:S(2)}, u32[]{:S(2)}) collective-permute-start(bf16[16,4096]{1,0:T(8,128)(2,1)S(1)} %split.49), channel_id=1, source_target_pairs={{0,8},{8,0},{16,24},{24,16},{1,9},{9,1},{17,25},{25,17},{2,10},{10... | collective-permute-start | bytes 393224 | tf_op jit(solution)/shard_map/ppermute | solution.py:20
  81.8 1.5 %collective-permute-start.29 = (bf16[16,4096]{1,0:T(8,128)(2,1)S(1)}, bf16[16,4096]{1,0:T(8,128)(2,1)S(1)}, u32[]{:S(2)}, u32[]{:S(2)}) collective-permute-start(bf16[16,4096]{1,0:T(8,128)(2,1)S(1)} %split.51), channel_id=1, source_target_pairs={{0,16},{16,0},{8,24},{24,8},{1,17},{17,1},{9,25},{25,9},{2,18},{18... | collective-permute-start | bytes 393224 | tf_op jit(solution)/shard_map/ppermute | solution.py:20
  83.4 9.0 %collective-permute-done.27 = bf16[16,4096]{1,0:T(8,128)(2,1)S(1)} collective-permute-done((bf16[16,4096]{1,0:T(8,128)(2,1)S(1)}, bf16[16,4096]{1,0:T(8,128)(2,1)S(1)}, u32[]{:S(2)}, u32[]{:S(2)}) %collective-permute-start.27) | collective-permute-done | bytes 131104 | tf_op jit(solution)/shard_map/ppermute | solution.py:20
  93.4 1.3 %collective-permute-start.30 = (bf16[32,4096]{1,0:T(8,128)(2,1)S(1)}, bf16[32,4096]{1,0:T(8,128)(2,1)S(1)}, u32[]{:S(2)}, u32[]{:S(2)}) collective-permute-start(bf16[32,4096]{1,0:T(8,128)(2,1)S(1)} %pad_maximum_fusion.6), channel_id=1, source_target_pairs={{0,2},{1,3},{2,0},{3,1},{4,6},{5,7},{6,4},{7,5},{8,10},{9,11},{10,... | collective-permute-start | bytes 786440 | tf_op jit(solution)/shard_map/ppermute | solution.py:237
  95.7 3.5 %collective-permute-done.24 = bf16[32,4096]{1,0:T(8,128)(2,1)S(1)} collective-permute-done((bf16[32,4096]{1,0:T(8,128)(2,1)S(1)}, bf16[32,4096]{1,0:T(8,128)(2,1)S(1)}, u32[]{:S(2)}, u32[]{:S(2)}) %collective-permute-start.24) | collective-permute-done | bytes 262176 | tf_op jit(solution)/shard_map/ppermute | solution.py:20
  99.3 1.9 %collective-permute-done.23 = bf16[32,4096]{1,0:T(8,128)(2,1)S(1)} collective-permute-done((bf16[32,4096]{1,0:T(8,128)(2,1)S(1)}, bf16[32,4096]{1,0:T(8,128)(2,1)S(1)}, u32[]{:S(2)}, u32[]{:S(2)}) %collective-permute-start.23) | collective-permute-done | bytes 262176 | tf_op jit(solution)/shard_map/ppermute | solution.py:20
  102.0 1.3 %collective-permute-start.32 = (bf16[32,4096]{1,0:T(8,128)(2,1)S(1)}, bf16[32,4096]{1,0:T(8,128)(2,1)S(1)}, u32[]{:S(2)}, u32[]{:S(2)}) collective-permute-start(bf16[32,4096]{1,0:T(8,128)(2,1)S(1)} %add_convert_fusion.6), channel_id=1, source_target_pairs={{0,2},{1,3},{2,0},{3,1},{4,6},{5,7},{6,4},{7,5},{8,10},{9,11},{10,... | collective-permute-start | bytes 786440 | tf_op jit(solution)/shard_map/ppermute | solution.py:237
  104.1 1.7 %collective-permute-start.25 = (bf16[16,4096]{1,0:T(8,128)(2,1)S(1)}, bf16[16,4096]{1,0:T(8,128)(2,1)S(1)}, u32[]{:S(2)}, u32[]{:S(2)}) collective-permute-start(bf16[16,4096]{1,0:T(8,128)(2,1)S(1)} %split.41), channel_id=1, source_target_pairs={{0,8},{8,0},{16,24},{24,16},{1,9},{9,1},{17,25},{25,17},{2,10},{10... | collective-permute-start | bytes 393224 | tf_op jit(solution)/shard_map/ppermute | solution.py:20
  105.8 2.6 %collective-permute-done.33 = bf16[16,4096]{1,0:T(8,128)(2,1)S(1)} collective-permute-done((bf16[16,4096]{1,0:T(8,128)(2,1)S(1)}, bf16[16,4096]{1,0:T(8,128)(2,1)S(1)}, u32[]{:S(2)}, u32[]{:S(2)}) %collective-permute-start.33) | collective-permute-done | bytes 131104 | tf_op jit(solution)/shard_map/ppermute | solution.py:20
  109.1 2.3 %collective-permute-done.31 = bf16[32,4096]{1,0:T(8,128)(2,1)S(1)} collective-permute-done((bf16[32,4096]{1,0:T(8,128)(2,1)S(1)}, bf16[32,4096]{1,0:T(8,128)(2,1)S(1)}, u32[]{:S(2)}, u32[]{:S(2)}) %collective-permute-start.31) | collective-permute-done | bytes 262176 | tf_op jit(solution)/shard_map/ppermute | solution.py:237
  (89 shorter events, 14.0 us)
Async XLA Ops:
  2.1 14.0 %collective-permute-start.3 = (bf16[16,4224]{1,0:T(8,128)(2,1)S(1)}, bf16[16,4224]{1,0:T(8,128)(2,1)S(1)}, u32[]{:S(2)}, u32[]{:S(2)}) collective-permute-start(bf16[16,4224]{1,0:T(8,128)(2,1)S(1)} %concatenate.38), channel_id=1, source_target_pairs={{0,4},{1,5},{2,6},{3,7},{4,0},{5,1},{6,2},{7,3},{8,12},{9,13},{10,... | collective-permute-start | bytes 405512 | tf_op jit(solution)/shard_map/ppermute | solution.py:237
  6.1 10.0 %collective-permute-start.2 = (bf16[16,4224]{1,0:T(8,128)(2,1)S(1)}, bf16[16,4224]{1,0:T(8,128)(2,1)S(1)}, u32[]{:S(2)}, u32[]{:S(2)}) collective-permute-start(bf16[16,4224]{1,0:T(8,128)(2,1)S(1)} %concatenate.38), channel_id=1, source_target_pairs={{0,2},{1,3},{2,0},{3,1},{4,6},{5,7},{6,4},{7,5},{8,10},{9,11},{10,... | collective-permute-start | bytes 405512 | tf_op jit(solution)/shard_map/ppermute | solution.py:237
  7.7 8.4 %collective-permute-start = (bf16[16,4224]{1,0:T(8,128)(2,1)S(1)}, bf16[16,4224]{1,0:T(8,128)(2,1)S(1)}, u32[]{:S(2)}, u32[]{:S(2)}) collective-permute-start(bf16[16,4224]{1,0:T(8,128)(2,1)S(1)} %concatenate.38), channel_id=1, source_target_pairs={{0,8},{8,0},{16,24},{24,16},{1,9},{9,1},{17,25},{25,17},{2,10},{10... | collective-permute-start | bytes 405512 | tf_op jit(solution)/shard_map/ppermute | solution.py:20
  9.2 6.8 %collective-permute-start.1 = (bf16[16,4224]{1,0:T(8,128)(2,1)S(1)}, bf16[16,4224]{1,0:T(8,128)(2,1)S(1)}, u32[]{:S(2)}, u32[]{:S(2)}) collective-permute-start(bf16[16,4224]{1,0:T(8,128)(2,1)S(1)} %concatenate.39), channel_id=1, source_target_pairs={{0,16},{16,0},{8,24},{24,8},{1,17},{17,1},{9,25},{25,9},{2,18},{18... | collective-permute-start | bytes 405512 | tf_op jit(solution)/shard_map/ppermute | solution.py:20
  16.1 20.8 %collective-permute-start.11 = (bf16[4096,768]{1,0:T(8,128)(2,1)S(1)}, bf16[4096,768]{1,0:T(8,128)(2,1)S(1)}, u32[]{:S(2)}, u32[]{:S(2)}) collective-permute-start(bf16[4096,768]{1,0:T(8,128)(2,1)S(1)} %get-tuple-element.95.refs_4_), channel_id=1, source_target_pairs={{0,1},{1,0},{2,3},{3,2},{4,5},{5,4},{6,7},{7,6},{8,9},{9,8},{10,11... | collective-permute-start | bytes 18874376 | tf_op jit(solution)/shard_map/ppermute | solution.py:20
  16.2 10.2 %collective-permute-start.4 = (bf16[32,4224]{1,0:T(8,128)(2,1)S(1)}, bf16[32,4224]{1,0:T(8,128)(2,1)S(1)}, u32[]{:S(2)}, u32[]{:S(2)}) collective-permute-start(bf16[32,4224]{1,0:T(8,128)(2,1)S(1)} %pad_maximum_fusion.2.refs_0_), channel_id=1, source_target_pairs={{0,16},{16,0},{8,24},{24,8},{1,17},{17,1},{9,25},{25,9},{2,18},{18... | collective-permute-start | bytes 811016 | tf_op jit(solution)/shard_map/ppermute | solution.py:20
  16.8 9.6 %collective-permute-start.5 = (bf16[32,4224]{1,0:T(8,128)(2,1)S(1)}, bf16[32,4224]{1,0:T(8,128)(2,1)S(1)}, u32[]{:S(2)}, u32[]{:S(2)}) collective-permute-start(bf16[32,4224]{1,0:T(8,128)(2,1)S(1)} %pad_maximum_fusion.3.refs_2_), channel_id=1, source_target_pairs={{0,8},{8,0},{16,24},{24,16},{1,9},{9,1},{17,25},{25,17},{2,10},{10... | collective-permute-start | bytes 811016 | tf_op jit(solution)/shard_map/ppermute | solution.py:20
  17.3 9.1 %collective-permute-start.7 = (bf16[16,4224]{1,0:T(8,128)(2,1)S(1)}, bf16[16,4224]{1,0:T(8,128)(2,1)S(1)}, u32[]{:S(2)}, u32[]{:S(2)}) collective-permute-start(bf16[16,4224]{1,0:T(8,128)(2,1)S(1)} %concatenate.39), channel_id=1, source_target_pairs={{0,4},{1,5},{2,6},{3,7},{4,0},{5,1},{6,2},{7,3},{8,12},{9,13},{10,... | collective-permute-start | bytes 405512 | tf_op jit(solution)/shard_map/ppermute | solution.py:237
  17.6 8.7 %collective-permute-start.6 = (bf16[16,4224]{1,0:T(8,128)(2,1)S(1)}, bf16[16,4224]{1,0:T(8,128)(2,1)S(1)}, u32[]{:S(2)}, u32[]{:S(2)}) collective-permute-start(bf16[16,4224]{1,0:T(8,128)(2,1)S(1)} %concatenate.39), channel_id=1, source_target_pairs={{0,2},{1,3},{2,0},{3,1},{4,6},{5,7},{6,4},{7,5},{8,10},{9,11},{10,... | collective-permute-start | bytes 405512 | tf_op jit(solution)/shard_map/ppermute | solution.py:237
  26.4 10.5 %collective-permute-start.12 = (bf16[384,4096]{1,0:T(8,128)(2,1)S(1)}, bf16[384,4096]{1,0:T(8,128)(2,1)S(1)}, u32[]{:S(2)}, u32[]{:S(2)}) collective-permute-start(bf16[384,4096]{1,0:T(8,128)(2,1)S(1)} %get-tuple-element.96.refs_6_), channel_id=1, source_target_pairs={{0,1},{1,0},{2,3},{3,2},{4,5},{5,4},{6,7},{7,6},{8,9},{9,8},{10,11... | collective-permute-start | bytes 9437192 | tf_op jit(solution)/shard_map/ppermute | solution.py:20
  26.5 10.4 %collective-permute-start.10 = (bf16[32,4224]{1,0:T(8,128)(2,1)S(1)}, bf16[32,4224]{1,0:T(8,128)(2,1)S(1)}, u32[]{:S(2)}, u32[]{:S(2)}) collective-permute-start(bf16[32,4224]{1,0:T(8,128)(2,1)S(1)} %constant_dynamic-update-slice_fusion.2), channel_id=1, source_target_pairs={{0,2},{1,3},{2,0},{3,1},{4,6},{5,7},{6,4},{7,5},{8,10},{9,11},{10,... | collective-permute-start | bytes 811016 | tf_op jit(solution)/shard_map/ppermute | solution.py:237
  26.6 8.9 %collective-permute-start.9 = (bf16[32,4224]{1,0:T(8,128)(2,1)S(1)}, bf16[32,4224]{1,0:T(8,128)(2,1)S(1)}, u32[]{:S(2)}, u32[]{:S(2)}) collective-permute-start(bf16[32,4224]{1,0:T(8,128)(2,1)S(1)} %constant_dynamic-update-slice_fusion.2), channel_id=1, source_target_pairs={{0,16},{16,0},{8,24},{24,8},{1,17},{17,1},{9,25},{25,9},{2,18},{18... | collective-permute-start | bytes 811016 | tf_op jit(solution)/shard_map/ppermute | solution.py:20
  28.2 8.7 %collective-permute-start.8 = (bf16[32,4224]{1,0:T(8,128)(2,1)S(1)}, bf16[32,4224]{1,0:T(8,128)(2,1)S(1)}, u32[]{:S(2)}, u32[]{:S(2)}) collective-permute-start(bf16[32,4224]{1,0:T(8,128)(2,1)S(1)} %constant_dynamic-update-slice_fusion), channel_id=1, source_target_pairs={{0,8},{8,0},{16,24},{24,16},{1,9},{9,1},{17,25},{25,17},{2,10},{10... | collective-permute-start | bytes 811016 | tf_op jit(solution)/shard_map/ppermute | solution.py:20
  37.0 5.4 %collective-permute-start.15 = (bf16[16,4224]{1,0:T(8,128)(2,1)S(1)}, bf16[16,4224]{1,0:T(8,128)(2,1)S(1)}, u32[]{:S(2)}, u32[]{:S(2)}) collective-permute-start(bf16[16,4224]{1,0:T(8,128)(2,1)S(1)} %get-tuple-element.154), channel_id=1, source_target_pairs={{0,8},{8,0},{16,24},{24,16},{1,9},{9,1},{17,25},{25,17},{2,10},{10... | collective-permute-start | bytes 405512 | tf_op jit(solution)/shard_map/ppermute | solution.py:20
  38.5 6.5 %collective-permute-start.17 = (bf16[16,4224]{1,0:T(8,128)(2,1)S(1)}, bf16[16,4224]{1,0:T(8,128)(2,1)S(1)}, u32[]{:S(2)}, u32[]{:S(2)}) collective-permute-start(bf16[16,4224]{1,0:T(8,128)(2,1)S(1)} %get-tuple-element.153), channel_id=1, source_target_pairs={{0,16},{16,0},{8,24},{24,8},{1,17},{17,1},{9,25},{25,9},{2,18},{18... | collective-permute-start | bytes 405512 | tf_op jit(solution)/shard_map/ppermute | solution.py:20
  39.0 21.5 %collective-permute-start.13 = (bf16[64,4224]{1,0:T(8,128)(2,1)S(1)}, bf16[64,4224]{1,0:T(8,128)(2,1)S(1)}, u32[]{:S(2)}, u32[]{:S(2)}) collective-permute-start(bf16[64,4224]{1,0:T(8,128)(2,1)S(1)} %pad_maximum_fusion.refs_0_), channel_id=1, source_target_pairs={{0,16},{16,0},{8,24},{24,8},{1,17},{17,1},{9,25},{25,9},{2,18},{18... | collective-permute-start | bytes 1622024 | tf_op jit(solution)/shard_map/ppermute | solution.py:20
  40.6 19.9 %collective-permute-start.14 = (bf16[64,4224]{1,0:T(8,128)(2,1)S(1)}, bf16[64,4224]{1,0:T(8,128)(2,1)S(1)}, u32[]{:S(2)}, u32[]{:S(2)}) collective-permute-start(bf16[64,4224]{1,0:T(8,128)(2,1)S(1)} %pad_maximum_fusion.1.refs_2_), channel_id=1, source_target_pairs={{0,8},{8,0},{16,24},{24,16},{1,9},{9,1},{17,25},{25,17},{2,10},{10... | collective-permute-start | bytes 1622024 | tf_op jit(solution)/shard_map/ppermute | solution.py:20
  42.4 18.1 %collective-permute-start.16 = (bf16[32,4224]{1,0:T(8,128)(2,1)S(1)}, bf16[32,4224]{1,0:T(8,128)(2,1)S(1)}, u32[]{:S(2)}, u32[]{:S(2)}) collective-permute-start(bf16[32,4224]{1,0:T(8,128)(2,1)S(1)} %pad_maximum_fusion.4.refs_0_), channel_id=1, source_target_pairs={{0,16},{16,0},{8,24},{24,8},{1,17},{17,1},{9,25},{25,9},{2,18},{18... | collective-permute-start | bytes 811016 | tf_op jit(solution)/shard_map/ppermute | solution.py:20
  45.1 15.4 %collective-permute-start.18 = (bf16[32,4224]{1,0:T(8,128)(2,1)S(1)}, bf16[32,4224]{1,0:T(8,128)(2,1)S(1)}, u32[]{:S(2)}, u32[]{:S(2)}) collective-permute-start(bf16[32,4224]{1,0:T(8,128)(2,1)S(1)} %pad_maximum_fusion.5.refs_2_), channel_id=1, source_target_pairs={{0,8},{8,0},{16,24},{24,16},{1,9},{9,1},{17,25},{25,17},{2,10},{10... | collective-permute-start | bytes 811016 | tf_op jit(solution)/shard_map/ppermute | solution.py:20
  60.5 6.9 %collective-permute-start.19 = (bf16[32,4096]{1,0:T(8,128)(2,1)S(1)}, bf16[32,4096]{1,0:T(8,128)(2,1)S(1)}, u32[]{:S(2)}, u32[]{:S(2)}) collective-permute-start(bf16[32,4096]{1,0:T(8,128)(2,1)S(1)} %get-tuple-element.120), channel_id=1, source_target_pairs={{0,16},{16,0},{8,24},{24,8},{1,17},{17,1},{9,25},{25,9},{2,18},{18... | collective-permute-start | bytes 786440 | tf_op jit(solution)/shard_map/ppermute | solution.py:20
  61.1 6.4 %collective-permute-start.20 = (bf16[32,4096]{1,0:T(8,128)(2,1)S(1)}, bf16[32,4096]{1,0:T(8,128)(2,1)S(1)}, u32[]{:S(2)}, u32[]{:S(2)}) collective-permute-start(bf16[32,4096]{1,0:T(8,128)(2,1)S(1)} %get-tuple-element.122), channel_id=1, source_target_pairs={{0,8},{8,0},{16,24},{24,16},{1,9},{9,1},{17,25},{25,17},{2,10},{10... | collective-permute-start | bytes 786440 | tf_op jit(solution)/shard_map/ppermute | solution.py:20
  70.8 9.3 %collective-permute-start.26 = (bf16[32,4096]{1,0:T(8,128)(2,1)S(1)}, bf16[32,4096]{1,0:T(8,128)(2,1)S(1)}, u32[]{:S(2)}, u32[]{:S(2)}) collective-permute-start(bf16[32,4096]{1,0:T(8,128)(2,1)S(1)} %get-tuple-element.138), channel_id=1, source_target_pairs={{0,16},{16,0},{8,24},{24,8},{1,17},{17,1},{9,25},{25,9},{2,18},{18... | collective-permute-start | bytes 786440 | tf_op jit(solution)/shard_map/ppermute | solution.py:20
  72.3 9.4 %collective-permute-start.28 = (bf16[32,4096]{1,0:T(8,128)(2,1)S(1)}, bf16[32,4096]{1,0:T(8,128)(2,1)S(1)}, u32[]{:S(2)}, u32[]{:S(2)}) collective-permute-start(bf16[32,4096]{1,0:T(8,128)(2,1)S(1)} %get-tuple-element.140), channel_id=1, source_target_pairs={{0,8},{8,0},{16,24},{24,16},{1,9},{9,1},{17,25},{25,17},{2,10},{10... | collective-permute-start | bytes 786440 | tf_op jit(solution)/shard_map/ppermute | solution.py:20
  73.8 18.6 %collective-permute-start.21 = (bf16[64,4096]{1,0:T(8,128)(2,1)S(1)}, bf16[64,4096]{1,0:T(8,128)(2,1)S(1)}, u32[]{:S(2)}, u32[]{:S(2)}) collective-permute-start(bf16[64,4096]{1,0:T(8,128)(2,1)S(1)} %get-tuple-element.130), channel_id=1, source_target_pairs={{0,16},{16,0},{8,24},{24,8},{1,17},{17,1},{9,25},{25,9},{2,18},{18... | collective-permute-start | bytes 1572872 | tf_op jit(solution)/shard_map/ppermute | solution.py:20
  74.4 18.2 %collective-permute-start.22 = (bf16[64,4096]{1,0:T(8,128)(2,1)S(1)}, bf16[64,4096]{1,0:T(8,128)(2,1)S(1)}, u32[]{:S(2)}, u32[]{:S(2)}) collective-permute-start(bf16[64,4096]{1,0:T(8,128)(2,1)S(1)} %get-tuple-element.132), channel_id=1, source_target_pairs={{0,8},{8,0},{16,24},{24,16},{1,9},{9,1},{17,25},{25,17},{2,10},{10... | collective-permute-start | bytes 1572872 | tf_op jit(solution)/shard_map/ppermute | solution.py:20
  80.2 12.2 %collective-permute-start.27 = (bf16[16,4096]{1,0:T(8,128)(2,1)S(1)}, bf16[16,4096]{1,0:T(8,128)(2,1)S(1)}, u32[]{:S(2)}, u32[]{:S(2)}) collective-permute-start(bf16[16,4096]{1,0:T(8,128)(2,1)S(1)} %split.49), channel_id=1, source_target_pairs={{0,8},{8,0},{16,24},{24,16},{1,9},{9,1},{17,25},{25,17},{2,10},{10... | collective-permute-start | bytes 393224 | tf_op jit(solution)/shard_map/ppermute | solution.py:20
  81.8 10.6 %collective-permute-start.29 = (bf16[16,4096]{1,0:T(8,128)(2,1)S(1)}, bf16[16,4096]{1,0:T(8,128)(2,1)S(1)}, u32[]{:S(2)}, u32[]{:S(2)}) collective-permute-start(bf16[16,4096]{1,0:T(8,128)(2,1)S(1)} %split.51), channel_id=1, source_target_pairs={{0,16},{16,0},{8,24},{24,8},{1,17},{17,1},{9,25},{25,9},{2,18},{18... | collective-permute-start | bytes 393224 | tf_op jit(solution)/shard_map/ppermute | solution.py:20
  92.7 6.4 %collective-permute-start.24 = (bf16[32,4096]{1,0:T(8,128)(2,1)S(1)}, bf16[32,4096]{1,0:T(8,128)(2,1)S(1)}, u32[]{:S(2)}, u32[]{:S(2)}) collective-permute-start(bf16[32,4096]{1,0:T(8,128)(2,1)S(1)} %split.39), channel_id=1, source_target_pairs={{0,16},{16,0},{8,24},{24,8},{1,17},{17,1},{9,25},{25,9},{2,18},{18... | collective-permute-start | bytes 786440 | tf_op jit(solution)/shard_map/ppermute | solution.py:20
  93.4 7.8 %collective-permute-start.30 = (bf16[32,4096]{1,0:T(8,128)(2,1)S(1)}, bf16[32,4096]{1,0:T(8,128)(2,1)S(1)}, u32[]{:S(2)}, u32[]{:S(2)}) collective-permute-start(bf16[32,4096]{1,0:T(8,128)(2,1)S(1)} %pad_maximum_fusion.6), channel_id=1, source_target_pairs={{0,2},{1,3},{2,0},{3,1},{4,6},{5,7},{6,4},{7,5},{8,10},{9,11},{10,... | collective-permute-start | bytes 786440 | tf_op jit(solution)/shard_map/ppermute | solution.py:237
  94.7 6.4 %collective-permute-start.23 = (bf16[32,4096]{1,0:T(8,128)(2,1)S(1)}, bf16[32,4096]{1,0:T(8,128)(2,1)S(1)}, u32[]{:S(2)}, u32[]{:S(2)}) collective-permute-start(bf16[32,4096]{1,0:T(8,128)(2,1)S(1)} %split.37), channel_id=1, source_target_pairs={{0,8},{8,0},{16,24},{24,16},{1,9},{9,1},{17,25},{25,17},{2,10},{10... | collective-permute-start | bytes 786440 | tf_op jit(solution)/shard_map/ppermute | solution.py:20
  101.3 10.1 %collective-permute-start.31 = (bf16[32,4096]{1,0:T(8,128)(2,1)S(1)}, bf16[32,4096]{1,0:T(8,128)(2,1)S(1)}, u32[]{:S(2)}, u32[]{:S(2)}) collective-permute-start(bf16[32,4096]{1,0:T(8,128)(2,1)S(1)} %add_convert_fusion.2), channel_id=1, source_target_pairs={{0,4},{1,5},{2,6},{3,7},{4,0},{5,1},{6,2},{7,3},{8,12},{9,13},{10,... | collective-permute-start | bytes 786440 | tf_op jit(solution)/shard_map/ppermute | solution.py:237
  102.0 9.4 %collective-permute-start.32 = (bf16[32,4096]{1,0:T(8,128)(2,1)S(1)}, bf16[32,4096]{1,0:T(8,128)(2,1)S(1)}, u32[]{:S(2)}, u32[]{:S(2)}) collective-permute-start(bf16[32,4096]{1,0:T(8,128)(2,1)S(1)} %add_convert_fusion.6), channel_id=1, source_target_pairs={{0,2},{1,3},{2,0},{3,1},{4,6},{5,7},{6,4},{7,5},{8,10},{9,11},{10,... | collective-permute-start | bytes 786440 | tf_op jit(solution)/shard_map/ppermute | solution.py:237
  (6 other events, 54.3 us)

commit v16 on v15

--- a/solution.py
+++ b/solution.py
@@ -99,78 +99,87 @@
     return (block.astype(jnp.float32) * scale).astype(jnp.bfloat16)
 
 
-def dequantize_kernel(gate_scales, up_scales, down_scales, gate, up, down, in_out, down_out, *scratch):
-    gate_raw, up_raw, down_raw, in_sems, down_sems = scratch
+def chunk_copies(sources, targets, sems):
+    chunks = sems.shape[1]
+    depth = sources[0].shape[0] // chunks
+
+    def copy(part, chunk):
+        at = pl.ds(pl.multiple_of(chunk * depth, depth), depth)
+        return pltpu.make_async_copy(sources[part].at[at], targets[part].at[at], sems.at[part, chunk])
+
+    for chunk in range(chunks):
+        for part in range(len(sources)):
+            copy(part, chunk).start()
+    return copy
+
+
+def in_kernel(gate_scales, up_scales, gate, up, out, gate_raw, up_raw, sems):
     rows, cols = gate.shape
-    chunks, down_chunks = in_sems.shape[1], down_sems.shape[0]
-    depth, down_depth = rows // chunks, down.shape[0] // down_chunks
-
-    def in_copy(part, chunk):
-        source, target = ((gate, gate_raw), (up, up_raw))[part]
-        at = pl.ds(pl.multiple_of(chunk * depth, depth), depth)
-        return pltpu.make_async_copy(source.at[at], target.at[at], in_sems.at[part, chunk])
-
-    def down_copy(chunk):
-        at = pl.ds(pl.multiple_of(chunk * down_depth, down_depth), down_depth)
-        return pltpu.make_async_copy(down.at[at], down_raw.at[at], down_sems.at[chunk])
-
-    for chunk in range(chunks):
-        for part in range(2):
-            in_copy(part, chunk).start()
-    for chunk in range(down_chunks):
-        down_copy(chunk).start()
+    chunks = sems.shape[1]
+    strip = rows // chunks // BLOCK
+    copy = chunk_copies((gate, up), (gate_raw, up_raw), sems)
 
     @pl.loop(0, chunks)
     def _(chunk):
-        in_copy(0, chunk).wait()
-        in_copy(1, chunk).wait()
-        for block in range(depth // BLOCK):
-            row = chunk * (depth // BLOCK) + block
+        copy(0, chunk).wait()
+        copy(1, chunk).wait()
+        for block in range(strip):
+            row = chunk * strip + block
             at = pl.ds(pl.multiple_of(row * BLOCK, BLOCK), BLOCK)
             for col in range(cols // BLOCK):
-                from_cols = slice(col * BLOCK, (col + 1) * BLOCK)
-                to = 2 * col * BLOCK
-                value = scaled(gate_raw[at, from_cols], gate_scales[col, row])
-                in_out[at, to : to + BLOCK] = value
+                source, to = slice(col * BLOCK, (col + 1) * BLOCK), 2 * col * BLOCK
+                out[at, to : to + BLOCK] = scaled(gate_raw[at, source], gate_scales[col, row])
                 to += BLOCK
-                value = scaled(up_raw[at, from_cols], up_scales[col, row])
-                in_out[at, to : to + BLOCK] = value
-
-    @pl.loop(0, down_chunks)
+                out[at, to : to + BLOCK] = scaled(up_raw[at, source], up_scales[col, row])
+
+
+def down_kernel(scales, down, out, raw, sems):
+    chunks = sems.shape[1]
+    strip = down.shape[0] // chunks // BLOCK
+    copy = chunk_copies((down,), (raw,), sems)
+
+    @pl.loop(0, chunks)
     def _(chunk):
-        down_copy(chunk).wait()
-        for block in range(down_depth // BLOCK):
-            row = chunk * (down_depth // BLOCK) + block
+        copy(0, chunk).wait()
+        for block in range(strip):
+            row = chunk * strip + block
             at = pl.ds(pl.multiple_of(row * BLOCK, BLOCK), BLOCK)
             for col in range(down.shape[1] // BLOCK):
-                cols_at = slice(col * BLOCK, (col + 1) * BLOCK)
-                down_out[at, cols_at] = scaled(down_raw[at, cols_at], down_scales[row, col])
-
-
-def dequantize_half(quants, scales):
+                cols = slice(col * BLOCK, (col + 1) * BLOCK)
+                out[at, cols] = scaled(raw[at, cols], scales[row, col])
+
+
+def dequantize_call(kernel, name, quants, scales, width, chunks):
     rows, cols = quants[0].shape
-    chunks, down_chunks = max(1, rows // (4 * BLOCK)), max(1, cols // BLOCK)
     quants = [pltpu.with_memory_space_constraint(quant, pltpu.HBM) for quant in quants]
-    whole = pl.BlockSpec(memory_space=pltpu.VMEM)
     return pl.pallas_call(
-        dequantize_kernel,
-        in_specs=[pl.BlockSpec(memory_space=pltpu.SMEM)] * 3 + [pl.BlockSpec(memory_space=pl.ANY)] * 3,
-        out_specs=[whole] * 2,
-        out_shape=[
-            jax.ShapeDtypeStruct((rows, 2 * cols), jnp.bfloat16),
-            jax.ShapeDtypeStruct(quants[2].shape, jnp.bfloat16),
-        ],
+        kernel,
+        in_specs=[pl.BlockSpec(memory_space=pltpu.SMEM)] * len(scales)
+        + [pl.BlockSpec(memory_space=pl.ANY)] * len(quants),
+        out_specs=pl.BlockSpec(memory_space=pltpu.VMEM),
+        out_shape=jax.ShapeDtypeStruct((rows, width), jnp.bfloat16),
         scratch_shapes=[
             *(pltpu.VMEM(quant.shape, jnp.bfloat16) for quant in quants),
-            pltpu.SemaphoreType.DMA((2, chunks)),
-            pltpu.SemaphoreType.DMA((down_chunks,)),
+            pltpu.SemaphoreType.DMA((len(quants), chunks)),
         ],
         cost_estimate=pl.CostEstimate(
-            flops=3 * rows * cols, bytes_accessed=12 * rows * cols, transcendentals=0
+            flops=rows * width, bytes_accessed=4 * rows * width, transcendentals=0
         ),
-        compiler_params=pltpu.CompilerParams(vmem_limit_bytes=24 * 1024 * 1024),
-        name="dequantize_half",
+        compiler_params=pltpu.CompilerParams(vmem_limit_bytes=16 * 1024 * 1024),
+        name=name,
     )(*scales, *quants)
+
+
+def dequantize_in(gate, up, gate_scales, up_scales):
+    rows, cols = gate.shape
+    chunks = max(1, rows // (4 * BLOCK))
+    scales = (gate_scales, up_scales)
+    return dequantize_call(in_kernel, "dequantize_in", (gate, up), scales, 2 * cols, chunks)
+
+
+def dequantize_down(down, scales):
+    rows, cols = down.shape
+    return dequantize_call(down_kernel, "dequantize_down", (down,), (scales,), cols, rows // BLOCK)
 
 
 def silu(v):
@@ -288,11 +297,10 @@
     lanes, outs = {0: payload}, {}
     near = [{far: across_chips(payload[0], far) for far in groups[1]}]
     gather_turn(0, 0)
-    in_own, down_own = dequantize_half(
-        (gate_q[0], up_q[0], down_q[0]), (gate_scale[0].T, up_scale[0].T, down_scale[0])
-    )
-    lanes, near, payload, in_own, down_own = together((lanes, near, payload, in_own, down_own))
+    in_own = dequantize_in(gate_q[0], up_q[0], gate_scale[0].T, up_scale[0].T)
+    lanes, near, payload, in_own, down_own = together((lanes, near, payload, in_own, down_q[0]))
     in_other = from_partner(in_own, "expert", 0)
+    down_own = dequantize_down(down_own, down_scale[0])
     near.append({far: across_chips(payload[1], far) for far in groups[1]})
     for turn in range(1, turns):
         gather_turn(0, turn)
@@ -351,7 +359,7 @@
                 whole = across_chips(block, low)
                 parts.append([whole[rows] for rows in halves])
 
-    lanes, outs = together((lanes, outs))
+    lanes[final - 1], outs = together((lanes[final - 1], outs))
     sum_turn(0, turns - 1)
     outs[final - 1] = layer(final - 1)
     lanes, outs, sums = together((lanes, outs, sums))

time: 112 us -> 110 us (0.982)
  waiting for transfers between devices: 54 us -> 48.9 us
  starting transfers between devices: 36.5 us -> 38.6 us
    ppermute x8, waiting for transfers between devices: 8.97 us -> 5.17 us  [across_chips(): lax.ppermute(block, 'expert', [(low, low ^ 2 * far) for low in range(coun...]
    ppermute x26, waiting for transfers between devices: 45.1 us -> 43.7 us  [from_partner(): return lax.ppermute(block, axis, route)]
    pallas_call x1 -> x2, Pallas kernels: 5.28 us -> 6.46 us  [dequantize_call(): pl.pallas_call(kernel, in_specs=[pl.BlockSpec(memory_space=pltpu.SMEM)] *...]
  transfers between devices with their start and end apart: 34 -> 34, of which waited for: 13 -> 15; matrix products, arithmetic and copies ran while one was open for 1% -> 1% of each run, Pallas kernels for 13% -> 14%
where the time goes in v16:
time: 110 us
  waiting for transfers between devices  48.9 us (44%)
  starting transfers between devices  38.6 us (35%)
  Pallas kernels  18.3 us (17%)
  other arithmetic  2.59 us (2%)
  local copies, waits for them, and re-layouts  1.44 us (1%)
    ppermute x26, waiting for transfers between devices, from_partner(): return lax.ppermute(block, axis, route)  43.7 us
    ppermute x26, starting transfers between devices, from_partner(): return lax.ppermute(block, axis, route)  26.1 us
    ppermute x8, starting transfers between devices, across_chips(): lax.ppermute(block, 'expert', [(low, low ^ 2 * far) for low in range(coun...  12.6 us
    pallas_call x3, Pallas kernels, expert_layer(): pl.pallas_call(functools.partial(expert_kernel, count, experts), in_specs...  11.8 us
    pallas_call x2, Pallas kernels, dequantize_call(): pl.pallas_call(kernel, in_specs=[pl.BlockSpec(memory_space=pltpu.SMEM)] *...  6.46 us
    ppermute x8, waiting for transfers between devices, across_chips(): lax.ppermute(block, 'expert', [(low, low ^ 2 * far) for low in range(coun...  5.17 us
  transfers between devices with their start and end apart: 34, of which 15 were waited for; matrix products, arithmetic and copies ran while one was open for 1% of the time, Pallas kernels for 14%

profile of v16, /device:TPU:0, one launch (start us, length us, event | category | flops | bytes accessed | tf_op | source)
XLA Modules:
  0.0 110.3 jit_solution(6064333234615599493)
XLA Ops:
  2.1 4.0 %collective-permute-start.3 = (bf16[16,4224]{1,0:T(8,128)(2,1)S(1)}, bf16[16,4224]{1,0:T(8,128)(2,1)S(1)}, u32[]{:S(2)}, u32[]{:S(2)}) collective-permute-start(bf16[16,4224]{1,0:T(8,128)(2,1)S(1)} %concatenate.38), channel_id=1, source_target_pairs={{0,4},{1,5},{2,6},{3,7},{4,0},{5,1},{6,2},{7,3},{8,12},{9,13},{10,... | collective-permute-start | bytes 405512 | tf_op jit(solution)/shard_map/ppermute | solution.py:246
  6.1 1.6 %collective-permute-start.2 = (bf16[16,4224]{1,0:T(8,128)(2,1)S(1)}, bf16[16,4224]{1,0:T(8,128)(2,1)S(1)}, u32[]{:S(2)}, u32[]{:S(2)}) collective-permute-start(bf16[16,4224]{1,0:T(8,128)(2,1)S(1)} %concatenate.38), channel_id=1, source_target_pairs={{0,2},{1,3},{2,0},{3,1},{4,6},{5,7},{6,4},{7,5},{8,10},{9,11},{10,... | collective-permute-start | bytes 405512 | tf_op jit(solution)/shard_map/ppermute | solution.py:246
  7.7 1.5 %collective-permute-start = (bf16[16,4224]{1,0:T(8,128)(2,1)S(1)}, bf16[16,4224]{1,0:T(8,128)(2,1)S(1)}, u32[]{:S(2)}, u32[]{:S(2)}) collective-permute-start(bf16[16,4224]{1,0:T(8,128)(2,1)S(1)} %concatenate.38), channel_id=1, source_target_pairs={{0,8},{8,0},{16,24},{24,16},{1,9},{9,1},{17,25},{25,17},{2,10},{10... | collective-permute-start | bytes 405512 | tf_op jit(solution)/shard_map/ppermute | solution.py:20
  9.2 1.5 %collective-permute-start.1 = (bf16[16,4224]{1,0:T(8,128)(2,1)S(1)}, bf16[16,4224]{1,0:T(8,128)(2,1)S(1)}, u32[]{:S(2)}, u32[]{:S(2)}) collective-permute-start(bf16[16,4224]{1,0:T(8,128)(2,1)S(1)} %concatenate.39), channel_id=1, source_target_pairs={{0,16},{16,0},{8,24},{24,8},{1,17},{17,1},{9,25},{25,9},{2,18},{18... | collective-permute-start | bytes 405512 | tf_op jit(solution)/shard_map/ppermute | solution.py:20
  10.7 3.7 %dequantize_in.1.refs_4_ = bf16[4096,768]{1,0:T(8,128)(2,1)S(1)} custom-call(f32[3,32]{1,0:T(4,128)S(1)} %get-tuple-element.152.gate_scales, f32[3,32]{1,0:T(4,128)S(1)} %get-tuple-element.151.up_scales, bf16[4096,384]{1,0:T(8,128)(2,1)} %bitcast.17, bf16[4096,384]{1,0:T(8,128)(2,1)} %bitcast.18), custom_call_target="tpu_custom_call" | custom-call | flops 3145728 | bytes 12582912 | tf_op jit(solution)/shard_map/dequantize_in/pallas_call | solution.py:155
  14.6 1.3 %collective-permute-start.4 = (bf16[32,4224]{1,0:T(8,128)(2,1)S(1)}, bf16[32,4224]{1,0:T(8,128)(2,1)S(1)}, u32[]{:S(2)}, u32[]{:S(2)}) collective-permute-start(bf16[32,4224]{1,0:T(8,128)(2,1)S(1)} %pad_maximum_fusion.2.refs_0_), channel_id=1, source_target_pairs={{0,16},{16,0},{8,24},{24,8},{1,17},{17,1},{9,25},{25,9},{2,18},{18... | collective-permute-start | bytes 811016 | tf_op jit(solution)/shard_map/ppermute | solution.py:20
  17.3 2.4 %collective-permute-start.6 = (bf16[16,4224]{1,0:T(8,128)(2,1)S(1)}, bf16[16,4224]{1,0:T(8,128)(2,1)S(1)}, u32[]{:S(2)}, u32[]{:S(2)}) collective-permute-start(bf16[16,4224]{1,0:T(8,128)(2,1)S(1)} %concatenate.39), channel_id=1, source_target_pairs={{0,2},{1,3},{2,0},{3,1},{4,6},{5,7},{6,4},{7,5},{8,10},{9,11},{10,... | collective-permute-start | bytes 405512 | tf_op jit(solution)/shard_map/ppermute | solution.py:246
  19.7 2.8 %dequantize_down.1.refs_6_ = bf16[384,4096]{1,0:T(8,128)(2,1)S(1)} custom-call(f32[3,32]{1,0:T(4,128)S(1)} %bitcast.15, bf16[384,4096]{1,0:T(8,128)(2,1)} %bitcast.16), custom_call_target="tpu_custom_call" | custom-call | flops 1572864 | bytes 6291456 | tf_op jit(solution)/shard_map/dequantize_down/pallas_call | solution.py:155
  22.5 3.2 %collective-permute-done.7 = bf16[16,4224]{1,0:T(8,128)(2,1)S(1)} collective-permute-done((bf16[16,4224]{1,0:T(8,128)(2,1)S(1)}, bf16[16,4224]{1,0:T(8,128)(2,1)S(1)}, u32[]{:S(2)}, u32[]{:S(2)}) %collective-permute-start.7) | collective-permute-done | bytes 135200 | tf_op jit(solution)/shard_map/ppermute | solution.py:246
  26.7 1.4 %collective-permute-start.8 = (bf16[32,4224]{1,0:T(8,128)(2,1)S(1)}, bf16[32,4224]{1,0:T(8,128)(2,1)S(1)}, u32[]{:S(2)}, u32[]{:S(2)}) collective-permute-start(bf16[32,4224]{1,0:T(8,128)(2,1)S(1)} %constant_dynamic-update-slice_fusion), channel_id=1, source_target_pairs={{0,8},{8,0},{16,24},{24,16},{1,9},{9,1},{17,25},{25,17},{2,10},{10... | collective-permute-start | bytes 811016 | tf_op jit(solution)/shard_map/ppermute | solution.py:20
  28.1 6.6 %collective-permute-done.9 = bf16[32,4224]{1,0:T(8,128)(2,1)S(1)} collective-permute-done((bf16[32,4224]{1,0:T(8,128)(2,1)S(1)}, bf16[32,4224]{1,0:T(8,128)(2,1)S(1)}, u32[]{:S(2)}, u32[]{:S(2)}) %collective-permute-start.9) | collective-permute-done | bytes 270368 | tf_op jit(solution)/shard_map/ppermute | solution.py:20
  35.5 1.3 %collective-permute-start.17 = (bf16[16,4224]{1,0:T(8,128)(2,1)S(1)}, bf16[16,4224]{1,0:T(8,128)(2,1)S(1)}, u32[]{:S(2)}, u32[]{:S(2)}) collective-permute-start(bf16[16,4224]{1,0:T(8,128)(2,1)S(1)} %get-tuple-element.141), channel_id=1, source_target_pairs={{0,16},{16,0},{8,24},{24,8},{1,17},{17,1},{9,25},{25,9},{2,18},{18... | collective-permute-start | bytes 405512 | tf_op jit(solution)/shard_map/ppermute | solution.py:20
  36.8 1.4 %collective-permute-start.15 = (bf16[16,4224]{1,0:T(8,128)(2,1)S(1)}, bf16[16,4224]{1,0:T(8,128)(2,1)S(1)}, u32[]{:S(2)}, u32[]{:S(2)}) collective-permute-start(bf16[16,4224]{1,0:T(8,128)(2,1)S(1)} %get-tuple-element.142), channel_id=1, source_target_pairs={{0,8},{8,0},{16,24},{24,16},{1,9},{9,1},{17,25},{25,17},{2,10},{10... | collective-permute-start | bytes 405512 | tf_op jit(solution)/shard_map/ppermute | solution.py:20
  39.6 3.1 %expert_layer.3 = (bf16[32,4096]{1,0:T(8,128)(2,1)S(1)}, bf16[32,4096]{1,0:T(8,128)(2,1)S(1)}, bf16[32,4096]{1,0:T(8,128)(2,1)S(1)}, bf16[32,4096]{1,0:T(8,128)(2,1)S(1)}) custom-call(s32[1]{0:T(128)} %bitcast.own_expert, bf16[32,4224]{1,0:T(8,128)(2,1)S(1)} %pad_maximum_fusion.2.refs_0_, bf16[32,4224]{1,0:T(8,128)(2,1)S(1)} %collective-permute-done.4.refs_1_, ...), custom_call_target="tpu_custom_call" | custom-call | flops 2415919104 | bytes 20971520 | tf_op jit(solution)/shard_map/expert_layer/pallas_call | solution.py:225
  44.1 1.6 %collective-permute-start.18 = (bf16[32,4224]{1,0:T(8,128)(2,1)S(1)}, bf16[32,4224]{1,0:T(8,128)(2,1)S(1)}, u32[]{:S(2)}, u32[]{:S(2)}) collective-permute-start(bf16[32,4224]{1,0:T(8,128)(2,1)S(1)} %pad_maximum_fusion.5.refs_2_), channel_id=1, source_target_pairs={{0,8},{8,0},{16,24},{24,16},{1,9},{9,1},{17,25},{25,17},{2,10},{10... | collective-permute-start | bytes 811016 | tf_op jit(solution)/shard_map/ppermute | solution.py:20
  45.6 7.8 %collective-permute-done.13.refs_1_ = bf16[64,4224]{1,0:T(8,128)(2,1)S(1)} collective-permute-done((bf16[64,4224]{1,0:T(8,128)(2,1)S(1)}, bf16[64,4224]{1,0:T(8,128)(2,1)S(1)}, u32[]{:S(2)}, u32[]{:S(2)}) %collective-permute-start.13) | collective-permute-done | bytes 540704 | tf_op jit(solution)/shard_map/ppermute | solution.py:20
  53.4 1.5 %collective-permute-done.14.refs_3_ = bf16[64,4224]{1,0:T(8,128)(2,1)S(1)} collective-permute-done((bf16[64,4224]{1,0:T(8,128)(2,1)S(1)}, bf16[64,4224]{1,0:T(8,128)(2,1)S(1)}, u32[]{:S(2)}, u32[]{:S(2)}) %collective-permute-start.14) | collective-permute-done | bytes 540704 | tf_op jit(solution)/shard_map/ppermute | solution.py:20
  55.4 1.7 %collective-permute-start.20 = (bf16[32,4096]{1,0:T(8,128)(2,1)S(1)}, bf16[32,4096]{1,0:T(8,128)(2,1)S(1)}, u32[]{:S(2)}, u32[]{:S(2)}) collective-permute-start(bf16[32,4096]{1,0:T(8,128)(2,1)S(1)} %get-tuple-element.110), channel_id=1, source_target_pairs={{0,8},{8,0},{16,24},{24,16},{1,9},{9,1},{17,25},{25,17},{2,10},{10... | collective-permute-start | bytes 786440 | tf_op jit(solution)/shard_map/ppermute | solution.py:20
  57.0 5.7 %expert_layer.4 = (bf16[64,4096]{1,0:T(8,128)(2,1)S(1)}, bf16[64,4096]{1,0:T(8,128)(2,1)S(1)}, bf16[64,4096]{1,0:T(8,128)(2,1)S(1)}, bf16[64,4096]{1,0:T(8,128)(2,1)S(1)}) custom-call(s32[1]{0:T(128)} %bitcast.own_expert, bf16[64,4224]{1,0:T(8,128)(2,1)S(1)} %pad_maximum_fusion.refs_0_, bf16[64,4224]{1,0:T(8,128)(2,1)S(1)} %collective-permute-done.13.refs_1_, ...), custom_call_target="tpu_custom_call" | custom-call | flops 4831838208 | bytes 23068672 | tf_op jit(solution)/shard_map/expert_layer/pallas_call | solution.py:225
  64.6 3.1 %expert_layer.5 = (bf16[32,4096]{1,0:T(8,128)(2,1)S(1)}, bf16[32,4096]{1,0:T(8,128)(2,1)S(1)}, bf16[32,4096]{1,0:T(8,128)(2,1)S(1)}, bf16[32,4096]{1,0:T(8,128)(2,1)S(1)}) custom-call(s32[1]{0:T(128)} %bitcast.own_expert, bf16[32,4224]{1,0:T(8,128)(2,1)S(1)} %pad_maximum_fusion.4.refs_0_, bf16[32,4224]{1,0:T(8,128)(2,1)S(1)} %collective-permute-done.16.refs_1_, ...), custom_call_target="tpu_custom_call" | custom-call | flops 2415919104 | bytes 20971520 | tf_op jit(solution)/shard_map/expert_layer/pallas_call | solution.py:225
  69.8 1.3 %collective-permute-start.21 = (bf16[64,4096]{1,0:T(8,128)(2,1)S(1)}, bf16[64,4096]{1,0:T(8,128)(2,1)S(1)}, u32[]{:S(2)}, u32[]{:S(2)}) collective-permute-start(bf16[64,4096]{1,0:T(8,128)(2,1)S(1)} %get-tuple-element.118), channel_id=1, source_target_pairs={{0,16},{16,0},{8,24},{24,8},{1,17},{17,1},{9,25},{25,9},{2,18},{18... | collective-permute-start | bytes 1572872 | tf_op jit(solution)/shard_map/ppermute | solution.py:20
  71.8 5.2 %collective-permute-done.26 = bf16[32,4096]{1,0:T(8,128)(2,1)S(1)} collective-permute-done((bf16[32,4096]{1,0:T(8,128)(2,1)S(1)}, bf16[32,4096]{1,0:T(8,128)(2,1)S(1)}, u32[]{:S(2)}, u32[]{:S(2)}) %collective-permute-start.26) | collective-permute-done | bytes 262176 | tf_op jit(solution)/shard_map/ppermute | solution.py:20
  77.1 1.3 %collective-permute-start.27 = (bf16[16,4096]{1,0:T(8,128)(2,1)S(1)}, bf16[16,4096]{1,0:T(8,128)(2,1)S(1)}, u32[]{:S(2)}, u32[]{:S(2)}) collective-permute-start(bf16[16,4096]{1,0:T(8,128)(2,1)S(1)} %split.49), channel_id=1, source_target_pairs={{0,8},{8,0},{16,24},{24,16},{1,9},{9,1},{17,25},{25,17},{2,10},{10... | collective-permute-start | bytes 393224 | tf_op jit(solution)/shard_map/ppermute | solution.py:20
  79.3 10.4 %collective-permute-done.27 = bf16[16,4096]{1,0:T(8,128)(2,1)S(1)} collective-permute-done((bf16[16,4096]{1,0:T(8,128)(2,1)S(1)}, bf16[16,4096]{1,0:T(8,128)(2,1)S(1)}, u32[]{:S(2)}, u32[]{:S(2)}) %collective-permute-start.27) | collective-permute-done | bytes 131104 | tf_op jit(solution)/shard_map/ppermute | solution.py:20
  90.6 1.3 %collective-permute-start.30 = (bf16[32,4096]{1,0:T(8,128)(2,1)S(1)}, bf16[32,4096]{1,0:T(8,128)(2,1)S(1)}, u32[]{:S(2)}, u32[]{:S(2)}) collective-permute-start(bf16[32,4096]{1,0:T(8,128)(2,1)S(1)} %pad_maximum_fusion.6), channel_id=1, source_target_pairs={{0,2},{1,3},{2,0},{3,1},{4,6},{5,7},{6,4},{7,5},{8,10},{9,11},{10,... | collective-permute-start | bytes 786440 | tf_op jit(solution)/shard_map/ppermute | solution.py:246
  92.9 3.7 %collective-permute-done.24 = bf16[32,4096]{1,0:T(8,128)(2,1)S(1)} collective-permute-done((bf16[32,4096]{1,0:T(8,128)(2,1)S(1)}, bf16[32,4096]{1,0:T(8,128)(2,1)S(1)}, u32[]{:S(2)}, u32[]{:S(2)}) %collective-permute-start.24) | collective-permute-done | bytes 262176 | tf_op jit(solution)/shard_map/ppermute | solution.py:20
  96.6 1.8 %collective-permute-done.23 = bf16[32,4096]{1,0:T(8,128)(2,1)S(1)} collective-permute-done((bf16[32,4096]{1,0:T(8,128)(2,1)S(1)}, bf16[32,4096]{1,0:T(8,128)(2,1)S(1)}, u32[]{:S(2)}, u32[]{:S(2)}) %collective-permute-start.23) | collective-permute-done | bytes 262176 | tf_op jit(solution)/shard_map/ppermute | solution.py:20
  99.3 1.6 %collective-permute-start.32 = (bf16[32,4096]{1,0:T(8,128)(2,1)S(1)}, bf16[32,4096]{1,0:T(8,128)(2,1)S(1)}, u32[]{:S(2)}, u32[]{:S(2)}) collective-permute-start(bf16[32,4096]{1,0:T(8,128)(2,1)S(1)} %add_convert_fusion.6), channel_id=1, source_target_pairs={{0,2},{1,3},{2,0},{3,1},{4,6},{5,7},{6,4},{7,5},{8,10},{9,11},{10,... | collective-permute-start | bytes 786440 | tf_op jit(solution)/shard_map/ppermute | solution.py:246
  100.9 1.5 %collective-permute-start.33 = (bf16[16,4096]{1,0:T(8,128)(2,1)S(1)}, bf16[16,4096]{1,0:T(8,128)(2,1)S(1)}, u32[]{:S(2)}, u32[]{:S(2)}) collective-permute-start(bf16[16,4096]{1,0:T(8,128)(2,1)S(1)} %split.47), channel_id=1, source_target_pairs={{0,16},{16,0},{8,24},{24,8},{1,17},{17,1},{9,25},{25,9},{2,18},{18... | collective-permute-start | bytes 393224 | tf_op jit(solution)/shard_map/ppermute | solution.py:20
  103.3 2.6 %collective-permute-done.33 = bf16[16,4096]{1,0:T(8,128)(2,1)S(1)} collective-permute-done((bf16[16,4096]{1,0:T(8,128)(2,1)S(1)}, bf16[16,4096]{1,0:T(8,128)(2,1)S(1)}, u32[]{:S(2)}, u32[]{:S(2)}) %collective-permute-start.33) | collective-permute-done | bytes 131104 | tf_op jit(solution)/shard_map/ppermute | solution.py:20
  105.9 1.5 %collective-permute-done.25 = bf16[16,4096]{1,0:T(8,128)(2,1)S(1)} collective-permute-done((bf16[16,4096]{1,0:T(8,128)(2,1)S(1)}, bf16[16,4096]{1,0:T(8,128)(2,1)S(1)}, u32[]{:S(2)}, u32[]{:S(2)}) %collective-permute-start.25) | collective-permute-done | bytes 131104 | tf_op jit(solution)/shard_map/ppermute | solution.py:20
  107.4 2.0 %collective-permute-done.31 = bf16[32,4096]{1,0:T(8,128)(2,1)S(1)} collective-permute-done((bf16[32,4096]{1,0:T(8,128)(2,1)S(1)}, bf16[32,4096]{1,0:T(8,128)(2,1)S(1)}, u32[]{:S(2)}, u32[]{:S(2)}) %collective-permute-start.31) | collective-permute-done | bytes 262176 | tf_op jit(solution)/shard_map/ppermute | solution.py:246
  (90 shorter events, 18.7 us)
Async XLA Ops:
  2.1 12.4 %collective-permute-start.3 = (bf16[16,4224]{1,0:T(8,128)(2,1)S(1)}, bf16[16,4224]{1,0:T(8,128)(2,1)S(1)}, u32[]{:S(2)}, u32[]{:S(2)}) collective-permute-start(bf16[16,4224]{1,0:T(8,128)(2,1)S(1)} %concatenate.38), channel_id=1, source_target_pairs={{0,4},{1,5},{2,6},{3,7},{4,0},{5,1},{6,2},{7,3},{8,12},{9,13},{10,... | collective-permute-start | bytes 405512 | tf_op jit(solution)/shard_map/ppermute | solution.py:246
  6.1 8.4 %collective-permute-start.2 = (bf16[16,4224]{1,0:T(8,128)(2,1)S(1)}, bf16[16,4224]{1,0:T(8,128)(2,1)S(1)}, u32[]{:S(2)}, u32[]{:S(2)}) collective-permute-start(bf16[16,4224]{1,0:T(8,128)(2,1)S(1)} %concatenate.38), channel_id=1, source_target_pairs={{0,2},{1,3},{2,0},{3,1},{4,6},{5,7},{6,4},{7,5},{8,10},{9,11},{10,... | collective-permute-start | bytes 405512 | tf_op jit(solution)/shard_map/ppermute | solution.py:246
  7.7 6.8 %collective-permute-start = (bf16[16,4224]{1,0:T(8,128)(2,1)S(1)}, bf16[16,4224]{1,0:T(8,128)(2,1)S(1)}, u32[]{:S(2)}, u32[]{:S(2)}) collective-permute-start(bf16[16,4224]{1,0:T(8,128)(2,1)S(1)} %concatenate.38), channel_id=1, source_target_pairs={{0,8},{8,0},{16,24},{24,16},{1,9},{9,1},{17,25},{25,17},{2,10},{10... | collective-permute-start | bytes 405512 | tf_op jit(solution)/shard_map/ppermute | solution.py:20
  9.2 5.3 %collective-permute-start.1 = (bf16[16,4224]{1,0:T(8,128)(2,1)S(1)}, bf16[16,4224]{1,0:T(8,128)(2,1)S(1)}, u32[]{:S(2)}, u32[]{:S(2)}) collective-permute-start(bf16[16,4224]{1,0:T(8,128)(2,1)S(1)} %concatenate.39), channel_id=1, source_target_pairs={{0,16},{16,0},{8,24},{24,8},{1,17},{17,1},{9,25},{25,9},{2,18},{18... | collective-permute-start | bytes 405512 | tf_op jit(solution)/shard_map/ppermute | solution.py:20
  14.5 20.9 %collective-permute-start.11 = (bf16[4096,768]{1,0:T(8,128)(2,1)S(1)}, bf16[4096,768]{1,0:T(8,128)(2,1)S(1)}, u32[]{:S(2)}, u32[]{:S(2)}) collective-permute-start(bf16[4096,768]{1,0:T(8,128)(2,1)S(1)} %dequantize_in.1.refs_4_), channel_id=1, source_target_pairs={{0,1},{1,0},{2,3},{3,2},{4,5},{5,4},{6,7},{7,6},{8,9},{9,8},{10,11... | collective-permute-start | bytes 18874376 | tf_op jit(solution)/shard_map/ppermute | solution.py:20
  14.6 11.0 %collective-permute-start.4 = (bf16[32,4224]{1,0:T(8,128)(2,1)S(1)}, bf16[32,4224]{1,0:T(8,128)(2,1)S(1)}, u32[]{:S(2)}, u32[]{:S(2)}) collective-permute-start(bf16[32,4224]{1,0:T(8,128)(2,1)S(1)} %pad_maximum_fusion.2.refs_0_), channel_id=1, source_target_pairs={{0,16},{16,0},{8,24},{24,8},{1,17},{17,1},{9,25},{25,9},{2,18},{18... | collective-permute-start | bytes 811016 | tf_op jit(solution)/shard_map/ppermute | solution.py:20
  15.9 9.7 %collective-permute-start.5 = (bf16[32,4224]{1,0:T(8,128)(2,1)S(1)}, bf16[32,4224]{1,0:T(8,128)(2,1)S(1)}, u32[]{:S(2)}, u32[]{:S(2)}) collective-permute-start(bf16[32,4224]{1,0:T(8,128)(2,1)S(1)} %pad_maximum_fusion.3.refs_2_), channel_id=1, source_target_pairs={{0,8},{8,0},{16,24},{24,16},{1,9},{9,1},{17,25},{25,17},{2,10},{10... | collective-permute-start | bytes 811016 | tf_op jit(solution)/shard_map/ppermute | solution.py:20
  16.5 9.2 %collective-permute-start.7 = (bf16[16,4224]{1,0:T(8,128)(2,1)S(1)}, bf16[16,4224]{1,0:T(8,128)(2,1)S(1)}, u32[]{:S(2)}, u32[]{:S(2)}) collective-permute-start(bf16[16,4224]{1,0:T(8,128)(2,1)S(1)} %concatenate.39), channel_id=1, source_target_pairs={{0,4},{1,5},{2,6},{3,7},{4,0},{5,1},{6,2},{7,3},{8,12},{9,13},{10,... | collective-permute-start | bytes 405512 | tf_op jit(solution)/shard_map/ppermute | solution.py:246
  17.3 8.4 %collective-permute-start.6 = (bf16[16,4224]{1,0:T(8,128)(2,1)S(1)}, bf16[16,4224]{1,0:T(8,128)(2,1)S(1)}, u32[]{:S(2)}, u32[]{:S(2)}) collective-permute-start(bf16[16,4224]{1,0:T(8,128)(2,1)S(1)} %concatenate.39), channel_id=1, source_target_pairs={{0,2},{1,3},{2,0},{3,1},{4,6},{5,7},{6,4},{7,5},{8,10},{9,11},{10,... | collective-permute-start | bytes 405512 | tf_op jit(solution)/shard_map/ppermute | solution.py:246
  25.6 9.8 %collective-permute-start.12 = (bf16[384,4096]{1,0:T(8,128)(2,1)S(1)}, bf16[384,4096]{1,0:T(8,128)(2,1)S(1)}, u32[]{:S(2)}, u32[]{:S(2)}) collective-permute-start(bf16[384,4096]{1,0:T(8,128)(2,1)S(1)} %dequantize_down.1.refs_6_), channel_id=1, source_target_pairs={{0,1},{1,0},{2,3},{3,2},{4,5},{5,4},{6,7},{7,6},{8,9},{9,8},{10,11... | collective-permute-start | bytes 9437192 | tf_op jit(solution)/shard_map/ppermute | solution.py:20
  25.8 9.6 %collective-permute-start.10 = (bf16[32,4224]{1,0:T(8,128)(2,1)S(1)}, bf16[32,4224]{1,0:T(8,128)(2,1)S(1)}, u32[]{:S(2)}, u32[]{:S(2)}) collective-permute-start(bf16[32,4224]{1,0:T(8,128)(2,1)S(1)} %constant_dynamic-update-slice_fusion.2), channel_id=1, source_target_pairs={{0,2},{1,3},{2,0},{3,1},{4,6},{5,7},{6,4},{7,5},{8,10},{9,11},{10,... | collective-permute-start | bytes 811016 | tf_op jit(solution)/shard_map/ppermute | solution.py:246
  25.8 8.9 %collective-permute-start.9 = (bf16[32,4224]{1,0:T(8,128)(2,1)S(1)}, bf16[32,4224]{1,0:T(8,128)(2,1)S(1)}, u32[]{:S(2)}, u32[]{:S(2)}) collective-permute-start(bf16[32,4224]{1,0:T(8,128)(2,1)S(1)} %constant_dynamic-update-slice_fusion.2), channel_id=1, source_target_pairs={{0,16},{16,0},{8,24},{24,8},{1,17},{17,1},{9,25},{25,9},{2,18},{18... | collective-permute-start | bytes 811016 | tf_op jit(solution)/shard_map/ppermute | solution.py:20
  26.7 8.7 %collective-permute-start.8 = (bf16[32,4224]{1,0:T(8,128)(2,1)S(1)}, bf16[32,4224]{1,0:T(8,128)(2,1)S(1)}, u32[]{:S(2)}, u32[]{:S(2)}) collective-permute-start(bf16[32,4224]{1,0:T(8,128)(2,1)S(1)} %constant_dynamic-update-slice_fusion), channel_id=1, source_target_pairs={{0,8},{8,0},{16,24},{24,16},{1,9},{9,1},{17,25},{25,17},{2,10},{10... | collective-permute-start | bytes 811016 | tf_op jit(solution)/shard_map/ppermute | solution.py:20
  35.5 8.6 %collective-permute-start.17 = (bf16[16,4224]{1,0:T(8,128)(2,1)S(1)}, bf16[16,4224]{1,0:T(8,128)(2,1)S(1)}, u32[]{:S(2)}, u32[]{:S(2)}) collective-permute-start(bf16[16,4224]{1,0:T(8,128)(2,1)S(1)} %get-tuple-element.141), channel_id=1, source_target_pairs={{0,16},{16,0},{8,24},{24,8},{1,17},{17,1},{9,25},{25,9},{2,18},{18... | collective-permute-start | bytes 405512 | tf_op jit(solution)/shard_map/ppermute | solution.py:20
  36.8 6.5 %collective-permute-start.15 = (bf16[16,4224]{1,0:T(8,128)(2,1)S(1)}, bf16[16,4224]{1,0:T(8,128)(2,1)S(1)}, u32[]{:S(2)}, u32[]{:S(2)}) collective-permute-start(bf16[16,4224]{1,0:T(8,128)(2,1)S(1)} %get-tuple-element.142), channel_id=1, source_target_pairs={{0,8},{8,0},{16,24},{24,16},{1,9},{9,1},{17,25},{25,17},{2,10},{10... | collective-permute-start | bytes 405512 | tf_op jit(solution)/shard_map/ppermute | solution.py:20
  38.2 15.2 %collective-permute-start.13 = (bf16[64,4224]{1,0:T(8,128)(2,1)S(1)}, bf16[64,4224]{1,0:T(8,128)(2,1)S(1)}, u32[]{:S(2)}, u32[]{:S(2)}) collective-permute-start(bf16[64,4224]{1,0:T(8,128)(2,1)S(1)} %pad_maximum_fusion.refs_0_), channel_id=1, source_target_pairs={{0,16},{16,0},{8,24},{24,8},{1,17},{17,1},{9,25},{25,9},{2,18},{18... | collective-permute-start | bytes 1622024 | tf_op jit(solution)/shard_map/ppermute | solution.py:20
  38.9 15.9 %collective-permute-start.14 = (bf16[64,4224]{1,0:T(8,128)(2,1)S(1)}, bf16[64,4224]{1,0:T(8,128)(2,1)S(1)}, u32[]{:S(2)}, u32[]{:S(2)}) collective-permute-start(bf16[64,4224]{1,0:T(8,128)(2,1)S(1)} %pad_maximum_fusion.1.refs_2_), channel_id=1, source_target_pairs={{0,8},{8,0},{16,24},{24,16},{1,9},{9,1},{17,25},{25,17},{2,10},{10... | collective-permute-start | bytes 1622024 | tf_op jit(solution)/shard_map/ppermute | solution.py:20
  43.3 21.3 %collective-permute-start.16 = (bf16[32,4224]{1,0:T(8,128)(2,1)S(1)}, bf16[32,4224]{1,0:T(8,128)(2,1)S(1)}, u32[]{:S(2)}, u32[]{:S(2)}) collective-permute-start(bf16[32,4224]{1,0:T(8,128)(2,1)S(1)} %pad_maximum_fusion.4.refs_0_), channel_id=1, source_target_pairs={{0,16},{16,0},{8,24},{24,8},{1,17},{17,1},{9,25},{25,9},{2,18},{18... | collective-permute-start | bytes 811016 | tf_op jit(solution)/shard_map/ppermute | solution.py:20
  44.1 20.5 %collective-permute-start.18 = (bf16[32,4224]{1,0:T(8,128)(2,1)S(1)}, bf16[32,4224]{1,0:T(8,128)(2,1)S(1)}, u32[]{:S(2)}, u32[]{:S(2)}) collective-permute-start(bf16[32,4224]{1,0:T(8,128)(2,1)S(1)} %pad_maximum_fusion.5.refs_2_), channel_id=1, source_target_pairs={{0,8},{8,0},{16,24},{24,16},{1,9},{9,1},{17,25},{25,17},{2,10},{10... | collective-permute-start | bytes 811016 | tf_op jit(solution)/shard_map/ppermute | solution.py:20
  54.8 8.7 %collective-permute-start.19 = (bf16[32,4096]{1,0:T(8,128)(2,1)S(1)}, bf16[32,4096]{1,0:T(8,128)(2,1)S(1)}, u32[]{:S(2)}, u32[]{:S(2)}) collective-permute-start(bf16[32,4096]{1,0:T(8,128)(2,1)S(1)} %get-tuple-element.108), channel_id=1, source_target_pairs={{0,16},{16,0},{8,24},{24,8},{1,17},{17,1},{9,25},{25,9},{2,18},{18... | collective-permute-start | bytes 786440 | tf_op jit(solution)/shard_map/ppermute | solution.py:20
  55.4 9.2 %collective-permute-start.20 = (bf16[32,4096]{1,0:T(8,128)(2,1)S(1)}, bf16[32,4096]{1,0:T(8,128)(2,1)S(1)}, u32[]{:S(2)}, u32[]{:S(2)}) collective-permute-start(bf16[32,4096]{1,0:T(8,128)(2,1)S(1)} %get-tuple-element.110), channel_id=1, source_target_pairs={{0,8},{8,0},{16,24},{24,16},{1,9},{9,1},{17,25},{25,17},{2,10},{10... | collective-permute-start | bytes 786440 | tf_op jit(solution)/shard_map/ppermute | solution.py:20
  67.7 9.3 %collective-permute-start.26 = (bf16[32,4096]{1,0:T(8,128)(2,1)S(1)}, bf16[32,4096]{1,0:T(8,128)(2,1)S(1)}, u32[]{:S(2)}, u32[]{:S(2)}) collective-permute-start(bf16[32,4096]{1,0:T(8,128)(2,1)S(1)} %get-tuple-element.126), channel_id=1, source_target_pairs={{0,16},{16,0},{8,24},{24,8},{1,17},{17,1},{9,25},{25,9},{2,18},{18... | collective-permute-start | bytes 786440 | tf_op jit(solution)/shard_map/ppermute | solution.py:20
  68.8 9.6 %collective-permute-start.28 = (bf16[32,4096]{1,0:T(8,128)(2,1)S(1)}, bf16[32,4096]{1,0:T(8,128)(2,1)S(1)}, u32[]{:S(2)}, u32[]{:S(2)}) collective-permute-start(bf16[32,4096]{1,0:T(8,128)(2,1)S(1)} %get-tuple-element.128), channel_id=1, source_target_pairs={{0,8},{8,0},{16,24},{24,16},{1,9},{9,1},{17,25},{25,17},{2,10},{10... | collective-permute-start | bytes 786440 | tf_op jit(solution)/shard_map/ppermute | solution.py:20
  69.8 20.0 %collective-permute-start.21 = (bf16[64,4096]{1,0:T(8,128)(2,1)S(1)}, bf16[64,4096]{1,0:T(8,128)(2,1)S(1)}, u32[]{:S(2)}, u32[]{:S(2)}) collective-permute-start(bf16[64,4096]{1,0:T(8,128)(2,1)S(1)} %get-tuple-element.118), channel_id=1, source_target_pairs={{0,16},{16,0},{8,24},{24,8},{1,17},{17,1},{9,25},{25,9},{2,18},{18... | collective-permute-start | bytes 1572872 | tf_op jit(solution)/shard_map/ppermute | solution.py:20
  71.1 18.9 %collective-permute-start.22 = (bf16[64,4096]{1,0:T(8,128)(2,1)S(1)}, bf16[64,4096]{1,0:T(8,128)(2,1)S(1)}, u32[]{:S(2)}, u32[]{:S(2)}) collective-permute-start(bf16[64,4096]{1,0:T(8,128)(2,1)S(1)} %get-tuple-element.120), channel_id=1, source_target_pairs={{0,8},{8,0},{16,24},{24,16},{1,9},{9,1},{17,25},{25,17},{2,10},{10... | collective-permute-start | bytes 1572872 | tf_op jit(solution)/shard_map/ppermute | solution.py:20
  77.1 12.6 %collective-permute-start.27 = (bf16[16,4096]{1,0:T(8,128)(2,1)S(1)}, bf16[16,4096]{1,0:T(8,128)(2,1)S(1)}, u32[]{:S(2)}, u32[]{:S(2)}) collective-permute-start(bf16[16,4096]{1,0:T(8,128)(2,1)S(1)} %split.49), channel_id=1, source_target_pairs={{0,8},{8,0},{16,24},{24,16},{1,9},{9,1},{17,25},{25,17},{2,10},{10... | collective-permute-start | bytes 393224 | tf_op jit(solution)/shard_map/ppermute | solution.py:20
  78.5 11.2 %collective-permute-start.29 = (bf16[16,4096]{1,0:T(8,128)(2,1)S(1)}, bf16[16,4096]{1,0:T(8,128)(2,1)S(1)}, u32[]{:S(2)}, u32[]{:S(2)}) collective-permute-start(bf16[16,4096]{1,0:T(8,128)(2,1)S(1)} %split.51), channel_id=1, source_target_pairs={{0,16},{16,0},{8,24},{24,8},{1,17},{17,1},{9,25},{25,9},{2,18},{18... | collective-permute-start | bytes 393224 | tf_op jit(solution)/shard_map/ppermute | solution.py:20
  90.1 6.4 %collective-permute-start.24 = (bf16[32,4096]{1,0:T(8,128)(2,1)S(1)}, bf16[32,4096]{1,0:T(8,128)(2,1)S(1)}, u32[]{:S(2)}, u32[]{:S(2)}) collective-permute-start(bf16[32,4096]{1,0:T(8,128)(2,1)S(1)} %split.39), channel_id=1, source_target_pairs={{0,16},{16,0},{8,24},{24,8},{1,17},{17,1},{9,25},{25,9},{2,18},{18... | collective-permute-start | bytes 786440 | tf_op jit(solution)/shard_map/ppermute | solution.py:20
  90.6 7.8 %collective-permute-start.30 = (bf16[32,4096]{1,0:T(8,128)(2,1)S(1)}, bf16[32,4096]{1,0:T(8,128)(2,1)S(1)}, u32[]{:S(2)}, u32[]{:S(2)}) collective-permute-start(bf16[32,4096]{1,0:T(8,128)(2,1)S(1)} %pad_maximum_fusion.6), channel_id=1, source_target_pairs={{0,2},{1,3},{2,0},{3,1},{4,6},{5,7},{6,4},{7,5},{8,10},{9,11},{10,... | collective-permute-start | bytes 786440 | tf_op jit(solution)/shard_map/ppermute | solution.py:246
  92.0 6.4 %collective-permute-start.23 = (bf16[32,4096]{1,0:T(8,128)(2,1)S(1)}, bf16[32,4096]{1,0:T(8,128)(2,1)S(1)}, u32[]{:S(2)}, u32[]{:S(2)}) collective-permute-start(bf16[32,4096]{1,0:T(8,128)(2,1)S(1)} %split.37), channel_id=1, source_target_pairs={{0,8},{8,0},{16,24},{24,16},{1,9},{9,1},{17,25},{25,17},{2,10},{10... | collective-permute-start | bytes 786440 | tf_op jit(solution)/shard_map/ppermute | solution.py:20
  98.5 10.8 %collective-permute-start.31 = (bf16[32,4096]{1,0:T(8,128)(2,1)S(1)}, bf16[32,4096]{1,0:T(8,128)(2,1)S(1)}, u32[]{:S(2)}, u32[]{:S(2)}) collective-permute-start(bf16[32,4096]{1,0:T(8,128)(2,1)S(1)} %add_convert_fusion.2), channel_id=1, source_target_pairs={{0,4},{1,5},{2,6},{3,7},{4,0},{5,1},{6,2},{7,3},{8,12},{9,13},{10,... | collective-permute-start | bytes 786440 | tf_op jit(solution)/shard_map/ppermute | solution.py:246
  99.3 10.1 %collective-permute-start.32 = (bf16[32,4096]{1,0:T(8,128)(2,1)S(1)}, bf16[32,4096]{1,0:T(8,128)(2,1)S(1)}, u32[]{:S(2)}, u32[]{:S(2)}) collective-permute-start(bf16[32,4096]{1,0:T(8,128)(2,1)S(1)} %add_convert_fusion.6), channel_id=1, source_target_pairs={{0,2},{1,3},{2,0},{3,1},{4,6},{5,7},{6,4},{7,5},{8,10},{9,11},{10,... | collective-permute-start | bytes 786440 | tf_op jit(solution)/shard_map/ppermute | solution.py:246
  (6 other events, 49.5 us)

commit v17 on v16

--- a/solution.py
+++ b/solution.py
@@ -362,16 +362,17 @@
     lanes[final - 1], outs = together((lanes[final - 1], outs))
     sum_turn(0, turns - 1)
     outs[final - 1] = layer(final - 1)
-    lanes, outs, sums = together((lanes, outs, sums))
+    lanes, outs = together((lanes, outs))
     outs[final] = layer(final)
+    outs[final], sums = together((outs[final], sums))
     for number in range(final, 0, -1):
         for turn in range(turns - 1 - int(number < final), -1, -1):
             sum_turn(number, turn)
             if turn == 0 and number > 1:
                 sum_turn(number - 1, turns - 1)
         if number > 1:
+            sums, outs = together((sums, outs))
             leave(number)
-        sums, outs = together((sums, outs))
     leave(1)
     for turn in range(turns - 2, -1, -1):
         sum_turn(0, turn)

time: 110 us -> 114 us (1.036)
  waiting for transfers between devices: 48.9 us -> 54.3 us
  starting transfers between devices: 38.6 us -> 36.6 us
    ppermute x26, waiting for transfers between devices: 43.7 us -> 46.6 us  [from_partner(): return lax.ppermute(block, axis, route)]
    ppermute x8, waiting for transfers between devices: 5.17 us -> 7.8 us  [across_chips(): lax.ppermute(block, 'expert', [(low, low ^ 2 * far) for low in range(coun...]
    ppermute x8, starting transfers between devices: 12.6 us -> 10 us  [across_chips(): lax.ppermute(block, 'expert', [(low, low ^ 2 * far) for low in range(coun...]
  transfers between devices with their start and end apart: 34 -> 34, of which waited for: 15 -> 15; matrix products, arithmetic and copies ran while one was open for 1% -> 1% of each run, Pallas kernels for 14% -> 16%
where the time goes in v17:
time: 114 us
  waiting for transfers between devices  54.3 us (48%)
  starting transfers between devices  36.6 us (32%)
  Pallas kernels  18.3 us (16%)
  other arithmetic  2.54 us (2%)
  local copies, waits for them, and re-layouts  1.46 us (1%)
    ppermute x26, waiting for transfers between devices, from_partner(): return lax.ppermute(block, axis, route)  46.6 us
    ppermute x26, starting transfers between devices, from_partner(): return lax.ppermute(block, axis, route)  26.6 us
    pallas_call x3, Pallas kernels, expert_layer(): pl.pallas_call(functools.partial(expert_kernel, count, experts), in_specs...  11.9 us
    ppermute x8, starting transfers between devices, across_chips(): lax.ppermute(block, 'expert', [(low, low ^ 2 * far) for low in range(coun...  10 us
    ppermute x8, waiting for transfers between devices, across_chips(): lax.ppermute(block, 'expert', [(low, low ^ 2 * far) for low in range(coun...  7.8 us
    pallas_call x2, Pallas kernels, dequantize_call(): pl.pallas_call(kernel, in_specs=[pl.BlockSpec(memory_space=pltpu.SMEM)] *...  6.46 us
  transfers between devices with their start and end apart: 34, of which 15 were waited for; matrix products, arithmetic and copies ran while one was open for 1% of the time, Pallas kernels for 16%

profile of v17, /device:TPU:0, one launch (start us, length us, event | category | flops | bytes accessed | tf_op | source)
XLA Modules:
  0.0 113.6 jit_solution(3434021818643374447)
XLA Ops:
  2.0 2.9 %collective-permute-start = (bf16[16,4224]{1,0:T(8,128)(2,1)S(1)}, bf16[16,4224]{1,0:T(8,128)(2,1)S(1)}, u32[]{:S(2)}, u32[]{:S(2)}) collective-permute-start(bf16[16,4224]{1,0:T(8,128)(2,1)S(1)} %concatenate.38), channel_id=1, source_target_pairs={{0,8},{8,0},{16,24},{24,16},{1,9},{9,1},{17,25},{25,17},{2,10},{10... | collective-permute-start | bytes 405512 | tf_op jit(solution)/shard_map/ppermute | solution.py:20
  5.0 1.6 %collective-permute-start.2 = (bf16[16,4224]{1,0:T(8,128)(2,1)S(1)}, bf16[16,4224]{1,0:T(8,128)(2,1)S(1)}, u32[]{:S(2)}, u32[]{:S(2)}) collective-permute-start(bf16[16,4224]{1,0:T(8,128)(2,1)S(1)} %concatenate.38), channel_id=1, source_target_pairs={{0,2},{1,3},{2,0},{3,1},{4,6},{5,7},{6,4},{7,5},{8,10},{9,11},{10,... | collective-permute-start | bytes 405512 | tf_op jit(solution)/shard_map/ppermute | solution.py:246
  6.6 2.6 %collective-permute-start.3 = (bf16[16,4224]{1,0:T(8,128)(2,1)S(1)}, bf16[16,4224]{1,0:T(8,128)(2,1)S(1)}, u32[]{:S(2)}, u32[]{:S(2)}) collective-permute-start(bf16[16,4224]{1,0:T(8,128)(2,1)S(1)} %concatenate.38), channel_id=1, source_target_pairs={{0,4},{1,5},{2,6},{3,7},{4,0},{5,1},{6,2},{7,3},{8,12},{9,13},{10,... | collective-permute-start | bytes 405512 | tf_op jit(solution)/shard_map/ppermute | solution.py:246
  9.1 1.5 %collective-permute-start.1 = (bf16[16,4224]{1,0:T(8,128)(2,1)S(1)}, bf16[16,4224]{1,0:T(8,128)(2,1)S(1)}, u32[]{:S(2)}, u32[]{:S(2)}) collective-permute-start(bf16[16,4224]{1,0:T(8,128)(2,1)S(1)} %concatenate.39), channel_id=1, source_target_pairs={{0,16},{16,0},{8,24},{24,8},{1,17},{17,1},{9,25},{25,9},{2,18},{18... | collective-permute-start | bytes 405512 | tf_op jit(solution)/shard_map/ppermute | solution.py:20
  10.7 3.7 %dequantize_in.1.refs_4_ = bf16[4096,768]{1,0:T(8,128)(2,1)S(1)} custom-call(f32[3,32]{1,0:T(4,128)S(1)} %get-tuple-element.156.gate_scales, f32[3,32]{1,0:T(4,128)S(1)} %get-tuple-element.155.up_scales, bf16[4096,384]{1,0:T(8,128)(2,1)} %bitcast.17, bf16[4096,384]{1,0:T(8,128)(2,1)} %bitcast.18), custom_call_target="tpu_custom_call" | custom-call | flops 3145728 | bytes 12582912 | tf_op jit(solution)/shard_map/dequantize_in/pallas_call | solution.py:155
  15.2 1.5 %collective-permute-start.4 = (bf16[32,4224]{1,0:T(8,128)(2,1)S(1)}, bf16[32,4224]{1,0:T(8,128)(2,1)S(1)}, u32[]{:S(2)}, u32[]{:S(2)}) collective-permute-start(bf16[32,4224]{1,0:T(8,128)(2,1)S(1)} %pad_maximum_fusion.2.refs_0_), channel_id=1, source_target_pairs={{0,16},{16,0},{8,24},{24,8},{1,17},{17,1},{9,25},{25,9},{2,18},{18... | collective-permute-start | bytes 811016 | tf_op jit(solution)/shard_map/ppermute | solution.py:20
  17.6 2.7 %collective-permute-start.7 = (bf16[16,4224]{1,0:T(8,128)(2,1)S(1)}, bf16[16,4224]{1,0:T(8,128)(2,1)S(1)}, u32[]{:S(2)}, u32[]{:S(2)}) collective-permute-start(bf16[16,4224]{1,0:T(8,128)(2,1)S(1)} %concatenate.39), channel_id=1, source_target_pairs={{0,4},{1,5},{2,6},{3,7},{4,0},{5,1},{6,2},{7,3},{8,12},{9,13},{10,... | collective-permute-start | bytes 405512 | tf_op jit(solution)/shard_map/ppermute | solution.py:246
  20.3 2.8 %dequantize_down.1.refs_6_ = bf16[384,4096]{1,0:T(8,128)(2,1)S(1)} custom-call(f32[3,32]{1,0:T(4,128)S(1)} %bitcast.15, bf16[384,4096]{1,0:T(8,128)(2,1)} %bitcast.16), custom_call_target="tpu_custom_call" | custom-call | flops 1572864 | bytes 6291456 | tf_op jit(solution)/shard_map/dequantize_down/pallas_call | solution.py:155
  23.0 2.3 %collective-permute-done.6 = bf16[16,4224]{1,0:T(8,128)(2,1)S(1)} collective-permute-done((bf16[16,4224]{1,0:T(8,128)(2,1)S(1)}, bf16[16,4224]{1,0:T(8,128)(2,1)S(1)}, u32[]{:S(2)}, u32[]{:S(2)}) %collective-permute-start.6) | collective-permute-done | bytes 135200 | tf_op jit(solution)/shard_map/ppermute | solution.py:246
  25.3 1.3 %collective-permute-done.7 = bf16[16,4224]{1,0:T(8,128)(2,1)S(1)} collective-permute-done((bf16[16,4224]{1,0:T(8,128)(2,1)S(1)}, bf16[16,4224]{1,0:T(8,128)(2,1)S(1)}, u32[]{:S(2)}, u32[]{:S(2)}) %collective-permute-start.7) | collective-permute-done | bytes 135200 | tf_op jit(solution)/shard_map/ppermute | solution.py:246
  26.7 1.6 %collective-permute-start.8 = (bf16[32,4224]{1,0:T(8,128)(2,1)S(1)}, bf16[32,4224]{1,0:T(8,128)(2,1)S(1)}, u32[]{:S(2)}, u32[]{:S(2)}) collective-permute-start(bf16[32,4224]{1,0:T(8,128)(2,1)S(1)} %constant_dynamic-update-slice_fusion), channel_id=1, source_target_pairs={{0,8},{8,0},{16,24},{24,16},{1,9},{9,1},{17,25},{25,17},{2,10},{10... | collective-permute-start | bytes 811016 | tf_op jit(solution)/shard_map/ppermute | solution.py:20
  29.2 6.5 %collective-permute-done.8 = bf16[32,4224]{1,0:T(8,128)(2,1)S(1)} collective-permute-done((bf16[32,4224]{1,0:T(8,128)(2,1)S(1)}, bf16[32,4224]{1,0:T(8,128)(2,1)S(1)}, u32[]{:S(2)}, u32[]{:S(2)}) %collective-permute-start.8) | collective-permute-done | bytes 270368 | tf_op jit(solution)/shard_map/ppermute | solution.py:20
  35.7 1.3 %collective-permute-done.9 = bf16[32,4224]{1,0:T(8,128)(2,1)S(1)} collective-permute-done((bf16[32,4224]{1,0:T(8,128)(2,1)S(1)}, bf16[32,4224]{1,0:T(8,128)(2,1)S(1)}, u32[]{:S(2)}, u32[]{:S(2)}) %collective-permute-start.9) | collective-permute-done | bytes 270368 | tf_op jit(solution)/shard_map/ppermute | solution.py:20
  37.2 1.5 %collective-permute-start.13 = (bf16[64,4224]{1,0:T(8,128)(2,1)S(1)}, bf16[64,4224]{1,0:T(8,128)(2,1)S(1)}, u32[]{:S(2)}, u32[]{:S(2)}) collective-permute-start(bf16[64,4224]{1,0:T(8,128)(2,1)S(1)} %pad_maximum_fusion.refs_0_), channel_id=1, source_target_pairs={{0,16},{16,0},{8,24},{24,8},{1,17},{17,1},{9,25},{25,9},{2,18},{18... | collective-permute-start | bytes 1622024 | tf_op jit(solution)/shard_map/ppermute | solution.py:20
  39.2 1.6 %collective-permute-start.15 = (bf16[16,4224]{1,0:T(8,128)(2,1)S(1)}, bf16[16,4224]{1,0:T(8,128)(2,1)S(1)}, u32[]{:S(2)}, u32[]{:S(2)}) collective-permute-start(bf16[16,4224]{1,0:T(8,128)(2,1)S(1)} %get-tuple-element.146), channel_id=1, source_target_pairs={{0,8},{8,0},{16,24},{24,16},{1,9},{9,1},{17,25},{25,17},{2,10},{10... | collective-permute-start | bytes 405512 | tf_op jit(solution)/shard_map/ppermute | solution.py:20
  41.3 3.1 %expert_layer.3 = (bf16[32,4096]{1,0:T(8,128)(2,1)S(1)}, bf16[32,4096]{1,0:T(8,128)(2,1)S(1)}, bf16[32,4096]{1,0:T(8,128)(2,1)S(1)}, bf16[32,4096]{1,0:T(8,128)(2,1)S(1)}) custom-call(s32[1]{0:T(128)} %bitcast.own_expert, bf16[32,4224]{1,0:T(8,128)(2,1)S(1)} %pad_maximum_fusion.2.refs_0_, bf16[32,4224]{1,0:T(8,128)(2,1)S(1)} %collective-permute-done.4.refs_1_, ...), custom_call_target="tpu_custom_call" | custom-call | flops 2415919104 | bytes 20971520 | tf_op jit(solution)/shard_map/expert_layer/pallas_call | solution.py:225
  44.4 10.2 %collective-permute-done.15 = bf16[16,4224]{1,0:T(8,128)(2,1)S(1)} collective-permute-done((bf16[16,4224]{1,0:T(8,128)(2,1)S(1)}, bf16[16,4224]{1,0:T(8,128)(2,1)S(1)}, u32[]{:S(2)}, u32[]{:S(2)}) %collective-permute-start.15) | collective-permute-done | bytes 135200 | tf_op jit(solution)/shard_map/ppermute | solution.py:20
  56.0 1.3 %collective-permute-start.19 = (bf16[32,4096]{1,0:T(8,128)(2,1)S(1)}, bf16[32,4096]{1,0:T(8,128)(2,1)S(1)}, u32[]{:S(2)}, u32[]{:S(2)}) collective-permute-start(bf16[32,4096]{1,0:T(8,128)(2,1)S(1)} %get-tuple-element.110), channel_id=1, source_target_pairs={{0,16},{16,0},{8,24},{24,8},{1,17},{17,1},{9,25},{25,9},{2,18},{18... | collective-permute-start | bytes 786440 | tf_op jit(solution)/shard_map/ppermute | solution.py:20
  57.3 1.5 %collective-permute-start.20 = (bf16[32,4096]{1,0:T(8,128)(2,1)S(1)}, bf16[32,4096]{1,0:T(8,128)(2,1)S(1)}, u32[]{:S(2)}, u32[]{:S(2)}) collective-permute-start(bf16[32,4096]{1,0:T(8,128)(2,1)S(1)} %get-tuple-element.112), channel_id=1, source_target_pairs={{0,8},{8,0},{16,24},{24,16},{1,9},{9,1},{17,25},{25,17},{2,10},{10... | collective-permute-start | bytes 786440 | tf_op jit(solution)/shard_map/ppermute | solution.py:20
  58.8 5.7 %expert_layer.4 = (bf16[64,4096]{1,0:T(8,128)(2,1)S(1)}, bf16[64,4096]{1,0:T(8,128)(2,1)S(1)}, bf16[64,4096]{1,0:T(8,128)(2,1)S(1)}, bf16[64,4096]{1,0:T(8,128)(2,1)S(1)}) custom-call(s32[1]{0:T(128)} %bitcast.own_expert, bf16[64,4224]{1,0:T(8,128)(2,1)S(1)} %pad_maximum_fusion.refs_0_, bf16[64,4224]{1,0:T(8,128)(2,1)S(1)} %collective-permute-done.13.refs_1_, ...), custom_call_target="tpu_custom_call" | custom-call | flops 4831838208 | bytes 23068672 | tf_op jit(solution)/shard_map/expert_layer/pallas_call | solution.py:225
  64.5 3.1 %expert_layer.5 = (bf16[32,4096]{1,0:T(8,128)(2,1)S(1)}, bf16[32,4096]{1,0:T(8,128)(2,1)S(1)}, bf16[32,4096]{1,0:T(8,128)(2,1)S(1)}, bf16[32,4096]{1,0:T(8,128)(2,1)S(1)}) custom-call(s32[1]{0:T(128)} %bitcast.own_expert, bf16[32,4224]{1,0:T(8,128)(2,1)S(1)} %pad_maximum_fusion.4.refs_0_, bf16[32,4224]{1,0:T(8,128)(2,1)S(1)} %collective-permute-done.16.refs_1_, ...), custom_call_target="tpu_custom_call" | custom-call | flops 2415919104 | bytes 20971520 | tf_op jit(solution)/shard_map/expert_layer/pallas_call | solution.py:225
  67.8 1.1 collective-permute-start.23
  68.9 1.0 collective-permute-start.21
  70.4 1.5 %collective-permute-start.25 = (bf16[32,4096]{1,0:T(8,128)(2,1)S(1)}, bf16[32,4096]{1,0:T(8,128)(2,1)S(1)}, u32[]{:S(2)}, u32[]{:S(2)}) collective-permute-start(bf16[32,4096]{1,0:T(8,128)(2,1)S(1)} %get-tuple-element.134), channel_id=1, source_target_pairs={{0,8},{8,0},{16,24},{24,16},{1,9},{9,1},{17,25},{25,17},{2,10},{10... | collective-permute-start | bytes 786440 | tf_op jit(solution)/shard_map/ppermute | solution.py:20
  71.9 5.2 %collective-permute-done.23 = bf16[32,4096]{1,0:T(8,128)(2,1)S(1)} collective-permute-done((bf16[32,4096]{1,0:T(8,128)(2,1)S(1)}, bf16[32,4096]{1,0:T(8,128)(2,1)S(1)}, u32[]{:S(2)}, u32[]{:S(2)}) %collective-permute-start.23) | collective-permute-done | bytes 262176 | tf_op jit(solution)/shard_map/ppermute | solution.py:20
  77.8 9.2 %collective-permute-done.25 = bf16[32,4096]{1,0:T(8,128)(2,1)S(1)} collective-permute-done((bf16[32,4096]{1,0:T(8,128)(2,1)S(1)}, bf16[32,4096]{1,0:T(8,128)(2,1)S(1)}, u32[]{:S(2)}, u32[]{:S(2)}) %collective-permute-start.25) | collective-permute-done | bytes 262176 | tf_op jit(solution)/shard_map/ppermute | solution.py:20
  88.4 4.6 %collective-permute-done.26 = bf16[16,4096]{1,0:T(8,128)(2,1)S(1)} collective-permute-done((bf16[16,4096]{1,0:T(8,128)(2,1)S(1)}, bf16[16,4096]{1,0:T(8,128)(2,1)S(1)}, u32[]{:S(2)}, u32[]{:S(2)}) %collective-permute-start.26) | collective-permute-done | bytes 131104 | tf_op jit(solution)/shard_map/ppermute | solution.py:20
  94.3 1.1 collective-permute-start.28
  95.3 5.6 %collective-permute-done.31 = bf16[32,4096]{1,0:T(8,128)(2,1)S(1)} collective-permute-done((bf16[32,4096]{1,0:T(8,128)(2,1)S(1)}, bf16[32,4096]{1,0:T(8,128)(2,1)S(1)}, u32[]{:S(2)}, u32[]{:S(2)}) %collective-permute-start.31) | collective-permute-done | bytes 262176 | tf_op jit(solution)/shard_map/ppermute | solution.py:20
  102.5 2.0 %collective-permute-start.30 = (bf16[32,4096]{1,0:T(8,128)(2,1)S(1)}, bf16[32,4096]{1,0:T(8,128)(2,1)S(1)}, u32[]{:S(2)}, u32[]{:S(2)}) collective-permute-start(bf16[32,4096]{1,0:T(8,128)(2,1)S(1)} %add_convert_fusion.3), channel_id=1, source_target_pairs={{0,4},{1,5},{2,6},{3,7},{4,0},{5,1},{6,2},{7,3},{8,12},{9,13},{10,... | collective-permute-start | bytes 786440 | tf_op jit(solution)/shard_map/ppermute | solution.py:246
  106.4 3.2 %collective-permute-done.27 = bf16[16,4096]{1,0:T(8,128)(2,1)S(1)} collective-permute-done((bf16[16,4096]{1,0:T(8,128)(2,1)S(1)}, bf16[16,4096]{1,0:T(8,128)(2,1)S(1)}, u32[]{:S(2)}, u32[]{:S(2)}) %collective-permute-start.27) | collective-permute-done | bytes 131104 | tf_op jit(solution)/shard_map/ppermute | solution.py:20
  110.4 2.3 %collective-permute-done.30 = bf16[32,4096]{1,0:T(8,128)(2,1)S(1)} collective-permute-done((bf16[32,4096]{1,0:T(8,128)(2,1)S(1)}, bf16[32,4096]{1,0:T(8,128)(2,1)S(1)}, u32[]{:S(2)}, u32[]{:S(2)}) %collective-permute-start.30) | collective-permute-done | bytes 262176 | tf_op jit(solution)/shard_map/ppermute | solution.py:246
  (89 shorter events, 16.5 us)
Async XLA Ops:
  2.0 12.4 %collective-permute-start = (bf16[16,4224]{1,0:T(8,128)(2,1)S(1)}, bf16[16,4224]{1,0:T(8,128)(2,1)S(1)}, u32[]{:S(2)}, u32[]{:S(2)}) collective-permute-start(bf16[16,4224]{1,0:T(8,128)(2,1)S(1)} %concatenate.38), channel_id=1, source_target_pairs={{0,8},{8,0},{16,24},{24,16},{1,9},{9,1},{17,25},{25,17},{2,10},{10... | collective-permute-start | bytes 405512 | tf_op jit(solution)/shard_map/ppermute | solution.py:20
  5.0 9.5 %collective-permute-start.2 = (bf16[16,4224]{1,0:T(8,128)(2,1)S(1)}, bf16[16,4224]{1,0:T(8,128)(2,1)S(1)}, u32[]{:S(2)}, u32[]{:S(2)}) collective-permute-start(bf16[16,4224]{1,0:T(8,128)(2,1)S(1)} %concatenate.38), channel_id=1, source_target_pairs={{0,2},{1,3},{2,0},{3,1},{4,6},{5,7},{6,4},{7,5},{8,10},{9,11},{10,... | collective-permute-start | bytes 405512 | tf_op jit(solution)/shard_map/ppermute | solution.py:246
  6.6 8.6 %collective-permute-start.3 = (bf16[16,4224]{1,0:T(8,128)(2,1)S(1)}, bf16[16,4224]{1,0:T(8,128)(2,1)S(1)}, u32[]{:S(2)}, u32[]{:S(2)}) collective-permute-start(bf16[16,4224]{1,0:T(8,128)(2,1)S(1)} %concatenate.38), channel_id=1, source_target_pairs={{0,4},{1,5},{2,6},{3,7},{4,0},{5,1},{6,2},{7,3},{8,12},{9,13},{10,... | collective-permute-start | bytes 405512 | tf_op jit(solution)/shard_map/ppermute | solution.py:246
  9.1 5.3 %collective-permute-start.1 = (bf16[16,4224]{1,0:T(8,128)(2,1)S(1)}, bf16[16,4224]{1,0:T(8,128)(2,1)S(1)}, u32[]{:S(2)}, u32[]{:S(2)}) collective-permute-start(bf16[16,4224]{1,0:T(8,128)(2,1)S(1)} %concatenate.39), channel_id=1, source_target_pairs={{0,16},{16,0},{8,24},{24,8},{1,17},{17,1},{9,25},{25,9},{2,18},{18... | collective-permute-start | bytes 405512 | tf_op jit(solution)/shard_map/ppermute | solution.py:20
  15.2 22.0 %collective-permute-start.11 = (bf16[4096,768]{1,0:T(8,128)(2,1)S(1)}, bf16[4096,768]{1,0:T(8,128)(2,1)S(1)}, u32[]{:S(2)}, u32[]{:S(2)}) collective-permute-start(bf16[4096,768]{1,0:T(8,128)(2,1)S(1)} %dequantize_in.1.refs_4_), channel_id=1, source_target_pairs={{0,1},{1,0},{2,3},{3,2},{4,5},{5,4},{6,7},{7,6},{8,9},{9,8},{10,11... | collective-permute-start | bytes 18874376 | tf_op jit(solution)/shard_map/ppermute | solution.py:20
  15.2 11.5 %collective-permute-start.4 = (bf16[32,4224]{1,0:T(8,128)(2,1)S(1)}, bf16[32,4224]{1,0:T(8,128)(2,1)S(1)}, u32[]{:S(2)}, u32[]{:S(2)}) collective-permute-start(bf16[32,4224]{1,0:T(8,128)(2,1)S(1)} %pad_maximum_fusion.2.refs_0_), channel_id=1, source_target_pairs={{0,16},{16,0},{8,24},{24,8},{1,17},{17,1},{9,25},{25,9},{2,18},{18... | collective-permute-start | bytes 811016 | tf_op jit(solution)/shard_map/ppermute | solution.py:20
  16.7 9.9 %collective-permute-start.5 = (bf16[32,4224]{1,0:T(8,128)(2,1)S(1)}, bf16[32,4224]{1,0:T(8,128)(2,1)S(1)}, u32[]{:S(2)}, u32[]{:S(2)}) collective-permute-start(bf16[32,4224]{1,0:T(8,128)(2,1)S(1)} %pad_maximum_fusion.3.refs_2_), channel_id=1, source_target_pairs={{0,8},{8,0},{16,24},{24,16},{1,9},{9,1},{17,25},{25,17},{2,10},{10... | collective-permute-start | bytes 811016 | tf_op jit(solution)/shard_map/ppermute | solution.py:20
  17.2 8.1 %collective-permute-start.6 = (bf16[16,4224]{1,0:T(8,128)(2,1)S(1)}, bf16[16,4224]{1,0:T(8,128)(2,1)S(1)}, u32[]{:S(2)}, u32[]{:S(2)}) collective-permute-start(bf16[16,4224]{1,0:T(8,128)(2,1)S(1)} %concatenate.39), channel_id=1, source_target_pairs={{0,2},{1,3},{2,0},{3,1},{4,6},{5,7},{6,4},{7,5},{8,10},{9,11},{10,... | collective-permute-start | bytes 405512 | tf_op jit(solution)/shard_map/ppermute | solution.py:246
  17.6 9.0 %collective-permute-start.7 = (bf16[16,4224]{1,0:T(8,128)(2,1)S(1)}, bf16[16,4224]{1,0:T(8,128)(2,1)S(1)}, u32[]{:S(2)}, u32[]{:S(2)}) collective-permute-start(bf16[16,4224]{1,0:T(8,128)(2,1)S(1)} %concatenate.39), channel_id=1, source_target_pairs={{0,4},{1,5},{2,6},{3,7},{4,0},{5,1},{6,2},{7,3},{8,12},{9,13},{10,... | collective-permute-start | bytes 405512 | tf_op jit(solution)/shard_map/ppermute | solution.py:246
  26.6 10.5 %collective-permute-start.12 = (bf16[384,4096]{1,0:T(8,128)(2,1)S(1)}, bf16[384,4096]{1,0:T(8,128)(2,1)S(1)}, u32[]{:S(2)}, u32[]{:S(2)}) collective-permute-start(bf16[384,4096]{1,0:T(8,128)(2,1)S(1)} %dequantize_down.1.refs_6_), channel_id=1, source_target_pairs={{0,1},{1,0},{2,3},{3,2},{4,5},{5,4},{6,7},{7,6},{8,9},{9,8},{10,11... | collective-permute-start | bytes 9437192 | tf_op jit(solution)/shard_map/ppermute | solution.py:20
  26.7 8.9 %collective-permute-start.8 = (bf16[32,4224]{1,0:T(8,128)(2,1)S(1)}, bf16[32,4224]{1,0:T(8,128)(2,1)S(1)}, u32[]{:S(2)}, u32[]{:S(2)}) collective-permute-start(bf16[32,4224]{1,0:T(8,128)(2,1)S(1)} %constant_dynamic-update-slice_fusion), channel_id=1, source_target_pairs={{0,8},{8,0},{16,24},{24,16},{1,9},{9,1},{17,25},{25,17},{2,10},{10... | collective-permute-start | bytes 811016 | tf_op jit(solution)/shard_map/ppermute | solution.py:20
  28.3 8.7 %collective-permute-start.9 = (bf16[32,4224]{1,0:T(8,128)(2,1)S(1)}, bf16[32,4224]{1,0:T(8,128)(2,1)S(1)}, u32[]{:S(2)}, u32[]{:S(2)}) collective-permute-start(bf16[32,4224]{1,0:T(8,128)(2,1)S(1)} %constant_dynamic-update-slice_fusion.2), channel_id=1, source_target_pairs={{0,16},{16,0},{8,24},{24,8},{1,17},{17,1},{9,25},{25,9},{2,18},{18... | collective-permute-start | bytes 811016 | tf_op jit(solution)/shard_map/ppermute | solution.py:20
  28.8 8.3 %collective-permute-start.10 = (bf16[32,4224]{1,0:T(8,128)(2,1)S(1)}, bf16[32,4224]{1,0:T(8,128)(2,1)S(1)}, u32[]{:S(2)}, u32[]{:S(2)}) collective-permute-start(bf16[32,4224]{1,0:T(8,128)(2,1)S(1)} %constant_dynamic-update-slice_fusion.2), channel_id=1, source_target_pairs={{0,2},{1,3},{2,0},{3,1},{4,6},{5,7},{6,4},{7,5},{8,10},{9,11},{10,... | collective-permute-start | bytes 811016 | tf_op jit(solution)/shard_map/ppermute | solution.py:246
  37.2 18.9 %collective-permute-start.13 = (bf16[64,4224]{1,0:T(8,128)(2,1)S(1)}, bf16[64,4224]{1,0:T(8,128)(2,1)S(1)}, u32[]{:S(2)}, u32[]{:S(2)}) collective-permute-start(bf16[64,4224]{1,0:T(8,128)(2,1)S(1)} %pad_maximum_fusion.refs_0_), channel_id=1, source_target_pairs={{0,16},{16,0},{8,24},{24,8},{1,17},{17,1},{9,25},{25,9},{2,18},{18... | collective-permute-start | bytes 1622024 | tf_op jit(solution)/shard_map/ppermute | solution.py:20
  38.7 17.4 %collective-permute-start.14 = (bf16[64,4224]{1,0:T(8,128)(2,1)S(1)}, bf16[64,4224]{1,0:T(8,128)(2,1)S(1)}, u32[]{:S(2)}, u32[]{:S(2)}) collective-permute-start(bf16[64,4224]{1,0:T(8,128)(2,1)S(1)} %pad_maximum_fusion.1.refs_2_), channel_id=1, source_target_pairs={{0,8},{8,0},{16,24},{24,16},{1,9},{9,1},{17,25},{25,17},{2,10},{10... | collective-permute-start | bytes 1622024 | tf_op jit(solution)/shard_map/ppermute | solution.py:20
  39.2 15.3 %collective-permute-start.15 = (bf16[16,4224]{1,0:T(8,128)(2,1)S(1)}, bf16[16,4224]{1,0:T(8,128)(2,1)S(1)}, u32[]{:S(2)}, u32[]{:S(2)}) collective-permute-start(bf16[16,4224]{1,0:T(8,128)(2,1)S(1)} %get-tuple-element.146), channel_id=1, source_target_pairs={{0,8},{8,0},{16,24},{24,16},{1,9},{9,1},{17,25},{25,17},{2,10},{10... | collective-permute-start | bytes 405512 | tf_op jit(solution)/shard_map/ppermute | solution.py:20
  40.8 14.6 %collective-permute-start.17 = (bf16[16,4224]{1,0:T(8,128)(2,1)S(1)}, bf16[16,4224]{1,0:T(8,128)(2,1)S(1)}, u32[]{:S(2)}, u32[]{:S(2)}) collective-permute-start(bf16[16,4224]{1,0:T(8,128)(2,1)S(1)} %get-tuple-element.145), channel_id=1, source_target_pairs={{0,16},{16,0},{8,24},{24,8},{1,17},{17,1},{9,25},{25,9},{2,18},{18... | collective-permute-start | bytes 405512 | tf_op jit(solution)/shard_map/ppermute | solution.py:20
  54.6 9.9 %collective-permute-start.16 = (bf16[32,4224]{1,0:T(8,128)(2,1)S(1)}, bf16[32,4224]{1,0:T(8,128)(2,1)S(1)}, u32[]{:S(2)}, u32[]{:S(2)}) collective-permute-start(bf16[32,4224]{1,0:T(8,128)(2,1)S(1)} %pad_maximum_fusion.4.refs_0_), channel_id=1, source_target_pairs={{0,16},{16,0},{8,24},{24,8},{1,17},{17,1},{9,25},{25,9},{2,18},{18... | collective-permute-start | bytes 811016 | tf_op jit(solution)/shard_map/ppermute | solution.py:20
  55.4 9.1 %collective-permute-start.18 = (bf16[32,4224]{1,0:T(8,128)(2,1)S(1)}, bf16[32,4224]{1,0:T(8,128)(2,1)S(1)}, u32[]{:S(2)}, u32[]{:S(2)}) collective-permute-start(bf16[32,4224]{1,0:T(8,128)(2,1)S(1)} %pad_maximum_fusion.5.refs_2_), channel_id=1, source_target_pairs={{0,8},{8,0},{16,24},{24,16},{1,9},{9,1},{17,25},{25,17},{2,10},{10... | collective-permute-start | bytes 811016 | tf_op jit(solution)/shard_map/ppermute | solution.py:20
  56.0 11.6 %collective-permute-start.19 = (bf16[32,4096]{1,0:T(8,128)(2,1)S(1)}, bf16[32,4096]{1,0:T(8,128)(2,1)S(1)}, u32[]{:S(2)}, u32[]{:S(2)}) collective-permute-start(bf16[32,4096]{1,0:T(8,128)(2,1)S(1)} %get-tuple-element.110), channel_id=1, source_target_pairs={{0,16},{16,0},{8,24},{24,8},{1,17},{17,1},{9,25},{25,9},{2,18},{18... | collective-permute-start | bytes 786440 | tf_op jit(solution)/shard_map/ppermute | solution.py:20
  57.3 10.4 %collective-permute-start.20 = (bf16[32,4096]{1,0:T(8,128)(2,1)S(1)}, bf16[32,4096]{1,0:T(8,128)(2,1)S(1)}, u32[]{:S(2)}, u32[]{:S(2)}) collective-permute-start(bf16[32,4096]{1,0:T(8,128)(2,1)S(1)} %get-tuple-element.112), channel_id=1, source_target_pairs={{0,8},{8,0},{16,24},{24,16},{1,9},{9,1},{17,25},{25,17},{2,10},{10... | collective-permute-start | bytes 786440 | tf_op jit(solution)/shard_map/ppermute | solution.py:20
  67.8 9.3 %collective-permute-start.23 = (bf16[32,4096]{1,0:T(8,128)(2,1)S(1)}, bf16[32,4096]{1,0:T(8,128)(2,1)S(1)}, u32[]{:S(2)}, u32[]{:S(2)}) collective-permute-start(bf16[32,4096]{1,0:T(8,128)(2,1)S(1)} %get-tuple-element.132), channel_id=1, source_target_pairs={{0,16},{16,0},{8,24},{24,8},{1,17},{17,1},{9,25},{25,9},{2,18},{18... | collective-permute-start | bytes 786440 | tf_op jit(solution)/shard_map/ppermute | solution.py:20
  68.9 19.2 %collective-permute-start.21 = (bf16[64,4096]{1,0:T(8,128)(2,1)S(1)}, bf16[64,4096]{1,0:T(8,128)(2,1)S(1)}, u32[]{:S(2)}, u32[]{:S(2)}) collective-permute-start(bf16[64,4096]{1,0:T(8,128)(2,1)S(1)} %get-tuple-element.128), channel_id=1, source_target_pairs={{0,16},{16,0},{8,24},{24,8},{1,17},{17,1},{9,25},{25,9},{2,18},{18... | collective-permute-start | bytes 1572872 | tf_op jit(solution)/shard_map/ppermute | solution.py:20
  69.9 18.3 %collective-permute-start.22 = (bf16[64,4096]{1,0:T(8,128)(2,1)S(1)}, bf16[64,4096]{1,0:T(8,128)(2,1)S(1)}, u32[]{:S(2)}, u32[]{:S(2)}) collective-permute-start(bf16[64,4096]{1,0:T(8,128)(2,1)S(1)} %get-tuple-element.130), channel_id=1, source_target_pairs={{0,8},{8,0},{16,24},{24,16},{1,9},{9,1},{17,25},{25,17},{2,10},{10... | collective-permute-start | bytes 1572872 | tf_op jit(solution)/shard_map/ppermute | solution.py:20
  70.4 16.5 %collective-permute-start.25 = (bf16[32,4096]{1,0:T(8,128)(2,1)S(1)}, bf16[32,4096]{1,0:T(8,128)(2,1)S(1)}, u32[]{:S(2)}, u32[]{:S(2)}) collective-permute-start(bf16[32,4096]{1,0:T(8,128)(2,1)S(1)} %get-tuple-element.134), channel_id=1, source_target_pairs={{0,8},{8,0},{16,24},{24,16},{1,9},{9,1},{17,25},{25,17},{2,10},{10... | collective-permute-start | bytes 786440 | tf_op jit(solution)/shard_map/ppermute | solution.py:20
  77.2 11.1 %collective-permute-start.24 = (bf16[16,4096]{1,0:T(8,128)(2,1)S(1)}, bf16[16,4096]{1,0:T(8,128)(2,1)S(1)}, u32[]{:S(2)}, u32[]{:S(2)}) collective-permute-start(bf16[16,4096]{1,0:T(8,128)(2,1)S(1)} %split.49), channel_id=1, source_target_pairs={{0,8},{8,0},{16,24},{24,16},{1,9},{9,1},{17,25},{25,17},{2,10},{10... | collective-permute-start | bytes 393224 | tf_op jit(solution)/shard_map/ppermute | solution.py:20
  87.0 6.0 %collective-permute-start.26 = (bf16[16,4096]{1,0:T(8,128)(2,1)S(1)}, bf16[16,4096]{1,0:T(8,128)(2,1)S(1)}, u32[]{:S(2)}, u32[]{:S(2)}) collective-permute-start(bf16[16,4096]{1,0:T(8,128)(2,1)S(1)} %split.51), channel_id=1, source_target_pairs={{0,16},{16,0},{8,24},{24,8},{1,17},{17,1},{9,25},{25,9},{2,18},{18... | collective-permute-start | bytes 393224 | tf_op jit(solution)/shard_map/ppermute | solution.py:20
  93.1 7.8 %collective-permute-start.31 = (bf16[32,4096]{1,0:T(8,128)(2,1)S(1)}, bf16[32,4096]{1,0:T(8,128)(2,1)S(1)}, u32[]{:S(2)}, u32[]{:S(2)}) collective-permute-start(bf16[32,4096]{1,0:T(8,128)(2,1)S(1)} %split.45), channel_id=1, source_target_pairs={{0,8},{8,0},{16,24},{24,16},{1,9},{9,1},{17,25},{25,17},{2,10},{10... | collective-permute-start | bytes 786440 | tf_op jit(solution)/shard_map/ppermute | solution.py:20
  94.1 8.3 %collective-permute-start.29 = (bf16[32,4096]{1,0:T(8,128)(2,1)S(1)}, bf16[32,4096]{1,0:T(8,128)(2,1)S(1)}, u32[]{:S(2)}, u32[]{:S(2)}) collective-permute-start(bf16[32,4096]{1,0:T(8,128)(2,1)S(1)} %pad_maximum_fusion.6), channel_id=1, source_target_pairs={{0,2},{1,3},{2,0},{3,1},{4,6},{5,7},{6,4},{7,5},{8,10},{9,11},{10,... | collective-permute-start | bytes 786440 | tf_op jit(solution)/shard_map/ppermute | solution.py:246
  94.3 8.2 %collective-permute-start.28 = (bf16[32,4096]{1,0:T(8,128)(2,1)S(1)}, bf16[32,4096]{1,0:T(8,128)(2,1)S(1)}, u32[]{:S(2)}, u32[]{:S(2)}) collective-permute-start(bf16[32,4096]{1,0:T(8,128)(2,1)S(1)} %split.43), channel_id=1, source_target_pairs={{0,16},{16,0},{8,24},{24,8},{1,17},{17,1},{9,25},{25,9},{2,18},{18... | collective-permute-start | bytes 786440 | tf_op jit(solution)/shard_map/ppermute | solution.py:20
  101.0 9.4 %collective-permute-start.32 = (bf16[32,4096]{1,0:T(8,128)(2,1)S(1)}, bf16[32,4096]{1,0:T(8,128)(2,1)S(1)}, u32[]{:S(2)}, u32[]{:S(2)}) collective-permute-start(bf16[32,4096]{1,0:T(8,128)(2,1)S(1)} %add_convert_fusion.2), channel_id=1, source_target_pairs={{0,2},{1,3},{2,0},{3,1},{4,6},{5,7},{6,4},{7,5},{8,10},{9,11},{10,... | collective-permute-start | bytes 786440 | tf_op jit(solution)/shard_map/ppermute | solution.py:246
  102.5 10.2 %collective-permute-start.30 = (bf16[32,4096]{1,0:T(8,128)(2,1)S(1)}, bf16[32,4096]{1,0:T(8,128)(2,1)S(1)}, u32[]{:S(2)}, u32[]{:S(2)}) collective-permute-start(bf16[32,4096]{1,0:T(8,128)(2,1)S(1)} %add_convert_fusion.3), channel_id=1, source_target_pairs={{0,4},{1,5},{2,6},{3,7},{4,0},{5,1},{6,2},{7,3},{8,12},{9,13},{10,... | collective-permute-start | bytes 786440 | tf_op jit(solution)/shard_map/ppermute | solution.py:246
  (6 other events, 55.8 us)

commit v18 on v17

--- a/solution.py
+++ b/solution.py
@@ -366,12 +366,13 @@
     outs[final] = layer(final)
     outs[final], sums = together((outs[final], sums))
     for number in range(final, 0, -1):
-        for turn in range(turns - 1 - int(number < final), -1, -1):
+        first = turns - 1 if number == final else turns - 2
+        for turn in range(first, -1, -1):
             sum_turn(number, turn)
-            if turn == 0 and number > 1:
+            if turn == first and number > 1:
                 sum_turn(number - 1, turns - 1)
+                sums = together(sums)
         if number > 1:
-            sums, outs = together((sums, outs))
             leave(number)
     leave(1)
     for turn in range(turns - 2, -1, -1):

time: 114 us -> 115 us (level)
    ppermute x8, waiting for transfers between devices: 7.8 us -> 15.4 us  [across_chips(): lax.ppermute(block, 'expert', [(low, low ^ 2 * far) for low in range(coun...]
    ppermute x26, waiting for transfers between devices: 46.6 us -> 39.9 us  [from_partner(): return lax.ppermute(block, axis, route)]
  transfers between devices with their start and end apart: 34 -> 34, of which waited for: 15 -> 18; matrix products, arithmetic and copies ran while one was open for 1% -> 1% of each run, Pallas kernels for 16% -> 16%
where the time goes in v18:
time: 115 us
  waiting for transfers between devices  55.3 us (48%)
  starting transfers between devices  36.7 us (32%)
  Pallas kernels  18.3 us (16%)
  other arithmetic  2.54 us (2%)
  local copies, waits for them, and re-layouts  1.46 us (1%)
    ppermute x26, waiting for transfers between devices, from_partner(): return lax.ppermute(block, axis, route)  39.9 us
    ppermute x26, starting transfers between devices, from_partner(): return lax.ppermute(block, axis, route)  26 us
    ppermute x8, waiting for transfers between devices, across_chips(): lax.ppermute(block, 'expert', [(low, low ^ 2 * far) for low in range(coun...  15.4 us
    pallas_call x3, Pallas kernels, expert_layer(): pl.pallas_call(functools.partial(expert_kernel, count, experts), in_specs...  11.9 us
    ppermute x8, starting transfers between devices, across_chips(): lax.ppermute(block, 'expert', [(low, low ^ 2 * far) for low in range(coun...  10.7 us
    pallas_call x2, Pallas kernels, dequantize_call(): pl.pallas_call(kernel, in_specs=[pl.BlockSpec(memory_space=pltpu.SMEM)] *...  6.46 us
  transfers between devices with their start and end apart: 34, of which 18 were waited for; matrix products, arithmetic and copies ran while one was open for 1% of the time, Pallas kernels for 16%

profile of v18, /device:TPU:0, one launch (start us, length us, event | category | flops | bytes accessed | tf_op | source)
XLA Modules:
  0.0 114.6 jit_solution(2051451684624312975)
XLA Ops:
  2.0 2.9 %collective-permute-start = (bf16[16,4224]{1,0:T(8,128)(2,1)S(1)}, bf16[16,4224]{1,0:T(8,128)(2,1)S(1)}, u32[]{:S(2)}, u32[]{:S(2)}) collective-permute-start(bf16[16,4224]{1,0:T(8,128)(2,1)S(1)} %concatenate.38), channel_id=1, source_target_pairs={{0,8},{8,0},{16,24},{24,16},{1,9},{9,1},{17,25},{25,17},{2,10},{10... | collective-permute-start | bytes 405512 | tf_op jit(solution)/shard_map/ppermute | solution.py:20
  5.0 1.6 %collective-permute-start.2 = (bf16[16,4224]{1,0:T(8,128)(2,1)S(1)}, bf16[16,4224]{1,0:T(8,128)(2,1)S(1)}, u32[]{:S(2)}, u32[]{:S(2)}) collective-permute-start(bf16[16,4224]{1,0:T(8,128)(2,1)S(1)} %concatenate.38), channel_id=1, source_target_pairs={{0,2},{1,3},{2,0},{3,1},{4,6},{5,7},{6,4},{7,5},{8,10},{9,11},{10,... | collective-permute-start | bytes 405512 | tf_op jit(solution)/shard_map/ppermute | solution.py:246
  6.6 2.6 %collective-permute-start.3 = (bf16[16,4224]{1,0:T(8,128)(2,1)S(1)}, bf16[16,4224]{1,0:T(8,128)(2,1)S(1)}, u32[]{:S(2)}, u32[]{:S(2)}) collective-permute-start(bf16[16,4224]{1,0:T(8,128)(2,1)S(1)} %concatenate.38), channel_id=1, source_target_pairs={{0,4},{1,5},{2,6},{3,7},{4,0},{5,1},{6,2},{7,3},{8,12},{9,13},{10,... | collective-permute-start | bytes 405512 | tf_op jit(solution)/shard_map/ppermute | solution.py:246
  9.1 1.5 %collective-permute-start.1 = (bf16[16,4224]{1,0:T(8,128)(2,1)S(1)}, bf16[16,4224]{1,0:T(8,128)(2,1)S(1)}, u32[]{:S(2)}, u32[]{:S(2)}) collective-permute-start(bf16[16,4224]{1,0:T(8,128)(2,1)S(1)} %concatenate.39), channel_id=1, source_target_pairs={{0,16},{16,0},{8,24},{24,8},{1,17},{17,1},{9,25},{25,9},{2,18},{18... | collective-permute-start | bytes 405512 | tf_op jit(solution)/shard_map/ppermute | solution.py:20
  10.7 3.7 %dequantize_in.1.refs_4_ = bf16[4096,768]{1,0:T(8,128)(2,1)S(1)} custom-call(f32[3,32]{1,0:T(4,128)S(1)} %get-tuple-element.156.gate_scales, f32[3,32]{1,0:T(4,128)S(1)} %get-tuple-element.155.up_scales, bf16[4096,384]{1,0:T(8,128)(2,1)} %bitcast.17, bf16[4096,384]{1,0:T(8,128)(2,1)} %bitcast.18), custom_call_target="tpu_custom_call" | custom-call | flops 3145728 | bytes 12582912 | tf_op jit(solution)/shard_map/dequantize_in/pallas_call | solution.py:155
  15.2 1.5 %collective-permute-start.4 = (bf16[32,4224]{1,0:T(8,128)(2,1)S(1)}, bf16[32,4224]{1,0:T(8,128)(2,1)S(1)}, u32[]{:S(2)}, u32[]{:S(2)}) collective-permute-start(bf16[32,4224]{1,0:T(8,128)(2,1)S(1)} %pad_maximum_fusion.2.refs_0_), channel_id=1, source_target_pairs={{0,16},{16,0},{8,24},{24,8},{1,17},{17,1},{9,25},{25,9},{2,18},{18... | collective-permute-start | bytes 811016 | tf_op jit(solution)/shard_map/ppermute | solution.py:20
  17.6 2.7 %collective-permute-start.7 = (bf16[16,4224]{1,0:T(8,128)(2,1)S(1)}, bf16[16,4224]{1,0:T(8,128)(2,1)S(1)}, u32[]{:S(2)}, u32[]{:S(2)}) collective-permute-start(bf16[16,4224]{1,0:T(8,128)(2,1)S(1)} %concatenate.39), channel_id=1, source_target_pairs={{0,4},{1,5},{2,6},{3,7},{4,0},{5,1},{6,2},{7,3},{8,12},{9,13},{10,... | collective-permute-start | bytes 405512 | tf_op jit(solution)/shard_map/ppermute | solution.py:246
  20.3 2.8 %dequantize_down.1.refs_6_ = bf16[384,4096]{1,0:T(8,128)(2,1)S(1)} custom-call(f32[3,32]{1,0:T(4,128)S(1)} %bitcast.15, bf16[384,4096]{1,0:T(8,128)(2,1)} %bitcast.16), custom_call_target="tpu_custom_call" | custom-call | flops 1572864 | bytes 6291456 | tf_op jit(solution)/shard_map/dequantize_down/pallas_call | solution.py:155
  23.0 2.3 %collective-permute-done.6 = bf16[16,4224]{1,0:T(8,128)(2,1)S(1)} collective-permute-done((bf16[16,4224]{1,0:T(8,128)(2,1)S(1)}, bf16[16,4224]{1,0:T(8,128)(2,1)S(1)}, u32[]{:S(2)}, u32[]{:S(2)}) %collective-permute-start.6) | collective-permute-done | bytes 135200 | tf_op jit(solution)/shard_map/ppermute | solution.py:246
  25.3 1.3 %collective-permute-done.7 = bf16[16,4224]{1,0:T(8,128)(2,1)S(1)} collective-permute-done((bf16[16,4224]{1,0:T(8,128)(2,1)S(1)}, bf16[16,4224]{1,0:T(8,128)(2,1)S(1)}, u32[]{:S(2)}, u32[]{:S(2)}) %collective-permute-start.7) | collective-permute-done | bytes 135200 | tf_op jit(solution)/shard_map/ppermute | solution.py:246
  26.7 1.6 %collective-permute-start.8 = (bf16[32,4224]{1,0:T(8,128)(2,1)S(1)}, bf16[32,4224]{1,0:T(8,128)(2,1)S(1)}, u32[]{:S(2)}, u32[]{:S(2)}) collective-permute-start(bf16[32,4224]{1,0:T(8,128)(2,1)S(1)} %constant_dynamic-update-slice_fusion), channel_id=1, source_target_pairs={{0,8},{8,0},{16,24},{24,16},{1,9},{9,1},{17,25},{25,17},{2,10},{10... | collective-permute-start | bytes 811016 | tf_op jit(solution)/shard_map/ppermute | solution.py:20
  29.2 6.5 %collective-permute-done.8 = bf16[32,4224]{1,0:T(8,128)(2,1)S(1)} collective-permute-done((bf16[32,4224]{1,0:T(8,128)(2,1)S(1)}, bf16[32,4224]{1,0:T(8,128)(2,1)S(1)}, u32[]{:S(2)}, u32[]{:S(2)}) %collective-permute-start.8) | collective-permute-done | bytes 270368 | tf_op jit(solution)/shard_map/ppermute | solution.py:20
  35.7 1.3 %collective-permute-done.9 = bf16[32,4224]{1,0:T(8,128)(2,1)S(1)} collective-permute-done((bf16[32,4224]{1,0:T(8,128)(2,1)S(1)}, bf16[32,4224]{1,0:T(8,128)(2,1)S(1)}, u32[]{:S(2)}, u32[]{:S(2)}) %collective-permute-start.9) | collective-permute-done | bytes 270368 | tf_op jit(solution)/shard_map/ppermute | solution.py:20
  37.2 1.5 %collective-permute-start.13 = (bf16[64,4224]{1,0:T(8,128)(2,1)S(1)}, bf16[64,4224]{1,0:T(8,128)(2,1)S(1)}, u32[]{:S(2)}, u32[]{:S(2)}) collective-permute-start(bf16[64,4224]{1,0:T(8,128)(2,1)S(1)} %pad_maximum_fusion.refs_0_), channel_id=1, source_target_pairs={{0,16},{16,0},{8,24},{24,8},{1,17},{17,1},{9,25},{25,9},{2,18},{18... | collective-permute-start | bytes 1622024 | tf_op jit(solution)/shard_map/ppermute | solution.py:20
  39.2 1.6 %collective-permute-start.15 = (bf16[16,4224]{1,0:T(8,128)(2,1)S(1)}, bf16[16,4224]{1,0:T(8,128)(2,1)S(1)}, u32[]{:S(2)}, u32[]{:S(2)}) collective-permute-start(bf16[16,4224]{1,0:T(8,128)(2,1)S(1)} %get-tuple-element.146), channel_id=1, source_target_pairs={{0,8},{8,0},{16,24},{24,16},{1,9},{9,1},{17,25},{25,17},{2,10},{10... | collective-permute-start | bytes 405512 | tf_op jit(solution)/shard_map/ppermute | solution.py:20
  41.3 3.1 %expert_layer.3 = (bf16[32,4096]{1,0:T(8,128)(2,1)S(1)}, bf16[32,4096]{1,0:T(8,128)(2,1)S(1)}, bf16[32,4096]{1,0:T(8,128)(2,1)S(1)}, bf16[32,4096]{1,0:T(8,128)(2,1)S(1)}) custom-call(s32[1]{0:T(128)} %bitcast.own_expert, bf16[32,4224]{1,0:T(8,128)(2,1)S(1)} %pad_maximum_fusion.2.refs_0_, bf16[32,4224]{1,0:T(8,128)(2,1)S(1)} %collective-permute-done.4.refs_1_, ...), custom_call_target="tpu_custom_call" | custom-call | flops 2415919104 | bytes 20971520 | tf_op jit(solution)/shard_map/expert_layer/pallas_call | solution.py:225
  44.4 10.2 %collective-permute-done.15 = bf16[16,4224]{1,0:T(8,128)(2,1)S(1)} collective-permute-done((bf16[16,4224]{1,0:T(8,128)(2,1)S(1)}, bf16[16,4224]{1,0:T(8,128)(2,1)S(1)}, u32[]{:S(2)}, u32[]{:S(2)}) %collective-permute-start.15) | collective-permute-done | bytes 135200 | tf_op jit(solution)/shard_map/ppermute | solution.py:20
  56.0 1.3 %collective-permute-start.19 = (bf16[32,4096]{1,0:T(8,128)(2,1)S(1)}, bf16[32,4096]{1,0:T(8,128)(2,1)S(1)}, u32[]{:S(2)}, u32[]{:S(2)}) collective-permute-start(bf16[32,4096]{1,0:T(8,128)(2,1)S(1)} %get-tuple-element.110), channel_id=1, source_target_pairs={{0,16},{16,0},{8,24},{24,8},{1,17},{17,1},{9,25},{25,9},{2,18},{18... | collective-permute-start | bytes 786440 | tf_op jit(solution)/shard_map/ppermute | solution.py:20
  57.3 1.5 %collective-permute-start.20 = (bf16[32,4096]{1,0:T(8,128)(2,1)S(1)}, bf16[32,4096]{1,0:T(8,128)(2,1)S(1)}, u32[]{:S(2)}, u32[]{:S(2)}) collective-permute-start(bf16[32,4096]{1,0:T(8,128)(2,1)S(1)} %get-tuple-element.112), channel_id=1, source_target_pairs={{0,8},{8,0},{16,24},{24,16},{1,9},{9,1},{17,25},{25,17},{2,10},{10... | collective-permute-start | bytes 786440 | tf_op jit(solution)/shard_map/ppermute | solution.py:20
  58.8 5.7 %expert_layer.4 = (bf16[64,4096]{1,0:T(8,128)(2,1)S(1)}, bf16[64,4096]{1,0:T(8,128)(2,1)S(1)}, bf16[64,4096]{1,0:T(8,128)(2,1)S(1)}, bf16[64,4096]{1,0:T(8,128)(2,1)S(1)}) custom-call(s32[1]{0:T(128)} %bitcast.own_expert, bf16[64,4224]{1,0:T(8,128)(2,1)S(1)} %pad_maximum_fusion.refs_0_, bf16[64,4224]{1,0:T(8,128)(2,1)S(1)} %collective-permute-done.13.refs_1_, ...), custom_call_target="tpu_custom_call" | custom-call | flops 4831838208 | bytes 23068672 | tf_op jit(solution)/shard_map/expert_layer/pallas_call | solution.py:225
  66.1 3.1 %expert_layer.5 = (bf16[32,4096]{1,0:T(8,128)(2,1)S(1)}, bf16[32,4096]{1,0:T(8,128)(2,1)S(1)}, bf16[32,4096]{1,0:T(8,128)(2,1)S(1)}, bf16[32,4096]{1,0:T(8,128)(2,1)S(1)}) custom-call(s32[1]{0:T(128)} %bitcast.own_expert, bf16[32,4224]{1,0:T(8,128)(2,1)S(1)} %pad_maximum_fusion.4.refs_0_, bf16[32,4224]{1,0:T(8,128)(2,1)S(1)} %collective-permute-done.16.refs_1_, ...), custom_call_target="tpu_custom_call" | custom-call | flops 2415919104 | bytes 20971520 | tf_op jit(solution)/shard_map/expert_layer/pallas_call | solution.py:225
  70.0 1.1 collective-permute-start.23
  72.0 8.3 %collective-permute-done.21 = bf16[64,4096]{1,0:T(8,128)(2,1)S(1)} collective-permute-done((bf16[64,4096]{1,0:T(8,128)(2,1)S(1)}, bf16[64,4096]{1,0:T(8,128)(2,1)S(1)}, u32[]{:S(2)}, u32[]{:S(2)}) %collective-permute-start.21) | collective-permute-done | bytes 524320 | tf_op jit(solution)/shard_map/ppermute | solution.py:20
  81.3 2.1 %collective-permute-done.23 = bf16[32,4096]{1,0:T(8,128)(2,1)S(1)} collective-permute-done((bf16[32,4096]{1,0:T(8,128)(2,1)S(1)}, bf16[32,4096]{1,0:T(8,128)(2,1)S(1)}, u32[]{:S(2)}, u32[]{:S(2)}) %collective-permute-start.23) | collective-permute-done | bytes 262176 | tf_op jit(solution)/shard_map/ppermute | solution.py:20
  84.2 1.1 collective-permute-start.28
  86.0 1.6 %collective-permute-start.27 = (bf16[16,4096]{1,0:T(8,128)(2,1)S(1)}, bf16[16,4096]{1,0:T(8,128)(2,1)S(1)}, u32[]{:S(2)}, u32[]{:S(2)}) collective-permute-start(bf16[16,4096]{1,0:T(8,128)(2,1)S(1)} %split.41), channel_id=1, source_target_pairs={{0,8},{8,0},{16,24},{24,16},{1,9},{9,1},{17,25},{25,17},{2,10},{10... | collective-permute-start | bytes 393224 | tf_op jit(solution)/shard_map/ppermute | solution.py:20
  88.6 2.1 %collective-permute-done.28 = bf16[16,4096]{1,0:T(8,128)(2,1)S(1)} collective-permute-done((bf16[16,4096]{1,0:T(8,128)(2,1)S(1)}, bf16[16,4096]{1,0:T(8,128)(2,1)S(1)}, u32[]{:S(2)}, u32[]{:S(2)}) %collective-permute-start.28) | collective-permute-done | bytes 131104 | tf_op jit(solution)/shard_map/ppermute | solution.py:20
  90.7 3.0 %collective-permute-done.27 = bf16[16,4096]{1,0:T(8,128)(2,1)S(1)} collective-permute-done((bf16[16,4096]{1,0:T(8,128)(2,1)S(1)}, bf16[16,4096]{1,0:T(8,128)(2,1)S(1)}, u32[]{:S(2)}, u32[]{:S(2)}) %collective-permute-start.27) | collective-permute-done | bytes 131104 | tf_op jit(solution)/shard_map/ppermute | solution.py:20
  94.3 1.8 %collective-permute-start.32 = (bf16[32,4096]{1,0:T(8,128)(2,1)S(1)}, bf16[32,4096]{1,0:T(8,128)(2,1)S(1)}, u32[]{:S(2)}, u32[]{:S(2)}) collective-permute-start(bf16[32,4096]{1,0:T(8,128)(2,1)S(1)} %add_convert_fusion.2), channel_id=1, source_target_pairs={{0,2},{1,3},{2,0},{3,1},{4,6},{5,7},{6,4},{7,5},{8,10},{9,11},{10,... | collective-permute-start | bytes 786440 | tf_op jit(solution)/shard_map/ppermute | solution.py:246
  96.0 8.0 %collective-permute-done.29 = bf16[32,4096]{1,0:T(8,128)(2,1)S(1)} collective-permute-done((bf16[32,4096]{1,0:T(8,128)(2,1)S(1)}, bf16[32,4096]{1,0:T(8,128)(2,1)S(1)}, u32[]{:S(2)}, u32[]{:S(2)}) %collective-permute-start.29) | collective-permute-done | bytes 262176 | tf_op jit(solution)/shard_map/ppermute | solution.py:246
  106.3 3.8 %collective-permute-done.25 = bf16[16,4096]{1,0:T(8,128)(2,1)S(1)} collective-permute-done((bf16[16,4096]{1,0:T(8,128)(2,1)S(1)}, bf16[16,4096]{1,0:T(8,128)(2,1)S(1)}, u32[]{:S(2)}, u32[]{:S(2)}) %collective-permute-start.25) | collective-permute-done | bytes 131104 | tf_op jit(solution)/shard_map/ppermute | solution.py:20
  110.8 2.9 %collective-permute-done.30 = bf16[32,4096]{1,0:T(8,128)(2,1)S(1)} collective-permute-done((bf16[32,4096]{1,0:T(8,128)(2,1)S(1)}, bf16[32,4096]{1,0:T(8,128)(2,1)S(1)}, u32[]{:S(2)}, u32[]{:S(2)}) %collective-permute-start.30) | collective-permute-done | bytes 262176 | tf_op jit(solution)/shard_map/ppermute | solution.py:246
  (89 shorter events, 18.4 us)
Async XLA Ops:
  2.0 12.4 %collective-permute-start = (bf16[16,4224]{1,0:T(8,128)(2,1)S(1)}, bf16[16,4224]{1,0:T(8,128)(2,1)S(1)}, u32[]{:S(2)}, u32[]{:S(2)}) collective-permute-start(bf16[16,4224]{1,0:T(8,128)(2,1)S(1)} %concatenate.38), channel_id=1, source_target_pairs={{0,8},{8,0},{16,24},{24,16},{1,9},{9,1},{17,25},{25,17},{2,10},{10... | collective-permute-start | bytes 405512 | tf_op jit(solution)/shard_map/ppermute | solution.py:20
  5.0 9.5 %collective-permute-start.2 = (bf16[16,4224]{1,0:T(8,128)(2,1)S(1)}, bf16[16,4224]{1,0:T(8,128)(2,1)S(1)}, u32[]{:S(2)}, u32[]{:S(2)}) collective-permute-start(bf16[16,4224]{1,0:T(8,128)(2,1)S(1)} %concatenate.38), channel_id=1, source_target_pairs={{0,2},{1,3},{2,0},{3,1},{4,6},{5,7},{6,4},{7,5},{8,10},{9,11},{10,... | collective-permute-start | bytes 405512 | tf_op jit(solution)/shard_map/ppermute | solution.py:246
  6.6 8.6 %collective-permute-start.3 = (bf16[16,4224]{1,0:T(8,128)(2,1)S(1)}, bf16[16,4224]{1,0:T(8,128)(2,1)S(1)}, u32[]{:S(2)}, u32[]{:S(2)}) collective-permute-start(bf16[16,4224]{1,0:T(8,128)(2,1)S(1)} %concatenate.38), channel_id=1, source_target_pairs={{0,4},{1,5},{2,6},{3,7},{4,0},{5,1},{6,2},{7,3},{8,12},{9,13},{10,... | collective-permute-start | bytes 405512 | tf_op jit(solution)/shard_map/ppermute | solution.py:246
  9.1 5.3 %collective-permute-start.1 = (bf16[16,4224]{1,0:T(8,128)(2,1)S(1)}, bf16[16,4224]{1,0:T(8,128)(2,1)S(1)}, u32[]{:S(2)}, u32[]{:S(2)}) collective-permute-start(bf16[16,4224]{1,0:T(8,128)(2,1)S(1)} %concatenate.39), channel_id=1, source_target_pairs={{0,16},{16,0},{8,24},{24,8},{1,17},{17,1},{9,25},{25,9},{2,18},{18... | collective-permute-start | bytes 405512 | tf_op jit(solution)/shard_map/ppermute | solution.py:20
  15.2 22.0 %collective-permute-start.11 = (bf16[4096,768]{1,0:T(8,128)(2,1)S(1)}, bf16[4096,768]{1,0:T(8,128)(2,1)S(1)}, u32[]{:S(2)}, u32[]{:S(2)}) collective-permute-start(bf16[4096,768]{1,0:T(8,128)(2,1)S(1)} %dequantize_in.1.refs_4_), channel_id=1, source_target_pairs={{0,1},{1,0},{2,3},{3,2},{4,5},{5,4},{6,7},{7,6},{8,9},{9,8},{10,11... | collective-permute-start | bytes 18874376 | tf_op jit(solution)/shard_map/ppermute | solution.py:20
  15.2 11.5 %collective-permute-start.4 = (bf16[32,4224]{1,0:T(8,128)(2,1)S(1)}, bf16[32,4224]{1,0:T(8,128)(2,1)S(1)}, u32[]{:S(2)}, u32[]{:S(2)}) collective-permute-start(bf16[32,4224]{1,0:T(8,128)(2,1)S(1)} %pad_maximum_fusion.2.refs_0_), channel_id=1, source_target_pairs={{0,16},{16,0},{8,24},{24,8},{1,17},{17,1},{9,25},{25,9},{2,18},{18... | collective-permute-start | bytes 811016 | tf_op jit(solution)/shard_map/ppermute | solution.py:20
  16.7 9.9 %collective-permute-start.5 = (bf16[32,4224]{1,0:T(8,128)(2,1)S(1)}, bf16[32,4224]{1,0:T(8,128)(2,1)S(1)}, u32[]{:S(2)}, u32[]{:S(2)}) collective-permute-start(bf16[32,4224]{1,0:T(8,128)(2,1)S(1)} %pad_maximum_fusion.3.refs_2_), channel_id=1, source_target_pairs={{0,8},{8,0},{16,24},{24,16},{1,9},{9,1},{17,25},{25,17},{2,10},{10... | collective-permute-start | bytes 811016 | tf_op jit(solution)/shard_map/ppermute | solution.py:20
  17.2 8.1 %collective-permute-start.6 = (bf16[16,4224]{1,0:T(8,128)(2,1)S(1)}, bf16[16,4224]{1,0:T(8,128)(2,1)S(1)}, u32[]{:S(2)}, u32[]{:S(2)}) collective-permute-start(bf16[16,4224]{1,0:T(8,128)(2,1)S(1)} %concatenate.39), channel_id=1, source_target_pairs={{0,2},{1,3},{2,0},{3,1},{4,6},{5,7},{6,4},{7,5},{8,10},{9,11},{10,... | collective-permute-start | bytes 405512 | tf_op jit(solution)/shard_map/ppermute | solution.py:246
  17.6 9.0 %collective-permute-start.7 = (bf16[16,4224]{1,0:T(8,128)(2,1)S(1)}, bf16[16,4224]{1,0:T(8,128)(2,1)S(1)}, u32[]{:S(2)}, u32[]{:S(2)}) collective-permute-start(bf16[16,4224]{1,0:T(8,128)(2,1)S(1)} %concatenate.39), channel_id=1, source_target_pairs={{0,4},{1,5},{2,6},{3,7},{4,0},{5,1},{6,2},{7,3},{8,12},{9,13},{10,... | collective-permute-start | bytes 405512 | tf_op jit(solution)/shard_map/ppermute | solution.py:246
  26.6 10.5 %collective-permute-start.12 = (bf16[384,4096]{1,0:T(8,128)(2,1)S(1)}, bf16[384,4096]{1,0:T(8,128)(2,1)S(1)}, u32[]{:S(2)}, u32[]{:S(2)}) collective-permute-start(bf16[384,4096]{1,0:T(8,128)(2,1)S(1)} %dequantize_down.1.refs_6_), channel_id=1, source_target_pairs={{0,1},{1,0},{2,3},{3,2},{4,5},{5,4},{6,7},{7,6},{8,9},{9,8},{10,11... | collective-permute-start | bytes 9437192 | tf_op jit(solution)/shard_map/ppermute | solution.py:20
  26.7 8.9 %collective-permute-start.8 = (bf16[32,4224]{1,0:T(8,128)(2,1)S(1)}, bf16[32,4224]{1,0:T(8,128)(2,1)S(1)}, u32[]{:S(2)}, u32[]{:S(2)}) collective-permute-start(bf16[32,4224]{1,0:T(8,128)(2,1)S(1)} %constant_dynamic-update-slice_fusion), channel_id=1, source_target_pairs={{0,8},{8,0},{16,24},{24,16},{1,9},{9,1},{17,25},{25,17},{2,10},{10... | collective-permute-start | bytes 811016 | tf_op jit(solution)/shard_map/ppermute | solution.py:20
  28.3 8.7 %collective-permute-start.9 = (bf16[32,4224]{1,0:T(8,128)(2,1)S(1)}, bf16[32,4224]{1,0:T(8,128)(2,1)S(1)}, u32[]{:S(2)}, u32[]{:S(2)}) collective-permute-start(bf16[32,4224]{1,0:T(8,128)(2,1)S(1)} %constant_dynamic-update-slice_fusion.2), channel_id=1, source_target_pairs={{0,16},{16,0},{8,24},{24,8},{1,17},{17,1},{9,25},{25,9},{2,18},{18... | collective-permute-start | bytes 811016 | tf_op jit(solution)/shard_map/ppermute | solution.py:20
  28.8 8.3 %collective-permute-start.10 = (bf16[32,4224]{1,0:T(8,128)(2,1)S(1)}, bf16[32,4224]{1,0:T(8,128)(2,1)S(1)}, u32[]{:S(2)}, u32[]{:S(2)}) collective-permute-start(bf16[32,4224]{1,0:T(8,128)(2,1)S(1)} %constant_dynamic-update-slice_fusion.2), channel_id=1, source_target_pairs={{0,2},{1,3},{2,0},{3,1},{4,6},{5,7},{6,4},{7,5},{8,10},{9,11},{10,... | collective-permute-start | bytes 811016 | tf_op jit(solution)/shard_map/ppermute | solution.py:246
  37.2 18.9 %collective-permute-start.13 = (bf16[64,4224]{1,0:T(8,128)(2,1)S(1)}, bf16[64,4224]{1,0:T(8,128)(2,1)S(1)}, u32[]{:S(2)}, u32[]{:S(2)}) collective-permute-start(bf16[64,4224]{1,0:T(8,128)(2,1)S(1)} %pad_maximum_fusion.refs_0_), channel_id=1, source_target_pairs={{0,16},{16,0},{8,24},{24,8},{1,17},{17,1},{9,25},{25,9},{2,18},{18... | collective-permute-start | bytes 1622024 | tf_op jit(solution)/shard_map/ppermute | solution.py:20
  38.7 17.4 %collective-permute-start.14 = (bf16[64,4224]{1,0:T(8,128)(2,1)S(1)}, bf16[64,4224]{1,0:T(8,128)(2,1)S(1)}, u32[]{:S(2)}, u32[]{:S(2)}) collective-permute-start(bf16[64,4224]{1,0:T(8,128)(2,1)S(1)} %pad_maximum_fusion.1.refs_2_), channel_id=1, source_target_pairs={{0,8},{8,0},{16,24},{24,16},{1,9},{9,1},{17,25},{25,17},{2,10},{10... | collective-permute-start | bytes 1622024 | tf_op jit(solution)/shard_map/ppermute | solution.py:20
  39.2 15.3 %collective-permute-start.15 = (bf16[16,4224]{1,0:T(8,128)(2,1)S(1)}, bf16[16,4224]{1,0:T(8,128)(2,1)S(1)}, u32[]{:S(2)}, u32[]{:S(2)}) collective-permute-start(bf16[16,4224]{1,0:T(8,128)(2,1)S(1)} %get-tuple-element.146), channel_id=1, source_target_pairs={{0,8},{8,0},{16,24},{24,16},{1,9},{9,1},{17,25},{25,17},{2,10},{10... | collective-permute-start | bytes 405512 | tf_op jit(solution)/shard_map/ppermute | solution.py:20
  40.8 14.6 %collective-permute-start.17 = (bf16[16,4224]{1,0:T(8,128)(2,1)S(1)}, bf16[16,4224]{1,0:T(8,128)(2,1)S(1)}, u32[]{:S(2)}, u32[]{:S(2)}) collective-permute-start(bf16[16,4224]{1,0:T(8,128)(2,1)S(1)} %get-tuple-element.145), channel_id=1, source_target_pairs={{0,16},{16,0},{8,24},{24,8},{1,17},{17,1},{9,25},{25,9},{2,18},{18... | collective-permute-start | bytes 405512 | tf_op jit(solution)/shard_map/ppermute | solution.py:20
  54.6 9.9 %collective-permute-start.16 = (bf16[32,4224]{1,0:T(8,128)(2,1)S(1)}, bf16[32,4224]{1,0:T(8,128)(2,1)S(1)}, u32[]{:S(2)}, u32[]{:S(2)}) collective-permute-start(bf16[32,4224]{1,0:T(8,128)(2,1)S(1)} %pad_maximum_fusion.4.refs_0_), channel_id=1, source_target_pairs={{0,16},{16,0},{8,24},{24,8},{1,17},{17,1},{9,25},{25,9},{2,18},{18... | collective-permute-start | bytes 811016 | tf_op jit(solution)/shard_map/ppermute | solution.py:20
  55.4 9.1 %collective-permute-start.18 = (bf16[32,4224]{1,0:T(8,128)(2,1)S(1)}, bf16[32,4224]{1,0:T(8,128)(2,1)S(1)}, u32[]{:S(2)}, u32[]{:S(2)}) collective-permute-start(bf16[32,4224]{1,0:T(8,128)(2,1)S(1)} %pad_maximum_fusion.5.refs_2_), channel_id=1, source_target_pairs={{0,8},{8,0},{16,24},{24,16},{1,9},{9,1},{17,25},{25,17},{2,10},{10... | collective-permute-start | bytes 811016 | tf_op jit(solution)/shard_map/ppermute | solution.py:20
  56.0 13.1 %collective-permute-start.19 = (bf16[32,4096]{1,0:T(8,128)(2,1)S(1)}, bf16[32,4096]{1,0:T(8,128)(2,1)S(1)}, u32[]{:S(2)}, u32[]{:S(2)}) collective-permute-start(bf16[32,4096]{1,0:T(8,128)(2,1)S(1)} %get-tuple-element.110), channel_id=1, source_target_pairs={{0,16},{16,0},{8,24},{24,8},{1,17},{17,1},{9,25},{25,9},{2,18},{18... | collective-permute-start | bytes 786440 | tf_op jit(solution)/shard_map/ppermute | solution.py:20
  57.3 12.6 %collective-permute-start.20 = (bf16[32,4096]{1,0:T(8,128)(2,1)S(1)}, bf16[32,4096]{1,0:T(8,128)(2,1)S(1)}, u32[]{:S(2)}, u32[]{:S(2)}) collective-permute-start(bf16[32,4096]{1,0:T(8,128)(2,1)S(1)} %get-tuple-element.112), channel_id=1, source_target_pairs={{0,8},{8,0},{16,24},{24,16},{1,9},{9,1},{17,25},{25,17},{2,10},{10... | collective-permute-start | bytes 786440 | tf_op jit(solution)/shard_map/ppermute | solution.py:20
  64.5 15.7 %collective-permute-start.21 = (bf16[64,4096]{1,0:T(8,128)(2,1)S(1)}, bf16[64,4096]{1,0:T(8,128)(2,1)S(1)}, u32[]{:S(2)}, u32[]{:S(2)}) collective-permute-start(bf16[64,4096]{1,0:T(8,128)(2,1)S(1)} %get-tuple-element.128), channel_id=1, source_target_pairs={{0,16},{16,0},{8,24},{24,8},{1,17},{17,1},{9,25},{25,9},{2,18},{18... | collective-permute-start | bytes 1572872 | tf_op jit(solution)/shard_map/ppermute | solution.py:20
  65.6 15.6 %collective-permute-start.22 = (bf16[64,4096]{1,0:T(8,128)(2,1)S(1)}, bf16[64,4096]{1,0:T(8,128)(2,1)S(1)}, u32[]{:S(2)}, u32[]{:S(2)}) collective-permute-start(bf16[64,4096]{1,0:T(8,128)(2,1)S(1)} %get-tuple-element.130), channel_id=1, source_target_pairs={{0,8},{8,0},{16,24},{24,16},{1,9},{9,1},{17,25},{25,17},{2,10},{10... | collective-permute-start | bytes 1572872 | tf_op jit(solution)/shard_map/ppermute | solution.py:20
  70.0 13.4 %collective-permute-start.23 = (bf16[32,4096]{1,0:T(8,128)(2,1)S(1)}, bf16[32,4096]{1,0:T(8,128)(2,1)S(1)}, u32[]{:S(2)}, u32[]{:S(2)}) collective-permute-start(bf16[32,4096]{1,0:T(8,128)(2,1)S(1)} %get-tuple-element.132), channel_id=1, source_target_pairs={{0,16},{16,0},{8,24},{24,8},{1,17},{17,1},{9,25},{25,9},{2,18},{18... | collective-permute-start | bytes 786440 | tf_op jit(solution)/shard_map/ppermute | solution.py:20
  71.1 13.1 %collective-permute-start.24 = (bf16[32,4096]{1,0:T(8,128)(2,1)S(1)}, bf16[32,4096]{1,0:T(8,128)(2,1)S(1)}, u32[]{:S(2)}, u32[]{:S(2)}) collective-permute-start(bf16[32,4096]{1,0:T(8,128)(2,1)S(1)} %get-tuple-element.134), channel_id=1, source_target_pairs={{0,8},{8,0},{16,24},{24,16},{1,9},{9,1},{17,25},{25,17},{2,10},{10... | collective-permute-start | bytes 786440 | tf_op jit(solution)/shard_map/ppermute | solution.py:20
  84.2 6.4 %collective-permute-start.28 = (bf16[16,4096]{1,0:T(8,128)(2,1)S(1)}, bf16[16,4096]{1,0:T(8,128)(2,1)S(1)}, u32[]{:S(2)}, u32[]{:S(2)}) collective-permute-start(bf16[16,4096]{1,0:T(8,128)(2,1)S(1)} %split.43), channel_id=1, source_target_pairs={{0,16},{16,0},{8,24},{24,8},{1,17},{17,1},{9,25},{25,9},{2,18},{18... | collective-permute-start | bytes 393224 | tf_op jit(solution)/shard_map/ppermute | solution.py:20
  85.4 8.8 %collective-permute-start.31 = (bf16[32,4096]{1,0:T(8,128)(2,1)S(1)}, bf16[32,4096]{1,0:T(8,128)(2,1)S(1)}, u32[]{:S(2)}, u32[]{:S(2)}) collective-permute-start(bf16[32,4096]{1,0:T(8,128)(2,1)S(1)} %split.45), channel_id=1, source_target_pairs={{0,8},{8,0},{16,24},{24,16},{1,9},{9,1},{17,25},{25,17},{2,10},{10... | collective-permute-start | bytes 786440 | tf_op jit(solution)/shard_map/ppermute | solution.py:20
  86.0 7.7 %collective-permute-start.27 = (bf16[16,4096]{1,0:T(8,128)(2,1)S(1)}, bf16[16,4096]{1,0:T(8,128)(2,1)S(1)}, u32[]{:S(2)}, u32[]{:S(2)}) collective-permute-start(bf16[16,4096]{1,0:T(8,128)(2,1)S(1)} %split.41), channel_id=1, source_target_pairs={{0,8},{8,0},{16,24},{24,16},{1,9},{9,1},{17,25},{25,17},{2,10},{10... | collective-permute-start | bytes 393224 | tf_op jit(solution)/shard_map/ppermute | solution.py:20
  87.6 8.4 %collective-permute-start.26 = (bf16[32,4096]{1,0:T(8,128)(2,1)S(1)}, bf16[32,4096]{1,0:T(8,128)(2,1)S(1)}, u32[]{:S(2)}, u32[]{:S(2)}) collective-permute-start(bf16[32,4096]{1,0:T(8,128)(2,1)S(1)} %split.39), channel_id=1, source_target_pairs={{0,16},{16,0},{8,24},{24,8},{1,17},{17,1},{9,25},{25,9},{2,18},{18... | collective-permute-start | bytes 786440 | tf_op jit(solution)/shard_map/ppermute | solution.py:20
  93.8 10.2 %collective-permute-start.29 = (bf16[32,4096]{1,0:T(8,128)(2,1)S(1)}, bf16[32,4096]{1,0:T(8,128)(2,1)S(1)}, u32[]{:S(2)}, u32[]{:S(2)}) collective-permute-start(bf16[32,4096]{1,0:T(8,128)(2,1)S(1)} %pad_maximum_fusion.6), channel_id=1, source_target_pairs={{0,2},{1,3},{2,0},{3,1},{4,6},{5,7},{6,4},{7,5},{8,10},{9,11},{10,... | collective-permute-start | bytes 786440 | tf_op jit(solution)/shard_map/ppermute | solution.py:246
  94.3 16.5 %collective-permute-start.32 = (bf16[32,4096]{1,0:T(8,128)(2,1)S(1)}, bf16[32,4096]{1,0:T(8,128)(2,1)S(1)}, u32[]{:S(2)}, u32[]{:S(2)}) collective-permute-start(bf16[32,4096]{1,0:T(8,128)(2,1)S(1)} %add_convert_fusion.2), channel_id=1, source_target_pairs={{0,2},{1,3},{2,0},{3,1},{4,6},{5,7},{6,4},{7,5},{8,10},{9,11},{10,... | collective-permute-start | bytes 786440 | tf_op jit(solution)/shard_map/ppermute | solution.py:246
  104.1 9.6 %collective-permute-start.30 = (bf16[32,4096]{1,0:T(8,128)(2,1)S(1)}, bf16[32,4096]{1,0:T(8,128)(2,1)S(1)}, u32[]{:S(2)}, u32[]{:S(2)}) collective-permute-start(bf16[32,4096]{1,0:T(8,128)(2,1)S(1)} %add_convert_fusion.3), channel_id=1, source_target_pairs={{0,4},{1,5},{2,6},{3,7},{4,0},{5,1},{6,2},{7,3},{8,12},{9,13},{10,... | collective-permute-start | bytes 786440 | tf_op jit(solution)/shard_map/ppermute | solution.py:246
  (6 other events, 57.2 us)

commit v19 on v16

--- a/solution.py
+++ b/solution.py
@@ -362,7 +362,7 @@
     lanes[final - 1], outs = together((lanes[final - 1], outs))
     sum_turn(0, turns - 1)
     outs[final - 1] = layer(final - 1)
-    lanes, outs, sums = together((lanes, outs, sums))
+    lanes, outs, sums[0][0] = together((lanes, outs, sums[0][0]))
     outs[final] = layer(final)
     for number in range(final, 0, -1):
         for turn in range(turns - 1 - int(number < final), -1, -1):

time: 110 us -> 113 us (1.027)
  starting transfers between devices: 38.6 us -> 40.1 us
    ppermute x26, starting transfers between devices: 26.1 us -> 28.9 us  [from_partner(): return lax.ppermute(block, axis, route)]
    ppermute x8, starting transfers between devices: 12.6 us -> 11.2 us  [across_chips(): lax.ppermute(block, 'expert', [(low, low ^ 2 * far) for low in range(coun...]
  transfers between devices with their start and end apart: 34 -> 34, of which waited for: 15 -> 16; matrix products, arithmetic and copies ran while one was open for 1% -> 1% of each run, Pallas kernels for 14% -> 16%
where the time goes in v19:
time: 113 us
  waiting for transfers between devices  50 us (44%)
  starting transfers between devices  40.1 us (35%)
  Pallas kernels  18.3 us (16%)
  other arithmetic  2.6 us (2%)
  local copies, waits for them, and re-layouts  1.44 us (1%)
    ppermute x26, waiting for transfers between devices, from_partner(): return lax.ppermute(block, axis, route)  44.3 us
    ppermute x26, starting transfers between devices, from_partner(): return lax.ppermute(block, axis, route)  28.9 us
    pallas_call x3, Pallas kernels, expert_layer(): pl.pallas_call(functools.partial(expert_kernel, count, experts), in_specs...  11.9 us
    ppermute x8, starting transfers between devices, across_chips(): lax.ppermute(block, 'expert', [(low, low ^ 2 * far) for low in range(coun...  11.2 us
    pallas_call x2, Pallas kernels, dequantize_call(): pl.pallas_call(kernel, in_specs=[pl.BlockSpec(memory_space=pltpu.SMEM)] *...  6.46 us
    ppermute x8, waiting for transfers between devices, across_chips(): lax.ppermute(block, 'expert', [(low, low ^ 2 * far) for low in range(coun...  5.67 us
  transfers between devices with their start and end apart: 34, of which 16 were waited for; matrix products, arithmetic and copies ran while one was open for 1% of the time, Pallas kernels for 16%

profile of v19, /device:TPU:0, one launch (start us, length us, event | category | flops | bytes accessed | tf_op | source)
XLA Modules:
  0.0 112.8 jit_solution(12456260929548981834)
XLA Ops:
  2.1 2.9 %collective-permute-start = (bf16[16,4224]{1,0:T(8,128)(2,1)S(1)}, bf16[16,4224]{1,0:T(8,128)(2,1)S(1)}, u32[]{:S(2)}, u32[]{:S(2)}) collective-permute-start(bf16[16,4224]{1,0:T(8,128)(2,1)S(1)} %concatenate.38), channel_id=1, source_target_pairs={{0,8},{8,0},{16,24},{24,16},{1,9},{9,1},{17,25},{25,17},{2,10},{10... | collective-permute-start | bytes 405512 | tf_op jit(solution)/shard_map/ppermute | solution.py:20
  5.0 1.6 %collective-permute-start.2 = (bf16[16,4224]{1,0:T(8,128)(2,1)S(1)}, bf16[16,4224]{1,0:T(8,128)(2,1)S(1)}, u32[]{:S(2)}, u32[]{:S(2)}) collective-permute-start(bf16[16,4224]{1,0:T(8,128)(2,1)S(1)} %concatenate.38), channel_id=1, source_target_pairs={{0,2},{1,3},{2,0},{3,1},{4,6},{5,7},{6,4},{7,5},{8,10},{9,11},{10,... | collective-permute-start | bytes 405512 | tf_op jit(solution)/shard_map/ppermute | solution.py:246
  6.6 2.6 %collective-permute-start.3 = (bf16[16,4224]{1,0:T(8,128)(2,1)S(1)}, bf16[16,4224]{1,0:T(8,128)(2,1)S(1)}, u32[]{:S(2)}, u32[]{:S(2)}) collective-permute-start(bf16[16,4224]{1,0:T(8,128)(2,1)S(1)} %concatenate.38), channel_id=1, source_target_pairs={{0,4},{1,5},{2,6},{3,7},{4,0},{5,1},{6,2},{7,3},{8,12},{9,13},{10,... | collective-permute-start | bytes 405512 | tf_op jit(solution)/shard_map/ppermute | solution.py:246
  9.2 1.5 %collective-permute-start.1 = (bf16[16,4224]{1,0:T(8,128)(2,1)S(1)}, bf16[16,4224]{1,0:T(8,128)(2,1)S(1)}, u32[]{:S(2)}, u32[]{:S(2)}) collective-permute-start(bf16[16,4224]{1,0:T(8,128)(2,1)S(1)} %concatenate.39), channel_id=1, source_target_pairs={{0,16},{16,0},{8,24},{24,8},{1,17},{17,1},{9,25},{25,9},{2,18},{18... | collective-permute-start | bytes 405512 | tf_op jit(solution)/shard_map/ppermute | solution.py:20
  10.7 3.7 %dequantize_in.1.refs_4_ = bf16[4096,768]{1,0:T(8,128)(2,1)S(1)} custom-call(f32[3,32]{1,0:T(4,128)S(1)} %get-tuple-element.150.gate_scales, f32[3,32]{1,0:T(4,128)S(1)} %get-tuple-element.149.up_scales, bf16[4096,384]{1,0:T(8,128)(2,1)} %bitcast.17, bf16[4096,384]{1,0:T(8,128)(2,1)} %bitcast.18), custom_call_target="tpu_custom_call" | custom-call | flops 3145728 | bytes 12582912 | tf_op jit(solution)/shard_map/dequantize_in/pallas_call | solution.py:155
  15.2 1.5 %collective-permute-start.4 = (bf16[32,4224]{1,0:T(8,128)(2,1)S(1)}, bf16[32,4224]{1,0:T(8,128)(2,1)S(1)}, u32[]{:S(2)}, u32[]{:S(2)}) collective-permute-start(bf16[32,4224]{1,0:T(8,128)(2,1)S(1)} %pad_maximum_fusion.2.refs_0_), channel_id=1, source_target_pairs={{0,16},{16,0},{8,24},{24,8},{1,17},{17,1},{9,25},{25,9},{2,18},{18... | collective-permute-start | bytes 811016 | tf_op jit(solution)/shard_map/ppermute | solution.py:20
  17.6 2.7 %collective-permute-start.7 = (bf16[16,4224]{1,0:T(8,128)(2,1)S(1)}, bf16[16,4224]{1,0:T(8,128)(2,1)S(1)}, u32[]{:S(2)}, u32[]{:S(2)}) collective-permute-start(bf16[16,4224]{1,0:T(8,128)(2,1)S(1)} %concatenate.39), channel_id=1, source_target_pairs={{0,4},{1,5},{2,6},{3,7},{4,0},{5,1},{6,2},{7,3},{8,12},{9,13},{10,... | collective-permute-start | bytes 405512 | tf_op jit(solution)/shard_map/ppermute | solution.py:246
  20.3 2.8 %dequantize_down.1.refs_6_ = bf16[384,4096]{1,0:T(8,128)(2,1)S(1)} custom-call(f32[3,32]{1,0:T(4,128)S(1)} %bitcast.15, bf16[384,4096]{1,0:T(8,128)(2,1)} %bitcast.16), custom_call_target="tpu_custom_call" | custom-call | flops 1572864 | bytes 6291456 | tf_op jit(solution)/shard_map/dequantize_down/pallas_call | solution.py:155
  23.0 2.3 %collective-permute-done.6 = bf16[16,4224]{1,0:T(8,128)(2,1)S(1)} collective-permute-done((bf16[16,4224]{1,0:T(8,128)(2,1)S(1)}, bf16[16,4224]{1,0:T(8,128)(2,1)S(1)}, u32[]{:S(2)}, u32[]{:S(2)}) %collective-permute-start.6) | collective-permute-done | bytes 135200 | tf_op jit(solution)/shard_map/ppermute | solution.py:246
  25.3 1.3 %collective-permute-done.7 = bf16[16,4224]{1,0:T(8,128)(2,1)S(1)} collective-permute-done((bf16[16,4224]{1,0:T(8,128)(2,1)S(1)}, bf16[16,4224]{1,0:T(8,128)(2,1)S(1)}, u32[]{:S(2)}, u32[]{:S(2)}) %collective-permute-start.7) | collective-permute-done | bytes 135200 | tf_op jit(solution)/shard_map/ppermute | solution.py:246
  27.6 1.6 %collective-permute-start.8 = (bf16[32,4224]{1,0:T(8,128)(2,1)S(1)}, bf16[32,4224]{1,0:T(8,128)(2,1)S(1)}, u32[]{:S(2)}, u32[]{:S(2)}) collective-permute-start(bf16[32,4224]{1,0:T(8,128)(2,1)S(1)} %constant_dynamic-update-slice_fusion), channel_id=1, source_target_pairs={{0,8},{8,0},{16,24},{24,16},{1,9},{9,1},{17,25},{25,17},{2,10},{10... | collective-permute-start | bytes 811016 | tf_op jit(solution)/shard_map/ppermute | solution.py:20
  29.2 6.5 %collective-permute-done.9 = bf16[32,4224]{1,0:T(8,128)(2,1)S(1)} collective-permute-done((bf16[32,4224]{1,0:T(8,128)(2,1)S(1)}, bf16[32,4224]{1,0:T(8,128)(2,1)S(1)}, u32[]{:S(2)}, u32[]{:S(2)}) %collective-permute-start.9) | collective-permute-done | bytes 270368 | tf_op jit(solution)/shard_map/ppermute | solution.py:20
  36.1 1.6 %collective-permute-start.13 = (bf16[64,4224]{1,0:T(8,128)(2,1)S(1)}, bf16[64,4224]{1,0:T(8,128)(2,1)S(1)}, u32[]{:S(2)}, u32[]{:S(2)}) collective-permute-start(bf16[64,4224]{1,0:T(8,128)(2,1)S(1)} %pad_maximum_fusion.refs_0_), channel_id=1, source_target_pairs={{0,16},{16,0},{8,24},{24,8},{1,17},{17,1},{9,25},{25,9},{2,18},{18... | collective-permute-start | bytes 1622024 | tf_op jit(solution)/shard_map/ppermute | solution.py:20
  37.7 1.5 %collective-permute-start.14 = (bf16[64,4224]{1,0:T(8,128)(2,1)S(1)}, bf16[64,4224]{1,0:T(8,128)(2,1)S(1)}, u32[]{:S(2)}, u32[]{:S(2)}) collective-permute-start(bf16[64,4224]{1,0:T(8,128)(2,1)S(1)} %pad_maximum_fusion.1.refs_2_), channel_id=1, source_target_pairs={{0,8},{8,0},{16,24},{24,16},{1,9},{9,1},{17,25},{25,17},{2,10},{10... | collective-permute-start | bytes 1622024 | tf_op jit(solution)/shard_map/ppermute | solution.py:20
  40.3 3.1 %expert_layer.3 = (bf16[32,4096]{1,0:T(8,128)(2,1)S(1)}, bf16[32,4096]{1,0:T(8,128)(2,1)S(1)}, bf16[32,4096]{1,0:T(8,128)(2,1)S(1)}, bf16[32,4096]{1,0:T(8,128)(2,1)S(1)}) custom-call(s32[1]{0:T(128)} %bitcast.own_expert, bf16[32,4224]{1,0:T(8,128)(2,1)S(1)} %pad_maximum_fusion.2.refs_0_, bf16[32,4224]{1,0:T(8,128)(2,1)S(1)} %collective-permute-done.4.refs_1_, ...), custom_call_target="tpu_custom_call" | custom-call | flops 2415919104 | bytes 20971520 | tf_op jit(solution)/shard_map/expert_layer/pallas_call | solution.py:225
  43.4 9.3 %collective-permute-done.17 = bf16[16,4224]{1,0:T(8,128)(2,1)S(1)} collective-permute-done((bf16[16,4224]{1,0:T(8,128)(2,1)S(1)}, bf16[16,4224]{1,0:T(8,128)(2,1)S(1)}, u32[]{:S(2)}, u32[]{:S(2)}) %collective-permute-start.17) | collective-permute-done | bytes 135200 | tf_op jit(solution)/shard_map/ppermute | solution.py:20
  52.7 1.6 %collective-permute-start.18 = (bf16[32,4224]{1,0:T(8,128)(2,1)S(1)}, bf16[32,4224]{1,0:T(8,128)(2,1)S(1)}, u32[]{:S(2)}, u32[]{:S(2)}) collective-permute-start(bf16[32,4224]{1,0:T(8,128)(2,1)S(1)} %pad_maximum_fusion.5.refs_2_), channel_id=1, source_target_pairs={{0,8},{8,0},{16,24},{24,16},{1,9},{9,1},{17,25},{25,17},{2,10},{10... | collective-permute-start | bytes 811016 | tf_op jit(solution)/shard_map/ppermute | solution.py:20
  54.3 1.3 %collective-permute-start.16 = (bf16[32,4224]{1,0:T(8,128)(2,1)S(1)}, bf16[32,4224]{1,0:T(8,128)(2,1)S(1)}, u32[]{:S(2)}, u32[]{:S(2)}) collective-permute-start(bf16[32,4224]{1,0:T(8,128)(2,1)S(1)} %pad_maximum_fusion.4.refs_0_), channel_id=1, source_target_pairs={{0,16},{16,0},{8,24},{24,8},{1,17},{17,1},{9,25},{25,9},{2,18},{18... | collective-permute-start | bytes 811016 | tf_op jit(solution)/shard_map/ppermute | solution.py:20
  57.2 5.7 %expert_layer.4 = (bf16[64,4096]{1,0:T(8,128)(2,1)S(1)}, bf16[64,4096]{1,0:T(8,128)(2,1)S(1)}, bf16[64,4096]{1,0:T(8,128)(2,1)S(1)}, bf16[64,4096]{1,0:T(8,128)(2,1)S(1)}) custom-call(s32[1]{0:T(128)} %bitcast.own_expert, bf16[64,4224]{1,0:T(8,128)(2,1)S(1)} %pad_maximum_fusion.refs_0_, bf16[64,4224]{1,0:T(8,128)(2,1)S(1)} %collective-permute-done.13.refs_1_, ...), custom_call_target="tpu_custom_call" | custom-call | flops 4831838208 | bytes 23068672 | tf_op jit(solution)/shard_map/expert_layer/pallas_call | solution.py:225
  62.9 3.6 %collective-permute-done.19 = bf16[32,4096]{1,0:T(8,128)(2,1)S(1)} collective-permute-done((bf16[32,4096]{1,0:T(8,128)(2,1)S(1)}, bf16[32,4096]{1,0:T(8,128)(2,1)S(1)}, u32[]{:S(2)}, u32[]{:S(2)}) %collective-permute-start.19) | collective-permute-done | bytes 262176 | tf_op jit(solution)/shard_map/ppermute | solution.py:20
  66.6 3.1 %expert_layer.5 = (bf16[32,4096]{1,0:T(8,128)(2,1)S(1)}, bf16[32,4096]{1,0:T(8,128)(2,1)S(1)}, bf16[32,4096]{1,0:T(8,128)(2,1)S(1)}, bf16[32,4096]{1,0:T(8,128)(2,1)S(1)}) custom-call(s32[1]{0:T(128)} %bitcast.own_expert, bf16[32,4224]{1,0:T(8,128)(2,1)S(1)} %pad_maximum_fusion.4.refs_0_, bf16[32,4224]{1,0:T(8,128)(2,1)S(1)} %collective-permute-done.16.refs_1_, ...), custom_call_target="tpu_custom_call" | custom-call | flops 2415919104 | bytes 20971520 | tf_op jit(solution)/shard_map/expert_layer/pallas_call | solution.py:225
  71.4 1.3 %collective-permute-start.22 = (bf16[64,4096]{1,0:T(8,128)(2,1)S(1)}, bf16[64,4096]{1,0:T(8,128)(2,1)S(1)}, u32[]{:S(2)}, u32[]{:S(2)}) collective-permute-start(bf16[64,4096]{1,0:T(8,128)(2,1)S(1)} %get-tuple-element.118), channel_id=1, source_target_pairs={{0,8},{8,0},{16,24},{24,16},{1,9},{9,1},{17,25},{25,17},{2,10},{10... | collective-permute-start | bytes 1572872 | tf_op jit(solution)/shard_map/ppermute | solution.py:20
  73.9 5.1 %collective-permute-done.26 = bf16[32,4096]{1,0:T(8,128)(2,1)S(1)} collective-permute-done((bf16[32,4096]{1,0:T(8,128)(2,1)S(1)}, bf16[32,4096]{1,0:T(8,128)(2,1)S(1)}, u32[]{:S(2)}, u32[]{:S(2)}) %collective-permute-start.26) | collective-permute-done | bytes 262176 | tf_op jit(solution)/shard_map/ppermute | solution.py:20
  81.2 8.5 %collective-permute-done.27 = bf16[16,4096]{1,0:T(8,128)(2,1)S(1)} collective-permute-done((bf16[16,4096]{1,0:T(8,128)(2,1)S(1)}, bf16[16,4096]{1,0:T(8,128)(2,1)S(1)}, u32[]{:S(2)}, u32[]{:S(2)}) %collective-permute-start.27) | collective-permute-done | bytes 131104 | tf_op jit(solution)/shard_map/ppermute | solution.py:20
  91.5 1.4 %collective-permute-start.30 = (bf16[32,4096]{1,0:T(8,128)(2,1)S(1)}, bf16[32,4096]{1,0:T(8,128)(2,1)S(1)}, u32[]{:S(2)}, u32[]{:S(2)}) collective-permute-start(bf16[32,4096]{1,0:T(8,128)(2,1)S(1)} %pad_maximum_fusion.6), channel_id=1, source_target_pairs={{0,2},{1,3},{2,0},{3,1},{4,6},{5,7},{6,4},{7,5},{8,10},{9,11},{10,... | collective-permute-start | bytes 786440 | tf_op jit(solution)/shard_map/ppermute | solution.py:246
  93.6 3.1 %collective-permute-done.24 = bf16[32,4096]{1,0:T(8,128)(2,1)S(1)} collective-permute-done((bf16[32,4096]{1,0:T(8,128)(2,1)S(1)}, bf16[32,4096]{1,0:T(8,128)(2,1)S(1)}, u32[]{:S(2)}, u32[]{:S(2)}) %collective-permute-start.24) | collective-permute-done | bytes 262176 | tf_op jit(solution)/shard_map/ppermute | solution.py:20
  96.7 3.6 %collective-permute-done.23 = bf16[32,4096]{1,0:T(8,128)(2,1)S(1)} collective-permute-done((bf16[32,4096]{1,0:T(8,128)(2,1)S(1)}, bf16[32,4096]{1,0:T(8,128)(2,1)S(1)}, u32[]{:S(2)}, u32[]{:S(2)}) %collective-permute-start.23) | collective-permute-done | bytes 262176 | tf_op jit(solution)/shard_map/ppermute | solution.py:20
  100.4 1.4 %collective-permute-done.30 = bf16[32,4096]{1,0:T(8,128)(2,1)S(1)} collective-permute-done((bf16[32,4096]{1,0:T(8,128)(2,1)S(1)}, bf16[32,4096]{1,0:T(8,128)(2,1)S(1)}, u32[]{:S(2)}, u32[]{:S(2)}) %collective-permute-start.30) | collective-permute-done | bytes 262176 | tf_op jit(solution)/shard_map/ppermute | solution.py:246
  102.7 1.4 %collective-permute-start.32 = (bf16[32,4096]{1,0:T(8,128)(2,1)S(1)}, bf16[32,4096]{1,0:T(8,128)(2,1)S(1)}, u32[]{:S(2)}, u32[]{:S(2)}) collective-permute-start(bf16[32,4096]{1,0:T(8,128)(2,1)S(1)} %add_convert_fusion.6), channel_id=1, source_target_pairs={{0,2},{1,3},{2,0},{3,1},{4,6},{5,7},{6,4},{7,5},{8,10},{9,11},{10,... | collective-permute-start | bytes 786440 | tf_op jit(solution)/shard_map/ppermute | solution.py:246
  104.1 2.7 %collective-permute-start.25 = (bf16[16,4096]{1,0:T(8,128)(2,1)S(1)}, bf16[16,4096]{1,0:T(8,128)(2,1)S(1)}, u32[]{:S(2)}, u32[]{:S(2)}) collective-permute-start(bf16[16,4096]{1,0:T(8,128)(2,1)S(1)} %split.41), channel_id=1, source_target_pairs={{0,8},{8,0},{16,24},{24,16},{1,9},{9,1},{17,25},{25,17},{2,10},{10... | collective-permute-start | bytes 393224 | tf_op jit(solution)/shard_map/ppermute | solution.py:20
  107.9 1.9 %collective-permute-done.25 = bf16[16,4096]{1,0:T(8,128)(2,1)S(1)} collective-permute-done((bf16[16,4096]{1,0:T(8,128)(2,1)S(1)}, bf16[16,4096]{1,0:T(8,128)(2,1)S(1)}, u32[]{:S(2)}, u32[]{:S(2)}) %collective-permute-start.25) | collective-permute-done | bytes 131104 | tf_op jit(solution)/shard_map/ppermute | solution.py:20
  109.8 2.1 %collective-permute-done.33 = bf16[16,4096]{1,0:T(8,128)(2,1)S(1)} collective-permute-done((bf16[16,4096]{1,0:T(8,128)(2,1)S(1)}, bf16[16,4096]{1,0:T(8,128)(2,1)S(1)}, u32[]{:S(2)}, u32[]{:S(2)}) %collective-permute-start.33) | collective-permute-done | bytes 131104 | tf_op jit(solution)/shard_map/ppermute | solution.py:20
  (90 shorter events, 18.3 us)
Async XLA Ops:
  2.1 12.4 %collective-permute-start = (bf16[16,4224]{1,0:T(8,128)(2,1)S(1)}, bf16[16,4224]{1,0:T(8,128)(2,1)S(1)}, u32[]{:S(2)}, u32[]{:S(2)}) collective-permute-start(bf16[16,4224]{1,0:T(8,128)(2,1)S(1)} %concatenate.38), channel_id=1, source_target_pairs={{0,8},{8,0},{16,24},{24,16},{1,9},{9,1},{17,25},{25,17},{2,10},{10... | collective-permute-start | bytes 405512 | tf_op jit(solution)/shard_map/ppermute | solution.py:20
  5.0 9.5 %collective-permute-start.2 = (bf16[16,4224]{1,0:T(8,128)(2,1)S(1)}, bf16[16,4224]{1,0:T(8,128)(2,1)S(1)}, u32[]{:S(2)}, u32[]{:S(2)}) collective-permute-start(bf16[16,4224]{1,0:T(8,128)(2,1)S(1)} %concatenate.38), channel_id=1, source_target_pairs={{0,2},{1,3},{2,0},{3,1},{4,6},{5,7},{6,4},{7,5},{8,10},{9,11},{10,... | collective-permute-start | bytes 405512 | tf_op jit(solution)/shard_map/ppermute | solution.py:246
  6.6 8.6 %collective-permute-start.3 = (bf16[16,4224]{1,0:T(8,128)(2,1)S(1)}, bf16[16,4224]{1,0:T(8,128)(2,1)S(1)}, u32[]{:S(2)}, u32[]{:S(2)}) collective-permute-start(bf16[16,4224]{1,0:T(8,128)(2,1)S(1)} %concatenate.38), channel_id=1, source_target_pairs={{0,4},{1,5},{2,6},{3,7},{4,0},{5,1},{6,2},{7,3},{8,12},{9,13},{10,... | collective-permute-start | bytes 405512 | tf_op jit(solution)/shard_map/ppermute | solution.py:246
  15.2 20.9 %collective-permute-start.11 = (bf16[4096,768]{1,0:T(8,128)(2,1)S(1)}, bf16[4096,768]{1,0:T(8,128)(2,1)S(1)}, u32[]{:S(2)}, u32[]{:S(2)}) collective-permute-start(bf16[4096,768]{1,0:T(8,128)(2,1)S(1)} %dequantize_in.1.refs_4_), channel_id=1, source_target_pairs={{0,1},{1,0},{2,3},{3,2},{4,5},{5,4},{6,7},{7,6},{8,9},{9,8},{10,11... | collective-permute-start | bytes 18874376 | tf_op jit(solution)/shard_map/ppermute | solution.py:20
  15.2 11.5 %collective-permute-start.4 = (bf16[32,4224]{1,0:T(8,128)(2,1)S(1)}, bf16[32,4224]{1,0:T(8,128)(2,1)S(1)}, u32[]{:S(2)}, u32[]{:S(2)}) collective-permute-start(bf16[32,4224]{1,0:T(8,128)(2,1)S(1)} %pad_maximum_fusion.2.refs_0_), channel_id=1, source_target_pairs={{0,16},{16,0},{8,24},{24,8},{1,17},{17,1},{9,25},{25,9},{2,18},{18... | collective-permute-start | bytes 811016 | tf_op jit(solution)/shard_map/ppermute | solution.py:20
  16.7 9.9 %collective-permute-start.5 = (bf16[32,4224]{1,0:T(8,128)(2,1)S(1)}, bf16[32,4224]{1,0:T(8,128)(2,1)S(1)}, u32[]{:S(2)}, u32[]{:S(2)}) collective-permute-start(bf16[32,4224]{1,0:T(8,128)(2,1)S(1)} %pad_maximum_fusion.3.refs_2_), channel_id=1, source_target_pairs={{0,8},{8,0},{16,24},{24,16},{1,9},{9,1},{17,25},{25,17},{2,10},{10... | collective-permute-start | bytes 811016 | tf_op jit(solution)/shard_map/ppermute | solution.py:20
  17.2 8.1 %collective-permute-start.6 = (bf16[16,4224]{1,0:T(8,128)(2,1)S(1)}, bf16[16,4224]{1,0:T(8,128)(2,1)S(1)}, u32[]{:S(2)}, u32[]{:S(2)}) collective-permute-start(bf16[16,4224]{1,0:T(8,128)(2,1)S(1)} %concatenate.39), channel_id=1, source_target_pairs={{0,2},{1,3},{2,0},{3,1},{4,6},{5,7},{6,4},{7,5},{8,10},{9,11},{10,... | collective-permute-start | bytes 405512 | tf_op jit(solution)/shard_map/ppermute | solution.py:246
  17.6 9.0 %collective-permute-start.7 = (bf16[16,4224]{1,0:T(8,128)(2,1)S(1)}, bf16[16,4224]{1,0:T(8,128)(2,1)S(1)}, u32[]{:S(2)}, u32[]{:S(2)}) collective-permute-start(bf16[16,4224]{1,0:T(8,128)(2,1)S(1)} %concatenate.39), channel_id=1, source_target_pairs={{0,4},{1,5},{2,6},{3,7},{4,0},{5,1},{6,2},{7,3},{8,12},{9,13},{10,... | collective-permute-start | bytes 405512 | tf_op jit(solution)/shard_map/ppermute | solution.py:246
  26.6 9.4 %collective-permute-start.12 = (bf16[384,4096]{1,0:T(8,128)(2,1)S(1)}, bf16[384,4096]{1,0:T(8,128)(2,1)S(1)}, u32[]{:S(2)}, u32[]{:S(2)}) collective-permute-start(bf16[384,4096]{1,0:T(8,128)(2,1)S(1)} %dequantize_down.1.refs_6_), channel_id=1, source_target_pairs={{0,1},{1,0},{2,3},{3,2},{4,5},{5,4},{6,7},{7,6},{8,9},{9,8},{10,11... | collective-permute-start | bytes 9437192 | tf_op jit(solution)/shard_map/ppermute | solution.py:20
  26.7 8.9 %collective-permute-start.9 = (bf16[32,4224]{1,0:T(8,128)(2,1)S(1)}, bf16[32,4224]{1,0:T(8,128)(2,1)S(1)}, u32[]{:S(2)}, u32[]{:S(2)}) collective-permute-start(bf16[32,4224]{1,0:T(8,128)(2,1)S(1)} %constant_dynamic-update-slice_fusion.2), channel_id=1, source_target_pairs={{0,16},{16,0},{8,24},{24,8},{1,17},{17,1},{9,25},{25,9},{2,18},{18... | collective-permute-start | bytes 811016 | tf_op jit(solution)/shard_map/ppermute | solution.py:20
  27.3 8.8 %collective-permute-start.10 = (bf16[32,4224]{1,0:T(8,128)(2,1)S(1)}, bf16[32,4224]{1,0:T(8,128)(2,1)S(1)}, u32[]{:S(2)}, u32[]{:S(2)}) collective-permute-start(bf16[32,4224]{1,0:T(8,128)(2,1)S(1)} %constant_dynamic-update-slice_fusion.2), channel_id=1, source_target_pairs={{0,2},{1,3},{2,0},{3,1},{4,6},{5,7},{6,4},{7,5},{8,10},{9,11},{10,... | collective-permute-start | bytes 811016 | tf_op jit(solution)/shard_map/ppermute | solution.py:246
  27.6 8.4 %collective-permute-start.8 = (bf16[32,4224]{1,0:T(8,128)(2,1)S(1)}, bf16[32,4224]{1,0:T(8,128)(2,1)S(1)}, u32[]{:S(2)}, u32[]{:S(2)}) collective-permute-start(bf16[32,4224]{1,0:T(8,128)(2,1)S(1)} %constant_dynamic-update-slice_fusion), channel_id=1, source_target_pairs={{0,8},{8,0},{16,24},{24,16},{1,9},{9,1},{17,25},{25,17},{2,10},{10... | collective-permute-start | bytes 811016 | tf_op jit(solution)/shard_map/ppermute | solution.py:20
  36.1 19.5 %collective-permute-start.13 = (bf16[64,4224]{1,0:T(8,128)(2,1)S(1)}, bf16[64,4224]{1,0:T(8,128)(2,1)S(1)}, u32[]{:S(2)}, u32[]{:S(2)}) collective-permute-start(bf16[64,4224]{1,0:T(8,128)(2,1)S(1)} %pad_maximum_fusion.refs_0_), channel_id=1, source_target_pairs={{0,16},{16,0},{8,24},{24,8},{1,17},{17,1},{9,25},{25,9},{2,18},{18... | collective-permute-start | bytes 1622024 | tf_op jit(solution)/shard_map/ppermute | solution.py:20
  37.7 17.9 %collective-permute-start.14 = (bf16[64,4224]{1,0:T(8,128)(2,1)S(1)}, bf16[64,4224]{1,0:T(8,128)(2,1)S(1)}, u32[]{:S(2)}, u32[]{:S(2)}) collective-permute-start(bf16[64,4224]{1,0:T(8,128)(2,1)S(1)} %pad_maximum_fusion.1.refs_2_), channel_id=1, source_target_pairs={{0,8},{8,0},{16,24},{24,16},{1,9},{9,1},{17,25},{25,17},{2,10},{10... | collective-permute-start | bytes 1622024 | tf_op jit(solution)/shard_map/ppermute | solution.py:20
  39.2 13.4 %collective-permute-start.17 = (bf16[16,4224]{1,0:T(8,128)(2,1)S(1)}, bf16[16,4224]{1,0:T(8,128)(2,1)S(1)}, u32[]{:S(2)}, u32[]{:S(2)}) collective-permute-start(bf16[16,4224]{1,0:T(8,128)(2,1)S(1)} %get-tuple-element.139), channel_id=1, source_target_pairs={{0,16},{16,0},{8,24},{24,8},{1,17},{17,1},{9,25},{25,9},{2,18},{18... | collective-permute-start | bytes 405512 | tf_op jit(solution)/shard_map/ppermute | solution.py:20
  39.8 14.5 %collective-permute-start.15 = (bf16[16,4224]{1,0:T(8,128)(2,1)S(1)}, bf16[16,4224]{1,0:T(8,128)(2,1)S(1)}, u32[]{:S(2)}, u32[]{:S(2)}) collective-permute-start(bf16[16,4224]{1,0:T(8,128)(2,1)S(1)} %get-tuple-element.140), channel_id=1, source_target_pairs={{0,8},{8,0},{16,24},{24,16},{1,9},{9,1},{17,25},{25,17},{2,10},{10... | collective-permute-start | bytes 405512 | tf_op jit(solution)/shard_map/ppermute | solution.py:20
  52.7 13.9 %collective-permute-start.18 = (bf16[32,4224]{1,0:T(8,128)(2,1)S(1)}, bf16[32,4224]{1,0:T(8,128)(2,1)S(1)}, u32[]{:S(2)}, u32[]{:S(2)}) collective-permute-start(bf16[32,4224]{1,0:T(8,128)(2,1)S(1)} %pad_maximum_fusion.5.refs_2_), channel_id=1, source_target_pairs={{0,8},{8,0},{16,24},{24,16},{1,9},{9,1},{17,25},{25,17},{2,10},{10... | collective-permute-start | bytes 811016 | tf_op jit(solution)/shard_map/ppermute | solution.py:20
  54.3 12.3 %collective-permute-start.16 = (bf16[32,4224]{1,0:T(8,128)(2,1)S(1)}, bf16[32,4224]{1,0:T(8,128)(2,1)S(1)}, u32[]{:S(2)}, u32[]{:S(2)}) collective-permute-start(bf16[32,4224]{1,0:T(8,128)(2,1)S(1)} %pad_maximum_fusion.4.refs_0_), channel_id=1, source_target_pairs={{0,16},{16,0},{8,24},{24,8},{1,17},{17,1},{9,25},{25,9},{2,18},{18... | collective-permute-start | bytes 811016 | tf_op jit(solution)/shard_map/ppermute | solution.py:20
  55.6 11.0 %collective-permute-start.19 = (bf16[32,4096]{1,0:T(8,128)(2,1)S(1)}, bf16[32,4096]{1,0:T(8,128)(2,1)S(1)}, u32[]{:S(2)}, u32[]{:S(2)}) collective-permute-start(bf16[32,4096]{1,0:T(8,128)(2,1)S(1)} %get-tuple-element.107), channel_id=1, source_target_pairs={{0,16},{16,0},{8,24},{24,8},{1,17},{17,1},{9,25},{25,9},{2,18},{18... | collective-permute-start | bytes 786440 | tf_op jit(solution)/shard_map/ppermute | solution.py:20
  56.4 17.5 %collective-permute-start.20 = (bf16[32,4096]{1,0:T(8,128)(2,1)S(1)}, bf16[32,4096]{1,0:T(8,128)(2,1)S(1)}, u32[]{:S(2)}, u32[]{:S(2)}) collective-permute-start(bf16[32,4096]{1,0:T(8,128)(2,1)S(1)} %get-tuple-element.109), channel_id=1, source_target_pairs={{0,8},{8,0},{16,24},{24,16},{1,9},{9,1},{17,25},{25,17},{2,10},{10... | collective-permute-start | bytes 786440 | tf_op jit(solution)/shard_map/ppermute | solution.py:20
  69.7 9.3 %collective-permute-start.26 = (bf16[32,4096]{1,0:T(8,128)(2,1)S(1)}, bf16[32,4096]{1,0:T(8,128)(2,1)S(1)}, u32[]{:S(2)}, u32[]{:S(2)}) collective-permute-start(bf16[32,4096]{1,0:T(8,128)(2,1)S(1)} %get-tuple-element.124), channel_id=1, source_target_pairs={{0,16},{16,0},{8,24},{24,8},{1,17},{17,1},{9,25},{25,9},{2,18},{18... | collective-permute-start | bytes 786440 | tf_op jit(solution)/shard_map/ppermute | solution.py:20
  70.8 9.2 %collective-permute-start.28 = (bf16[32,4096]{1,0:T(8,128)(2,1)S(1)}, bf16[32,4096]{1,0:T(8,128)(2,1)S(1)}, u32[]{:S(2)}, u32[]{:S(2)}) collective-permute-start(bf16[32,4096]{1,0:T(8,128)(2,1)S(1)} %get-tuple-element.126), channel_id=1, source_target_pairs={{0,8},{8,0},{16,24},{24,16},{1,9},{9,1},{17,25},{25,17},{2,10},{10... | collective-permute-start | bytes 786440 | tf_op jit(solution)/shard_map/ppermute | solution.py:20
  71.4 18.5 %collective-permute-start.22 = (bf16[64,4096]{1,0:T(8,128)(2,1)S(1)}, bf16[64,4096]{1,0:T(8,128)(2,1)S(1)}, u32[]{:S(2)}, u32[]{:S(2)}) collective-permute-start(bf16[64,4096]{1,0:T(8,128)(2,1)S(1)} %get-tuple-element.118), channel_id=1, source_target_pairs={{0,8},{8,0},{16,24},{24,16},{1,9},{9,1},{17,25},{25,17},{2,10},{10... | collective-permute-start | bytes 1572872 | tf_op jit(solution)/shard_map/ppermute | solution.py:20
  72.8 17.3 %collective-permute-start.21 = (bf16[64,4096]{1,0:T(8,128)(2,1)S(1)}, bf16[64,4096]{1,0:T(8,128)(2,1)S(1)}, u32[]{:S(2)}, u32[]{:S(2)}) collective-permute-start(bf16[64,4096]{1,0:T(8,128)(2,1)S(1)} %get-tuple-element.116), channel_id=1, source_target_pairs={{0,16},{16,0},{8,24},{24,8},{1,17},{17,1},{9,25},{25,9},{2,18},{18... | collective-permute-start | bytes 1572872 | tf_op jit(solution)/shard_map/ppermute | solution.py:20
  79.1 10.6 %collective-permute-start.27 = (bf16[16,4096]{1,0:T(8,128)(2,1)S(1)}, bf16[16,4096]{1,0:T(8,128)(2,1)S(1)}, u32[]{:S(2)}, u32[]{:S(2)}) collective-permute-start(bf16[16,4096]{1,0:T(8,128)(2,1)S(1)} %split.49), channel_id=1, source_target_pairs={{0,8},{8,0},{16,24},{24,16},{1,9},{9,1},{17,25},{25,17},{2,10},{10... | collective-permute-start | bytes 393224 | tf_op jit(solution)/shard_map/ppermute | solution.py:20
  80.1 9.8 %collective-permute-start.29 = (bf16[16,4096]{1,0:T(8,128)(2,1)S(1)}, bf16[16,4096]{1,0:T(8,128)(2,1)S(1)}, u32[]{:S(2)}, u32[]{:S(2)}) collective-permute-start(bf16[16,4096]{1,0:T(8,128)(2,1)S(1)} %split.51), channel_id=1, source_target_pairs={{0,16},{16,0},{8,24},{24,8},{1,17},{17,1},{9,25},{25,9},{2,18},{18... | collective-permute-start | bytes 393224 | tf_op jit(solution)/shard_map/ppermute | solution.py:20
  90.2 6.4 %collective-permute-start.24 = (bf16[32,4096]{1,0:T(8,128)(2,1)S(1)}, bf16[32,4096]{1,0:T(8,128)(2,1)S(1)}, u32[]{:S(2)}, u32[]{:S(2)}) collective-permute-start(bf16[32,4096]{1,0:T(8,128)(2,1)S(1)} %split.39), channel_id=1, source_target_pairs={{0,16},{16,0},{8,24},{24,8},{1,17},{17,1},{9,25},{25,9},{2,18},{18... | collective-permute-start | bytes 786440 | tf_op jit(solution)/shard_map/ppermute | solution.py:20
  91.5 10.3 %collective-permute-start.30 = (bf16[32,4096]{1,0:T(8,128)(2,1)S(1)}, bf16[32,4096]{1,0:T(8,128)(2,1)S(1)}, u32[]{:S(2)}, u32[]{:S(2)}) collective-permute-start(bf16[32,4096]{1,0:T(8,128)(2,1)S(1)} %pad_maximum_fusion.6), channel_id=1, source_target_pairs={{0,2},{1,3},{2,0},{3,1},{4,6},{5,7},{6,4},{7,5},{8,10},{9,11},{10,... | collective-permute-start | bytes 786440 | tf_op jit(solution)/shard_map/ppermute | solution.py:246
  93.0 7.4 %collective-permute-start.23 = (bf16[32,4096]{1,0:T(8,128)(2,1)S(1)}, bf16[32,4096]{1,0:T(8,128)(2,1)S(1)}, u32[]{:S(2)}, u32[]{:S(2)}) collective-permute-start(bf16[32,4096]{1,0:T(8,128)(2,1)S(1)} %split.37), channel_id=1, source_target_pairs={{0,8},{8,0},{16,24},{24,16},{1,9},{9,1},{17,25},{25,17},{2,10},{10... | collective-permute-start | bytes 786440 | tf_op jit(solution)/shard_map/ppermute | solution.py:20
  101.9 10.0 %collective-permute-start.31 = (bf16[32,4096]{1,0:T(8,128)(2,1)S(1)}, bf16[32,4096]{1,0:T(8,128)(2,1)S(1)}, u32[]{:S(2)}, u32[]{:S(2)}) collective-permute-start(bf16[32,4096]{1,0:T(8,128)(2,1)S(1)} %add_convert_fusion.2), channel_id=1, source_target_pairs={{0,4},{1,5},{2,6},{3,7},{4,0},{5,1},{6,2},{7,3},{8,12},{9,13},{10,... | collective-permute-start | bytes 786440 | tf_op jit(solution)/shard_map/ppermute | solution.py:246
  102.7 9.2 %collective-permute-start.32 = (bf16[32,4096]{1,0:T(8,128)(2,1)S(1)}, bf16[32,4096]{1,0:T(8,128)(2,1)S(1)}, u32[]{:S(2)}, u32[]{:S(2)}) collective-permute-start(bf16[32,4096]{1,0:T(8,128)(2,1)S(1)} %add_convert_fusion.6), channel_id=1, source_target_pairs={{0,2},{1,3},{2,0},{3,1},{4,6},{5,7},{6,4},{7,5},{8,10},{9,11},{10,... | collective-permute-start | bytes 786440 | tf_op jit(solution)/shard_map/ppermute | solution.py:246
  104.1 5.7 %collective-permute-start.25 = (bf16[16,4096]{1,0:T(8,128)(2,1)S(1)}, bf16[16,4096]{1,0:T(8,128)(2,1)S(1)}, u32[]{:S(2)}, u32[]{:S(2)}) collective-permute-start(bf16[16,4096]{1,0:T(8,128)(2,1)S(1)} %split.41), channel_id=1, source_target_pairs={{0,8},{8,0},{16,24},{24,16},{1,9},{9,1},{17,25},{25,17},{2,10},{10... | collective-permute-start | bytes 393224 | tf_op jit(solution)/shard_map/ppermute | solution.py:20
  (6 other events, 52.7 us)

commit v20 on v16

--- a/solution.py
+++ b/solution.py
@@ -359,7 +359,6 @@
                 whole = across_chips(block, low)
                 parts.append([whole[rows] for rows in halves])
 
-    lanes[final - 1], outs = together((lanes[final - 1], outs))
     sum_turn(0, turns - 1)
     outs[final - 1] = layer(final - 1)
     lanes, outs, sums = together((lanes, outs, sums))

time: 110 us -> 113 us (1.027)
  waiting for transfers between devices: 48.9 us -> 52.5 us
    ppermute x26, waiting for transfers between devices: 43.7 us -> 46.3 us  [from_partner(): return lax.ppermute(block, axis, route)]
  transfers between devices with their start and end apart: 34 -> 34, of which waited for: 15 -> 13; matrix products, arithmetic and copies ran while one was open for 1% -> 1% of each run, Pallas kernels for 14% -> 14%
where the time goes in v20:
time: 113 us
  waiting for transfers between devices  52.5 us (46%)
  starting transfers between devices  37.6 us (33%)
  Pallas kernels  18.3 us (16%)
  other arithmetic  2.6 us (2%)
  local copies, waits for them, and re-layouts  1.44 us (1%)
    ppermute x26, waiting for transfers between devices, from_partner(): return lax.ppermute(block, axis, route)  46.3 us
    ppermute x26, starting transfers between devices, from_partner(): return lax.ppermute(block, axis, route)  26.1 us
    pallas_call x3, Pallas kernels, expert_layer(): pl.pallas_call(functools.partial(expert_kernel, count, experts), in_specs...  11.9 us
    ppermute x8, starting transfers between devices, across_chips(): lax.ppermute(block, 'expert', [(low, low ^ 2 * far) for low in range(coun...  11.4 us
    pallas_call x2, Pallas kernels, dequantize_call(): pl.pallas_call(kernel, in_specs=[pl.BlockSpec(memory_space=pltpu.SMEM)] *...  6.46 us
    ppermute x8, waiting for transfers between devices, across_chips(): lax.ppermute(block, 'expert', [(low, low ^ 2 * far) for low in range(coun...  6.27 us
  transfers between devices with their start and end apart: 34, of which 13 were waited for; matrix products, arithmetic and copies ran while one was open for 1% of the time, Pallas kernels for 14%

profile of v20, /device:TPU:0, one launch (start us, length us, event | category | flops | bytes accessed | tf_op | source)
XLA Modules:
  0.0 112.9 jit_solution(2500597291803251947)
XLA Ops:
  2.1 4.0 %collective-permute-start.3 = (bf16[16,4224]{1,0:T(8,128)(2,1)S(1)}, bf16[16,4224]{1,0:T(8,128)(2,1)S(1)}, u32[]{:S(2)}, u32[]{:S(2)}) collective-permute-start(bf16[16,4224]{1,0:T(8,128)(2,1)S(1)} %concatenate.38), channel_id=1, source_target_pairs={{0,4},{1,5},{2,6},{3,7},{4,0},{5,1},{6,2},{7,3},{8,12},{9,13},{10,... | collective-permute-start | bytes 405512 | tf_op jit(solution)/shard_map/ppermute | solution.py:246
  6.1 1.6 %collective-permute-start.2 = (bf16[16,4224]{1,0:T(8,128)(2,1)S(1)}, bf16[16,4224]{1,0:T(8,128)(2,1)S(1)}, u32[]{:S(2)}, u32[]{:S(2)}) collective-permute-start(bf16[16,4224]{1,0:T(8,128)(2,1)S(1)} %concatenate.38), channel_id=1, source_target_pairs={{0,2},{1,3},{2,0},{3,1},{4,6},{5,7},{6,4},{7,5},{8,10},{9,11},{10,... | collective-permute-start | bytes 405512 | tf_op jit(solution)/shard_map/ppermute | solution.py:246
  7.7 1.5 %collective-permute-start = (bf16[16,4224]{1,0:T(8,128)(2,1)S(1)}, bf16[16,4224]{1,0:T(8,128)(2,1)S(1)}, u32[]{:S(2)}, u32[]{:S(2)}) collective-permute-start(bf16[16,4224]{1,0:T(8,128)(2,1)S(1)} %concatenate.38), channel_id=1, source_target_pairs={{0,8},{8,0},{16,24},{24,16},{1,9},{9,1},{17,25},{25,17},{2,10},{10... | collective-permute-start | bytes 405512 | tf_op jit(solution)/shard_map/ppermute | solution.py:20
  9.2 1.5 %collective-permute-start.1 = (bf16[16,4224]{1,0:T(8,128)(2,1)S(1)}, bf16[16,4224]{1,0:T(8,128)(2,1)S(1)}, u32[]{:S(2)}, u32[]{:S(2)}) collective-permute-start(bf16[16,4224]{1,0:T(8,128)(2,1)S(1)} %concatenate.39), channel_id=1, source_target_pairs={{0,16},{16,0},{8,24},{24,8},{1,17},{17,1},{9,25},{25,9},{2,18},{18... | collective-permute-start | bytes 405512 | tf_op jit(solution)/shard_map/ppermute | solution.py:20
  10.7 3.7 %dequantize_in.1.refs_4_ = bf16[4096,768]{1,0:T(8,128)(2,1)S(1)} custom-call(f32[3,32]{1,0:T(4,128)S(1)} %get-tuple-element.136.gate_scales, f32[3,32]{1,0:T(4,128)S(1)} %get-tuple-element.135.up_scales, bf16[4096,384]{1,0:T(8,128)(2,1)} %bitcast.17, bf16[4096,384]{1,0:T(8,128)(2,1)} %bitcast.18), custom_call_target="tpu_custom_call" | custom-call | flops 3145728 | bytes 12582912 | tf_op jit(solution)/shard_map/dequantize_in/pallas_call | solution.py:155
  14.6 1.3 %collective-permute-start.4 = (bf16[32,4224]{1,0:T(8,128)(2,1)S(1)}, bf16[32,4224]{1,0:T(8,128)(2,1)S(1)}, u32[]{:S(2)}, u32[]{:S(2)}) collective-permute-start(bf16[32,4224]{1,0:T(8,128)(2,1)S(1)} %pad_maximum_fusion.2.refs_0_), channel_id=1, source_target_pairs={{0,16},{16,0},{8,24},{24,8},{1,17},{17,1},{9,25},{25,9},{2,18},{18... | collective-permute-start | bytes 811016 | tf_op jit(solution)/shard_map/ppermute | solution.py:20
  17.3 2.4 %collective-permute-start.6 = (bf16[16,4224]{1,0:T(8,128)(2,1)S(1)}, bf16[16,4224]{1,0:T(8,128)(2,1)S(1)}, u32[]{:S(2)}, u32[]{:S(2)}) collective-permute-start(bf16[16,4224]{1,0:T(8,128)(2,1)S(1)} %concatenate.39), channel_id=1, source_target_pairs={{0,2},{1,3},{2,0},{3,1},{4,6},{5,7},{6,4},{7,5},{8,10},{9,11},{10,... | collective-permute-start | bytes 405512 | tf_op jit(solution)/shard_map/ppermute | solution.py:246
  19.7 2.8 %dequantize_down.1.refs_6_ = bf16[384,4096]{1,0:T(8,128)(2,1)S(1)} custom-call(f32[3,32]{1,0:T(4,128)S(1)} %bitcast.15, bf16[384,4096]{1,0:T(8,128)(2,1)} %bitcast.16), custom_call_target="tpu_custom_call" | custom-call | flops 1572864 | bytes 6291456 | tf_op jit(solution)/shard_map/dequantize_down/pallas_call | solution.py:155
  22.5 3.2 %collective-permute-done.7 = bf16[16,4224]{1,0:T(8,128)(2,1)S(1)} collective-permute-done((bf16[16,4224]{1,0:T(8,128)(2,1)S(1)}, bf16[16,4224]{1,0:T(8,128)(2,1)S(1)}, u32[]{:S(2)}, u32[]{:S(2)}) %collective-permute-start.7) | collective-permute-done | bytes 135200 | tf_op jit(solution)/shard_map/ppermute | solution.py:246
  26.7 1.4 %collective-permute-start.8 = (bf16[32,4224]{1,0:T(8,128)(2,1)S(1)}, bf16[32,4224]{1,0:T(8,128)(2,1)S(1)}, u32[]{:S(2)}, u32[]{:S(2)}) collective-permute-start(bf16[32,4224]{1,0:T(8,128)(2,1)S(1)} %constant_dynamic-update-slice_fusion), channel_id=1, source_target_pairs={{0,8},{8,0},{16,24},{24,16},{1,9},{9,1},{17,25},{25,17},{2,10},{10... | collective-permute-start | bytes 811016 | tf_op jit(solution)/shard_map/ppermute | solution.py:20
  28.1 6.6 %collective-permute-done.9 = bf16[32,4224]{1,0:T(8,128)(2,1)S(1)} collective-permute-done((bf16[32,4224]{1,0:T(8,128)(2,1)S(1)}, bf16[32,4224]{1,0:T(8,128)(2,1)S(1)}, u32[]{:S(2)}, u32[]{:S(2)}) %collective-permute-start.9) | collective-permute-done | bytes 270368 | tf_op jit(solution)/shard_map/ppermute | solution.py:20
  35.5 1.3 %collective-permute-start.17 = (bf16[16,4224]{1,0:T(8,128)(2,1)S(1)}, bf16[16,4224]{1,0:T(8,128)(2,1)S(1)}, u32[]{:S(2)}, u32[]{:S(2)}) collective-permute-start(bf16[16,4224]{1,0:T(8,128)(2,1)S(1)} %get-tuple-element.125), channel_id=1, source_target_pairs={{0,16},{16,0},{8,24},{24,8},{1,17},{17,1},{9,25},{25,9},{2,18},{18... | collective-permute-start | bytes 405512 | tf_op jit(solution)/shard_map/ppermute | solution.py:20
  36.8 1.4 %collective-permute-start.15 = (bf16[16,4224]{1,0:T(8,128)(2,1)S(1)}, bf16[16,4224]{1,0:T(8,128)(2,1)S(1)}, u32[]{:S(2)}, u32[]{:S(2)}) collective-permute-start(bf16[16,4224]{1,0:T(8,128)(2,1)S(1)} %get-tuple-element.126), channel_id=1, source_target_pairs={{0,8},{8,0},{16,24},{24,16},{1,9},{9,1},{17,25},{25,17},{2,10},{10... | collective-permute-start | bytes 405512 | tf_op jit(solution)/shard_map/ppermute | solution.py:20
  39.6 3.1 %expert_layer.3 = (bf16[32,4096]{1,0:T(8,128)(2,1)S(1)}, bf16[32,4096]{1,0:T(8,128)(2,1)S(1)}, bf16[32,4096]{1,0:T(8,128)(2,1)S(1)}, bf16[32,4096]{1,0:T(8,128)(2,1)S(1)}) custom-call(s32[1]{0:T(128)} %bitcast.own_expert, bf16[32,4224]{1,0:T(8,128)(2,1)S(1)} %pad_maximum_fusion.2.refs_0_, bf16[32,4224]{1,0:T(8,128)(2,1)S(1)} %collective-permute-done.4.refs_1_, ...), custom_call_target="tpu_custom_call" | custom-call | flops 2415919104 | bytes 20971520 | tf_op jit(solution)/shard_map/expert_layer/pallas_call | solution.py:225
  42.7 1.3 %collective-permute-start.19 = (bf16[32,4096]{1,0:T(8,128)(2,1)S(1)}, bf16[32,4096]{1,0:T(8,128)(2,1)S(1)}, u32[]{:S(2)}, u32[]{:S(2)}) collective-permute-start(bf16[32,4096]{1,0:T(8,128)(2,1)S(1)} %get-tuple-element.92), channel_id=1, source_target_pairs={{0,16},{16,0},{8,24},{24,8},{1,17},{17,1},{9,25},{25,9},{2,18},{18... | collective-permute-start | bytes 786440 | tf_op jit(solution)/shard_map/ppermute | solution.py:20
  44.0 1.4 %collective-permute-start.20 = (bf16[32,4096]{1,0:T(8,128)(2,1)S(1)}, bf16[32,4096]{1,0:T(8,128)(2,1)S(1)}, u32[]{:S(2)}, u32[]{:S(2)}) collective-permute-start(bf16[32,4096]{1,0:T(8,128)(2,1)S(1)} %get-tuple-element.94), channel_id=1, source_target_pairs={{0,8},{8,0},{16,24},{24,16},{1,9},{9,1},{17,25},{25,17},{2,10},{10... | collective-permute-start | bytes 786440 | tf_op jit(solution)/shard_map/ppermute | solution.py:20
  46.3 12.7 %collective-permute-done.19 = bf16[32,4096]{1,0:T(8,128)(2,1)S(1)} collective-permute-done((bf16[32,4096]{1,0:T(8,128)(2,1)S(1)}, bf16[32,4096]{1,0:T(8,128)(2,1)S(1)}, u32[]{:S(2)}, u32[]{:S(2)}) %collective-permute-start.19) | collective-permute-done | bytes 262176 | tf_op jit(solution)/shard_map/ppermute | solution.py:20
  59.0 1.6 %collective-permute-start.18 = (bf16[32,4224]{1,0:T(8,128)(2,1)S(1)}, bf16[32,4224]{1,0:T(8,128)(2,1)S(1)}, u32[]{:S(2)}, u32[]{:S(2)}) collective-permute-start(bf16[32,4224]{1,0:T(8,128)(2,1)S(1)} %pad_maximum_fusion.5.refs_2_), channel_id=1, source_target_pairs={{0,8},{8,0},{16,24},{24,16},{1,9},{9,1},{17,25},{25,17},{2,10},{10... | collective-permute-start | bytes 811016 | tf_op jit(solution)/shard_map/ppermute | solution.py:20
  60.8 5.7 %expert_layer.4 = (bf16[64,4096]{1,0:T(8,128)(2,1)S(1)}, bf16[64,4096]{1,0:T(8,128)(2,1)S(1)}, bf16[64,4096]{1,0:T(8,128)(2,1)S(1)}, bf16[64,4096]{1,0:T(8,128)(2,1)S(1)}) custom-call(s32[1]{0:T(128)} %bitcast.own_expert, bf16[64,4224]{1,0:T(8,128)(2,1)S(1)} %pad_maximum_fusion.refs_0_, bf16[64,4224]{1,0:T(8,128)(2,1)S(1)} %collective-permute-done.13.refs_1_, ...), custom_call_target="tpu_custom_call" | custom-call | flops 4831838208 | bytes 23068672 | tf_op jit(solution)/shard_map/expert_layer/pallas_call | solution.py:225
  66.6 3.1 %expert_layer.5 = (bf16[32,4096]{1,0:T(8,128)(2,1)S(1)}, bf16[32,4096]{1,0:T(8,128)(2,1)S(1)}, bf16[32,4096]{1,0:T(8,128)(2,1)S(1)}, bf16[32,4096]{1,0:T(8,128)(2,1)S(1)}) custom-call(s32[1]{0:T(128)} %bitcast.own_expert, bf16[32,4224]{1,0:T(8,128)(2,1)S(1)} %pad_maximum_fusion.4.refs_0_, bf16[32,4224]{1,0:T(8,128)(2,1)S(1)} %collective-permute-done.16.refs_1_, ...), custom_call_target="tpu_custom_call" | custom-call | flops 2415919104 | bytes 20971520 | tf_op jit(solution)/shard_map/expert_layer/pallas_call | solution.py:225
  72.3 1.5 %collective-permute-start.22 = (bf16[64,4096]{1,0:T(8,128)(2,1)S(1)}, bf16[64,4096]{1,0:T(8,128)(2,1)S(1)}, u32[]{:S(2)}, u32[]{:S(2)}) collective-permute-start(bf16[64,4096]{1,0:T(8,128)(2,1)S(1)} %get-tuple-element.104), channel_id=1, source_target_pairs={{0,8},{8,0},{16,24},{24,16},{1,9},{9,1},{17,25},{25,17},{2,10},{10... | collective-permute-start | bytes 1572872 | tf_op jit(solution)/shard_map/ppermute | solution.py:20
  73.8 5.2 %collective-permute-done.26 = bf16[32,4096]{1,0:T(8,128)(2,1)S(1)} collective-permute-done((bf16[32,4096]{1,0:T(8,128)(2,1)S(1)}, bf16[32,4096]{1,0:T(8,128)(2,1)S(1)}, u32[]{:S(2)}, u32[]{:S(2)}) %collective-permute-start.26) | collective-permute-done | bytes 262176 | tf_op jit(solution)/shard_map/ppermute | solution.py:20
  81.1 8.5 %collective-permute-done.27 = bf16[16,4096]{1,0:T(8,128)(2,1)S(1)} collective-permute-done((bf16[16,4096]{1,0:T(8,128)(2,1)S(1)}, bf16[16,4096]{1,0:T(8,128)(2,1)S(1)}, u32[]{:S(2)}, u32[]{:S(2)}) %collective-permute-start.27) | collective-permute-done | bytes 131104 | tf_op jit(solution)/shard_map/ppermute | solution.py:20
  90.1 1.5 %collective-permute-start.24 = (bf16[32,4096]{1,0:T(8,128)(2,1)S(1)}, bf16[32,4096]{1,0:T(8,128)(2,1)S(1)}, u32[]{:S(2)}, u32[]{:S(2)}) collective-permute-start(bf16[32,4096]{1,0:T(8,128)(2,1)S(1)} %split.39), channel_id=1, source_target_pairs={{0,16},{16,0},{8,24},{24,8},{1,17},{17,1},{9,25},{25,9},{2,18},{18... | collective-permute-start | bytes 786440 | tf_op jit(solution)/shard_map/ppermute | solution.py:20
  91.5 1.6 %collective-permute-start.30 = (bf16[32,4096]{1,0:T(8,128)(2,1)S(1)}, bf16[32,4096]{1,0:T(8,128)(2,1)S(1)}, u32[]{:S(2)}, u32[]{:S(2)}) collective-permute-start(bf16[32,4096]{1,0:T(8,128)(2,1)S(1)} %pad_maximum_fusion.6), channel_id=1, source_target_pairs={{0,2},{1,3},{2,0},{3,1},{4,6},{5,7},{6,4},{7,5},{8,10},{9,11},{10,... | collective-permute-start | bytes 786440 | tf_op jit(solution)/shard_map/ppermute | solution.py:246
  93.8 2.7 %collective-permute-done.24 = bf16[32,4096]{1,0:T(8,128)(2,1)S(1)} collective-permute-done((bf16[32,4096]{1,0:T(8,128)(2,1)S(1)}, bf16[32,4096]{1,0:T(8,128)(2,1)S(1)}, u32[]{:S(2)}, u32[]{:S(2)}) %collective-permute-start.24) | collective-permute-done | bytes 262176 | tf_op jit(solution)/shard_map/ppermute | solution.py:20
  96.6 4.4 %collective-permute-done.23 = bf16[32,4096]{1,0:T(8,128)(2,1)S(1)} collective-permute-done((bf16[32,4096]{1,0:T(8,128)(2,1)S(1)}, bf16[32,4096]{1,0:T(8,128)(2,1)S(1)}, u32[]{:S(2)}, u32[]{:S(2)}) %collective-permute-start.23) | collective-permute-done | bytes 262176 | tf_op jit(solution)/shard_map/ppermute | solution.py:20
  101.0 1.6 %collective-permute-done.30 = bf16[32,4096]{1,0:T(8,128)(2,1)S(1)} collective-permute-done((bf16[32,4096]{1,0:T(8,128)(2,1)S(1)}, bf16[32,4096]{1,0:T(8,128)(2,1)S(1)}, u32[]{:S(2)}, u32[]{:S(2)}) %collective-permute-start.30) | collective-permute-done | bytes 262176 | tf_op jit(solution)/shard_map/ppermute | solution.py:246
  103.6 1.9 %collective-permute-start.33 = (bf16[16,4096]{1,0:T(8,128)(2,1)S(1)}, bf16[16,4096]{1,0:T(8,128)(2,1)S(1)}, u32[]{:S(2)}, u32[]{:S(2)}) collective-permute-start(bf16[16,4096]{1,0:T(8,128)(2,1)S(1)} %split.47), channel_id=1, source_target_pairs={{0,16},{16,0},{8,24},{24,8},{1,17},{17,1},{9,25},{25,9},{2,18},{18... | collective-permute-start | bytes 393224 | tf_op jit(solution)/shard_map/ppermute | solution.py:20
  105.5 3.2 %collective-permute-done.33 = bf16[16,4096]{1,0:T(8,128)(2,1)S(1)} collective-permute-done((bf16[16,4096]{1,0:T(8,128)(2,1)S(1)}, bf16[16,4096]{1,0:T(8,128)(2,1)S(1)}, u32[]{:S(2)}, u32[]{:S(2)}) %collective-permute-start.33) | collective-permute-done | bytes 131104 | tf_op jit(solution)/shard_map/ppermute | solution.py:20
  108.7 1.8 %collective-permute-done.25 = bf16[16,4096]{1,0:T(8,128)(2,1)S(1)} collective-permute-done((bf16[16,4096]{1,0:T(8,128)(2,1)S(1)}, bf16[16,4096]{1,0:T(8,128)(2,1)S(1)}, u32[]{:S(2)}, u32[]{:S(2)}) %collective-permute-start.25) | collective-permute-done | bytes 131104 | tf_op jit(solution)/shard_map/ppermute | solution.py:20
  110.5 1.5 %collective-permute-done.31 = bf16[32,4096]{1,0:T(8,128)(2,1)S(1)} collective-permute-done((bf16[32,4096]{1,0:T(8,128)(2,1)S(1)}, bf16[32,4096]{1,0:T(8,128)(2,1)S(1)}, u32[]{:S(2)}, u32[]{:S(2)}) %collective-permute-start.31) | collective-permute-done | bytes 262176 | tf_op jit(solution)/shard_map/ppermute | solution.py:246
  (90 shorter events, 15.5 us)
Async XLA Ops:
  2.1 12.4 %collective-permute-start.3 = (bf16[16,4224]{1,0:T(8,128)(2,1)S(1)}, bf16[16,4224]{1,0:T(8,128)(2,1)S(1)}, u32[]{:S(2)}, u32[]{:S(2)}) collective-permute-start(bf16[16,4224]{1,0:T(8,128)(2,1)S(1)} %concatenate.38), channel_id=1, source_target_pairs={{0,4},{1,5},{2,6},{3,7},{4,0},{5,1},{6,2},{7,3},{8,12},{9,13},{10,... | collective-permute-start | bytes 405512 | tf_op jit(solution)/shard_map/ppermute | solution.py:246
  6.1 8.4 %collective-permute-start.2 = (bf16[16,4224]{1,0:T(8,128)(2,1)S(1)}, bf16[16,4224]{1,0:T(8,128)(2,1)S(1)}, u32[]{:S(2)}, u32[]{:S(2)}) collective-permute-start(bf16[16,4224]{1,0:T(8,128)(2,1)S(1)} %concatenate.38), channel_id=1, source_target_pairs={{0,2},{1,3},{2,0},{3,1},{4,6},{5,7},{6,4},{7,5},{8,10},{9,11},{10,... | collective-permute-start | bytes 405512 | tf_op jit(solution)/shard_map/ppermute | solution.py:246
  7.7 6.8 %collective-permute-start = (bf16[16,4224]{1,0:T(8,128)(2,1)S(1)}, bf16[16,4224]{1,0:T(8,128)(2,1)S(1)}, u32[]{:S(2)}, u32[]{:S(2)}) collective-permute-start(bf16[16,4224]{1,0:T(8,128)(2,1)S(1)} %concatenate.38), channel_id=1, source_target_pairs={{0,8},{8,0},{16,24},{24,16},{1,9},{9,1},{17,25},{25,17},{2,10},{10... | collective-permute-start | bytes 405512 | tf_op jit(solution)/shard_map/ppermute | solution.py:20
  9.2 5.3 %collective-permute-start.1 = (bf16[16,4224]{1,0:T(8,128)(2,1)S(1)}, bf16[16,4224]{1,0:T(8,128)(2,1)S(1)}, u32[]{:S(2)}, u32[]{:S(2)}) collective-permute-start(bf16[16,4224]{1,0:T(8,128)(2,1)S(1)} %concatenate.39), channel_id=1, source_target_pairs={{0,16},{16,0},{8,24},{24,8},{1,17},{17,1},{9,25},{25,9},{2,18},{18... | collective-permute-start | bytes 405512 | tf_op jit(solution)/shard_map/ppermute | solution.py:20
  14.5 20.9 %collective-permute-start.11 = (bf16[4096,768]{1,0:T(8,128)(2,1)S(1)}, bf16[4096,768]{1,0:T(8,128)(2,1)S(1)}, u32[]{:S(2)}, u32[]{:S(2)}) collective-permute-start(bf16[4096,768]{1,0:T(8,128)(2,1)S(1)} %dequantize_in.1.refs_4_), channel_id=1, source_target_pairs={{0,1},{1,0},{2,3},{3,2},{4,5},{5,4},{6,7},{7,6},{8,9},{9,8},{10,11... | collective-permute-start | bytes 18874376 | tf_op jit(solution)/shard_map/ppermute | solution.py:20
  14.6 11.0 %collective-permute-start.4 = (bf16[32,4224]{1,0:T(8,128)(2,1)S(1)}, bf16[32,4224]{1,0:T(8,128)(2,1)S(1)}, u32[]{:S(2)}, u32[]{:S(2)}) collective-permute-start(bf16[32,4224]{1,0:T(8,128)(2,1)S(1)} %pad_maximum_fusion.2.refs_0_), channel_id=1, source_target_pairs={{0,16},{16,0},{8,24},{24,8},{1,17},{17,1},{9,25},{25,9},{2,18},{18... | collective-permute-start | bytes 811016 | tf_op jit(solution)/shard_map/ppermute | solution.py:20
  15.9 9.7 %collective-permute-start.5 = (bf16[32,4224]{1,0:T(8,128)(2,1)S(1)}, bf16[32,4224]{1,0:T(8,128)(2,1)S(1)}, u32[]{:S(2)}, u32[]{:S(2)}) collective-permute-start(bf16[32,4224]{1,0:T(8,128)(2,1)S(1)} %pad_maximum_fusion.3.refs_2_), channel_id=1, source_target_pairs={{0,8},{8,0},{16,24},{24,16},{1,9},{9,1},{17,25},{25,17},{2,10},{10... | collective-permute-start | bytes 811016 | tf_op jit(solution)/shard_map/ppermute | solution.py:20
  16.5 9.2 %collective-permute-start.7 = (bf16[16,4224]{1,0:T(8,128)(2,1)S(1)}, bf16[16,4224]{1,0:T(8,128)(2,1)S(1)}, u32[]{:S(2)}, u32[]{:S(2)}) collective-permute-start(bf16[16,4224]{1,0:T(8,128)(2,1)S(1)} %concatenate.39), channel_id=1, source_target_pairs={{0,4},{1,5},{2,6},{3,7},{4,0},{5,1},{6,2},{7,3},{8,12},{9,13},{10,... | collective-permute-start | bytes 405512 | tf_op jit(solution)/shard_map/ppermute | solution.py:246
  17.3 8.4 %collective-permute-start.6 = (bf16[16,4224]{1,0:T(8,128)(2,1)S(1)}, bf16[16,4224]{1,0:T(8,128)(2,1)S(1)}, u32[]{:S(2)}, u32[]{:S(2)}) collective-permute-start(bf16[16,4224]{1,0:T(8,128)(2,1)S(1)} %concatenate.39), channel_id=1, source_target_pairs={{0,2},{1,3},{2,0},{3,1},{4,6},{5,7},{6,4},{7,5},{8,10},{9,11},{10,... | collective-permute-start | bytes 405512 | tf_op jit(solution)/shard_map/ppermute | solution.py:246
  25.6 9.8 %collective-permute-start.12 = (bf16[384,4096]{1,0:T(8,128)(2,1)S(1)}, bf16[384,4096]{1,0:T(8,128)(2,1)S(1)}, u32[]{:S(2)}, u32[]{:S(2)}) collective-permute-start(bf16[384,4096]{1,0:T(8,128)(2,1)S(1)} %dequantize_down.1.refs_6_), channel_id=1, source_target_pairs={{0,1},{1,0},{2,3},{3,2},{4,5},{5,4},{6,7},{7,6},{8,9},{9,8},{10,11... | collective-permute-start | bytes 9437192 | tf_op jit(solution)/shard_map/ppermute | solution.py:20
  25.8 9.7 %collective-permute-start.10 = (bf16[32,4224]{1,0:T(8,128)(2,1)S(1)}, bf16[32,4224]{1,0:T(8,128)(2,1)S(1)}, u32[]{:S(2)}, u32[]{:S(2)}) collective-permute-start(bf16[32,4224]{1,0:T(8,128)(2,1)S(1)} %constant_dynamic-update-slice_fusion.2), channel_id=1, source_target_pairs={{0,2},{1,3},{2,0},{3,1},{4,6},{5,7},{6,4},{7,5},{8,10},{9,11},{10,... | collective-permute-start | bytes 811016 | tf_op jit(solution)/shard_map/ppermute | solution.py:246
  25.8 8.9 %collective-permute-start.9 = (bf16[32,4224]{1,0:T(8,128)(2,1)S(1)}, bf16[32,4224]{1,0:T(8,128)(2,1)S(1)}, u32[]{:S(2)}, u32[]{:S(2)}) collective-permute-start(bf16[32,4224]{1,0:T(8,128)(2,1)S(1)} %constant_dynamic-update-slice_fusion.2), channel_id=1, source_target_pairs={{0,16},{16,0},{8,24},{24,8},{1,17},{17,1},{9,25},{25,9},{2,18},{18... | collective-permute-start | bytes 811016 | tf_op jit(solution)/shard_map/ppermute | solution.py:20
  26.7 8.7 %collective-permute-start.8 = (bf16[32,4224]{1,0:T(8,128)(2,1)S(1)}, bf16[32,4224]{1,0:T(8,128)(2,1)S(1)}, u32[]{:S(2)}, u32[]{:S(2)}) collective-permute-start(bf16[32,4224]{1,0:T(8,128)(2,1)S(1)} %constant_dynamic-update-slice_fusion), channel_id=1, source_target_pairs={{0,8},{8,0},{16,24},{24,16},{1,9},{9,1},{17,25},{25,17},{2,10},{10... | collective-permute-start | bytes 811016 | tf_op jit(solution)/shard_map/ppermute | solution.py:20
  35.5 9.9 %collective-permute-start.17 = (bf16[16,4224]{1,0:T(8,128)(2,1)S(1)}, bf16[16,4224]{1,0:T(8,128)(2,1)S(1)}, u32[]{:S(2)}, u32[]{:S(2)}) collective-permute-start(bf16[16,4224]{1,0:T(8,128)(2,1)S(1)} %get-tuple-element.125), channel_id=1, source_target_pairs={{0,16},{16,0},{8,24},{24,8},{1,17},{17,1},{9,25},{25,9},{2,18},{18... | collective-permute-start | bytes 405512 | tf_op jit(solution)/shard_map/ppermute | solution.py:20
  36.8 7.2 %collective-permute-start.15 = (bf16[16,4224]{1,0:T(8,128)(2,1)S(1)}, bf16[16,4224]{1,0:T(8,128)(2,1)S(1)}, u32[]{:S(2)}, u32[]{:S(2)}) collective-permute-start(bf16[16,4224]{1,0:T(8,128)(2,1)S(1)} %get-tuple-element.126), channel_id=1, source_target_pairs={{0,8},{8,0},{16,24},{24,16},{1,9},{9,1},{17,25},{25,17},{2,10},{10... | collective-permute-start | bytes 405512 | tf_op jit(solution)/shard_map/ppermute | solution.py:20
  38.2 22.6 %collective-permute-start.13 = (bf16[64,4224]{1,0:T(8,128)(2,1)S(1)}, bf16[64,4224]{1,0:T(8,128)(2,1)S(1)}, u32[]{:S(2)}, u32[]{:S(2)}) collective-permute-start(bf16[64,4224]{1,0:T(8,128)(2,1)S(1)} %pad_maximum_fusion.refs_0_), channel_id=1, source_target_pairs={{0,16},{16,0},{8,24},{24,8},{1,17},{17,1},{9,25},{25,9},{2,18},{18... | collective-permute-start | bytes 1622024 | tf_op jit(solution)/shard_map/ppermute | solution.py:20
  38.9 21.9 %collective-permute-start.14 = (bf16[64,4224]{1,0:T(8,128)(2,1)S(1)}, bf16[64,4224]{1,0:T(8,128)(2,1)S(1)}, u32[]{:S(2)}, u32[]{:S(2)}) collective-permute-start(bf16[64,4224]{1,0:T(8,128)(2,1)S(1)} %pad_maximum_fusion.1.refs_2_), channel_id=1, source_target_pairs={{0,8},{8,0},{16,24},{24,16},{1,9},{9,1},{17,25},{25,17},{2,10},{10... | collective-permute-start | bytes 1622024 | tf_op jit(solution)/shard_map/ppermute | solution.py:20
  42.7 16.4 %collective-permute-start.19 = (bf16[32,4096]{1,0:T(8,128)(2,1)S(1)}, bf16[32,4096]{1,0:T(8,128)(2,1)S(1)}, u32[]{:S(2)}, u32[]{:S(2)}) collective-permute-start(bf16[32,4096]{1,0:T(8,128)(2,1)S(1)} %get-tuple-element.92), channel_id=1, source_target_pairs={{0,16},{16,0},{8,24},{24,8},{1,17},{17,1},{9,25},{25,9},{2,18},{18... | collective-permute-start | bytes 786440 | tf_op jit(solution)/shard_map/ppermute | solution.py:20
  44.0 16.7 %collective-permute-start.20 = (bf16[32,4096]{1,0:T(8,128)(2,1)S(1)}, bf16[32,4096]{1,0:T(8,128)(2,1)S(1)}, u32[]{:S(2)}, u32[]{:S(2)}) collective-permute-start(bf16[32,4096]{1,0:T(8,128)(2,1)S(1)} %get-tuple-element.94), channel_id=1, source_target_pairs={{0,8},{8,0},{16,24},{24,16},{1,9},{9,1},{17,25},{25,17},{2,10},{10... | collective-permute-start | bytes 786440 | tf_op jit(solution)/shard_map/ppermute | solution.py:20
  45.4 21.1 %collective-permute-start.16 = (bf16[32,4224]{1,0:T(8,128)(2,1)S(1)}, bf16[32,4224]{1,0:T(8,128)(2,1)S(1)}, u32[]{:S(2)}, u32[]{:S(2)}) collective-permute-start(bf16[32,4224]{1,0:T(8,128)(2,1)S(1)} %pad_maximum_fusion.4.refs_0_), channel_id=1, source_target_pairs={{0,16},{16,0},{8,24},{24,8},{1,17},{17,1},{9,25},{25,9},{2,18},{18... | collective-permute-start | bytes 811016 | tf_op jit(solution)/shard_map/ppermute | solution.py:20
  59.0 7.5 %collective-permute-start.18 = (bf16[32,4224]{1,0:T(8,128)(2,1)S(1)}, bf16[32,4224]{1,0:T(8,128)(2,1)S(1)}, u32[]{:S(2)}, u32[]{:S(2)}) collective-permute-start(bf16[32,4224]{1,0:T(8,128)(2,1)S(1)} %pad_maximum_fusion.5.refs_2_), channel_id=1, source_target_pairs={{0,8},{8,0},{16,24},{24,16},{1,9},{9,1},{17,25},{25,17},{2,10},{10... | collective-permute-start | bytes 811016 | tf_op jit(solution)/shard_map/ppermute | solution.py:20
  69.7 9.3 %collective-permute-start.26 = (bf16[32,4096]{1,0:T(8,128)(2,1)S(1)}, bf16[32,4096]{1,0:T(8,128)(2,1)S(1)}, u32[]{:S(2)}, u32[]{:S(2)}) collective-permute-start(bf16[32,4096]{1,0:T(8,128)(2,1)S(1)} %get-tuple-element.110), channel_id=1, source_target_pairs={{0,16},{16,0},{8,24},{24,8},{1,17},{17,1},{9,25},{25,9},{2,18},{18... | collective-permute-start | bytes 786440 | tf_op jit(solution)/shard_map/ppermute | solution.py:20
  71.0 9.2 %collective-permute-start.28 = (bf16[32,4096]{1,0:T(8,128)(2,1)S(1)}, bf16[32,4096]{1,0:T(8,128)(2,1)S(1)}, u32[]{:S(2)}, u32[]{:S(2)}) collective-permute-start(bf16[32,4096]{1,0:T(8,128)(2,1)S(1)} %get-tuple-element.112), channel_id=1, source_target_pairs={{0,8},{8,0},{16,24},{24,16},{1,9},{9,1},{17,25},{25,17},{2,10},{10... | collective-permute-start | bytes 786440 | tf_op jit(solution)/shard_map/ppermute | solution.py:20
  71.6 18.2 %collective-permute-start.21 = (bf16[64,4096]{1,0:T(8,128)(2,1)S(1)}, bf16[64,4096]{1,0:T(8,128)(2,1)S(1)}, u32[]{:S(2)}, u32[]{:S(2)}) collective-permute-start(bf16[64,4096]{1,0:T(8,128)(2,1)S(1)} %get-tuple-element.102), channel_id=1, source_target_pairs={{0,16},{16,0},{8,24},{24,8},{1,17},{17,1},{9,25},{25,9},{2,18},{18... | collective-permute-start | bytes 1572872 | tf_op jit(solution)/shard_map/ppermute | solution.py:20
  72.3 17.6 %collective-permute-start.22 = (bf16[64,4096]{1,0:T(8,128)(2,1)S(1)}, bf16[64,4096]{1,0:T(8,128)(2,1)S(1)}, u32[]{:S(2)}, u32[]{:S(2)}) collective-permute-start(bf16[64,4096]{1,0:T(8,128)(2,1)S(1)} %get-tuple-element.104), channel_id=1, source_target_pairs={{0,8},{8,0},{16,24},{24,16},{1,9},{9,1},{17,25},{25,17},{2,10},{10... | collective-permute-start | bytes 1572872 | tf_op jit(solution)/shard_map/ppermute | solution.py:20
  79.1 10.6 %collective-permute-start.27 = (bf16[16,4096]{1,0:T(8,128)(2,1)S(1)}, bf16[16,4096]{1,0:T(8,128)(2,1)S(1)}, u32[]{:S(2)}, u32[]{:S(2)}) collective-permute-start(bf16[16,4096]{1,0:T(8,128)(2,1)S(1)} %split.49), channel_id=1, source_target_pairs={{0,8},{8,0},{16,24},{24,16},{1,9},{9,1},{17,25},{25,17},{2,10},{10... | collective-permute-start | bytes 393224 | tf_op jit(solution)/shard_map/ppermute | solution.py:20
  80.3 9.4 %collective-permute-start.29 = (bf16[16,4096]{1,0:T(8,128)(2,1)S(1)}, bf16[16,4096]{1,0:T(8,128)(2,1)S(1)}, u32[]{:S(2)}, u32[]{:S(2)}) collective-permute-start(bf16[16,4096]{1,0:T(8,128)(2,1)S(1)} %split.51), channel_id=1, source_target_pairs={{0,16},{16,0},{8,24},{24,8},{1,17},{17,1},{9,25},{25,9},{2,18},{18... | collective-permute-start | bytes 393224 | tf_op jit(solution)/shard_map/ppermute | solution.py:20
  90.1 6.4 %collective-permute-start.24 = (bf16[32,4096]{1,0:T(8,128)(2,1)S(1)}, bf16[32,4096]{1,0:T(8,128)(2,1)S(1)}, u32[]{:S(2)}, u32[]{:S(2)}) collective-permute-start(bf16[32,4096]{1,0:T(8,128)(2,1)S(1)} %split.39), channel_id=1, source_target_pairs={{0,16},{16,0},{8,24},{24,8},{1,17},{17,1},{9,25},{25,9},{2,18},{18... | collective-permute-start | bytes 786440 | tf_op jit(solution)/shard_map/ppermute | solution.py:20
  91.5 11.1 %collective-permute-start.30 = (bf16[32,4096]{1,0:T(8,128)(2,1)S(1)}, bf16[32,4096]{1,0:T(8,128)(2,1)S(1)}, u32[]{:S(2)}, u32[]{:S(2)}) collective-permute-start(bf16[32,4096]{1,0:T(8,128)(2,1)S(1)} %pad_maximum_fusion.6), channel_id=1, source_target_pairs={{0,2},{1,3},{2,0},{3,1},{4,6},{5,7},{6,4},{7,5},{8,10},{9,11},{10,... | collective-permute-start | bytes 786440 | tf_op jit(solution)/shard_map/ppermute | solution.py:246
  93.1 7.8 %collective-permute-start.23 = (bf16[32,4096]{1,0:T(8,128)(2,1)S(1)}, bf16[32,4096]{1,0:T(8,128)(2,1)S(1)}, u32[]{:S(2)}, u32[]{:S(2)}) collective-permute-start(bf16[32,4096]{1,0:T(8,128)(2,1)S(1)} %split.37), channel_id=1, source_target_pairs={{0,8},{8,0},{16,24},{24,16},{1,9},{9,1},{17,25},{25,17},{2,10},{10... | collective-permute-start | bytes 786440 | tf_op jit(solution)/shard_map/ppermute | solution.py:20
  102.7 9.3 %collective-permute-start.31 = (bf16[32,4096]{1,0:T(8,128)(2,1)S(1)}, bf16[32,4096]{1,0:T(8,128)(2,1)S(1)}, u32[]{:S(2)}, u32[]{:S(2)}) collective-permute-start(bf16[32,4096]{1,0:T(8,128)(2,1)S(1)} %add_convert_fusion.2), channel_id=1, source_target_pairs={{0,4},{1,5},{2,6},{3,7},{4,0},{5,1},{6,2},{7,3},{8,12},{9,13},{10,... | collective-permute-start | bytes 786440 | tf_op jit(solution)/shard_map/ppermute | solution.py:246
  102.8 9.2 %collective-permute-start.32 = (bf16[32,4096]{1,0:T(8,128)(2,1)S(1)}, bf16[32,4096]{1,0:T(8,128)(2,1)S(1)}, u32[]{:S(2)}, u32[]{:S(2)}) collective-permute-start(bf16[32,4096]{1,0:T(8,128)(2,1)S(1)} %add_convert_fusion.6), channel_id=1, source_target_pairs={{0,2},{1,3},{2,0},{3,1},{4,6},{5,7},{6,4},{7,5},{8,10},{9,11},{10,... | collective-permute-start | bytes 786440 | tf_op jit(solution)/shard_map/ppermute | solution.py:246
  (6 other events, 52.1 us)

commit v21 on v16

--- a/solution.py
+++ b/solution.py
@@ -367,11 +367,13 @@
     for number in range(final, 0, -1):
         for turn in range(turns - 1 - int(number < final), -1, -1):
             sum_turn(number, turn)
+            if turn == turns - 1:
+                sums[number], outs[number - 1] = together((sums[number], outs[number - 1]))
             if turn == 0 and number > 1:
                 sum_turn(number - 1, turns - 1)
         if number > 1:
             leave(number)
-        sums, outs = together((sums, outs))
+        sums, outs, merged = together((sums, outs, merged))
     leave(1)
     for turn in range(turns - 2, -1, -1):
         sum_turn(0, turn)

time: 110 us -> 111 us (level)
  transfers between devices with their start and end apart: 34 -> 34, of which waited for: 15 -> 19; matrix products, arithmetic and copies ran while one was open for 1% -> 1% of each run, Pallas kernels for 14% -> 14%
where the time goes in v21:
time: 111 us; the launch traced here: 110 us
  waiting for transfers between devices  49.5 us (45%)
  starting transfers between devices  38.1 us (34%)
  Pallas kernels  18.3 us (16%)
  other arithmetic  2.58 us (2%)
  local copies, waits for them, and re-layouts  1.44 us (1%)
    ppermute x26, waiting for transfers between devices, from_partner(): return lax.ppermute(block, axis, route)  43.3 us
    ppermute x26, starting transfers between devices, from_partner(): return lax.ppermute(block, axis, route)  26.5 us
    pallas_call x3, Pallas kernels, expert_layer(): pl.pallas_call(functools.partial(expert_kernel, count, experts), in_specs...  11.8 us
    ppermute x8, starting transfers between devices, across_chips(): lax.ppermute(block, 'expert', [(low, low ^ 2 * far) for low in range(coun...  11.7 us
    pallas_call x2, Pallas kernels, dequantize_call(): pl.pallas_call(kernel, in_specs=[pl.BlockSpec(memory_space=pltpu.SMEM)] *...  6.46 us
    ppermute x8, waiting for transfers between devices, across_chips(): lax.ppermute(block, 'expert', [(low, low ^ 2 * far) for low in range(coun...  6.27 us
  transfers between devices with their start and end apart: 34, of which 19 were waited for; matrix products, arithmetic and copies ran while one was open for 1% of the time, Pallas kernels for 14%

profile of v21, /device:TPU:0, one launch (start us, length us, event | category | flops | bytes accessed | tf_op | source)
XLA Modules:
  0.0 110.4 jit_solution(12155287606265818412)
XLA Ops:
  2.1 4.0 %collective-permute-start.3 = (bf16[16,4224]{1,0:T(8,128)(2,1)S(1)}, bf16[16,4224]{1,0:T(8,128)(2,1)S(1)}, u32[]{:S(2)}, u32[]{:S(2)}) collective-permute-start(bf16[16,4224]{1,0:T(8,128)(2,1)S(1)} %concatenate.38), channel_id=1, source_target_pairs={{0,4},{1,5},{2,6},{3,7},{4,0},{5,1},{6,2},{7,3},{8,12},{9,13},{10,... | collective-permute-start | bytes 405512 | tf_op jit(solution)/shard_map/ppermute | solution.py:246
  6.1 1.6 %collective-permute-start.2 = (bf16[16,4224]{1,0:T(8,128)(2,1)S(1)}, bf16[16,4224]{1,0:T(8,128)(2,1)S(1)}, u32[]{:S(2)}, u32[]{:S(2)}) collective-permute-start(bf16[16,4224]{1,0:T(8,128)(2,1)S(1)} %concatenate.38), channel_id=1, source_target_pairs={{0,2},{1,3},{2,0},{3,1},{4,6},{5,7},{6,4},{7,5},{8,10},{9,11},{10,... | collective-permute-start | bytes 405512 | tf_op jit(solution)/shard_map/ppermute | solution.py:246
  7.7 1.5 %collective-permute-start = (bf16[16,4224]{1,0:T(8,128)(2,1)S(1)}, bf16[16,4224]{1,0:T(8,128)(2,1)S(1)}, u32[]{:S(2)}, u32[]{:S(2)}) collective-permute-start(bf16[16,4224]{1,0:T(8,128)(2,1)S(1)} %concatenate.38), channel_id=1, source_target_pairs={{0,8},{8,0},{16,24},{24,16},{1,9},{9,1},{17,25},{25,17},{2,10},{10... | collective-permute-start | bytes 405512 | tf_op jit(solution)/shard_map/ppermute | solution.py:20
  9.2 1.5 %collective-permute-start.1 = (bf16[16,4224]{1,0:T(8,128)(2,1)S(1)}, bf16[16,4224]{1,0:T(8,128)(2,1)S(1)}, u32[]{:S(2)}, u32[]{:S(2)}) collective-permute-start(bf16[16,4224]{1,0:T(8,128)(2,1)S(1)} %concatenate.39), channel_id=1, source_target_pairs={{0,16},{16,0},{8,24},{24,8},{1,17},{17,1},{9,25},{25,9},{2,18},{18... | collective-permute-start | bytes 405512 | tf_op jit(solution)/shard_map/ppermute | solution.py:20
  10.7 3.7 %dequantize_in.1.refs_4_ = bf16[4096,768]{1,0:T(8,128)(2,1)S(1)} custom-call(f32[3,32]{1,0:T(4,128)S(1)} %get-tuple-element.168.gate_scales, f32[3,32]{1,0:T(4,128)S(1)} %get-tuple-element.167.up_scales, bf16[4096,384]{1,0:T(8,128)(2,1)} %bitcast.17, bf16[4096,384]{1,0:T(8,128)(2,1)} %bitcast.18), custom_call_target="tpu_custom_call" | custom-call | flops 3145728 | bytes 12582912 | tf_op jit(solution)/shard_map/dequantize_in/pallas_call | solution.py:155
  14.6 1.3 %collective-permute-start.4 = (bf16[32,4224]{1,0:T(8,128)(2,1)S(1)}, bf16[32,4224]{1,0:T(8,128)(2,1)S(1)}, u32[]{:S(2)}, u32[]{:S(2)}) collective-permute-start(bf16[32,4224]{1,0:T(8,128)(2,1)S(1)} %pad_maximum_fusion.2.refs_0_), channel_id=1, source_target_pairs={{0,16},{16,0},{8,24},{24,8},{1,17},{17,1},{9,25},{25,9},{2,18},{18... | collective-permute-start | bytes 811016 | tf_op jit(solution)/shard_map/ppermute | solution.py:20
  17.3 2.4 %collective-permute-start.6 = (bf16[16,4224]{1,0:T(8,128)(2,1)S(1)}, bf16[16,4224]{1,0:T(8,128)(2,1)S(1)}, u32[]{:S(2)}, u32[]{:S(2)}) collective-permute-start(bf16[16,4224]{1,0:T(8,128)(2,1)S(1)} %concatenate.39), channel_id=1, source_target_pairs={{0,2},{1,3},{2,0},{3,1},{4,6},{5,7},{6,4},{7,5},{8,10},{9,11},{10,... | collective-permute-start | bytes 405512 | tf_op jit(solution)/shard_map/ppermute | solution.py:246
  19.7 2.8 %dequantize_down.1.refs_6_ = bf16[384,4096]{1,0:T(8,128)(2,1)S(1)} custom-call(f32[3,32]{1,0:T(4,128)S(1)} %bitcast.15, bf16[384,4096]{1,0:T(8,128)(2,1)} %bitcast.16), custom_call_target="tpu_custom_call" | custom-call | flops 1572864 | bytes 6291456 | tf_op jit(solution)/shard_map/dequantize_down/pallas_call | solution.py:155
  22.5 3.2 %collective-permute-done.7 = bf16[16,4224]{1,0:T(8,128)(2,1)S(1)} collective-permute-done((bf16[16,4224]{1,0:T(8,128)(2,1)S(1)}, bf16[16,4224]{1,0:T(8,128)(2,1)S(1)}, u32[]{:S(2)}, u32[]{:S(2)}) %collective-permute-start.7) | collective-permute-done | bytes 135200 | tf_op jit(solution)/shard_map/ppermute | solution.py:246
  26.7 1.4 %collective-permute-start.8 = (bf16[32,4224]{1,0:T(8,128)(2,1)S(1)}, bf16[32,4224]{1,0:T(8,128)(2,1)S(1)}, u32[]{:S(2)}, u32[]{:S(2)}) collective-permute-start(bf16[32,4224]{1,0:T(8,128)(2,1)S(1)} %constant_dynamic-update-slice_fusion), channel_id=1, source_target_pairs={{0,8},{8,0},{16,24},{24,16},{1,9},{9,1},{17,25},{25,17},{2,10},{10... | collective-permute-start | bytes 811016 | tf_op jit(solution)/shard_map/ppermute | solution.py:20
  28.1 6.6 %collective-permute-done.9 = bf16[32,4224]{1,0:T(8,128)(2,1)S(1)} collective-permute-done((bf16[32,4224]{1,0:T(8,128)(2,1)S(1)}, bf16[32,4224]{1,0:T(8,128)(2,1)S(1)}, u32[]{:S(2)}, u32[]{:S(2)}) %collective-permute-start.9) | collective-permute-done | bytes 270368 | tf_op jit(solution)/shard_map/ppermute | solution.py:20
  35.5 1.3 %collective-permute-start.17 = (bf16[16,4224]{1,0:T(8,128)(2,1)S(1)}, bf16[16,4224]{1,0:T(8,128)(2,1)S(1)}, u32[]{:S(2)}, u32[]{:S(2)}) collective-permute-start(bf16[16,4224]{1,0:T(8,128)(2,1)S(1)} %get-tuple-element.157), channel_id=1, source_target_pairs={{0,16},{16,0},{8,24},{24,8},{1,17},{17,1},{9,25},{25,9},{2,18},{18... | collective-permute-start | bytes 405512 | tf_op jit(solution)/shard_map/ppermute | solution.py:20
  36.8 1.4 %collective-permute-start.15 = (bf16[16,4224]{1,0:T(8,128)(2,1)S(1)}, bf16[16,4224]{1,0:T(8,128)(2,1)S(1)}, u32[]{:S(2)}, u32[]{:S(2)}) collective-permute-start(bf16[16,4224]{1,0:T(8,128)(2,1)S(1)} %get-tuple-element.158), channel_id=1, source_target_pairs={{0,8},{8,0},{16,24},{24,16},{1,9},{9,1},{17,25},{25,17},{2,10},{10... | collective-permute-start | bytes 405512 | tf_op jit(solution)/shard_map/ppermute | solution.py:20
  39.6 3.1 %expert_layer.3 = (bf16[32,4096]{1,0:T(8,128)(2,1)S(1)}, bf16[32,4096]{1,0:T(8,128)(2,1)S(1)}, bf16[32,4096]{1,0:T(8,128)(2,1)S(1)}, bf16[32,4096]{1,0:T(8,128)(2,1)S(1)}) custom-call(s32[1]{0:T(128)} %bitcast.own_expert, bf16[32,4224]{1,0:T(8,128)(2,1)S(1)} %pad_maximum_fusion.2.refs_0_, bf16[32,4224]{1,0:T(8,128)(2,1)S(1)} %collective-permute-done.4.refs_1_, ...), custom_call_target="tpu_custom_call" | custom-call | flops 2415919104 | bytes 20971520 | tf_op jit(solution)/shard_map/expert_layer/pallas_call | solution.py:225
  44.1 1.6 %collective-permute-start.18 = (bf16[32,4224]{1,0:T(8,128)(2,1)S(1)}, bf16[32,4224]{1,0:T(8,128)(2,1)S(1)}, u32[]{:S(2)}, u32[]{:S(2)}) collective-permute-start(bf16[32,4224]{1,0:T(8,128)(2,1)S(1)} %pad_maximum_fusion.5.refs_2_), channel_id=1, source_target_pairs={{0,8},{8,0},{16,24},{24,16},{1,9},{9,1},{17,25},{25,17},{2,10},{10... | collective-permute-start | bytes 811016 | tf_op jit(solution)/shard_map/ppermute | solution.py:20
  45.6 7.8 %collective-permute-done.13.refs_1_ = bf16[64,4224]{1,0:T(8,128)(2,1)S(1)} collective-permute-done((bf16[64,4224]{1,0:T(8,128)(2,1)S(1)}, bf16[64,4224]{1,0:T(8,128)(2,1)S(1)}, u32[]{:S(2)}, u32[]{:S(2)}) %collective-permute-start.13) | collective-permute-done | bytes 540704 | tf_op jit(solution)/shard_map/ppermute | solution.py:20
  53.4 1.5 %collective-permute-done.14.refs_3_ = bf16[64,4224]{1,0:T(8,128)(2,1)S(1)} collective-permute-done((bf16[64,4224]{1,0:T(8,128)(2,1)S(1)}, bf16[64,4224]{1,0:T(8,128)(2,1)S(1)}, u32[]{:S(2)}, u32[]{:S(2)}) %collective-permute-start.14) | collective-permute-done | bytes 540704 | tf_op jit(solution)/shard_map/ppermute | solution.py:20
  55.4 1.7 %collective-permute-start.20 = (bf16[32,4096]{1,0:T(8,128)(2,1)S(1)}, bf16[32,4096]{1,0:T(8,128)(2,1)S(1)}, u32[]{:S(2)}, u32[]{:S(2)}) collective-permute-start(bf16[32,4096]{1,0:T(8,128)(2,1)S(1)} %get-tuple-element.118), channel_id=1, source_target_pairs={{0,8},{8,0},{16,24},{24,16},{1,9},{9,1},{17,25},{25,17},{2,10},{10... | collective-permute-start | bytes 786440 | tf_op jit(solution)/shard_map/ppermute | solution.py:20
  57.0 5.7 %expert_layer.4 = (bf16[64,4096]{1,0:T(8,128)(2,1)S(1)}, bf16[64,4096]{1,0:T(8,128)(2,1)S(1)}, bf16[64,4096]{1,0:T(8,128)(2,1)S(1)}, bf16[64,4096]{1,0:T(8,128)(2,1)S(1)}) custom-call(s32[1]{0:T(128)} %bitcast.own_expert, bf16[64,4224]{1,0:T(8,128)(2,1)S(1)} %pad_maximum_fusion.refs_0_, bf16[64,4224]{1,0:T(8,128)(2,1)S(1)} %collective-permute-done.13.refs_1_, ...), custom_call_target="tpu_custom_call" | custom-call | flops 4831838208 | bytes 23068672 | tf_op jit(solution)/shard_map/expert_layer/pallas_call | solution.py:225
  64.6 3.1 %expert_layer.5 = (bf16[32,4096]{1,0:T(8,128)(2,1)S(1)}, bf16[32,4096]{1,0:T(8,128)(2,1)S(1)}, bf16[32,4096]{1,0:T(8,128)(2,1)S(1)}, bf16[32,4096]{1,0:T(8,128)(2,1)S(1)}) custom-call(s32[1]{0:T(128)} %bitcast.own_expert, bf16[32,4224]{1,0:T(8,128)(2,1)S(1)} %pad_maximum_fusion.4.refs_0_, bf16[32,4224]{1,0:T(8,128)(2,1)S(1)} %collective-permute-done.16.refs_1_, ...), custom_call_target="tpu_custom_call" | custom-call | flops 2415919104 | bytes 20971520 | tf_op jit(solution)/shard_map/expert_layer/pallas_call | solution.py:225
  69.8 4.6 %collective-permute-done.21 = bf16[32,4096]{1,0:T(8,128)(2,1)S(1)} collective-permute-done((bf16[32,4096]{1,0:T(8,128)(2,1)S(1)}, bf16[32,4096]{1,0:T(8,128)(2,1)S(1)}, u32[]{:S(2)}, u32[]{:S(2)}) %collective-permute-start.21) | collective-permute-done | bytes 262176 | tf_op jit(solution)/shard_map/ppermute | solution.py:20
  76.3 1.3 %collective-permute-start.25 = (bf16[16,4096]{1,0:T(8,128)(2,1)S(1)}, bf16[16,4096]{1,0:T(8,128)(2,1)S(1)}, u32[]{:S(2)}, u32[]{:S(2)}) collective-permute-start(bf16[16,4096]{1,0:T(8,128)(2,1)S(1)} %split.37), channel_id=1, source_target_pairs={{0,8},{8,0},{16,24},{24,16},{1,9},{9,1},{17,25},{25,17},{2,10},{10... | collective-permute-start | bytes 393224 | tf_op jit(solution)/shard_map/ppermute | solution.py:20
  78.4 1.5 %collective-permute-start.24 = (bf16[64,4096]{1,0:T(8,128)(2,1)S(1)}, bf16[64,4096]{1,0:T(8,128)(2,1)S(1)}, u32[]{:S(2)}, u32[]{:S(2)}) collective-permute-start(bf16[64,4096]{1,0:T(8,128)(2,1)S(1)} %get-tuple-element.140), channel_id=1, source_target_pairs={{0,8},{8,0},{16,24},{24,16},{1,9},{9,1},{17,25},{25,17},{2,10},{10... | collective-permute-start | bytes 1572872 | tf_op jit(solution)/shard_map/ppermute | solution.py:20
  79.9 2.3 %collective-permute-done.26 = bf16[16,4096]{1,0:T(8,128)(2,1)S(1)} collective-permute-done((bf16[16,4096]{1,0:T(8,128)(2,1)S(1)}, bf16[16,4096]{1,0:T(8,128)(2,1)S(1)}, u32[]{:S(2)}, u32[]{:S(2)}) %collective-permute-start.26) | collective-permute-done | bytes 131104 | tf_op jit(solution)/shard_map/ppermute | solution.py:20
  82.9 1.4 %collective-permute-start.27 = (bf16[32,4096]{1,0:T(8,128)(2,1)S(1)}, bf16[32,4096]{1,0:T(8,128)(2,1)S(1)}, u32[]{:S(2)}, u32[]{:S(2)}) collective-permute-start(bf16[32,4096]{1,0:T(8,128)(2,1)S(1)} %pad_maximum_fusion.6), channel_id=1, source_target_pairs={{0,2},{1,3},{2,0},{3,1},{4,6},{5,7},{6,4},{7,5},{8,10},{9,11},{10,... | collective-permute-start | bytes 786440 | tf_op jit(solution)/shard_map/ppermute | solution.py:246
  84.3 5.9 %collective-permute-done.23 = bf16[64,4096]{1,0:T(8,128)(2,1)S(1)} collective-permute-done((bf16[64,4096]{1,0:T(8,128)(2,1)S(1)}, bf16[64,4096]{1,0:T(8,128)(2,1)S(1)}, u32[]{:S(2)}, u32[]{:S(2)}) %collective-permute-start.23) | collective-permute-done | bytes 524320 | tf_op jit(solution)/shard_map/ppermute | solution.py:20
  90.8 1.5 %collective-permute-start.29 = (bf16[32,4096]{1,0:T(8,128)(2,1)S(1)}, bf16[32,4096]{1,0:T(8,128)(2,1)S(1)}, u32[]{:S(2)}, u32[]{:S(2)}) collective-permute-start(bf16[32,4096]{1,0:T(8,128)(2,1)S(1)} %split.43), channel_id=1, source_target_pairs={{0,16},{16,0},{8,24},{24,8},{1,17},{17,1},{9,25},{25,9},{2,18},{18... | collective-permute-start | bytes 786440 | tf_op jit(solution)/shard_map/ppermute | solution.py:20
  93.0 4.2 %collective-permute-done.29 = bf16[32,4096]{1,0:T(8,128)(2,1)S(1)} collective-permute-done((bf16[32,4096]{1,0:T(8,128)(2,1)S(1)}, bf16[32,4096]{1,0:T(8,128)(2,1)S(1)}, u32[]{:S(2)}, u32[]{:S(2)}) %collective-permute-start.29) | collective-permute-done | bytes 262176 | tf_op jit(solution)/shard_map/ppermute | solution.py:20
  97.3 1.9 %collective-permute-done.28 = bf16[32,4096]{1,0:T(8,128)(2,1)S(1)} collective-permute-done((bf16[32,4096]{1,0:T(8,128)(2,1)S(1)}, bf16[32,4096]{1,0:T(8,128)(2,1)S(1)}, u32[]{:S(2)}, u32[]{:S(2)}) %collective-permute-start.28) | collective-permute-done | bytes 262176 | tf_op jit(solution)/shard_map/ppermute | solution.py:20
  101.4 1.3 %collective-permute-start.30 = (bf16[16,4096]{1,0:T(8,128)(2,1)S(1)}, bf16[16,4096]{1,0:T(8,128)(2,1)S(1)}, u32[]{:S(2)}, u32[]{:S(2)}) collective-permute-start(bf16[16,4096]{1,0:T(8,128)(2,1)S(1)} %split.45), channel_id=1, source_target_pairs={{0,8},{8,0},{16,24},{24,16},{1,9},{9,1},{17,25},{25,17},{2,10},{10... | collective-permute-start | bytes 393224 | tf_op jit(solution)/shard_map/ppermute | solution.py:20
  102.7 3.0 %collective-permute-done.33 = bf16[16,4096]{1,0:T(8,128)(2,1)S(1)} collective-permute-done((bf16[16,4096]{1,0:T(8,128)(2,1)S(1)}, bf16[16,4096]{1,0:T(8,128)(2,1)S(1)}, u32[]{:S(2)}, u32[]{:S(2)}) %collective-permute-start.33) | collective-permute-done | bytes 131104 | tf_op jit(solution)/shard_map/ppermute | solution.py:20
  106.4 3.1 %collective-permute-done.31 = bf16[32,4096]{1,0:T(8,128)(2,1)S(1)} collective-permute-done((bf16[32,4096]{1,0:T(8,128)(2,1)S(1)}, bf16[32,4096]{1,0:T(8,128)(2,1)S(1)}, u32[]{:S(2)}, u32[]{:S(2)}) %collective-permute-start.31) | collective-permute-done | bytes 262176 | tf_op jit(solution)/shard_map/ppermute | solution.py:246
  (90 shorter events, 20.9 us)
Async XLA Ops:
  2.1 12.4 %collective-permute-start.3 = (bf16[16,4224]{1,0:T(8,128)(2,1)S(1)}, bf16[16,4224]{1,0:T(8,128)(2,1)S(1)}, u32[]{:S(2)}, u32[]{:S(2)}) collective-permute-start(bf16[16,4224]{1,0:T(8,128)(2,1)S(1)} %concatenate.38), channel_id=1, source_target_pairs={{0,4},{1,5},{2,6},{3,7},{4,0},{5,1},{6,2},{7,3},{8,12},{9,13},{10,... | collective-permute-start | bytes 405512 | tf_op jit(solution)/shard_map/ppermute | solution.py:246
  6.1 8.4 %collective-permute-start.2 = (bf16[16,4224]{1,0:T(8,128)(2,1)S(1)}, bf16[16,4224]{1,0:T(8,128)(2,1)S(1)}, u32[]{:S(2)}, u32[]{:S(2)}) collective-permute-start(bf16[16,4224]{1,0:T(8,128)(2,1)S(1)} %concatenate.38), channel_id=1, source_target_pairs={{0,2},{1,3},{2,0},{3,1},{4,6},{5,7},{6,4},{7,5},{8,10},{9,11},{10,... | collective-permute-start | bytes 405512 | tf_op jit(solution)/shard_map/ppermute | solution.py:246
  7.7 6.8 %collective-permute-start = (bf16[16,4224]{1,0:T(8,128)(2,1)S(1)}, bf16[16,4224]{1,0:T(8,128)(2,1)S(1)}, u32[]{:S(2)}, u32[]{:S(2)}) collective-permute-start(bf16[16,4224]{1,0:T(8,128)(2,1)S(1)} %concatenate.38), channel_id=1, source_target_pairs={{0,8},{8,0},{16,24},{24,16},{1,9},{9,1},{17,25},{25,17},{2,10},{10... | collective-permute-start | bytes 405512 | tf_op jit(solution)/shard_map/ppermute | solution.py:20
  9.2 5.3 %collective-permute-start.1 = (bf16[16,4224]{1,0:T(8,128)(2,1)S(1)}, bf16[16,4224]{1,0:T(8,128)(2,1)S(1)}, u32[]{:S(2)}, u32[]{:S(2)}) collective-permute-start(bf16[16,4224]{1,0:T(8,128)(2,1)S(1)} %concatenate.39), channel_id=1, source_target_pairs={{0,16},{16,0},{8,24},{24,8},{1,17},{17,1},{9,25},{25,9},{2,18},{18... | collective-permute-start | bytes 405512 | tf_op jit(solution)/shard_map/ppermute | solution.py:20
  14.5 20.9 %collective-permute-start.11 = (bf16[4096,768]{1,0:T(8,128)(2,1)S(1)}, bf16[4096,768]{1,0:T(8,128)(2,1)S(1)}, u32[]{:S(2)}, u32[]{:S(2)}) collective-permute-start(bf16[4096,768]{1,0:T(8,128)(2,1)S(1)} %dequantize_in.1.refs_4_), channel_id=1, source_target_pairs={{0,1},{1,0},{2,3},{3,2},{4,5},{5,4},{6,7},{7,6},{8,9},{9,8},{10,11... | collective-permute-start | bytes 18874376 | tf_op jit(solution)/shard_map/ppermute | solution.py:20
  14.6 11.0 %collective-permute-start.4 = (bf16[32,4224]{1,0:T(8,128)(2,1)S(1)}, bf16[32,4224]{1,0:T(8,128)(2,1)S(1)}, u32[]{:S(2)}, u32[]{:S(2)}) collective-permute-start(bf16[32,4224]{1,0:T(8,128)(2,1)S(1)} %pad_maximum_fusion.2.refs_0_), channel_id=1, source_target_pairs={{0,16},{16,0},{8,24},{24,8},{1,17},{17,1},{9,25},{25,9},{2,18},{18... | collective-permute-start | bytes 811016 | tf_op jit(solution)/shard_map/ppermute | solution.py:20
  15.9 9.7 %collective-permute-start.5 = (bf16[32,4224]{1,0:T(8,128)(2,1)S(1)}, bf16[32,4224]{1,0:T(8,128)(2,1)S(1)}, u32[]{:S(2)}, u32[]{:S(2)}) collective-permute-start(bf16[32,4224]{1,0:T(8,128)(2,1)S(1)} %pad_maximum_fusion.3.refs_2_), channel_id=1, source_target_pairs={{0,8},{8,0},{16,24},{24,16},{1,9},{9,1},{17,25},{25,17},{2,10},{10... | collective-permute-start | bytes 811016 | tf_op jit(solution)/shard_map/ppermute | solution.py:20
  16.5 9.2 %collective-permute-start.7 = (bf16[16,4224]{1,0:T(8,128)(2,1)S(1)}, bf16[16,4224]{1,0:T(8,128)(2,1)S(1)}, u32[]{:S(2)}, u32[]{:S(2)}) collective-permute-start(bf16[16,4224]{1,0:T(8,128)(2,1)S(1)} %concatenate.39), channel_id=1, source_target_pairs={{0,4},{1,5},{2,6},{3,7},{4,0},{5,1},{6,2},{7,3},{8,12},{9,13},{10,... | collective-permute-start | bytes 405512 | tf_op jit(solution)/shard_map/ppermute | solution.py:246
  17.3 8.4 %collective-permute-start.6 = (bf16[16,4224]{1,0:T(8,128)(2,1)S(1)}, bf16[16,4224]{1,0:T(8,128)(2,1)S(1)}, u32[]{:S(2)}, u32[]{:S(2)}) collective-permute-start(bf16[16,4224]{1,0:T(8,128)(2,1)S(1)} %concatenate.39), channel_id=1, source_target_pairs={{0,2},{1,3},{2,0},{3,1},{4,6},{5,7},{6,4},{7,5},{8,10},{9,11},{10,... | collective-permute-start | bytes 405512 | tf_op jit(solution)/shard_map/ppermute | solution.py:246
  25.6 9.8 %collective-permute-start.12 = (bf16[384,4096]{1,0:T(8,128)(2,1)S(1)}, bf16[384,4096]{1,0:T(8,128)(2,1)S(1)}, u32[]{:S(2)}, u32[]{:S(2)}) collective-permute-start(bf16[384,4096]{1,0:T(8,128)(2,1)S(1)} %dequantize_down.1.refs_6_), channel_id=1, source_target_pairs={{0,1},{1,0},{2,3},{3,2},{4,5},{5,4},{6,7},{7,6},{8,9},{9,8},{10,11... | collective-permute-start | bytes 9437192 | tf_op jit(solution)/shard_map/ppermute | solution.py:20
  25.8 9.6 %collective-permute-start.10 = (bf16[32,4224]{1,0:T(8,128)(2,1)S(1)}, bf16[32,4224]{1,0:T(8,128)(2,1)S(1)}, u32[]{:S(2)}, u32[]{:S(2)}) collective-permute-start(bf16[32,4224]{1,0:T(8,128)(2,1)S(1)} %constant_dynamic-update-slice_fusion.2), channel_id=1, source_target_pairs={{0,2},{1,3},{2,0},{3,1},{4,6},{5,7},{6,4},{7,5},{8,10},{9,11},{10,... | collective-permute-start | bytes 811016 | tf_op jit(solution)/shard_map/ppermute | solution.py:246
  25.8 8.9 %collective-permute-start.9 = (bf16[32,4224]{1,0:T(8,128)(2,1)S(1)}, bf16[32,4224]{1,0:T(8,128)(2,1)S(1)}, u32[]{:S(2)}, u32[]{:S(2)}) collective-permute-start(bf16[32,4224]{1,0:T(8,128)(2,1)S(1)} %constant_dynamic-update-slice_fusion.2), channel_id=1, source_target_pairs={{0,16},{16,0},{8,24},{24,8},{1,17},{17,1},{9,25},{25,9},{2,18},{18... | collective-permute-start | bytes 811016 | tf_op jit(solution)/shard_map/ppermute | solution.py:20
  26.7 8.7 %collective-permute-start.8 = (bf16[32,4224]{1,0:T(8,128)(2,1)S(1)}, bf16[32,4224]{1,0:T(8,128)(2,1)S(1)}, u32[]{:S(2)}, u32[]{:S(2)}) collective-permute-start(bf16[32,4224]{1,0:T(8,128)(2,1)S(1)} %constant_dynamic-update-slice_fusion), channel_id=1, source_target_pairs={{0,8},{8,0},{16,24},{24,16},{1,9},{9,1},{17,25},{25,17},{2,10},{10... | collective-permute-start | bytes 811016 | tf_op jit(solution)/shard_map/ppermute | solution.py:20
  35.5 8.6 %collective-permute-start.17 = (bf16[16,4224]{1,0:T(8,128)(2,1)S(1)}, bf16[16,4224]{1,0:T(8,128)(2,1)S(1)}, u32[]{:S(2)}, u32[]{:S(2)}) collective-permute-start(bf16[16,4224]{1,0:T(8,128)(2,1)S(1)} %get-tuple-element.157), channel_id=1, source_target_pairs={{0,16},{16,0},{8,24},{24,8},{1,17},{17,1},{9,25},{25,9},{2,18},{18... | collective-permute-start | bytes 405512 | tf_op jit(solution)/shard_map/ppermute | solution.py:20
  36.8 6.5 %collective-permute-start.15 = (bf16[16,4224]{1,0:T(8,128)(2,1)S(1)}, bf16[16,4224]{1,0:T(8,128)(2,1)S(1)}, u32[]{:S(2)}, u32[]{:S(2)}) collective-permute-start(bf16[16,4224]{1,0:T(8,128)(2,1)S(1)} %get-tuple-element.158), channel_id=1, source_target_pairs={{0,8},{8,0},{16,24},{24,16},{1,9},{9,1},{17,25},{25,17},{2,10},{10... | collective-permute-start | bytes 405512 | tf_op jit(solution)/shard_map/ppermute | solution.py:20
  38.2 15.2 %collective-permute-start.13 = (bf16[64,4224]{1,0:T(8,128)(2,1)S(1)}, bf16[64,4224]{1,0:T(8,128)(2,1)S(1)}, u32[]{:S(2)}, u32[]{:S(2)}) collective-permute-start(bf16[64,4224]{1,0:T(8,128)(2,1)S(1)} %pad_maximum_fusion.refs_0_), channel_id=1, source_target_pairs={{0,16},{16,0},{8,24},{24,8},{1,17},{17,1},{9,25},{25,9},{2,18},{18... | collective-permute-start | bytes 1622024 | tf_op jit(solution)/shard_map/ppermute | solution.py:20
  38.9 15.9 %collective-permute-start.14 = (bf16[64,4224]{1,0:T(8,128)(2,1)S(1)}, bf16[64,4224]{1,0:T(8,128)(2,1)S(1)}, u32[]{:S(2)}, u32[]{:S(2)}) collective-permute-start(bf16[64,4224]{1,0:T(8,128)(2,1)S(1)} %pad_maximum_fusion.1.refs_2_), channel_id=1, source_target_pairs={{0,8},{8,0},{16,24},{24,16},{1,9},{9,1},{17,25},{25,17},{2,10},{10... | collective-permute-start | bytes 1622024 | tf_op jit(solution)/shard_map/ppermute | solution.py:20
  43.3 21.3 %collective-permute-start.16 = (bf16[32,4224]{1,0:T(8,128)(2,1)S(1)}, bf16[32,4224]{1,0:T(8,128)(2,1)S(1)}, u32[]{:S(2)}, u32[]{:S(2)}) collective-permute-start(bf16[32,4224]{1,0:T(8,128)(2,1)S(1)} %pad_maximum_fusion.4.refs_0_), channel_id=1, source_target_pairs={{0,16},{16,0},{8,24},{24,8},{1,17},{17,1},{9,25},{25,9},{2,18},{18... | collective-permute-start | bytes 811016 | tf_op jit(solution)/shard_map/ppermute | solution.py:20
  44.1 20.5 %collective-permute-start.18 = (bf16[32,4224]{1,0:T(8,128)(2,1)S(1)}, bf16[32,4224]{1,0:T(8,128)(2,1)S(1)}, u32[]{:S(2)}, u32[]{:S(2)}) collective-permute-start(bf16[32,4224]{1,0:T(8,128)(2,1)S(1)} %pad_maximum_fusion.5.refs_2_), channel_id=1, source_target_pairs={{0,8},{8,0},{16,24},{24,16},{1,9},{9,1},{17,25},{25,17},{2,10},{10... | collective-permute-start | bytes 811016 | tf_op jit(solution)/shard_map/ppermute | solution.py:20
  54.8 8.7 %collective-permute-start.19 = (bf16[32,4096]{1,0:T(8,128)(2,1)S(1)}, bf16[32,4096]{1,0:T(8,128)(2,1)S(1)}, u32[]{:S(2)}, u32[]{:S(2)}) collective-permute-start(bf16[32,4096]{1,0:T(8,128)(2,1)S(1)} %get-tuple-element.116), channel_id=1, source_target_pairs={{0,16},{16,0},{8,24},{24,8},{1,17},{17,1},{9,25},{25,9},{2,18},{18... | collective-permute-start | bytes 786440 | tf_op jit(solution)/shard_map/ppermute | solution.py:20
  55.4 9.2 %collective-permute-start.20 = (bf16[32,4096]{1,0:T(8,128)(2,1)S(1)}, bf16[32,4096]{1,0:T(8,128)(2,1)S(1)}, u32[]{:S(2)}, u32[]{:S(2)}) collective-permute-start(bf16[32,4096]{1,0:T(8,128)(2,1)S(1)} %get-tuple-element.118), channel_id=1, source_target_pairs={{0,8},{8,0},{16,24},{24,16},{1,9},{9,1},{17,25},{25,17},{2,10},{10... | collective-permute-start | bytes 786440 | tf_op jit(solution)/shard_map/ppermute | solution.py:20
  67.7 6.7 %collective-permute-start.21 = (bf16[32,4096]{1,0:T(8,128)(2,1)S(1)}, bf16[32,4096]{1,0:T(8,128)(2,1)S(1)}, u32[]{:S(2)}, u32[]{:S(2)}) collective-permute-start(bf16[32,4096]{1,0:T(8,128)(2,1)S(1)} %get-tuple-element.130), channel_id=1, source_target_pairs={{0,16},{16,0},{8,24},{24,8},{1,17},{17,1},{9,25},{25,9},{2,18},{18... | collective-permute-start | bytes 786440 | tf_op jit(solution)/shard_map/ppermute | solution.py:20
  68.8 6.8 %collective-permute-start.22 = (bf16[32,4096]{1,0:T(8,128)(2,1)S(1)}, bf16[32,4096]{1,0:T(8,128)(2,1)S(1)}, u32[]{:S(2)}, u32[]{:S(2)}) collective-permute-start(bf16[32,4096]{1,0:T(8,128)(2,1)S(1)} %get-tuple-element.132), channel_id=1, source_target_pairs={{0,8},{8,0},{16,24},{24,16},{1,9},{9,1},{17,25},{25,17},{2,10},{10... | collective-permute-start | bytes 786440 | tf_op jit(solution)/shard_map/ppermute | solution.py:20
  75.7 6.5 %collective-permute-start.26 = (bf16[16,4096]{1,0:T(8,128)(2,1)S(1)}, bf16[16,4096]{1,0:T(8,128)(2,1)S(1)}, u32[]{:S(2)}, u32[]{:S(2)}) collective-permute-start(bf16[16,4096]{1,0:T(8,128)(2,1)S(1)} %split.39), channel_id=1, source_target_pairs={{0,16},{16,0},{8,24},{24,8},{1,17},{17,1},{9,25},{25,9},{2,18},{18... | collective-permute-start | bytes 393224 | tf_op jit(solution)/shard_map/ppermute | solution.py:20
  76.3 6.5 %collective-permute-start.25 = (bf16[16,4096]{1,0:T(8,128)(2,1)S(1)}, bf16[16,4096]{1,0:T(8,128)(2,1)S(1)}, u32[]{:S(2)}, u32[]{:S(2)}) collective-permute-start(bf16[16,4096]{1,0:T(8,128)(2,1)S(1)} %split.37), channel_id=1, source_target_pairs={{0,8},{8,0},{16,24},{24,16},{1,9},{9,1},{17,25},{25,17},{2,10},{10... | collective-permute-start | bytes 393224 | tf_op jit(solution)/shard_map/ppermute | solution.py:20
  77.7 12.5 %collective-permute-start.23 = (bf16[64,4096]{1,0:T(8,128)(2,1)S(1)}, bf16[64,4096]{1,0:T(8,128)(2,1)S(1)}, u32[]{:S(2)}, u32[]{:S(2)}) collective-permute-start(bf16[64,4096]{1,0:T(8,128)(2,1)S(1)} %get-tuple-element.138), channel_id=1, source_target_pairs={{0,16},{16,0},{8,24},{24,8},{1,17},{17,1},{9,25},{25,9},{2,18},{18... | collective-permute-start | bytes 1572872 | tf_op jit(solution)/shard_map/ppermute | solution.py:20
  78.4 12.2 %collective-permute-start.24 = (bf16[64,4096]{1,0:T(8,128)(2,1)S(1)}, bf16[64,4096]{1,0:T(8,128)(2,1)S(1)}, u32[]{:S(2)}, u32[]{:S(2)}) collective-permute-start(bf16[64,4096]{1,0:T(8,128)(2,1)S(1)} %get-tuple-element.140), channel_id=1, source_target_pairs={{0,8},{8,0},{16,24},{24,16},{1,9},{9,1},{17,25},{25,17},{2,10},{10... | collective-permute-start | bytes 1572872 | tf_op jit(solution)/shard_map/ppermute | solution.py:20
  82.9 7.8 %collective-permute-start.27 = (bf16[32,4096]{1,0:T(8,128)(2,1)S(1)}, bf16[32,4096]{1,0:T(8,128)(2,1)S(1)}, u32[]{:S(2)}, u32[]{:S(2)}) collective-permute-start(bf16[32,4096]{1,0:T(8,128)(2,1)S(1)} %pad_maximum_fusion.6), channel_id=1, source_target_pairs={{0,2},{1,3},{2,0},{3,1},{4,6},{5,7},{6,4},{7,5},{8,10},{9,11},{10,... | collective-permute-start | bytes 786440 | tf_op jit(solution)/shard_map/ppermute | solution.py:246
  90.8 6.4 %collective-permute-start.29 = (bf16[32,4096]{1,0:T(8,128)(2,1)S(1)}, bf16[32,4096]{1,0:T(8,128)(2,1)S(1)}, u32[]{:S(2)}, u32[]{:S(2)}) collective-permute-start(bf16[32,4096]{1,0:T(8,128)(2,1)S(1)} %split.43), channel_id=1, source_target_pairs={{0,16},{16,0},{8,24},{24,8},{1,17},{17,1},{9,25},{25,9},{2,18},{18... | collective-permute-start | bytes 786440 | tf_op jit(solution)/shard_map/ppermute | solution.py:20
  92.2 7.0 %collective-permute-start.28 = (bf16[32,4096]{1,0:T(8,128)(2,1)S(1)}, bf16[32,4096]{1,0:T(8,128)(2,1)S(1)}, u32[]{:S(2)}, u32[]{:S(2)}) collective-permute-start(bf16[32,4096]{1,0:T(8,128)(2,1)S(1)} %split.41), channel_id=1, source_target_pairs={{0,8},{8,0},{16,24},{24,16},{1,9},{9,1},{17,25},{25,17},{2,10},{10... | collective-permute-start | bytes 786440 | tf_op jit(solution)/shard_map/ppermute | solution.py:20
  99.3 10.1 %collective-permute-start.31 = (bf16[32,4096]{1,0:T(8,128)(2,1)S(1)}, bf16[32,4096]{1,0:T(8,128)(2,1)S(1)}, u32[]{:S(2)}, u32[]{:S(2)}) collective-permute-start(bf16[32,4096]{1,0:T(8,128)(2,1)S(1)} %add_convert_fusion.2), channel_id=1, source_target_pairs={{0,4},{1,5},{2,6},{3,7},{4,0},{5,1},{6,2},{7,3},{8,12},{9,13},{10,... | collective-permute-start | bytes 786440 | tf_op jit(solution)/shard_map/ppermute | solution.py:246
  100.0 9.4 %collective-permute-start.32 = (bf16[32,4096]{1,0:T(8,128)(2,1)S(1)}, bf16[32,4096]{1,0:T(8,128)(2,1)S(1)}, u32[]{:S(2)}, u32[]{:S(2)}) collective-permute-start(bf16[32,4096]{1,0:T(8,128)(2,1)S(1)} %add_convert_fusion.4), channel_id=1, source_target_pairs={{0,2},{1,3},{2,0},{3,1},{4,6},{5,7},{6,4},{7,5},{8,10},{9,11},{10,... | collective-permute-start | bytes 786440 | tf_op jit(solution)/shard_map/ppermute | solution.py:246
  (6 other events, 48.9 us)
